TPU v7x, 32 devices: a whole 2x2x4 slice. The times are simulated.
32 devices in a mesh: outer: 4 (over y, x), inner: 8 (over z, core).
Axes of the slice: x: 2, y: 2, z: 4, core: 2. Of those that a mesh axis runs over, the one named last changes fastest.
Arguments:
- query: bfloat16 [4096, 512], P(('outer', 'inner')), may hold values from -6 to 6
- key: bfloat16 [4096, 128], P(('outer', 'inner')), may hold values from -6 to 6
- value: bfloat16 [4096, 128], P(('outer', 'inner')), may hold values from -6 to 6
- out: bfloat16 [4096, 512], P(('outer', 'inner')), may hold values from -4 to 4
- grad_out: bfloat16 [4096, 512], P(('outer', 'inner')), may hold values from -12 to 12
- lse: float32 [4, 4096], P(None, ('outer', 'inner')), may hold values from -60 to 60, as said below
- positions: int32 [4096], P(('outer', 'inner')), may hold values from 0 to 4095, as said below
Outputs:
- grad_query: bfloat16 [4096, 512], P(('outer', 'inner'))
- grad_key: bfloat16 [4096, 128], P(('outer', 'inner'))
- grad_value: bfloat16 [4096, 128], P(('outer', 'inner'))
Inputs may be any that keep to these rules, and one draw needn't show every extreme that they name: positions is a permutation of 0 to 4095; every aligned run of 64 rows holds 64 consecutive positions in increasing order, starting at a multiple of 64. lse[h, i] is the log of the sum of exp(scores[h, i, j]) over all j with positions[j] <= positions[i].
All inputs are finite; a program needn't handle non-finite values.
Results may differ from a plain program's by a relative error of at most 0.005.
Values may be sent and summed in bfloat16 or wider, within the bound.
No kernel may reach another device: no remote copies, remote signals or barrier semaphores. Data moves between devices by JAX's collectives and lax.ppermute only.
A program may use at most 64 MiB of HBM per device.

v0:
```python
import jax
import jax.numpy as jnp
from jax import lax
from jax.sharding import PartitionSpec as P


def passed_along(block, axis, distance):
    devices = range(lax.axis_size(axis))
    route = [((i - distance) % len(devices), i) for i in devices]
    return lax.ppermute(block, axis, route)


def block_terms(q3, g3, lse, delta, my_pos, keys, values, key_pos, scale):
    scores = scale * jnp.einsum("rhd,kd->hrk", q3, keys, preferred_element_type=jnp.float32)
    allowed = key_pos[None, None, :] <= my_pos[None, :, None]
    probs = jnp.where(allowed, jnp.exp(scores - lse[:, :, None]), 0.0)
    grad_v = jnp.einsum(
        "hrk,rhd->kd", probs.astype(jnp.bfloat16), g3, preferred_element_type=jnp.float32
    )
    dprobs = jnp.einsum("rhd,kd->hrk", g3, values, preferred_element_type=jnp.float32)
    dscores = (probs * (dprobs - delta[:, :, None])).astype(jnp.bfloat16)
    grad_q = jnp.einsum("hrk,kd->rhd", dscores, keys, preferred_element_type=jnp.float32)
    grad_k = jnp.einsum("hrk,rhd->kd", dscores, q3, preferred_element_type=jnp.float32)
    return (grad_q, grad_k, grad_v)


def process(q3, g3, lse, delta, my_pos, key_stack, value_stack, pos_stack, scale):
    count, rows, width = key_stack.shape
    grad_q, grad_k, grad_v = block_terms(
        q3,
        g3,
        lse,
        delta,
        my_pos,
        key_stack.reshape(count * rows, width),
        value_stack.reshape(count * rows, width),
        pos_stack.reshape(count * rows),
        scale,
    )
    return (grad_q, grad_k.reshape(count, rows, width), grad_v.reshape(count, rows, width))


def on_device(query, key, value, out, grad_out, lse, positions):
    rows, width = key.shape
    heads = query.shape[1] // width
    scale = width ** (-0.5)
    q3 = query.reshape(rows, heads, width)
    g3 = grad_out.reshape(rows, heads, width)
    delta = jnp.einsum(
        "rhd,rhd->hr", g3.astype(jnp.float32), out.reshape(rows, heads, width).astype(jnp.float32)
    )
    n_outer = lax.axis_size("outer")
    n_inner = lax.axis_size("inner")
    inner_index = lax.axis_index("inner")
    pos_all = lax.all_gather(positions, ("outer", "inner"), axis=0, tiled=True)
    table = pos_all.reshape(n_outer, n_inner, rows)
    key_stack, value_stack = (
        lax.all_gather(key[None], "outer", axis=0, tiled=True),
        lax.all_gather(value[None], "outer", axis=0, tiled=True),
    )

    def visit(step, sign, part_table, key_part, value_part, grad_q, acc_k, acc_v):
        anchor = (inner_index - sign * step) % n_inner
        pos_stack = lax.dynamic_index_in_dim(part_table, anchor, 1, keepdims=False)
        part_q, part_k, part_v = process(
            q3, g3, lse, delta, positions, key_part, value_part, pos_stack, scale
        )
        return (grad_q + part_q, acc_k + part_k, acc_v + part_v)

    grad_q = jnp.zeros((rows, heads, width), jnp.float32)
    zeros = jnp.zeros((n_outer, rows, width), jnp.float32)
    grad_q, acc_k, acc_v = visit(0, 1, table, key_stack, value_stack, grad_q, zeros, zeros)

    def turn(step, carry):
        keys_now, vals_now, grad_q, acc_k, acc_v = carry
        keys_now, vals_now = passed_along((keys_now, vals_now), "inner", 1)
        acc_k, acc_v = passed_along((acc_k, acc_v), "inner", 1)
        grad_q, acc_k, acc_v = visit(step, 1, table, keys_now, vals_now, grad_q, acc_k, acc_v)
        return (keys_now, vals_now, grad_q, acc_k, acc_v)

    carry = lax.fori_loop(1, n_inner, turn, (key_stack, value_stack, grad_q, acc_k, acc_v))
    grad_q, acc_k, acc_v = (carry[2], carry[3], carry[4])
    acc_k, acc_v = passed_along((acc_k, acc_v), "inner", 1)
    sum_k, sum_v = (
        lax.psum_scatter(acc_k, "outer", scatter_dimension=0, tiled=True),
        lax.psum_scatter(acc_v, "outer", scatter_dimension=0, tiled=True),
    )
    grad_query = (scale * grad_q).reshape(rows, heads * width).astype(jnp.bfloat16)
    return (grad_query, (scale * sum_k[0]).astype(jnp.bfloat16), sum_v[0].astype(jnp.bfloat16))


def solution(mesh):
    return jax.shard_map(
        on_device,
        mesh=mesh,
        in_specs=(
            P(("outer", "inner"), None),
            P(("outer", "inner"), None),
            P(("outer", "inner"), None),
            P(("outer", "inner"), None),
            P(("outer", "inner"), None),
            P(None, ("outer", "inner")),
            P(("outer", "inner")),
        ),
        out_specs=(
            P(("outer", "inner"), None),
            P(("outer", "inner"), None),
            P(("outer", "inner"), None),
        ),
        check_vma=False,
    )
```

profile of v0, /device:TPU:0, one launch (start us, length us, event | category | flops | bytes accessed | tf_op | source)
XLA Modules:
  0.0 232.3 jit_solution(15719814354498268818)
XLA Ops:
  7.2 43.2 %all-gather.2 = s32[32,1,128]{2,1,0:T(1,128)S(1)} all-gather(s32[1,1,128]{2,1,0:T(1,128)} %bitcast.181), channel_id=1, replica_groups=mesh['outer'=4,'inner'=8] {'outer','inner'}, dimensions={0}, use_global_device_ids=true | all-gather | bytes 16896 | tf_op jit(solution)/shard_map/all_gather | solution.py:55
  52.8 7.4 %all-gather.1 = bf16[512,128]{1,0:T(8,128)(2,1)S(1)} all-gather(bf16[128,128]{1,0:T(8,128)(2,1)S(1)} %copy-done.6), channel_id=3, replica_groups=mesh['outer'=4,'inner'=8] {'outer'}, dimensions={0}, use_global_device_ids=true | all-gather | bytes 163840 | tf_op jit(solution)/shard_map/all_gather | solution.py:59
  62.4 8.5 %all-gather = bf16[512,128]{1,0:T(8,128)(2,1)S(1)} all-gather(bf16[128,128]{1,0:T(8,128)(2,1)S(1)} %copy-done.7), channel_id=2, replica_groups=mesh['outer'=4,'inner'=8] {'outer'}, dimensions={0}, use_global_device_ids=true | all-gather | bytes 163840 | tf_op jit(solution)/shard_map/all_gather | solution.py:58
  73.9 93.1 %while.23 = (s32[]{:T(128)}, bf16[4,128,128]{2,1,0:T(8,128)(2,1)S(1)}, bf16[4,128,128]{2,1,0:T(8,128)(2,1)S(1)}, f32[128,4,128]{2,0,1:T(8,128)S(1)}, f32[4,128,1...) while((s32[]{:T(128)}, ...), condition=%wide.region_1.2_spmd, body=%wide.region_0.1_spmd.sunk | while | flops 337641472 | bytes 12069852 | solution.py:81
  74.2 5.9 %collective-permute-done = bf16[4,128,128]{2,1,0:T(8,128)(2,1)S(1)} collective-permute-done((bf16[4,128,128]{2,1,0:T(8,128)(2,1)S(1)}, bf16[4,128,128]{2,1,0:T(8,128)(2,1)S(1)}, u32[]{:S(2)}, u32[]{:S(2)}) %collective-permute-start) | collective-permute-done | bytes 131104 | tf_op jit(solution)/shard_map/while/body/eval_jaxpr/ppermute | solution.py:10
  82.9 1.5 collective-permute-done.2
  84.4 2.8 %collective-permute-done.3 = f32[4,128,128]{2,1,0:T(8,128)S(1)} collective-permute-done((f32[4,128,128]{2,1,0:T(8,128)S(1)}, f32[4,128,128]{2,1,0:T(8,128)S(1)}, u32[]{:S(2)}, u32[]{:S(2)}) %collective-permute-start.3) | collective-permute-done | bytes 262176 | tf_op jit(solution)/shard_map/while/body/eval_jaxpr/ppermute | solution.py:10
  87.6 5.8 %collective-permute-done = bf16[4,128,128]{2,1,0:T(8,128)(2,1)S(1)} collective-permute-done((bf16[4,128,128]{2,1,0:T(8,128)(2,1)S(1)}, bf16[4,128,128]{2,1,0:T(8,128)(2,1)S(1)}, u32[]{:S(2)}, u32[]{:S(2)}) %collective-permute-start) | collective-permute-done | bytes 131104 | tf_op jit(solution)/shard_map/while/body/eval_jaxpr/ppermute | solution.py:10
  96.2 1.5 collective-permute-done.2
  97.7 2.8 %collective-permute-done.3 = f32[4,128,128]{2,1,0:T(8,128)S(1)} collective-permute-done((f32[4,128,128]{2,1,0:T(8,128)S(1)}, f32[4,128,128]{2,1,0:T(8,128)S(1)}, u32[]{:S(2)}, u32[]{:S(2)}) %collective-permute-start.3) | collective-permute-done | bytes 262176 | tf_op jit(solution)/shard_map/while/body/eval_jaxpr/ppermute | solution.py:10
  101.0 5.8 %collective-permute-done = bf16[4,128,128]{2,1,0:T(8,128)(2,1)S(1)} collective-permute-done((bf16[4,128,128]{2,1,0:T(8,128)(2,1)S(1)}, bf16[4,128,128]{2,1,0:T(8,128)(2,1)S(1)}, u32[]{:S(2)}, u32[]{:S(2)}) %collective-permute-start) | collective-permute-done | bytes 131104 | tf_op jit(solution)/shard_map/while/body/eval_jaxpr/ppermute | solution.py:10
  107.1 1.0 collective-permute-done.1
  109.5 1.5 collective-permute-done.2
  111.0 2.8 %collective-permute-done.3 = f32[4,128,128]{2,1,0:T(8,128)S(1)} collective-permute-done((f32[4,128,128]{2,1,0:T(8,128)S(1)}, f32[4,128,128]{2,1,0:T(8,128)S(1)}, u32[]{:S(2)}, u32[]{:S(2)}) %collective-permute-start.3) | collective-permute-done | bytes 262176 | tf_op jit(solution)/shard_map/while/body/eval_jaxpr/ppermute | solution.py:10
  114.3 5.8 %collective-permute-done = bf16[4,128,128]{2,1,0:T(8,128)(2,1)S(1)} collective-permute-done((bf16[4,128,128]{2,1,0:T(8,128)(2,1)S(1)}, bf16[4,128,128]{2,1,0:T(8,128)(2,1)S(1)}, u32[]{:S(2)}, u32[]{:S(2)}) %collective-permute-start) | collective-permute-done | bytes 131104 | tf_op jit(solution)/shard_map/while/body/eval_jaxpr/ppermute | solution.py:10
  122.8 1.5 collective-permute-done.2
  124.3 2.8 %collective-permute-done.3 = f32[4,128,128]{2,1,0:T(8,128)S(1)} collective-permute-done((f32[4,128,128]{2,1,0:T(8,128)S(1)}, f32[4,128,128]{2,1,0:T(8,128)S(1)}, u32[]{:S(2)}, u32[]{:S(2)}) %collective-permute-start.3) | collective-permute-done | bytes 262176 | tf_op jit(solution)/shard_map/while/body/eval_jaxpr/ppermute | solution.py:10
  127.6 5.8 %collective-permute-done = bf16[4,128,128]{2,1,0:T(8,128)(2,1)S(1)} collective-permute-done((bf16[4,128,128]{2,1,0:T(8,128)(2,1)S(1)}, bf16[4,128,128]{2,1,0:T(8,128)(2,1)S(1)}, u32[]{:S(2)}, u32[]{:S(2)}) %collective-permute-start) | collective-permute-done | bytes 131104 | tf_op jit(solution)/shard_map/while/body/eval_jaxpr/ppermute | solution.py:10
  136.1 1.5 collective-permute-done.2
  137.6 2.8 %collective-permute-done.3 = f32[4,128,128]{2,1,0:T(8,128)S(1)} collective-permute-done((f32[4,128,128]{2,1,0:T(8,128)S(1)}, f32[4,128,128]{2,1,0:T(8,128)S(1)}, u32[]{:S(2)}, u32[]{:S(2)}) %collective-permute-start.3) | collective-permute-done | bytes 262176 | tf_op jit(solution)/shard_map/while/body/eval_jaxpr/ppermute | solution.py:10
  140.9 5.8 %collective-permute-done = bf16[4,128,128]{2,1,0:T(8,128)(2,1)S(1)} collective-permute-done((bf16[4,128,128]{2,1,0:T(8,128)(2,1)S(1)}, bf16[4,128,128]{2,1,0:T(8,128)(2,1)S(1)}, u32[]{:S(2)}, u32[]{:S(2)}) %collective-permute-start) | collective-permute-done | bytes 131104 | tf_op jit(solution)/shard_map/while/body/eval_jaxpr/ppermute | solution.py:10
  149.4 1.5 collective-permute-done.2
  150.9 2.8 %collective-permute-done.3 = f32[4,128,128]{2,1,0:T(8,128)S(1)} collective-permute-done((f32[4,128,128]{2,1,0:T(8,128)S(1)}, f32[4,128,128]{2,1,0:T(8,128)S(1)}, u32[]{:S(2)}, u32[]{:S(2)}) %collective-permute-start.3) | collective-permute-done | bytes 262176 | tf_op jit(solution)/shard_map/while/body/eval_jaxpr/ppermute | solution.py:10
  154.2 5.8 %collective-permute-done = bf16[4,128,128]{2,1,0:T(8,128)(2,1)S(1)} collective-permute-done((bf16[4,128,128]{2,1,0:T(8,128)(2,1)S(1)}, bf16[4,128,128]{2,1,0:T(8,128)(2,1)S(1)}, u32[]{:S(2)}, u32[]{:S(2)}) %collective-permute-start) | collective-permute-done | bytes 131104 | tf_op jit(solution)/shard_map/while/body/eval_jaxpr/ppermute | solution.py:10
  162.7 1.5 collective-permute-done.2
  164.2 2.8 %collective-permute-done.3 = f32[4,128,128]{2,1,0:T(8,128)S(1)} collective-permute-done((f32[4,128,128]{2,1,0:T(8,128)S(1)}, f32[4,128,128]{2,1,0:T(8,128)S(1)}, u32[]{:S(2)}, u32[]{:S(2)}) %collective-permute-start.3) | collective-permute-done | bytes 262176 | tf_op jit(solution)/shard_map/while/body/eval_jaxpr/ppermute | solution.py:10
  167.1 7.6 %collective-permute-done.5 = f32[4,128,128]{2,1,0:T(8,128)S(1)} collective-permute-done((f32[4,128,128]{2,1,0:T(8,128)S(1)}, f32[4,128,128]{2,1,0:T(8,128)S(1)}, u32[]{:S(2)}, u32[]{:S(2)}) %collective-permute-start.5) | collective-permute-done | bytes 262176 | tf_op jit(solution)/shard_map/ppermute | solution.py:10
  175.6 7.6 %collective-permute-done.4 = f32[4,128,128]{2,1,0:T(8,128)S(1)} collective-permute-done((f32[4,128,128]{2,1,0:T(8,128)S(1)}, f32[4,128,128]{2,1,0:T(8,128)S(1)}, u32[]{:S(2)}, u32[]{:S(2)}) %collective-permute-start.4) | collective-permute-done | bytes 262176 | tf_op jit(solution)/shard_map/ppermute | solution.py:10
  184.5 12.4 %reduce-scatter.9.cloned.1.call-done = f32[1,128,128]{2,1,0:T(8,128)} async-done(((f32[4,128,128]{2,1,0:T(8,128)}), f32[1,128,128]{2,1,0:T(8,128)}) %reduce-scatter.9.cloned.1.call-update) | async-done | bytes 65552
  196.9 1.5 convert_bitcast_fusion
  198.4 25.6 %reduce-scatter.7.cloned.1.call-done = f32[1,128,128]{2,1,0:T(8,128)} async-done(((f32[4,128,128]{2,1,0:T(8,128)}), f32[1,128,128]{2,1,0:T(8,128)}) %reduce-scatter.7.cloned.1.call-update) | async-done | bytes 65552
  224.0 1.5 fusion.29
  (152 shorter events, 30.3 us)
Async XLA Ops:
  7.2 189.7 %reduce-scatter.9.cloned.1.call-start = ((), (), s32[]{:S(2)}) async-start(), calls=%async_computation.3 | async-start | bytes 327680
  73.9 6.2 %collective-permute-start = (bf16[4,128,128]{2,1,0:T(8,128)(2,1)S(1)}, bf16[4,128,128]{2,1,0:T(8,128)(2,1)S(1)}, u32[]{:S(2)}, u32[]{:S(2)}) collective-permute-start(bf16[4,128,128]{2,1,0:T(8,128)(2,1)S(1)} %get-tuple-element.469), channel_id=1, source_target_pairs={{7,0},{0,1},{1,2},{2,3},{3,4},{4,5},{5,6},{6,7},{15,8},{8,9},{9,10... | collective-permute-start | bytes 393224 | tf_op jit(solution)/shard_map/while/body/eval_jaxpr/ppermute | solution.py:10
  73.9 7.6 %collective-permute-start.1 = (bf16[4,128,128]{2,1,0:T(8,128)(2,1)S(1)}, bf16[4,128,128]{2,1,0:T(8,128)(2,1)S(1)}, u32[]{:S(2)}, u32[]{:S(2)}) collective-permute-start(bf16[4,128,128]{2,1,0:T(8,128)(2,1)S(1)} %get-tuple-element.470), channel_id=1, source_target_pairs={{7,0},{0,1},{1,2},{2,3},{3,4},{4,5},{5,6},{6,7},{15,8},{8,9},{9,10... | collective-permute-start | bytes 393224 | tf_op jit(solution)/shard_map/while/body/eval_jaxpr/ppermute | solution.py:10
  74.0 10.4 %collective-permute-start.2 = (f32[4,128,128]{2,1,0:T(8,128)S(1)}, f32[4,128,128]{2,1,0:T(8,128)S(1)}, u32[]{:S(2)}, u32[]{:S(2)}) collective-permute-start(f32[4,128,128]{2,1,0:T(8,128)S(1)} %get-tuple-element.472), channel_id=1, source_target_pairs={{7,0},{0,1},{1,2},{2,3},{3,4},{4,5},{5,6},{6,7},{15,8},{8,9},{9,10... | collective-permute-start | bytes 786440 | tf_op jit(solution)/shard_map/while/body/eval_jaxpr/ppermute | solution.py:10
  74.0 13.2 %collective-permute-start.3 = (f32[4,128,128]{2,1,0:T(8,128)S(1)}, f32[4,128,128]{2,1,0:T(8,128)S(1)}, u32[]{:S(2)}, u32[]{:S(2)}) collective-permute-start(f32[4,128,128]{2,1,0:T(8,128)S(1)} %get-tuple-element.473), channel_id=1, source_target_pairs={{7,0},{0,1},{1,2},{2,3},{3,4},{4,5},{5,6},{6,7},{15,8},{8,9},{9,10... | collective-permute-start | bytes 786440 | tf_op jit(solution)/shard_map/while/body/eval_jaxpr/ppermute | solution.py:10
  87.2 6.2 %collective-permute-start = (bf16[4,128,128]{2,1,0:T(8,128)(2,1)S(1)}, bf16[4,128,128]{2,1,0:T(8,128)(2,1)S(1)}, u32[]{:S(2)}, u32[]{:S(2)}) collective-permute-start(bf16[4,128,128]{2,1,0:T(8,128)(2,1)S(1)} %get-tuple-element.469), channel_id=1, source_target_pairs={{7,0},{0,1},{1,2},{2,3},{3,4},{4,5},{5,6},{6,7},{15,8},{8,9},{9,10... | collective-permute-start | bytes 393224 | tf_op jit(solution)/shard_map/while/body/eval_jaxpr/ppermute | solution.py:10
  87.3 7.6 %collective-permute-start.1 = (bf16[4,128,128]{2,1,0:T(8,128)(2,1)S(1)}, bf16[4,128,128]{2,1,0:T(8,128)(2,1)S(1)}, u32[]{:S(2)}, u32[]{:S(2)}) collective-permute-start(bf16[4,128,128]{2,1,0:T(8,128)(2,1)S(1)} %get-tuple-element.470), channel_id=1, source_target_pairs={{7,0},{0,1},{1,2},{2,3},{3,4},{4,5},{5,6},{6,7},{15,8},{8,9},{9,10... | collective-permute-start | bytes 393224 | tf_op jit(solution)/shard_map/while/body/eval_jaxpr/ppermute | solution.py:10
  87.3 10.3 %collective-permute-start.2 = (f32[4,128,128]{2,1,0:T(8,128)S(1)}, f32[4,128,128]{2,1,0:T(8,128)S(1)}, u32[]{:S(2)}, u32[]{:S(2)}) collective-permute-start(f32[4,128,128]{2,1,0:T(8,128)S(1)} %get-tuple-element.472), channel_id=1, source_target_pairs={{7,0},{0,1},{1,2},{2,3},{3,4},{4,5},{5,6},{6,7},{15,8},{8,9},{9,10... | collective-permute-start | bytes 786440 | tf_op jit(solution)/shard_map/while/body/eval_jaxpr/ppermute | solution.py:10
  87.4 13.1 %collective-permute-start.3 = (f32[4,128,128]{2,1,0:T(8,128)S(1)}, f32[4,128,128]{2,1,0:T(8,128)S(1)}, u32[]{:S(2)}, u32[]{:S(2)}) collective-permute-start(f32[4,128,128]{2,1,0:T(8,128)S(1)} %get-tuple-element.473), channel_id=1, source_target_pairs={{7,0},{0,1},{1,2},{2,3},{3,4},{4,5},{5,6},{6,7},{15,8},{8,9},{9,10... | collective-permute-start | bytes 786440 | tf_op jit(solution)/shard_map/while/body/eval_jaxpr/ppermute | solution.py:10
  100.5 6.2 %collective-permute-start = (bf16[4,128,128]{2,1,0:T(8,128)(2,1)S(1)}, bf16[4,128,128]{2,1,0:T(8,128)(2,1)S(1)}, u32[]{:S(2)}, u32[]{:S(2)}) collective-permute-start(bf16[4,128,128]{2,1,0:T(8,128)(2,1)S(1)} %get-tuple-element.469), channel_id=1, source_target_pairs={{7,0},{0,1},{1,2},{2,3},{3,4},{4,5},{5,6},{6,7},{15,8},{8,9},{9,10... | collective-permute-start | bytes 393224 | tf_op jit(solution)/shard_map/while/body/eval_jaxpr/ppermute | solution.py:10
  100.6 7.6 %collective-permute-start.1 = (bf16[4,128,128]{2,1,0:T(8,128)(2,1)S(1)}, bf16[4,128,128]{2,1,0:T(8,128)(2,1)S(1)}, u32[]{:S(2)}, u32[]{:S(2)}) collective-permute-start(bf16[4,128,128]{2,1,0:T(8,128)(2,1)S(1)} %get-tuple-element.470), channel_id=1, source_target_pairs={{7,0},{0,1},{1,2},{2,3},{3,4},{4,5},{5,6},{6,7},{15,8},{8,9},{9,10... | collective-permute-start | bytes 393224 | tf_op jit(solution)/shard_map/while/body/eval_jaxpr/ppermute | solution.py:10
  100.6 10.3 %collective-permute-start.2 = (f32[4,128,128]{2,1,0:T(8,128)S(1)}, f32[4,128,128]{2,1,0:T(8,128)S(1)}, u32[]{:S(2)}, u32[]{:S(2)}) collective-permute-start(f32[4,128,128]{2,1,0:T(8,128)S(1)} %get-tuple-element.472), channel_id=1, source_target_pairs={{7,0},{0,1},{1,2},{2,3},{3,4},{4,5},{5,6},{6,7},{15,8},{8,9},{9,10... | collective-permute-start | bytes 786440 | tf_op jit(solution)/shard_map/while/body/eval_jaxpr/ppermute | solution.py:10
  100.7 13.1 %collective-permute-start.3 = (f32[4,128,128]{2,1,0:T(8,128)S(1)}, f32[4,128,128]{2,1,0:T(8,128)S(1)}, u32[]{:S(2)}, u32[]{:S(2)}) collective-permute-start(f32[4,128,128]{2,1,0:T(8,128)S(1)} %get-tuple-element.473), channel_id=1, source_target_pairs={{7,0},{0,1},{1,2},{2,3},{3,4},{4,5},{5,6},{6,7},{15,8},{8,9},{9,10... | collective-permute-start | bytes 786440 | tf_op jit(solution)/shard_map/while/body/eval_jaxpr/ppermute | solution.py:10
  113.8 6.2 %collective-permute-start = (bf16[4,128,128]{2,1,0:T(8,128)(2,1)S(1)}, bf16[4,128,128]{2,1,0:T(8,128)(2,1)S(1)}, u32[]{:S(2)}, u32[]{:S(2)}) collective-permute-start(bf16[4,128,128]{2,1,0:T(8,128)(2,1)S(1)} %get-tuple-element.469), channel_id=1, source_target_pairs={{7,0},{0,1},{1,2},{2,3},{3,4},{4,5},{5,6},{6,7},{15,8},{8,9},{9,10... | collective-permute-start | bytes 393224 | tf_op jit(solution)/shard_map/while/body/eval_jaxpr/ppermute | solution.py:10
  113.9 7.6 %collective-permute-start.1 = (bf16[4,128,128]{2,1,0:T(8,128)(2,1)S(1)}, bf16[4,128,128]{2,1,0:T(8,128)(2,1)S(1)}, u32[]{:S(2)}, u32[]{:S(2)}) collective-permute-start(bf16[4,128,128]{2,1,0:T(8,128)(2,1)S(1)} %get-tuple-element.470), channel_id=1, source_target_pairs={{7,0},{0,1},{1,2},{2,3},{3,4},{4,5},{5,6},{6,7},{15,8},{8,9},{9,10... | collective-permute-start | bytes 393224 | tf_op jit(solution)/shard_map/while/body/eval_jaxpr/ppermute | solution.py:10
  114.0 10.3 %collective-permute-start.2 = (f32[4,128,128]{2,1,0:T(8,128)S(1)}, f32[4,128,128]{2,1,0:T(8,128)S(1)}, u32[]{:S(2)}, u32[]{:S(2)}) collective-permute-start(f32[4,128,128]{2,1,0:T(8,128)S(1)} %get-tuple-element.472), channel_id=1, source_target_pairs={{7,0},{0,1},{1,2},{2,3},{3,4},{4,5},{5,6},{6,7},{15,8},{8,9},{9,10... | collective-permute-start | bytes 786440 | tf_op jit(solution)/shard_map/while/body/eval_jaxpr/ppermute | solution.py:10
  114.0 13.1 %collective-permute-start.3 = (f32[4,128,128]{2,1,0:T(8,128)S(1)}, f32[4,128,128]{2,1,0:T(8,128)S(1)}, u32[]{:S(2)}, u32[]{:S(2)}) collective-permute-start(f32[4,128,128]{2,1,0:T(8,128)S(1)} %get-tuple-element.473), channel_id=1, source_target_pairs={{7,0},{0,1},{1,2},{2,3},{3,4},{4,5},{5,6},{6,7},{15,8},{8,9},{9,10... | collective-permute-start | bytes 786440 | tf_op jit(solution)/shard_map/while/body/eval_jaxpr/ppermute | solution.py:10
  127.1 6.2 %collective-permute-start = (bf16[4,128,128]{2,1,0:T(8,128)(2,1)S(1)}, bf16[4,128,128]{2,1,0:T(8,128)(2,1)S(1)}, u32[]{:S(2)}, u32[]{:S(2)}) collective-permute-start(bf16[4,128,128]{2,1,0:T(8,128)(2,1)S(1)} %get-tuple-element.469), channel_id=1, source_target_pairs={{7,0},{0,1},{1,2},{2,3},{3,4},{4,5},{5,6},{6,7},{15,8},{8,9},{9,10... | collective-permute-start | bytes 393224 | tf_op jit(solution)/shard_map/while/body/eval_jaxpr/ppermute | solution.py:10
  127.2 7.6 %collective-permute-start.1 = (bf16[4,128,128]{2,1,0:T(8,128)(2,1)S(1)}, bf16[4,128,128]{2,1,0:T(8,128)(2,1)S(1)}, u32[]{:S(2)}, u32[]{:S(2)}) collective-permute-start(bf16[4,128,128]{2,1,0:T(8,128)(2,1)S(1)} %get-tuple-element.470), channel_id=1, source_target_pairs={{7,0},{0,1},{1,2},{2,3},{3,4},{4,5},{5,6},{6,7},{15,8},{8,9},{9,10... | collective-permute-start | bytes 393224 | tf_op jit(solution)/shard_map/while/body/eval_jaxpr/ppermute | solution.py:10
  127.3 10.3 %collective-permute-start.2 = (f32[4,128,128]{2,1,0:T(8,128)S(1)}, f32[4,128,128]{2,1,0:T(8,128)S(1)}, u32[]{:S(2)}, u32[]{:S(2)}) collective-permute-start(f32[4,128,128]{2,1,0:T(8,128)S(1)} %get-tuple-element.472), channel_id=1, source_target_pairs={{7,0},{0,1},{1,2},{2,3},{3,4},{4,5},{5,6},{6,7},{15,8},{8,9},{9,10... | collective-permute-start | bytes 786440 | tf_op jit(solution)/shard_map/while/body/eval_jaxpr/ppermute | solution.py:10
  127.3 13.1 %collective-permute-start.3 = (f32[4,128,128]{2,1,0:T(8,128)S(1)}, f32[4,128,128]{2,1,0:T(8,128)S(1)}, u32[]{:S(2)}, u32[]{:S(2)}) collective-permute-start(f32[4,128,128]{2,1,0:T(8,128)S(1)} %get-tuple-element.473), channel_id=1, source_target_pairs={{7,0},{0,1},{1,2},{2,3},{3,4},{4,5},{5,6},{6,7},{15,8},{8,9},{9,10... | collective-permute-start | bytes 786440 | tf_op jit(solution)/shard_map/while/body/eval_jaxpr/ppermute | solution.py:10
  140.4 6.2 %collective-permute-start = (bf16[4,128,128]{2,1,0:T(8,128)(2,1)S(1)}, bf16[4,128,128]{2,1,0:T(8,128)(2,1)S(1)}, u32[]{:S(2)}, u32[]{:S(2)}) collective-permute-start(bf16[4,128,128]{2,1,0:T(8,128)(2,1)S(1)} %get-tuple-element.469), channel_id=1, source_target_pairs={{7,0},{0,1},{1,2},{2,3},{3,4},{4,5},{5,6},{6,7},{15,8},{8,9},{9,10... | collective-permute-start | bytes 393224 | tf_op jit(solution)/shard_map/while/body/eval_jaxpr/ppermute | solution.py:10
  140.5 7.6 %collective-permute-start.1 = (bf16[4,128,128]{2,1,0:T(8,128)(2,1)S(1)}, bf16[4,128,128]{2,1,0:T(8,128)(2,1)S(1)}, u32[]{:S(2)}, u32[]{:S(2)}) collective-permute-start(bf16[4,128,128]{2,1,0:T(8,128)(2,1)S(1)} %get-tuple-element.470), channel_id=1, source_target_pairs={{7,0},{0,1},{1,2},{2,3},{3,4},{4,5},{5,6},{6,7},{15,8},{8,9},{9,10... | collective-permute-start | bytes 393224 | tf_op jit(solution)/shard_map/while/body/eval_jaxpr/ppermute | solution.py:10
  140.6 10.3 %collective-permute-start.2 = (f32[4,128,128]{2,1,0:T(8,128)S(1)}, f32[4,128,128]{2,1,0:T(8,128)S(1)}, u32[]{:S(2)}, u32[]{:S(2)}) collective-permute-start(f32[4,128,128]{2,1,0:T(8,128)S(1)} %get-tuple-element.472), channel_id=1, source_target_pairs={{7,0},{0,1},{1,2},{2,3},{3,4},{4,5},{5,6},{6,7},{15,8},{8,9},{9,10... | collective-permute-start | bytes 786440 | tf_op jit(solution)/shard_map/while/body/eval_jaxpr/ppermute | solution.py:10
  140.6 13.1 %collective-permute-start.3 = (f32[4,128,128]{2,1,0:T(8,128)S(1)}, f32[4,128,128]{2,1,0:T(8,128)S(1)}, u32[]{:S(2)}, u32[]{:S(2)}) collective-permute-start(f32[4,128,128]{2,1,0:T(8,128)S(1)} %get-tuple-element.473), channel_id=1, source_target_pairs={{7,0},{0,1},{1,2},{2,3},{3,4},{4,5},{5,6},{6,7},{15,8},{8,9},{9,10... | collective-permute-start | bytes 786440 | tf_op jit(solution)/shard_map/while/body/eval_jaxpr/ppermute | solution.py:10
  153.8 6.2 %collective-permute-start = (bf16[4,128,128]{2,1,0:T(8,128)(2,1)S(1)}, bf16[4,128,128]{2,1,0:T(8,128)(2,1)S(1)}, u32[]{:S(2)}, u32[]{:S(2)}) collective-permute-start(bf16[4,128,128]{2,1,0:T(8,128)(2,1)S(1)} %get-tuple-element.469), channel_id=1, source_target_pairs={{7,0},{0,1},{1,2},{2,3},{3,4},{4,5},{5,6},{6,7},{15,8},{8,9},{9,10... | collective-permute-start | bytes 393224 | tf_op jit(solution)/shard_map/while/body/eval_jaxpr/ppermute | solution.py:10
  153.8 7.6 %collective-permute-start.1 = (bf16[4,128,128]{2,1,0:T(8,128)(2,1)S(1)}, bf16[4,128,128]{2,1,0:T(8,128)(2,1)S(1)}, u32[]{:S(2)}, u32[]{:S(2)}) collective-permute-start(bf16[4,128,128]{2,1,0:T(8,128)(2,1)S(1)} %get-tuple-element.470), channel_id=1, source_target_pairs={{7,0},{0,1},{1,2},{2,3},{3,4},{4,5},{5,6},{6,7},{15,8},{8,9},{9,10... | collective-permute-start | bytes 393224 | tf_op jit(solution)/shard_map/while/body/eval_jaxpr/ppermute | solution.py:10
  153.9 10.3 %collective-permute-start.2 = (f32[4,128,128]{2,1,0:T(8,128)S(1)}, f32[4,128,128]{2,1,0:T(8,128)S(1)}, u32[]{:S(2)}, u32[]{:S(2)}) collective-permute-start(f32[4,128,128]{2,1,0:T(8,128)S(1)} %get-tuple-element.472), channel_id=1, source_target_pairs={{7,0},{0,1},{1,2},{2,3},{3,4},{4,5},{5,6},{6,7},{15,8},{8,9},{9,10... | collective-permute-start | bytes 786440 | tf_op jit(solution)/shard_map/while/body/eval_jaxpr/ppermute | solution.py:10
  153.9 13.1 %collective-permute-start.3 = (f32[4,128,128]{2,1,0:T(8,128)S(1)}, f32[4,128,128]{2,1,0:T(8,128)S(1)}, u32[]{:S(2)}, u32[]{:S(2)}) collective-permute-start(f32[4,128,128]{2,1,0:T(8,128)S(1)} %get-tuple-element.473), channel_id=1, source_target_pairs={{7,0},{0,1},{1,2},{2,3},{3,4},{4,5},{5,6},{6,7},{15,8},{8,9},{9,10... | collective-permute-start | bytes 786440 | tf_op jit(solution)/shard_map/while/body/eval_jaxpr/ppermute | solution.py:10
  167.1 7.6 %collective-permute-start.5 = (f32[4,128,128]{2,1,0:T(8,128)S(1)}, f32[4,128,128]{2,1,0:T(8,128)S(1)}, u32[]{:S(2)}, u32[]{:S(2)}) collective-permute-start(f32[4,128,128]{2,1,0:T(8,128)S(1)} %get-tuple-element.316), channel_id=1, source_target_pairs={{7,0},{0,1},{1,2},{2,3},{3,4},{4,5},{5,6},{6,7},{15,8},{8,9},{9,10... | collective-permute-start | bytes 786440 | tf_op jit(solution)/shard_map/ppermute | solution.py:10
  175.4 48.6 %reduce-scatter.7.cloned.1.call-start = ((), (), s32[]{:S(2)}) async-start(), calls=%async_computation.2 | async-start | bytes 327680
  175.5 7.6 %collective-permute-start.4 = (f32[4,128,128]{2,1,0:T(8,128)S(1)}, f32[4,128,128]{2,1,0:T(8,128)S(1)}, u32[]{:S(2)}, u32[]{:S(2)}) collective-permute-start(f32[4,128,128]{2,1,0:T(8,128)S(1)} %get-tuple-element.315), channel_id=1, source_target_pairs={{7,0},{0,1},{1,2},{2,3},{3,4},{4,5},{5,6},{6,7},{15,8},{8,9},{9,10... | collective-permute-start | bytes 786440 | tf_op jit(solution)/shard_map/ppermute | solution.py:10
  (9 other events, 59.1 us)
Sparse Core Ops, SparseCore 0:
  175.6 21.3 reduce-scatter.8
  199.9 24.0 reduce-scatter.6
where the time goes:
time: 233 us; the launch traced here: 232 us
  waiting for transfers between devices  131 us (56%)
  blocking collectives  59.1 us (25%)
  between operations  14.2 us (6%)
  matrix products  13.1 us (6%)
  other arithmetic  6.74 us (3%)
  local copies, waits for them, and re-layouts  5.41 us (2%)
    ppermute x30, waiting for transfers between devices, passed_along(): return lax.ppermute(block, axis, route)  93.1 us
    all_gather x1, blocking collectives, on_device(): pos_all = lax.all_gather(positions, ('outer', 'inner'), axis=0, tiled=True)  43.2 us
    unnamed x4, waiting for transfers between devices  38 us
    all_gather x1, blocking collectives, on_device(): lax.all_gather(key[None], 'outer', axis=0, tiled=True)  8.46 us
    all_gather x1, blocking collectives, on_device(): lax.all_gather(value[None], 'outer', axis=0, tiled=True)  7.45 us
    unnamed x21, local copies, waits for them, and re-layouts  4.83 us
  transfers between devices with their start and end apart: 32, of which 32 were waited for; matrix products, arithmetic and copies ran while one was open for 6% of the time, Pallas kernels for 0%

commit v1 on v0

v1 whole, which is shorter than its diff:
```python
import functools
import math

import jax
import jax.numpy as jnp
from jax import lax
from jax.experimental import pallas as pl
from jax.experimental.pallas import tpu as pltpu
from jax.sharding import PartitionSpec as P

BF = jnp.bfloat16
F32 = jnp.float32
RUN = 64
LOG2E = math.log2(math.e)
VMEM = pl.BlockSpec(memory_space=pltpu.VMEM)
NT = (((1,), (1,)), ((), ()))


def swapped(block, axis, mask):
    pairs = [(i, i ^ mask) for i in range(lax.axis_size(axis))]
    return lax.ppermute(block, axis, pairs)


def three_parts(x):
    hi = x.astype(BF)
    rest = x - hi.astype(F32)
    mid = rest.astype(BF)
    low = (rest - mid.astype(F32)).astype(BF)
    return [hi, mid, low]


def dot(a, b, dims=(((1,), (0,)), ((), ()))):
    return lax.dot_general(a, b, dims, preferred_element_type=F32)


def pack_kernel(q_ref, k_ref, v_ref, o_ref, g_ref, lse_ref, pos_ref, x_ref, kv_ref):
    rows, width = k_ref.shape
    heads = q_ref.shape[1] // width
    ones = jnp.ones((8, width), BF)
    deltas = []
    for h in range(heads):
        cols = slice(h * width, (h + 1) * width)
        q = q_ref[:, cols]
        g = g_ref[:, cols]
        x_ref[h * rows : (h + 1) * rows, :] = q
        x_ref[(heads + h) * rows : (heads + h + 1) * rows, :] = g
        prod = g.astype(F32) * o_ref[:, cols].astype(F32)
        hi = prod.astype(BF)
        low = (prod - hi.astype(F32)).astype(BF)
        deltas.append((dot(ones, hi, NT) + dot(ones, low, NT))[:1])
    run = (pos_ref[...] // RUN).astype(F32)
    extra = (
        three_parts(lse_ref[...] * LOG2E)
        + three_parts(jnp.concatenate(deltas, axis=0))
        + [run.astype(BF), jnp.zeros((32 - 6 * heads - 1, rows), BF)]
    )
    x_ref[2 * heads * rows :, :] = jnp.concatenate([e.astype(F32) for e in extra], axis=0).astype(BF)
    kv_ref[:rows, :] = k_ref[...]
    kv_ref[rows : 2 * rows, :] = v_ref[...]
    lane = lax.broadcasted_iota(jnp.int32, run.shape, 1)
    ids = [
        jnp.max(jnp.where(lane == r * RUN, run, 0.0), axis=1, keepdims=True)
        for r in range(rows // RUN)
    ]
    wide = [jnp.broadcast_to(i, (1, width)) for i in ids]
    wide.append(jnp.zeros((16 - len(ids), width), F32))
    kv_ref[2 * rows :, :] = jnp.concatenate(wide, axis=0).astype(BF)


def core_kernel(nq, nk, rows, heads, scale, *refs):
    x_refs = refs[:nq]
    kv_refs = refs[nq : nq + nk]
    dq_own, dq_far, dkv_own, dkv_sib = refs[nq + nk : nq + nk + 4]
    q_s, g_s, k_s, kt_s, v_s, lse_s, del_s, run_s, krun_s, dqt_s, dk_s, dv_s = refs[nq + nk + 4 :]
    width = 128
    hr = heads * rows
    chunk = 2 * rows
    n_chunks = nk // 2
    runs = chunk // RUN
    for b in range(nq):
        q_s[b] = x_refs[b][:hr, :]
        g_s[b] = x_refs[b][hr : 2 * hr, :]
        e = x_refs[b][2 * hr :, :].astype(F32)
        lse = e[0:heads] + e[heads : 2 * heads] + e[2 * heads : 3 * heads]
        delta = e[3 * heads : 4 * heads] + e[4 * heads : 5 * heads] + e[5 * heads : 6 * heads]
        run = e[6 * heads : 6 * heads + 1]
        for h in range(heads):
            cols = slice(h * rows, (h + 1) * rows)
            lse_s[b, :, cols] = jnp.broadcast_to(lse[h : h + 1], (8, rows))
            del_s[b, :, cols] = jnp.broadcast_to(delta[h : h + 1], (8, rows))
            run_s[b, :, cols] = jnp.broadcast_to(run, (8, rows))
    for j in range(nk):
        at = slice(j * rows, (j + 1) * rows)
        k = kv_refs[j][:rows, :]
        k_s[at, :] = k
        v_s[at, :] = kv_refs[j][rows : 2 * rows, :]
        kt_s[:, at] = k.astype(F32).T.astype(BF)
        e = kv_refs[j][2 * rows :, :].astype(F32)
        for r in range(rows // RUN):
            krun_s[j * (rows // RUN) + r] = jnp.broadcast_to(e[r : r + 1], (8, width))
    dqt_s[...] = jnp.zeros_like(dqt_s)
    dk_s[...] = jnp.zeros_like(dk_s)
    dv_s[...] = jnp.zeros_like(dv_s)

    def unit(b, c, own):
        at = pl.ds(pl.multiple_of(c * chunk, chunk), chunk)
        k, v = k_s[at, :], v_s[at, :]
        q, g = q_s[b], g_s[b]
        st = dot(k, q, NT)
        dpt = dot(v, g, NT)
        lse = lse_s[b]
        delta = del_s[b]
        qrun = run_s[b]
        p_parts, d_parts = [], []
        for r in range(runs):
            sl = slice(r * RUN, (r + 1) * RUN)
            kr = krun_s[c * runs + r]
            kr = jnp.concatenate([kr] * (hr // width), axis=1)
            row = jnp.where(kr <= qrun, lse, 1e30)[:1]
            arg = st[sl] * (scale * LOG2E) - row
            if own and r < rows // RUN:
                shape = (RUN, hr)
                i = lax.rem(lax.broadcasted_iota(jnp.int32, shape, 1), rows)
                j = lax.broadcasted_iota(jnp.int32, shape, 0) + r * RUN
                same = (i >= r * RUN) & (i < (r + 1) * RUN)
                arg = jnp.where(same & (j > i), -1e30, arg)
            p = jnp.exp2(arg)
            p_parts.append(p.astype(BF))
            d_parts.append((p * (dpt[sl] - delta[:1])).astype(BF))
        p = jnp.concatenate(p_parts, axis=0)
        d = jnp.concatenate(d_parts, axis=0)
        dv_s[at, :] += dot(p, g)
        dk_s[at, :] += dot(d, q)
        dqt_s[b] += dot(kt_s[:, at], d)

    unit(0, 0, True)

    def body(n, carry):
        unit(n // n_chunks, n % n_chunks, False)
        return carry

    lax.fori_loop(1, nq * n_chunks, body, 0)
    dq_own[...] = dqt_s[0]
    for b in range(1, nq):
        dq_far[b - 1] = dqt_s[b].astype(BF)
    for c in range(n_chunks):
        here = slice(c * chunk, c * chunk + rows)
        there = slice(c * chunk + rows, (c + 1) * chunk)
        dkv_own[c, :rows, :] = dk_s[here, :]
        dkv_own[c, rows:, :] = dv_s[here, :]
        dkv_sib[c, :rows, :] = dk_s[there, :].astype(BF)
        dkv_sib[c, rows:, :] = dv_s[there, :].astype(BF)


def final_kernel(nq, nz, rows, heads, scale, dq_own, dkv_own, *refs):
    dq_refs = refs[: nq - 1]
    dkv_refs = refs[nq - 1 : nq - 1 + nz - 1]
    gq_ref, gk_ref, gv_ref = refs[nq - 1 + nz - 1 :]
    dq = dq_own[...]
    for r in dq_refs:
        dq = dq + r[...].astype(F32)
    for h in range(heads):
        part = dq[:, h * rows : (h + 1) * rows]
        gq_ref[:, h * 128 : (h + 1) * 128] = (scale * part).T.astype(BF)
    dkv = dkv_own[...]
    for r in dkv_refs:
        dkv = dkv + r[...].astype(F32)
    gk_ref[...] = (scale * dkv[:rows]).astype(BF)
    gv_ref[...] = dkv[rows:].astype(BF)


def on_device(query, key, value, out, grad_out, lse, positions):
    rows, width = key.shape
    heads = query.shape[1] // width
    hr = heads * rows
    scale = width ** (-0.5)
    nq = lax.axis_size("outer")
    nk = lax.axis_size("inner")
    nz = nk // 2
    sds = jax.ShapeDtypeStruct
    x, kv = pl.pallas_call(
        pack_kernel,
        out_shape=(sds((2 * hr + 32, width), BF), sds((2 * rows + 16, width), BF)),
        in_specs=[VMEM] * 7,
        out_specs=(VMEM, VMEM),
    )(query, key, value, out, grad_out, lse, positions[None, :])

    xs = [x] + [swapped(x, "outer", s) for s in range(1, nq)]
    mine = [kv] + [swapped(kv, "inner", 2 * s) for s in range(1, nz)]
    kvs = []
    for block in mine:
        kvs += [block, swapped(block, "inner", 1)]

    dq_own, dq_far, dkv_own, dkv_sib = pl.pallas_call(
        functools.partial(core_kernel, nq, nk, rows, heads, scale),
        out_shape=(
            sds((width, hr), F32),
            sds((nq - 1, width, hr), BF),
            sds((nz, 2 * rows, width), F32),
            sds((nz, 2 * rows, width), BF),
        ),
        in_specs=[VMEM] * (nq + nk),
        out_specs=(VMEM,) * 4,
        scratch_shapes=[
            pltpu.VMEM((nq, hr, width), BF),
            pltpu.VMEM((nq, hr, width), BF),
            pltpu.VMEM((nk * rows, width), BF),
            pltpu.VMEM((width, nk * rows), BF),
            pltpu.VMEM((nk * rows, width), BF),
            pltpu.VMEM((nq, 8, hr), F32),
            pltpu.VMEM((nq, 8, hr), F32),
            pltpu.VMEM((nq, 8, hr), F32),
            pltpu.VMEM((nk * rows // RUN, 8, width), F32),
            pltpu.VMEM((nq, width, hr), F32),
            pltpu.VMEM((nk * rows, width), F32),
            pltpu.VMEM((nk * rows, width), F32),
        ],
        compiler_params=pltpu.CompilerParams(vmem_limit_bytes=40 * 1024 * 1024),
    )(*xs, *kvs)

    dq_got = [swapped(dq_far[s - 1], "outer", s) for s in range(1, nq)]
    sib = swapped(dkv_sib, "inner", 1)
    total = dkv_own + sib.astype(F32)
    dkv_got = [swapped(total[s].astype(BF), "inner", 2 * s) for s in range(1, nz)]

    return pl.pallas_call(
        functools.partial(final_kernel, nq, nz, rows, heads, scale),
        out_shape=(sds((rows, heads * width), BF), sds((rows, width), BF), sds((rows, width), BF)),
        in_specs=[VMEM] * (2 + nq - 1 + nz - 1),
        out_specs=(VMEM,) * 3,
    )(dq_own, total[0], *dq_got, *dkv_got)


def solution(mesh):
    tokens = P(("outer", "inner"), None)
    return jax.shard_map(
        on_device,
        mesh=mesh,
        in_specs=(tokens,) * 5 + (P(None, ("outer", "inner")), P(("outer", "inner"))),
        out_specs=(tokens,) * 3,
        check_vma=False,
    )
```

time: 233 us -> 47.8 us (0.21)
  waiting for transfers between devices: 131 us -> 15.5 us
  blocking collectives: 59.1 us -> 0 us
  starting transfers between devices: 1.65 us -> 15.5 us
  between operations: 14.2 us -> 0.71 us
  matrix products: 13.1 us -> 0 us
  Pallas kernels: 0 us -> 11.9 us
  other arithmetic: 6.74 us -> 0.08 us
    ppermute x30 -> x17, waiting for transfers between devices: 93.1 us -> 15.5 us  [swapped(): return lax.ppermute(block, axis, pairs)]
    all_gather x3 -> x0, blocking collectives: 59.1 us -> none  [the longest x1 43.2 us: on_device(): pos_all = lax.all_gather(positions, ('outer', 'inner'), axis=0, tiled=True)]
    unnamed x4 -> x0, waiting for transfers between devices: 38 us -> none
    ppermute x30 -> x17, starting transfers between devices: 1.57 us -> 15.5 us  [swapped(): return lax.ppermute(block, axis, pairs)]
    dot_general x40 -> x0, matrix products: 13.1 us -> none  [the longest x8 3.07 us: block_terms(): jnp.einsum('hrk,kd->rhd', dscores, keys, preferred_element_type=jnp.float32)]
    pallas_call x0 -> x3, Pallas kernels: none -> 11.9 us  [the longest x1 7.9 us: on_device(): pl.pallas_call(functools.partial(core_kernel, nq, nk, rows, heads, scale)...]
    convert_element_type x3 -> x0, other arithmetic: 3.59 us -> none  [the longest x1 1.46 us: on_device(): (scale * sum_k[0]).astype(jnp.bfloat16)]
    le x9 -> x0, other arithmetic: 2.52 us -> none  [block_terms(): allowed = key_pos[None, None, :] <= my_pos[None, :, None]]
  transfers between devices with their start and end apart: 32 -> 17, of which waited for: 32 -> 11; matrix products, arithmetic and copies ran while one was open for 6% -> 2% of each run, Pallas kernels for 0% -> 0%
where the time goes in v1:
time: 47.8 us; the launch traced here: 47.5 us
  starting transfers between devices  15.5 us (32%)
  waiting for transfers between devices  15.5 us (32%)
  Pallas kernels  11.9 us (25%)
  local copies, waits for them, and re-layouts  3.73 us (8%)
  between operations  0.71 us (1%)
    ppermute x17, waiting for transfers between devices, swapped(): return lax.ppermute(block, axis, pairs)  15.5 us
    ppermute x17, starting transfers between devices, swapped(): return lax.ppermute(block, axis, pairs)  15.5 us
    pallas_call x1, Pallas kernels, on_device(): pl.pallas_call(functools.partial(core_kernel, nq, nk, rows, heads, scale)...  7.9 us
    unnamed x18, local copies, waits for them, and re-layouts  3.03 us
    pallas_call x1, Pallas kernels, on_device(): pl.pallas_call(pack_kernel, out_shape=(sds((2 * hr + 32, width), BF), sds...  2.06 us
    pallas_call x1, Pallas kernels, on_device(): pl.pallas_call(functools.partial(final_kernel, nq, nz, rows, heads, scale...  1.98 us
  transfers between devices with their start and end apart: 17, of which 11 were waited for; matrix products, arithmetic and copies ran while one was open for 2% of the time, Pallas kernels for 0%

profile of v1, /device:TPU:0, one launch (start us, length us, event | category | flops | bytes accessed | tf_op | source)
XLA Modules:
  0.0 47.5 jit_solution(17778053559453202132)
XLA Ops:
  0.6 2.1 %shard_map.94 = (bf16[1056,128]{1,0:T(8,128)(2,1)}, bf16[272,128]{1,0:T(8,128)(2,1)}) custom-call(bf16[128,512]{1,0:T(8,128)(2,1)} %q_ref.1, bf16[128,128]{1,0:T(8,128)(2,1)} %k_ref.1, bf16[128,128]{1,0:T(8,128)(2,1)} %v_ref.1, bf16[128,512]{1,0:T(8,128)(2,1)} %o_ref.1, bf16[128,512]{1,0:T(8,128)(2,1)} %g_ref.1, f32[4,128]{1,0:T(4,128)} %lse_ref.1, ...), custom_call_target="tpu_custom_call" | custom-call | tf_op jit(solution)/shard_map/pallas_call | solution.py:181
  2.7 5.0 %collective-permute-start.8 = (bf16[272,128]{1,0:T(8,128)(2,1)}, bf16[272,128]{1,0:T(8,128)(2,1)S(1)}, u32[]{:S(2)}, u32[]{:S(2)}) collective-permute-start(bf16[272,128]{1,0:T(8,128)(2,1)} %get-tuple-element.10.refs_4_), channel_id=1, source_target_pairs={{0,6},{1,7},{2,4},{3,5},{4,2},{5,3},{6,0},{7,1},{8,14},{9,15},{10,... | collective-permute-start | bytes 208904 | tf_op jit(solution)/shard_map/ppermute | solution.py:21
  7.7 2.4 %collective-permute-start.2 = (bf16[1056,128]{1,0:T(8,128)(2,1)}, bf16[1056,128]{1,0:T(8,128)(2,1)S(1)}, u32[]{:S(2)}, u32[]{:S(2)}) collective-permute-start(bf16[1056,128]{1,0:T(8,128)(2,1)} %get-tuple-element.9.refs_0_), channel_id=1, source_target_pairs={{0,24},{8,16},{16,8},{24,0},{1,25},{9,17},{17,9},{25,1},{2,26},{10... | collective-permute-start | bytes 811016 | tf_op jit(solution)/shard_map/ppermute | solution.py:21
  10.2 0.5 %collective-permute-start.1 = (bf16[1056,128]{1,0:T(8,128)(2,1)}, bf16[1056,128]{1,0:T(8,128)(2,1)S(1)}, u32[]{:S(2)}, u32[]{:S(2)}) collective-permute-start(bf16[1056,128]{1,0:T(8,128)(2,1)} %get-tuple-element.9.refs_0_), channel_id=1, source_target_pairs={{0,16},{8,24},{16,0},{24,8},{1,17},{9,25},{17,1},{25,9},{2,18},{10... | collective-permute-start | bytes 811016 | tf_op jit(solution)/shard_map/ppermute | solution.py:21
  10.7 0.5 %collective-permute-start = (bf16[1056,128]{1,0:T(8,128)(2,1)}, bf16[1056,128]{1,0:T(8,128)(2,1)S(1)}, u32[]{:S(2)}, u32[]{:S(2)}) collective-permute-start(bf16[1056,128]{1,0:T(8,128)(2,1)} %get-tuple-element.9.refs_0_), channel_id=1, source_target_pairs={{0,8},{8,0},{16,24},{24,16},{1,9},{9,1},{17,25},{25,17},{2,10},{10... | collective-permute-start | bytes 811016 | tf_op jit(solution)/shard_map/ppermute | solution.py:21
  11.2 0.6 %collective-permute-start.4 = (bf16[272,128]{1,0:T(8,128)(2,1)}, bf16[272,128]{1,0:T(8,128)(2,1)S(1)}, u32[]{:S(2)}, u32[]{:S(2)}) collective-permute-start(bf16[272,128]{1,0:T(8,128)(2,1)} %get-tuple-element.10.refs_4_), channel_id=1, source_target_pairs={{0,2},{1,3},{2,0},{3,1},{4,6},{5,7},{6,4},{7,5},{8,10},{9,11},{10,... | collective-permute-start | bytes 208904 | tf_op jit(solution)/shard_map/ppermute | solution.py:21
  11.8 5.1 %collective-permute-done.6.refs_8_ = bf16[272,128]{1,0:T(8,128)(2,1)S(1)} collective-permute-done((bf16[272,128]{1,0:T(8,128)(2,1)}, bf16[272,128]{1,0:T(8,128)(2,1)S(1)}, u32[]{:S(2)}, u32[]{:S(2)}) %collective-permute-start.6) | collective-permute-done | bytes 69664 | tf_op jit(solution)/shard_map/ppermute | solution.py:21
  16.9 0.5 %collective-permute-start.9 = (bf16[272,128]{1,0:T(8,128)(2,1)S(1)}, bf16[272,128]{1,0:T(8,128)(2,1)S(1)}, u32[]{:S(2)}, u32[]{:S(2)}) collective-permute-start(bf16[272,128]{1,0:T(8,128)(2,1)S(1)} %collective-permute-done.8.refs_10_), channel_id=1, source_target_pairs={{0,1},{1,0},{2,3},{3,2},{4,5},{5,4},{6,7},{7,6},{8,9},{9,8},{10,11... | collective-permute-start | bytes 208904 | tf_op jit(solution)/shard_map/ppermute | solution.py:21
  17.4 1.0 %collective-permute-done.3.refs_5_ = bf16[272,128]{1,0:T(8,128)(2,1)S(1)} collective-permute-done((bf16[272,128]{1,0:T(8,128)(2,1)}, bf16[272,128]{1,0:T(8,128)(2,1)S(1)}, u32[]{:S(2)}, u32[]{:S(2)}) %collective-permute-start.3) | collective-permute-done | bytes 69664 | tf_op jit(solution)/shard_map/ppermute | solution.py:21
  18.4 0.1 collective-permute-start.7
  18.5 0.4 collective-permute-start.5
  18.9 0.7 %collective-permute-done.7.refs_9_ = bf16[272,128]{1,0:T(8,128)(2,1)S(1)} collective-permute-done((bf16[272,128]{1,0:T(8,128)(2,1)S(1)}, bf16[272,128]{1,0:T(8,128)(2,1)S(1)}, u32[]{:S(2)}, u32[]{:S(2)}) %collective-permute-start.7) | collective-permute-done | bytes 69664 | tf_op jit(solution)/shard_map/ppermute | solution.py:21
  19.6 0.2 collective-permute-done.5.refs_7_
  19.8 2.8 %collective-permute-done.1.refs_2_ = bf16[1056,128]{1,0:T(8,128)(2,1)S(1)} collective-permute-done((bf16[1056,128]{1,0:T(8,128)(2,1)}, bf16[1056,128]{1,0:T(8,128)(2,1)S(1)}, u32[]{:S(2)}, u32[]{:S(2)}) %collective-permute-start.1) | collective-permute-done | bytes 270368 | tf_op jit(solution)/shard_map/ppermute | solution.py:21
  22.7 1.0 %copy-done = bf16[1056,128]{1,0:T(8,128)(2,1)S(1)} copy-done((bf16[1056,128]{1,0:T(8,128)(2,1)S(1)}, bf16[1056,128]{1,0:T(8,128)(2,1)}, u32[]{:S(2)}) %copy-start) | copy-done | bytes 270360
  23.6 0.9 %copy-done.2 = bf16[272,128]{1,0:T(8,128)(2,1)S(1)} copy-done((bf16[272,128]{1,0:T(8,128)(2,1)S(1)}, bf16[272,128]{1,0:T(8,128)(2,1)}, u32[]{:S(2)}) %copy-start.2) | copy-done | bytes 69656
  24.5 7.9 %shard_map.95 = (f32[128,512]{1,0:T(8,128)S(1)}, bf16[3,128,512]{2,1,0:T(8,128)(2,1)S(1)}, f32[4,256,128]{2,1,0:T(8,128)S(1)}, bf16[4,256,128]{2,1,0:T(8,128)(2,1)S(1)}) custom-call(bf16[1056,128]{1,0:T(8,128)(2,1)S(1)} %copy-done, bf16[1056,128]{1,0:T(8,128)(2,1)S(1)} %collective-permute-done.refs_1_, bf16[1056,128]{1,0:T(8,128)(2,1)S(1)} %collective-permute-done.1.refs_2_, ...), custom_call_target="tpu_custom_call" | custom-call | tf_op jit(solution)/shard_map/pallas_call | solution.py:194
  32.6 0.6 %copy-done.1 = f32[128,512]{1,0:T(8,128)} copy-done((f32[128,512]{1,0:T(8,128)}, f32[128,512]{1,0:T(8,128)S(1)}, u32[]{:S(2)}) %copy-start.1) | copy-done | bytes 262168
  33.1 1.6 %collective-permute-start.13 = (bf16[128,512]{1,0:T(8,128)(2,1)S(1)}, bf16[128,512]{1,0:T(8,128)(2,1)S(1)}, u32[]{:S(2)}, u32[]{:S(2)}) collective-permute-start(bf16[128,512]{1,0:T(8,128)(2,1)S(1)} %get-tuple-element.17), channel_id=1, source_target_pairs={{0,24},{8,16},{16,8},{24,0},{1,25},{9,17},{17,9},{25,1},{2,26},{10... | collective-permute-start | bytes 393224 | tf_op jit(solution)/shard_map/ppermute | solution.py:21
  34.8 1.3 %collective-permute-start.12 = (bf16[128,512]{1,0:T(8,128)(2,1)S(1)}, bf16[128,512]{1,0:T(8,128)(2,1)S(1)}, u32[]{:S(2)}, u32[]{:S(2)}) collective-permute-start(bf16[128,512]{1,0:T(8,128)(2,1)S(1)} %get-tuple-element.18), channel_id=1, source_target_pairs={{0,16},{8,24},{16,0},{24,8},{1,17},{9,25},{17,1},{25,9},{2,18},{10... | collective-permute-start | bytes 393224 | tf_op jit(solution)/shard_map/ppermute | solution.py:21
  36.1 0.6 %collective-permute-start.11 = (bf16[128,512]{1,0:T(8,128)(2,1)S(1)}, bf16[128,512]{1,0:T(8,128)(2,1)S(1)}, u32[]{:S(2)}, u32[]{:S(2)}) collective-permute-start(bf16[128,512]{1,0:T(8,128)(2,1)S(1)} %get-tuple-element.19), channel_id=1, source_target_pairs={{0,8},{8,0},{16,24},{24,16},{1,9},{9,1},{17,25},{25,17},{2,10},{10... | collective-permute-start | bytes 393224 | tf_op jit(solution)/shard_map/ppermute | solution.py:21
  36.7 0.3 collective-permute-start.16
  37.1 0.7 %collective-permute-start.15 = (bf16[256,128]{1,0:T(8,128)(2,1)S(1)}, bf16[256,128]{1,0:T(8,128)(2,1)S(1)}, u32[]{:S(2)}, u32[]{:S(2)}) collective-permute-start(bf16[256,128]{1,0:T(8,128)(2,1)S(1)} %get-tuple-element.21), channel_id=1, source_target_pairs={{0,4},{1,5},{2,6},{3,7},{4,0},{5,1},{6,2},{7,3},{8,12},{9,13},{10,... | collective-permute-start | bytes 196616 | tf_op jit(solution)/shard_map/ppermute | solution.py:21
  37.8 2.6 %collective-permute-done.13.refs_2_ = bf16[128,512]{1,0:T(8,128)(2,1)S(1)} collective-permute-done((bf16[128,512]{1,0:T(8,128)(2,1)S(1)}, bf16[128,512]{1,0:T(8,128)(2,1)S(1)}, u32[]{:S(2)}, u32[]{:S(2)}) %collective-permute-start.13) | collective-permute-done | bytes 131104 | tf_op jit(solution)/shard_map/ppermute | solution.py:21
  40.4 0.8 %collective-permute-start.14 = (bf16[256,128]{1,0:T(8,128)(2,1)S(1)}, bf16[256,128]{1,0:T(8,128)(2,1)S(1)}, u32[]{:S(2)}, u32[]{:S(2)}) collective-permute-start(bf16[256,128]{1,0:T(8,128)(2,1)S(1)} %get-tuple-element.22), channel_id=1, source_target_pairs={{0,2},{1,3},{2,0},{3,1},{4,6},{5,7},{6,4},{7,5},{8,10},{9,11},{10,... | collective-permute-start | bytes 196616 | tf_op jit(solution)/shard_map/ppermute | solution.py:21
  41.2 0.7 %slice_bitcast_fusion.dkv_own = f32[256,128]{1,0:T(8,128)} fusion(f32[4,256,128]{2,1,0:T(8,128)S(1)} %get-tuple-element.16), kind=kLoop, calls=%fused_computation.1 | loop fusion | bytes 262144 | tf_op jit(solution)/shard_map/squeeze | solution.py:231
  41.9 0.4 collective-permute-done.12.refs_1_
  42.2 1.0 %collective-permute-done.16.refs_5_ = bf16[256,128]{1,0:T(8,128)(2,1)S(1)} collective-permute-done((bf16[256,128]{1,0:T(8,128)(2,1)S(1)}, bf16[256,128]{1,0:T(8,128)(2,1)S(1)}, u32[]{:S(2)}, u32[]{:S(2)}) %collective-permute-start.16) | collective-permute-done | bytes 65568 | tf_op jit(solution)/shard_map/ppermute | solution.py:21
  43.2 1.1 %collective-permute-done.15.refs_4_ = bf16[256,128]{1,0:T(8,128)(2,1)S(1)} collective-permute-done((bf16[256,128]{1,0:T(8,128)(2,1)S(1)}, bf16[256,128]{1,0:T(8,128)(2,1)S(1)}, u32[]{:S(2)}, u32[]{:S(2)}) %collective-permute-start.15) | collective-permute-done | bytes 65568 | tf_op jit(solution)/shard_map/ppermute | solution.py:21
  44.3 0.7 %collective-permute-done.14.refs_3_ = bf16[256,128]{1,0:T(8,128)(2,1)S(1)} collective-permute-done((bf16[256,128]{1,0:T(8,128)(2,1)S(1)}, bf16[256,128]{1,0:T(8,128)(2,1)S(1)}, u32[]{:S(2)}, u32[]{:S(2)}) %collective-permute-start.14) | collective-permute-done | bytes 65568 | tf_op jit(solution)/shard_map/ppermute | solution.py:21
  45.0 0.6 %copy-done.8 = bf16[256,128]{1,0:T(8,128)(2,1)} copy-done((bf16[256,128]{1,0:T(8,128)(2,1)}, bf16[256,128]{1,0:T(8,128)(2,1)S(1)}, u32[]{:S(2)}) %copy-start.8) | copy-done | bytes 65560
  45.6 2.0 %shard_map.96 = (bf16[128,512]{1,0:T(8,128)(2,1)}, bf16[128,128]{1,0:T(8,128)(2,1)}, bf16[128,128]{1,0:T(8,128)(2,1)}) custom-call(f32[128,512]{1,0:T(8,128)} %copy-done.1, f32[256,128]{1,0:T(8,128)} %slice_bitcast_fusion.dkv_own, bf16[128,512]{1,0:T(8,128)(2,1)} %copy-done.5, bf16[128,512]{1,0:T(8,128)(2,1)} %copy-done.4, bf16[128,512]{1,0:T(8,128)(2,1)} %copy-done.3, ...), custom_call_target="tpu_custom_call" | custom-call | tf_op jit(solution)/shard_map/pallas_call | solution.py:226
  (27 shorter events, 0.3 us)
Async XLA Ops:
  2.7 8.5 %collective-permute-start.8 = (bf16[272,128]{1,0:T(8,128)(2,1)}, bf16[272,128]{1,0:T(8,128)(2,1)S(1)}, u32[]{:S(2)}, u32[]{:S(2)}) collective-permute-start(bf16[272,128]{1,0:T(8,128)(2,1)} %get-tuple-element.10.refs_4_), channel_id=1, source_target_pairs={{0,6},{1,7},{2,4},{3,5},{4,2},{5,3},{6,0},{7,1},{8,14},{9,15},{10,... | collective-permute-start | bytes 208904 | tf_op jit(solution)/shard_map/ppermute | solution.py:21
  7.7 12.1 %collective-permute-start.2 = (bf16[1056,128]{1,0:T(8,128)(2,1)}, bf16[1056,128]{1,0:T(8,128)(2,1)S(1)}, u32[]{:S(2)}, u32[]{:S(2)}) collective-permute-start(bf16[1056,128]{1,0:T(8,128)(2,1)} %get-tuple-element.9.refs_0_), channel_id=1, source_target_pairs={{0,24},{8,16},{16,8},{24,0},{1,25},{9,17},{17,9},{25,1},{2,26},{10... | collective-permute-start | bytes 811016 | tf_op jit(solution)/shard_map/ppermute | solution.py:21
  10.2 12.4 %collective-permute-start.1 = (bf16[1056,128]{1,0:T(8,128)(2,1)}, bf16[1056,128]{1,0:T(8,128)(2,1)S(1)}, u32[]{:S(2)}, u32[]{:S(2)}) collective-permute-start(bf16[1056,128]{1,0:T(8,128)(2,1)} %get-tuple-element.9.refs_0_), channel_id=1, source_target_pairs={{0,16},{8,24},{16,0},{24,8},{1,17},{9,25},{17,1},{25,9},{2,18},{10... | collective-permute-start | bytes 811016 | tf_op jit(solution)/shard_map/ppermute | solution.py:21
  10.7 12.0 %collective-permute-start = (bf16[1056,128]{1,0:T(8,128)(2,1)}, bf16[1056,128]{1,0:T(8,128)(2,1)S(1)}, u32[]{:S(2)}, u32[]{:S(2)}) collective-permute-start(bf16[1056,128]{1,0:T(8,128)(2,1)} %get-tuple-element.9.refs_0_), channel_id=1, source_target_pairs={{0,8},{8,0},{16,24},{24,16},{1,9},{9,1},{17,25},{25,17},{2,10},{10... | collective-permute-start | bytes 811016 | tf_op jit(solution)/shard_map/ppermute | solution.py:21
  11.2 5.7 %collective-permute-start.6 = (bf16[272,128]{1,0:T(8,128)(2,1)}, bf16[272,128]{1,0:T(8,128)(2,1)S(1)}, u32[]{:S(2)}, u32[]{:S(2)}) collective-permute-start(bf16[272,128]{1,0:T(8,128)(2,1)} %get-tuple-element.10.refs_4_), channel_id=1, source_target_pairs={{0,4},{1,5},{2,6},{3,7},{4,0},{5,1},{6,2},{7,3},{8,12},{9,13},{10,... | collective-permute-start | bytes 208904 | tf_op jit(solution)/shard_map/ppermute | solution.py:21
  11.2 5.7 %collective-permute-start.4 = (bf16[272,128]{1,0:T(8,128)(2,1)}, bf16[272,128]{1,0:T(8,128)(2,1)S(1)}, u32[]{:S(2)}, u32[]{:S(2)}) collective-permute-start(bf16[272,128]{1,0:T(8,128)(2,1)} %get-tuple-element.10.refs_4_), channel_id=1, source_target_pairs={{0,2},{1,3},{2,0},{3,1},{4,6},{5,7},{6,4},{7,5},{8,10},{9,11},{10,... | collective-permute-start | bytes 208904 | tf_op jit(solution)/shard_map/ppermute | solution.py:21
  16.9 1.5 %collective-permute-start.3 = (bf16[272,128]{1,0:T(8,128)(2,1)}, bf16[272,128]{1,0:T(8,128)(2,1)S(1)}, u32[]{:S(2)}, u32[]{:S(2)}) collective-permute-start(bf16[272,128]{1,0:T(8,128)(2,1)} %get-tuple-element.10.refs_4_), channel_id=1, source_target_pairs={{0,1},{1,0},{2,3},{3,2},{4,5},{5,4},{6,7},{7,6},{8,9},{9,8},{10,11... | collective-permute-start | bytes 208904 | tf_op jit(solution)/shard_map/ppermute | solution.py:21
  16.9 1.6 %collective-permute-start.9 = (bf16[272,128]{1,0:T(8,128)(2,1)S(1)}, bf16[272,128]{1,0:T(8,128)(2,1)S(1)}, u32[]{:S(2)}, u32[]{:S(2)}) collective-permute-start(bf16[272,128]{1,0:T(8,128)(2,1)S(1)} %collective-permute-done.8.refs_10_), channel_id=1, source_target_pairs={{0,1},{1,0},{2,3},{3,2},{4,5},{5,4},{6,7},{7,6},{8,9},{9,8},{10,11... | collective-permute-start | bytes 208904 | tf_op jit(solution)/shard_map/ppermute | solution.py:21
  18.4 1.3 %collective-permute-start.7 = (bf16[272,128]{1,0:T(8,128)(2,1)S(1)}, bf16[272,128]{1,0:T(8,128)(2,1)S(1)}, u32[]{:S(2)}, u32[]{:S(2)}) collective-permute-start(bf16[272,128]{1,0:T(8,128)(2,1)S(1)} %collective-permute-done.6.refs_8_), channel_id=1, source_target_pairs={{0,1},{1,0},{2,3},{3,2},{4,5},{5,4},{6,7},{7,6},{8,9},{9,8},{10,11... | collective-permute-start | bytes 208904 | tf_op jit(solution)/shard_map/ppermute | solution.py:21
  18.5 1.3 %collective-permute-start.5 = (bf16[272,128]{1,0:T(8,128)(2,1)S(1)}, bf16[272,128]{1,0:T(8,128)(2,1)S(1)}, u32[]{:S(2)}, u32[]{:S(2)}) collective-permute-start(bf16[272,128]{1,0:T(8,128)(2,1)S(1)} %collective-permute-done.4.refs_6_), channel_id=1, source_target_pairs={{0,1},{1,0},{2,3},{3,2},{4,5},{5,4},{6,7},{7,6},{8,9},{9,8},{10,11... | collective-permute-start | bytes 208904 | tf_op jit(solution)/shard_map/ppermute | solution.py:21
  22.7 1.0 %copy-start = (bf16[1056,128]{1,0:T(8,128)(2,1)S(1)}, bf16[1056,128]{1,0:T(8,128)(2,1)}, u32[]{:S(2)}) copy-start(bf16[1056,128]{1,0:T(8,128)(2,1)} %get-tuple-element.9.refs_0_) | copy-start | bytes 811012
  23.6 0.9 %copy-start.2 = (bf16[272,128]{1,0:T(8,128)(2,1)S(1)}, bf16[272,128]{1,0:T(8,128)(2,1)}, u32[]{:S(2)}) copy-start(bf16[272,128]{1,0:T(8,128)(2,1)} %get-tuple-element.10.refs_4_) | copy-start | bytes 208900
  32.4 0.7 %copy-start.1 = (f32[128,512]{1,0:T(8,128)}, f32[128,512]{1,0:T(8,128)S(1)}, u32[]{:S(2)}) copy-start(f32[128,512]{1,0:T(8,128)S(1)} %get-tuple-element.11.dq_own) | copy-start | bytes 786436
  32.4 4.2 %collective-permute-start.10 = (bf16[4,256,128]{2,1,0:T(8,128)(2,1)S(1)}, bf16[4,256,128]{2,1,0:T(8,128)(2,1)S(1)}, u32[]{:S(2)}, u32[]{:S(2)}) collective-permute-start(bf16[4,256,128]{2,1,0:T(8,128)(2,1)S(1)} %get-tuple-element.13), channel_id=1, source_target_pairs={{0,1},{1,0},{2,3},{3,2},{4,5},{5,4},{6,7},{7,6},{8,9},{9,8},{10,11... | collective-permute-start | bytes 786440 | tf_op jit(solution)/shard_map/ppermute | solution.py:21
  33.1 7.3 %collective-permute-start.13 = (bf16[128,512]{1,0:T(8,128)(2,1)S(1)}, bf16[128,512]{1,0:T(8,128)(2,1)S(1)}, u32[]{:S(2)}, u32[]{:S(2)}) collective-permute-start(bf16[128,512]{1,0:T(8,128)(2,1)S(1)} %get-tuple-element.17), channel_id=1, source_target_pairs={{0,24},{8,16},{16,8},{24,0},{1,25},{9,17},{17,9},{25,1},{2,26},{10... | collective-permute-start | bytes 393224 | tf_op jit(solution)/shard_map/ppermute | solution.py:21
  34.8 7.5 %collective-permute-start.12 = (bf16[128,512]{1,0:T(8,128)(2,1)S(1)}, bf16[128,512]{1,0:T(8,128)(2,1)S(1)}, u32[]{:S(2)}, u32[]{:S(2)}) collective-permute-start(bf16[128,512]{1,0:T(8,128)(2,1)S(1)} %get-tuple-element.18), channel_id=1, source_target_pairs={{0,16},{8,24},{16,0},{24,8},{1,17},{9,25},{17,1},{25,9},{2,18},{10... | collective-permute-start | bytes 393224 | tf_op jit(solution)/shard_map/ppermute | solution.py:21
  36.1 6.2 %collective-permute-start.11 = (bf16[128,512]{1,0:T(8,128)(2,1)S(1)}, bf16[128,512]{1,0:T(8,128)(2,1)S(1)}, u32[]{:S(2)}, u32[]{:S(2)}) collective-permute-start(bf16[128,512]{1,0:T(8,128)(2,1)S(1)} %get-tuple-element.19), channel_id=1, source_target_pairs={{0,8},{8,0},{16,24},{24,16},{1,9},{9,1},{17,25},{25,17},{2,10},{10... | collective-permute-start | bytes 393224 | tf_op jit(solution)/shard_map/ppermute | solution.py:21
  36.7 6.5 %collective-permute-start.16 = (bf16[256,128]{1,0:T(8,128)(2,1)S(1)}, bf16[256,128]{1,0:T(8,128)(2,1)S(1)}, u32[]{:S(2)}, u32[]{:S(2)}) collective-permute-start(bf16[256,128]{1,0:T(8,128)(2,1)S(1)} %get-tuple-element.20), channel_id=1, source_target_pairs={{0,6},{1,7},{2,4},{3,5},{4,2},{5,3},{6,0},{7,1},{8,14},{9,15},{10,... | collective-permute-start | bytes 196616 | tf_op jit(solution)/shard_map/ppermute | solution.py:21
  37.1 7.2 %collective-permute-start.15 = (bf16[256,128]{1,0:T(8,128)(2,1)S(1)}, bf16[256,128]{1,0:T(8,128)(2,1)S(1)}, u32[]{:S(2)}, u32[]{:S(2)}) collective-permute-start(bf16[256,128]{1,0:T(8,128)(2,1)S(1)} %get-tuple-element.21), channel_id=1, source_target_pairs={{0,4},{1,5},{2,6},{3,7},{4,0},{5,1},{6,2},{7,3},{8,12},{9,13},{10,... | collective-permute-start | bytes 196616 | tf_op jit(solution)/shard_map/ppermute | solution.py:21
  40.4 1.5 %copy-start.3 = (bf16[128,512]{1,0:T(8,128)(2,1)}, bf16[128,512]{1,0:T(8,128)(2,1)S(1)}, u32[]{:S(2)}) copy-start(bf16[128,512]{1,0:T(8,128)(2,1)S(1)} %collective-permute-done.13.refs_2_) | copy-start | bytes 393220
  40.4 4.5 %collective-permute-start.14 = (bf16[256,128]{1,0:T(8,128)(2,1)S(1)}, bf16[256,128]{1,0:T(8,128)(2,1)S(1)}, u32[]{:S(2)}, u32[]{:S(2)}) collective-permute-start(bf16[256,128]{1,0:T(8,128)(2,1)S(1)} %get-tuple-element.22), channel_id=1, source_target_pairs={{0,2},{1,3},{2,0},{3,1},{4,6},{5,7},{6,4},{7,5},{8,10},{9,11},{10,... | collective-permute-start | bytes 196616 | tf_op jit(solution)/shard_map/ppermute | solution.py:21
  42.2 2.7 %copy-start.4 = (bf16[128,512]{1,0:T(8,128)(2,1)}, bf16[128,512]{1,0:T(8,128)(2,1)S(1)}, u32[]{:S(2)}) copy-start(bf16[128,512]{1,0:T(8,128)(2,1)S(1)} %collective-permute-done.12.refs_1_) | copy-start | bytes 393220
  42.2 2.7 %copy-start.5 = (bf16[128,512]{1,0:T(8,128)(2,1)}, bf16[128,512]{1,0:T(8,128)(2,1)S(1)}, u32[]{:S(2)}) copy-start(bf16[128,512]{1,0:T(8,128)(2,1)S(1)} %collective-permute-done.11.refs_0_) | copy-start | bytes 393220
  43.2 1.8 %copy-start.6 = (bf16[256,128]{1,0:T(8,128)(2,1)}, bf16[256,128]{1,0:T(8,128)(2,1)S(1)}, u32[]{:S(2)}) copy-start(bf16[256,128]{1,0:T(8,128)(2,1)S(1)} %collective-permute-done.16.refs_5_) | copy-start | bytes 196612
  44.3 0.7 %copy-start.7 = (bf16[256,128]{1,0:T(8,128)(2,1)}, bf16[256,128]{1,0:T(8,128)(2,1)S(1)}, u32[]{:S(2)}) copy-start(bf16[256,128]{1,0:T(8,128)(2,1)S(1)} %collective-permute-done.15.refs_4_) | copy-start | bytes 196612
  44.9 0.6 %copy-start.8 = (bf16[256,128]{1,0:T(8,128)(2,1)}, bf16[256,128]{1,0:T(8,128)(2,1)S(1)}, u32[]{:S(2)}) copy-start(bf16[256,128]{1,0:T(8,128)(2,1)S(1)} %collective-permute-done.14.refs_3_) | copy-start | bytes 196612

commit v2 on v1

v2 whole, which is shorter than its diff:
```python
import functools
import math

import jax
import jax.numpy as jnp
from jax import lax
from jax.experimental import pallas as pl
from jax.experimental.pallas import tpu as pltpu
from jax.sharding import PartitionSpec as P

BF = jnp.bfloat16
F32 = jnp.float32
RUN = 64
LOG2E = math.log2(math.e)
VMEM = pl.BlockSpec(memory_space=pltpu.VMEM)
SMALL = pltpu.CompilerParams(vmem_limit_bytes=16 * 1024 * 1024)
NN = (((1,), (0,)), ((), ()))
NT = (((1,), (1,)), ((), ()))
KEYS = 256
COLS = 256


def swapped(block, axis, mask):
    pairs = [(i, i ^ mask) for i in range(lax.axis_size(axis))]
    return lax.ppermute(block, axis, pairs)


def three_parts(x):
    hi = x.astype(BF)
    rest = x - hi.astype(F32)
    mid = rest.astype(BF)
    low = (rest - mid.astype(F32)).astype(BF)
    return [hi, mid, low]


def dot(a, b, dims=NN):
    return lax.dot_general(a, b, dims, preferred_element_type=F32)


def pack_kernel(q_ref, k_ref, v_ref, o_ref, g_ref, lse_ref, pos_ref, x_ref, kv_ref):
    rows, width = k_ref.shape
    heads = q_ref.shape[1] // width
    ones = jnp.ones((8, width), BF)
    deltas = []
    for h in range(heads):
        cols = slice(h * width, (h + 1) * width)
        q = q_ref[:, cols]
        g = g_ref[:, cols]
        x_ref[h * rows : (h + 1) * rows, :] = q
        x_ref[(heads + h) * rows : (heads + h + 1) * rows, :] = g
        prod = g.astype(F32) * o_ref[:, cols].astype(F32)
        hi = prod.astype(BF)
        low = (prod - hi.astype(F32)).astype(BF)
        deltas.append((dot(ones, hi, NT) + dot(ones, low, NT))[:1])
    run = (pos_ref[...] // RUN).astype(F32)
    extra = (
        three_parts(lse_ref[...] * LOG2E)
        + three_parts(jnp.concatenate(deltas, axis=0))
        + [run.astype(BF), jnp.zeros((32 - 6 * heads - 1, rows), BF)]
    )
    x_ref[2 * heads * rows :, :] = jnp.concatenate([e.astype(F32) for e in extra], axis=0).astype(BF)
    kv_ref[:rows, :] = k_ref[...]
    kv_ref[rows : 2 * rows, :] = v_ref[...]
    lane = lax.broadcasted_iota(jnp.int32, run.shape, 1)
    ids = [
        jnp.max(jnp.where(lane == r * RUN, run, 0.0), axis=1, keepdims=True)
        for r in range(rows // RUN)
    ]
    wide = [jnp.broadcast_to(i, (1, width)) for i in ids]
    wide.append(jnp.zeros((16 - len(ids), width), F32))
    kv_ref[2 * rows :, :] = jnp.concatenate(wide, axis=0).astype(BF)


def stack_kernel(rows, *refs):
    kv_refs, (k_ref, kt_ref, v_ref, run_ref) = refs[:-4], refs[-4:]
    per = rows // RUN
    for j, kv_ref in enumerate(kv_refs):
        at = slice(j * rows, (j + 1) * rows)
        k = kv_ref[:rows, :]
        k_ref[at, :] = k
        kt_ref[:, at] = k.astype(F32).T.astype(BF)
        v_ref[at, :] = kv_ref[rows : 2 * rows, :]
        e = kv_ref[2 * rows :, :].astype(F32)
        for r in range(per):
            run_ref[j * per + r] = jnp.broadcast_to(e[r : r + 1], (8, e.shape[1]))


def pair_kernel(first, last, rows, heads, scale, *refs):
    x_refs, refs = refs[:2], refs[2:]
    (k_ref, kt_ref, v_ref, run_ref), refs = refs[:4], refs[4:]
    if not first:
        (acc_in,), refs = refs[:1], refs[1:]
    dq_ref, dq_sib_ref, acc_ref, *far_refs = refs
    keys, width = k_ref.shape
    hr = heads * rows
    per = KEYS // RUN
    dqt = [[None] * (hr // COLS) for _ in range(2)]
    rowed = []
    for b in range(2):
        e = x_refs[b][2 * hr :, :].astype(F32)
        lse = e[0:heads] + e[heads : 2 * heads] + e[2 * heads : 3 * heads]
        delta = e[3 * heads : 4 * heads] + e[4 * heads : 5 * heads] + e[5 * heads : 6 * heads]
        run = e[6 * heads : 6 * heads + 1]
        rowed.append((lse, delta, run))
    for c in range(keys // KEYS):
        at = slice(c * KEYS, (c + 1) * KEYS)
        k, kt, v = k_ref[at, :], kt_ref[:, at], v_ref[at, :]
        dk = dv = None
        for b in range(2):
            lse, delta, run = rowed[b]
            for n in range(hr // COLS):
                cols = slice(n * COLS, (n + 1) * COLS)
                q = x_refs[b][cols, :]
                g = x_refs[b][hr + n * COLS : hr + (n + 1) * COLS, :]
                st = dot(k, q, NT)
                dpt = dot(v, g, NT)
                p_rows, d_rows = [], []
                for r in range(per):
                    sl = slice(r * RUN, (r + 1) * RUN)
                    krun = run_ref[c * per + r][:1]
                    p_heads, d_heads = [], []
                    for h in range(COLS // rows):
                        hl = slice(h * rows, (h + 1) * rows)
                        head = n * (COLS // rows) + h
                        row = jnp.where(krun <= run, lse[head : head + 1], 1e30)
                        arg = st[sl, hl] * (scale * LOG2E) - row
                        start = c * KEYS + r * RUN
                        if first and b == 0 and start < rows:
                            i = lax.broadcasted_iota(jnp.int32, (RUN, rows), 1) - start
                            j = lax.broadcasted_iota(jnp.int32, (RUN, rows), 0)
                            arg = jnp.where((i >= 0) & (i < j), -1e30, arg)
                        p = jnp.exp2(arg)
                        p_heads.append(p.astype(BF))
                        d_heads.append((p * (dpt[sl, hl] - delta[head : head + 1])).astype(BF))
                    p_rows.append(jnp.concatenate(p_heads, axis=1))
                    d_rows.append(jnp.concatenate(d_heads, axis=1))
                p = jnp.concatenate(p_rows, axis=0)
                d = jnp.concatenate(d_rows, axis=0)
                dv_n, dk_n, dq_n = dot(p, g), dot(d, q), dot(kt, d)
                dv = dv_n if dv is None else dv + dv_n
                dk = dk_n if dk is None else dk + dk_n
                old = dqt[b][n]
                dqt[b][n] = dq_n if old is None else old + dq_n
        for j in range(KEYS // rows):
            block = c * (KEYS // rows) + j
            sl = slice(j * rows, (j + 1) * rows)
            dk_j, dv_j = dk[sl], dv[sl]
            if not first:
                dk_j += acc_in[block, :rows, :]
                dv_j += acc_in[block, rows:, :]
            if last and block:
                far_refs[block - 1][:rows, :] = dk_j.astype(BF)
                far_refs[block - 1][rows:, :] = dv_j.astype(BF)
            else:
                acc_ref[block, :rows, :] = dk_j
                acc_ref[block, rows:, :] = dv_j
    for n in range(hr // COLS):
        cols = slice(n * COLS, (n + 1) * COLS)
        dq_ref[:, cols] = dqt[0][n]
        dq_sib_ref[:, cols] = dqt[1][n].astype(BF)


def final_kernel(rows, heads, scale, n_dq, dq_own, acc, *refs):
    dq_refs, dkv_refs, (gq_ref, gk_ref, gv_ref) = refs[:n_dq], refs[n_dq:-3], refs[-3:]
    dq = dq_own[...]
    for r in dq_refs:
        dq = dq + r[...].astype(F32)
    for h in range(heads):
        part = dq[:, h * rows : (h + 1) * rows]
        gq_ref[:, h * 128 : (h + 1) * 128] = (scale * part).T.astype(BF)
    dkv = acc[0]
    for r in dkv_refs:
        dkv = dkv + r[...].astype(F32)
    gk_ref[...] = (scale * dkv[:rows]).astype(BF)
    gv_ref[...] = dkv[rows:].astype(BF)


def pair_call(x, x_sib, stacked, acc, last, rows, heads, scale):
    sds = jax.ShapeDtypeStruct
    keys, width = stacked[0].shape
    blocks = keys // rows
    hr = heads * rows
    first = acc is None
    far = (blocks - 1) if last else 0
    args = (x, x_sib, *stacked) + (() if first else (acc,))
    return pl.pallas_call(
        functools.partial(pair_kernel, first, last, rows, heads, scale),
        out_shape=(
            sds((width, hr), F32),
            sds((width, hr), BF),
            sds((1 if last else blocks, 2 * rows, width), F32),
        )
        + (sds((2 * rows, width), BF),) * far,
        in_specs=[VMEM] * len(args),
        out_specs=(VMEM,) * (3 + far),
        compiler_params=SMALL,
        cost_estimate=pl.CostEstimate(
            flops=20 * keys * hr * width, bytes_accessed=1 << 20, transcendentals=2 * keys * hr
        ),
    )(*args)


def on_device(query, key, value, out, grad_out, lse, positions):
    rows, width = key.shape
    heads = query.shape[1] // width
    hr = heads * rows
    scale = width ** (-0.5)
    nq = lax.axis_size("outer")
    nz = lax.axis_size("inner") // 2
    sds = jax.ShapeDtypeStruct
    x, kv = pl.pallas_call(
        pack_kernel,
        out_shape=(sds((2 * hr + 32, width), BF), sds((2 * rows + 16, width), BF)),
        in_specs=[VMEM] * 7,
        out_specs=(VMEM, VMEM),
        compiler_params=SMALL,
    )(query, key, value, out, grad_out, lse, positions[None, :])

    xs = [x] + [swapped(x, "outer", s) for s in range(1, nq)]
    kvs = [kv] + [swapped(kv, "inner", 2 * s) for s in range(1, nz)]
    xs_sib = [swapped(block, "inner", 1) for block in xs]
    per = rows // RUN
    stacked = pl.pallas_call(
        functools.partial(stack_kernel, rows),
        out_shape=(
            sds((nz * rows, width), BF),
            sds((width, nz * rows), BF),
            sds((nz * rows, width), BF),
            sds((nz * per, 8, width), F32),
        ),
        in_specs=[VMEM] * nz,
        out_specs=(VMEM,) * 4,
        compiler_params=SMALL,
    )(*kvs)

    acc = None
    got = []
    for s in range(nq):
        dq, dq_sib, acc, *far = pair_call(
            xs[s], xs_sib[s], stacked, acc, s == nq - 1, rows, heads, scale
        )
        other = swapped(dq_sib, "inner", 1)
        if s == 0:
            dq_own = dq
            got.append(other)
        else:
            got.append(swapped((dq + other.astype(F32)).astype(BF), "outer", s))
    dkv_got = [swapped(far[s - 1], "inner", 2 * s) for s in range(1, nz)]

    return pl.pallas_call(
        functools.partial(final_kernel, rows, heads, scale, len(got)),
        out_shape=(sds((rows, heads * width), BF), sds((rows, width), BF), sds((rows, width), BF)),
        in_specs=[VMEM] * (2 + len(got) + nz - 1),
        out_specs=(VMEM,) * 3,
        compiler_params=SMALL,
    )(dq_own, acc, *got, *dkv_got)


def solution(mesh):
    tokens = P(("outer", "inner"), None)
    return jax.shard_map(
        on_device,
        mesh=mesh,
        in_specs=(tokens,) * 5 + (P(None, ("outer", "inner")), P(("outer", "inner"))),
        out_specs=(tokens,) * 3,
        check_vma=False,
    )
```

time: 47.8 us -> 61 us (1.28)
  waiting for transfers between devices: 15.5 us -> 23 us
  starting transfers between devices: 15.5 us -> 21.7 us
  Pallas kernels: 11.9 us -> 9.55 us
  local copies, waits for them, and re-layouts: 3.73 us -> 5.56 us
    ppermute x17 -> x20, waiting for transfers between devices: 15.5 us -> 23 us  [swapped(): return lax.ppermute(block, axis, pairs)]
    ppermute x17 -> x20, starting transfers between devices: 15.5 us -> 21.7 us  [swapped(): return lax.ppermute(block, axis, pairs)]
    unnamed x18 -> x14, local copies, waits for them, and re-layouts: 3.03 us -> 5.56 us
    pallas_call x1, Pallas kernels: 2.06 us -> 0.26 us  [on_device(): pl.pallas_call(pack_kernel, out_shape=(sds((2 * hr + 32, width), BF), sds...]
    squeeze x2 -> x0, local copies, waits for them, and re-layouts: 0.69 us -> none  [the longest x1 0.66 us: on_device(): total[0]]
    pallas_call x2 -> x6, Pallas kernels: 9.88 us -> 9.29 us  [the longest x4 8.36 us: pair_call(): pl.pallas_call(functools.partial(pair_kernel, first, last, rows, heads, s...]
  transfers between devices with their start and end apart: 17 -> 20, of which waited for: 11 -> 7; matrix products, arithmetic and copies ran while one was open for 2% -> 0% of each run, Pallas kernels for 0% -> 11%
where the time goes in v2:
time: 61 us; the launch traced here: 60.7 us
  waiting for transfers between devices  23 us (38%)
  starting transfers between devices  21.7 us (36%)
  Pallas kernels  9.55 us (16%)
  local copies, waits for them, and re-layouts  5.56 us (9%)
  between operations  0.76 us (1%)
    ppermute x20, waiting for transfers between devices, swapped(): return lax.ppermute(block, axis, pairs)  23 us
    ppermute x20, starting transfers between devices, swapped(): return lax.ppermute(block, axis, pairs)  21.7 us
    pallas_call x4, Pallas kernels, pair_call(): pl.pallas_call(functools.partial(pair_kernel, first, last, rows, heads, s...  8.36 us
    unnamed x14, local copies, waits for them, and re-layouts  5.56 us
  transfers between devices with their start and end apart: 20, of which 7 were waited for; matrix products, arithmetic and copies ran while one was open for 0% of the time, Pallas kernels for 11%

profile of v2, /device:TPU:0, one launch (start us, length us, event | category | flops | bytes accessed | tf_op | source)
XLA Modules:
  0.0 60.7 jit_solution(329855828244407826)
XLA Ops:
  0.6 0.6 %copy-done.6 = s32[128]{0:T(128)S(1)} copy-done((s32[128]{0:T(128)S(1)}, s32[128]{0:T(128)}, u32[]{:S(2)}) %copy-start.6) | copy-done | bytes 536
  1.3 0.9 %copy-done = bf16[128,512]{1,0:T(8,128)(2,1)S(1)} copy-done((bf16[128,512]{1,0:T(8,128)(2,1)S(1)}, bf16[128,512]{1,0:T(8,128)(2,1)}, u32[]{:S(2)}) %copy-start) | copy-done | bytes 131096
  2.2 0.9 %copy-done.1 = bf16[128,512]{1,0:T(8,128)(2,1)S(1)} copy-done((bf16[128,512]{1,0:T(8,128)(2,1)S(1)}, bf16[128,512]{1,0:T(8,128)(2,1)}, u32[]{:S(2)}) %copy-start.1) | copy-done | bytes 131096
  3.1 0.9 %copy-done.2 = bf16[128,512]{1,0:T(8,128)(2,1)S(1)} copy-done((bf16[128,512]{1,0:T(8,128)(2,1)S(1)}, bf16[128,512]{1,0:T(8,128)(2,1)}, u32[]{:S(2)}) %copy-start.2) | copy-done | bytes 131096
  4.0 0.8 %copy-done.3 = bf16[128,128]{1,0:T(8,128)(2,1)S(1)} copy-done((bf16[128,128]{1,0:T(8,128)(2,1)S(1)}, bf16[128,128]{1,0:T(8,128)(2,1)}, u32[]{:S(2)}) %copy-start.3) | copy-done | bytes 32792
  4.8 0.8 %copy-done.4 = bf16[128,128]{1,0:T(8,128)(2,1)S(1)} copy-done((bf16[128,128]{1,0:T(8,128)(2,1)S(1)}, bf16[128,128]{1,0:T(8,128)(2,1)}, u32[]{:S(2)}) %copy-start.4) | copy-done | bytes 32792
  5.5 0.7 %copy-done.5 = f32[4,128]{1,0:T(4,128)S(1)} copy-done((f32[4,128]{1,0:T(4,128)S(1)}, f32[4,128]{1,0:T(4,128)}, u32[]{:S(2)}) %copy-start.5) | copy-done | bytes 2072
  6.2 0.3 shard_map.94
  6.5 3.0 %collective-permute-start.8 = (bf16[1056,128]{1,0:T(8,128)(2,1)S(1)}, bf16[1056,128]{1,0:T(8,128)(2,1)S(1)}, u32[]{:S(2)}, u32[]{:S(2)}) collective-permute-start(bf16[1056,128]{1,0:T(8,128)(2,1)S(1)} %get-tuple-element.24.refs_0_), channel_id=1, source_target_pairs={{0,8},{8,0},{16,24},{24,16},{1,9},{9,1},{17,25},{25,17},{2,10},{10... | collective-permute-start | bytes 811016 | tf_op jit(solution)/shard_map/ppermute | solution.py:25
  9.5 1.5 %collective-permute-start.6 = (bf16[1056,128]{1,0:T(8,128)(2,1)S(1)}, bf16[1056,128]{1,0:T(8,128)(2,1)S(1)}, u32[]{:S(2)}, u32[]{:S(2)}) collective-permute-start(bf16[1056,128]{1,0:T(8,128)(2,1)S(1)} %get-tuple-element.24.refs_0_), channel_id=1, source_target_pairs={{0,16},{8,24},{16,0},{24,8},{1,17},{9,25},{17,1},{25,9},{2,18},{10... | collective-permute-start | bytes 811016 | tf_op jit(solution)/shard_map/ppermute | solution.py:25
  11.0 2.0 %collective-permute-start.1 = (bf16[272,128]{1,0:T(8,128)(2,1)S(1)}, bf16[272,128]{1,0:T(8,128)(2,1)S(1)}, u32[]{:S(2)}, u32[]{:S(2)}) collective-permute-start(bf16[272,128]{1,0:T(8,128)(2,1)S(1)} %get-tuple-element.25.refs_0_), channel_id=1, source_target_pairs={{0,2},{1,3},{2,0},{3,1},{4,6},{5,7},{6,4},{7,5},{8,10},{9,11},{10,... | collective-permute-start | bytes 208904 | tf_op jit(solution)/shard_map/ppermute | solution.py:25
  13.0 3.7 %collective-permute-done.8.refs_0_ = bf16[1056,128]{1,0:T(8,128)(2,1)S(1)} collective-permute-done((bf16[1056,128]{1,0:T(8,128)(2,1)S(1)}, bf16[1056,128]{1,0:T(8,128)(2,1)S(1)}, u32[]{:S(2)}, u32[]{:S(2)}) %collective-permute-start.8) | collective-permute-done | bytes 270368 | tf_op jit(solution)/shard_map/ppermute | solution.py:25
  16.8 6.4 %collective-permute-done.6.refs_0_ = bf16[1056,128]{1,0:T(8,128)(2,1)S(1)} collective-permute-done((bf16[1056,128]{1,0:T(8,128)(2,1)S(1)}, bf16[1056,128]{1,0:T(8,128)(2,1)S(1)}, u32[]{:S(2)}, u32[]{:S(2)}) %collective-permute-start.6) | collective-permute-done | bytes 270368 | tf_op jit(solution)/shard_map/ppermute | solution.py:25
  23.2 2.6 %collective-permute-start.2 = (bf16[272,128]{1,0:T(8,128)(2,1)S(1)}, bf16[272,128]{1,0:T(8,128)(2,1)S(1)}, u32[]{:S(2)}, u32[]{:S(2)}) collective-permute-start(bf16[272,128]{1,0:T(8,128)(2,1)S(1)} %get-tuple-element.25.refs_0_), channel_id=1, source_target_pairs={{0,4},{1,5},{2,6},{3,7},{4,0},{5,1},{6,2},{7,3},{8,12},{9,13},{10,... | collective-permute-start | bytes 208904 | tf_op jit(solution)/shard_map/ppermute | solution.py:25
  26.0 4.2 %collective-permute-done.2.refs_2_ = bf16[272,128]{1,0:T(8,128)(2,1)S(1)} collective-permute-done((bf16[272,128]{1,0:T(8,128)(2,1)S(1)}, bf16[272,128]{1,0:T(8,128)(2,1)S(1)}, u32[]{:S(2)}, u32[]{:S(2)}) %collective-permute-start.2) | collective-permute-done | bytes 69664 | tf_op jit(solution)/shard_map/ppermute | solution.py:25
  30.2 3.5 %collective-permute-start.3 = (bf16[272,128]{1,0:T(8,128)(2,1)S(1)}, bf16[272,128]{1,0:T(8,128)(2,1)S(1)}, u32[]{:S(2)}, u32[]{:S(2)}) collective-permute-start(bf16[272,128]{1,0:T(8,128)(2,1)S(1)} %get-tuple-element.25.refs_0_), channel_id=1, source_target_pairs={{0,6},{1,7},{2,4},{3,5},{4,2},{5,3},{6,0},{7,1},{8,14},{9,15},{10,... | collective-permute-start | bytes 208904 | tf_op jit(solution)/shard_map/ppermute | solution.py:25
  33.7 2.6 %collective-permute-done.3.refs_3_ = bf16[272,128]{1,0:T(8,128)(2,1)S(1)} collective-permute-done((bf16[272,128]{1,0:T(8,128)(2,1)S(1)}, bf16[272,128]{1,0:T(8,128)(2,1)S(1)}, u32[]{:S(2)}, u32[]{:S(2)}) %collective-permute-start.3) | collective-permute-done | bytes 69664 | tf_op jit(solution)/shard_map/ppermute | solution.py:25
  36.4 2.1 %shard_map.96 = (f32[128,512]{1,0:T(8,128)S(1)}, bf16[128,512]{1,0:T(8,128)(2,1)S(1)}, f32[4,256,128]{2,1,0:T(8,128)S(1)}) custom-call(bf16[1056,128]{1,0:T(8,128)(2,1)S(1)} %get-tuple-element.24.refs_0_, bf16[1056,128]{1,0:T(8,128)(2,1)S(1)} %collective-permute-done.refs_1_, bf16[512,128]{1,0:T(8,128)(2,1)S(1)} %get-tuple-element.26.refs_2_, ...), custom_call_target="tpu_custom_call" | custom-call | flops 671088640 | bytes 1048576 | tf_op jit(solution)/shard_map/pallas_call | solution.py:186
  38.5 2.1 %shard_map.97 = (f32[128,512]{1,0:T(8,128)S(1)}, bf16[128,512]{1,0:T(8,128)(2,1)S(1)}, f32[4,256,128]{2,1,0:T(8,128)S(1)}) custom-call(bf16[1056,128]{1,0:T(8,128)(2,1)S(1)} %collective-permute-done.8.refs_0_, bf16[1056,128]{1,0:T(8,128)(2,1)S(1)} %collective-permute-done.9.refs_1_, bf16[512,128]{1,0:T(8,128)(2,1)S(1)} %get-tuple-element.26.refs_2_, ...), custom_call_target="tpu_custom_call" | custom-call | flops 671088640 | bytes 1048576 | tf_op jit(solution)/shard_map/pallas_call | solution.py:186
  40.6 2.1 %shard_map.98 = (f32[128,512]{1,0:T(8,128)S(1)}, bf16[128,512]{1,0:T(8,128)(2,1)S(1)}, f32[4,256,128]{2,1,0:T(8,128)S(1)}) custom-call(bf16[1056,128]{1,0:T(8,128)(2,1)S(1)} %collective-permute-done.6.refs_0_, bf16[1056,128]{1,0:T(8,128)(2,1)S(1)} %collective-permute-done.7.refs_1_, bf16[512,128]{1,0:T(8,128)(2,1)S(1)} %get-tuple-element.26.refs_2_, ...), custom_call_target="tpu_custom_call" | custom-call | flops 671088640 | bytes 1048576 | tf_op jit(solution)/shard_map/pallas_call | solution.py:186
  42.8 2.1 %shard_map.99 = (f32[128,512]{1,0:T(8,128)S(1)}, bf16[128,512]{1,0:T(8,128)(2,1)S(1)}, f32[1,256,128]{2,1,0:T(8,128)S(1)}, bf16[256,128]{1,0:T(8,128)(2,1)S(1)},...) custom-call(bf16[1056,128]{1,0:T(8,128)(2,1)S(1)} %collective-permute-done.4.refs_0_, ...), custom_call_target="tpu_custom_call" | custom-call | flops 671088640 | bytes 1048576 | tf_op jit(solution)/shard_map/pallas_call | solution.py:186
  44.9 0.5 collective-permute-start.10
  45.5 0.4 collective-permute-start.11
  45.9 0.3 collective-permute-done.15
  46.3 1.6 %collective-permute-start.16 = (bf16[128,512]{1,0:T(8,128)(2,1)S(1)}, bf16[128,512]{1,0:T(8,128)(2,1)S(1)}, u32[]{:S(2)}, u32[]{:S(2)}) collective-permute-start(bf16[128,512]{1,0:T(8,128)(2,1)S(1)} %add_convert_fusion), channel_id=1, source_target_pairs={{0,24},{8,16},{16,8},{24,0},{1,25},{9,17},{17,9},{25,1},{2,26},{10... | collective-permute-start | bytes 393224 | tf_op jit(solution)/shard_map/ppermute | solution.py:25
  47.9 0.5 collective-permute-start.14
  48.4 1.6 %collective-permute-start.12 = (bf16[128,512]{1,0:T(8,128)(2,1)S(1)}, bf16[128,512]{1,0:T(8,128)(2,1)S(1)}, u32[]{:S(2)}, u32[]{:S(2)}) collective-permute-start(bf16[128,512]{1,0:T(8,128)(2,1)S(1)} %add_convert_fusion.2), channel_id=1, source_target_pairs={{0,8},{8,0},{16,24},{24,16},{1,9},{9,1},{17,25},{25,17},{2,10},{10... | collective-permute-start | bytes 393224 | tf_op jit(solution)/shard_map/ppermute | solution.py:25
  50.1 3.7 %collective-permute-start.18 = (bf16[256,128]{1,0:T(8,128)(2,1)S(1)}, bf16[256,128]{1,0:T(8,128)(2,1)S(1)}, u32[]{:S(2)}, u32[]{:S(2)}) collective-permute-start(bf16[256,128]{1,0:T(8,128)(2,1)S(1)} %get-tuple-element.43), channel_id=1, source_target_pairs={{0,4},{1,5},{2,6},{3,7},{4,0},{5,1},{6,2},{7,3},{8,12},{9,13},{10,... | collective-permute-start | bytes 196616 | tf_op jit(solution)/shard_map/ppermute | solution.py:25
  53.8 0.4 collective-permute-start.19
  54.1 3.8 %collective-permute-done.18.refs_5_ = bf16[256,128]{1,0:T(8,128)(2,1)S(1)} collective-permute-done((bf16[256,128]{1,0:T(8,128)(2,1)S(1)}, bf16[256,128]{1,0:T(8,128)(2,1)S(1)}, u32[]{:S(2)}, u32[]{:S(2)}) %collective-permute-start.18) | collective-permute-done | bytes 65568 | tf_op jit(solution)/shard_map/ppermute | solution.py:25
  58.0 1.9 %collective-permute-done.19.refs_6_ = bf16[256,128]{1,0:T(8,128)(2,1)S(1)} collective-permute-done((bf16[256,128]{1,0:T(8,128)(2,1)S(1)}, bf16[256,128]{1,0:T(8,128)(2,1)S(1)}, u32[]{:S(2)}, u32[]{:S(2)}) %collective-permute-start.19) | collective-permute-done | bytes 65568 | tf_op jit(solution)/shard_map/ppermute | solution.py:25
  59.8 0.8 %shard_map.100 = (bf16[128,512]{1,0:T(8,128)(2,1)}, bf16[128,128]{1,0:T(8,128)(2,1)}, bf16[128,128]{1,0:T(8,128)(2,1)}) custom-call(f32[128,512]{1,0:T(8,128)S(1)} %get-tuple-element.30.dq_own, f32[1,256,128]{2,1,0:T(8,128)S(1)} %get-tuple-element.34.acc, bf16[128,512]{1,0:T(8,128)(2,1)S(1)} %collective-permute-done.10.refs_0_, ...), custom_call_target="tpu_custom_call" | custom-call | tf_op jit(solution)/shard_map/pallas_call | solution.py:250
  (32 shorter events, 0.6 us)
Async XLA Ops:
  0.6 0.7 %copy-start.6 = (s32[128]{0:T(128)S(1)}, s32[128]{0:T(128)}, u32[]{:S(2)}) copy-start(s32[128]{0:T(128)} %param.13) | copy-start | bytes 1540
  1.3 0.9 %copy-start = (bf16[128,512]{1,0:T(8,128)(2,1)S(1)}, bf16[128,512]{1,0:T(8,128)(2,1)}, u32[]{:S(2)}) copy-start(bf16[128,512]{1,0:T(8,128)(2,1)} %q_ref.1) | copy-start | bytes 393220
  2.2 0.9 %copy-start.1 = (bf16[128,512]{1,0:T(8,128)(2,1)S(1)}, bf16[128,512]{1,0:T(8,128)(2,1)}, u32[]{:S(2)}) copy-start(bf16[128,512]{1,0:T(8,128)(2,1)} %o_ref.1) | copy-start | bytes 393220
  3.1 0.9 %copy-start.2 = (bf16[128,512]{1,0:T(8,128)(2,1)S(1)}, bf16[128,512]{1,0:T(8,128)(2,1)}, u32[]{:S(2)}) copy-start(bf16[128,512]{1,0:T(8,128)(2,1)} %g_ref.1) | copy-start | bytes 393220
  4.0 0.8 %copy-start.3 = (bf16[128,128]{1,0:T(8,128)(2,1)S(1)}, bf16[128,128]{1,0:T(8,128)(2,1)}, u32[]{:S(2)}) copy-start(bf16[128,128]{1,0:T(8,128)(2,1)} %k_ref.1) | copy-start | bytes 98308
  4.8 0.8 %copy-start.4 = (bf16[128,128]{1,0:T(8,128)(2,1)S(1)}, bf16[128,128]{1,0:T(8,128)(2,1)}, u32[]{:S(2)}) copy-start(bf16[128,128]{1,0:T(8,128)(2,1)} %v_ref.1) | copy-start | bytes 98308
  5.5 0.7 %copy-start.5 = (f32[4,128]{1,0:T(4,128)S(1)}, f32[4,128]{1,0:T(4,128)}, u32[]{:S(2)}) copy-start(f32[4,128]{1,0:T(4,128)} %lse_ref.1) | copy-start | bytes 6148
  6.5 10.3 %collective-permute-start.8 = (bf16[1056,128]{1,0:T(8,128)(2,1)S(1)}, bf16[1056,128]{1,0:T(8,128)(2,1)S(1)}, u32[]{:S(2)}, u32[]{:S(2)}) collective-permute-start(bf16[1056,128]{1,0:T(8,128)(2,1)S(1)} %get-tuple-element.24.refs_0_), channel_id=1, source_target_pairs={{0,8},{8,0},{16,24},{24,16},{1,9},{9,1},{17,25},{25,17},{2,10},{10... | collective-permute-start | bytes 811016 | tf_op jit(solution)/shard_map/ppermute | solution.py:25
  9.5 13.7 %collective-permute-start.6 = (bf16[1056,128]{1,0:T(8,128)(2,1)S(1)}, bf16[1056,128]{1,0:T(8,128)(2,1)S(1)}, u32[]{:S(2)}, u32[]{:S(2)}) collective-permute-start(bf16[1056,128]{1,0:T(8,128)(2,1)S(1)} %get-tuple-element.24.refs_0_), channel_id=1, source_target_pairs={{0,16},{8,24},{16,0},{24,8},{1,17},{9,25},{17,1},{25,9},{2,18},{10... | collective-permute-start | bytes 811016 | tf_op jit(solution)/shard_map/ppermute | solution.py:25
  11.0 14.8 %collective-permute-start.4 = (bf16[1056,128]{1,0:T(8,128)(2,1)S(1)}, bf16[1056,128]{1,0:T(8,128)(2,1)S(1)}, u32[]{:S(2)}, u32[]{:S(2)}) collective-permute-start(bf16[1056,128]{1,0:T(8,128)(2,1)S(1)} %get-tuple-element.24.refs_0_), channel_id=1, source_target_pairs={{0,24},{8,16},{16,8},{24,0},{1,25},{9,17},{17,9},{25,1},{2,26},{10... | collective-permute-start | bytes 811016 | tf_op jit(solution)/shard_map/ppermute | solution.py:25
  11.0 25.4 %collective-permute-start = (bf16[1056,128]{1,0:T(8,128)(2,1)S(1)}, bf16[1056,128]{1,0:T(8,128)(2,1)S(1)}, u32[]{:S(2)}, u32[]{:S(2)}) collective-permute-start(bf16[1056,128]{1,0:T(8,128)(2,1)S(1)} %get-tuple-element.24.refs_0_), channel_id=1, source_target_pairs={{0,1},{1,0},{2,3},{3,2},{4,5},{5,4},{6,7},{7,6},{8,9},{9,8},{10,11... | collective-permute-start | bytes 811016 | tf_op jit(solution)/shard_map/ppermute | solution.py:25
  11.0 12.2 %collective-permute-start.1 = (bf16[272,128]{1,0:T(8,128)(2,1)S(1)}, bf16[272,128]{1,0:T(8,128)(2,1)S(1)}, u32[]{:S(2)}, u32[]{:S(2)}) collective-permute-start(bf16[272,128]{1,0:T(8,128)(2,1)S(1)} %get-tuple-element.25.refs_0_), channel_id=1, source_target_pairs={{0,2},{1,3},{2,0},{3,1},{4,6},{5,7},{6,4},{7,5},{8,10},{9,11},{10,... | collective-permute-start | bytes 208904 | tf_op jit(solution)/shard_map/ppermute | solution.py:25
  16.8 21.8 %collective-permute-start.9 = (bf16[1056,128]{1,0:T(8,128)(2,1)S(1)}, bf16[1056,128]{1,0:T(8,128)(2,1)S(1)}, u32[]{:S(2)}, u32[]{:S(2)}) collective-permute-start(bf16[1056,128]{1,0:T(8,128)(2,1)S(1)} %collective-permute-done.8.refs_0_), channel_id=1, source_target_pairs={{0,1},{1,0},{2,3},{3,2},{4,5},{5,4},{6,7},{7,6},{8,9},{9,8},{10,11... | collective-permute-start | bytes 811016 | tf_op jit(solution)/shard_map/ppermute | solution.py:25
  23.2 17.4 %collective-permute-start.7 = (bf16[1056,128]{1,0:T(8,128)(2,1)S(1)}, bf16[1056,128]{1,0:T(8,128)(2,1)S(1)}, u32[]{:S(2)}, u32[]{:S(2)}) collective-permute-start(bf16[1056,128]{1,0:T(8,128)(2,1)S(1)} %collective-permute-done.6.refs_0_), channel_id=1, source_target_pairs={{0,1},{1,0},{2,3},{3,2},{4,5},{5,4},{6,7},{7,6},{8,9},{9,8},{10,11... | collective-permute-start | bytes 811016 | tf_op jit(solution)/shard_map/ppermute | solution.py:25
  23.2 7.0 %collective-permute-start.2 = (bf16[272,128]{1,0:T(8,128)(2,1)S(1)}, bf16[272,128]{1,0:T(8,128)(2,1)S(1)}, u32[]{:S(2)}, u32[]{:S(2)}) collective-permute-start(bf16[272,128]{1,0:T(8,128)(2,1)S(1)} %get-tuple-element.25.refs_0_), channel_id=1, source_target_pairs={{0,4},{1,5},{2,6},{3,7},{4,0},{5,1},{6,2},{7,3},{8,12},{9,13},{10,... | collective-permute-start | bytes 208904 | tf_op jit(solution)/shard_map/ppermute | solution.py:25
  25.8 16.9 %collective-permute-start.5 = (bf16[1056,128]{1,0:T(8,128)(2,1)S(1)}, bf16[1056,128]{1,0:T(8,128)(2,1)S(1)}, u32[]{:S(2)}, u32[]{:S(2)}) collective-permute-start(bf16[1056,128]{1,0:T(8,128)(2,1)S(1)} %collective-permute-done.4.refs_0_), channel_id=1, source_target_pairs={{0,1},{1,0},{2,3},{3,2},{4,5},{5,4},{6,7},{7,6},{8,9},{9,8},{10,11... | collective-permute-start | bytes 811016 | tf_op jit(solution)/shard_map/ppermute | solution.py:25
  30.2 6.1 %collective-permute-start.3 = (bf16[272,128]{1,0:T(8,128)(2,1)S(1)}, bf16[272,128]{1,0:T(8,128)(2,1)S(1)}, u32[]{:S(2)}, u32[]{:S(2)}) collective-permute-start(bf16[272,128]{1,0:T(8,128)(2,1)S(1)} %get-tuple-element.25.refs_0_), channel_id=1, source_target_pairs={{0,6},{1,7},{2,4},{3,5},{4,2},{5,3},{6,0},{7,1},{8,14},{9,15},{10,... | collective-permute-start | bytes 208904 | tf_op jit(solution)/shard_map/ppermute | solution.py:25
  44.9 1.4 %collective-permute-start.15 = (bf16[128,512]{1,0:T(8,128)(2,1)S(1)}, bf16[128,512]{1,0:T(8,128)(2,1)S(1)}, u32[]{:S(2)}, u32[]{:S(2)}) collective-permute-start(bf16[128,512]{1,0:T(8,128)(2,1)S(1)} %get-tuple-element.41), channel_id=1, source_target_pairs={{0,1},{1,0},{2,3},{3,2},{4,5},{5,4},{6,7},{7,6},{8,9},{9,8},{10,11... | collective-permute-start | bytes 393224 | tf_op jit(solution)/shard_map/ppermute | solution.py:25
  44.9 5.1 %collective-permute-start.10 = (bf16[128,512]{1,0:T(8,128)(2,1)S(1)}, bf16[128,512]{1,0:T(8,128)(2,1)S(1)}, u32[]{:S(2)}, u32[]{:S(2)}) collective-permute-start(bf16[128,512]{1,0:T(8,128)(2,1)S(1)} %get-tuple-element.35), channel_id=1, source_target_pairs={{0,1},{1,0},{2,3},{3,2},{4,5},{5,4},{6,7},{7,6},{8,9},{9,8},{10,11... | collective-permute-start | bytes 393224 | tf_op jit(solution)/shard_map/ppermute | solution.py:25
  45.4 2.4 %collective-permute-start.13 = (bf16[128,512]{1,0:T(8,128)(2,1)S(1)}, bf16[128,512]{1,0:T(8,128)(2,1)S(1)}, u32[]{:S(2)}, u32[]{:S(2)}) collective-permute-start(bf16[128,512]{1,0:T(8,128)(2,1)S(1)} %get-tuple-element.39), channel_id=1, source_target_pairs={{0,1},{1,0},{2,3},{3,2},{4,5},{5,4},{6,7},{7,6},{8,9},{9,8},{10,11... | collective-permute-start | bytes 393224 | tf_op jit(solution)/shard_map/ppermute | solution.py:25
  45.5 2.9 %collective-permute-start.11 = (bf16[128,512]{1,0:T(8,128)(2,1)S(1)}, bf16[128,512]{1,0:T(8,128)(2,1)S(1)}, u32[]{:S(2)}, u32[]{:S(2)}) collective-permute-start(bf16[128,512]{1,0:T(8,128)(2,1)S(1)} %get-tuple-element.37), channel_id=1, source_target_pairs={{0,1},{1,0},{2,3},{3,2},{4,5},{5,4},{6,7},{7,6},{8,9},{9,8},{10,11... | collective-permute-start | bytes 393224 | tf_op jit(solution)/shard_map/ppermute | solution.py:25
  45.9 7.8 %collective-permute-start.17 = (bf16[256,128]{1,0:T(8,128)(2,1)S(1)}, bf16[256,128]{1,0:T(8,128)(2,1)S(1)}, u32[]{:S(2)}, u32[]{:S(2)}) collective-permute-start(bf16[256,128]{1,0:T(8,128)(2,1)S(1)} %get-tuple-element.42), channel_id=1, source_target_pairs={{0,2},{1,3},{2,0},{3,1},{4,6},{5,7},{6,4},{7,5},{8,10},{9,11},{10,... | collective-permute-start | bytes 196616 | tf_op jit(solution)/shard_map/ppermute | solution.py:25
  46.3 13.5 %collective-permute-start.16 = (bf16[128,512]{1,0:T(8,128)(2,1)S(1)}, bf16[128,512]{1,0:T(8,128)(2,1)S(1)}, u32[]{:S(2)}, u32[]{:S(2)}) collective-permute-start(bf16[128,512]{1,0:T(8,128)(2,1)S(1)} %add_convert_fusion), channel_id=1, source_target_pairs={{0,24},{8,16},{16,8},{24,0},{1,25},{9,17},{17,9},{25,1},{2,26},{10... | collective-permute-start | bytes 393224 | tf_op jit(solution)/shard_map/ppermute | solution.py:25
  47.9 11.9 %collective-permute-start.14 = (bf16[128,512]{1,0:T(8,128)(2,1)S(1)}, bf16[128,512]{1,0:T(8,128)(2,1)S(1)}, u32[]{:S(2)}, u32[]{:S(2)}) collective-permute-start(bf16[128,512]{1,0:T(8,128)(2,1)S(1)} %add_convert_fusion.1), channel_id=1, source_target_pairs={{0,16},{8,24},{16,0},{24,8},{1,17},{9,25},{17,1},{25,9},{2,18},{10... | collective-permute-start | bytes 393224 | tf_op jit(solution)/shard_map/ppermute | solution.py:25
  48.4 11.4 %collective-permute-start.12 = (bf16[128,512]{1,0:T(8,128)(2,1)S(1)}, bf16[128,512]{1,0:T(8,128)(2,1)S(1)}, u32[]{:S(2)}, u32[]{:S(2)}) collective-permute-start(bf16[128,512]{1,0:T(8,128)(2,1)S(1)} %add_convert_fusion.2), channel_id=1, source_target_pairs={{0,8},{8,0},{16,24},{24,16},{1,9},{9,1},{17,25},{25,17},{2,10},{10... | collective-permute-start | bytes 393224 | tf_op jit(solution)/shard_map/ppermute | solution.py:25
  50.1 7.9 %collective-permute-start.18 = (bf16[256,128]{1,0:T(8,128)(2,1)S(1)}, bf16[256,128]{1,0:T(8,128)(2,1)S(1)}, u32[]{:S(2)}, u32[]{:S(2)}) collective-permute-start(bf16[256,128]{1,0:T(8,128)(2,1)S(1)} %get-tuple-element.43), channel_id=1, source_target_pairs={{0,4},{1,5},{2,6},{3,7},{4,0},{5,1},{6,2},{7,3},{8,12},{9,13},{10,... | collective-permute-start | bytes 196616 | tf_op jit(solution)/shard_map/ppermute | solution.py:25
  53.8 6.1 %collective-permute-start.19 = (bf16[256,128]{1,0:T(8,128)(2,1)S(1)}, bf16[256,128]{1,0:T(8,128)(2,1)S(1)}, u32[]{:S(2)}, u32[]{:S(2)}) collective-permute-start(bf16[256,128]{1,0:T(8,128)(2,1)S(1)} %get-tuple-element.44), channel_id=1, source_target_pairs={{0,6},{1,7},{2,4},{3,5},{4,2},{5,3},{6,0},{7,1},{8,14},{9,15},{10,... | collective-permute-start | bytes 196616 | tf_op jit(solution)/shard_map/ppermute | solution.py:25

commit v3 on v2

--- a/solution.py
+++ b/solution.py
@@ -25,6 +25,10 @@
     return lax.ppermute(block, axis, pairs)
 
 
+def after(x, *first):
+    return lax.optimization_barrier((x, *first))[0]
+
+
 def three_parts(x):
     hi = x.astype(BF)
     rest = x - hi.astype(F32)
@@ -37,30 +41,38 @@
     return lax.dot_general(a, b, dims, preferred_element_type=F32)
 
 
-def pack_kernel(q_ref, k_ref, v_ref, o_ref, g_ref, lse_ref, pos_ref, x_ref, kv_ref):
+def pack_kernel(q_ref, k_ref, v_ref, o_ref, g_ref, lse_ref, pos_ref, x_ref, kv_ref, o_s, lse_s, pos_s, sems):
     rows, width = k_ref.shape
     heads = q_ref.shape[1] // width
+    moves = [(lse_ref, lse_s), (pos_ref, pos_s), (o_ref, o_s)]
+    for h in range(heads):
+        cols = pl.ds(h * width, width)
+        moves.append((g_ref.at[:, cols], x_ref.at[pl.ds((heads + h) * rows, rows), :]))
+    for h in range(heads):
+        cols = pl.ds(h * width, width)
+        moves.append((q_ref.at[:, cols], x_ref.at[pl.ds(h * rows, rows), :]))
+    moves.append((k_ref, kv_ref.at[pl.ds(0, rows), :]))
+    moves.append((v_ref, kv_ref.at[pl.ds(rows, rows), :]))
+    copies = [pltpu.make_async_copy(a, b, sems.at[n]) for n, (a, b) in enumerate(moves)]
+    for copy in copies:
+        copy.start()
+    for copy in copies[: 3 + heads]:
+        copy.wait()
     ones = jnp.ones((8, width), BF)
     deltas = []
     for h in range(heads):
-        cols = slice(h * width, (h + 1) * width)
-        q = q_ref[:, cols]
-        g = g_ref[:, cols]
-        x_ref[h * rows : (h + 1) * rows, :] = q
-        x_ref[(heads + h) * rows : (heads + h + 1) * rows, :] = g
-        prod = g.astype(F32) * o_ref[:, cols].astype(F32)
+        g = x_ref[(heads + h) * rows : (heads + h + 1) * rows, :]
+        prod = g.astype(F32) * o_s[:, h * width : (h + 1) * width].astype(F32)
         hi = prod.astype(BF)
         low = (prod - hi.astype(F32)).astype(BF)
         deltas.append((dot(ones, hi, NT) + dot(ones, low, NT))[:1])
-    run = (pos_ref[...] // RUN).astype(F32)
+    run = (pos_s[...] // RUN).astype(F32)
     extra = (
-        three_parts(lse_ref[...] * LOG2E)
+        three_parts(lse_s[...] * LOG2E)
         + three_parts(jnp.concatenate(deltas, axis=0))
         + [run.astype(BF), jnp.zeros((32 - 6 * heads - 1, rows), BF)]
     )
     x_ref[2 * heads * rows :, :] = jnp.concatenate([e.astype(F32) for e in extra], axis=0).astype(BF)
-    kv_ref[:rows, :] = k_ref[...]
-    kv_ref[rows : 2 * rows, :] = v_ref[...]
     lane = lax.broadcasted_iota(jnp.int32, run.shape, 1)
     ids = [
         jnp.max(jnp.where(lane == r * RUN, run, 0.0), axis=1, keepdims=True)
@@ -69,6 +81,8 @@
     wide = [jnp.broadcast_to(i, (1, width)) for i in ids]
     wide.append(jnp.zeros((16 - len(ids), width), F32))
     kv_ref[2 * rows :, :] = jnp.concatenate(wide, axis=0).astype(BF)
+    for copy in copies[3 + heads :]:
+        copy.wait()
 
 
 def stack_kernel(rows, *refs):
@@ -211,14 +225,24 @@
     x, kv = pl.pallas_call(
         pack_kernel,
         out_shape=(sds((2 * hr + 32, width), BF), sds((2 * rows + 16, width), BF)),
-        in_specs=[VMEM] * 7,
+        in_specs=[pl.BlockSpec(memory_space=pltpu.HBM)] * 7,
         out_specs=(VMEM, VMEM),
+        scratch_shapes=[
+            pltpu.VMEM(out.shape, BF),
+            pltpu.VMEM(lse.shape, F32),
+            pltpu.VMEM((1, rows), jnp.int32),
+            pltpu.SemaphoreType.DMA((5 + 2 * heads,)),
+        ],
         compiler_params=SMALL,
     )(query, key, value, out, grad_out, lse, positions[None, :])
 
-    xs = [x] + [swapped(x, "outer", s) for s in range(1, nq)]
-    kvs = [kv] + [swapped(kv, "inner", 2 * s) for s in range(1, nz)]
-    xs_sib = [swapped(block, "inner", 1) for block in xs]
+    x_sib = swapped(x, "inner", 1)
+    kvs = [kv] + [None] * (nz - 1)
+    for s in range(nz - 1, 1, -1):
+        kvs[s] = swapped(kv, "inner", 2 * s)
+    kvs[1] = swapped(after(kv, x_sib), "inner", 2)
+    xs = [x] + [swapped(x if s < 3 else after(x, kvs[1]), "outer", s) for s in range(1, nq)]
+    xs_sib = [x_sib] + [swapped(block, "inner", 1) for block in xs[1:]]
     per = rows // RUN
     stacked = pl.pallas_call(
         functools.partial(stack_kernel, rows),
@@ -235,16 +259,19 @@
 
     acc = None
     got = []
+    others = []
     for s in range(nq):
+        block = after(xs[s], others[s - 2]) if s > 1 else xs[s]
         dq, dq_sib, acc, *far = pair_call(
-            xs[s], xs_sib[s], stacked, acc, s == nq - 1, rows, heads, scale
+            block, xs_sib[s], stacked, acc, s == nq - 1, rows, heads, scale
         )
-        other = swapped(dq_sib, "inner", 1)
+        others.append(swapped(dq_sib, "inner", 1))
         if s == 0:
             dq_own = dq
-            got.append(other)
+            got.append(others[0])
         else:
-            got.append(swapped((dq + other.astype(F32)).astype(BF), "outer", s))
+            total = (dq + others[s].astype(F32)).astype(BF)
+            got.append(swapped(total, "outer", s))
     dkv_got = [swapped(far[s - 1], "inner", 2 * s) for s in range(1, nz)]
 
     return pl.pallas_call(

time: 61 us -> 57.4 us (0.941)
  waiting for transfers between devices: 23 us -> 18.7 us
    ppermute x20, waiting for transfers between devices: 23 us -> 18.7 us  [swapped(): return lax.ppermute(block, axis, pairs)]
  transfers between devices with their start and end apart: 20 -> 20, of which waited for: 7 -> 7; matrix products, arithmetic and copies ran while one was open for 0% -> 0% of each run, Pallas kernels for 11% -> 15%
where the time goes in v3:
time: 57.4 us; the launch traced here: 57.1 us
  starting transfers between devices  22.1 us (39%)
  waiting for transfers between devices  18.7 us (33%)
  Pallas kernels  9.93 us (17%)
  local copies, waits for them, and re-layouts  5.56 us (10%)
  between operations  0.73 us (1%)
    ppermute x20, starting transfers between devices, swapped(): return lax.ppermute(block, axis, pairs)  22.1 us
    ppermute x20, waiting for transfers between devices, swapped(): return lax.ppermute(block, axis, pairs)  18.7 us
    pallas_call x4, Pallas kernels, pair_call(): pl.pallas_call(functools.partial(pair_kernel, first, last, rows, heads, s...  8.33 us
    unnamed x14, local copies, waits for them, and re-layouts  5.56 us
  transfers between devices with their start and end apart: 20, of which 7 were waited for; matrix products, arithmetic and copies ran while one was open for 0% of the time, Pallas kernels for 15%

profile of v3, /device:TPU:0, one launch (start us, length us, event | category | flops | bytes accessed | tf_op | source)
XLA Modules:
  0.0 57.1 jit_solution(3367855904448844559)
XLA Ops:
  0.6 0.6 %copy-done.6 = s32[128]{0:T(128)S(1)} copy-done((s32[128]{0:T(128)S(1)}, s32[128]{0:T(128)}, u32[]{:S(2)}) %copy-start.6) | copy-done | bytes 536
  1.3 0.9 %copy-done = bf16[128,512]{1,0:T(8,128)(2,1)S(1)} copy-done((bf16[128,512]{1,0:T(8,128)(2,1)S(1)}, bf16[128,512]{1,0:T(8,128)(2,1)}, u32[]{:S(2)}) %copy-start) | copy-done | bytes 131096
  2.2 0.9 %copy-done.1 = bf16[128,512]{1,0:T(8,128)(2,1)S(1)} copy-done((bf16[128,512]{1,0:T(8,128)(2,1)S(1)}, bf16[128,512]{1,0:T(8,128)(2,1)}, u32[]{:S(2)}) %copy-start.1) | copy-done | bytes 131096
  3.1 0.9 %copy-done.2 = bf16[128,512]{1,0:T(8,128)(2,1)S(1)} copy-done((bf16[128,512]{1,0:T(8,128)(2,1)S(1)}, bf16[128,512]{1,0:T(8,128)(2,1)}, u32[]{:S(2)}) %copy-start.2) | copy-done | bytes 131096
  4.0 0.8 %copy-done.3 = bf16[128,128]{1,0:T(8,128)(2,1)S(1)} copy-done((bf16[128,128]{1,0:T(8,128)(2,1)S(1)}, bf16[128,128]{1,0:T(8,128)(2,1)}, u32[]{:S(2)}) %copy-start.3) | copy-done | bytes 32792
  4.8 0.8 %copy-done.4 = bf16[128,128]{1,0:T(8,128)(2,1)S(1)} copy-done((bf16[128,128]{1,0:T(8,128)(2,1)S(1)}, bf16[128,128]{1,0:T(8,128)(2,1)}, u32[]{:S(2)}) %copy-start.4) | copy-done | bytes 32792
  5.5 0.7 %copy-done.5 = f32[4,128]{1,0:T(4,128)S(1)} copy-done((f32[4,128]{1,0:T(4,128)S(1)}, f32[4,128]{1,0:T(4,128)}, u32[]{:S(2)}) %copy-start.5) | copy-done | bytes 2072
  6.2 0.7 %shard_map.94 = (bf16[1056,128]{1,0:T(8,128)(2,1)S(1)}, bf16[272,128]{1,0:T(8,128)(2,1)S(1)}) custom-call(bf16[128,512]{1,0:T(8,128)(2,1)S(1)} %copy-done, bf16[128,128]{1,0:T(8,128)(2,1)S(1)} %copy-done.3, bf16[128,128]{1,0:T(8,128)(2,1)S(1)} %copy-done.4, bf16[128,512]{1,0:T(8,128)(2,1)S(1)} %copy-done.1, bf16[128,512]{1,0:T(8,128)(2,1)S(1)} %copy-done.2, ...), custom_call_target="tpu_custom_call" | custom-call | tf_op jit(solution)/shard_map/pallas_call | solution.py:225
  6.9 3.0 %collective-permute-start.5 = (bf16[1056,128]{1,0:T(8,128)(2,1)S(1)}, bf16[1056,128]{1,0:T(8,128)(2,1)S(1)}, u32[]{:S(2)}, u32[]{:S(2)}) collective-permute-start(bf16[1056,128]{1,0:T(8,128)(2,1)S(1)} %get-tuple-element.36.refs_0_), channel_id=1, source_target_pairs={{0,8},{8,0},{16,24},{24,16},{1,9},{9,1},{17,25},{25,17},{2,10},{10... | collective-permute-start | bytes 811016 | tf_op jit(solution)/shard_map/ppermute | solution.py:25
  9.9 1.5 %collective-permute-start.9 = (bf16[1056,128]{1,0:T(8,128)(2,1)S(1)}, bf16[1056,128]{1,0:T(8,128)(2,1)S(1)}, u32[]{:S(2)}, u32[]{:S(2)}) collective-permute-start(bf16[1056,128]{1,0:T(8,128)(2,1)S(1)} %get-tuple-element.36.refs_0_), channel_id=1, source_target_pairs={{0,16},{8,24},{16,0},{24,8},{1,17},{9,25},{17,1},{25,9},{2,18},{10... | collective-permute-start | bytes 811016 | tf_op jit(solution)/shard_map/ppermute | solution.py:25
  11.4 5.0 %collective-permute-done.5.refs_0_ = bf16[1056,128]{1,0:T(8,128)(2,1)S(1)} collective-permute-done((bf16[1056,128]{1,0:T(8,128)(2,1)S(1)}, bf16[1056,128]{1,0:T(8,128)(2,1)S(1)}, u32[]{:S(2)}, u32[]{:S(2)}) %collective-permute-start.5) | collective-permute-done | bytes 270368 | tf_op jit(solution)/shard_map/ppermute | solution.py:25
  16.4 2.8 %collective-permute-start.2 = (bf16[272,128]{1,0:T(8,128)(2,1)S(1)}, bf16[272,128]{1,0:T(8,128)(2,1)S(1)}, u32[]{:S(2)}, u32[]{:S(2)}) collective-permute-start(bf16[272,128]{1,0:T(8,128)(2,1)S(1)} %get-tuple-element.30.refs_0_), channel_id=1, source_target_pairs={{0,4},{1,5},{2,6},{3,7},{4,0},{5,1},{6,2},{7,3},{8,12},{9,13},{10,... | collective-permute-start | bytes 208904 | tf_op jit(solution)/shard_map/ppermute | solution.py:25
  19.2 1.3 %collective-permute-start.3 = (bf16[272,128]{1,0:T(8,128)(2,1)S(1)}, bf16[272,128]{1,0:T(8,128)(2,1)S(1)}, u32[]{:S(2)}, u32[]{:S(2)}) collective-permute-start(bf16[272,128]{1,0:T(8,128)(2,1)S(1)} %get-tuple-element.30.refs_0_), channel_id=1, source_target_pairs={{0,6},{1,7},{2,4},{3,5},{4,2},{5,3},{6,0},{7,1},{8,14},{9,15},{10,... | collective-permute-start | bytes 208904 | tf_op jit(solution)/shard_map/ppermute | solution.py:25
  20.8 3.0 %collective-permute-done.2.refs_2_ = bf16[272,128]{1,0:T(8,128)(2,1)S(1)} collective-permute-done((bf16[272,128]{1,0:T(8,128)(2,1)S(1)}, bf16[272,128]{1,0:T(8,128)(2,1)S(1)}, u32[]{:S(2)}, u32[]{:S(2)}) %collective-permute-start.2) | collective-permute-done | bytes 69664 | tf_op jit(solution)/shard_map/ppermute | solution.py:25
  23.8 2.2 %collective-permute-done.3.refs_3_ = bf16[272,128]{1,0:T(8,128)(2,1)S(1)} collective-permute-done((bf16[272,128]{1,0:T(8,128)(2,1)S(1)}, bf16[272,128]{1,0:T(8,128)(2,1)S(1)}, u32[]{:S(2)}, u32[]{:S(2)}) %collective-permute-start.3) | collective-permute-done | bytes 69664 | tf_op jit(solution)/shard_map/ppermute | solution.py:25
  26.0 0.4 collective-permute-done.1.refs_1_
  26.5 2.1 %shard_map.96 = (f32[128,512]{1,0:T(8,128)S(1)}, bf16[128,512]{1,0:T(8,128)(2,1)S(1)}, f32[4,256,128]{2,1,0:T(8,128)S(1)}) custom-call(bf16[1056,128]{1,0:T(8,128)(2,1)S(1)} %get-tuple-element.36.refs_0_, bf16[1056,128]{1,0:T(8,128)(2,1)S(1)} %collective-permute-done.refs_1_, bf16[512,128]{1,0:T(8,128)(2,1)S(1)} %get-tuple-element.31.refs_2_, ...), custom_call_target="tpu_custom_call" | custom-call | flops 671088640 | bytes 1048576 | tf_op jit(solution)/shard_map/pallas_call | solution.py:200
  28.7 2.6 %collective-permute-start.4 = (bf16[1056,128]{1,0:T(8,128)(2,1)S(1)}, bf16[1056,128]{1,0:T(8,128)(2,1)S(1)}, u32[]{:S(2)}, u32[]{:S(2)}) collective-permute-start(bf16[1056,128]{1,0:T(8,128)(2,1)S(1)} %get-tuple-element.36.refs_0_), channel_id=1, source_target_pairs={{0,24},{8,16},{16,8},{24,0},{1,25},{9,17},{17,9},{25,1},{2,26},{10... | collective-permute-start | bytes 811016 | tf_op jit(solution)/shard_map/ppermute | solution.py:25
  31.3 2.1 %shard_map.97 = (f32[128,512]{1,0:T(8,128)S(1)}, bf16[128,512]{1,0:T(8,128)(2,1)S(1)}, f32[4,256,128]{2,1,0:T(8,128)S(1)}) custom-call(bf16[1056,128]{1,0:T(8,128)(2,1)S(1)} %collective-permute-done.5.refs_0_, bf16[1056,128]{1,0:T(8,128)(2,1)S(1)} %collective-permute-done.6.refs_1_, bf16[512,128]{1,0:T(8,128)(2,1)S(1)} %get-tuple-element.31.refs_2_, ...), custom_call_target="tpu_custom_call" | custom-call | flops 671088640 | bytes 1048576 | tf_op jit(solution)/shard_map/pallas_call | solution.py:200
  33.6 2.1 %shard_map.98 = (f32[128,512]{1,0:T(8,128)S(1)}, bf16[128,512]{1,0:T(8,128)(2,1)S(1)}, f32[4,256,128]{2,1,0:T(8,128)S(1)}) custom-call(bf16[1056,128]{1,0:T(8,128)(2,1)S(1)} %collective-permute-done.9.refs_0_, bf16[1056,128]{1,0:T(8,128)(2,1)S(1)} %collective-permute-done.11.refs_1_, bf16[512,128]{1,0:T(8,128)(2,1)S(1)} %get-tuple-element.31.refs_2_, ...), custom_call_target="tpu_custom_call" | custom-call | flops 671088640 | bytes 1048576 | tf_op jit(solution)/shard_map/pallas_call | solution.py:200
  35.7 0.4 collective-permute-start.13
  36.1 2.4 %collective-permute-done.4.refs_0_ = bf16[1056,128]{1,0:T(8,128)(2,1)S(1)} collective-permute-done((bf16[1056,128]{1,0:T(8,128)(2,1)S(1)}, bf16[1056,128]{1,0:T(8,128)(2,1)S(1)}, u32[]{:S(2)}, u32[]{:S(2)}) %collective-permute-start.4) | collective-permute-done | bytes 270368 | tf_op jit(solution)/shard_map/ppermute | solution.py:25
  38.6 1.6 %collective-permute-start.14 = (bf16[128,512]{1,0:T(8,128)(2,1)S(1)}, bf16[128,512]{1,0:T(8,128)(2,1)S(1)}, u32[]{:S(2)}, u32[]{:S(2)}) collective-permute-start(bf16[128,512]{1,0:T(8,128)(2,1)S(1)} %add_convert_fusion.1), channel_id=1, source_target_pairs={{0,16},{8,24},{16,0},{24,8},{1,17},{9,25},{17,1},{25,9},{2,18},{10... | collective-permute-start | bytes 393224 | tf_op jit(solution)/shard_map/ppermute | solution.py:25
  40.2 2.1 %shard_map.99 = (f32[128,512]{1,0:T(8,128)S(1)}, bf16[128,512]{1,0:T(8,128)(2,1)S(1)}, f32[1,256,128]{2,1,0:T(8,128)S(1)}, bf16[256,128]{1,0:T(8,128)(2,1)S(1)},...) custom-call(bf16[1056,128]{1,0:T(8,128)(2,1)S(1)} %collective-permute-done.4.refs_0_, ...), custom_call_target="tpu_custom_call" | custom-call | flops 671088640 | bytes 1048576 | tf_op jit(solution)/shard_map/pallas_call | solution.py:200
  42.6 1.6 %collective-permute-start.12 = (bf16[128,512]{1,0:T(8,128)(2,1)S(1)}, bf16[128,512]{1,0:T(8,128)(2,1)S(1)}, u32[]{:S(2)}, u32[]{:S(2)}) collective-permute-start(bf16[128,512]{1,0:T(8,128)(2,1)S(1)} %add_convert_fusion.2), channel_id=1, source_target_pairs={{0,8},{8,0},{16,24},{24,16},{1,9},{9,1},{17,25},{25,17},{2,10},{10... | collective-permute-start | bytes 393224 | tf_op jit(solution)/shard_map/ppermute | solution.py:25
  44.2 2.0 %collective-permute-start.16 = (bf16[128,512]{1,0:T(8,128)(2,1)S(1)}, bf16[128,512]{1,0:T(8,128)(2,1)S(1)}, u32[]{:S(2)}, u32[]{:S(2)}) collective-permute-start(bf16[128,512]{1,0:T(8,128)(2,1)S(1)} %add_convert_fusion), channel_id=1, source_target_pairs={{0,24},{8,16},{16,8},{24,0},{1,25},{9,17},{17,9},{25,1},{2,26},{10... | collective-permute-start | bytes 393224 | tf_op jit(solution)/shard_map/ppermute | solution.py:25
  46.2 0.9 %collective-permute-start.17 = (bf16[256,128]{1,0:T(8,128)(2,1)S(1)}, bf16[256,128]{1,0:T(8,128)(2,1)S(1)}, u32[]{:S(2)}, u32[]{:S(2)}) collective-permute-start(bf16[256,128]{1,0:T(8,128)(2,1)S(1)} %get-tuple-element.50), channel_id=1, source_target_pairs={{0,2},{1,3},{2,0},{3,1},{4,6},{5,7},{6,4},{7,5},{8,10},{9,11},{10,... | collective-permute-start | bytes 196616 | tf_op jit(solution)/shard_map/ppermute | solution.py:25
  47.0 3.1 %collective-permute-start.18 = (bf16[256,128]{1,0:T(8,128)(2,1)S(1)}, bf16[256,128]{1,0:T(8,128)(2,1)S(1)}, u32[]{:S(2)}, u32[]{:S(2)}) collective-permute-start(bf16[256,128]{1,0:T(8,128)(2,1)S(1)} %get-tuple-element.51), channel_id=1, source_target_pairs={{0,4},{1,5},{2,6},{3,7},{4,0},{5,1},{6,2},{7,3},{8,12},{9,13},{10,... | collective-permute-start | bytes 196616 | tf_op jit(solution)/shard_map/ppermute | solution.py:25
  50.1 0.5 collective-permute-start.19
  50.6 4.3 %collective-permute-done.18.refs_5_ = bf16[256,128]{1,0:T(8,128)(2,1)S(1)} collective-permute-done((bf16[256,128]{1,0:T(8,128)(2,1)S(1)}, bf16[256,128]{1,0:T(8,128)(2,1)S(1)}, u32[]{:S(2)}, u32[]{:S(2)}) %collective-permute-start.18) | collective-permute-done | bytes 65568 | tf_op jit(solution)/shard_map/ppermute | solution.py:25
  54.9 1.4 %collective-permute-done.19.refs_6_ = bf16[256,128]{1,0:T(8,128)(2,1)S(1)} collective-permute-done((bf16[256,128]{1,0:T(8,128)(2,1)S(1)}, bf16[256,128]{1,0:T(8,128)(2,1)S(1)}, u32[]{:S(2)}, u32[]{:S(2)}) %collective-permute-start.19) | collective-permute-done | bytes 65568 | tf_op jit(solution)/shard_map/ppermute | solution.py:25
  56.3 0.8 %shard_map.100 = (bf16[128,512]{1,0:T(8,128)(2,1)}, bf16[128,128]{1,0:T(8,128)(2,1)}, bf16[128,128]{1,0:T(8,128)(2,1)}) custom-call(f32[128,512]{1,0:T(8,128)S(1)} %get-tuple-element.35.dq_own, f32[1,256,128]{2,1,0:T(8,128)S(1)} %get-tuple-element.44.acc, bf16[128,512]{1,0:T(8,128)(2,1)S(1)} %collective-permute-done.10.refs_0_, ...), custom_call_target="tpu_custom_call" | custom-call | tf_op jit(solution)/shard_map/pallas_call | solution.py:277
  (32 shorter events, 1.1 us)
Async XLA Ops:
  0.6 0.7 %copy-start.6 = (s32[128]{0:T(128)S(1)}, s32[128]{0:T(128)}, u32[]{:S(2)}) copy-start(s32[128]{0:T(128)} %param.13) | copy-start | bytes 1540
  1.3 0.9 %copy-start = (bf16[128,512]{1,0:T(8,128)(2,1)S(1)}, bf16[128,512]{1,0:T(8,128)(2,1)}, u32[]{:S(2)}) copy-start(bf16[128,512]{1,0:T(8,128)(2,1)} %q_ref.1) | copy-start | bytes 393220
  2.2 0.9 %copy-start.1 = (bf16[128,512]{1,0:T(8,128)(2,1)S(1)}, bf16[128,512]{1,0:T(8,128)(2,1)}, u32[]{:S(2)}) copy-start(bf16[128,512]{1,0:T(8,128)(2,1)} %o_ref.1) | copy-start | bytes 393220
  3.1 0.9 %copy-start.2 = (bf16[128,512]{1,0:T(8,128)(2,1)S(1)}, bf16[128,512]{1,0:T(8,128)(2,1)}, u32[]{:S(2)}) copy-start(bf16[128,512]{1,0:T(8,128)(2,1)} %g_ref.1) | copy-start | bytes 393220
  4.0 0.8 %copy-start.3 = (bf16[128,128]{1,0:T(8,128)(2,1)S(1)}, bf16[128,128]{1,0:T(8,128)(2,1)}, u32[]{:S(2)}) copy-start(bf16[128,128]{1,0:T(8,128)(2,1)} %k_ref.1) | copy-start | bytes 98308
  4.8 0.8 %copy-start.4 = (bf16[128,128]{1,0:T(8,128)(2,1)S(1)}, bf16[128,128]{1,0:T(8,128)(2,1)}, u32[]{:S(2)}) copy-start(bf16[128,128]{1,0:T(8,128)(2,1)} %v_ref.1) | copy-start | bytes 98308
  5.5 0.7 %copy-start.5 = (f32[4,128]{1,0:T(4,128)S(1)}, f32[4,128]{1,0:T(4,128)}, u32[]{:S(2)}) copy-start(f32[4,128]{1,0:T(4,128)} %lse_ref.1) | copy-start | bytes 6148
  6.9 9.5 %collective-permute-start.5 = (bf16[1056,128]{1,0:T(8,128)(2,1)S(1)}, bf16[1056,128]{1,0:T(8,128)(2,1)S(1)}, u32[]{:S(2)}, u32[]{:S(2)}) collective-permute-start(bf16[1056,128]{1,0:T(8,128)(2,1)S(1)} %get-tuple-element.36.refs_0_), channel_id=1, source_target_pairs={{0,8},{8,0},{16,24},{24,16},{1,9},{9,1},{17,25},{25,17},{2,10},{10... | collective-permute-start | bytes 811016 | tf_op jit(solution)/shard_map/ppermute | solution.py:25
  9.9 10.7 %collective-permute-start = (bf16[1056,128]{1,0:T(8,128)(2,1)S(1)}, bf16[1056,128]{1,0:T(8,128)(2,1)S(1)}, u32[]{:S(2)}, u32[]{:S(2)}) collective-permute-start(bf16[1056,128]{1,0:T(8,128)(2,1)S(1)} %get-tuple-element.36.refs_0_), channel_id=1, source_target_pairs={{0,1},{1,0},{2,3},{3,2},{4,5},{5,4},{6,7},{7,6},{8,9},{9,8},{10,11... | collective-permute-start | bytes 811016 | tf_op jit(solution)/shard_map/ppermute | solution.py:25
  9.9 10.9 %collective-permute-start.9 = (bf16[1056,128]{1,0:T(8,128)(2,1)S(1)}, bf16[1056,128]{1,0:T(8,128)(2,1)S(1)}, u32[]{:S(2)}, u32[]{:S(2)}) collective-permute-start(bf16[1056,128]{1,0:T(8,128)(2,1)S(1)} %get-tuple-element.36.refs_0_), channel_id=1, source_target_pairs={{0,16},{8,24},{16,0},{24,8},{1,17},{9,25},{17,1},{25,9},{2,18},{10... | collective-permute-start | bytes 811016 | tf_op jit(solution)/shard_map/ppermute | solution.py:25
  16.4 14.9 %collective-permute-start.6 = (bf16[1056,128]{1,0:T(8,128)(2,1)S(1)}, bf16[1056,128]{1,0:T(8,128)(2,1)S(1)}, u32[]{:S(2)}, u32[]{:S(2)}) collective-permute-start(bf16[1056,128]{1,0:T(8,128)(2,1)S(1)} %collective-permute-done.5.refs_0_), channel_id=1, source_target_pairs={{0,1},{1,0},{2,3},{3,2},{4,5},{5,4},{6,7},{7,6},{8,9},{9,8},{10,11... | collective-permute-start | bytes 811016 | tf_op jit(solution)/shard_map/ppermute | solution.py:25
  16.4 7.4 %collective-permute-start.2 = (bf16[272,128]{1,0:T(8,128)(2,1)S(1)}, bf16[272,128]{1,0:T(8,128)(2,1)S(1)}, u32[]{:S(2)}, u32[]{:S(2)}) collective-permute-start(bf16[272,128]{1,0:T(8,128)(2,1)S(1)} %get-tuple-element.30.refs_0_), channel_id=1, source_target_pairs={{0,4},{1,5},{2,6},{3,7},{4,0},{5,1},{6,2},{7,3},{8,12},{9,13},{10,... | collective-permute-start | bytes 208904 | tf_op jit(solution)/shard_map/ppermute | solution.py:25
  19.2 6.8 %collective-permute-start.3 = (bf16[272,128]{1,0:T(8,128)(2,1)S(1)}, bf16[272,128]{1,0:T(8,128)(2,1)S(1)}, u32[]{:S(2)}, u32[]{:S(2)}) collective-permute-start(bf16[272,128]{1,0:T(8,128)(2,1)S(1)} %get-tuple-element.30.refs_0_), channel_id=1, source_target_pairs={{0,6},{1,7},{2,4},{3,5},{4,2},{5,3},{6,0},{7,1},{8,14},{9,15},{10,... | collective-permute-start | bytes 208904 | tf_op jit(solution)/shard_map/ppermute | solution.py:25
  20.6 5.8 %collective-permute-start.1 = (bf16[272,128]{1,0:T(8,128)(2,1)S(1)}, bf16[272,128]{1,0:T(8,128)(2,1)S(1)}, u32[]{:S(2)}, u32[]{:S(2)}) collective-permute-start(bf16[272,128]{1,0:T(8,128)(2,1)S(1)} %get-tuple-element.30.refs_0_), channel_id=1, source_target_pairs={{0,2},{1,3},{2,0},{3,1},{4,6},{5,7},{6,4},{7,5},{8,10},{9,11},{10,... | collective-permute-start | bytes 208904 | tf_op jit(solution)/shard_map/ppermute | solution.py:25
  20.8 12.8 %collective-permute-start.11 = (bf16[1056,128]{1,0:T(8,128)(2,1)S(1)}, bf16[1056,128]{1,0:T(8,128)(2,1)S(1)}, u32[]{:S(2)}, u32[]{:S(2)}) collective-permute-start(bf16[1056,128]{1,0:T(8,128)(2,1)S(1)} %collective-permute-done.9.refs_0_), channel_id=1, source_target_pairs={{0,1},{1,0},{2,3},{3,2},{4,5},{5,4},{6,7},{7,6},{8,9},{9,8},{10,11... | collective-permute-start | bytes 811016 | tf_op jit(solution)/shard_map/ppermute | solution.py:25
  28.6 2.6 %collective-permute-start.10 = (bf16[128,512]{1,0:T(8,128)(2,1)S(1)}, bf16[128,512]{1,0:T(8,128)(2,1)S(1)}, u32[]{:S(2)}, u32[]{:S(2)}) collective-permute-start(bf16[128,512]{1,0:T(8,128)(2,1)S(1)} %get-tuple-element.40), channel_id=1, source_target_pairs={{0,1},{1,0},{2,3},{3,2},{4,5},{5,4},{6,7},{7,6},{8,9},{9,8},{10,11... | collective-permute-start | bytes 393224 | tf_op jit(solution)/shard_map/ppermute | solution.py:25
  28.7 9.8 %collective-permute-start.4 = (bf16[1056,128]{1,0:T(8,128)(2,1)S(1)}, bf16[1056,128]{1,0:T(8,128)(2,1)S(1)}, u32[]{:S(2)}, u32[]{:S(2)}) collective-permute-start(bf16[1056,128]{1,0:T(8,128)(2,1)S(1)} %get-tuple-element.36.refs_0_), channel_id=1, source_target_pairs={{0,24},{8,16},{16,8},{24,0},{1,25},{9,17},{17,9},{25,1},{2,26},{10... | collective-permute-start | bytes 811016 | tf_op jit(solution)/shard_map/ppermute | solution.py:25
  33.4 5.2 %collective-permute-start.7 = (bf16[128,512]{1,0:T(8,128)(2,1)S(1)}, bf16[128,512]{1,0:T(8,128)(2,1)S(1)}, u32[]{:S(2)}, u32[]{:S(2)}) collective-permute-start(bf16[128,512]{1,0:T(8,128)(2,1)S(1)} %get-tuple-element.38), channel_id=1, source_target_pairs={{0,1},{1,0},{2,3},{3,2},{4,5},{5,4},{6,7},{7,6},{8,9},{9,8},{10,11... | collective-permute-start | bytes 393224 | tf_op jit(solution)/shard_map/ppermute | solution.py:25
  35.7 2.8 %collective-permute-start.13 = (bf16[128,512]{1,0:T(8,128)(2,1)S(1)}, bf16[128,512]{1,0:T(8,128)(2,1)S(1)}, u32[]{:S(2)}, u32[]{:S(2)}) collective-permute-start(bf16[128,512]{1,0:T(8,128)(2,1)S(1)} %get-tuple-element.47), channel_id=1, source_target_pairs={{0,1},{1,0},{2,3},{3,2},{4,5},{5,4},{6,7},{7,6},{8,9},{9,8},{10,11... | collective-permute-start | bytes 393224 | tf_op jit(solution)/shard_map/ppermute | solution.py:25
  38.5 1.7 %collective-permute-start.8 = (bf16[1056,128]{1,0:T(8,128)(2,1)S(1)}, bf16[1056,128]{1,0:T(8,128)(2,1)S(1)}, u32[]{:S(2)}, u32[]{:S(2)}) collective-permute-start(bf16[1056,128]{1,0:T(8,128)(2,1)S(1)} %collective-permute-done.4.refs_0_), channel_id=1, source_target_pairs={{0,1},{1,0},{2,3},{3,2},{4,5},{5,4},{6,7},{7,6},{8,9},{9,8},{10,11... | collective-permute-start | bytes 811016 | tf_op jit(solution)/shard_map/ppermute | solution.py:25
  38.6 11.5 %collective-permute-start.14 = (bf16[128,512]{1,0:T(8,128)(2,1)S(1)}, bf16[128,512]{1,0:T(8,128)(2,1)S(1)}, u32[]{:S(2)}, u32[]{:S(2)}) collective-permute-start(bf16[128,512]{1,0:T(8,128)(2,1)S(1)} %add_convert_fusion.1), channel_id=1, source_target_pairs={{0,16},{8,24},{16,0},{24,8},{1,17},{9,25},{17,1},{25,9},{2,18},{10... | collective-permute-start | bytes 393224 | tf_op jit(solution)/shard_map/ppermute | solution.py:25
  42.3 1.9 %collective-permute-start.15 = (bf16[128,512]{1,0:T(8,128)(2,1)S(1)}, bf16[128,512]{1,0:T(8,128)(2,1)S(1)}, u32[]{:S(2)}, u32[]{:S(2)}) collective-permute-start(bf16[128,512]{1,0:T(8,128)(2,1)S(1)} %get-tuple-element.49), channel_id=1, source_target_pairs={{0,1},{1,0},{2,3},{3,2},{4,5},{5,4},{6,7},{7,6},{8,9},{9,8},{10,11... | collective-permute-start | bytes 393224 | tf_op jit(solution)/shard_map/ppermute | solution.py:25
  42.6 7.9 %collective-permute-start.12 = (bf16[128,512]{1,0:T(8,128)(2,1)S(1)}, bf16[128,512]{1,0:T(8,128)(2,1)S(1)}, u32[]{:S(2)}, u32[]{:S(2)}) collective-permute-start(bf16[128,512]{1,0:T(8,128)(2,1)S(1)} %add_convert_fusion.2), channel_id=1, source_target_pairs={{0,8},{8,0},{16,24},{24,16},{1,9},{9,1},{17,25},{25,17},{2,10},{10... | collective-permute-start | bytes 393224 | tf_op jit(solution)/shard_map/ppermute | solution.py:25
  44.2 12.1 %collective-permute-start.16 = (bf16[128,512]{1,0:T(8,128)(2,1)S(1)}, bf16[128,512]{1,0:T(8,128)(2,1)S(1)}, u32[]{:S(2)}, u32[]{:S(2)}) collective-permute-start(bf16[128,512]{1,0:T(8,128)(2,1)S(1)} %add_convert_fusion), channel_id=1, source_target_pairs={{0,24},{8,16},{16,8},{24,0},{1,25},{9,17},{17,9},{25,1},{2,26},{10... | collective-permute-start | bytes 393224 | tf_op jit(solution)/shard_map/ppermute | solution.py:25
  46.2 4.4 %collective-permute-start.17 = (bf16[256,128]{1,0:T(8,128)(2,1)S(1)}, bf16[256,128]{1,0:T(8,128)(2,1)S(1)}, u32[]{:S(2)}, u32[]{:S(2)}) collective-permute-start(bf16[256,128]{1,0:T(8,128)(2,1)S(1)} %get-tuple-element.50), channel_id=1, source_target_pairs={{0,2},{1,3},{2,0},{3,1},{4,6},{5,7},{6,4},{7,5},{8,10},{9,11},{10,... | collective-permute-start | bytes 196616 | tf_op jit(solution)/shard_map/ppermute | solution.py:25
  47.0 7.8 %collective-permute-start.18 = (bf16[256,128]{1,0:T(8,128)(2,1)S(1)}, bf16[256,128]{1,0:T(8,128)(2,1)S(1)}, u32[]{:S(2)}, u32[]{:S(2)}) collective-permute-start(bf16[256,128]{1,0:T(8,128)(2,1)S(1)} %get-tuple-element.51), channel_id=1, source_target_pairs={{0,4},{1,5},{2,6},{3,7},{4,0},{5,1},{6,2},{7,3},{8,12},{9,13},{10,... | collective-permute-start | bytes 196616 | tf_op jit(solution)/shard_map/ppermute | solution.py:25
  50.1 6.2 %collective-permute-start.19 = (bf16[256,128]{1,0:T(8,128)(2,1)S(1)}, bf16[256,128]{1,0:T(8,128)(2,1)S(1)}, u32[]{:S(2)}, u32[]{:S(2)}) collective-permute-start(bf16[256,128]{1,0:T(8,128)(2,1)S(1)} %get-tuple-element.52), channel_id=1, source_target_pairs={{0,6},{1,7},{2,4},{3,5},{4,2},{5,3},{6,0},{7,1},{8,14},{9,15},{10,... | collective-permute-start | bytes 196616 | tf_op jit(solution)/shard_map/ppermute | solution.py:25

commit v4 on v3

v4 whole, which is shorter than its diff:
```python
import functools
import math

import jax
import jax.numpy as jnp
from jax import lax
from jax.experimental import pallas as pl
from jax.experimental.pallas import tpu as pltpu
from jax.sharding import PartitionSpec as P

BF = jnp.bfloat16
F32 = jnp.float32
RUN = 64
LOG2E = math.log2(math.e)
VMEM = pl.BlockSpec(memory_space=pltpu.VMEM)
SMALL = pltpu.CompilerParams(vmem_limit_bytes=16 * 1024 * 1024)
NN = (((1,), (0,)), ((), ()))
NT = (((1,), (1,)), ((), ()))
QUICK = pl.CostEstimate(flops=1000, bytes_accessed=1000, transcendentals=0)
COLS = 256


def swapped(block, axis, mask):
    pairs = [(i, i ^ mask) for i in range(lax.axis_size(axis))]
    return lax.ppermute(block, axis, pairs)


def three_parts(x):
    hi = x.astype(BF)
    rest = x - hi.astype(F32)
    mid = rest.astype(BF)
    low = (rest - mid.astype(F32)).astype(BF)
    return [hi, mid, low]


def dot(a, b, dims=NN):
    return lax.dot_general(a, b, dims, preferred_element_type=F32)


def pack_kernel(q_ref, k_ref, v_ref, o_ref, g_ref, lse_ref, pos_ref, x_ref, kv_ref, o_s, lse_s, pos_s, sems):
    rows, width = k_ref.shape
    heads = q_ref.shape[1] // width
    moves = [(lse_ref, lse_s), (pos_ref, pos_s), (o_ref, o_s)]
    for h in range(heads):
        cols = pl.ds(h * width, width)
        moves.append((g_ref.at[:, cols], x_ref.at[pl.ds((heads + h) * rows, rows), :]))
    for h in range(heads):
        cols = pl.ds(h * width, width)
        moves.append((q_ref.at[:, cols], x_ref.at[pl.ds(h * rows, rows), :]))
    moves.append((k_ref, kv_ref.at[pl.ds(0, rows), :]))
    moves.append((v_ref, kv_ref.at[pl.ds(rows, rows), :]))
    copies = [pltpu.make_async_copy(a, b, sems.at[n]) for n, (a, b) in enumerate(moves)]
    for copy in copies:
        copy.start()
    for copy in copies[: 3 + heads]:
        copy.wait()
    ones = jnp.ones((8, width), BF)
    deltas = []
    for h in range(heads):
        g = x_ref[(heads + h) * rows : (heads + h + 1) * rows, :]
        prod = g.astype(F32) * o_s[:, h * width : (h + 1) * width].astype(F32)
        hi = prod.astype(BF)
        low = (prod - hi.astype(F32)).astype(BF)
        deltas.append((dot(ones, hi, NT) + dot(ones, low, NT))[:1])
    run = (pos_s[...] // RUN).astype(F32)
    extra = (
        three_parts(lse_s[...] * LOG2E)
        + three_parts(jnp.concatenate(deltas, axis=0))
        + [run.astype(BF), jnp.zeros((32 - 6 * heads - 1, rows), BF)]
    )
    x_ref[2 * heads * rows :, :] = jnp.concatenate([e.astype(F32) for e in extra], axis=0).astype(BF)
    lane = lax.broadcasted_iota(jnp.int32, run.shape, 1)
    ids = [
        jnp.max(jnp.where(lane == r * RUN, run, 0.0), axis=1, keepdims=True)
        for r in range(rows // RUN)
    ]
    wide = [jnp.broadcast_to(i, (1, width)) for i in ids]
    wide.append(jnp.zeros((16 - len(ids), width), F32))
    kv_ref[2 * rows :, :] = jnp.concatenate(wide, axis=0).astype(BF)
    for copy in copies[3 + heads :]:
        copy.wait()


def blocks_kernel(plan, rows, heads, scale, *refs):
    x_refs = refs[: plan["queries"]]
    refs = refs[plan["queries"] :]
    kv_refs = refs[: plan["kv"]]
    refs = refs[plan["kv"] :]
    acc_refs = refs[: plan["acc"]]
    refs = refs[plan["acc"] :]
    dq_in = None
    if plan["dq_in"]:
        dq_in, refs = refs[0], refs[1:]
    dq_refs, dkv_ref = refs[:-1], refs[-1]
    width = x_refs[0].shape[1]
    hr = heads * rows
    per = rows // RUN
    step = COLS // rows
    slots = plan["slots"]
    rowed = []
    for x_ref in x_refs:
        e = x_ref[2 * hr :, :].astype(F32)
        lse = e[0:heads] + e[heads : 2 * heads] + e[2 * heads : 3 * heads]
        delta = e[3 * heads : 4 * heads] + e[4 * heads : 5 * heads] + e[5 * heads : 6 * heads]
        rowed.append((lse, delta, e[6 * heads : 6 * heads + 1]))
    dqt = [[None] * (hr // COLS) for _ in x_refs]
    for c in range(0, len(slots), 2):
        ks, vs, runs = [], [], []
        for n, start in (s[:2] for s in slots[c : c + 2]):
            ks.append(kv_refs[n][start : start + rows, :])
            vs.append(kv_refs[n][start + rows : start + 2 * rows, :])
            e = kv_refs[n][start + 2 * rows : start + 2 * rows + 16, :].astype(F32)
            runs += [e[r : r + 1] for r in range(per)]
        k = jnp.concatenate(ks, axis=0)
        v = jnp.concatenate(vs, axis=0)
        kt = jnp.concatenate([b.astype(F32).T.astype(BF) for b in ks], axis=1)
        dk = dv = None
        for b, x_ref in enumerate(x_refs):
            lse, delta, run = rowed[b]
            for n in range(hr // COLS):
                q = x_ref[n * COLS : (n + 1) * COLS, :]
                g = x_ref[hr + n * COLS : hr + (n + 1) * COLS, :]
                st = dot(k, q, NT)
                dpt = dot(v, g, NT)
                p_rows, d_rows = [], []
                for r in range(2 * per):
                    sl = slice(r * RUN, (r + 1) * RUN)
                    p_heads, d_heads = [], []
                    for h in range(step):
                        hl = slice(h * rows, (h + 1) * rows)
                        head = n * step + h
                        row = jnp.where(runs[r] <= run, lse[head : head + 1], 1e30)
                        arg = st[sl, hl] * (scale * LOG2E) - row
                        if plan["diagonal"] and b == 0 and c == 0 and r < per:
                            i = lax.broadcasted_iota(jnp.int32, (RUN, rows), 1) - r * RUN
                            j = lax.broadcasted_iota(jnp.int32, (RUN, rows), 0)
                            arg = jnp.where((i >= 0) & (i < j), -1e30, arg)
                        p = jnp.exp2(arg)
                        p_heads.append(p.astype(BF))
                        d_heads.append((p * (dpt[sl, hl] - delta[head : head + 1])).astype(BF))
                    p_rows.append(jnp.concatenate(p_heads, axis=1))
                    d_rows.append(jnp.concatenate(d_heads, axis=1))
                p = jnp.concatenate(p_rows, axis=0)
                d = jnp.concatenate(d_rows, axis=0)
                dv_n, dk_n, dq_n = dot(p, g), dot(d, q), dot(kt, d)
                dv = dv_n if dv is None else dv + dv_n
                dk = dk_n if dk is None else dk + dk_n
                old = dqt[b][n]
                dqt[b][n] = dq_n if old is None else old + dq_n
        for j, slot in enumerate(slots[c : c + 2]):
            dk_j, dv_j = dk[j * rows : (j + 1) * rows], dv[j * rows : (j + 1) * rows]
            if plan["acc"]:
                acc_ref, at = acc_refs[slot[2]], slot[3]
                dk_j += acc_ref[at, :rows, :]
                dv_j += acc_ref[at, rows:, :]
            dkv_ref[c + j, :rows, :] = dk_j.astype(dkv_ref.dtype)
            dkv_ref[c + j, rows:, :] = dv_j.astype(dkv_ref.dtype)
    for b, dq_ref in enumerate(dq_refs):
        for n in range(hr // COLS):
            cols = slice(n * COLS, (n + 1) * COLS)
            total = dqt[b][n] if dq_in is None else dqt[b][n] + dq_in[b, :, cols]
            dq_ref[:, cols] = total.astype(dq_ref.dtype)


def first_kernel(plan, rows, heads, scale, *refs):
    dq_ref = refs[-2]
    dq_refs = [dq_ref.at[b] for b in range(plan["queries"])]
    blocks_kernel(plan, rows, heads, scale, *refs[:-2], *dq_refs, refs[-1])


def blocks_call(xs, kvs, slots, rows, heads, scale, dkv_type, dq_types, acc=(), dq_in=None, diagonal=False):
    sds = jax.ShapeDtypeStruct
    width = xs[0].shape[1]
    hr = heads * rows
    plan = {
        "queries": len(xs),
        "kv": len(kvs),
        "acc": len(acc),
        "dq_in": dq_in is not None,
        "slots": slots,
        "diagonal": diagonal,
    }
    args = (*xs, *kvs, *acc) + (() if dq_in is None else (dq_in,))
    if dq_types is None:
        body = first_kernel
        outs = (sds((len(xs), width, hr), F32),)
    else:
        body = blocks_kernel
        outs = tuple(sds((width, hr), t) for t in dq_types)
    outs += (sds((len(slots), 2 * rows, width), dkv_type),)
    return pl.pallas_call(
        functools.partial(body, plan, rows, heads, scale),
        out_shape=outs,
        in_specs=[VMEM] * len(args),
        out_specs=(VMEM,) * len(outs),
        compiler_params=SMALL,
        cost_estimate=QUICK,
    )(*args)


def add_kernel(own_ref, got_ref, first_ref, *refs):
    first_ref[...] = own_ref[0] + got_ref[0].astype(F32)
    for n, ref in enumerate(refs):
        ref[...] = (own_ref[n + 1] + got_ref[n + 1].astype(F32)).astype(BF)


def final_kernel(rows, heads, scale, n_dq, dq_own, dkv_own, *refs):
    dq_refs, dkv_refs, (gq_ref, gk_ref, gv_ref) = refs[:n_dq], refs[n_dq:-3], refs[-3:]
    dq = dq_own[...]
    for r in dq_refs:
        dq = dq + r[...].astype(F32)
    for h in range(heads):
        part = dq[:, h * rows : (h + 1) * rows]
        gq_ref[:, h * 128 : (h + 1) * 128] = (scale * part).T.astype(BF)
    dkv = dkv_own[...]
    for r in dkv_refs:
        dkv = dkv + r[...].astype(F32)
    gk_ref[...] = (scale * dkv[:rows]).astype(BF)
    gv_ref[...] = dkv[rows:].astype(BF)


def crossed(block, t, other):
    pairs = []
    for i in range(lax.axis_size("inner")):
        chip, core = i // 2, i % 2
        pairs.append((i, 2 * (chip ^ (2 * t + (core if other else 1 - core))) + core))
    return lax.ppermute(block, "inner", pairs)


def on_device(query, key, value, out, grad_out, lse, positions):
    rows, width = key.shape
    heads = query.shape[1] // width
    hr = heads * rows
    scale = width ** (-0.5)
    nq = lax.axis_size("outer")
    nz = lax.axis_size("inner") // 2
    sds = jax.ShapeDtypeStruct
    inputs = (query, key, value, out, grad_out, lse, positions[None, :])
    x, kv = pl.pallas_call(
        pack_kernel,
        out_shape=(sds((2 * hr + 32, width), BF), sds((2 * rows + 16, width), BF)),
        in_specs=[pl.BlockSpec(memory_space=pltpu.HBM)] * 7,
        out_specs=(VMEM, VMEM),
        scratch_shapes=[
            pltpu.VMEM(out.shape, BF),
            pltpu.VMEM(lse.shape, F32),
            pltpu.VMEM((1, rows), jnp.int32),
            pltpu.SemaphoreType.DMA((5 + 2 * heads,)),
        ],
        compiler_params=SMALL,
        cost_estimate=QUICK,
    )(*[pltpu.with_memory_space_constraint(a, pltpu.HBM) for a in inputs])

    sib = swapped(kv, "inner", 1)
    near = swapped(kv, "inner", 2)
    pair = jnp.concatenate([kv, sib], axis=0)
    direct = [crossed(pair, t, False) for t in range(1, nz // 2)]
    xs = [x] + [swapped(x, "outer", s) for s in range(1, nq)]
    early = lax.optimization_barrier((near, *direct, *xs[1:-1]))
    near, direct, xs = early[0], early[1 : nz // 2], [x, *early[nz // 2 :], xs[-1]]
    traded = swapped(jnp.concatenate([near, *direct], axis=0), "inner", 1)

    size = kv.shape[0]
    group_a = [(0, 0), (1, 0)]
    group_b = [(0, 0), (1, 0)]
    for t in range(1, nz // 2):
        group_a += [(t + 1, 0), (t + 1, size)]
        group_b += [(1, (2 * t - 1) * size), (1, 2 * t * size)]
    common = (rows, heads, scale)
    dqs, acc_a = blocks_call(xs[:-1], [kv, sib, *direct], group_a, *common, F32, None, diagonal=True)
    *dqs, acc_b = blocks_call(
        xs[:-1], [near, traded], group_b, *common, F32, [F32] + [BF] * (nq - 2), dq_in=dqs
    )
    arrays = [kv, sib, *direct, near, traded]
    base = len(arrays) - 2
    in_a = [(n, start, 0, i) for i, (n, start) in enumerate(group_a)]
    in_b = [(base + n, start, 1, i) for i, (n, start) in enumerate(group_b)]
    theirs, ours = [in_a[1], in_b[1]], [in_a[0], in_b[0]]
    for t in range(1, nz // 2):
        theirs += [in_b[2 * t], in_a[2 * t + 1]]
        ours += [in_a[2 * t], in_b[2 * t + 1]]
    dq_last, dkv_sib = blocks_call([xs[-1]], arrays, theirs, *common, BF, None, acc=(acc_a, acc_b))
    dkv_got = swapped(dkv_sib, "inner", 1)
    dq_last, dkv_own = blocks_call(
        [xs[-1]], arrays, ours, *common, F32, [BF], acc=(acc_a, acc_b), dq_in=dq_last
    )
    got = [swapped(dq, "outer", s + 1) for s, dq in enumerate([*dqs[1:], dq_last])]
    dkv_own, *send = pl.pallas_call(
        add_kernel,
        out_shape=(sds((2 * rows, width), F32),) + (sds((2 * rows, width), BF),) * (nz - 1),
        in_specs=[VMEM] * 2,
        out_specs=(VMEM,) * nz,
        compiler_params=SMALL,
        cost_estimate=QUICK,
    )(dkv_own, dkv_got)
    dkv = [swapped(send[0], "inner", 2)]
    for t in range(1, nz // 2):
        dkv.append(crossed(send[2 * t - 1], t, False))
        dkv.append(crossed(send[2 * t], t, True))

    return pl.pallas_call(
        functools.partial(final_kernel, rows, heads, scale, len(got)),
        out_shape=(sds((rows, heads * width), BF), sds((rows, width), BF), sds((rows, width), BF)),
        in_specs=[VMEM] * (2 + len(got) + len(dkv)),
        out_specs=(VMEM,) * 3,
        compiler_params=SMALL,
        cost_estimate=QUICK,
    )(dqs[0], dkv_own, *got, *dkv)


def solution(mesh):
    tokens = P(("outer", "inner"), None)
    return jax.shard_map(
        on_device,
        mesh=mesh,
        in_specs=(tokens,) * 5 + (P(None, ("outer", "inner")), P(("outer", "inner"))),
        out_specs=(tokens,) * 3,
        check_vma=False,
    )
```

time: 57.4 us -> 43.1 us (0.75)
  waiting for transfers between devices: 18.7 us -> 11.3 us
  local copies, waits for them, and re-layouts: 5.56 us -> 0 us
  starting transfers between devices: 22.1 us -> 20.3 us
  Pallas kernels: 9.93 us -> 10.6 us
    ppermute x20 -> x11, waiting for transfers between devices: 18.7 us -> 7.58 us  [swapped(): return lax.ppermute(block, axis, pairs)]
    ppermute x20 -> x11, starting transfers between devices: 22.1 us -> 12 us  [swapped(): return lax.ppermute(block, axis, pairs)]
    ppermute x0 -> x3, starting transfers between devices: none -> 8.31 us  [crossed(): return lax.ppermute(block, 'inner', pairs)]
    unnamed x14 -> x0, local copies, waits for them, and re-layouts: 5.56 us -> none
    ppermute x0 -> x3, waiting for transfers between devices: none -> 3.69 us  [crossed(): return lax.ppermute(block, 'inner', pairs)]
    pallas_call x1, Pallas kernels: 0.69 us -> 1.34 us  [on_device(): pl.pallas_call(pack_kernel, out_shape=(sds((2 * hr + 32, width), BF), sds...]
  transfers between devices with their start and end apart: 20 -> 14, of which waited for: 7 -> 4; matrix products, arithmetic and copies ran while one was open for 0% -> 0% of each run, Pallas kernels for 15% -> 17%
where the time goes in v4:
time: 43.1 us; the launch traced here: 42.9 us
  starting transfers between devices  20.3 us (47%)
  waiting for transfers between devices  11.3 us (26%)
  Pallas kernels  10.6 us (25%)
  between operations  0.71 us (2%)
    ppermute x11, starting transfers between devices, swapped(): return lax.ppermute(block, axis, pairs)  12 us
    pallas_call x4, Pallas kernels, blocks_call(): pl.pallas_call(functools.partial(body, plan, rows, heads, scale), out_sha...  8.39 us
    ppermute x3, starting transfers between devices, crossed(): return lax.ppermute(block, 'inner', pairs)  8.31 us
    ppermute x11, waiting for transfers between devices, swapped(): return lax.ppermute(block, axis, pairs)  7.58 us
    ppermute x3, waiting for transfers between devices, crossed(): return lax.ppermute(block, 'inner', pairs)  3.69 us
    pallas_call x1, Pallas kernels, on_device(): pl.pallas_call(pack_kernel, out_shape=(sds((2 * hr + 32, width), BF), sds...  1.34 us
  transfers between devices with their start and end apart: 14, of which 4 were waited for; matrix products, arithmetic and copies ran while one was open for 0% of the time, Pallas kernels for 17%

profile of v4, /device:TPU:0, one launch (start us, length us, event | category | flops | bytes accessed | tf_op | source)
XLA Modules:
  0.0 42.9 jit_solution(15982621032472795050)
XLA Ops:
  0.6 1.3 %shard_map.94 = (bf16[1056,128]{1,0:T(8,128)(2,1)S(1)}, bf16[272,128]{1,0:T(8,128)(2,1)S(1)}) custom-call(bf16[128,512]{1,0:T(8,128)(2,1)} %q_ref.1, bf16[128,128]{1,0:T(8,128)(2,1)} %k_ref.1, bf16[128,128]{1,0:T(8,128)(2,1)} %v_ref.1, bf16[128,512]{1,0:T(8,128)(2,1)} %o_ref.1, bf16[128,512]{1,0:T(8,128)(2,1)} %g_ref.1, f32[4,128]{1,0:T(4,128)} %lse_ref.1, ...), custom_call_target="tpu_custom_call" | custom-call | flops 1000 | bytes 1000 | tf_op jit(solution)/shard_map/pallas_call | solution.py:239
  2.0 0.5 %collective-permute-start.1 = (bf16[272,128]{1,0:T(8,128)(2,1)S(1)}, bf16[272,128]{1,0:T(8,128)(2,1)S(1)}, u32[]{:S(2)}, u32[]{:S(2)}) collective-permute-start(bf16[272,128]{1,0:T(8,128)(2,1)S(1)} %get-tuple-element.24.refs_3_.refs_1_), channel_id=1, source_target_pairs={{0,1},{1,0},{2,3},{3,2},{4,5},{5,4},{6,7},{7,6},{8,9},{9,8},{10,11... | collective-permute-start | bytes 208904 | tf_op jit(solution)/shard_map/ppermute | solution.py:25
  2.5 2.6 %collective-permute-start.3 = (bf16[1056,128]{1,0:T(8,128)(2,1)S(1)}, bf16[1056,128]{1,0:T(8,128)(2,1)S(1)}, u32[]{:S(2)}, u32[]{:S(2)}) collective-permute-start(bf16[1056,128]{1,0:T(8,128)(2,1)S(1)} %get-tuple-element.23.refs_0_), channel_id=1, source_target_pairs={{0,8},{8,0},{16,24},{24,16},{1,9},{9,1},{17,25},{25,17},{2,10},{10... | collective-permute-start | bytes 811016 | tf_op jit(solution)/shard_map/ppermute | solution.py:25
  5.1 1.5 %collective-permute-start.4 = (bf16[1056,128]{1,0:T(8,128)(2,1)S(1)}, bf16[1056,128]{1,0:T(8,128)(2,1)S(1)}, u32[]{:S(2)}, u32[]{:S(2)}) collective-permute-start(bf16[1056,128]{1,0:T(8,128)(2,1)S(1)} %get-tuple-element.23.refs_0_), channel_id=1, source_target_pairs={{0,16},{8,24},{16,0},{24,8},{1,17},{9,25},{17,1},{25,9},{2,18},{10... | collective-permute-start | bytes 811016 | tf_op jit(solution)/shard_map/ppermute | solution.py:25
  6.6 0.0 collective-permute-done.1.refs_4_.refs_2_
  6.6 3.7 %collective-permute-start.2 = (bf16[544,128]{1,0:T(8,128)(2,1)S(1)}, bf16[544,128]{1,0:T(8,128)(2,1)S(1)}, u32[]{:S(2)}, u32[]{:S(2)}) collective-permute-start(bf16[544,128]{1,0:T(8,128)(2,1)S(1)} %pad_maximum_fusion.1), channel_id=1, source_target_pairs={{0,6},{1,5},{2,4},{3,7},{4,2},{5,1},{6,0},{7,3},{8,14},{9,13},{10,... | collective-permute-start | bytes 417800 | tf_op jit(solution)/shard_map/ppermute | solution.py:227
  10.3 0.0 collective-permute-start
  10.3 0.6 %collective-permute-start.6 = (bf16[1056,128]{1,0:T(8,128)(2,1)S(1)}, bf16[1056,128]{1,0:T(8,128)(2,1)S(1)}, u32[]{:S(2)}, u32[]{:S(2)}) collective-permute-start(bf16[1056,128]{1,0:T(8,128)(2,1)S(1)} %get-tuple-element.23.refs_0_), channel_id=1, source_target_pairs={{0,24},{8,16},{16,8},{24,0},{1,25},{9,17},{17,9},{25,1},{2,26},{10... | collective-permute-start | bytes 811016 | tf_op jit(solution)/shard_map/ppermute | solution.py:25
  10.9 4.5 %collective-permute-done.refs_3_.refs_4_ = bf16[272,128]{1,0:T(8,128)(2,1)S(1)} collective-permute-done((bf16[272,128]{1,0:T(8,128)(2,1)S(1)}, bf16[272,128]{1,0:T(8,128)(2,1)S(1)}, u32[]{:S(2)}, u32[]{:S(2)}) %collective-permute-start) | collective-permute-done | bytes 69664 | tf_op jit(solution)/shard_map/ppermute | solution.py:25
  15.4 0.0 collective-permute-done.2.refs_5_.refs_3_
  15.4 0.0 collective-permute-done.3.refs_1_
  15.4 3.0 %collective-permute-done.4.refs_2_ = bf16[1056,128]{1,0:T(8,128)(2,1)S(1)} collective-permute-done((bf16[1056,128]{1,0:T(8,128)(2,1)S(1)}, bf16[1056,128]{1,0:T(8,128)(2,1)S(1)}, u32[]{:S(2)}, u32[]{:S(2)}) %collective-permute-start.4) | collective-permute-done | bytes 270368 | tf_op jit(solution)/shard_map/ppermute | solution.py:25
  18.5 0.1 collective-permute-start.5
  18.5 3.1 %shard_map.95 = (f32[3,128,512]{2,1,0:T(8,128)S(1)}, f32[4,256,128]{2,1,0:T(8,128)S(1)}) custom-call(bf16[1056,128]{1,0:T(8,128)(2,1)S(1)} %get-tuple-element.23.refs_0_, bf16[1056,128]{1,0:T(8,128)(2,1)S(1)} %collective-permute-done.3.refs_1_, bf16[1056,128]{1,0:T(8,128)(2,1)S(1)} %collective-permute-done.4.refs_2_, ...), custom_call_target="tpu_custom_call" | custom-call | flops 1000 | bytes 1000 | tf_op jit(solution)/shard_map/pallas_call | solution.py:191
  21.6 3.1 %shard_map.96 = (f32[128,512]{1,0:T(8,128)S(1)}, bf16[128,512]{1,0:T(8,128)(2,1)S(1)}, bf16[128,512]{1,0:T(8,128)(2,1)S(1)}, f32[4,256,128]{2,1,0:T(8,128)S(1)}) custom-call(bf16[1056,128]{1,0:T(8,128)(2,1)S(1)} %get-tuple-element.23.refs_0_, bf16[1056,128]{1,0:T(8,128)(2,1)S(1)} %collective-permute-done.3.refs_1_, ...), custom_call_target="tpu_custom_call" | custom-call | flops 1000 | bytes 1000 | tf_op jit(solution)/shard_map/pallas_call | solution.py:191
  24.7 0.0 collective-permute-done.6.refs_0_
  24.7 1.1 %shard_map.97 = (f32[1,128,512]{2,1,0:T(8,128)S(1)}, bf16[4,256,128]{2,1,0:T(8,128)(2,1)S(1)}) custom-call(bf16[1056,128]{1,0:T(8,128)(2,1)S(1)} %collective-permute-done.6.refs_0_, bf16[272,128]{1,0:T(8,128)(2,1)S(1)} %get-tuple-element.24.refs_3_.refs_1_, bf16[272,128]{1,0:T(8,128)(2,1)S(1)} %collective-permute-done.1.refs_4_.refs_2_, ...), custom_call_target="tpu_custom_call" | custom-call | flops 1000 | bytes 1000 | tf_op jit(solution)/shard_map/pallas_call | solution.py:191
  25.8 0.6 %collective-permute-start.7 = (bf16[4,256,128]{2,1,0:T(8,128)(2,1)S(1)}, bf16[4,256,128]{2,1,0:T(8,128)(2,1)S(1)}, u32[]{:S(2)}, u32[]{:S(2)}) collective-permute-start(bf16[4,256,128]{2,1,0:T(8,128)(2,1)S(1)} %get-tuple-element.35), channel_id=1, source_target_pairs={{0,1},{1,0},{2,3},{3,2},{4,5},{5,4},{6,7},{7,6},{8,9},{9,8},{10,11... | collective-permute-start | bytes 786440 | tf_op jit(solution)/shard_map/ppermute | solution.py:25
  26.4 1.1 %shard_map.98 = (bf16[128,512]{1,0:T(8,128)(2,1)S(1)}, f32[4,256,128]{2,1,0:T(8,128)S(1)}) custom-call(bf16[1056,128]{1,0:T(8,128)(2,1)S(1)} %collective-permute-done.6.refs_0_, bf16[272,128]{1,0:T(8,128)(2,1)S(1)} %get-tuple-element.24.refs_3_.refs_1_, bf16[272,128]{1,0:T(8,128)(2,1)S(1)} %collective-permute-done.1.refs_4_.refs_2_, ...), custom_call_target="tpu_custom_call" | custom-call | flops 1000 | bytes 1000 | tf_op jit(solution)/shard_map/pallas_call | solution.py:191
  27.5 2.5 %collective-permute-start.10 = (bf16[128,512]{1,0:T(8,128)(2,1)S(1)}, bf16[128,512]{1,0:T(8,128)(2,1)S(1)}, u32[]{:S(2)}, u32[]{:S(2)}) collective-permute-start(bf16[128,512]{1,0:T(8,128)(2,1)S(1)} %get-tuple-element.39), channel_id=1, source_target_pairs={{0,24},{8,16},{16,8},{24,0},{1,25},{9,17},{17,9},{25,1},{2,26},{10... | collective-permute-start | bytes 393224 | tf_op jit(solution)/shard_map/ppermute | solution.py:25
  30.0 1.5 %collective-permute-start.8 = (bf16[128,512]{1,0:T(8,128)(2,1)S(1)}, bf16[128,512]{1,0:T(8,128)(2,1)S(1)}, u32[]{:S(2)}, u32[]{:S(2)}) collective-permute-start(bf16[128,512]{1,0:T(8,128)(2,1)S(1)} %get-tuple-element.37), channel_id=1, source_target_pairs={{0,8},{8,0},{16,24},{24,16},{1,9},{9,1},{17,25},{25,17},{2,10},{10... | collective-permute-start | bytes 393224 | tf_op jit(solution)/shard_map/ppermute | solution.py:25
  31.5 0.1 shard_map.99
  31.6 2.1 %collective-permute-start.11 = (bf16[256,128]{1,0:T(8,128)(2,1)S(1)}, bf16[256,128]{1,0:T(8,128)(2,1)S(1)}, u32[]{:S(2)}, u32[]{:S(2)}) collective-permute-start(bf16[256,128]{1,0:T(8,128)(2,1)S(1)} %get-tuple-element.40), channel_id=1, source_target_pairs={{0,2},{1,3},{2,0},{3,1},{4,6},{5,7},{6,4},{7,5},{8,10},{9,11},{10,... | collective-permute-start | bytes 196616 | tf_op jit(solution)/shard_map/ppermute | solution.py:25
  33.8 2.5 %collective-permute-start.12 = (bf16[256,128]{1,0:T(8,128)(2,1)S(1)}, bf16[256,128]{1,0:T(8,128)(2,1)S(1)}, u32[]{:S(2)}, u32[]{:S(2)}) collective-permute-start(bf16[256,128]{1,0:T(8,128)(2,1)S(1)} %get-tuple-element.41), channel_id=1, source_target_pairs={{0,6},{1,5},{2,4},{3,7},{4,2},{5,1},{6,0},{7,3},{8,14},{9,13},{10,... | collective-permute-start | bytes 196616 | tf_op jit(solution)/shard_map/ppermute | solution.py:227
  36.2 0.0 collective-permute-done.10.refs_2_
  36.2 2.2 %collective-permute-start.13 = (bf16[256,128]{1,0:T(8,128)(2,1)S(1)}, bf16[256,128]{1,0:T(8,128)(2,1)S(1)}, u32[]{:S(2)}, u32[]{:S(2)}) collective-permute-start(bf16[256,128]{1,0:T(8,128)(2,1)S(1)} %get-tuple-element.42), channel_id=1, source_target_pairs={{0,4},{1,7},{2,6},{3,5},{4,0},{5,3},{6,2},{7,1},{8,12},{9,15},{10,... | collective-permute-start | bytes 196616 | tf_op jit(solution)/shard_map/ppermute | solution.py:227
  38.4 0.0 collective-permute-done.8.refs_0_
  38.4 0.0 collective-permute-done.9.refs_1_
  38.4 0.0 collective-permute-done.11.refs_3_
  38.4 1.9 %collective-permute-done.12.refs_4_ = bf16[256,128]{1,0:T(8,128)(2,1)S(1)} collective-permute-done((bf16[256,128]{1,0:T(8,128)(2,1)S(1)}, bf16[256,128]{1,0:T(8,128)(2,1)S(1)}, u32[]{:S(2)}, u32[]{:S(2)}) %collective-permute-start.12) | collective-permute-done | bytes 65568 | tf_op jit(solution)/shard_map/ppermute | solution.py:227
  40.3 1.8 %collective-permute-done.13.refs_5_ = bf16[256,128]{1,0:T(8,128)(2,1)S(1)} collective-permute-done((bf16[256,128]{1,0:T(8,128)(2,1)S(1)}, bf16[256,128]{1,0:T(8,128)(2,1)S(1)}, u32[]{:S(2)}, u32[]{:S(2)}) %collective-permute-start.13) | collective-permute-done | bytes 65568 | tf_op jit(solution)/shard_map/ppermute | solution.py:227
  42.1 0.8 %shard_map.100 = (bf16[128,512]{1,0:T(8,128)(2,1)}, bf16[128,128]{1,0:T(8,128)(2,1)}, bf16[128,128]{1,0:T(8,128)(2,1)}) custom-call(f32[128,512]{1,0:T(8,128)S(1)} %get-tuple-element.30.dq_own, f32[256,128]{1,0:T(8,128)S(1)} %get-tuple-element.36.dkv_own, bf16[128,512]{1,0:T(8,128)(2,1)S(1)} %collective-permute-done.8.refs_0_, ...), custom_call_target="tpu_custom_call" | custom-call | flops 1000 | bytes 1000 | tf_op jit(solution)/shard_map/pallas_call | solution.py:301
  (5 shorter events, 0.0 us)
Async XLA Ops:
  2.0 4.6 %collective-permute-start.1 = (bf16[272,128]{1,0:T(8,128)(2,1)S(1)}, bf16[272,128]{1,0:T(8,128)(2,1)S(1)}, u32[]{:S(2)}, u32[]{:S(2)}) collective-permute-start(bf16[272,128]{1,0:T(8,128)(2,1)S(1)} %get-tuple-element.24.refs_3_.refs_1_), channel_id=1, source_target_pairs={{0,1},{1,0},{2,3},{3,2},{4,5},{5,4},{6,7},{7,6},{8,9},{9,8},{10,11... | collective-permute-start | bytes 208904 | tf_op jit(solution)/shard_map/ppermute | solution.py:25
  2.5 12.9 %collective-permute-start.3 = (bf16[1056,128]{1,0:T(8,128)(2,1)S(1)}, bf16[1056,128]{1,0:T(8,128)(2,1)S(1)}, u32[]{:S(2)}, u32[]{:S(2)}) collective-permute-start(bf16[1056,128]{1,0:T(8,128)(2,1)S(1)} %get-tuple-element.23.refs_0_), channel_id=1, source_target_pairs={{0,8},{8,0},{16,24},{24,16},{1,9},{9,1},{17,25},{25,17},{2,10},{10... | collective-permute-start | bytes 811016 | tf_op jit(solution)/shard_map/ppermute | solution.py:25
  5.1 13.4 %collective-permute-start.4 = (bf16[1056,128]{1,0:T(8,128)(2,1)S(1)}, bf16[1056,128]{1,0:T(8,128)(2,1)S(1)}, u32[]{:S(2)}, u32[]{:S(2)}) collective-permute-start(bf16[1056,128]{1,0:T(8,128)(2,1)S(1)} %get-tuple-element.23.refs_0_), channel_id=1, source_target_pairs={{0,16},{8,24},{16,0},{24,8},{1,17},{9,25},{17,1},{25,9},{2,18},{10... | collective-permute-start | bytes 811016 | tf_op jit(solution)/shard_map/ppermute | solution.py:25
  6.6 8.8 %collective-permute-start.2 = (bf16[544,128]{1,0:T(8,128)(2,1)S(1)}, bf16[544,128]{1,0:T(8,128)(2,1)S(1)}, u32[]{:S(2)}, u32[]{:S(2)}) collective-permute-start(bf16[544,128]{1,0:T(8,128)(2,1)S(1)} %pad_maximum_fusion.1), channel_id=1, source_target_pairs={{0,6},{1,5},{2,4},{3,7},{4,2},{5,1},{6,0},{7,3},{8,14},{9,13},{10,... | collective-permute-start | bytes 417800 | tf_op jit(solution)/shard_map/ppermute | solution.py:227
  10.3 5.1 %collective-permute-start = (bf16[272,128]{1,0:T(8,128)(2,1)S(1)}, bf16[272,128]{1,0:T(8,128)(2,1)S(1)}, u32[]{:S(2)}, u32[]{:S(2)}) collective-permute-start(bf16[272,128]{1,0:T(8,128)(2,1)S(1)} %get-tuple-element.24.refs_3_.refs_1_), channel_id=1, source_target_pairs={{0,2},{1,3},{2,0},{3,1},{4,6},{5,7},{6,4},{7,5},{8,10},{9,11},{10,... | collective-permute-start | bytes 208904 | tf_op jit(solution)/shard_map/ppermute | solution.py:25
  10.3 14.4 %collective-permute-start.6 = (bf16[1056,128]{1,0:T(8,128)(2,1)S(1)}, bf16[1056,128]{1,0:T(8,128)(2,1)S(1)}, u32[]{:S(2)}, u32[]{:S(2)}) collective-permute-start(bf16[1056,128]{1,0:T(8,128)(2,1)S(1)} %get-tuple-element.23.refs_0_), channel_id=1, source_target_pairs={{0,24},{8,16},{16,8},{24,0},{1,25},{9,17},{17,9},{25,1},{2,26},{10... | collective-permute-start | bytes 811016 | tf_op jit(solution)/shard_map/ppermute | solution.py:25
  18.5 3.1 %collective-permute-start.5 = (bf16[816,128]{1,0:T(8,128)(2,1)S(1)}, bf16[816,128]{1,0:T(8,128)(2,1)S(1)}, u32[]{:S(2)}, u32[]{:S(2)}) collective-permute-start(bf16[816,128]{1,0:T(8,128)(2,1)S(1)} %pad_maximum_fusion), channel_id=1, source_target_pairs={{0,1},{1,0},{2,3},{3,2},{4,5},{5,4},{6,7},{7,6},{8,9},{9,8},{10,11... | collective-permute-start | bytes 626696 | tf_op jit(solution)/shard_map/ppermute | solution.py:25
  25.8 5.7 %collective-permute-start.7 = (bf16[4,256,128]{2,1,0:T(8,128)(2,1)S(1)}, bf16[4,256,128]{2,1,0:T(8,128)(2,1)S(1)}, u32[]{:S(2)}, u32[]{:S(2)}) collective-permute-start(bf16[4,256,128]{2,1,0:T(8,128)(2,1)S(1)} %get-tuple-element.35), channel_id=1, source_target_pairs={{0,1},{1,0},{2,3},{3,2},{4,5},{5,4},{6,7},{7,6},{8,9},{9,8},{10,11... | collective-permute-start | bytes 786440 | tf_op jit(solution)/shard_map/ppermute | solution.py:25
  27.5 8.7 %collective-permute-start.10 = (bf16[128,512]{1,0:T(8,128)(2,1)S(1)}, bf16[128,512]{1,0:T(8,128)(2,1)S(1)}, u32[]{:S(2)}, u32[]{:S(2)}) collective-permute-start(bf16[128,512]{1,0:T(8,128)(2,1)S(1)} %get-tuple-element.39), channel_id=1, source_target_pairs={{0,24},{8,16},{16,8},{24,0},{1,25},{9,17},{17,9},{25,1},{2,26},{10... | collective-permute-start | bytes 393224 | tf_op jit(solution)/shard_map/ppermute | solution.py:25
  30.0 8.4 %collective-permute-start.8 = (bf16[128,512]{1,0:T(8,128)(2,1)S(1)}, bf16[128,512]{1,0:T(8,128)(2,1)S(1)}, u32[]{:S(2)}, u32[]{:S(2)}) collective-permute-start(bf16[128,512]{1,0:T(8,128)(2,1)S(1)} %get-tuple-element.37), channel_id=1, source_target_pairs={{0,8},{8,0},{16,24},{24,16},{1,9},{9,1},{17,25},{25,17},{2,10},{10... | collective-permute-start | bytes 393224 | tf_op jit(solution)/shard_map/ppermute | solution.py:25
  31.5 6.9 %collective-permute-start.9 = (bf16[128,512]{1,0:T(8,128)(2,1)S(1)}, bf16[128,512]{1,0:T(8,128)(2,1)S(1)}, u32[]{:S(2)}, u32[]{:S(2)}) collective-permute-start(bf16[128,512]{1,0:T(8,128)(2,1)S(1)} %get-tuple-element.38), channel_id=1, source_target_pairs={{0,16},{8,24},{16,0},{24,8},{1,17},{9,25},{17,1},{25,9},{2,18},{10... | collective-permute-start | bytes 393224 | tf_op jit(solution)/shard_map/ppermute | solution.py:25
  31.6 6.8 %collective-permute-start.11 = (bf16[256,128]{1,0:T(8,128)(2,1)S(1)}, bf16[256,128]{1,0:T(8,128)(2,1)S(1)}, u32[]{:S(2)}, u32[]{:S(2)}) collective-permute-start(bf16[256,128]{1,0:T(8,128)(2,1)S(1)} %get-tuple-element.40), channel_id=1, source_target_pairs={{0,2},{1,3},{2,0},{3,1},{4,6},{5,7},{6,4},{7,5},{8,10},{9,11},{10,... | collective-permute-start | bytes 196616 | tf_op jit(solution)/shard_map/ppermute | solution.py:25
  33.8 6.5 %collective-permute-start.12 = (bf16[256,128]{1,0:T(8,128)(2,1)S(1)}, bf16[256,128]{1,0:T(8,128)(2,1)S(1)}, u32[]{:S(2)}, u32[]{:S(2)}) collective-permute-start(bf16[256,128]{1,0:T(8,128)(2,1)S(1)} %get-tuple-element.41), channel_id=1, source_target_pairs={{0,6},{1,5},{2,4},{3,7},{4,2},{5,1},{6,0},{7,3},{8,14},{9,13},{10,... | collective-permute-start | bytes 196616 | tf_op jit(solution)/shard_map/ppermute | solution.py:227
  36.2 5.9 %collective-permute-start.13 = (bf16[256,128]{1,0:T(8,128)(2,1)S(1)}, bf16[256,128]{1,0:T(8,128)(2,1)S(1)}, u32[]{:S(2)}, u32[]{:S(2)}) collective-permute-start(bf16[256,128]{1,0:T(8,128)(2,1)S(1)} %get-tuple-element.42), channel_id=1, source_target_pairs={{0,4},{1,7},{2,6},{3,5},{4,0},{5,3},{6,2},{7,1},{8,12},{9,15},{10,... | collective-permute-start | bytes 196616 | tf_op jit(solution)/shard_map/ppermute | solution.py:227

commit v5 on v4

--- a/solution.py
+++ b/solution.py
@@ -17,7 +17,7 @@
 NN = (((1,), (0,)), ((), ()))
 NT = (((1,), (1,)), ((), ()))
 QUICK = pl.CostEstimate(flops=1000, bytes_accessed=1000, transcendentals=0)
-COLS = 256
+COLS = 512
 
 
 def swapped(block, axis, mask):
@@ -256,8 +256,7 @@
     pair = jnp.concatenate([kv, sib], axis=0)
     direct = [crossed(pair, t, False) for t in range(1, nz // 2)]
     xs = [x] + [swapped(x, "outer", s) for s in range(1, nq)]
-    early = lax.optimization_barrier((near, *direct, *xs[1:-1]))
-    near, direct, xs = early[0], early[1 : nz // 2], [x, *early[nz // 2 :], xs[-1]]
+    near, *direct = lax.optimization_barrier((near, *direct))
     traded = swapped(jnp.concatenate([near, *direct], axis=0), "inner", 1)
 
     size = kv.shape[0]
@@ -267,24 +266,28 @@
         group_a += [(t + 1, 0), (t + 1, size)]
         group_b += [(1, (2 * t - 1) * size), (1, 2 * t * size)]
     common = (rows, heads, scale)
-    dqs, acc_a = blocks_call(xs[:-1], [kv, sib, *direct], group_a, *common, F32, None, diagonal=True)
-    *dqs, acc_b = blocks_call(
-        xs[:-1], [near, traded], group_b, *common, F32, [F32] + [BF] * (nq - 2), dq_in=dqs
-    )
+    dq_own, acc_a = blocks_call([x], [kv, sib, *direct], group_a, *common, F32, None, diagonal=True)
+    dq_own, acc_b = blocks_call([x], [near, traded], group_b, *common, F32, [F32], dq_in=dq_own)
     arrays = [kv, sib, *direct, near, traded]
     base = len(arrays) - 2
-    in_a = [(n, start, 0, i) for i, (n, start) in enumerate(group_a)]
-    in_b = [(base + n, start, 1, i) for i, (n, start) in enumerate(group_b)]
+    slots = [(n, start, 0, i) for i, (n, start) in enumerate(group_a)]
+    slots += [(base + n, start, 1, i) for i, (n, start) in enumerate(group_b)]
+    acc = (acc_a, acc_b)
+    got = []
+    for s in range(1, nq - 1):
+        dq, acc = blocks_call([xs[s]], arrays, slots, *common, F32, [BF], acc=acc)
+        got.append(swapped(dq, "outer", s))
+        slots = [(n, start, 0, i) for i, (n, start, _, _) in enumerate(slots)]
+        acc = (acc,)
+    in_a, in_b = slots[:nz], slots[nz:]
     theirs, ours = [in_a[1], in_b[1]], [in_a[0], in_b[0]]
     for t in range(1, nz // 2):
         theirs += [in_b[2 * t], in_a[2 * t + 1]]
         ours += [in_a[2 * t], in_b[2 * t + 1]]
-    dq_last, dkv_sib = blocks_call([xs[-1]], arrays, theirs, *common, BF, None, acc=(acc_a, acc_b))
+    dq_last, dkv_sib = blocks_call([xs[-1]], arrays, theirs, *common, BF, None, acc=acc)
     dkv_got = swapped(dkv_sib, "inner", 1)
-    dq_last, dkv_own = blocks_call(
-        [xs[-1]], arrays, ours, *common, F32, [BF], acc=(acc_a, acc_b), dq_in=dq_last
-    )
-    got = [swapped(dq, "outer", s + 1) for s, dq in enumerate([*dqs[1:], dq_last])]
+    dq_last, dkv_own = blocks_call([xs[-1]], arrays, ours, *common, F32, [BF], acc=acc, dq_in=dq_last)
+    got.append(swapped(dq_last, "outer", nq - 1))
     dkv_own, *send = pl.pallas_call(
         add_kernel,
         out_shape=(sds((2 * rows, width), F32),) + (sds((2 * rows, width), BF),) * (nz - 1),
@@ -305,7 +308,7 @@
         out_specs=(VMEM,) * 3,
         compiler_params=SMALL,
         cost_estimate=QUICK,
-    )(dqs[0], dkv_own, *got, *dkv)
+    )(dq_own, dkv_own, *got, *dkv)
 
 
 def solution(mesh):

time: 43.1 us -> 41.2 us (0.956)
  waiting for transfers between devices: 11.3 us -> 17.1 us
  starting transfers between devices: 20.3 us -> 15 us
  Pallas kernels: 10.6 us -> 8.17 us
    ppermute x11, waiting for transfers between devices: 7.58 us -> 13.8 us  [swapped(): return lax.ppermute(block, axis, pairs)]
    ppermute x11, starting transfers between devices: 12 us -> 8.22 us  [swapped(): return lax.ppermute(block, axis, pairs)]
    pallas_call x4 -> x6, Pallas kernels: 8.39 us -> 5.97 us  [blocks_call(): pl.pallas_call(functools.partial(body, plan, rows, heads, scale), out_sha...]
    ppermute x3, starting transfers between devices: 8.31 us -> 6.74 us  [crossed(): return lax.ppermute(block, 'inner', pairs)]
  transfers between devices with their start and end apart: 14 -> 14, of which waited for: 4 -> 10; matrix products, arithmetic and copies ran while one was open for 0% -> 0% of each run, Pallas kernels for 17% -> 13%
where the time goes in v5:
time: 41.2 us; the launch traced here: 41 us
  waiting for transfers between devices  17.1 us (42%)
  starting transfers between devices  15 us (36%)
  Pallas kernels  8.17 us (20%)
  between operations  0.72 us (2%)
    ppermute x11, waiting for transfers between devices, swapped(): return lax.ppermute(block, axis, pairs)  13.8 us
    ppermute x11, starting transfers between devices, swapped(): return lax.ppermute(block, axis, pairs)  8.22 us
    ppermute x3, starting transfers between devices, crossed(): return lax.ppermute(block, 'inner', pairs)  6.74 us
    pallas_call x6, Pallas kernels, blocks_call(): pl.pallas_call(functools.partial(body, plan, rows, heads, scale), out_sha...  5.97 us
    ppermute x3, waiting for transfers between devices, crossed(): return lax.ppermute(block, 'inner', pairs)  3.34 us
    pallas_call x1, Pallas kernels, on_device(): pl.pallas_call(pack_kernel, out_shape=(sds((2 * hr + 32, width), BF), sds...  1.34 us
  transfers between devices with their start and end apart: 14, of which 10 were waited for; matrix products, arithmetic and copies ran while one was open for 0% of the time, Pallas kernels for 13%

profile of v5, /device:TPU:0, one launch (start us, length us, event | category | flops | bytes accessed | tf_op | source)
XLA Modules:
  0.0 41.0 jit_solution(13349380072315592948)
XLA Ops:
  0.6 1.3 %shard_map.94 = (bf16[1056,128]{1,0:T(8,128)(2,1)S(1)}, bf16[272,128]{1,0:T(8,128)(2,1)S(1)}) custom-call(bf16[128,512]{1,0:T(8,128)(2,1)} %q_ref.1, bf16[128,128]{1,0:T(8,128)(2,1)} %k_ref.1, bf16[128,128]{1,0:T(8,128)(2,1)} %v_ref.1, bf16[128,512]{1,0:T(8,128)(2,1)} %o_ref.1, bf16[128,512]{1,0:T(8,128)(2,1)} %g_ref.1, f32[4,128]{1,0:T(4,128)} %lse_ref.1, ...), custom_call_target="tpu_custom_call" | custom-call | flops 1000 | bytes 1000 | tf_op jit(solution)/shard_map/pallas_call | solution.py:239
  2.0 0.5 %collective-permute-start.1 = (bf16[272,128]{1,0:T(8,128)(2,1)S(1)}, bf16[272,128]{1,0:T(8,128)(2,1)S(1)}, u32[]{:S(2)}, u32[]{:S(2)}) collective-permute-start(bf16[272,128]{1,0:T(8,128)(2,1)S(1)} %get-tuple-element.24.refs_1_), channel_id=1, source_target_pairs={{0,1},{1,0},{2,3},{3,2},{4,5},{5,4},{6,7},{7,6},{8,9},{9,8},{10,11... | collective-permute-start | bytes 208904 | tf_op jit(solution)/shard_map/ppermute | solution.py:25
  2.5 0.9 %collective-permute-done.1.refs_2_ = bf16[272,128]{1,0:T(8,128)(2,1)S(1)} collective-permute-done((bf16[272,128]{1,0:T(8,128)(2,1)S(1)}, bf16[272,128]{1,0:T(8,128)(2,1)S(1)}, u32[]{:S(2)}, u32[]{:S(2)}) %collective-permute-start.1) | collective-permute-done | bytes 69664 | tf_op jit(solution)/shard_map/ppermute | solution.py:25
  3.4 5.0 %collective-permute-start.2 = (bf16[544,128]{1,0:T(8,128)(2,1)S(1)}, bf16[544,128]{1,0:T(8,128)(2,1)S(1)}, u32[]{:S(2)}, u32[]{:S(2)}) collective-permute-start(bf16[544,128]{1,0:T(8,128)(2,1)S(1)} %pad_maximum_fusion.1), channel_id=1, source_target_pairs={{0,6},{1,5},{2,4},{3,7},{4,2},{5,1},{6,0},{7,3},{8,14},{9,13},{10,... | collective-permute-start | bytes 417800 | tf_op jit(solution)/shard_map/ppermute | solution.py:227
  8.4 1.5 %collective-permute-start.6 = (bf16[1056,128]{1,0:T(8,128)(2,1)S(1)}, bf16[1056,128]{1,0:T(8,128)(2,1)S(1)}, u32[]{:S(2)}, u32[]{:S(2)}) collective-permute-start(bf16[1056,128]{1,0:T(8,128)(2,1)S(1)} %get-tuple-element.23.refs_0_), channel_id=1, source_target_pairs={{0,8},{8,0},{16,24},{24,16},{1,9},{9,1},{17,25},{25,17},{2,10},{10... | collective-permute-start | bytes 811016 | tf_op jit(solution)/shard_map/ppermute | solution.py:25
  9.9 1.5 %collective-permute-start.5 = (bf16[1056,128]{1,0:T(8,128)(2,1)S(1)}, bf16[1056,128]{1,0:T(8,128)(2,1)S(1)}, u32[]{:S(2)}, u32[]{:S(2)}) collective-permute-start(bf16[1056,128]{1,0:T(8,128)(2,1)S(1)} %get-tuple-element.23.refs_0_), channel_id=1, source_target_pairs={{0,16},{8,24},{16,0},{24,8},{1,17},{9,25},{17,1},{25,9},{2,18},{10... | collective-permute-start | bytes 811016 | tf_op jit(solution)/shard_map/ppermute | solution.py:25
  11.4 0.5 %collective-permute-start.4 = (bf16[1056,128]{1,0:T(8,128)(2,1)S(1)}, bf16[1056,128]{1,0:T(8,128)(2,1)S(1)}, u32[]{:S(2)}, u32[]{:S(2)}) collective-permute-start(bf16[1056,128]{1,0:T(8,128)(2,1)S(1)} %get-tuple-element.23.refs_0_), channel_id=1, source_target_pairs={{0,24},{8,16},{16,8},{24,0},{1,25},{9,17},{17,9},{25,1},{2,26},{10... | collective-permute-start | bytes 811016 | tf_op jit(solution)/shard_map/ppermute | solution.py:25
  11.9 1.7 %collective-permute-done.refs_1_.refs_4_ = bf16[272,128]{1,0:T(8,128)(2,1)S(1)} collective-permute-done((bf16[272,128]{1,0:T(8,128)(2,1)S(1)}, bf16[272,128]{1,0:T(8,128)(2,1)S(1)}, u32[]{:S(2)}, u32[]{:S(2)}) %collective-permute-start) | collective-permute-done | bytes 69664 | tf_op jit(solution)/shard_map/ppermute | solution.py:25
  13.7 0.1 collective-permute-start.3
  13.8 0.8 %shard_map.95 = (f32[1,128,512]{2,1,0:T(8,128)S(1)}, f32[4,256,128]{2,1,0:T(8,128)S(1)}) custom-call(bf16[1056,128]{1,0:T(8,128)(2,1)S(1)} %get-tuple-element.23.refs_0_, bf16[272,128]{1,0:T(8,128)(2,1)S(1)} %get-tuple-element.24.refs_1_, bf16[272,128]{1,0:T(8,128)(2,1)S(1)} %collective-permute-done.1.refs_2_, ...), custom_call_target="tpu_custom_call" | custom-call | flops 1000 | bytes 1000 | tf_op jit(solution)/shard_map/pallas_call | solution.py:191
  14.6 0.6 %collective-permute-done.3.refs_2_.refs_5_ = bf16[816,128]{1,0:T(8,128)(2,1)S(1)} collective-permute-done((bf16[816,128]{1,0:T(8,128)(2,1)S(1)}, bf16[816,128]{1,0:T(8,128)(2,1)S(1)}, u32[]{:S(2)}, u32[]{:S(2)}) %collective-permute-start.3) | collective-permute-done | bytes 208928 | tf_op jit(solution)/shard_map/ppermute | solution.py:25
  15.2 0.8 %shard_map.96 = (f32[128,512]{1,0:T(8,128)S(1)}, f32[4,256,128]{2,1,0:T(8,128)S(1)}) custom-call(bf16[1056,128]{1,0:T(8,128)(2,1)S(1)} %get-tuple-element.23.refs_0_, bf16[272,128]{1,0:T(8,128)(2,1)S(1)} %collective-permute-done.refs_1_.refs_4_, bf16[816,128]{1,0:T(8,128)(2,1)S(1)} %collective-permute-done.3.refs_2_.refs_5_, ...), custom_call_target="tpu_custom_call" | custom-call | flops 1000 | bytes 1000 | tf_op jit(solution)/shard_map/pallas_call | solution.py:191
  16.0 1.8 %collective-permute-done.6.refs_0_ = bf16[1056,128]{1,0:T(8,128)(2,1)S(1)} collective-permute-done((bf16[1056,128]{1,0:T(8,128)(2,1)S(1)}, bf16[1056,128]{1,0:T(8,128)(2,1)S(1)}, u32[]{:S(2)}, u32[]{:S(2)}) %collective-permute-start.6) | collective-permute-done | bytes 270368 | tf_op jit(solution)/shard_map/ppermute | solution.py:25
  17.8 1.4 %shard_map.97 = (bf16[128,512]{1,0:T(8,128)(2,1)S(1)}, f32[8,256,128]{2,1,0:T(8,128)S(1)}) custom-call(bf16[1056,128]{1,0:T(8,128)(2,1)S(1)} %collective-permute-done.6.refs_0_, bf16[272,128]{1,0:T(8,128)(2,1)S(1)} %get-tuple-element.24.refs_1_, bf16[272,128]{1,0:T(8,128)(2,1)S(1)} %collective-permute-done.1.refs_2_, ...), custom_call_target="tpu_custom_call" | custom-call | flops 1000 | bytes 1000 | tf_op jit(solution)/shard_map/pallas_call | solution.py:191
  19.2 4.8 %collective-permute-done.5.refs_0_ = bf16[1056,128]{1,0:T(8,128)(2,1)S(1)} collective-permute-done((bf16[1056,128]{1,0:T(8,128)(2,1)S(1)}, bf16[1056,128]{1,0:T(8,128)(2,1)S(1)}, u32[]{:S(2)}, u32[]{:S(2)}) %collective-permute-start.5) | collective-permute-done | bytes 270368 | tf_op jit(solution)/shard_map/ppermute | solution.py:25
  24.0 1.4 %shard_map.98 = (bf16[128,512]{1,0:T(8,128)(2,1)S(1)}, f32[8,256,128]{2,1,0:T(8,128)S(1)}) custom-call(bf16[1056,128]{1,0:T(8,128)(2,1)S(1)} %collective-permute-done.5.refs_0_, bf16[272,128]{1,0:T(8,128)(2,1)S(1)} %get-tuple-element.24.refs_1_, bf16[272,128]{1,0:T(8,128)(2,1)S(1)} %collective-permute-done.1.refs_2_, ...), custom_call_target="tpu_custom_call" | custom-call | flops 1000 | bytes 1000 | tf_op jit(solution)/shard_map/pallas_call | solution.py:191
  25.4 0.8 %shard_map.99 = (f32[1,128,512]{2,1,0:T(8,128)S(1)}, bf16[4,256,128]{2,1,0:T(8,128)(2,1)S(1)}) custom-call(bf16[1056,128]{1,0:T(8,128)(2,1)S(1)} %collective-permute-done.4.refs_0_, bf16[272,128]{1,0:T(8,128)(2,1)S(1)} %get-tuple-element.24.refs_1_, bf16[272,128]{1,0:T(8,128)(2,1)S(1)} %collective-permute-done.1.refs_2_, ...), custom_call_target="tpu_custom_call" | custom-call | flops 1000 | bytes 1000 | tf_op jit(solution)/shard_map/pallas_call | solution.py:191
  26.2 0.1 collective-permute-start.7
  26.3 0.8 %shard_map.100 = (bf16[128,512]{1,0:T(8,128)(2,1)S(1)}, f32[4,256,128]{2,1,0:T(8,128)S(1)}) custom-call(bf16[1056,128]{1,0:T(8,128)(2,1)S(1)} %collective-permute-done.4.refs_0_, bf16[272,128]{1,0:T(8,128)(2,1)S(1)} %get-tuple-element.24.refs_1_, bf16[272,128]{1,0:T(8,128)(2,1)S(1)} %collective-permute-done.1.refs_2_, ...), custom_call_target="tpu_custom_call" | custom-call | flops 1000 | bytes 1000 | tf_op jit(solution)/shard_map/pallas_call | solution.py:191
  27.1 1.6 %collective-permute-start.10 = (bf16[128,512]{1,0:T(8,128)(2,1)S(1)}, bf16[128,512]{1,0:T(8,128)(2,1)S(1)}, u32[]{:S(2)}, u32[]{:S(2)}) collective-permute-start(bf16[128,512]{1,0:T(8,128)(2,1)S(1)} %get-tuple-element.39), channel_id=1, source_target_pairs={{0,24},{8,16},{16,8},{24,0},{1,25},{9,17},{17,9},{25,1},{2,26},{10... | collective-permute-start | bytes 393224 | tf_op jit(solution)/shard_map/ppermute | solution.py:25
  28.6 0.1 collective-permute-start.9
  28.7 1.9 %collective-permute-start.8 = (bf16[128,512]{1,0:T(8,128)(2,1)S(1)}, bf16[128,512]{1,0:T(8,128)(2,1)S(1)}, u32[]{:S(2)}, u32[]{:S(2)}) collective-permute-start(bf16[128,512]{1,0:T(8,128)(2,1)S(1)} %get-tuple-element.37), channel_id=1, source_target_pairs={{0,8},{8,0},{16,24},{24,16},{1,9},{9,1},{17,25},{25,17},{2,10},{10... | collective-permute-start | bytes 393224 | tf_op jit(solution)/shard_map/ppermute | solution.py:25
  30.6 0.1 shard_map.101
  30.7 0.5 %collective-permute-start.11 = (bf16[256,128]{1,0:T(8,128)(2,1)S(1)}, bf16[256,128]{1,0:T(8,128)(2,1)S(1)}, u32[]{:S(2)}, u32[]{:S(2)}) collective-permute-start(bf16[256,128]{1,0:T(8,128)(2,1)S(1)} %get-tuple-element.40), channel_id=1, source_target_pairs={{0,2},{1,3},{2,0},{3,1},{4,6},{5,7},{6,4},{7,5},{8,10},{9,11},{10,... | collective-permute-start | bytes 196616 | tf_op jit(solution)/shard_map/ppermute | solution.py:25
  31.2 1.4 %collective-permute-start.12 = (bf16[256,128]{1,0:T(8,128)(2,1)S(1)}, bf16[256,128]{1,0:T(8,128)(2,1)S(1)}, u32[]{:S(2)}, u32[]{:S(2)}) collective-permute-start(bf16[256,128]{1,0:T(8,128)(2,1)S(1)} %get-tuple-element.41), channel_id=1, source_target_pairs={{0,6},{1,5},{2,4},{3,7},{4,2},{5,1},{6,0},{7,3},{8,14},{9,13},{10,... | collective-permute-start | bytes 196616 | tf_op jit(solution)/shard_map/ppermute | solution.py:227
  32.6 1.8 %collective-permute-done.10.refs_2_ = bf16[128,512]{1,0:T(8,128)(2,1)S(1)} collective-permute-done((bf16[128,512]{1,0:T(8,128)(2,1)S(1)}, bf16[128,512]{1,0:T(8,128)(2,1)S(1)}, u32[]{:S(2)}, u32[]{:S(2)}) %collective-permute-start.10) | collective-permute-done | bytes 131104 | tf_op jit(solution)/shard_map/ppermute | solution.py:25
  34.4 0.4 collective-permute-start.13
  34.7 2.0 %collective-permute-done.9.refs_1_ = bf16[128,512]{1,0:T(8,128)(2,1)S(1)} collective-permute-done((bf16[128,512]{1,0:T(8,128)(2,1)S(1)}, bf16[128,512]{1,0:T(8,128)(2,1)S(1)}, u32[]{:S(2)}, u32[]{:S(2)}) %collective-permute-start.9) | collective-permute-done | bytes 131104 | tf_op jit(solution)/shard_map/ppermute | solution.py:25
  36.7 0.1 collective-permute-done.8.refs_0_
  36.8 0.5 %collective-permute-done.12.refs_4_ = bf16[256,128]{1,0:T(8,128)(2,1)S(1)} collective-permute-done((bf16[256,128]{1,0:T(8,128)(2,1)S(1)}, bf16[256,128]{1,0:T(8,128)(2,1)S(1)}, u32[]{:S(2)}, u32[]{:S(2)}) %collective-permute-start.12) | collective-permute-done | bytes 65568 | tf_op jit(solution)/shard_map/ppermute | solution.py:227
  37.4 2.8 %collective-permute-done.13.refs_5_ = bf16[256,128]{1,0:T(8,128)(2,1)S(1)} collective-permute-done((bf16[256,128]{1,0:T(8,128)(2,1)S(1)}, bf16[256,128]{1,0:T(8,128)(2,1)S(1)}, u32[]{:S(2)}, u32[]{:S(2)}) %collective-permute-start.13) | collective-permute-done | bytes 65568 | tf_op jit(solution)/shard_map/ppermute | solution.py:227
  40.2 0.8 %shard_map.102 = (bf16[128,512]{1,0:T(8,128)(2,1)}, bf16[128,128]{1,0:T(8,128)(2,1)}, bf16[128,128]{1,0:T(8,128)(2,1)}) custom-call(f32[128,512]{1,0:T(8,128)S(1)} %get-tuple-element.28.dq_own, f32[256,128]{1,0:T(8,128)S(1)} %get-tuple-element.36.dkv_own, bf16[128,512]{1,0:T(8,128)(2,1)S(1)} %collective-permute-done.8.refs_0_, ...), custom_call_target="tpu_custom_call" | custom-call | flops 1000 | bytes 1000 | tf_op jit(solution)/shard_map/pallas_call | solution.py:304
  (7 shorter events, 0.0 us)
Async XLA Ops:
  2.0 1.4 %collective-permute-start.1 = (bf16[272,128]{1,0:T(8,128)(2,1)S(1)}, bf16[272,128]{1,0:T(8,128)(2,1)S(1)}, u32[]{:S(2)}, u32[]{:S(2)}) collective-permute-start(bf16[272,128]{1,0:T(8,128)(2,1)S(1)} %get-tuple-element.24.refs_1_), channel_id=1, source_target_pairs={{0,1},{1,0},{2,3},{3,2},{4,5},{5,4},{6,7},{7,6},{8,9},{9,8},{10,11... | collective-permute-start | bytes 208904 | tf_op jit(solution)/shard_map/ppermute | solution.py:25
  3.4 10.2 %collective-permute-start.2 = (bf16[544,128]{1,0:T(8,128)(2,1)S(1)}, bf16[544,128]{1,0:T(8,128)(2,1)S(1)}, u32[]{:S(2)}, u32[]{:S(2)}) collective-permute-start(bf16[544,128]{1,0:T(8,128)(2,1)S(1)} %pad_maximum_fusion.1), channel_id=1, source_target_pairs={{0,6},{1,5},{2,4},{3,7},{4,2},{5,1},{6,0},{7,3},{8,14},{9,13},{10,... | collective-permute-start | bytes 417800 | tf_op jit(solution)/shard_map/ppermute | solution.py:227
  8.4 5.2 %collective-permute-start = (bf16[272,128]{1,0:T(8,128)(2,1)S(1)}, bf16[272,128]{1,0:T(8,128)(2,1)S(1)}, u32[]{:S(2)}, u32[]{:S(2)}) collective-permute-start(bf16[272,128]{1,0:T(8,128)(2,1)S(1)} %get-tuple-element.24.refs_1_), channel_id=1, source_target_pairs={{0,2},{1,3},{2,0},{3,1},{4,6},{5,7},{6,4},{7,5},{8,10},{9,11},{10,... | collective-permute-start | bytes 208904 | tf_op jit(solution)/shard_map/ppermute | solution.py:25
  8.4 9.3 %collective-permute-start.6 = (bf16[1056,128]{1,0:T(8,128)(2,1)S(1)}, bf16[1056,128]{1,0:T(8,128)(2,1)S(1)}, u32[]{:S(2)}, u32[]{:S(2)}) collective-permute-start(bf16[1056,128]{1,0:T(8,128)(2,1)S(1)} %get-tuple-element.23.refs_0_), channel_id=1, source_target_pairs={{0,8},{8,0},{16,24},{24,16},{1,9},{9,1},{17,25},{25,17},{2,10},{10... | collective-permute-start | bytes 811016 | tf_op jit(solution)/shard_map/ppermute | solution.py:25
  9.9 14.1 %collective-permute-start.5 = (bf16[1056,128]{1,0:T(8,128)(2,1)S(1)}, bf16[1056,128]{1,0:T(8,128)(2,1)S(1)}, u32[]{:S(2)}, u32[]{:S(2)}) collective-permute-start(bf16[1056,128]{1,0:T(8,128)(2,1)S(1)} %get-tuple-element.23.refs_0_), channel_id=1, source_target_pairs={{0,16},{8,24},{16,0},{24,8},{1,17},{9,25},{17,1},{25,9},{2,18},{10... | collective-permute-start | bytes 811016 | tf_op jit(solution)/shard_map/ppermute | solution.py:25
  11.4 14.0 %collective-permute-start.4 = (bf16[1056,128]{1,0:T(8,128)(2,1)S(1)}, bf16[1056,128]{1,0:T(8,128)(2,1)S(1)}, u32[]{:S(2)}, u32[]{:S(2)}) collective-permute-start(bf16[1056,128]{1,0:T(8,128)(2,1)S(1)} %get-tuple-element.23.refs_0_), channel_id=1, source_target_pairs={{0,24},{8,16},{16,8},{24,0},{1,25},{9,17},{17,9},{25,1},{2,26},{10... | collective-permute-start | bytes 811016 | tf_op jit(solution)/shard_map/ppermute | solution.py:25
  13.7 1.5 %collective-permute-start.3 = (bf16[816,128]{1,0:T(8,128)(2,1)S(1)}, bf16[816,128]{1,0:T(8,128)(2,1)S(1)}, u32[]{:S(2)}, u32[]{:S(2)}) collective-permute-start(bf16[816,128]{1,0:T(8,128)(2,1)S(1)} %pad_maximum_fusion), channel_id=1, source_target_pairs={{0,1},{1,0},{2,3},{3,2},{4,5},{5,4},{6,7},{7,6},{8,9},{9,8},{10,11... | collective-permute-start | bytes 626696 | tf_op jit(solution)/shard_map/ppermute | solution.py:25
  26.2 4.4 %collective-permute-start.7 = (bf16[4,256,128]{2,1,0:T(8,128)(2,1)S(1)}, bf16[4,256,128]{2,1,0:T(8,128)(2,1)S(1)}, u32[]{:S(2)}, u32[]{:S(2)}) collective-permute-start(bf16[4,256,128]{2,1,0:T(8,128)(2,1)S(1)} %get-tuple-element.35), channel_id=1, source_target_pairs={{0,1},{1,0},{2,3},{3,2},{4,5},{5,4},{6,7},{7,6},{8,9},{9,8},{10,11... | collective-permute-start | bytes 786440 | tf_op jit(solution)/shard_map/ppermute | solution.py:25
  27.1 7.3 %collective-permute-start.10 = (bf16[128,512]{1,0:T(8,128)(2,1)S(1)}, bf16[128,512]{1,0:T(8,128)(2,1)S(1)}, u32[]{:S(2)}, u32[]{:S(2)}) collective-permute-start(bf16[128,512]{1,0:T(8,128)(2,1)S(1)} %get-tuple-element.39), channel_id=1, source_target_pairs={{0,24},{8,16},{16,8},{24,0},{1,25},{9,17},{17,9},{25,1},{2,26},{10... | collective-permute-start | bytes 393224 | tf_op jit(solution)/shard_map/ppermute | solution.py:25
  28.6 8.1 %collective-permute-start.9 = (bf16[128,512]{1,0:T(8,128)(2,1)S(1)}, bf16[128,512]{1,0:T(8,128)(2,1)S(1)}, u32[]{:S(2)}, u32[]{:S(2)}) collective-permute-start(bf16[128,512]{1,0:T(8,128)(2,1)S(1)} %get-tuple-element.38), channel_id=1, source_target_pairs={{0,16},{8,24},{16,0},{24,8},{1,17},{9,25},{17,1},{25,9},{2,18},{10... | collective-permute-start | bytes 393224 | tf_op jit(solution)/shard_map/ppermute | solution.py:25
  28.7 8.1 %collective-permute-start.8 = (bf16[128,512]{1,0:T(8,128)(2,1)S(1)}, bf16[128,512]{1,0:T(8,128)(2,1)S(1)}, u32[]{:S(2)}, u32[]{:S(2)}) collective-permute-start(bf16[128,512]{1,0:T(8,128)(2,1)S(1)} %get-tuple-element.37), channel_id=1, source_target_pairs={{0,8},{8,0},{16,24},{24,16},{1,9},{9,1},{17,25},{25,17},{2,10},{10... | collective-permute-start | bytes 393224 | tf_op jit(solution)/shard_map/ppermute | solution.py:25
  30.7 6.1 %collective-permute-start.11 = (bf16[256,128]{1,0:T(8,128)(2,1)S(1)}, bf16[256,128]{1,0:T(8,128)(2,1)S(1)}, u32[]{:S(2)}, u32[]{:S(2)}) collective-permute-start(bf16[256,128]{1,0:T(8,128)(2,1)S(1)} %get-tuple-element.40), channel_id=1, source_target_pairs={{0,2},{1,3},{2,0},{3,1},{4,6},{5,7},{6,4},{7,5},{8,10},{9,11},{10,... | collective-permute-start | bytes 196616 | tf_op jit(solution)/shard_map/ppermute | solution.py:25
  31.2 6.2 %collective-permute-start.12 = (bf16[256,128]{1,0:T(8,128)(2,1)S(1)}, bf16[256,128]{1,0:T(8,128)(2,1)S(1)}, u32[]{:S(2)}, u32[]{:S(2)}) collective-permute-start(bf16[256,128]{1,0:T(8,128)(2,1)S(1)} %get-tuple-element.41), channel_id=1, source_target_pairs={{0,6},{1,5},{2,4},{3,7},{4,2},{5,1},{6,0},{7,3},{8,14},{9,13},{10,... | collective-permute-start | bytes 196616 | tf_op jit(solution)/shard_map/ppermute | solution.py:227
  34.4 5.8 %collective-permute-start.13 = (bf16[256,128]{1,0:T(8,128)(2,1)S(1)}, bf16[256,128]{1,0:T(8,128)(2,1)S(1)}, u32[]{:S(2)}, u32[]{:S(2)}) collective-permute-start(bf16[256,128]{1,0:T(8,128)(2,1)S(1)} %get-tuple-element.42), channel_id=1, source_target_pairs={{0,4},{1,7},{2,6},{3,5},{4,0},{5,3},{6,2},{7,1},{8,12},{9,15},{10,... | collective-permute-start | bytes 196616 | tf_op jit(solution)/shard_map/ppermute | solution.py:227

commit v6 on v5

--- a/solution.py
+++ b/solution.py
@@ -82,8 +82,11 @@
 
 
 def blocks_kernel(plan, rows, heads, scale, *refs):
-    x_refs = refs[: plan["queries"]]
-    refs = refs[plan["queries"] :]
+    if plan["halves"]:
+        x_refs, refs = [refs[:2]], refs[2:]
+    else:
+        x_refs = [(x_ref, x_ref.at[heads * rows :, :]) for x_ref in refs[: plan["queries"]]]
+        refs = refs[plan["queries"] :]
     kv_refs = refs[: plan["kv"]]
     refs = refs[plan["kv"] :]
     acc_refs = refs[: plan["acc"]]
@@ -92,14 +95,14 @@
     if plan["dq_in"]:
         dq_in, refs = refs[0], refs[1:]
     dq_refs, dkv_ref = refs[:-1], refs[-1]
-    width = x_refs[0].shape[1]
+    width = x_refs[0][0].shape[1]
     hr = heads * rows
     per = rows // RUN
     step = COLS // rows
     slots = plan["slots"]
     rowed = []
-    for x_ref in x_refs:
-        e = x_ref[2 * hr :, :].astype(F32)
+    for _, g_ref in x_refs:
+        e = g_ref[hr:, :].astype(F32)
         lse = e[0:heads] + e[heads : 2 * heads] + e[2 * heads : 3 * heads]
         delta = e[3 * heads : 4 * heads] + e[4 * heads : 5 * heads] + e[5 * heads : 6 * heads]
         rowed.append((lse, delta, e[6 * heads : 6 * heads + 1]))
@@ -115,11 +118,11 @@
         v = jnp.concatenate(vs, axis=0)
         kt = jnp.concatenate([b.astype(F32).T.astype(BF) for b in ks], axis=1)
         dk = dv = None
-        for b, x_ref in enumerate(x_refs):
+        for b, (q_ref, g_ref) in enumerate(x_refs):
             lse, delta, run = rowed[b]
             for n in range(hr // COLS):
-                q = x_ref[n * COLS : (n + 1) * COLS, :]
-                g = x_ref[hr + n * COLS : hr + (n + 1) * COLS, :]
+                q = q_ref[n * COLS : (n + 1) * COLS, :]
+                g = g_ref[n * COLS : (n + 1) * COLS, :]
                 st = dot(k, q, NT)
                 dpt = dot(v, g, NT)
                 p_rows, d_rows = [], []
@@ -168,12 +171,16 @@
     blocks_kernel(plan, rows, heads, scale, *refs[:-2], *dq_refs, refs[-1])
 
 
-def blocks_call(xs, kvs, slots, rows, heads, scale, dkv_type, dq_types, acc=(), dq_in=None, diagonal=False):
+def blocks_call(
+    xs, kvs, slots, rows, heads, scale, dkv_type, dq_types, acc=(), dq_in=None, diagonal=False, halves=False
+):
     sds = jax.ShapeDtypeStruct
     width = xs[0].shape[1]
     hr = heads * rows
+    queries = 1 if halves else len(xs)
     plan = {
-        "queries": len(xs),
+        "halves": halves,
+        "queries": queries,
         "kv": len(kvs),
         "acc": len(acc),
         "dq_in": dq_in is not None,
@@ -183,7 +190,7 @@
     args = (*xs, *kvs, *acc) + (() if dq_in is None else (dq_in,))
     if dq_types is None:
         body = first_kernel
-        outs = (sds((len(xs), width, hr), F32),)
+        outs = (sds((queries, width, hr), F32),)
     else:
         body = blocks_kernel
         outs = tuple(sds((width, hr), t) for t in dq_types)
@@ -255,8 +262,11 @@
     near = swapped(kv, "inner", 2)
     pair = jnp.concatenate([kv, sib], axis=0)
     direct = [crossed(pair, t, False) for t in range(1, nz // 2)]
-    xs = [x] + [swapped(x, "outer", s) for s in range(1, nq)]
-    near, *direct = lax.optimization_barrier((near, *direct))
+    xs = [swapped(x, "outer", s) for s in range(1, nq - 1)]
+    near, *rest = lax.optimization_barrier((near, *direct, *xs))
+    direct, xs = rest[: len(direct)], [x, *rest[len(direct) :]]
+    one, two = xs[nq - 2], xs[(nq - 1) ^ (nq // 2)]
+    corner = [swapped(one[:hr], "outer", 1), swapped(two[hr:], "outer", nq // 2)]
     traded = swapped(jnp.concatenate([near, *direct], axis=0), "inner", 1)
 
     size = kv.shape[0]
@@ -273,10 +283,10 @@
     slots = [(n, start, 0, i) for i, (n, start) in enumerate(group_a)]
     slots += [(base + n, start, 1, i) for i, (n, start) in enumerate(group_b)]
     acc = (acc_a, acc_b)
-    got = []
+    dqs = []
     for s in range(1, nq - 1):
         dq, acc = blocks_call([xs[s]], arrays, slots, *common, F32, [BF], acc=acc)
-        got.append(swapped(dq, "outer", s))
+        dqs.append(dq)
         slots = [(n, start, 0, i) for i, (n, start, _, _) in enumerate(slots)]
         acc = (acc,)
     in_a, in_b = slots[:nz], slots[nz:]
@@ -284,10 +294,13 @@
     for t in range(1, nz // 2):
         theirs += [in_b[2 * t], in_a[2 * t + 1]]
         ours += [in_a[2 * t], in_b[2 * t + 1]]
-    dq_last, dkv_sib = blocks_call([xs[-1]], arrays, theirs, *common, BF, None, acc=acc)
+    dq_last, dkv_sib = blocks_call(
+        corner, arrays, theirs, *common, BF, None, acc=acc, halves=True
+    )
     dkv_got = swapped(dkv_sib, "inner", 1)
-    dq_last, dkv_own = blocks_call([xs[-1]], arrays, ours, *common, F32, [BF], acc=acc, dq_in=dq_last)
-    got.append(swapped(dq_last, "outer", nq - 1))
+    dq_last, dkv_own = blocks_call(
+        corner, arrays, ours, *common, F32, [BF], acc=acc, dq_in=dq_last, halves=True
+    )
     dkv_own, *send = pl.pallas_call(
         add_kernel,
         out_shape=(sds((2 * rows, width), F32),) + (sds((2 * rows, width), BF),) * (nz - 1),
@@ -296,6 +309,11 @@
         compiler_params=SMALL,
         cost_estimate=QUICK,
     )(dkv_own, dkv_got)
+    got = []
+    for s, dq in enumerate(dqs + [dq_last]):
+        if s:
+            dq = lax.optimization_barrier((dq, got[0], send[-1]))[0]
+        got.append(swapped(dq, "outer", s + 1))
     dkv = [swapped(send[0], "inner", 2)]
     for t in range(1, nz // 2):
         dkv.append(crossed(send[2 * t - 1], t, False))

time: 41.2 us -> 42.2 us (1.024)
  starting transfers between devices: 15 us -> 17.9 us
  waiting for transfers between devices: 17.1 us -> 15.2 us
    ppermute x11 -> x12, waiting for transfers between devices: 13.8 us -> 9.85 us  [swapped(): return lax.ppermute(block, axis, pairs)]
    ppermute x11 -> x12, starting transfers between devices: 8.22 us -> 11 us  [swapped(): return lax.ppermute(block, axis, pairs)]
    ppermute x3, waiting for transfers between devices: 3.34 us -> 5.31 us  [crossed(): return lax.ppermute(block, 'inner', pairs)]
  transfers between devices with their start and end apart: 14 -> 15, of which waited for: 10 -> 6; matrix products, arithmetic and copies ran while one was open for 0% -> 0% of each run, Pallas kernels for 13% -> 12%
where the time goes in v6:
time: 42.2 us; the launch traced here: 42 us
  starting transfers between devices  17.9 us (42%)
  waiting for transfers between devices  15.2 us (36%)
  Pallas kernels  8.17 us (19%)
  between operations  0.74 us (2%)
    ppermute x12, starting transfers between devices, swapped(): return lax.ppermute(block, axis, pairs)  11 us
    ppermute x12, waiting for transfers between devices, swapped(): return lax.ppermute(block, axis, pairs)  9.85 us
    ppermute x3, starting transfers between devices, crossed(): return lax.ppermute(block, 'inner', pairs)  6.96 us
    pallas_call x6, Pallas kernels, blocks_call(): pl.pallas_call(functools.partial(body, plan, rows, heads, scale), out_sha...  5.96 us
    ppermute x3, waiting for transfers between devices, crossed(): return lax.ppermute(block, 'inner', pairs)  5.31 us
    pallas_call x1, Pallas kernels, on_device(): pl.pallas_call(pack_kernel, out_shape=(sds((2 * hr + 32, width), BF), sds...  1.34 us
  transfers between devices with their start and end apart: 15, of which 6 were waited for; matrix products, arithmetic and copies ran while one was open for 0% of the time, Pallas kernels for 12%

profile of v6, /device:TPU:0, one launch (start us, length us, event | category | flops | bytes accessed | tf_op | source)
XLA Modules:
  0.0 42.0 jit_solution(10837784500549879587)
XLA Ops:
  0.6 1.3 %shard_map.94 = (bf16[1056,128]{1,0:T(8,128)(2,1)S(1)}, bf16[272,128]{1,0:T(8,128)(2,1)S(1)}) custom-call(bf16[128,512]{1,0:T(8,128)(2,1)} %q_ref.1, bf16[128,128]{1,0:T(8,128)(2,1)} %k_ref.1, bf16[128,128]{1,0:T(8,128)(2,1)} %v_ref.1, bf16[128,512]{1,0:T(8,128)(2,1)} %o_ref.1, bf16[128,512]{1,0:T(8,128)(2,1)} %g_ref.1, f32[4,128]{1,0:T(4,128)} %lse_ref.1, ...), custom_call_target="tpu_custom_call" | custom-call | flops 1000 | bytes 1000 | tf_op jit(solution)/shard_map/pallas_call | solution.py:246
  2.0 0.5 %collective-permute-start.1 = (bf16[272,128]{1,0:T(8,128)(2,1)S(1)}, bf16[272,128]{1,0:T(8,128)(2,1)S(1)}, u32[]{:S(2)}, u32[]{:S(2)}) collective-permute-start(bf16[272,128]{1,0:T(8,128)(2,1)S(1)} %get-tuple-element.28.refs_1_.refs_2_), channel_id=1, source_target_pairs={{0,1},{1,0},{2,3},{3,2},{4,5},{5,4},{6,7},{7,6},{8,9},{9,8},{10,11... | collective-permute-start | bytes 208904 | tf_op jit(solution)/shard_map/ppermute | solution.py:25
  2.5 2.6 %collective-permute-start.3 = (bf16[1056,128]{1,0:T(8,128)(2,1)S(1)}, bf16[1056,128]{1,0:T(8,128)(2,1)S(1)}, u32[]{:S(2)}, u32[]{:S(2)}) collective-permute-start(bf16[1056,128]{1,0:T(8,128)(2,1)S(1)} %get-tuple-element.27.refs_0_), channel_id=1, source_target_pairs={{0,8},{8,0},{16,24},{24,16},{1,9},{9,1},{17,25},{25,17},{2,10},{10... | collective-permute-start | bytes 811016 | tf_op jit(solution)/shard_map/ppermute | solution.py:25
  5.1 1.5 %collective-permute-start.4 = (bf16[1056,128]{1,0:T(8,128)(2,1)S(1)}, bf16[1056,128]{1,0:T(8,128)(2,1)S(1)}, u32[]{:S(2)}, u32[]{:S(2)}) collective-permute-start(bf16[1056,128]{1,0:T(8,128)(2,1)S(1)} %get-tuple-element.27.refs_0_), channel_id=1, source_target_pairs={{0,16},{8,24},{16,0},{24,8},{1,17},{9,25},{17,1},{25,9},{2,18},{10... | collective-permute-start | bytes 811016 | tf_op jit(solution)/shard_map/ppermute | solution.py:25
  6.6 0.0 collective-permute-done.1.refs_2_.refs_3_
  6.6 3.7 %collective-permute-start.2 = (bf16[544,128]{1,0:T(8,128)(2,1)S(1)}, bf16[544,128]{1,0:T(8,128)(2,1)S(1)}, u32[]{:S(2)}, u32[]{:S(2)}) collective-permute-start(bf16[544,128]{1,0:T(8,128)(2,1)S(1)} %pad_maximum_fusion.1), channel_id=1, source_target_pairs={{0,6},{1,5},{2,4},{3,7},{4,2},{5,1},{6,0},{7,3},{8,14},{9,13},{10,... | collective-permute-start | bytes 417800 | tf_op jit(solution)/shard_map/ppermute | solution.py:234
  10.3 0.0 collective-permute-start
  10.3 5.1 %collective-permute-done.refs_1_.refs_4_.refs_5_ = bf16[272,128]{1,0:T(8,128)(2,1)S(1)} collective-permute-done((bf16[272,128]{1,0:T(8,128)(2,1)S(1)}, bf16[272,128]{1,0:T(8,128)(2,1)S(1)}, u32[]{:S(2)}, u32[]{:S(2)}) %collective-permute-start) | collective-permute-done | bytes 69664 | tf_op jit(solution)/shard_map/ppermute | solution.py:25
  15.4 0.0 collective-permute-done.2.refs_3_.refs_4_
  15.4 0.0 collective-permute-done.3.refs_0_
  15.4 0.1 collective-permute-start.5
  15.5 0.6 %collective-permute-start.7 = (bf16[544,128]{1,0:T(8,128)(2,1)S(1)}, bf16[544,128]{1,0:T(8,128)(2,1)S(1)}, u32[]{:S(2)}, u32[]{:S(2)}) collective-permute-start(bf16[544,128]{1,0:T(8,128)(2,1)S(1)} %slice.7), channel_id=1, source_target_pairs={{0,16},{8,24},{16,0},{24,8},{1,17},{9,25},{17,1},{25,9},{2,18},{10... | collective-permute-start | bytes 417800 | tf_op jit(solution)/shard_map/ppermute | solution.py:25
  16.1 1.0 %collective-permute-start.6 = (bf16[512,128]{1,0:T(8,128)(2,1)S(1)}, bf16[512,128]{1,0:T(8,128)(2,1)S(1)}, u32[]{:S(2)}, u32[]{:S(2)}) collective-permute-start(bf16[512,128]{1,0:T(8,128)(2,1)S(1)} %slice.6), channel_id=1, source_target_pairs={{0,8},{8,0},{16,24},{24,16},{1,9},{9,1},{17,25},{25,17},{2,10},{10... | collective-permute-start | bytes 393224 | tf_op jit(solution)/shard_map/ppermute | solution.py:25
  17.1 0.8 %shard_map.95 = (f32[1,128,512]{2,1,0:T(8,128)S(1)}, f32[4,256,128]{2,1,0:T(8,128)S(1)}) custom-call(bf16[1056,128]{1,0:T(8,128)(2,1)S(1)} %get-tuple-element.27.refs_0_, bf16[272,128]{1,0:T(8,128)(2,1)S(1)} %get-tuple-element.28.refs_1_.refs_2_, bf16[272,128]{1,0:T(8,128)(2,1)S(1)} %collective-permute-done.1.refs_2_.refs_3_, ...), custom_call_target="tpu_custom_call" | custom-call | flops 1000 | bytes 1000 | tf_op jit(solution)/shard_map/pallas_call | solution.py:198
  17.9 0.8 %shard_map.96 = (f32[128,512]{1,0:T(8,128)S(1)}, f32[4,256,128]{2,1,0:T(8,128)S(1)}) custom-call(bf16[1056,128]{1,0:T(8,128)(2,1)S(1)} %get-tuple-element.27.refs_0_, bf16[272,128]{1,0:T(8,128)(2,1)S(1)} %collective-permute-done.refs_1_.refs_4_.refs_5_, bf16[816,128]{1,0:T(8,128)(2,1)S(1)} %collective-permute-done.5.refs_2_.refs_5_.refs_6_, ...), custom_call_target="tpu_custom_call" | custom-call | flops 1000 | bytes 1000 | tf_op jit(solution)/shard_map/pallas_call | solution.py:198
  18.7 1.4 %shard_map.97 = (bf16[128,512]{1,0:T(8,128)(2,1)S(1)}, f32[8,256,128]{2,1,0:T(8,128)S(1)}) custom-call(bf16[1056,128]{1,0:T(8,128)(2,1)S(1)} %collective-permute-done.3.refs_0_, bf16[272,128]{1,0:T(8,128)(2,1)S(1)} %get-tuple-element.28.refs_1_.refs_2_, bf16[272,128]{1,0:T(8,128)(2,1)S(1)} %collective-permute-done.1.refs_2_.refs_3_, ...), custom_call_target="tpu_custom_call" | custom-call | flops 1000 | bytes 1000 | tf_op jit(solution)/shard_map/pallas_call | solution.py:198
  20.1 1.4 %shard_map.98 = (bf16[128,512]{1,0:T(8,128)(2,1)S(1)}, f32[8,256,128]{2,1,0:T(8,128)S(1)}) custom-call(bf16[1056,128]{1,0:T(8,128)(2,1)S(1)} %collective-permute-done.4.refs_0_, bf16[272,128]{1,0:T(8,128)(2,1)S(1)} %get-tuple-element.28.refs_1_.refs_2_, bf16[272,128]{1,0:T(8,128)(2,1)S(1)} %collective-permute-done.1.refs_2_.refs_3_, ...), custom_call_target="tpu_custom_call" | custom-call | flops 1000 | bytes 1000 | tf_op jit(solution)/shard_map/pallas_call | solution.py:198
  21.5 0.3 collective-permute-done.6.refs_0_
  21.8 0.8 %shard_map.99 = (f32[1,128,512]{2,1,0:T(8,128)S(1)}, bf16[4,256,128]{2,1,0:T(8,128)(2,1)S(1)}) custom-call(bf16[512,128]{1,0:T(8,128)(2,1)S(1)} %collective-permute-done.6.refs_0_, bf16[544,128]{1,0:T(8,128)(2,1)S(1)} %collective-permute-done.7.refs_1_, bf16[272,128]{1,0:T(8,128)(2,1)S(1)} %get-tuple-element.28.refs_1_.refs_2_, ...), custom_call_target="tpu_custom_call" | custom-call | flops 1000 | bytes 1000 | tf_op jit(solution)/shard_map/pallas_call | solution.py:198
  22.6 0.1 collective-permute-start.8
  22.7 1.0 %collective-permute-start.9 = (bf16[128,512]{1,0:T(8,128)(2,1)S(1)}, bf16[128,512]{1,0:T(8,128)(2,1)S(1)}, u32[]{:S(2)}, u32[]{:S(2)}) collective-permute-start(bf16[128,512]{1,0:T(8,128)(2,1)S(1)} %get-tuple-element.43), channel_id=1, source_target_pairs={{0,8},{8,0},{16,24},{24,16},{1,9},{9,1},{17,25},{25,17},{2,10},{10... | collective-permute-start | bytes 393224 | tf_op jit(solution)/shard_map/ppermute | solution.py:25
  23.6 0.8 %shard_map.100 = (bf16[128,512]{1,0:T(8,128)(2,1)S(1)}, f32[4,256,128]{2,1,0:T(8,128)S(1)}) custom-call(bf16[512,128]{1,0:T(8,128)(2,1)S(1)} %collective-permute-done.6.refs_0_, bf16[544,128]{1,0:T(8,128)(2,1)S(1)} %collective-permute-done.7.refs_1_, bf16[272,128]{1,0:T(8,128)(2,1)S(1)} %get-tuple-element.28.refs_1_.refs_2_, ...), custom_call_target="tpu_custom_call" | custom-call | flops 1000 | bytes 1000 | tf_op jit(solution)/shard_map/pallas_call | solution.py:198
  24.4 0.1 shard_map.101
  24.5 4.1 %collective-permute-done.9.refs_0_ = bf16[128,512]{1,0:T(8,128)(2,1)S(1)} collective-permute-done((bf16[128,512]{1,0:T(8,128)(2,1)S(1)}, bf16[128,512]{1,0:T(8,128)(2,1)S(1)}, u32[]{:S(2)}, u32[]{:S(2)}) %collective-permute-start.9) | collective-permute-done | bytes 131104 | tf_op jit(solution)/shard_map/ppermute | solution.py:25
  28.6 1.8 %collective-permute-start.11 = (bf16[128,512]{1,0:T(8,128)(2,1)S(1)}, bf16[128,512]{1,0:T(8,128)(2,1)S(1)}, u32[]{:S(2)}, u32[]{:S(2)}) collective-permute-start(bf16[128,512]{1,0:T(8,128)(2,1)S(1)} %get-tuple-element.48), channel_id=1, source_target_pairs={{0,24},{8,16},{16,8},{24,0},{1,25},{9,17},{17,9},{25,1},{2,26},{10... | collective-permute-start | bytes 393224 | tf_op jit(solution)/shard_map/ppermute | solution.py:25
  30.4 0.5 %collective-permute-start.10 = (bf16[128,512]{1,0:T(8,128)(2,1)S(1)}, bf16[128,512]{1,0:T(8,128)(2,1)S(1)}, u32[]{:S(2)}, u32[]{:S(2)}) collective-permute-start(bf16[128,512]{1,0:T(8,128)(2,1)S(1)} %get-tuple-element.46), channel_id=1, source_target_pairs={{0,16},{8,24},{16,0},{24,8},{1,17},{9,25},{17,1},{25,9},{2,18},{10... | collective-permute-start | bytes 393224 | tf_op jit(solution)/shard_map/ppermute | solution.py:25
  31.0 1.3 %collective-permute-start.12 = (bf16[256,128]{1,0:T(8,128)(2,1)S(1)}, bf16[256,128]{1,0:T(8,128)(2,1)S(1)}, u32[]{:S(2)}, u32[]{:S(2)}) collective-permute-start(bf16[256,128]{1,0:T(8,128)(2,1)S(1)} %get-tuple-element.49), channel_id=1, source_target_pairs={{0,2},{1,3},{2,0},{3,1},{4,6},{5,7},{6,4},{7,5},{8,10},{9,11},{10,... | collective-permute-start | bytes 196616 | tf_op jit(solution)/shard_map/ppermute | solution.py:25
  32.3 3.3 %collective-permute-start.13 = (bf16[256,128]{1,0:T(8,128)(2,1)S(1)}, bf16[256,128]{1,0:T(8,128)(2,1)S(1)}, u32[]{:S(2)}, u32[]{:S(2)}) collective-permute-start(bf16[256,128]{1,0:T(8,128)(2,1)S(1)} %get-tuple-element.50), channel_id=1, source_target_pairs={{0,6},{1,5},{2,4},{3,7},{4,2},{5,1},{6,0},{7,3},{8,14},{9,13},{10,... | collective-permute-start | bytes 196616 | tf_op jit(solution)/shard_map/ppermute | solution.py:234
  35.6 0.4 collective-permute-done.12.refs_3_
  35.9 2.9 %collective-permute-done.13.refs_4_ = bf16[256,128]{1,0:T(8,128)(2,1)S(1)} collective-permute-done((bf16[256,128]{1,0:T(8,128)(2,1)S(1)}, bf16[256,128]{1,0:T(8,128)(2,1)S(1)}, u32[]{:S(2)}, u32[]{:S(2)}) %collective-permute-start.13) | collective-permute-done | bytes 65568 | tf_op jit(solution)/shard_map/ppermute | solution.py:234
  38.8 2.4 %collective-permute-done.14.refs_5_ = bf16[256,128]{1,0:T(8,128)(2,1)S(1)} collective-permute-done((bf16[256,128]{1,0:T(8,128)(2,1)S(1)}, bf16[256,128]{1,0:T(8,128)(2,1)S(1)}, u32[]{:S(2)}, u32[]{:S(2)}) %collective-permute-start.14) | collective-permute-done | bytes 65568 | tf_op jit(solution)/shard_map/ppermute | solution.py:234
  41.2 0.8 %shard_map.102 = (bf16[128,512]{1,0:T(8,128)(2,1)}, bf16[128,128]{1,0:T(8,128)(2,1)}, bf16[128,128]{1,0:T(8,128)(2,1)}) custom-call(f32[128,512]{1,0:T(8,128)S(1)} %get-tuple-element.32.dq_own, f32[256,128]{1,0:T(8,128)S(1)} %get-tuple-element.42.dkv_own, bf16[128,512]{1,0:T(8,128)(2,1)S(1)} %collective-permute-done.9.refs_0_, ...), custom_call_target="tpu_custom_call" | custom-call | flops 1000 | bytes 1000 | tf_op jit(solution)/shard_map/pallas_call | solution.py:322
  (11 shorter events, 0.1 us)
Async XLA Ops:
  2.0 4.6 %collective-permute-start.1 = (bf16[272,128]{1,0:T(8,128)(2,1)S(1)}, bf16[272,128]{1,0:T(8,128)(2,1)S(1)}, u32[]{:S(2)}, u32[]{:S(2)}) collective-permute-start(bf16[272,128]{1,0:T(8,128)(2,1)S(1)} %get-tuple-element.28.refs_1_.refs_2_), channel_id=1, source_target_pairs={{0,1},{1,0},{2,3},{3,2},{4,5},{5,4},{6,7},{7,6},{8,9},{9,8},{10,11... | collective-permute-start | bytes 208904 | tf_op jit(solution)/shard_map/ppermute | solution.py:25
  2.5 12.9 %collective-permute-start.3 = (bf16[1056,128]{1,0:T(8,128)(2,1)S(1)}, bf16[1056,128]{1,0:T(8,128)(2,1)S(1)}, u32[]{:S(2)}, u32[]{:S(2)}) collective-permute-start(bf16[1056,128]{1,0:T(8,128)(2,1)S(1)} %get-tuple-element.27.refs_0_), channel_id=1, source_target_pairs={{0,8},{8,0},{16,24},{24,16},{1,9},{9,1},{17,25},{25,17},{2,10},{10... | collective-permute-start | bytes 811016 | tf_op jit(solution)/shard_map/ppermute | solution.py:25
  5.1 10.3 %collective-permute-start.4 = (bf16[1056,128]{1,0:T(8,128)(2,1)S(1)}, bf16[1056,128]{1,0:T(8,128)(2,1)S(1)}, u32[]{:S(2)}, u32[]{:S(2)}) collective-permute-start(bf16[1056,128]{1,0:T(8,128)(2,1)S(1)} %get-tuple-element.27.refs_0_), channel_id=1, source_target_pairs={{0,16},{8,24},{16,0},{24,8},{1,17},{9,25},{17,1},{25,9},{2,18},{10... | collective-permute-start | bytes 811016 | tf_op jit(solution)/shard_map/ppermute | solution.py:25
  6.6 8.8 %collective-permute-start.2 = (bf16[544,128]{1,0:T(8,128)(2,1)S(1)}, bf16[544,128]{1,0:T(8,128)(2,1)S(1)}, u32[]{:S(2)}, u32[]{:S(2)}) collective-permute-start(bf16[544,128]{1,0:T(8,128)(2,1)S(1)} %pad_maximum_fusion.1), channel_id=1, source_target_pairs={{0,6},{1,5},{2,4},{3,7},{4,2},{5,1},{6,0},{7,3},{8,14},{9,13},{10,... | collective-permute-start | bytes 417800 | tf_op jit(solution)/shard_map/ppermute | solution.py:234
  10.3 5.1 %collective-permute-start = (bf16[272,128]{1,0:T(8,128)(2,1)S(1)}, bf16[272,128]{1,0:T(8,128)(2,1)S(1)}, u32[]{:S(2)}, u32[]{:S(2)}) collective-permute-start(bf16[272,128]{1,0:T(8,128)(2,1)S(1)} %get-tuple-element.28.refs_1_.refs_2_), channel_id=1, source_target_pairs={{0,2},{1,3},{2,0},{3,1},{4,6},{5,7},{6,4},{7,5},{8,10},{9,11},{10,... | collective-permute-start | bytes 208904 | tf_op jit(solution)/shard_map/ppermute | solution.py:25
  15.4 2.5 %collective-permute-start.5 = (bf16[816,128]{1,0:T(8,128)(2,1)S(1)}, bf16[816,128]{1,0:T(8,128)(2,1)S(1)}, u32[]{:S(2)}, u32[]{:S(2)}) collective-permute-start(bf16[816,128]{1,0:T(8,128)(2,1)S(1)} %pad_maximum_fusion), channel_id=1, source_target_pairs={{0,1},{1,0},{2,3},{3,2},{4,5},{5,4},{6,7},{7,6},{8,9},{9,8},{10,11... | collective-permute-start | bytes 626696 | tf_op jit(solution)/shard_map/ppermute | solution.py:25
  15.5 6.3 %collective-permute-start.7 = (bf16[544,128]{1,0:T(8,128)(2,1)S(1)}, bf16[544,128]{1,0:T(8,128)(2,1)S(1)}, u32[]{:S(2)}, u32[]{:S(2)}) collective-permute-start(bf16[544,128]{1,0:T(8,128)(2,1)S(1)} %slice.7), channel_id=1, source_target_pairs={{0,16},{8,24},{16,0},{24,8},{1,17},{9,25},{17,1},{25,9},{2,18},{10... | collective-permute-start | bytes 417800 | tf_op jit(solution)/shard_map/ppermute | solution.py:25
  16.1 5.7 %collective-permute-start.6 = (bf16[512,128]{1,0:T(8,128)(2,1)S(1)}, bf16[512,128]{1,0:T(8,128)(2,1)S(1)}, u32[]{:S(2)}, u32[]{:S(2)}) collective-permute-start(bf16[512,128]{1,0:T(8,128)(2,1)S(1)} %slice.6), channel_id=1, source_target_pairs={{0,8},{8,0},{16,24},{24,16},{1,9},{9,1},{17,25},{25,17},{2,10},{10... | collective-permute-start | bytes 393224 | tf_op jit(solution)/shard_map/ppermute | solution.py:25
  22.6 1.8 %collective-permute-start.8 = (bf16[4,256,128]{2,1,0:T(8,128)(2,1)S(1)}, bf16[4,256,128]{2,1,0:T(8,128)(2,1)S(1)}, u32[]{:S(2)}, u32[]{:S(2)}) collective-permute-start(bf16[4,256,128]{2,1,0:T(8,128)(2,1)S(1)} %get-tuple-element.41), channel_id=1, source_target_pairs={{0,1},{1,0},{2,3},{3,2},{4,5},{5,4},{6,7},{7,6},{8,9},{9,8},{10,11... | collective-permute-start | bytes 786440 | tf_op jit(solution)/shard_map/ppermute | solution.py:25
  22.7 5.9 %collective-permute-start.9 = (bf16[128,512]{1,0:T(8,128)(2,1)S(1)}, bf16[128,512]{1,0:T(8,128)(2,1)S(1)}, u32[]{:S(2)}, u32[]{:S(2)}) collective-permute-start(bf16[128,512]{1,0:T(8,128)(2,1)S(1)} %get-tuple-element.43), channel_id=1, source_target_pairs={{0,8},{8,0},{16,24},{24,16},{1,9},{9,1},{17,25},{25,17},{2,10},{10... | collective-permute-start | bytes 393224 | tf_op jit(solution)/shard_map/ppermute | solution.py:25
  28.6 12.7 %collective-permute-start.11 = (bf16[128,512]{1,0:T(8,128)(2,1)S(1)}, bf16[128,512]{1,0:T(8,128)(2,1)S(1)}, u32[]{:S(2)}, u32[]{:S(2)}) collective-permute-start(bf16[128,512]{1,0:T(8,128)(2,1)S(1)} %get-tuple-element.48), channel_id=1, source_target_pairs={{0,24},{8,16},{16,8},{24,0},{1,25},{9,17},{17,9},{25,1},{2,26},{10... | collective-permute-start | bytes 393224 | tf_op jit(solution)/shard_map/ppermute | solution.py:25
  30.4 10.8 %collective-permute-start.10 = (bf16[128,512]{1,0:T(8,128)(2,1)S(1)}, bf16[128,512]{1,0:T(8,128)(2,1)S(1)}, u32[]{:S(2)}, u32[]{:S(2)}) collective-permute-start(bf16[128,512]{1,0:T(8,128)(2,1)S(1)} %get-tuple-element.46), channel_id=1, source_target_pairs={{0,16},{8,24},{16,0},{24,8},{1,17},{9,25},{17,1},{25,9},{2,18},{10... | collective-permute-start | bytes 393224 | tf_op jit(solution)/shard_map/ppermute | solution.py:25
  31.0 5.0 %collective-permute-start.12 = (bf16[256,128]{1,0:T(8,128)(2,1)S(1)}, bf16[256,128]{1,0:T(8,128)(2,1)S(1)}, u32[]{:S(2)}, u32[]{:S(2)}) collective-permute-start(bf16[256,128]{1,0:T(8,128)(2,1)S(1)} %get-tuple-element.49), channel_id=1, source_target_pairs={{0,2},{1,3},{2,0},{3,1},{4,6},{5,7},{6,4},{7,5},{8,10},{9,11},{10,... | collective-permute-start | bytes 196616 | tf_op jit(solution)/shard_map/ppermute | solution.py:25
  32.3 6.5 %collective-permute-start.13 = (bf16[256,128]{1,0:T(8,128)(2,1)S(1)}, bf16[256,128]{1,0:T(8,128)(2,1)S(1)}, u32[]{:S(2)}, u32[]{:S(2)}) collective-permute-start(bf16[256,128]{1,0:T(8,128)(2,1)S(1)} %get-tuple-element.50), channel_id=1, source_target_pairs={{0,6},{1,5},{2,4},{3,7},{4,2},{5,1},{6,0},{7,3},{8,14},{9,13},{10,... | collective-permute-start | bytes 196616 | tf_op jit(solution)/shard_map/ppermute | solution.py:234
  35.6 5.7 %collective-permute-start.14 = (bf16[256,128]{1,0:T(8,128)(2,1)S(1)}, bf16[256,128]{1,0:T(8,128)(2,1)S(1)}, u32[]{:S(2)}, u32[]{:S(2)}) collective-permute-start(bf16[256,128]{1,0:T(8,128)(2,1)S(1)} %get-tuple-element.45), channel_id=1, source_target_pairs={{0,4},{1,7},{2,6},{3,5},{4,0},{5,3},{6,2},{7,1},{8,12},{9,15},{10,... | collective-permute-start | bytes 196616 | tf_op jit(solution)/shard_map/ppermute | solution.py:234

commit v7 on v6

--- a/solution.py
+++ b/solution.py
@@ -211,19 +211,23 @@
         ref[...] = (own_ref[n + 1] + got_ref[n + 1].astype(F32)).astype(BF)
 
 
-def final_kernel(rows, heads, scale, n_dq, dq_own, dkv_own, *refs):
-    dq_refs, dkv_refs, (gq_ref, gk_ref, gv_ref) = refs[:n_dq], refs[n_dq:-3], refs[-3:]
+def sum_kernel(own_ref, *refs):
+    total = own_ref[...]
+    for ref in refs[:-1]:
+        total = total + ref[...].astype(F32)
+    refs[-1][...] = total
+
+
+def final_kernel(rows, heads, scale, dq_own, dkv_ref, *refs):
+    dq_refs, (gq_ref, gk_ref, gv_ref) = refs[:-3], refs[-3:]
     dq = dq_own[...]
     for r in dq_refs:
         dq = dq + r[...].astype(F32)
     for h in range(heads):
         part = dq[:, h * rows : (h + 1) * rows]
         gq_ref[:, h * 128 : (h + 1) * 128] = (scale * part).T.astype(BF)
-    dkv = dkv_own[...]
-    for r in dkv_refs:
-        dkv = dkv + r[...].astype(F32)
-    gk_ref[...] = (scale * dkv[:rows]).astype(BF)
-    gv_ref[...] = dkv[rows:].astype(BF)
+    gk_ref[...] = (scale * dkv_ref[:rows, :]).astype(BF)
+    gv_ref[...] = dkv_ref[rows:, :].astype(BF)
 
 
 def crossed(block, t, other):
@@ -263,10 +267,10 @@
     pair = jnp.concatenate([kv, sib], axis=0)
     direct = [crossed(pair, t, False) for t in range(1, nz // 2)]
     xs = [swapped(x, "outer", s) for s in range(1, nq - 1)]
-    near, *rest = lax.optimization_barrier((near, *direct, *xs))
-    direct, xs = rest[: len(direct)], [x, *rest[len(direct) :]]
-    one, two = xs[nq - 2], xs[(nq - 1) ^ (nq // 2)]
-    corner = [swapped(one[:hr], "outer", 1), swapped(two[hr:], "outer", nq // 2)]
+    xs = [x, *lax.optimization_barrier(tuple(xs))]
+    halves = [xs[nq - 2][:hr], xs[(nq - 1) ^ (nq // 2)][hr:]]
+    corner = [swapped(halves[0], "outer", 1), swapped(halves[1], "outer", nq // 2)]
+    near, *direct = lax.optimization_barrier((near, *direct, *halves))[: nz // 2]
     traded = swapped(jnp.concatenate([near, *direct], axis=0), "inner", 1)
 
     size = kv.shape[0]
@@ -276,20 +280,15 @@
         group_a += [(t + 1, 0), (t + 1, size)]
         group_b += [(1, (2 * t - 1) * size), (1, 2 * t * size)]
     common = (rows, heads, scale)
-    dq_own, acc_a = blocks_call([x], [kv, sib, *direct], group_a, *common, F32, None, diagonal=True)
-    dq_own, acc_b = blocks_call([x], [near, traded], group_b, *common, F32, [F32], dq_in=dq_own)
+    dqs, acc_a = blocks_call(xs, [kv, sib, *direct], group_a, *common, F32, None, diagonal=True)
+    *dqs, acc_b = blocks_call(
+        xs, [near, traded], group_b, *common, F32, [F32] + [BF] * (nq - 2), dq_in=dqs
+    )
     arrays = [kv, sib, *direct, near, traded]
     base = len(arrays) - 2
-    slots = [(n, start, 0, i) for i, (n, start) in enumerate(group_a)]
-    slots += [(base + n, start, 1, i) for i, (n, start) in enumerate(group_b)]
+    in_a = [(n, start, 0, i) for i, (n, start) in enumerate(group_a)]
+    in_b = [(base + n, start, 1, i) for i, (n, start) in enumerate(group_b)]
     acc = (acc_a, acc_b)
-    dqs = []
-    for s in range(1, nq - 1):
-        dq, acc = blocks_call([xs[s]], arrays, slots, *common, F32, [BF], acc=acc)
-        dqs.append(dq)
-        slots = [(n, start, 0, i) for i, (n, start, _, _) in enumerate(slots)]
-        acc = (acc,)
-    in_a, in_b = slots[:nz], slots[nz:]
     theirs, ours = [in_a[1], in_b[1]], [in_a[0], in_b[0]]
     for t in range(1, nz // 2):
         theirs += [in_b[2 * t], in_a[2 * t + 1]]
@@ -309,24 +308,32 @@
         compiler_params=SMALL,
         cost_estimate=QUICK,
     )(dkv_own, dkv_got)
-    got = []
-    for s, dq in enumerate(dqs + [dq_last]):
-        if s:
-            dq = lax.optimization_barrier((dq, got[0], send[-1]))[0]
-        got.append(swapped(dq, "outer", s + 1))
+    dq_own, *dqs = dqs
+    got = [swapped(dq, "outer", s + 1) for s, dq in enumerate(dqs)]
+    dq_last, got[0] = lax.optimization_barrier((dq_last, got[0]))
+    got.append(swapped(dq_last, "outer", nq - 1))
     dkv = [swapped(send[0], "inner", 2)]
     for t in range(1, nz // 2):
         dkv.append(crossed(send[2 * t - 1], t, False))
         dkv.append(crossed(send[2 * t], t, True))
 
+    dkv_sum = pl.pallas_call(
+        sum_kernel,
+        out_shape=sds((2 * rows, width), F32),
+        in_specs=[VMEM] * nz,
+        out_specs=VMEM,
+        compiler_params=SMALL,
+        cost_estimate=pl.CostEstimate(flops=1_500_000_000, bytes_accessed=1000, transcendentals=0),
+    )(dkv_own, *dkv)
+
     return pl.pallas_call(
-        functools.partial(final_kernel, rows, heads, scale, len(got)),
+        functools.partial(final_kernel, rows, heads, scale),
         out_shape=(sds((rows, heads * width), BF), sds((rows, width), BF), sds((rows, width), BF)),
-        in_specs=[VMEM] * (2 + len(got) + len(dkv)),
+        in_specs=[VMEM] * (2 + len(got)),
         out_specs=(VMEM,) * 3,
         compiler_params=SMALL,
         cost_estimate=QUICK,
-    )(dq_own, dkv_own, *got, *dkv)
+    )(dq_own, dkv_sum, *got)
 
 
 def solution(mesh):

time: 42.2 us -> 37.8 us (0.90)
  waiting for transfers between devices: 15.2 us -> 10.5 us
    ppermute x12, waiting for transfers between devices: 9.85 us -> 6.98 us  [swapped(): return lax.ppermute(block, axis, pairs)]
    ppermute x3, waiting for transfers between devices: 5.31 us -> 3.57 us  [crossed(): return lax.ppermute(block, 'inner', pairs)]
    pallas_call x6 -> x4, Pallas kernels: 5.96 us -> 5.94 us  [blocks_call(): pl.pallas_call(functools.partial(body, plan, rows, heads, scale), out_sha...]
  transfers between devices with their start and end apart: 15 -> 15, of which waited for: 6 -> 7; matrix products, arithmetic and copies ran while one was open for 0% -> 0% of each run, Pallas kernels for 12% -> 14%
where the time goes in v7:
time: 37.8 us; the launch traced here: 37.7 us
  starting transfers between devices  18.2 us (48%)
  waiting for transfers between devices  10.5 us (28%)
  Pallas kernels  8.17 us (22%)
  between operations  0.73 us (2%)
    ppermute x12, starting transfers between devices, swapped(): return lax.ppermute(block, axis, pairs)  11.1 us
    ppermute x3, starting transfers between devices, crossed(): return lax.ppermute(block, 'inner', pairs)  7.02 us
    ppermute x12, waiting for transfers between devices, swapped(): return lax.ppermute(block, axis, pairs)  6.98 us
    pallas_call x4, Pallas kernels, blocks_call(): pl.pallas_call(functools.partial(body, plan, rows, heads, scale), out_sha...  5.94 us
    ppermute x3, waiting for transfers between devices, crossed(): return lax.ppermute(block, 'inner', pairs)  3.57 us
    pallas_call x1, Pallas kernels, on_device(): pl.pallas_call(pack_kernel, out_shape=(sds((2 * hr + 32, width), BF), sds...  1.33 us
    pallas_call x1, Pallas kernels, on_device(): pl.pallas_call(functools.partial(final_kernel, rows, heads, scale), out_s...  0.8 us
  transfers between devices with their start and end apart: 15, of which 7 were waited for; matrix products, arithmetic and copies ran while one was open for 0% of the time, Pallas kernels for 14%

profile of v7, /device:TPU:0, one launch (start us, length us, event | category | flops | bytes accessed | tf_op | source)
XLA Modules:
  0.0 37.7 jit_solution(8558841196345751473)
XLA Ops:
  0.6 1.3 %shard_map.94 = (bf16[1056,128]{1,0:T(8,128)(2,1)S(1)}, bf16[272,128]{1,0:T(8,128)(2,1)S(1)}) custom-call(bf16[128,512]{1,0:T(8,128)(2,1)} %q_ref.1, bf16[128,128]{1,0:T(8,128)(2,1)} %k_ref.1, bf16[128,128]{1,0:T(8,128)(2,1)} %v_ref.1, bf16[128,512]{1,0:T(8,128)(2,1)} %o_ref.1, bf16[128,512]{1,0:T(8,128)(2,1)} %g_ref.1, f32[4,128]{1,0:T(4,128)} %lse_ref.1, ...), custom_call_target="tpu_custom_call" | custom-call | flops 1000 | bytes 1000 | tf_op jit(solution)/shard_map/pallas_call | solution.py:250
  2.0 0.5 %collective-permute-start.3 = (bf16[272,128]{1,0:T(8,128)(2,1)S(1)}, bf16[272,128]{1,0:T(8,128)(2,1)S(1)}, u32[]{:S(2)}, u32[]{:S(2)}) collective-permute-start(bf16[272,128]{1,0:T(8,128)(2,1)S(1)} %get-tuple-element.28.refs_3_.refs_2_), channel_id=1, source_target_pairs={{0,1},{1,0},{2,3},{3,2},{4,5},{5,4},{6,7},{7,6},{8,9},{9,8},{10,11... | collective-permute-start | bytes 208904 | tf_op jit(solution)/shard_map/ppermute | solution.py:25
  2.5 2.6 %collective-permute-start.1 = (bf16[1056,128]{1,0:T(8,128)(2,1)S(1)}, bf16[1056,128]{1,0:T(8,128)(2,1)S(1)}, u32[]{:S(2)}, u32[]{:S(2)}) collective-permute-start(bf16[1056,128]{1,0:T(8,128)(2,1)S(1)} %get-tuple-element.25.refs_0_), channel_id=1, source_target_pairs={{0,16},{8,24},{16,0},{24,8},{1,17},{9,25},{17,1},{25,9},{2,18},{10... | collective-permute-start | bytes 811016 | tf_op jit(solution)/shard_map/ppermute | solution.py:25
  5.1 1.5 %collective-permute-start = (bf16[1056,128]{1,0:T(8,128)(2,1)S(1)}, bf16[1056,128]{1,0:T(8,128)(2,1)S(1)}, u32[]{:S(2)}, u32[]{:S(2)}) collective-permute-start(bf16[1056,128]{1,0:T(8,128)(2,1)S(1)} %get-tuple-element.25.refs_0_), channel_id=1, source_target_pairs={{0,8},{8,0},{16,24},{24,16},{1,9},{9,1},{17,25},{25,17},{2,10},{10... | collective-permute-start | bytes 811016 | tf_op jit(solution)/shard_map/ppermute | solution.py:25
  6.6 0.0 collective-permute-done.3.refs_4_.refs_3_
  6.6 3.7 %collective-permute-start.4 = (bf16[544,128]{1,0:T(8,128)(2,1)S(1)}, bf16[544,128]{1,0:T(8,128)(2,1)S(1)}, u32[]{:S(2)}, u32[]{:S(2)}) collective-permute-start(bf16[544,128]{1,0:T(8,128)(2,1)S(1)} %pad_maximum_fusion.1), channel_id=1, source_target_pairs={{0,6},{1,5},{2,4},{3,7},{4,2},{5,1},{6,0},{7,3},{8,14},{9,13},{10,... | collective-permute-start | bytes 417800 | tf_op jit(solution)/shard_map/ppermute | solution.py:238
  10.3 0.0 collective-permute-start.2
  10.3 1.9 %collective-permute-done.1.refs_2_ = bf16[1056,128]{1,0:T(8,128)(2,1)S(1)} collective-permute-done((bf16[1056,128]{1,0:T(8,128)(2,1)S(1)}, bf16[1056,128]{1,0:T(8,128)(2,1)S(1)}, u32[]{:S(2)}, u32[]{:S(2)}) %collective-permute-start.1) | collective-permute-done | bytes 270368 | tf_op jit(solution)/shard_map/ppermute | solution.py:25
  12.2 1.5 %collective-permute-done.refs_1_ = bf16[1056,128]{1,0:T(8,128)(2,1)S(1)} collective-permute-done((bf16[1056,128]{1,0:T(8,128)(2,1)S(1)}, bf16[1056,128]{1,0:T(8,128)(2,1)S(1)}, u32[]{:S(2)}, u32[]{:S(2)}) %collective-permute-start) | collective-permute-done | bytes 270368 | tf_op jit(solution)/shard_map/ppermute | solution.py:25
  13.7 1.7 %collective-permute-done.2.refs_3_.refs_5_ = bf16[272,128]{1,0:T(8,128)(2,1)S(1)} collective-permute-done((bf16[272,128]{1,0:T(8,128)(2,1)S(1)}, bf16[272,128]{1,0:T(8,128)(2,1)S(1)}, u32[]{:S(2)}, u32[]{:S(2)}) %collective-permute-start.2) | collective-permute-done | bytes 69664 | tf_op jit(solution)/shard_map/ppermute | solution.py:25
  15.4 0.1 collective-permute-start.5
  15.5 0.6 %collective-permute-start.7 = (bf16[544,128]{1,0:T(8,128)(2,1)S(1)}, bf16[544,128]{1,0:T(8,128)(2,1)S(1)}, u32[]{:S(2)}, u32[]{:S(2)}) collective-permute-start(bf16[544,128]{1,0:T(8,128)(2,1)S(1)} %slice.7), channel_id=1, source_target_pairs={{0,16},{8,24},{16,0},{24,8},{1,17},{9,25},{17,1},{25,9},{2,18},{10... | collective-permute-start | bytes 417800 | tf_op jit(solution)/shard_map/ppermute | solution.py:25
  16.1 0.9 %collective-permute-start.6 = (bf16[512,128]{1,0:T(8,128)(2,1)S(1)}, bf16[512,128]{1,0:T(8,128)(2,1)S(1)}, u32[]{:S(2)}, u32[]{:S(2)}) collective-permute-start(bf16[512,128]{1,0:T(8,128)(2,1)S(1)} %slice.6), channel_id=1, source_target_pairs={{0,8},{8,0},{16,24},{24,16},{1,9},{9,1},{17,25},{25,17},{2,10},{10... | collective-permute-start | bytes 393224 | tf_op jit(solution)/shard_map/ppermute | solution.py:25
  17.0 2.2 %shard_map.95 = (f32[3,128,512]{2,1,0:T(8,128)S(1)}, f32[4,256,128]{2,1,0:T(8,128)S(1)}) custom-call(bf16[1056,128]{1,0:T(8,128)(2,1)S(1)} %get-tuple-element.25.refs_0_, bf16[1056,128]{1,0:T(8,128)(2,1)S(1)} %collective-permute-done.refs_1_, bf16[1056,128]{1,0:T(8,128)(2,1)S(1)} %collective-permute-done.1.refs_2_, ...), custom_call_target="tpu_custom_call" | custom-call | flops 1000 | bytes 1000 | tf_op jit(solution)/shard_map/pallas_call | solution.py:198
  19.2 2.2 %shard_map.96 = (f32[128,512]{1,0:T(8,128)S(1)}, bf16[128,512]{1,0:T(8,128)(2,1)S(1)}, bf16[128,512]{1,0:T(8,128)(2,1)S(1)}, f32[4,256,128]{2,1,0:T(8,128)S(1)}) custom-call(bf16[1056,128]{1,0:T(8,128)(2,1)S(1)} %get-tuple-element.25.refs_0_, bf16[1056,128]{1,0:T(8,128)(2,1)S(1)} %collective-permute-done.refs_1_, ...), custom_call_target="tpu_custom_call" | custom-call | flops 1000 | bytes 1000 | tf_op jit(solution)/shard_map/pallas_call | solution.py:198
  21.4 0.3 collective-permute-done.6.refs_0_
  21.6 0.0 collective-permute-done.7.refs_1_
  21.6 0.8 %shard_map.97 = (f32[1,128,512]{2,1,0:T(8,128)S(1)}, bf16[4,256,128]{2,1,0:T(8,128)(2,1)S(1)}) custom-call(bf16[512,128]{1,0:T(8,128)(2,1)S(1)} %collective-permute-done.6.refs_0_, bf16[544,128]{1,0:T(8,128)(2,1)S(1)} %collective-permute-done.7.refs_1_, bf16[272,128]{1,0:T(8,128)(2,1)S(1)} %get-tuple-element.28.refs_3_.refs_2_, ...), custom_call_target="tpu_custom_call" | custom-call | flops 1000 | bytes 1000 | tf_op jit(solution)/shard_map/pallas_call | solution.py:198
  22.4 0.1 collective-permute-start.8
  22.5 1.0 %collective-permute-start.12 = (bf16[128,512]{1,0:T(8,128)(2,1)S(1)}, bf16[128,512]{1,0:T(8,128)(2,1)S(1)}, u32[]{:S(2)}, u32[]{:S(2)}) collective-permute-start(bf16[128,512]{1,0:T(8,128)(2,1)S(1)} %get-tuple-element.43), channel_id=1, source_target_pairs={{0,8},{8,0},{16,24},{24,16},{1,9},{9,1},{17,25},{25,17},{2,10},{10... | collective-permute-start | bytes 393224 | tf_op jit(solution)/shard_map/ppermute | solution.py:25
  23.5 0.8 %shard_map.98 = (bf16[128,512]{1,0:T(8,128)(2,1)S(1)}, f32[4,256,128]{2,1,0:T(8,128)S(1)}) custom-call(bf16[512,128]{1,0:T(8,128)(2,1)S(1)} %collective-permute-done.6.refs_0_, bf16[544,128]{1,0:T(8,128)(2,1)S(1)} %collective-permute-done.7.refs_1_, bf16[272,128]{1,0:T(8,128)(2,1)S(1)} %get-tuple-element.28.refs_3_.refs_2_, ...), custom_call_target="tpu_custom_call" | custom-call | flops 1000 | bytes 1000 | tf_op jit(solution)/shard_map/pallas_call | solution.py:198
  24.3 0.1 shard_map.99
  24.3 1.3 %collective-permute-start.9 = (bf16[256,128]{1,0:T(8,128)(2,1)S(1)}, bf16[256,128]{1,0:T(8,128)(2,1)S(1)}, u32[]{:S(2)}, u32[]{:S(2)}) collective-permute-start(bf16[256,128]{1,0:T(8,128)(2,1)S(1)} %get-tuple-element.39), channel_id=1, source_target_pairs={{0,2},{1,3},{2,0},{3,1},{4,6},{5,7},{6,4},{7,5},{8,10},{9,11},{10,... | collective-permute-start | bytes 196616 | tf_op jit(solution)/shard_map/ppermute | solution.py:25
  25.7 3.4 %collective-permute-start.10 = (bf16[256,128]{1,0:T(8,128)(2,1)S(1)}, bf16[256,128]{1,0:T(8,128)(2,1)S(1)}, u32[]{:S(2)}, u32[]{:S(2)}) collective-permute-start(bf16[256,128]{1,0:T(8,128)(2,1)S(1)} %get-tuple-element.40), channel_id=1, source_target_pairs={{0,6},{1,5},{2,4},{3,7},{4,2},{5,1},{6,0},{7,3},{8,14},{9,13},{10,... | collective-permute-start | bytes 196616 | tf_op jit(solution)/shard_map/ppermute | solution.py:238
  29.0 0.0 collective-permute-start.11
  29.0 1.5 %collective-permute-start.13 = (bf16[128,512]{1,0:T(8,128)(2,1)S(1)}, bf16[128,512]{1,0:T(8,128)(2,1)S(1)}, u32[]{:S(2)}, u32[]{:S(2)}) collective-permute-start(bf16[128,512]{1,0:T(8,128)(2,1)S(1)} %get-tuple-element.45), channel_id=1, source_target_pairs={{0,16},{8,24},{16,0},{24,8},{1,17},{9,25},{17,1},{25,9},{2,18},{10... | collective-permute-start | bytes 393224 | tf_op jit(solution)/shard_map/ppermute | solution.py:25
  30.6 0.0 collective-permute-done.12.refs_0_
  30.6 1.1 %collective-permute-start.14 = (bf16[128,512]{1,0:T(8,128)(2,1)S(1)}, bf16[128,512]{1,0:T(8,128)(2,1)S(1)}, u32[]{:S(2)}, u32[]{:S(2)}) collective-permute-start(bf16[128,512]{1,0:T(8,128)(2,1)S(1)} %get-tuple-element.46), channel_id=1, source_target_pairs={{0,24},{8,16},{16,8},{24,0},{1,25},{9,17},{17,9},{25,1},{2,26},{10... | collective-permute-start | bytes 393224 | tf_op jit(solution)/shard_map/ppermute | solution.py:25
  31.7 1.0 %collective-permute-done.10.refs_1_ = bf16[256,128]{1,0:T(8,128)(2,1)S(1)} collective-permute-done((bf16[256,128]{1,0:T(8,128)(2,1)S(1)}, bf16[256,128]{1,0:T(8,128)(2,1)S(1)}, u32[]{:S(2)}, u32[]{:S(2)}) %collective-permute-start.10) | collective-permute-done | bytes 65568 | tf_op jit(solution)/shard_map/ppermute | solution.py:238
  32.6 2.6 %collective-permute-done.11.refs_2_ = bf16[256,128]{1,0:T(8,128)(2,1)S(1)} collective-permute-done((bf16[256,128]{1,0:T(8,128)(2,1)S(1)}, bf16[256,128]{1,0:T(8,128)(2,1)S(1)}, u32[]{:S(2)}, u32[]{:S(2)}) %collective-permute-start.11) | collective-permute-done | bytes 65568 | tf_op jit(solution)/shard_map/ppermute | solution.py:238
  35.3 1.6 %collective-permute-done.13.refs_1_ = bf16[128,512]{1,0:T(8,128)(2,1)S(1)} collective-permute-done((bf16[128,512]{1,0:T(8,128)(2,1)S(1)}, bf16[128,512]{1,0:T(8,128)(2,1)S(1)}, u32[]{:S(2)}, u32[]{:S(2)}) %collective-permute-start.13) | collective-permute-done | bytes 131104 | tf_op jit(solution)/shard_map/ppermute | solution.py:25
  36.9 0.8 %shard_map.101 = (bf16[128,512]{1,0:T(8,128)(2,1)}, bf16[128,128]{1,0:T(8,128)(2,1)}, bf16[128,128]{1,0:T(8,128)(2,1)}) custom-call(f32[128,512]{1,0:T(8,128)S(1)} %get-tuple-element.32.dq_own, f32[256,128]{1,0:T(8,128)S(1)} %shard_map.100.dkv_ref, bf16[128,512]{1,0:T(8,128)(2,1)S(1)} %collective-permute-done.12.refs_0_, ...), custom_call_target="tpu_custom_call" | custom-call | flops 1000 | bytes 1000 | tf_op jit(solution)/shard_map/pallas_call | solution.py:329
  (10 shorter events, 0.1 us)
Async XLA Ops:
  2.0 4.6 %collective-permute-start.3 = (bf16[272,128]{1,0:T(8,128)(2,1)S(1)}, bf16[272,128]{1,0:T(8,128)(2,1)S(1)}, u32[]{:S(2)}, u32[]{:S(2)}) collective-permute-start(bf16[272,128]{1,0:T(8,128)(2,1)S(1)} %get-tuple-element.28.refs_3_.refs_2_), channel_id=1, source_target_pairs={{0,1},{1,0},{2,3},{3,2},{4,5},{5,4},{6,7},{7,6},{8,9},{9,8},{10,11... | collective-permute-start | bytes 208904 | tf_op jit(solution)/shard_map/ppermute | solution.py:25
  2.5 9.7 %collective-permute-start.1 = (bf16[1056,128]{1,0:T(8,128)(2,1)S(1)}, bf16[1056,128]{1,0:T(8,128)(2,1)S(1)}, u32[]{:S(2)}, u32[]{:S(2)}) collective-permute-start(bf16[1056,128]{1,0:T(8,128)(2,1)S(1)} %get-tuple-element.25.refs_0_), channel_id=1, source_target_pairs={{0,16},{8,24},{16,0},{24,8},{1,17},{9,25},{17,1},{25,9},{2,18},{10... | collective-permute-start | bytes 811016 | tf_op jit(solution)/shard_map/ppermute | solution.py:25
  5.1 8.6 %collective-permute-start = (bf16[1056,128]{1,0:T(8,128)(2,1)S(1)}, bf16[1056,128]{1,0:T(8,128)(2,1)S(1)}, u32[]{:S(2)}, u32[]{:S(2)}) collective-permute-start(bf16[1056,128]{1,0:T(8,128)(2,1)S(1)} %get-tuple-element.25.refs_0_), channel_id=1, source_target_pairs={{0,8},{8,0},{16,24},{24,16},{1,9},{9,1},{17,25},{25,17},{2,10},{10... | collective-permute-start | bytes 811016 | tf_op jit(solution)/shard_map/ppermute | solution.py:25
  6.6 8.8 %collective-permute-start.4 = (bf16[544,128]{1,0:T(8,128)(2,1)S(1)}, bf16[544,128]{1,0:T(8,128)(2,1)S(1)}, u32[]{:S(2)}, u32[]{:S(2)}) collective-permute-start(bf16[544,128]{1,0:T(8,128)(2,1)S(1)} %pad_maximum_fusion.1), channel_id=1, source_target_pairs={{0,6},{1,5},{2,4},{3,7},{4,2},{5,1},{6,0},{7,3},{8,14},{9,13},{10,... | collective-permute-start | bytes 417800 | tf_op jit(solution)/shard_map/ppermute | solution.py:238
  10.3 5.1 %collective-permute-start.2 = (bf16[272,128]{1,0:T(8,128)(2,1)S(1)}, bf16[272,128]{1,0:T(8,128)(2,1)S(1)}, u32[]{:S(2)}, u32[]{:S(2)}) collective-permute-start(bf16[272,128]{1,0:T(8,128)(2,1)S(1)} %get-tuple-element.28.refs_3_.refs_2_), channel_id=1, source_target_pairs={{0,2},{1,3},{2,0},{3,1},{4,6},{5,7},{6,4},{7,5},{8,10},{9,11},{10,... | collective-permute-start | bytes 208904 | tf_op jit(solution)/shard_map/ppermute | solution.py:25
  15.4 3.8 %collective-permute-start.5 = (bf16[816,128]{1,0:T(8,128)(2,1)S(1)}, bf16[816,128]{1,0:T(8,128)(2,1)S(1)}, u32[]{:S(2)}, u32[]{:S(2)}) collective-permute-start(bf16[816,128]{1,0:T(8,128)(2,1)S(1)} %pad_maximum_fusion), channel_id=1, source_target_pairs={{0,1},{1,0},{2,3},{3,2},{4,5},{5,4},{6,7},{7,6},{8,9},{9,8},{10,11... | collective-permute-start | bytes 626696 | tf_op jit(solution)/shard_map/ppermute | solution.py:25
  15.5 6.1 %collective-permute-start.7 = (bf16[544,128]{1,0:T(8,128)(2,1)S(1)}, bf16[544,128]{1,0:T(8,128)(2,1)S(1)}, u32[]{:S(2)}, u32[]{:S(2)}) collective-permute-start(bf16[544,128]{1,0:T(8,128)(2,1)S(1)} %slice.7), channel_id=1, source_target_pairs={{0,16},{8,24},{16,0},{24,8},{1,17},{9,25},{17,1},{25,9},{2,18},{10... | collective-permute-start | bytes 417800 | tf_op jit(solution)/shard_map/ppermute | solution.py:25
  16.1 5.6 %collective-permute-start.6 = (bf16[512,128]{1,0:T(8,128)(2,1)S(1)}, bf16[512,128]{1,0:T(8,128)(2,1)S(1)}, u32[]{:S(2)}, u32[]{:S(2)}) collective-permute-start(bf16[512,128]{1,0:T(8,128)(2,1)S(1)} %slice.6), channel_id=1, source_target_pairs={{0,8},{8,0},{16,24},{24,16},{1,9},{9,1},{17,25},{25,17},{2,10},{10... | collective-permute-start | bytes 393224 | tf_op jit(solution)/shard_map/ppermute | solution.py:25
  22.4 1.8 %collective-permute-start.8 = (bf16[4,256,128]{2,1,0:T(8,128)(2,1)S(1)}, bf16[4,256,128]{2,1,0:T(8,128)(2,1)S(1)}, u32[]{:S(2)}, u32[]{:S(2)}) collective-permute-start(bf16[4,256,128]{2,1,0:T(8,128)(2,1)S(1)} %get-tuple-element.37), channel_id=1, source_target_pairs={{0,1},{1,0},{2,3},{3,2},{4,5},{5,4},{6,7},{7,6},{8,9},{9,8},{10,11... | collective-permute-start | bytes 786440 | tf_op jit(solution)/shard_map/ppermute | solution.py:25
  22.5 8.0 %collective-permute-start.12 = (bf16[128,512]{1,0:T(8,128)(2,1)S(1)}, bf16[128,512]{1,0:T(8,128)(2,1)S(1)}, u32[]{:S(2)}, u32[]{:S(2)}) collective-permute-start(bf16[128,512]{1,0:T(8,128)(2,1)S(1)} %get-tuple-element.43), channel_id=1, source_target_pairs={{0,8},{8,0},{16,24},{24,16},{1,9},{9,1},{17,25},{25,17},{2,10},{10... | collective-permute-start | bytes 393224 | tf_op jit(solution)/shard_map/ppermute | solution.py:25
  24.3 7.3 %collective-permute-start.9 = (bf16[256,128]{1,0:T(8,128)(2,1)S(1)}, bf16[256,128]{1,0:T(8,128)(2,1)S(1)}, u32[]{:S(2)}, u32[]{:S(2)}) collective-permute-start(bf16[256,128]{1,0:T(8,128)(2,1)S(1)} %get-tuple-element.39), channel_id=1, source_target_pairs={{0,2},{1,3},{2,0},{3,1},{4,6},{5,7},{6,4},{7,5},{8,10},{9,11},{10,... | collective-permute-start | bytes 196616 | tf_op jit(solution)/shard_map/ppermute | solution.py:25
  25.7 6.9 %collective-permute-start.10 = (bf16[256,128]{1,0:T(8,128)(2,1)S(1)}, bf16[256,128]{1,0:T(8,128)(2,1)S(1)}, u32[]{:S(2)}, u32[]{:S(2)}) collective-permute-start(bf16[256,128]{1,0:T(8,128)(2,1)S(1)} %get-tuple-element.40), channel_id=1, source_target_pairs={{0,6},{1,5},{2,4},{3,7},{4,2},{5,1},{6,0},{7,3},{8,14},{9,13},{10,... | collective-permute-start | bytes 196616 | tf_op jit(solution)/shard_map/ppermute | solution.py:238
  29.0 6.2 %collective-permute-start.11 = (bf16[256,128]{1,0:T(8,128)(2,1)S(1)}, bf16[256,128]{1,0:T(8,128)(2,1)S(1)}, u32[]{:S(2)}, u32[]{:S(2)}) collective-permute-start(bf16[256,128]{1,0:T(8,128)(2,1)S(1)} %get-tuple-element.41), channel_id=1, source_target_pairs={{0,4},{1,7},{2,6},{3,5},{4,0},{5,3},{6,2},{7,1},{8,12},{9,15},{10,... | collective-permute-start | bytes 196616 | tf_op jit(solution)/shard_map/ppermute | solution.py:238
  29.0 7.8 %collective-permute-start.13 = (bf16[128,512]{1,0:T(8,128)(2,1)S(1)}, bf16[128,512]{1,0:T(8,128)(2,1)S(1)}, u32[]{:S(2)}, u32[]{:S(2)}) collective-permute-start(bf16[128,512]{1,0:T(8,128)(2,1)S(1)} %get-tuple-element.45), channel_id=1, source_target_pairs={{0,16},{8,24},{16,0},{24,8},{1,17},{9,25},{17,1},{25,9},{2,18},{10... | collective-permute-start | bytes 393224 | tf_op jit(solution)/shard_map/ppermute | solution.py:25
  30.6 6.3 %collective-permute-start.14 = (bf16[128,512]{1,0:T(8,128)(2,1)S(1)}, bf16[128,512]{1,0:T(8,128)(2,1)S(1)}, u32[]{:S(2)}, u32[]{:S(2)}) collective-permute-start(bf16[128,512]{1,0:T(8,128)(2,1)S(1)} %get-tuple-element.46), channel_id=1, source_target_pairs={{0,24},{8,16},{16,8},{24,0},{1,25},{9,17},{17,9},{25,1},{2,26},{10... | collective-permute-start | bytes 393224 | tf_op jit(solution)/shard_map/ppermute | solution.py:25

commit v8 on v7

--- a/solution.py
+++ b/solution.py
@@ -271,21 +271,23 @@
     halves = [xs[nq - 2][:hr], xs[(nq - 1) ^ (nq // 2)][hr:]]
     corner = [swapped(halves[0], "outer", 1), swapped(halves[1], "outer", nq // 2)]
     near, *direct = lax.optimization_barrier((near, *direct, *halves))[: nz // 2]
-    traded = swapped(jnp.concatenate([near, *direct], axis=0), "inner", 1)
-
     size = kv.shape[0]
+    near_sib = swapped(near, "inner", 1)
+    traded = [[swapped(p[n : n + size], "inner", 1) for n in (0, size)] for p in direct]
+
     group_a = [(0, 0), (1, 0)]
     group_b = [(0, 0), (1, 0)]
     for t in range(1, nz // 2):
         group_a += [(t + 1, 0), (t + 1, size)]
-        group_b += [(1, (2 * t - 1) * size), (1, 2 * t * size)]
+        group_b += [(2 * t, 0), (2 * t + 1, 0)]
+    far = [near, near_sib, *sum(traded, [])]
     common = (rows, heads, scale)
     dqs, acc_a = blocks_call(xs, [kv, sib, *direct], group_a, *common, F32, None, diagonal=True)
     *dqs, acc_b = blocks_call(
-        xs, [near, traded], group_b, *common, F32, [F32] + [BF] * (nq - 2), dq_in=dqs
-    )
-    arrays = [kv, sib, *direct, near, traded]
-    base = len(arrays) - 2
+        xs, far, group_b, *common, F32, [F32] + [BF] * (nq - 2), dq_in=dqs
+    )
+    arrays = [kv, sib, *direct, *far]
+    base = 1 + nz // 2
     in_a = [(n, start, 0, i) for i, (n, start) in enumerate(group_a)]
     in_b = [(base + n, start, 1, i) for i, (n, start) in enumerate(group_b)]
     acc = (acc_a, acc_b)
@@ -310,12 +312,13 @@
     )(dkv_own, dkv_got)
     dq_own, *dqs = dqs
     got = [swapped(dq, "outer", s + 1) for s, dq in enumerate(dqs)]
-    dq_last, got[0] = lax.optimization_barrier((dq_last, got[0]))
+    dq_last, *got = lax.optimization_barrier((dq_last, *got))
     got.append(swapped(dq_last, "outer", nq - 1))
-    dkv = [swapped(send[0], "inner", 2)]
+    dkv = []
     for t in range(1, nz // 2):
         dkv.append(crossed(send[2 * t - 1], t, False))
         dkv.append(crossed(send[2 * t], t, True))
+    dkv.append(swapped(send[0], "inner", 2))
 
     dkv_sum = pl.pallas_call(
         sum_kernel,

time: 37.8 us -> 36.4 us (0.963)
  waiting for transfers between devices: 10.5 us -> 7.79 us
  starting transfers between devices: 18.2 us -> 19.4 us
    ppermute x12 -> x14, waiting for transfers between devices: 6.98 us -> 4.65 us  [swapped(): return lax.ppermute(block, axis, pairs)]
    ppermute x12 -> x14, starting transfers between devices: 11.1 us -> 12.1 us  [swapped(): return lax.ppermute(block, axis, pairs)]
    ppermute x3, waiting for transfers between devices: 3.57 us -> 3.14 us  [crossed(): return lax.ppermute(block, 'inner', pairs)]
  transfers between devices with their start and end apart: 15 -> 17, of which waited for: 7 -> 5; matrix products, arithmetic and copies ran while one was open for 0% -> 0% of each run, Pallas kernels for 14% -> 15%
where the time goes in v8:
time: 36.4 us; the launch traced here: 36.2 us
  starting transfers between devices  19.4 us (53%)
  Pallas kernels  8.2 us (23%)
  waiting for transfers between devices  7.79 us (21%)
  between operations  0.76 us (2%)
    ppermute x14, starting transfers between devices, swapped(): return lax.ppermute(block, axis, pairs)  12.1 us
    ppermute x3, starting transfers between devices, crossed(): return lax.ppermute(block, 'inner', pairs)  7.34 us
    pallas_call x4, Pallas kernels, blocks_call(): pl.pallas_call(functools.partial(body, plan, rows, heads, scale), out_sha...  5.96 us
    ppermute x14, waiting for transfers between devices, swapped(): return lax.ppermute(block, axis, pairs)  4.65 us
    ppermute x3, waiting for transfers between devices, crossed(): return lax.ppermute(block, 'inner', pairs)  3.14 us
    pallas_call x1, Pallas kernels, on_device(): pl.pallas_call(pack_kernel, out_shape=(sds((2 * hr + 32, width), BF), sds...  1.34 us
    pallas_call x1, Pallas kernels, on_device(): pl.pallas_call(functools.partial(final_kernel, rows, heads, scale), out_s...  0.81 us
  transfers between devices with their start and end apart: 17, of which 5 were waited for; matrix products, arithmetic and copies ran while one was open for 0% of the time, Pallas kernels for 15%

profile of v8, /device:TPU:0, one launch (start us, length us, event | category | flops | bytes accessed | tf_op | source)
XLA Modules:
  0.0 36.2 jit_solution(18138100135559889602)
XLA Ops:
  0.6 1.3 %shard_map.94 = (bf16[1056,128]{1,0:T(8,128)(2,1)S(1)}, bf16[272,128]{1,0:T(8,128)(2,1)S(1)}) custom-call(bf16[128,512]{1,0:T(8,128)(2,1)} %q_ref.1, bf16[128,128]{1,0:T(8,128)(2,1)} %k_ref.1, bf16[128,128]{1,0:T(8,128)(2,1)} %v_ref.1, bf16[128,512]{1,0:T(8,128)(2,1)} %o_ref.1, bf16[128,512]{1,0:T(8,128)(2,1)} %g_ref.1, f32[4,128]{1,0:T(4,128)} %lse_ref.1, ...), custom_call_target="tpu_custom_call" | custom-call | flops 1000 | bytes 1000 | tf_op jit(solution)/shard_map/pallas_call | solution.py:250
  2.0 0.5 %collective-permute-start.3 = (bf16[272,128]{1,0:T(8,128)(2,1)S(1)}, bf16[272,128]{1,0:T(8,128)(2,1)S(1)}, u32[]{:S(2)}, u32[]{:S(2)}) collective-permute-start(bf16[272,128]{1,0:T(8,128)(2,1)S(1)} %get-tuple-element.29.refs_3_.refs_2_), channel_id=1, source_target_pairs={{0,1},{1,0},{2,3},{3,2},{4,5},{5,4},{6,7},{7,6},{8,9},{9,8},{10,11... | collective-permute-start | bytes 208904 | tf_op jit(solution)/shard_map/ppermute | solution.py:25
  2.5 2.6 %collective-permute-start.1 = (bf16[1056,128]{1,0:T(8,128)(2,1)S(1)}, bf16[1056,128]{1,0:T(8,128)(2,1)S(1)}, u32[]{:S(2)}, u32[]{:S(2)}) collective-permute-start(bf16[1056,128]{1,0:T(8,128)(2,1)S(1)} %get-tuple-element.26.refs_0_), channel_id=1, source_target_pairs={{0,16},{8,24},{16,0},{24,8},{1,17},{9,25},{17,1},{25,9},{2,18},{10... | collective-permute-start | bytes 811016 | tf_op jit(solution)/shard_map/ppermute | solution.py:25
  5.1 1.5 %collective-permute-start = (bf16[1056,128]{1,0:T(8,128)(2,1)S(1)}, bf16[1056,128]{1,0:T(8,128)(2,1)S(1)}, u32[]{:S(2)}, u32[]{:S(2)}) collective-permute-start(bf16[1056,128]{1,0:T(8,128)(2,1)S(1)} %get-tuple-element.26.refs_0_), channel_id=1, source_target_pairs={{0,8},{8,0},{16,24},{24,16},{1,9},{9,1},{17,25},{25,17},{2,10},{10... | collective-permute-start | bytes 811016 | tf_op jit(solution)/shard_map/ppermute | solution.py:25
  6.6 0.0 collective-permute-done.3.refs_4_.refs_3_
  6.6 3.7 %collective-permute-start.4 = (bf16[544,128]{1,0:T(8,128)(2,1)S(1)}, bf16[544,128]{1,0:T(8,128)(2,1)S(1)}, u32[]{:S(2)}, u32[]{:S(2)}) collective-permute-start(bf16[544,128]{1,0:T(8,128)(2,1)S(1)} %pad_maximum_fusion), channel_id=1, source_target_pairs={{0,6},{1,5},{2,4},{3,7},{4,2},{5,1},{6,0},{7,3},{8,14},{9,13},{10,... | collective-permute-start | bytes 417800 | tf_op jit(solution)/shard_map/ppermute | solution.py:238
  10.3 1.9 %collective-permute-done.1.refs_2_ = bf16[1056,128]{1,0:T(8,128)(2,1)S(1)} collective-permute-done((bf16[1056,128]{1,0:T(8,128)(2,1)S(1)}, bf16[1056,128]{1,0:T(8,128)(2,1)S(1)}, u32[]{:S(2)}, u32[]{:S(2)}) %collective-permute-start.1) | collective-permute-done | bytes 270368 | tf_op jit(solution)/shard_map/ppermute | solution.py:25
  12.2 1.5 %collective-permute-done.refs_1_ = bf16[1056,128]{1,0:T(8,128)(2,1)S(1)} collective-permute-done((bf16[1056,128]{1,0:T(8,128)(2,1)S(1)}, bf16[1056,128]{1,0:T(8,128)(2,1)S(1)}, u32[]{:S(2)}, u32[]{:S(2)}) %collective-permute-start) | collective-permute-done | bytes 270368 | tf_op jit(solution)/shard_map/ppermute | solution.py:25
  13.7 1.6 %collective-permute-start.8 = (bf16[512,128]{1,0:T(8,128)(2,1)S(1)}, bf16[512,128]{1,0:T(8,128)(2,1)S(1)}, u32[]{:S(2)}, u32[]{:S(2)}) collective-permute-start(bf16[512,128]{1,0:T(8,128)(2,1)S(1)} %slice.12), channel_id=1, source_target_pairs={{0,8},{8,0},{16,24},{24,16},{1,9},{9,1},{17,25},{25,17},{2,10},{10... | collective-permute-start | bytes 393224 | tf_op jit(solution)/shard_map/ppermute | solution.py:25
  15.2 0.5 %collective-permute-start.9 = (bf16[544,128]{1,0:T(8,128)(2,1)S(1)}, bf16[544,128]{1,0:T(8,128)(2,1)S(1)}, u32[]{:S(2)}, u32[]{:S(2)}) collective-permute-start(bf16[544,128]{1,0:T(8,128)(2,1)S(1)} %slice.13), channel_id=1, source_target_pairs={{0,16},{8,24},{16,0},{24,8},{1,17},{9,25},{17,1},{25,9},{2,18},{10... | collective-permute-start | bytes 417800 | tf_op jit(solution)/shard_map/ppermute | solution.py:25
  15.7 0.0 collective-permute-done.2.refs_3_.refs_5_
  15.7 0.0 collective-permute-done.4.refs_5_.refs_4_
  15.7 0.0 collective-permute-start.5
  15.8 0.6 %collective-permute-start.7 = (bf16[272,128]{1,0:T(8,128)(2,1)S(1)}, bf16[272,128]{1,0:T(8,128)(2,1)S(1)}, u32[]{:S(2)}, u32[]{:S(2)}) collective-permute-start(bf16[272,128]{1,0:T(8,128)(2,1)S(1)} %get-tuple-element.49), channel_id=1, source_target_pairs={{0,1},{1,0},{2,3},{3,2},{4,5},{5,4},{6,7},{7,6},{8,9},{9,8},{10,11... | collective-permute-start | bytes 208904 | tf_op jit(solution)/shard_map/ppermute | solution.py:25
  16.3 0.1 collective-permute-start.6
  16.4 2.2 %shard_map.95 = (f32[3,128,512]{2,1,0:T(8,128)S(1)}, f32[4,256,128]{2,1,0:T(8,128)S(1)}) custom-call(bf16[1056,128]{1,0:T(8,128)(2,1)S(1)} %get-tuple-element.26.refs_0_, bf16[1056,128]{1,0:T(8,128)(2,1)S(1)} %collective-permute-done.refs_1_, bf16[1056,128]{1,0:T(8,128)(2,1)S(1)} %collective-permute-done.1.refs_2_, ...), custom_call_target="tpu_custom_call" | custom-call | flops 1000 | bytes 1000 | tf_op jit(solution)/shard_map/pallas_call | solution.py:198
  18.6 0.0 collective-permute-done.5.refs_4_.refs_6_
  18.7 2.2 %shard_map.96 = (f32[128,512]{1,0:T(8,128)S(1)}, bf16[128,512]{1,0:T(8,128)(2,1)S(1)}, bf16[128,512]{1,0:T(8,128)(2,1)S(1)}, f32[4,256,128]{2,1,0:T(8,128)S(1)}) custom-call(bf16[1056,128]{1,0:T(8,128)(2,1)S(1)} %get-tuple-element.26.refs_0_, bf16[1056,128]{1,0:T(8,128)(2,1)S(1)} %collective-permute-done.refs_1_, ...), custom_call_target="tpu_custom_call" | custom-call | flops 1000 | bytes 1000 | tf_op jit(solution)/shard_map/pallas_call | solution.py:198
  20.8 0.0 collective-permute-done.8.refs_0_
  20.9 0.8 %shard_map.97 = (f32[1,128,512]{2,1,0:T(8,128)S(1)}, bf16[4,256,128]{2,1,0:T(8,128)(2,1)S(1)}) custom-call(bf16[512,128]{1,0:T(8,128)(2,1)S(1)} %collective-permute-done.8.refs_0_, bf16[544,128]{1,0:T(8,128)(2,1)S(1)} %collective-permute-done.9.refs_1_, bf16[272,128]{1,0:T(8,128)(2,1)S(1)} %get-tuple-element.29.refs_3_.refs_2_, ...), custom_call_target="tpu_custom_call" | custom-call | flops 1000 | bytes 1000 | tf_op jit(solution)/shard_map/pallas_call | solution.py:198
  21.7 0.5 %collective-permute-start.10 = (bf16[4,256,128]{2,1,0:T(8,128)(2,1)S(1)}, bf16[4,256,128]{2,1,0:T(8,128)(2,1)S(1)}, u32[]{:S(2)}, u32[]{:S(2)}) collective-permute-start(bf16[4,256,128]{2,1,0:T(8,128)(2,1)S(1)} %get-tuple-element.38), channel_id=1, source_target_pairs={{0,1},{1,0},{2,3},{3,2},{4,5},{5,4},{6,7},{7,6},{8,9},{9,8},{10,11... | collective-permute-start | bytes 786440 | tf_op jit(solution)/shard_map/ppermute | solution.py:25
  22.2 0.3 collective-permute-start.14
  22.5 1.7 %collective-permute-start.15 = (bf16[128,512]{1,0:T(8,128)(2,1)S(1)}, bf16[128,512]{1,0:T(8,128)(2,1)S(1)}, u32[]{:S(2)}, u32[]{:S(2)}) collective-permute-start(bf16[128,512]{1,0:T(8,128)(2,1)S(1)} %get-tuple-element.45), channel_id=1, source_target_pairs={{0,16},{8,24},{16,0},{24,8},{1,17},{9,25},{17,1},{25,9},{2,18},{10... | collective-permute-start | bytes 393224 | tf_op jit(solution)/shard_map/ppermute | solution.py:25
  24.2 0.8 %shard_map.98 = (bf16[128,512]{1,0:T(8,128)(2,1)S(1)}, f32[4,256,128]{2,1,0:T(8,128)S(1)}) custom-call(bf16[512,128]{1,0:T(8,128)(2,1)S(1)} %collective-permute-done.8.refs_0_, bf16[544,128]{1,0:T(8,128)(2,1)S(1)} %collective-permute-done.9.refs_1_, bf16[272,128]{1,0:T(8,128)(2,1)S(1)} %get-tuple-element.29.refs_3_.refs_2_, ...), custom_call_target="tpu_custom_call" | custom-call | flops 1000 | bytes 1000 | tf_op jit(solution)/shard_map/pallas_call | solution.py:198
  25.0 0.1 shard_map.99
  25.1 3.7 %collective-permute-start.11 = (bf16[256,128]{1,0:T(8,128)(2,1)S(1)}, bf16[256,128]{1,0:T(8,128)(2,1)S(1)}, u32[]{:S(2)}, u32[]{:S(2)}) collective-permute-start(bf16[256,128]{1,0:T(8,128)(2,1)S(1)} %get-tuple-element.40), channel_id=1, source_target_pairs={{0,6},{1,5},{2,4},{3,7},{4,2},{5,1},{6,0},{7,3},{8,14},{9,13},{10,... | collective-permute-start | bytes 196616 | tf_op jit(solution)/shard_map/ppermute | solution.py:238
  28.7 0.8 %collective-permute-start.13 = (bf16[256,128]{1,0:T(8,128)(2,1)S(1)}, bf16[256,128]{1,0:T(8,128)(2,1)S(1)}, u32[]{:S(2)}, u32[]{:S(2)}) collective-permute-start(bf16[256,128]{1,0:T(8,128)(2,1)S(1)} %get-tuple-element.42), channel_id=1, source_target_pairs={{0,2},{1,3},{2,0},{3,1},{4,6},{5,7},{6,4},{7,5},{8,10},{9,11},{10,... | collective-permute-start | bytes 196616 | tf_op jit(solution)/shard_map/ppermute | solution.py:25
  29.5 1.4 %collective-permute-start.16 = (bf16[128,512]{1,0:T(8,128)(2,1)S(1)}, bf16[128,512]{1,0:T(8,128)(2,1)S(1)}, u32[]{:S(2)}, u32[]{:S(2)}) collective-permute-start(bf16[128,512]{1,0:T(8,128)(2,1)S(1)} %get-tuple-element.48), channel_id=1, source_target_pairs={{0,24},{8,16},{16,8},{24,0},{1,25},{9,17},{17,9},{25,1},{2,26},{10... | collective-permute-start | bytes 393224 | tf_op jit(solution)/shard_map/ppermute | solution.py:25
  31.0 0.4 %collective-permute-done.11.refs_0_ = bf16[256,128]{1,0:T(8,128)(2,1)S(1)} collective-permute-done((bf16[256,128]{1,0:T(8,128)(2,1)S(1)}, bf16[256,128]{1,0:T(8,128)(2,1)S(1)}, u32[]{:S(2)}, u32[]{:S(2)}) %collective-permute-start.11) | collective-permute-done | bytes 65568 | tf_op jit(solution)/shard_map/ppermute | solution.py:238
  31.4 2.7 %collective-permute-done.12.refs_1_ = bf16[256,128]{1,0:T(8,128)(2,1)S(1)} collective-permute-done((bf16[256,128]{1,0:T(8,128)(2,1)S(1)}, bf16[256,128]{1,0:T(8,128)(2,1)S(1)}, u32[]{:S(2)}, u32[]{:S(2)}) %collective-permute-start.12) | collective-permute-done | bytes 65568 | tf_op jit(solution)/shard_map/ppermute | solution.py:238
  34.1 1.3 %collective-permute-done.16.refs_2_ = bf16[128,512]{1,0:T(8,128)(2,1)S(1)} collective-permute-done((bf16[128,512]{1,0:T(8,128)(2,1)S(1)}, bf16[128,512]{1,0:T(8,128)(2,1)S(1)}, u32[]{:S(2)}, u32[]{:S(2)}) %collective-permute-start.16) | collective-permute-done | bytes 131104 | tf_op jit(solution)/shard_map/ppermute | solution.py:25
  35.4 0.8 %shard_map.101 = (bf16[128,512]{1,0:T(8,128)(2,1)}, bf16[128,128]{1,0:T(8,128)(2,1)}, bf16[128,128]{1,0:T(8,128)(2,1)}) custom-call(f32[128,512]{1,0:T(8,128)S(1)} %get-tuple-element.33.dq_own, f32[256,128]{1,0:T(8,128)S(1)} %shard_map.100.dkv_ref, bf16[128,512]{1,0:T(8,128)(2,1)S(1)} %collective-permute-done.14.refs_0_, ...), custom_call_target="tpu_custom_call" | custom-call | flops 1000 | bytes 1000 | tf_op jit(solution)/shard_map/pallas_call | solution.py:332
  (14 shorter events, 0.1 us)
Async XLA Ops:
  2.0 4.6 %collective-permute-start.3 = (bf16[272,128]{1,0:T(8,128)(2,1)S(1)}, bf16[272,128]{1,0:T(8,128)(2,1)S(1)}, u32[]{:S(2)}, u32[]{:S(2)}) collective-permute-start(bf16[272,128]{1,0:T(8,128)(2,1)S(1)} %get-tuple-element.29.refs_3_.refs_2_), channel_id=1, source_target_pairs={{0,1},{1,0},{2,3},{3,2},{4,5},{5,4},{6,7},{7,6},{8,9},{9,8},{10,11... | collective-permute-start | bytes 208904 | tf_op jit(solution)/shard_map/ppermute | solution.py:25
  2.5 9.7 %collective-permute-start.1 = (bf16[1056,128]{1,0:T(8,128)(2,1)S(1)}, bf16[1056,128]{1,0:T(8,128)(2,1)S(1)}, u32[]{:S(2)}, u32[]{:S(2)}) collective-permute-start(bf16[1056,128]{1,0:T(8,128)(2,1)S(1)} %get-tuple-element.26.refs_0_), channel_id=1, source_target_pairs={{0,16},{8,24},{16,0},{24,8},{1,17},{9,25},{17,1},{25,9},{2,18},{10... | collective-permute-start | bytes 811016 | tf_op jit(solution)/shard_map/ppermute | solution.py:25
  5.1 8.6 %collective-permute-start = (bf16[1056,128]{1,0:T(8,128)(2,1)S(1)}, bf16[1056,128]{1,0:T(8,128)(2,1)S(1)}, u32[]{:S(2)}, u32[]{:S(2)}) collective-permute-start(bf16[1056,128]{1,0:T(8,128)(2,1)S(1)} %get-tuple-element.26.refs_0_), channel_id=1, source_target_pairs={{0,8},{8,0},{16,24},{24,16},{1,9},{9,1},{17,25},{25,17},{2,10},{10... | collective-permute-start | bytes 811016 | tf_op jit(solution)/shard_map/ppermute | solution.py:25
  6.6 9.1 %collective-permute-start.4 = (bf16[544,128]{1,0:T(8,128)(2,1)S(1)}, bf16[544,128]{1,0:T(8,128)(2,1)S(1)}, u32[]{:S(2)}, u32[]{:S(2)}) collective-permute-start(bf16[544,128]{1,0:T(8,128)(2,1)S(1)} %pad_maximum_fusion), channel_id=1, source_target_pairs={{0,6},{1,5},{2,4},{3,7},{4,2},{5,1},{6,0},{7,3},{8,14},{9,13},{10,... | collective-permute-start | bytes 417800 | tf_op jit(solution)/shard_map/ppermute | solution.py:238
  10.3 5.5 %collective-permute-start.2 = (bf16[272,128]{1,0:T(8,128)(2,1)S(1)}, bf16[272,128]{1,0:T(8,128)(2,1)S(1)}, u32[]{:S(2)}, u32[]{:S(2)}) collective-permute-start(bf16[272,128]{1,0:T(8,128)(2,1)S(1)} %get-tuple-element.29.refs_3_.refs_2_), channel_id=1, source_target_pairs={{0,2},{1,3},{2,0},{3,1},{4,6},{5,7},{6,4},{7,5},{8,10},{9,11},{10,... | collective-permute-start | bytes 208904 | tf_op jit(solution)/shard_map/ppermute | solution.py:25
  13.7 7.2 %collective-permute-start.8 = (bf16[512,128]{1,0:T(8,128)(2,1)S(1)}, bf16[512,128]{1,0:T(8,128)(2,1)S(1)}, u32[]{:S(2)}, u32[]{:S(2)}) collective-permute-start(bf16[512,128]{1,0:T(8,128)(2,1)S(1)} %slice.12), channel_id=1, source_target_pairs={{0,8},{8,0},{16,24},{24,16},{1,9},{9,1},{17,25},{25,17},{2,10},{10... | collective-permute-start | bytes 393224 | tf_op jit(solution)/shard_map/ppermute | solution.py:25
  15.2 5.6 %collective-permute-start.9 = (bf16[544,128]{1,0:T(8,128)(2,1)S(1)}, bf16[544,128]{1,0:T(8,128)(2,1)S(1)}, u32[]{:S(2)}, u32[]{:S(2)}) collective-permute-start(bf16[544,128]{1,0:T(8,128)(2,1)S(1)} %slice.13), channel_id=1, source_target_pairs={{0,16},{8,24},{16,0},{24,8},{1,17},{9,25},{17,1},{25,9},{2,18},{10... | collective-permute-start | bytes 417800 | tf_op jit(solution)/shard_map/ppermute | solution.py:25
  15.7 2.9 %collective-permute-start.5 = (bf16[272,128]{1,0:T(8,128)(2,1)S(1)}, bf16[272,128]{1,0:T(8,128)(2,1)S(1)}, u32[]{:S(2)}, u32[]{:S(2)}) collective-permute-start(bf16[272,128]{1,0:T(8,128)(2,1)S(1)} %collective-permute-done.2.refs_3_.refs_5_), channel_id=1, source_target_pairs={{0,1},{1,0},{2,3},{3,2},{4,5},{5,4},{6,7},{7,6},{8,9},{9,8},{10,11... | collective-permute-start | bytes 208904 | tf_op jit(solution)/shard_map/ppermute | solution.py:25
  15.8 2.9 %collective-permute-start.7 = (bf16[272,128]{1,0:T(8,128)(2,1)S(1)}, bf16[272,128]{1,0:T(8,128)(2,1)S(1)}, u32[]{:S(2)}, u32[]{:S(2)}) collective-permute-start(bf16[272,128]{1,0:T(8,128)(2,1)S(1)} %get-tuple-element.49), channel_id=1, source_target_pairs={{0,1},{1,0},{2,3},{3,2},{4,5},{5,4},{6,7},{7,6},{8,9},{9,8},{10,11... | collective-permute-start | bytes 208904 | tf_op jit(solution)/shard_map/ppermute | solution.py:25
  16.3 2.3 %collective-permute-start.6 = (bf16[272,128]{1,0:T(8,128)(2,1)S(1)}, bf16[272,128]{1,0:T(8,128)(2,1)S(1)}, u32[]{:S(2)}, u32[]{:S(2)}) collective-permute-start(bf16[272,128]{1,0:T(8,128)(2,1)S(1)} %get-tuple-element.50), channel_id=1, source_target_pairs={{0,1},{1,0},{2,3},{3,2},{4,5},{5,4},{6,7},{7,6},{8,9},{9,8},{10,11... | collective-permute-start | bytes 208904 | tf_op jit(solution)/shard_map/ppermute | solution.py:25
  21.7 3.3 %collective-permute-start.10 = (bf16[4,256,128]{2,1,0:T(8,128)(2,1)S(1)}, bf16[4,256,128]{2,1,0:T(8,128)(2,1)S(1)}, u32[]{:S(2)}, u32[]{:S(2)}) collective-permute-start(bf16[4,256,128]{2,1,0:T(8,128)(2,1)S(1)} %get-tuple-element.38), channel_id=1, source_target_pairs={{0,1},{1,0},{2,3},{3,2},{4,5},{5,4},{6,7},{7,6},{8,9},{9,8},{10,11... | collective-permute-start | bytes 786440 | tf_op jit(solution)/shard_map/ppermute | solution.py:25
  22.2 7.4 %collective-permute-start.14 = (bf16[128,512]{1,0:T(8,128)(2,1)S(1)}, bf16[128,512]{1,0:T(8,128)(2,1)S(1)}, u32[]{:S(2)}, u32[]{:S(2)}) collective-permute-start(bf16[128,512]{1,0:T(8,128)(2,1)S(1)} %get-tuple-element.44), channel_id=1, source_target_pairs={{0,8},{8,0},{16,24},{24,16},{1,9},{9,1},{17,25},{25,17},{2,10},{10... | collective-permute-start | bytes 393224 | tf_op jit(solution)/shard_map/ppermute | solution.py:25
  22.5 7.1 %collective-permute-start.15 = (bf16[128,512]{1,0:T(8,128)(2,1)S(1)}, bf16[128,512]{1,0:T(8,128)(2,1)S(1)}, u32[]{:S(2)}, u32[]{:S(2)}) collective-permute-start(bf16[128,512]{1,0:T(8,128)(2,1)S(1)} %get-tuple-element.45), channel_id=1, source_target_pairs={{0,16},{8,24},{16,0},{24,8},{1,17},{9,25},{17,1},{25,9},{2,18},{10... | collective-permute-start | bytes 393224 | tf_op jit(solution)/shard_map/ppermute | solution.py:25
  25.1 6.3 %collective-permute-start.11 = (bf16[256,128]{1,0:T(8,128)(2,1)S(1)}, bf16[256,128]{1,0:T(8,128)(2,1)S(1)}, u32[]{:S(2)}, u32[]{:S(2)}) collective-permute-start(bf16[256,128]{1,0:T(8,128)(2,1)S(1)} %get-tuple-element.40), channel_id=1, source_target_pairs={{0,6},{1,5},{2,4},{3,7},{4,2},{5,1},{6,0},{7,3},{8,14},{9,13},{10,... | collective-permute-start | bytes 196616 | tf_op jit(solution)/shard_map/ppermute | solution.py:238
  28.7 5.4 %collective-permute-start.12 = (bf16[256,128]{1,0:T(8,128)(2,1)S(1)}, bf16[256,128]{1,0:T(8,128)(2,1)S(1)}, u32[]{:S(2)}, u32[]{:S(2)}) collective-permute-start(bf16[256,128]{1,0:T(8,128)(2,1)S(1)} %get-tuple-element.41), channel_id=1, source_target_pairs={{0,4},{1,7},{2,6},{3,5},{4,0},{5,3},{6,2},{7,1},{8,12},{9,15},{10,... | collective-permute-start | bytes 196616 | tf_op jit(solution)/shard_map/ppermute | solution.py:238
  28.7 5.4 %collective-permute-start.13 = (bf16[256,128]{1,0:T(8,128)(2,1)S(1)}, bf16[256,128]{1,0:T(8,128)(2,1)S(1)}, u32[]{:S(2)}, u32[]{:S(2)}) collective-permute-start(bf16[256,128]{1,0:T(8,128)(2,1)S(1)} %get-tuple-element.42), channel_id=1, source_target_pairs={{0,2},{1,3},{2,0},{3,1},{4,6},{5,7},{6,4},{7,5},{8,10},{9,11},{10,... | collective-permute-start | bytes 196616 | tf_op jit(solution)/shard_map/ppermute | solution.py:25
  29.5 5.9 %collective-permute-start.16 = (bf16[128,512]{1,0:T(8,128)(2,1)S(1)}, bf16[128,512]{1,0:T(8,128)(2,1)S(1)}, u32[]{:S(2)}, u32[]{:S(2)}) collective-permute-start(bf16[128,512]{1,0:T(8,128)(2,1)S(1)} %get-tuple-element.48), channel_id=1, source_target_pairs={{0,24},{8,16},{16,8},{24,0},{1,25},{9,17},{17,9},{25,1},{2,26},{10... | collective-permute-start | bytes 393224 | tf_op jit(solution)/shard_map/ppermute | solution.py:25

commit v9 on v8

--- a/solution.py
+++ b/solution.py
@@ -82,18 +82,14 @@
 
 
 def blocks_kernel(plan, rows, heads, scale, *refs):
-    if plan["halves"]:
-        x_refs, refs = [refs[:2]], refs[2:]
-    else:
-        x_refs = [(x_ref, x_ref.at[heads * rows :, :]) for x_ref in refs[: plan["queries"]]]
-        refs = refs[plan["queries"] :]
-    kv_refs = refs[: plan["kv"]]
-    refs = refs[plan["kv"] :]
-    acc_refs = refs[: plan["acc"]]
-    refs = refs[plan["acc"] :]
-    dq_in = None
-    if plan["dq_in"]:
-        dq_in, refs = refs[0], refs[1:]
+    refs = list(refs)
+    x_refs = []
+    for parts in plan["parts"]:
+        whole = refs.pop(0)
+        x_refs.append((whole, whole.at[heads * rows :, :] if parts == 1 else refs.pop(0)))
+    kv_refs = [refs.pop(0) for _ in range(plan["kv"])]
+    acc_refs = [refs.pop(0) for _ in range(plan["acc"])]
+    dq_in = [refs.pop(0) for _ in range(plan["dq_in"])]
     dq_refs, dkv_ref = refs[:-1], refs[-1]
     width = x_refs[0][0].shape[1]
     hr = heads * rows
@@ -107,12 +103,13 @@
         delta = e[3 * heads : 4 * heads] + e[4 * heads : 5 * heads] + e[5 * heads : 6 * heads]
         rowed.append((lse, delta, e[6 * heads : 6 * heads + 1]))
     dqt = [[None] * (hr // COLS) for _ in x_refs]
-    for c in range(0, len(slots), 2):
+    group = 3 if len(slots) == 3 else 2
+    for c in range(0, len(slots), group):
         ks, vs, runs = [], [], []
-        for n, start in (s[:2] for s in slots[c : c + 2]):
-            ks.append(kv_refs[n][start : start + rows, :])
-            vs.append(kv_refs[n][start + rows : start + 2 * rows, :])
-            e = kv_refs[n][start + 2 * rows : start + 2 * rows + 16, :].astype(F32)
+        for n in slots[c : c + group]:
+            ks.append(kv_refs[n][:rows, :])
+            vs.append(kv_refs[n][rows : 2 * rows, :])
+            e = kv_refs[n][2 * rows :, :].astype(F32)
             runs += [e[r : r + 1] for r in range(per)]
         k = jnp.concatenate(ks, axis=0)
         v = jnp.concatenate(vs, axis=0)
@@ -126,7 +123,7 @@
                 st = dot(k, q, NT)
                 dpt = dot(v, g, NT)
                 p_rows, d_rows = [], []
-                for r in range(2 * per):
+                for r in range(len(runs)):
                     sl = slice(r * RUN, (r + 1) * RUN)
                     p_heads, d_heads = [], []
                     for h in range(step):
@@ -150,10 +147,10 @@
                 dk = dk_n if dk is None else dk + dk_n
                 old = dqt[b][n]
                 dqt[b][n] = dq_n if old is None else old + dq_n
-        for j, slot in enumerate(slots[c : c + 2]):
+        for j, n in enumerate(slots[c : c + group]):
             dk_j, dv_j = dk[j * rows : (j + 1) * rows], dv[j * rows : (j + 1) * rows]
             if plan["acc"]:
-                acc_ref, at = acc_refs[slot[2]], slot[3]
+                acc_ref, at = acc_refs[plan["at"][n][0]], plan["at"][n][1]
                 dk_j += acc_ref[at, :rows, :]
                 dv_j += acc_ref[at, rows:, :]
             dkv_ref[c + j, :rows, :] = dk_j.astype(dkv_ref.dtype)
@@ -161,42 +158,35 @@
     for b, dq_ref in enumerate(dq_refs):
         for n in range(hr // COLS):
             cols = slice(n * COLS, (n + 1) * COLS)
-            total = dqt[b][n] if dq_in is None else dqt[b][n] + dq_in[b, :, cols]
+            total = dqt[b][n] + dq_in[b][:, cols] if dq_in else dqt[b][n]
             dq_ref[:, cols] = total.astype(dq_ref.dtype)
 
 
-def first_kernel(plan, rows, heads, scale, *refs):
-    dq_ref = refs[-2]
-    dq_refs = [dq_ref.at[b] for b in range(plan["queries"])]
-    blocks_kernel(plan, rows, heads, scale, *refs[:-2], *dq_refs, refs[-1])
-
-
-def blocks_call(
-    xs, kvs, slots, rows, heads, scale, dkv_type, dq_types, acc=(), dq_in=None, diagonal=False, halves=False
-):
+def blocks_call(xs, kvs, slots, rows, heads, scale, dkv_type, dq_type, acc=(), dq_in=(), diagonal=False):
     sds = jax.ShapeDtypeStruct
-    width = xs[0].shape[1]
-    hr = heads * rows
-    queries = 1 if halves else len(xs)
+    width = kvs[0].shape[1]
+    xs = [x if isinstance(x, list) else [x] for x in xs]
+    slots = list(slots)
+    totals = []
+    for a, _ in acc:
+        if all(a is not t for t in totals):
+            totals.append(a)
+    at = [([a is t for t in totals].index(True), n) for a, n in acc]
     plan = {
-        "halves": halves,
-        "queries": queries,
+        "parts": [len(x) for x in xs],
         "kv": len(kvs),
-        "acc": len(acc),
-        "dq_in": dq_in is not None,
+        "acc": len(totals),
+        "at": at,
+        "dq_in": len(dq_in),
         "slots": slots,
         "diagonal": diagonal,
     }
-    args = (*xs, *kvs, *acc) + (() if dq_in is None else (dq_in,))
-    if dq_types is None:
-        body = first_kernel
-        outs = (sds((queries, width, hr), F32),)
-    else:
-        body = blocks_kernel
-        outs = tuple(sds((width, hr), t) for t in dq_types)
+    args = (*sum(xs, []), *kvs, *totals, *dq_in)
+    types = dq_type if isinstance(dq_type, list) else [dq_type] * len(xs)
+    outs = tuple(sds((width, heads * rows), t) for t in types)
     outs += (sds((len(slots), 2 * rows, width), dkv_type),)
     return pl.pallas_call(
-        functools.partial(body, plan, rows, heads, scale),
+        functools.partial(blocks_kernel, plan, rows, heads, scale),
         out_shape=outs,
         in_specs=[VMEM] * len(args),
         out_specs=(VMEM,) * len(outs),
@@ -262,46 +252,36 @@
         cost_estimate=QUICK,
     )(*[pltpu.with_memory_space_constraint(a, pltpu.HBM) for a in inputs])
 
+    common = (rows, heads, scale)
     sib = swapped(kv, "inner", 1)
     near = swapped(kv, "inner", 2)
-    pair = jnp.concatenate([kv, sib], axis=0)
-    direct = [crossed(pair, t, False) for t in range(1, nz // 2)]
+    direct = [crossed(block, t, False) for t in range(1, nz // 2) for block in (kv, sib)]
+    early = [kv, sib, near]
+    dq_own, acc = blocks_call([x], early, range(3), *common, F32, F32, diagonal=True)
+
     xs = [swapped(x, "outer", s) for s in range(1, nq - 1)]
-    xs = [x, *lax.optimization_barrier(tuple(xs))]
-    halves = [xs[nq - 2][:hr], xs[(nq - 1) ^ (nq // 2)][hr:]]
+    dq_own, acc, *xs = lax.optimization_barrier((dq_own, acc, *xs))
+    halves = [xs[nq - 3][:hr], xs[((nq - 1) ^ (nq // 2)) - 1][hr:]]
     corner = [swapped(halves[0], "outer", 1), swapped(halves[1], "outer", nq // 2)]
-    near, *direct = lax.optimization_barrier((near, *direct, *halves))[: nz // 2]
-    size = kv.shape[0]
-    near_sib = swapped(near, "inner", 1)
-    traded = [[swapped(p[n : n + size], "inner", 1) for n in (0, size)] for p in direct]
-
-    group_a = [(0, 0), (1, 0)]
-    group_b = [(0, 0), (1, 0)]
-    for t in range(1, nz // 2):
-        group_a += [(t + 1, 0), (t + 1, size)]
-        group_b += [(2 * t, 0), (2 * t + 1, 0)]
-    far = [near, near_sib, *sum(traded, [])]
-    common = (rows, heads, scale)
-    dqs, acc_a = blocks_call(xs, [kv, sib, *direct], group_a, *common, F32, None, diagonal=True)
-    *dqs, acc_b = blocks_call(
-        xs, far, group_b, *common, F32, [F32] + [BF] * (nq - 2), dq_in=dqs
-    )
-    arrays = [kv, sib, *direct, *far]
-    base = 1 + nz // 2
-    in_a = [(n, start, 0, i) for i, (n, start) in enumerate(group_a)]
-    in_b = [(base + n, start, 1, i) for i, (n, start) in enumerate(group_b)]
-    acc = (acc_a, acc_b)
-    theirs, ours = [in_a[1], in_b[1]], [in_a[0], in_b[0]]
-    for t in range(1, nz // 2):
-        theirs += [in_b[2 * t], in_a[2 * t + 1]]
-        ours += [in_a[2 * t], in_b[2 * t + 1]]
-    dq_last, dkv_sib = blocks_call(
-        corner, arrays, theirs, *common, BF, None, acc=acc, halves=True
-    )
+    *dqs, acc = blocks_call(xs, early, range(3), *common, F32, F32, acc=[(acc, n) for n in range(3)])
+
+    *direct, acc = lax.optimization_barrier((*direct, acc))
+    traded = [swapped(block, "inner", 1) for block in (near, *direct)]
+    xs = [x, *xs]
+    n_d, n_t = len(direct), len(traded)
+    *dqs, acc_d = blocks_call(xs, direct, range(n_d), *common, F32, F32, dq_in=(dq_own, *dqs))
+    types = [F32] + [BF] * (nq - 2)
+    dq_own, *dqs, acc_t = blocks_call(xs, traded, range(n_t), *common, F32, types, dq_in=dqs)
+
+    arrays = [*early, *direct, *traded]
+    accs = [(a, n) for a, count in ((acc, 3), (acc_d, n_d), (acc_t, n_t)) for n in range(count)]
+    theirs, ours = [1, 3 + n_d], [0, 2]
+    for t in range(0, n_d, 2):
+        theirs += [4 + n_d + t, 3 + t + 1]
+        ours += [3 + t, 4 + n_d + t + 1]
+    dq_last, dkv_sib = blocks_call([corner], arrays, theirs, *common, BF, F32, acc=accs)
     dkv_got = swapped(dkv_sib, "inner", 1)
-    dq_last, dkv_own = blocks_call(
-        corner, arrays, ours, *common, F32, [BF], acc=acc, dq_in=dq_last, halves=True
-    )
+    dq_last, dkv_own = blocks_call([corner], arrays, ours, *common, F32, BF, acc=accs, dq_in=[dq_last])
     dkv_own, *send = pl.pallas_call(
         add_kernel,
         out_shape=(sds((2 * rows, width), F32),) + (sds((2 * rows, width), BF),) * (nz - 1),
@@ -310,7 +290,6 @@
         compiler_params=SMALL,
         cost_estimate=QUICK,
     )(dkv_own, dkv_got)
-    dq_own, *dqs = dqs
     got = [swapped(dq, "outer", s + 1) for s, dq in enumerate(dqs)]
     dq_last, *got = lax.optimization_barrier((dq_last, *got))
     got.append(swapped(dq_last, "outer", nq - 1))

time: 36.4 us -> 35.3 us (0.970)
  waiting for transfers between devices: 7.79 us -> 4.61 us
  starting transfers between devices: 19.4 us -> 21.3 us
    ppermute x14, waiting for transfers between devices: 4.65 us -> 1.73 us  [swapped(): return lax.ppermute(block, axis, pairs)]
    ppermute x14, starting transfers between devices: 12.1 us -> 13.8 us  [swapped(): return lax.ppermute(block, axis, pairs)]
    pallas_call x4 -> x6, Pallas kernels: 5.96 us -> 6.23 us  [blocks_call(): pl.pallas_call(functools.partial(blocks_kernel, plan, rows, heads, scale)...]
    ppermute x3 -> x4, waiting for transfers between devices: 3.14 us -> 2.88 us  [crossed(): return lax.ppermute(block, 'inner', pairs)]
    ppermute x3 -> x4, starting transfers between devices: 7.34 us -> 7.5 us  [crossed(): return lax.ppermute(block, 'inner', pairs)]
  transfers between devices with their start and end apart: 17 -> 18, of which waited for: 5 -> 5; matrix products, arithmetic and copies ran while one was open for 0% -> 0% of each run, Pallas kernels for 15% -> 16%
where the time goes in v9:
time: 35.3 us; the launch traced here: 35.2 us
  starting transfers between devices  21.3 us (60%)
  Pallas kernels  8.46 us (24%)
  waiting for transfers between devices  4.61 us (13%)
  between operations  0.76 us (2%)
    ppermute x14, starting transfers between devices, swapped(): return lax.ppermute(block, axis, pairs)  13.8 us
    ppermute x4, starting transfers between devices, crossed(): return lax.ppermute(block, 'inner', pairs)  7.5 us
    pallas_call x6, Pallas kernels, blocks_call(): pl.pallas_call(functools.partial(blocks_kernel, plan, rows, heads, scale)...  6.23 us
    ppermute x4, waiting for transfers between devices, crossed(): return lax.ppermute(block, 'inner', pairs)  2.88 us
    ppermute x14, waiting for transfers between devices, swapped(): return lax.ppermute(block, axis, pairs)  1.73 us
    pallas_call x1, Pallas kernels, on_device(): pl.pallas_call(pack_kernel, out_shape=(sds((2 * hr + 32, width), BF), sds...  1.33 us
    pallas_call x1, Pallas kernels, on_device(): pl.pallas_call(functools.partial(final_kernel, rows, heads, scale), out_s...  0.81 us
  transfers between devices with their start and end apart: 18, of which 5 were waited for; matrix products, arithmetic and copies ran while one was open for 0% of the time, Pallas kernels for 16%

profile of v9, /device:TPU:0, one launch (start us, length us, event | category | flops | bytes accessed | tf_op | source)
XLA Modules:
  0.0 35.2 jit_solution(6799733900858250234)
XLA Ops:
  0.6 1.3 %shard_map.94 = (bf16[1056,128]{1,0:T(8,128)(2,1)S(1)}, bf16[272,128]{1,0:T(8,128)(2,1)S(1)}) custom-call(bf16[128,512]{1,0:T(8,128)(2,1)} %q_ref.1, bf16[128,128]{1,0:T(8,128)(2,1)} %k_ref.1, bf16[128,128]{1,0:T(8,128)(2,1)} %v_ref.1, bf16[128,512]{1,0:T(8,128)(2,1)} %o_ref.1, bf16[128,512]{1,0:T(8,128)(2,1)} %g_ref.1, f32[4,128]{1,0:T(4,128)} %lse_ref.1, ...), custom_call_target="tpu_custom_call" | custom-call | flops 1000 | bytes 1000 | tf_op jit(solution)/shard_map/pallas_call | solution.py:240
  2.0 3.0 %collective-permute-start.2 = (bf16[1056,128]{1,0:T(8,128)(2,1)S(1)}, bf16[1056,128]{1,0:T(8,128)(2,1)S(1)}, u32[]{:S(2)}, u32[]{:S(2)}) collective-permute-start(bf16[1056,128]{1,0:T(8,128)(2,1)S(1)} %get-tuple-element.36.refs_0_), channel_id=1, source_target_pairs={{0,8},{8,0},{16,24},{24,16},{1,9},{9,1},{17,25},{25,17},{2,10},{10... | collective-permute-start | bytes 811016 | tf_op jit(solution)/shard_map/ppermute | solution.py:25
  5.0 1.5 %collective-permute-start.3 = (bf16[1056,128]{1,0:T(8,128)(2,1)S(1)}, bf16[1056,128]{1,0:T(8,128)(2,1)S(1)}, u32[]{:S(2)}, u32[]{:S(2)}) collective-permute-start(bf16[1056,128]{1,0:T(8,128)(2,1)S(1)} %get-tuple-element.36.refs_0_), channel_id=1, source_target_pairs={{0,16},{8,24},{16,0},{24,8},{1,17},{9,25},{17,1},{25,9},{2,18},{10... | collective-permute-start | bytes 811016 | tf_op jit(solution)/shard_map/ppermute | solution.py:25
  6.5 0.0 collective-permute-start
  6.5 1.6 %collective-permute-start.1 = (bf16[272,128]{1,0:T(8,128)(2,1)S(1)}, bf16[272,128]{1,0:T(8,128)(2,1)S(1)}, u32[]{:S(2)}, u32[]{:S(2)}) collective-permute-start(bf16[272,128]{1,0:T(8,128)(2,1)S(1)} %get-tuple-element.37.refs_1_.refs_2_), channel_id=1, source_target_pairs={{0,2},{1,3},{2,0},{3,1},{4,6},{5,7},{6,4},{7,5},{8,10},{9,11},{10,... | collective-permute-start | bytes 208904 | tf_op jit(solution)/shard_map/ppermute | solution.py:25
  8.1 2.5 %collective-permute-start.5 = (bf16[272,128]{1,0:T(8,128)(2,1)S(1)}, bf16[272,128]{1,0:T(8,128)(2,1)S(1)}, u32[]{:S(2)}, u32[]{:S(2)}) collective-permute-start(bf16[272,128]{1,0:T(8,128)(2,1)S(1)} %get-tuple-element.37.refs_1_.refs_2_), channel_id=1, source_target_pairs={{0,6},{1,5},{2,4},{3,7},{4,2},{5,1},{6,0},{7,3},{8,14},{9,13},{10,... | collective-permute-start | bytes 208904 | tf_op jit(solution)/shard_map/ppermute | solution.py:228
  10.6 1.3 %collective-permute-start.6 = (bf16[272,128]{1,0:T(8,128)(2,1)S(1)}, bf16[272,128]{1,0:T(8,128)(2,1)S(1)}, u32[]{:S(2)}, u32[]{:S(2)}) collective-permute-start(bf16[272,128]{1,0:T(8,128)(2,1)S(1)} %collective-permute-done.refs_2_.refs_3_), channel_id=1, source_target_pairs={{0,6},{1,5},{2,4},{3,7},{4,2},{5,1},{6,0},{7,3},{8,14},{9,13},{10,... | collective-permute-start | bytes 208904 | tf_op jit(solution)/shard_map/ppermute | solution.py:228
  11.9 0.0 collective-permute-done.1.refs_3_.refs_4_
  11.9 0.7 %shard_map.95 = (f32[128,512]{1,0:T(8,128)S(1)}, f32[3,256,128]{2,1,0:T(8,128)S(1)}) custom-call(bf16[1056,128]{1,0:T(8,128)(2,1)S(1)} %get-tuple-element.36.refs_0_, bf16[272,128]{1,0:T(8,128)(2,1)S(1)} %get-tuple-element.37.refs_1_.refs_2_, bf16[272,128]{1,0:T(8,128)(2,1)S(1)} %collective-permute-done.refs_2_.refs_3_, ...), custom_call_target="tpu_custom_call" | custom-call | flops 1000 | bytes 1000 | tf_op jit(solution)/shard_map/pallas_call | solution.py:188
  12.6 0.3 collective-permute-done.3.refs_1_.refs_2_
  12.9 1.6 %collective-permute-start.10 = (bf16[544,128]{1,0:T(8,128)(2,1)S(1)}, bf16[544,128]{1,0:T(8,128)(2,1)S(1)}, u32[]{:S(2)}, u32[]{:S(2)}) collective-permute-start(bf16[544,128]{1,0:T(8,128)(2,1)S(1)} %slice.7), channel_id=1, source_target_pairs={{0,16},{8,24},{16,0},{24,8},{1,17},{9,25},{17,1},{25,9},{2,18},{10... | collective-permute-start | bytes 417800 | tf_op jit(solution)/shard_map/ppermute | solution.py:25
  14.5 0.6 %collective-permute-start.9 = (bf16[512,128]{1,0:T(8,128)(2,1)S(1)}, bf16[512,128]{1,0:T(8,128)(2,1)S(1)}, u32[]{:S(2)}, u32[]{:S(2)}) collective-permute-start(bf16[512,128]{1,0:T(8,128)(2,1)S(1)} %slice.6), channel_id=1, source_target_pairs={{0,8},{8,0},{16,24},{24,16},{1,9},{9,1},{17,25},{25,17},{2,10},{10... | collective-permute-start | bytes 393224 | tf_op jit(solution)/shard_map/ppermute | solution.py:25
  15.1 1.3 %shard_map.96 = (f32[128,512]{1,0:T(8,128)S(1)}, f32[128,512]{1,0:T(8,128)S(1)}, f32[3,256,128]{2,1,0:T(8,128)S(1)}) custom-call(bf16[1056,128]{1,0:T(8,128)(2,1)S(1)} %collective-permute-done.2.refs_0_.refs_1_, bf16[1056,128]{1,0:T(8,128)(2,1)S(1)} %collective-permute-done.3.refs_1_.refs_2_, bf16[272,128]{1,0:T(8,128)(2,1)S(1)} %get-tuple-element.37.refs_1_.refs_2_, ...), custom_call_target="tpu_custom_call" | custom-call | flops 1000 | bytes 1000 | tf_op jit(solution)/shard_map/pallas_call | solution.py:188
  16.4 0.0 collective-permute-done.5.refs_3_.refs_5_
  16.4 0.3 collective-permute-done.6.refs_4_.refs_6_
  16.8 0.8 %collective-permute-start.7 = (bf16[272,128]{1,0:T(8,128)(2,1)S(1)}, bf16[272,128]{1,0:T(8,128)(2,1)S(1)}, u32[]{:S(2)}, u32[]{:S(2)}) collective-permute-start(bf16[272,128]{1,0:T(8,128)(2,1)S(1)} %collective-permute-done.5.refs_3_.refs_5_), channel_id=1, source_target_pairs={{0,1},{1,0},{2,3},{3,2},{4,5},{5,4},{6,7},{7,6},{8,9},{9,8},{10,11... | collective-permute-start | bytes 208904 | tf_op jit(solution)/shard_map/ppermute | solution.py:25
  17.6 0.0 collective-permute-start.8
  17.6 1.1 %shard_map.97 = (f32[128,512]{1,0:T(8,128)S(1)}, f32[128,512]{1,0:T(8,128)S(1)}, f32[128,512]{1,0:T(8,128)S(1)}, f32[2,256,128]{2,1,0:T(8,128)S(1)}) custom-call(bf16[1056,128]{1,0:T(8,128)(2,1)S(1)} %get-tuple-element.36.refs_0_, bf16[1056,128]{1,0:T(8,128)(2,1)S(1)} %collective-permute-done.2.refs_0_.refs_1_, ...), custom_call_target="tpu_custom_call" | custom-call | flops 1000 | bytes 1000 | tf_op jit(solution)/shard_map/pallas_call | solution.py:188
  18.7 0.1 collective-permute-done.8.refs_5_.refs_9_
  18.8 1.6 %shard_map.98 = (f32[128,512]{1,0:T(8,128)S(1)}, bf16[128,512]{1,0:T(8,128)(2,1)S(1)}, bf16[128,512]{1,0:T(8,128)(2,1)S(1)}, f32[3,256,128]{2,1,0:T(8,128)S(1)}) custom-call(bf16[1056,128]{1,0:T(8,128)(2,1)S(1)} %get-tuple-element.36.refs_0_, bf16[1056,128]{1,0:T(8,128)(2,1)S(1)} %collective-permute-done.2.refs_0_.refs_1_, ...), custom_call_target="tpu_custom_call" | custom-call | flops 1000 | bytes 1000 | tf_op jit(solution)/shard_map/pallas_call | solution.py:188
  20.5 0.8 %shard_map.99 = (f32[128,512]{1,0:T(8,128)S(1)}, bf16[4,256,128]{2,1,0:T(8,128)(2,1)S(1)}) custom-call(bf16[512,128]{1,0:T(8,128)(2,1)S(1)} %collective-permute-done.9.refs_0_, bf16[544,128]{1,0:T(8,128)(2,1)S(1)} %collective-permute-done.10.refs_1_, bf16[272,128]{1,0:T(8,128)(2,1)S(1)} %get-tuple-element.37.refs_1_.refs_2_, ...), custom_call_target="tpu_custom_call" | custom-call | flops 1000 | bytes 1000 | tf_op jit(solution)/shard_map/pallas_call | solution.py:188
  21.3 0.4 %collective-permute-start.11 = (bf16[4,256,128]{2,1,0:T(8,128)(2,1)S(1)}, bf16[4,256,128]{2,1,0:T(8,128)(2,1)S(1)}, u32[]{:S(2)}, u32[]{:S(2)}) collective-permute-start(bf16[4,256,128]{2,1,0:T(8,128)(2,1)S(1)} %get-tuple-element.58), channel_id=1, source_target_pairs={{0,1},{1,0},{2,3},{3,2},{4,5},{5,4},{6,7},{7,6},{8,9},{9,8},{10,11... | collective-permute-start | bytes 786440 | tf_op jit(solution)/shard_map/ppermute | solution.py:25
  21.7 0.9 %collective-permute-start.15 = (bf16[128,512]{1,0:T(8,128)(2,1)S(1)}, bf16[128,512]{1,0:T(8,128)(2,1)S(1)}, u32[]{:S(2)}, u32[]{:S(2)}) collective-permute-start(bf16[128,512]{1,0:T(8,128)(2,1)S(1)} %get-tuple-element.64), channel_id=1, source_target_pairs={{0,8},{8,0},{16,24},{24,16},{1,9},{9,1},{17,25},{25,17},{2,10},{10... | collective-permute-start | bytes 393224 | tf_op jit(solution)/shard_map/ppermute | solution.py:25
  22.6 0.5 %collective-permute-start.16 = (bf16[128,512]{1,0:T(8,128)(2,1)S(1)}, bf16[128,512]{1,0:T(8,128)(2,1)S(1)}, u32[]{:S(2)}, u32[]{:S(2)}) collective-permute-start(bf16[128,512]{1,0:T(8,128)(2,1)S(1)} %get-tuple-element.65), channel_id=1, source_target_pairs={{0,16},{8,24},{16,0},{24,8},{1,17},{9,25},{17,1},{25,9},{2,18},{10... | collective-permute-start | bytes 393224 | tf_op jit(solution)/shard_map/ppermute | solution.py:25
  23.1 0.8 %shard_map.100 = (bf16[128,512]{1,0:T(8,128)(2,1)S(1)}, f32[4,256,128]{2,1,0:T(8,128)S(1)}) custom-call(bf16[512,128]{1,0:T(8,128)(2,1)S(1)} %collective-permute-done.9.refs_0_, bf16[544,128]{1,0:T(8,128)(2,1)S(1)} %collective-permute-done.10.refs_1_, bf16[272,128]{1,0:T(8,128)(2,1)S(1)} %get-tuple-element.37.refs_1_.refs_2_, ...), custom_call_target="tpu_custom_call" | custom-call | flops 1000 | bytes 1000 | tf_op jit(solution)/shard_map/pallas_call | solution.py:188
  24.0 0.1 shard_map.101
  24.0 3.7 %collective-permute-start.12 = (bf16[256,128]{1,0:T(8,128)(2,1)S(1)}, bf16[256,128]{1,0:T(8,128)(2,1)S(1)}, u32[]{:S(2)}, u32[]{:S(2)}) collective-permute-start(bf16[256,128]{1,0:T(8,128)(2,1)S(1)} %get-tuple-element.60), channel_id=1, source_target_pairs={{0,6},{1,5},{2,4},{3,7},{4,2},{5,1},{6,0},{7,3},{8,14},{9,13},{10,... | collective-permute-start | bytes 196616 | tf_op jit(solution)/shard_map/ppermute | solution.py:228
  27.7 0.8 %collective-permute-start.14 = (bf16[256,128]{1,0:T(8,128)(2,1)S(1)}, bf16[256,128]{1,0:T(8,128)(2,1)S(1)}, u32[]{:S(2)}, u32[]{:S(2)}) collective-permute-start(bf16[256,128]{1,0:T(8,128)(2,1)S(1)} %get-tuple-element.62), channel_id=1, source_target_pairs={{0,2},{1,3},{2,0},{3,1},{4,6},{5,7},{6,4},{7,5},{8,10},{9,11},{10,... | collective-permute-start | bytes 196616 | tf_op jit(solution)/shard_map/ppermute | solution.py:25
  28.5 2.1 %collective-permute-start.17 = (bf16[128,512]{1,0:T(8,128)(2,1)S(1)}, bf16[128,512]{1,0:T(8,128)(2,1)S(1)}, u32[]{:S(2)}, u32[]{:S(2)}) collective-permute-start(bf16[128,512]{1,0:T(8,128)(2,1)S(1)} %get-tuple-element.68), channel_id=1, source_target_pairs={{0,24},{8,16},{16,8},{24,0},{1,25},{9,17},{17,9},{25,1},{2,26},{10... | collective-permute-start | bytes 393224 | tf_op jit(solution)/shard_map/ppermute | solution.py:25
  30.6 2.5 %collective-permute-done.13.refs_1_ = bf16[256,128]{1,0:T(8,128)(2,1)S(1)} collective-permute-done((bf16[256,128]{1,0:T(8,128)(2,1)S(1)}, bf16[256,128]{1,0:T(8,128)(2,1)S(1)}, u32[]{:S(2)}, u32[]{:S(2)}) %collective-permute-start.13) | collective-permute-done | bytes 65568 | tf_op jit(solution)/shard_map/ppermute | solution.py:228
  33.1 1.2 %collective-permute-done.17.refs_2_ = bf16[128,512]{1,0:T(8,128)(2,1)S(1)} collective-permute-done((bf16[128,512]{1,0:T(8,128)(2,1)S(1)}, bf16[128,512]{1,0:T(8,128)(2,1)S(1)}, u32[]{:S(2)}, u32[]{:S(2)}) %collective-permute-start.17) | collective-permute-done | bytes 131104 | tf_op jit(solution)/shard_map/ppermute | solution.py:25
  34.4 0.8 %shard_map.103 = (bf16[128,512]{1,0:T(8,128)(2,1)}, bf16[128,128]{1,0:T(8,128)(2,1)}, bf16[128,128]{1,0:T(8,128)(2,1)}) custom-call(f32[128,512]{1,0:T(8,128)S(1)} %get-tuple-element.52.dq_own, f32[256,128]{1,0:T(8,128)S(1)} %shard_map.102.dkv_ref, bf16[128,512]{1,0:T(8,128)(2,1)S(1)} %collective-permute-done.15.refs_0_, ...), custom_call_target="tpu_custom_call" | custom-call | flops 1000 | bytes 1000 | tf_op jit(solution)/shard_map/pallas_call | solution.py:311
  (16 shorter events, 0.1 us)
Async XLA Ops:
  2.0 10.6 %collective-permute-start.2 = (bf16[1056,128]{1,0:T(8,128)(2,1)S(1)}, bf16[1056,128]{1,0:T(8,128)(2,1)S(1)}, u32[]{:S(2)}, u32[]{:S(2)}) collective-permute-start(bf16[1056,128]{1,0:T(8,128)(2,1)S(1)} %get-tuple-element.36.refs_0_), channel_id=1, source_target_pairs={{0,8},{8,0},{16,24},{24,16},{1,9},{9,1},{17,25},{25,17},{2,10},{10... | collective-permute-start | bytes 811016 | tf_op jit(solution)/shard_map/ppermute | solution.py:25
  5.0 7.9 %collective-permute-start.3 = (bf16[1056,128]{1,0:T(8,128)(2,1)S(1)}, bf16[1056,128]{1,0:T(8,128)(2,1)S(1)}, u32[]{:S(2)}, u32[]{:S(2)}) collective-permute-start(bf16[1056,128]{1,0:T(8,128)(2,1)S(1)} %get-tuple-element.36.refs_0_), channel_id=1, source_target_pairs={{0,16},{8,24},{16,0},{24,8},{1,17},{9,25},{17,1},{25,9},{2,18},{10... | collective-permute-start | bytes 811016 | tf_op jit(solution)/shard_map/ppermute | solution.py:25
  6.5 4.1 %collective-permute-start = (bf16[272,128]{1,0:T(8,128)(2,1)S(1)}, bf16[272,128]{1,0:T(8,128)(2,1)S(1)}, u32[]{:S(2)}, u32[]{:S(2)}) collective-permute-start(bf16[272,128]{1,0:T(8,128)(2,1)S(1)} %get-tuple-element.37.refs_1_.refs_2_), channel_id=1, source_target_pairs={{0,1},{1,0},{2,3},{3,2},{4,5},{5,4},{6,7},{7,6},{8,9},{9,8},{10,11... | collective-permute-start | bytes 208904 | tf_op jit(solution)/shard_map/ppermute | solution.py:25
  6.5 5.4 %collective-permute-start.1 = (bf16[272,128]{1,0:T(8,128)(2,1)S(1)}, bf16[272,128]{1,0:T(8,128)(2,1)S(1)}, u32[]{:S(2)}, u32[]{:S(2)}) collective-permute-start(bf16[272,128]{1,0:T(8,128)(2,1)S(1)} %get-tuple-element.37.refs_1_.refs_2_), channel_id=1, source_target_pairs={{0,2},{1,3},{2,0},{3,1},{4,6},{5,7},{6,4},{7,5},{8,10},{9,11},{10,... | collective-permute-start | bytes 208904 | tf_op jit(solution)/shard_map/ppermute | solution.py:25
  8.1 8.3 %collective-permute-start.5 = (bf16[272,128]{1,0:T(8,128)(2,1)S(1)}, bf16[272,128]{1,0:T(8,128)(2,1)S(1)}, u32[]{:S(2)}, u32[]{:S(2)}) collective-permute-start(bf16[272,128]{1,0:T(8,128)(2,1)S(1)} %get-tuple-element.37.refs_1_.refs_2_), channel_id=1, source_target_pairs={{0,6},{1,5},{2,4},{3,7},{4,2},{5,1},{6,0},{7,3},{8,14},{9,13},{10,... | collective-permute-start | bytes 208904 | tf_op jit(solution)/shard_map/ppermute | solution.py:228
  10.6 6.2 %collective-permute-start.6 = (bf16[272,128]{1,0:T(8,128)(2,1)S(1)}, bf16[272,128]{1,0:T(8,128)(2,1)S(1)}, u32[]{:S(2)}, u32[]{:S(2)}) collective-permute-start(bf16[272,128]{1,0:T(8,128)(2,1)S(1)} %collective-permute-done.refs_2_.refs_3_), channel_id=1, source_target_pairs={{0,6},{1,5},{2,4},{3,7},{4,2},{5,1},{6,0},{7,3},{8,14},{9,13},{10,... | collective-permute-start | bytes 208904 | tf_op jit(solution)/shard_map/ppermute | solution.py:228
  12.9 7.5 %collective-permute-start.10 = (bf16[544,128]{1,0:T(8,128)(2,1)S(1)}, bf16[544,128]{1,0:T(8,128)(2,1)S(1)}, u32[]{:S(2)}, u32[]{:S(2)}) collective-permute-start(bf16[544,128]{1,0:T(8,128)(2,1)S(1)} %slice.7), channel_id=1, source_target_pairs={{0,16},{8,24},{16,0},{24,8},{1,17},{9,25},{17,1},{25,9},{2,18},{10... | collective-permute-start | bytes 417800 | tf_op jit(solution)/shard_map/ppermute | solution.py:25
  14.5 5.9 %collective-permute-start.9 = (bf16[512,128]{1,0:T(8,128)(2,1)S(1)}, bf16[512,128]{1,0:T(8,128)(2,1)S(1)}, u32[]{:S(2)}, u32[]{:S(2)}) collective-permute-start(bf16[512,128]{1,0:T(8,128)(2,1)S(1)} %slice.6), channel_id=1, source_target_pairs={{0,8},{8,0},{16,24},{24,16},{1,9},{9,1},{17,25},{25,17},{2,10},{10... | collective-permute-start | bytes 393224 | tf_op jit(solution)/shard_map/ppermute | solution.py:25
  15.1 3.5 %collective-permute-start.4 = (bf16[272,128]{1,0:T(8,128)(2,1)S(1)}, bf16[272,128]{1,0:T(8,128)(2,1)S(1)}, u32[]{:S(2)}, u32[]{:S(2)}) collective-permute-start(bf16[272,128]{1,0:T(8,128)(2,1)S(1)} %collective-permute-done.1.refs_3_.refs_4_), channel_id=1, source_target_pairs={{0,1},{1,0},{2,3},{3,2},{4,5},{5,4},{6,7},{7,6},{8,9},{9,8},{10,11... | collective-permute-start | bytes 208904 | tf_op jit(solution)/shard_map/ppermute | solution.py:25
  16.8 1.9 %collective-permute-start.7 = (bf16[272,128]{1,0:T(8,128)(2,1)S(1)}, bf16[272,128]{1,0:T(8,128)(2,1)S(1)}, u32[]{:S(2)}, u32[]{:S(2)}) collective-permute-start(bf16[272,128]{1,0:T(8,128)(2,1)S(1)} %collective-permute-done.5.refs_3_.refs_5_), channel_id=1, source_target_pairs={{0,1},{1,0},{2,3},{3,2},{4,5},{5,4},{6,7},{7,6},{8,9},{9,8},{10,11... | collective-permute-start | bytes 208904 | tf_op jit(solution)/shard_map/ppermute | solution.py:25
  17.6 1.3 %collective-permute-start.8 = (bf16[272,128]{1,0:T(8,128)(2,1)S(1)}, bf16[272,128]{1,0:T(8,128)(2,1)S(1)}, u32[]{:S(2)}, u32[]{:S(2)}) collective-permute-start(bf16[272,128]{1,0:T(8,128)(2,1)S(1)} %collective-permute-done.6.refs_4_.refs_6_), channel_id=1, source_target_pairs={{0,1},{1,0},{2,3},{3,2},{4,5},{5,4},{6,7},{7,6},{8,9},{9,8},{10,11... | collective-permute-start | bytes 208904 | tf_op jit(solution)/shard_map/ppermute | solution.py:25
  21.3 2.7 %collective-permute-start.11 = (bf16[4,256,128]{2,1,0:T(8,128)(2,1)S(1)}, bf16[4,256,128]{2,1,0:T(8,128)(2,1)S(1)}, u32[]{:S(2)}, u32[]{:S(2)}) collective-permute-start(bf16[4,256,128]{2,1,0:T(8,128)(2,1)S(1)} %get-tuple-element.58), channel_id=1, source_target_pairs={{0,1},{1,0},{2,3},{3,2},{4,5},{5,4},{6,7},{7,6},{8,9},{9,8},{10,11... | collective-permute-start | bytes 786440 | tf_op jit(solution)/shard_map/ppermute | solution.py:25
  21.7 6.8 %collective-permute-start.15 = (bf16[128,512]{1,0:T(8,128)(2,1)S(1)}, bf16[128,512]{1,0:T(8,128)(2,1)S(1)}, u32[]{:S(2)}, u32[]{:S(2)}) collective-permute-start(bf16[128,512]{1,0:T(8,128)(2,1)S(1)} %get-tuple-element.64), channel_id=1, source_target_pairs={{0,8},{8,0},{16,24},{24,16},{1,9},{9,1},{17,25},{25,17},{2,10},{10... | collective-permute-start | bytes 393224 | tf_op jit(solution)/shard_map/ppermute | solution.py:25
  22.6 5.8 %collective-permute-start.16 = (bf16[128,512]{1,0:T(8,128)(2,1)S(1)}, bf16[128,512]{1,0:T(8,128)(2,1)S(1)}, u32[]{:S(2)}, u32[]{:S(2)}) collective-permute-start(bf16[128,512]{1,0:T(8,128)(2,1)S(1)} %get-tuple-element.65), channel_id=1, source_target_pairs={{0,16},{8,24},{16,0},{24,8},{1,17},{9,25},{17,1},{25,9},{2,18},{10... | collective-permute-start | bytes 393224 | tf_op jit(solution)/shard_map/ppermute | solution.py:25
  24.0 6.5 %collective-permute-start.12 = (bf16[256,128]{1,0:T(8,128)(2,1)S(1)}, bf16[256,128]{1,0:T(8,128)(2,1)S(1)}, u32[]{:S(2)}, u32[]{:S(2)}) collective-permute-start(bf16[256,128]{1,0:T(8,128)(2,1)S(1)} %get-tuple-element.60), channel_id=1, source_target_pairs={{0,6},{1,5},{2,4},{3,7},{4,2},{5,1},{6,0},{7,3},{8,14},{9,13},{10,... | collective-permute-start | bytes 196616 | tf_op jit(solution)/shard_map/ppermute | solution.py:228
  27.7 5.4 %collective-permute-start.13 = (bf16[256,128]{1,0:T(8,128)(2,1)S(1)}, bf16[256,128]{1,0:T(8,128)(2,1)S(1)}, u32[]{:S(2)}, u32[]{:S(2)}) collective-permute-start(bf16[256,128]{1,0:T(8,128)(2,1)S(1)} %get-tuple-element.61), channel_id=1, source_target_pairs={{0,4},{1,7},{2,6},{3,5},{4,0},{5,3},{6,2},{7,1},{8,12},{9,15},{10,... | collective-permute-start | bytes 196616 | tf_op jit(solution)/shard_map/ppermute | solution.py:228
  27.7 5.4 %collective-permute-start.14 = (bf16[256,128]{1,0:T(8,128)(2,1)S(1)}, bf16[256,128]{1,0:T(8,128)(2,1)S(1)}, u32[]{:S(2)}, u32[]{:S(2)}) collective-permute-start(bf16[256,128]{1,0:T(8,128)(2,1)S(1)} %get-tuple-element.62), channel_id=1, source_target_pairs={{0,2},{1,3},{2,0},{3,1},{4,6},{5,7},{6,4},{7,5},{8,10},{9,11},{10,... | collective-permute-start | bytes 196616 | tf_op jit(solution)/shard_map/ppermute | solution.py:25
  28.5 5.9 %collective-permute-start.17 = (bf16[128,512]{1,0:T(8,128)(2,1)S(1)}, bf16[128,512]{1,0:T(8,128)(2,1)S(1)}, u32[]{:S(2)}, u32[]{:S(2)}) collective-permute-start(bf16[128,512]{1,0:T(8,128)(2,1)S(1)} %get-tuple-element.68), channel_id=1, source_target_pairs={{0,24},{8,16},{16,8},{24,0},{1,25},{9,17},{17,9},{25,1},{2,26},{10... | collective-permute-start | bytes 393224 | tf_op jit(solution)/shard_map/ppermute | solution.py:25

commit v10 on v9

--- a/solution.py
+++ b/solution.py
@@ -208,7 +208,7 @@
     refs[-1][...] = total
 
 
-def final_kernel(rows, heads, scale, dq_own, dkv_ref, *refs):
+def final_kernel(rows, heads, scale, dq_own, dkv_ref, near_ref, *refs):
     dq_refs, (gq_ref, gk_ref, gv_ref) = refs[:-3], refs[-3:]
     dq = dq_own[...]
     for r in dq_refs:
@@ -216,8 +216,9 @@
     for h in range(heads):
         part = dq[:, h * rows : (h + 1) * rows]
         gq_ref[:, h * 128 : (h + 1) * 128] = (scale * part).T.astype(BF)
-    gk_ref[...] = (scale * dkv_ref[:rows, :]).astype(BF)
-    gv_ref[...] = dkv_ref[rows:, :].astype(BF)
+    dkv = dkv_ref[...] + near_ref[...].astype(F32)
+    gk_ref[...] = (scale * dkv[:rows]).astype(BF)
+    gv_ref[...] = dkv[rows:].astype(BF)
 
 
 def crossed(block, t, other):
@@ -265,8 +266,9 @@
     corner = [swapped(halves[0], "outer", 1), swapped(halves[1], "outer", nq // 2)]
     *dqs, acc = blocks_call(xs, early, range(3), *common, F32, F32, acc=[(acc, n) for n in range(3)])
 
-    *direct, acc = lax.optimization_barrier((*direct, acc))
-    traded = [swapped(block, "inner", 1) for block in (near, *direct)]
+    *fetched, acc = lax.optimization_barrier((near, *direct, acc))
+    direct = fetched[1:]
+    traded = [swapped(block, "inner", 1) for block in fetched]
     xs = [x, *xs]
     n_d, n_t = len(direct), len(traded)
     *dqs, acc_d = blocks_call(xs, direct, range(n_d), *common, F32, F32, dq_in=(dq_own, *dqs))
@@ -297,12 +299,12 @@
     for t in range(1, nz // 2):
         dkv.append(crossed(send[2 * t - 1], t, False))
         dkv.append(crossed(send[2 * t], t, True))
-    dkv.append(swapped(send[0], "inner", 2))
+    dkv_near = swapped(send[0], "inner", 2)
 
     dkv_sum = pl.pallas_call(
         sum_kernel,
         out_shape=sds((2 * rows, width), F32),
-        in_specs=[VMEM] * nz,
+        in_specs=[VMEM] * (nz - 1),
         out_specs=VMEM,
         compiler_params=SMALL,
         cost_estimate=pl.CostEstimate(flops=1_500_000_000, bytes_accessed=1000, transcendentals=0),
@@ -311,11 +313,11 @@
     return pl.pallas_call(
         functools.partial(final_kernel, rows, heads, scale),
         out_shape=(sds((rows, heads * width), BF), sds((rows, width), BF), sds((rows, width), BF)),
-        in_specs=[VMEM] * (2 + len(got)),
+        in_specs=[VMEM] * (3 + len(got)),
         out_specs=(VMEM,) * 3,
         compiler_params=SMALL,
         cost_estimate=QUICK,
-    )(dq_own, dkv_sum, *got)
+    )(dq_own, dkv_sum, dkv_near, *got)
 
 
 def solution(mesh):

time: 35.3 us -> 34.8 us (0.986)
  waiting for transfers between devices: 4.61 us -> 3.96 us
    ppermute x14, waiting for transfers between devices: 1.73 us -> 1.21 us  [swapped(): return lax.ppermute(block, axis, pairs)]
where the time goes in v10:
time: 34.8 us; the launch traced here: 34.6 us
  starting transfers between devices  21.4 us (61%)
  Pallas kernels  8.46 us (24%)
  waiting for transfers between devices  3.96 us (11%)
  between operations  0.76 us (2%)
    ppermute x14, starting transfers between devices, swapped(): return lax.ppermute(block, axis, pairs)  13.9 us
    ppermute x4, starting transfers between devices, crossed(): return lax.ppermute(block, 'inner', pairs)  7.49 us
    pallas_call x6, Pallas kernels, blocks_call(): pl.pallas_call(functools.partial(blocks_kernel, plan, rows, heads, scale)...  6.23 us
    ppermute x4, waiting for transfers between devices, crossed(): return lax.ppermute(block, 'inner', pairs)  2.75 us
    pallas_call x1, Pallas kernels, on_device(): pl.pallas_call(pack_kernel, out_shape=(sds((2 * hr + 32, width), BF), sds...  1.33 us
    ppermute x14, waiting for transfers between devices, swapped(): return lax.ppermute(block, axis, pairs)  1.21 us
    pallas_call x1, Pallas kernels, on_device(): pl.pallas_call(functools.partial(final_kernel, rows, heads, scale), out_s...  0.81 us
  transfers between devices with their start and end apart: 18, of which 5 were waited for; matrix products, arithmetic and copies ran while one was open for 0% of the time, Pallas kernels for 16%

profile of v10, /device:TPU:0, one launch (start us, length us, event | category | flops | bytes accessed | tf_op | source)
XLA Modules:
  0.0 34.6 jit_solution(8856137367225380794)
XLA Ops:
  0.6 1.3 %shard_map.94 = (bf16[1056,128]{1,0:T(8,128)(2,1)S(1)}, bf16[272,128]{1,0:T(8,128)(2,1)S(1)}) custom-call(bf16[128,512]{1,0:T(8,128)(2,1)} %q_ref.1, bf16[128,128]{1,0:T(8,128)(2,1)} %k_ref.1, bf16[128,128]{1,0:T(8,128)(2,1)} %v_ref.1, bf16[128,512]{1,0:T(8,128)(2,1)} %o_ref.1, bf16[128,512]{1,0:T(8,128)(2,1)} %g_ref.1, f32[4,128]{1,0:T(4,128)} %lse_ref.1, ...), custom_call_target="tpu_custom_call" | custom-call | flops 1000 | bytes 1000 | tf_op jit(solution)/shard_map/pallas_call | solution.py:241
  2.0 3.0 %collective-permute-start.2 = (bf16[1056,128]{1,0:T(8,128)(2,1)S(1)}, bf16[1056,128]{1,0:T(8,128)(2,1)S(1)}, u32[]{:S(2)}, u32[]{:S(2)}) collective-permute-start(bf16[1056,128]{1,0:T(8,128)(2,1)S(1)} %get-tuple-element.37.refs_0_), channel_id=1, source_target_pairs={{0,8},{8,0},{16,24},{24,16},{1,9},{9,1},{17,25},{25,17},{2,10},{10... | collective-permute-start | bytes 811016 | tf_op jit(solution)/shard_map/ppermute | solution.py:25
  5.0 1.5 %collective-permute-start.3 = (bf16[1056,128]{1,0:T(8,128)(2,1)S(1)}, bf16[1056,128]{1,0:T(8,128)(2,1)S(1)}, u32[]{:S(2)}, u32[]{:S(2)}) collective-permute-start(bf16[1056,128]{1,0:T(8,128)(2,1)S(1)} %get-tuple-element.37.refs_0_), channel_id=1, source_target_pairs={{0,16},{8,24},{16,0},{24,8},{1,17},{9,25},{17,1},{25,9},{2,18},{10... | collective-permute-start | bytes 811016 | tf_op jit(solution)/shard_map/ppermute | solution.py:25
  6.5 1.6 %collective-permute-start.1 = (bf16[272,128]{1,0:T(8,128)(2,1)S(1)}, bf16[272,128]{1,0:T(8,128)(2,1)S(1)}, u32[]{:S(2)}, u32[]{:S(2)}) collective-permute-start(bf16[272,128]{1,0:T(8,128)(2,1)S(1)} %get-tuple-element.38.refs_1_.refs_2_), channel_id=1, source_target_pairs={{0,2},{1,3},{2,0},{3,1},{4,6},{5,7},{6,4},{7,5},{8,10},{9,11},{10,... | collective-permute-start | bytes 208904 | tf_op jit(solution)/shard_map/ppermute | solution.py:25
  8.1 2.5 %collective-permute-start.4 = (bf16[272,128]{1,0:T(8,128)(2,1)S(1)}, bf16[272,128]{1,0:T(8,128)(2,1)S(1)}, u32[]{:S(2)}, u32[]{:S(2)}) collective-permute-start(bf16[272,128]{1,0:T(8,128)(2,1)S(1)} %get-tuple-element.38.refs_1_.refs_2_), channel_id=1, source_target_pairs={{0,6},{1,5},{2,4},{3,7},{4,2},{5,1},{6,0},{7,3},{8,14},{9,13},{10,... | collective-permute-start | bytes 208904 | tf_op jit(solution)/shard_map/ppermute | solution.py:229
  10.6 1.3 %collective-permute-start.5 = (bf16[272,128]{1,0:T(8,128)(2,1)S(1)}, bf16[272,128]{1,0:T(8,128)(2,1)S(1)}, u32[]{:S(2)}, u32[]{:S(2)}) collective-permute-start(bf16[272,128]{1,0:T(8,128)(2,1)S(1)} %collective-permute-done.refs_2_.refs_3_), channel_id=1, source_target_pairs={{0,6},{1,5},{2,4},{3,7},{4,2},{5,1},{6,0},{7,3},{8,14},{9,13},{10,... | collective-permute-start | bytes 208904 | tf_op jit(solution)/shard_map/ppermute | solution.py:229
  11.9 0.7 %shard_map.95 = (f32[128,512]{1,0:T(8,128)S(1)}, f32[3,256,128]{2,1,0:T(8,128)S(1)}) custom-call(bf16[1056,128]{1,0:T(8,128)(2,1)S(1)} %get-tuple-element.37.refs_0_, bf16[272,128]{1,0:T(8,128)(2,1)S(1)} %get-tuple-element.38.refs_1_.refs_2_, bf16[272,128]{1,0:T(8,128)(2,1)S(1)} %collective-permute-done.refs_2_.refs_3_, ...), custom_call_target="tpu_custom_call" | custom-call | flops 1000 | bytes 1000 | tf_op jit(solution)/shard_map/pallas_call | solution.py:188
  12.6 0.0 collective-permute-done.2.refs_0_.refs_1_
  12.6 0.3 collective-permute-done.3.refs_1_.refs_2_
  12.9 1.6 %collective-permute-start.10 = (bf16[544,128]{1,0:T(8,128)(2,1)S(1)}, bf16[544,128]{1,0:T(8,128)(2,1)S(1)}, u32[]{:S(2)}, u32[]{:S(2)}) collective-permute-start(bf16[544,128]{1,0:T(8,128)(2,1)S(1)} %slice.7), channel_id=1, source_target_pairs={{0,16},{8,24},{16,0},{24,8},{1,17},{9,25},{17,1},{25,9},{2,18},{10... | collective-permute-start | bytes 417800 | tf_op jit(solution)/shard_map/ppermute | solution.py:25
  14.5 0.6 %collective-permute-start.9 = (bf16[512,128]{1,0:T(8,128)(2,1)S(1)}, bf16[512,128]{1,0:T(8,128)(2,1)S(1)}, u32[]{:S(2)}, u32[]{:S(2)}) collective-permute-start(bf16[512,128]{1,0:T(8,128)(2,1)S(1)} %slice.6), channel_id=1, source_target_pairs={{0,8},{8,0},{16,24},{24,16},{1,9},{9,1},{17,25},{25,17},{2,10},{10... | collective-permute-start | bytes 393224 | tf_op jit(solution)/shard_map/ppermute | solution.py:25
  15.1 1.3 %shard_map.96 = (f32[128,512]{1,0:T(8,128)S(1)}, f32[128,512]{1,0:T(8,128)S(1)}, f32[3,256,128]{2,1,0:T(8,128)S(1)}) custom-call(bf16[1056,128]{1,0:T(8,128)(2,1)S(1)} %collective-permute-done.2.refs_0_.refs_1_, bf16[1056,128]{1,0:T(8,128)(2,1)S(1)} %collective-permute-done.3.refs_1_.refs_2_, bf16[272,128]{1,0:T(8,128)(2,1)S(1)} %get-tuple-element.38.refs_1_.refs_2_, ...), custom_call_target="tpu_custom_call" | custom-call | flops 1000 | bytes 1000 | tf_op jit(solution)/shard_map/pallas_call | solution.py:188
  16.4 0.4 %collective-permute-done.5.refs_4_.refs_6_ = bf16[272,128]{1,0:T(8,128)(2,1)S(1)} collective-permute-done((bf16[272,128]{1,0:T(8,128)(2,1)S(1)}, bf16[272,128]{1,0:T(8,128)(2,1)S(1)}, u32[]{:S(2)}, u32[]{:S(2)}) %collective-permute-start.5) | collective-permute-done | bytes 69664 | tf_op jit(solution)/shard_map/ppermute | solution.py:229
  16.8 0.8 %collective-permute-start.6 = (bf16[272,128]{1,0:T(8,128)(2,1)S(1)}, bf16[272,128]{1,0:T(8,128)(2,1)S(1)}, u32[]{:S(2)}, u32[]{:S(2)}) collective-permute-start(bf16[272,128]{1,0:T(8,128)(2,1)S(1)} %collective-permute-done.1.refs_3_.refs_4_), channel_id=1, source_target_pairs={{0,1},{1,0},{2,3},{3,2},{4,5},{5,4},{6,7},{7,6},{8,9},{9,8},{10,11... | collective-permute-start | bytes 208904 | tf_op jit(solution)/shard_map/ppermute | solution.py:25
  17.6 0.0 collective-permute-start.7
  17.6 0.5 %collective-permute-start.8 = (bf16[272,128]{1,0:T(8,128)(2,1)S(1)}, bf16[272,128]{1,0:T(8,128)(2,1)S(1)}, u32[]{:S(2)}, u32[]{:S(2)}) collective-permute-start(bf16[272,128]{1,0:T(8,128)(2,1)S(1)} %collective-permute-done.5.refs_4_.refs_6_), channel_id=1, source_target_pairs={{0,1},{1,0},{2,3},{3,2},{4,5},{5,4},{6,7},{7,6},{8,9},{9,8},{10,11... | collective-permute-start | bytes 208904 | tf_op jit(solution)/shard_map/ppermute | solution.py:25
  18.1 1.1 %shard_map.97 = (f32[128,512]{1,0:T(8,128)S(1)}, f32[128,512]{1,0:T(8,128)S(1)}, f32[128,512]{1,0:T(8,128)S(1)}, f32[2,256,128]{2,1,0:T(8,128)S(1)}) custom-call(bf16[1056,128]{1,0:T(8,128)(2,1)S(1)} %get-tuple-element.37.refs_0_, bf16[1056,128]{1,0:T(8,128)(2,1)S(1)} %collective-permute-done.2.refs_0_.refs_1_, ...), custom_call_target="tpu_custom_call" | custom-call | flops 1000 | bytes 1000 | tf_op jit(solution)/shard_map/pallas_call | solution.py:188
  19.2 1.6 %shard_map.98 = (f32[128,512]{1,0:T(8,128)S(1)}, bf16[128,512]{1,0:T(8,128)(2,1)S(1)}, bf16[128,512]{1,0:T(8,128)(2,1)S(1)}, f32[3,256,128]{2,1,0:T(8,128)S(1)}) custom-call(bf16[1056,128]{1,0:T(8,128)(2,1)S(1)} %get-tuple-element.37.refs_0_, bf16[1056,128]{1,0:T(8,128)(2,1)S(1)} %collective-permute-done.2.refs_0_.refs_1_, ...), custom_call_target="tpu_custom_call" | custom-call | flops 1000 | bytes 1000 | tf_op jit(solution)/shard_map/pallas_call | solution.py:188
  20.9 0.8 %shard_map.99 = (f32[128,512]{1,0:T(8,128)S(1)}, bf16[4,256,128]{2,1,0:T(8,128)(2,1)S(1)}) custom-call(bf16[512,128]{1,0:T(8,128)(2,1)S(1)} %collective-permute-done.9.refs_0_, bf16[544,128]{1,0:T(8,128)(2,1)S(1)} %collective-permute-done.10.refs_1_, bf16[272,128]{1,0:T(8,128)(2,1)S(1)} %get-tuple-element.38.refs_1_.refs_2_, ...), custom_call_target="tpu_custom_call" | custom-call | flops 1000 | bytes 1000 | tf_op jit(solution)/shard_map/pallas_call | solution.py:188
  21.7 0.2 collective-permute-start.11
  21.9 0.8 %collective-permute-start.15 = (bf16[128,512]{1,0:T(8,128)(2,1)S(1)}, bf16[128,512]{1,0:T(8,128)(2,1)S(1)}, u32[]{:S(2)}, u32[]{:S(2)}) collective-permute-start(bf16[128,512]{1,0:T(8,128)(2,1)S(1)} %get-tuple-element.66), channel_id=1, source_target_pairs={{0,8},{8,0},{16,24},{24,16},{1,9},{9,1},{17,25},{25,17},{2,10},{10... | collective-permute-start | bytes 393224 | tf_op jit(solution)/shard_map/ppermute | solution.py:25
  22.6 0.5 %collective-permute-start.16 = (bf16[128,512]{1,0:T(8,128)(2,1)S(1)}, bf16[128,512]{1,0:T(8,128)(2,1)S(1)}, u32[]{:S(2)}, u32[]{:S(2)}) collective-permute-start(bf16[128,512]{1,0:T(8,128)(2,1)S(1)} %get-tuple-element.67), channel_id=1, source_target_pairs={{0,16},{8,24},{16,0},{24,8},{1,17},{9,25},{17,1},{25,9},{2,18},{10... | collective-permute-start | bytes 393224 | tf_op jit(solution)/shard_map/ppermute | solution.py:25
  23.2 0.8 %shard_map.100 = (bf16[128,512]{1,0:T(8,128)(2,1)S(1)}, f32[4,256,128]{2,1,0:T(8,128)S(1)}) custom-call(bf16[512,128]{1,0:T(8,128)(2,1)S(1)} %collective-permute-done.9.refs_0_, bf16[544,128]{1,0:T(8,128)(2,1)S(1)} %collective-permute-done.10.refs_1_, bf16[272,128]{1,0:T(8,128)(2,1)S(1)} %get-tuple-element.38.refs_1_.refs_2_, ...), custom_call_target="tpu_custom_call" | custom-call | flops 1000 | bytes 1000 | tf_op jit(solution)/shard_map/pallas_call | solution.py:188
  24.0 0.1 shard_map.101
  24.0 3.7 %collective-permute-start.12 = (bf16[256,128]{1,0:T(8,128)(2,1)S(1)}, bf16[256,128]{1,0:T(8,128)(2,1)S(1)}, u32[]{:S(2)}, u32[]{:S(2)}) collective-permute-start(bf16[256,128]{1,0:T(8,128)(2,1)S(1)} %get-tuple-element.62), channel_id=1, source_target_pairs={{0,6},{1,5},{2,4},{3,7},{4,2},{5,1},{6,0},{7,3},{8,14},{9,13},{10,... | collective-permute-start | bytes 196616 | tf_op jit(solution)/shard_map/ppermute | solution.py:229
  27.7 0.2 collective-permute-done.16.refs_1_
  27.9 1.4 %collective-permute-start.17 = (bf16[128,512]{1,0:T(8,128)(2,1)S(1)}, bf16[128,512]{1,0:T(8,128)(2,1)S(1)}, u32[]{:S(2)}, u32[]{:S(2)}) collective-permute-start(bf16[128,512]{1,0:T(8,128)(2,1)S(1)} %get-tuple-element.70), channel_id=1, source_target_pairs={{0,24},{8,16},{16,8},{24,0},{1,25},{9,17},{17,9},{25,1},{2,26},{10... | collective-permute-start | bytes 393224 | tf_op jit(solution)/shard_map/ppermute | solution.py:25
  29.3 1.4 %collective-permute-start.14 = (bf16[256,128]{1,0:T(8,128)(2,1)S(1)}, bf16[256,128]{1,0:T(8,128)(2,1)S(1)}, u32[]{:S(2)}, u32[]{:S(2)}) collective-permute-start(bf16[256,128]{1,0:T(8,128)(2,1)S(1)} %get-tuple-element.64), channel_id=1, source_target_pairs={{0,2},{1,3},{2,0},{3,1},{4,6},{5,7},{6,4},{7,5},{8,10},{9,11},{10,... | collective-permute-start | bytes 196616 | tf_op jit(solution)/shard_map/ppermute | solution.py:25
  30.7 2.4 %collective-permute-done.13.refs_1_ = bf16[256,128]{1,0:T(8,128)(2,1)S(1)} collective-permute-done((bf16[256,128]{1,0:T(8,128)(2,1)S(1)}, bf16[256,128]{1,0:T(8,128)(2,1)S(1)}, u32[]{:S(2)}, u32[]{:S(2)}) %collective-permute-start.13) | collective-permute-done | bytes 65568 | tf_op jit(solution)/shard_map/ppermute | solution.py:229
  33.1 0.6 %collective-permute-done.17.refs_2_ = bf16[128,512]{1,0:T(8,128)(2,1)S(1)} collective-permute-done((bf16[128,512]{1,0:T(8,128)(2,1)S(1)}, bf16[128,512]{1,0:T(8,128)(2,1)S(1)}, u32[]{:S(2)}, u32[]{:S(2)}) %collective-permute-start.17) | collective-permute-done | bytes 131104 | tf_op jit(solution)/shard_map/ppermute | solution.py:25
  33.8 0.0 collective-permute-done.14.near_ref
  33.8 0.8 %shard_map.103 = (bf16[128,512]{1,0:T(8,128)(2,1)}, bf16[128,128]{1,0:T(8,128)(2,1)}, bf16[128,128]{1,0:T(8,128)(2,1)}) custom-call(f32[128,512]{1,0:T(8,128)S(1)} %get-tuple-element.54.dq_own, f32[256,128]{1,0:T(8,128)S(1)} %shard_map.102.dkv_ref, bf16[256,128]{1,0:T(8,128)(2,1)S(1)} %collective-permute-done.14.near_ref, ...), custom_call_target="tpu_custom_call" | custom-call | flops 1000 | bytes 1000 | tf_op jit(solution)/shard_map/pallas_call | solution.py:313
  (16 shorter events, 0.1 us)
Async XLA Ops:
  2.0 10.6 %collective-permute-start.2 = (bf16[1056,128]{1,0:T(8,128)(2,1)S(1)}, bf16[1056,128]{1,0:T(8,128)(2,1)S(1)}, u32[]{:S(2)}, u32[]{:S(2)}) collective-permute-start(bf16[1056,128]{1,0:T(8,128)(2,1)S(1)} %get-tuple-element.37.refs_0_), channel_id=1, source_target_pairs={{0,8},{8,0},{16,24},{24,16},{1,9},{9,1},{17,25},{25,17},{2,10},{10... | collective-permute-start | bytes 811016 | tf_op jit(solution)/shard_map/ppermute | solution.py:25
  5.0 7.9 %collective-permute-start.3 = (bf16[1056,128]{1,0:T(8,128)(2,1)S(1)}, bf16[1056,128]{1,0:T(8,128)(2,1)S(1)}, u32[]{:S(2)}, u32[]{:S(2)}) collective-permute-start(bf16[1056,128]{1,0:T(8,128)(2,1)S(1)} %get-tuple-element.37.refs_0_), channel_id=1, source_target_pairs={{0,16},{8,24},{16,0},{24,8},{1,17},{9,25},{17,1},{25,9},{2,18},{10... | collective-permute-start | bytes 811016 | tf_op jit(solution)/shard_map/ppermute | solution.py:25
  6.5 4.1 %collective-permute-start = (bf16[272,128]{1,0:T(8,128)(2,1)S(1)}, bf16[272,128]{1,0:T(8,128)(2,1)S(1)}, u32[]{:S(2)}, u32[]{:S(2)}) collective-permute-start(bf16[272,128]{1,0:T(8,128)(2,1)S(1)} %get-tuple-element.38.refs_1_.refs_2_), channel_id=1, source_target_pairs={{0,1},{1,0},{2,3},{3,2},{4,5},{5,4},{6,7},{7,6},{8,9},{9,8},{10,11... | collective-permute-start | bytes 208904 | tf_op jit(solution)/shard_map/ppermute | solution.py:25
  6.5 5.4 %collective-permute-start.1 = (bf16[272,128]{1,0:T(8,128)(2,1)S(1)}, bf16[272,128]{1,0:T(8,128)(2,1)S(1)}, u32[]{:S(2)}, u32[]{:S(2)}) collective-permute-start(bf16[272,128]{1,0:T(8,128)(2,1)S(1)} %get-tuple-element.38.refs_1_.refs_2_), channel_id=1, source_target_pairs={{0,2},{1,3},{2,0},{3,1},{4,6},{5,7},{6,4},{7,5},{8,10},{9,11},{10,... | collective-permute-start | bytes 208904 | tf_op jit(solution)/shard_map/ppermute | solution.py:25
  8.1 8.3 %collective-permute-start.4 = (bf16[272,128]{1,0:T(8,128)(2,1)S(1)}, bf16[272,128]{1,0:T(8,128)(2,1)S(1)}, u32[]{:S(2)}, u32[]{:S(2)}) collective-permute-start(bf16[272,128]{1,0:T(8,128)(2,1)S(1)} %get-tuple-element.38.refs_1_.refs_2_), channel_id=1, source_target_pairs={{0,6},{1,5},{2,4},{3,7},{4,2},{5,1},{6,0},{7,3},{8,14},{9,13},{10,... | collective-permute-start | bytes 208904 | tf_op jit(solution)/shard_map/ppermute | solution.py:229
  10.6 6.2 %collective-permute-start.5 = (bf16[272,128]{1,0:T(8,128)(2,1)S(1)}, bf16[272,128]{1,0:T(8,128)(2,1)S(1)}, u32[]{:S(2)}, u32[]{:S(2)}) collective-permute-start(bf16[272,128]{1,0:T(8,128)(2,1)S(1)} %collective-permute-done.refs_2_.refs_3_), channel_id=1, source_target_pairs={{0,6},{1,5},{2,4},{3,7},{4,2},{5,1},{6,0},{7,3},{8,14},{9,13},{10,... | collective-permute-start | bytes 208904 | tf_op jit(solution)/shard_map/ppermute | solution.py:229
  12.9 7.9 %collective-permute-start.10 = (bf16[544,128]{1,0:T(8,128)(2,1)S(1)}, bf16[544,128]{1,0:T(8,128)(2,1)S(1)}, u32[]{:S(2)}, u32[]{:S(2)}) collective-permute-start(bf16[544,128]{1,0:T(8,128)(2,1)S(1)} %slice.7), channel_id=1, source_target_pairs={{0,16},{8,24},{16,0},{24,8},{1,17},{9,25},{17,1},{25,9},{2,18},{10... | collective-permute-start | bytes 417800 | tf_op jit(solution)/shard_map/ppermute | solution.py:25
  14.5 6.3 %collective-permute-start.9 = (bf16[512,128]{1,0:T(8,128)(2,1)S(1)}, bf16[512,128]{1,0:T(8,128)(2,1)S(1)}, u32[]{:S(2)}, u32[]{:S(2)}) collective-permute-start(bf16[512,128]{1,0:T(8,128)(2,1)S(1)} %slice.6), channel_id=1, source_target_pairs={{0,8},{8,0},{16,24},{24,16},{1,9},{9,1},{17,25},{25,17},{2,10},{10... | collective-permute-start | bytes 393224 | tf_op jit(solution)/shard_map/ppermute | solution.py:25
  16.8 2.4 %collective-permute-start.6 = (bf16[272,128]{1,0:T(8,128)(2,1)S(1)}, bf16[272,128]{1,0:T(8,128)(2,1)S(1)}, u32[]{:S(2)}, u32[]{:S(2)}) collective-permute-start(bf16[272,128]{1,0:T(8,128)(2,1)S(1)} %collective-permute-done.1.refs_3_.refs_4_), channel_id=1, source_target_pairs={{0,1},{1,0},{2,3},{3,2},{4,5},{5,4},{6,7},{7,6},{8,9},{9,8},{10,11... | collective-permute-start | bytes 208904 | tf_op jit(solution)/shard_map/ppermute | solution.py:25
  17.6 1.6 %collective-permute-start.7 = (bf16[272,128]{1,0:T(8,128)(2,1)S(1)}, bf16[272,128]{1,0:T(8,128)(2,1)S(1)}, u32[]{:S(2)}, u32[]{:S(2)}) collective-permute-start(bf16[272,128]{1,0:T(8,128)(2,1)S(1)} %collective-permute-done.4.refs_3_.refs_5_), channel_id=1, source_target_pairs={{0,1},{1,0},{2,3},{3,2},{4,5},{5,4},{6,7},{7,6},{8,9},{9,8},{10,11... | collective-permute-start | bytes 208904 | tf_op jit(solution)/shard_map/ppermute | solution.py:25
  17.6 1.6 %collective-permute-start.8 = (bf16[272,128]{1,0:T(8,128)(2,1)S(1)}, bf16[272,128]{1,0:T(8,128)(2,1)S(1)}, u32[]{:S(2)}, u32[]{:S(2)}) collective-permute-start(bf16[272,128]{1,0:T(8,128)(2,1)S(1)} %collective-permute-done.5.refs_4_.refs_6_), channel_id=1, source_target_pairs={{0,1},{1,0},{2,3},{3,2},{4,5},{5,4},{6,7},{7,6},{8,9},{9,8},{10,11... | collective-permute-start | bytes 208904 | tf_op jit(solution)/shard_map/ppermute | solution.py:25
  21.7 2.3 %collective-permute-start.11 = (bf16[4,256,128]{2,1,0:T(8,128)(2,1)S(1)}, bf16[4,256,128]{2,1,0:T(8,128)(2,1)S(1)}, u32[]{:S(2)}, u32[]{:S(2)}) collective-permute-start(bf16[4,256,128]{2,1,0:T(8,128)(2,1)S(1)} %get-tuple-element.60), channel_id=1, source_target_pairs={{0,1},{1,0},{2,3},{3,2},{4,5},{5,4},{6,7},{7,6},{8,9},{9,8},{10,11... | collective-permute-start | bytes 786440 | tf_op jit(solution)/shard_map/ppermute | solution.py:25
  21.9 5.8 %collective-permute-start.15 = (bf16[128,512]{1,0:T(8,128)(2,1)S(1)}, bf16[128,512]{1,0:T(8,128)(2,1)S(1)}, u32[]{:S(2)}, u32[]{:S(2)}) collective-permute-start(bf16[128,512]{1,0:T(8,128)(2,1)S(1)} %get-tuple-element.66), channel_id=1, source_target_pairs={{0,8},{8,0},{16,24},{24,16},{1,9},{9,1},{17,25},{25,17},{2,10},{10... | collective-permute-start | bytes 393224 | tf_op jit(solution)/shard_map/ppermute | solution.py:25
  22.6 5.3 %collective-permute-start.16 = (bf16[128,512]{1,0:T(8,128)(2,1)S(1)}, bf16[128,512]{1,0:T(8,128)(2,1)S(1)}, u32[]{:S(2)}, u32[]{:S(2)}) collective-permute-start(bf16[128,512]{1,0:T(8,128)(2,1)S(1)} %get-tuple-element.67), channel_id=1, source_target_pairs={{0,16},{8,24},{16,0},{24,8},{1,17},{9,25},{17,1},{25,9},{2,18},{10... | collective-permute-start | bytes 393224 | tf_op jit(solution)/shard_map/ppermute | solution.py:25
  24.0 6.7 %collective-permute-start.12 = (bf16[256,128]{1,0:T(8,128)(2,1)S(1)}, bf16[256,128]{1,0:T(8,128)(2,1)S(1)}, u32[]{:S(2)}, u32[]{:S(2)}) collective-permute-start(bf16[256,128]{1,0:T(8,128)(2,1)S(1)} %get-tuple-element.62), channel_id=1, source_target_pairs={{0,6},{1,5},{2,4},{3,7},{4,2},{5,1},{6,0},{7,3},{8,14},{9,13},{10,... | collective-permute-start | bytes 196616 | tf_op jit(solution)/shard_map/ppermute | solution.py:229
  27.7 5.4 %collective-permute-start.13 = (bf16[256,128]{1,0:T(8,128)(2,1)S(1)}, bf16[256,128]{1,0:T(8,128)(2,1)S(1)}, u32[]{:S(2)}, u32[]{:S(2)}) collective-permute-start(bf16[256,128]{1,0:T(8,128)(2,1)S(1)} %get-tuple-element.63), channel_id=1, source_target_pairs={{0,4},{1,7},{2,6},{3,5},{4,0},{5,3},{6,2},{7,1},{8,12},{9,15},{10,... | collective-permute-start | bytes 196616 | tf_op jit(solution)/shard_map/ppermute | solution.py:229
  27.9 5.9 %collective-permute-start.17 = (bf16[128,512]{1,0:T(8,128)(2,1)S(1)}, bf16[128,512]{1,0:T(8,128)(2,1)S(1)}, u32[]{:S(2)}, u32[]{:S(2)}) collective-permute-start(bf16[128,512]{1,0:T(8,128)(2,1)S(1)} %get-tuple-element.70), channel_id=1, source_target_pairs={{0,24},{8,16},{16,8},{24,0},{1,25},{9,17},{17,9},{25,1},{2,26},{10... | collective-permute-start | bytes 393224 | tf_op jit(solution)/shard_map/ppermute | solution.py:25
  29.3 4.5 %collective-permute-start.14 = (bf16[256,128]{1,0:T(8,128)(2,1)S(1)}, bf16[256,128]{1,0:T(8,128)(2,1)S(1)}, u32[]{:S(2)}, u32[]{:S(2)}) collective-permute-start(bf16[256,128]{1,0:T(8,128)(2,1)S(1)} %get-tuple-element.64), channel_id=1, source_target_pairs={{0,2},{1,3},{2,0},{3,1},{4,6},{5,7},{6,4},{7,5},{8,10},{9,11},{10,... | collective-permute-start | bytes 196616 | tf_op jit(solution)/shard_map/ppermute | solution.py:25

commit v11 on v10

--- a/solution.py
+++ b/solution.py
@@ -195,10 +195,20 @@
     )(*args)
 
 
-def add_kernel(own_ref, got_ref, first_ref, *refs):
-    first_ref[...] = own_ref[0] + got_ref[0].astype(F32)
+def add_kernel(start, own_ref, got_ref, *refs):
     for n, ref in enumerate(refs):
-        ref[...] = (own_ref[n + 1] + got_ref[n + 1].astype(F32)).astype(BF)
+        ref[...] = (own_ref[n] + got_ref[start + n].astype(F32)).astype(ref.dtype)
+
+
+def add_call(own, got, start, types):
+    return pl.pallas_call(
+        functools.partial(add_kernel, start),
+        out_shape=tuple(jax.ShapeDtypeStruct(own.shape[1:], t) for t in types),
+        in_specs=[VMEM] * 2,
+        out_specs=(VMEM,) * len(types),
+        compiler_params=SMALL,
+        cost_estimate=QUICK,
+    )(own, got)
 
 
 def sum_kernel(own_ref, *refs):
@@ -283,23 +293,19 @@
         ours += [3 + t, 4 + n_d + t + 1]
     dq_last, dkv_sib = blocks_call([corner], arrays, theirs, *common, BF, F32, acc=accs)
     dkv_got = swapped(dkv_sib, "inner", 1)
-    dq_last, dkv_own = blocks_call([corner], arrays, ours, *common, F32, BF, acc=accs, dq_in=[dq_last])
-    dkv_own, *send = pl.pallas_call(
-        add_kernel,
-        out_shape=(sds((2 * rows, width), F32),) + (sds((2 * rows, width), BF),) * (nz - 1),
-        in_specs=[VMEM] * 2,
-        out_specs=(VMEM,) * nz,
-        compiler_params=SMALL,
-        cost_estimate=QUICK,
-    )(dkv_own, dkv_got)
+    dq_last, dkv_far = blocks_call([corner], arrays, ours[2:], *common, F32, F32, acc=accs, dq_in=[dq_last])
+    dq_last, dkv_own = blocks_call([corner], arrays, ours[:2], *common, F32, BF, acc=accs, dq_in=[dq_last])
+    far = add_call(dkv_far, dkv_got, 2, [BF] * (nz - 2))
+    dkv_own, dkv_near = add_call(dkv_own, dkv_got, 0, [F32, BF])
+
     got = [swapped(dq, "outer", s + 1) for s, dq in enumerate(dqs)]
-    dq_last, *got = lax.optimization_barrier((dq_last, *got))
+    dq_last, got[0] = lax.optimization_barrier((dq_last, got[0]))
     got.append(swapped(dq_last, "outer", nq - 1))
     dkv = []
     for t in range(1, nz // 2):
-        dkv.append(crossed(send[2 * t - 1], t, False))
-        dkv.append(crossed(send[2 * t], t, True))
-    dkv_near = swapped(send[0], "inner", 2)
+        dkv.append(crossed(far[2 * t - 2], t, False))
+        dkv.append(crossed(far[2 * t - 1], t, True))
+    dkv_near = swapped(dkv_near, "inner", 2)
 
     dkv_sum = pl.pallas_call(
         sum_kernel,

time: 34.8 us -> 35.7 us (1.026)
  waiting for transfers between devices: 3.96 us -> 4.51 us
    ppermute x14, waiting for transfers between devices: 1.21 us -> 2.44 us  [swapped(): return lax.ppermute(block, axis, pairs)]
    ppermute x4, waiting for transfers between devices: 2.75 us -> 2.07 us  [crossed(): return lax.ppermute(block, 'inner', pairs)]
    pallas_call x6 -> x7, Pallas kernels: 6.23 us -> 6.39 us  [blocks_call(): pl.pallas_call(functools.partial(blocks_kernel, plan, rows, heads, scale)...]
where the time goes in v11:
time: 35.7 us; the launch traced here: 35.5 us
  starting transfers between devices  21.6 us (61%)
  Pallas kernels  8.62 us (24%)
  waiting for transfers between devices  4.51 us (13%)
  between operations  0.77 us (2%)
    ppermute x14, starting transfers between devices, swapped(): return lax.ppermute(block, axis, pairs)  14.2 us
    ppermute x4, starting transfers between devices, crossed(): return lax.ppermute(block, 'inner', pairs)  7.36 us
    pallas_call x7, Pallas kernels, blocks_call(): pl.pallas_call(functools.partial(blocks_kernel, plan, rows, heads, scale)...  6.39 us
    ppermute x14, waiting for transfers between devices, swapped(): return lax.ppermute(block, axis, pairs)  2.44 us
    ppermute x4, waiting for transfers between devices, crossed(): return lax.ppermute(block, 'inner', pairs)  2.07 us
    pallas_call x1, Pallas kernels, on_device(): pl.pallas_call(pack_kernel, out_shape=(sds((2 * hr + 32, width), BF), sds...  1.33 us
    pallas_call x1, Pallas kernels, on_device(): pl.pallas_call(functools.partial(final_kernel, rows, heads, scale), out_s...  0.8 us
  transfers between devices with their start and end apart: 18, of which 5 were waited for; matrix products, arithmetic and copies ran while one was open for 0% of the time, Pallas kernels for 16%

profile of v11, /device:TPU:0, one launch (start us, length us, event | category | flops | bytes accessed | tf_op | source)
XLA Modules:
  0.0 35.5 jit_solution(9683382048107836703)
XLA Ops:
  0.6 1.3 %shard_map.94 = (bf16[1056,128]{1,0:T(8,128)(2,1)S(1)}, bf16[272,128]{1,0:T(8,128)(2,1)S(1)}) custom-call(bf16[128,512]{1,0:T(8,128)(2,1)} %q_ref.1, bf16[128,128]{1,0:T(8,128)(2,1)} %k_ref.1, bf16[128,128]{1,0:T(8,128)(2,1)} %v_ref.1, bf16[128,512]{1,0:T(8,128)(2,1)} %o_ref.1, bf16[128,512]{1,0:T(8,128)(2,1)} %g_ref.1, f32[4,128]{1,0:T(4,128)} %lse_ref.1, ...), custom_call_target="tpu_custom_call" | custom-call | flops 1000 | bytes 1000 | tf_op jit(solution)/shard_map/pallas_call | solution.py:251
  2.0 3.0 %collective-permute-start.2 = (bf16[1056,128]{1,0:T(8,128)(2,1)S(1)}, bf16[1056,128]{1,0:T(8,128)(2,1)S(1)}, u32[]{:S(2)}, u32[]{:S(2)}) collective-permute-start(bf16[1056,128]{1,0:T(8,128)(2,1)S(1)} %get-tuple-element.38.refs_0_), channel_id=1, source_target_pairs={{0,8},{8,0},{16,24},{24,16},{1,9},{9,1},{17,25},{25,17},{2,10},{10... | collective-permute-start | bytes 811016 | tf_op jit(solution)/shard_map/ppermute | solution.py:25
  5.0 1.5 %collective-permute-start.3 = (bf16[1056,128]{1,0:T(8,128)(2,1)S(1)}, bf16[1056,128]{1,0:T(8,128)(2,1)S(1)}, u32[]{:S(2)}, u32[]{:S(2)}) collective-permute-start(bf16[1056,128]{1,0:T(8,128)(2,1)S(1)} %get-tuple-element.38.refs_0_), channel_id=1, source_target_pairs={{0,16},{8,24},{16,0},{24,8},{1,17},{9,25},{17,1},{25,9},{2,18},{10... | collective-permute-start | bytes 811016 | tf_op jit(solution)/shard_map/ppermute | solution.py:25
  6.5 1.6 %collective-permute-start.1 = (bf16[272,128]{1,0:T(8,128)(2,1)S(1)}, bf16[272,128]{1,0:T(8,128)(2,1)S(1)}, u32[]{:S(2)}, u32[]{:S(2)}) collective-permute-start(bf16[272,128]{1,0:T(8,128)(2,1)S(1)} %get-tuple-element.39.refs_1_.refs_2_), channel_id=1, source_target_pairs={{0,2},{1,3},{2,0},{3,1},{4,6},{5,7},{6,4},{7,5},{8,10},{9,11},{10,... | collective-permute-start | bytes 208904 | tf_op jit(solution)/shard_map/ppermute | solution.py:25
  8.1 2.5 %collective-permute-start.4 = (bf16[272,128]{1,0:T(8,128)(2,1)S(1)}, bf16[272,128]{1,0:T(8,128)(2,1)S(1)}, u32[]{:S(2)}, u32[]{:S(2)}) collective-permute-start(bf16[272,128]{1,0:T(8,128)(2,1)S(1)} %get-tuple-element.39.refs_1_.refs_2_), channel_id=1, source_target_pairs={{0,6},{1,5},{2,4},{3,7},{4,2},{5,1},{6,0},{7,3},{8,14},{9,13},{10,... | collective-permute-start | bytes 208904 | tf_op jit(solution)/shard_map/ppermute | solution.py:239
  10.6 1.3 %collective-permute-start.5 = (bf16[272,128]{1,0:T(8,128)(2,1)S(1)}, bf16[272,128]{1,0:T(8,128)(2,1)S(1)}, u32[]{:S(2)}, u32[]{:S(2)}) collective-permute-start(bf16[272,128]{1,0:T(8,128)(2,1)S(1)} %collective-permute-done.refs_2_.refs_3_), channel_id=1, source_target_pairs={{0,6},{1,5},{2,4},{3,7},{4,2},{5,1},{6,0},{7,3},{8,14},{9,13},{10,... | collective-permute-start | bytes 208904 | tf_op jit(solution)/shard_map/ppermute | solution.py:239
  11.9 0.7 %shard_map.95 = (f32[128,512]{1,0:T(8,128)S(1)}, f32[3,256,128]{2,1,0:T(8,128)S(1)}) custom-call(bf16[1056,128]{1,0:T(8,128)(2,1)S(1)} %get-tuple-element.38.refs_0_, bf16[272,128]{1,0:T(8,128)(2,1)S(1)} %get-tuple-element.39.refs_1_.refs_2_, bf16[272,128]{1,0:T(8,128)(2,1)S(1)} %collective-permute-done.refs_2_.refs_3_, ...), custom_call_target="tpu_custom_call" | custom-call | flops 1000 | bytes 1000 | tf_op jit(solution)/shard_map/pallas_call | solution.py:188
  12.6 0.0 collective-permute-done.2.refs_0_.refs_1_
  12.6 0.3 collective-permute-done.3.refs_1_.refs_2_
  12.9 1.6 %collective-permute-start.10 = (bf16[544,128]{1,0:T(8,128)(2,1)S(1)}, bf16[544,128]{1,0:T(8,128)(2,1)S(1)}, u32[]{:S(2)}, u32[]{:S(2)}) collective-permute-start(bf16[544,128]{1,0:T(8,128)(2,1)S(1)} %slice.7), channel_id=1, source_target_pairs={{0,16},{8,24},{16,0},{24,8},{1,17},{9,25},{17,1},{25,9},{2,18},{10... | collective-permute-start | bytes 417800 | tf_op jit(solution)/shard_map/ppermute | solution.py:25
  14.5 0.6 %collective-permute-start.9 = (bf16[512,128]{1,0:T(8,128)(2,1)S(1)}, bf16[512,128]{1,0:T(8,128)(2,1)S(1)}, u32[]{:S(2)}, u32[]{:S(2)}) collective-permute-start(bf16[512,128]{1,0:T(8,128)(2,1)S(1)} %slice.6), channel_id=1, source_target_pairs={{0,8},{8,0},{16,24},{24,16},{1,9},{9,1},{17,25},{25,17},{2,10},{10... | collective-permute-start | bytes 393224 | tf_op jit(solution)/shard_map/ppermute | solution.py:25
  15.1 1.3 %shard_map.96 = (f32[128,512]{1,0:T(8,128)S(1)}, f32[128,512]{1,0:T(8,128)S(1)}, f32[3,256,128]{2,1,0:T(8,128)S(1)}) custom-call(bf16[1056,128]{1,0:T(8,128)(2,1)S(1)} %collective-permute-done.2.refs_0_.refs_1_, bf16[1056,128]{1,0:T(8,128)(2,1)S(1)} %collective-permute-done.3.refs_1_.refs_2_, bf16[272,128]{1,0:T(8,128)(2,1)S(1)} %get-tuple-element.39.refs_1_.refs_2_, ...), custom_call_target="tpu_custom_call" | custom-call | flops 1000 | bytes 1000 | tf_op jit(solution)/shard_map/pallas_call | solution.py:188
  16.4 0.0 collective-permute-done.4.refs_3_.refs_5_
  16.4 0.4 collective-permute-done.5.refs_4_.refs_6_
  16.8 0.8 %collective-permute-start.6 = (bf16[272,128]{1,0:T(8,128)(2,1)S(1)}, bf16[272,128]{1,0:T(8,128)(2,1)S(1)}, u32[]{:S(2)}, u32[]{:S(2)}) collective-permute-start(bf16[272,128]{1,0:T(8,128)(2,1)S(1)} %collective-permute-done.1.refs_3_.refs_4_), channel_id=1, source_target_pairs={{0,1},{1,0},{2,3},{3,2},{4,5},{5,4},{6,7},{7,6},{8,9},{9,8},{10,11... | collective-permute-start | bytes 208904 | tf_op jit(solution)/shard_map/ppermute | solution.py:25
  17.6 0.0 collective-permute-start.7
  17.6 0.5 %collective-permute-start.8 = (bf16[272,128]{1,0:T(8,128)(2,1)S(1)}, bf16[272,128]{1,0:T(8,128)(2,1)S(1)}, u32[]{:S(2)}, u32[]{:S(2)}) collective-permute-start(bf16[272,128]{1,0:T(8,128)(2,1)S(1)} %collective-permute-done.5.refs_4_.refs_6_), channel_id=1, source_target_pairs={{0,1},{1,0},{2,3},{3,2},{4,5},{5,4},{6,7},{7,6},{8,9},{9,8},{10,11... | collective-permute-start | bytes 208904 | tf_op jit(solution)/shard_map/ppermute | solution.py:25
  18.1 1.1 %shard_map.97 = (f32[128,512]{1,0:T(8,128)S(1)}, f32[128,512]{1,0:T(8,128)S(1)}, f32[128,512]{1,0:T(8,128)S(1)}, f32[2,256,128]{2,1,0:T(8,128)S(1)}) custom-call(bf16[1056,128]{1,0:T(8,128)(2,1)S(1)} %get-tuple-element.38.refs_0_, bf16[1056,128]{1,0:T(8,128)(2,1)S(1)} %collective-permute-done.2.refs_0_.refs_1_, ...), custom_call_target="tpu_custom_call" | custom-call | flops 1000 | bytes 1000 | tf_op jit(solution)/shard_map/pallas_call | solution.py:188
  19.2 1.6 %shard_map.98 = (f32[128,512]{1,0:T(8,128)S(1)}, bf16[128,512]{1,0:T(8,128)(2,1)S(1)}, bf16[128,512]{1,0:T(8,128)(2,1)S(1)}, f32[3,256,128]{2,1,0:T(8,128)S(1)}) custom-call(bf16[1056,128]{1,0:T(8,128)(2,1)S(1)} %get-tuple-element.38.refs_0_, bf16[1056,128]{1,0:T(8,128)(2,1)S(1)} %collective-permute-done.2.refs_0_.refs_1_, ...), custom_call_target="tpu_custom_call" | custom-call | flops 1000 | bytes 1000 | tf_op jit(solution)/shard_map/pallas_call | solution.py:188
  20.9 0.8 %shard_map.99 = (f32[128,512]{1,0:T(8,128)S(1)}, bf16[4,256,128]{2,1,0:T(8,128)(2,1)S(1)}) custom-call(bf16[512,128]{1,0:T(8,128)(2,1)S(1)} %collective-permute-done.9.refs_0_, bf16[544,128]{1,0:T(8,128)(2,1)S(1)} %collective-permute-done.10.refs_1_, bf16[272,128]{1,0:T(8,128)(2,1)S(1)} %get-tuple-element.39.refs_1_.refs_2_, ...), custom_call_target="tpu_custom_call" | custom-call | flops 1000 | bytes 1000 | tf_op jit(solution)/shard_map/pallas_call | solution.py:188
  21.7 0.2 collective-permute-start.11
  21.9 0.8 %collective-permute-start.15 = (bf16[128,512]{1,0:T(8,128)(2,1)S(1)}, bf16[128,512]{1,0:T(8,128)(2,1)S(1)}, u32[]{:S(2)}, u32[]{:S(2)}) collective-permute-start(bf16[128,512]{1,0:T(8,128)(2,1)S(1)} %get-tuple-element.69), channel_id=1, source_target_pairs={{0,8},{8,0},{16,24},{24,16},{1,9},{9,1},{17,25},{25,17},{2,10},{10... | collective-permute-start | bytes 393224 | tf_op jit(solution)/shard_map/ppermute | solution.py:25
  22.6 0.5 %shard_map.100 = (f32[128,512]{1,0:T(8,128)S(1)}, f32[2,256,128]{2,1,0:T(8,128)S(1)}) custom-call(bf16[512,128]{1,0:T(8,128)(2,1)S(1)} %collective-permute-done.9.refs_0_, bf16[544,128]{1,0:T(8,128)(2,1)S(1)} %collective-permute-done.10.refs_1_, bf16[272,128]{1,0:T(8,128)(2,1)S(1)} %get-tuple-element.39.refs_1_.refs_2_, ...), custom_call_target="tpu_custom_call" | custom-call | flops 1000 | bytes 1000 | tf_op jit(solution)/shard_map/pallas_call | solution.py:188
  23.1 0.1 collective-permute-done.11.got_ref
  23.3 3.5 %collective-permute-start.12 = (bf16[256,128]{1,0:T(8,128)(2,1)S(1)}, bf16[256,128]{1,0:T(8,128)(2,1)S(1)}, u32[]{:S(2)}, u32[]{:S(2)}) collective-permute-start(bf16[256,128]{1,0:T(8,128)(2,1)S(1)} %get-tuple-element.65), channel_id=1, source_target_pairs={{0,6},{1,5},{2,4},{3,7},{4,2},{5,1},{6,0},{7,3},{8,14},{9,13},{10,... | collective-permute-start | bytes 196616 | tf_op jit(solution)/shard_map/ppermute | solution.py:239
  26.8 0.5 %collective-permute-start.16 = (bf16[128,512]{1,0:T(8,128)(2,1)S(1)}, bf16[128,512]{1,0:T(8,128)(2,1)S(1)}, u32[]{:S(2)}, u32[]{:S(2)}) collective-permute-start(bf16[128,512]{1,0:T(8,128)(2,1)S(1)} %get-tuple-element.71), channel_id=1, source_target_pairs={{0,16},{8,24},{16,0},{24,8},{1,17},{9,25},{17,1},{25,9},{2,18},{10... | collective-permute-start | bytes 393224 | tf_op jit(solution)/shard_map/ppermute | solution.py:25
  27.3 0.5 %shard_map.101 = (bf16[128,512]{1,0:T(8,128)(2,1)S(1)}, f32[2,256,128]{2,1,0:T(8,128)S(1)}) custom-call(bf16[512,128]{1,0:T(8,128)(2,1)S(1)} %collective-permute-done.9.refs_0_, bf16[544,128]{1,0:T(8,128)(2,1)S(1)} %collective-permute-done.10.refs_1_, bf16[272,128]{1,0:T(8,128)(2,1)S(1)} %get-tuple-element.39.refs_1_.refs_2_, ...), custom_call_target="tpu_custom_call" | custom-call | flops 1000 | bytes 1000 | tf_op jit(solution)/shard_map/pallas_call | solution.py:188
  27.8 1.7 %collective-permute-start.17 = (bf16[128,512]{1,0:T(8,128)(2,1)S(1)}, bf16[128,512]{1,0:T(8,128)(2,1)S(1)}, u32[]{:S(2)}, u32[]{:S(2)}) collective-permute-start(bf16[128,512]{1,0:T(8,128)(2,1)S(1)} %get-tuple-element.72), channel_id=1, source_target_pairs={{0,24},{8,16},{16,8},{24,0},{1,25},{9,17},{17,9},{25,1},{2,26},{10... | collective-permute-start | bytes 393224 | tf_op jit(solution)/shard_map/ppermute | solution.py:25
  29.6 1.4 %collective-permute-start.14 = (bf16[256,128]{1,0:T(8,128)(2,1)S(1)}, bf16[256,128]{1,0:T(8,128)(2,1)S(1)}, u32[]{:S(2)}, u32[]{:S(2)}) collective-permute-start(bf16[256,128]{1,0:T(8,128)(2,1)S(1)} %get-tuple-element.67), channel_id=1, source_target_pairs={{0,2},{1,3},{2,0},{3,1},{4,6},{5,7},{6,4},{7,5},{8,10},{9,11},{10,... | collective-permute-start | bytes 196616 | tf_op jit(solution)/shard_map/ppermute | solution.py:25
  31.0 1.7 %collective-permute-done.13.refs_1_ = bf16[256,128]{1,0:T(8,128)(2,1)S(1)} collective-permute-done((bf16[256,128]{1,0:T(8,128)(2,1)S(1)}, bf16[256,128]{1,0:T(8,128)(2,1)S(1)}, u32[]{:S(2)}, u32[]{:S(2)}) %collective-permute-start.13) | collective-permute-done | bytes 65568 | tf_op jit(solution)/shard_map/ppermute | solution.py:239
  32.7 1.9 %collective-permute-done.16.refs_1_ = bf16[128,512]{1,0:T(8,128)(2,1)S(1)} collective-permute-done((bf16[128,512]{1,0:T(8,128)(2,1)S(1)}, bf16[128,512]{1,0:T(8,128)(2,1)S(1)}, u32[]{:S(2)}, u32[]{:S(2)}) %collective-permute-start.16) | collective-permute-done | bytes 131104 | tf_op jit(solution)/shard_map/ppermute | solution.py:25
  34.7 0.8 %shard_map.105 = (bf16[128,512]{1,0:T(8,128)(2,1)}, bf16[128,128]{1,0:T(8,128)(2,1)}, bf16[128,128]{1,0:T(8,128)(2,1)}) custom-call(f32[128,512]{1,0:T(8,128)S(1)} %get-tuple-element.55.dq_own, f32[256,128]{1,0:T(8,128)S(1)} %shard_map.104.dkv_ref, bf16[256,128]{1,0:T(8,128)(2,1)S(1)} %collective-permute-done.14.near_ref, ...), custom_call_target="tpu_custom_call" | custom-call | flops 1000 | bytes 1000 | tf_op jit(solution)/shard_map/pallas_call | solution.py:319
  (18 shorter events, 0.1 us)
Async XLA Ops:
  2.0 10.6 %collective-permute-start.2 = (bf16[1056,128]{1,0:T(8,128)(2,1)S(1)}, bf16[1056,128]{1,0:T(8,128)(2,1)S(1)}, u32[]{:S(2)}, u32[]{:S(2)}) collective-permute-start(bf16[1056,128]{1,0:T(8,128)(2,1)S(1)} %get-tuple-element.38.refs_0_), channel_id=1, source_target_pairs={{0,8},{8,0},{16,24},{24,16},{1,9},{9,1},{17,25},{25,17},{2,10},{10... | collective-permute-start | bytes 811016 | tf_op jit(solution)/shard_map/ppermute | solution.py:25
  5.0 7.9 %collective-permute-start.3 = (bf16[1056,128]{1,0:T(8,128)(2,1)S(1)}, bf16[1056,128]{1,0:T(8,128)(2,1)S(1)}, u32[]{:S(2)}, u32[]{:S(2)}) collective-permute-start(bf16[1056,128]{1,0:T(8,128)(2,1)S(1)} %get-tuple-element.38.refs_0_), channel_id=1, source_target_pairs={{0,16},{8,24},{16,0},{24,8},{1,17},{9,25},{17,1},{25,9},{2,18},{10... | collective-permute-start | bytes 811016 | tf_op jit(solution)/shard_map/ppermute | solution.py:25
  6.5 4.1 %collective-permute-start = (bf16[272,128]{1,0:T(8,128)(2,1)S(1)}, bf16[272,128]{1,0:T(8,128)(2,1)S(1)}, u32[]{:S(2)}, u32[]{:S(2)}) collective-permute-start(bf16[272,128]{1,0:T(8,128)(2,1)S(1)} %get-tuple-element.39.refs_1_.refs_2_), channel_id=1, source_target_pairs={{0,1},{1,0},{2,3},{3,2},{4,5},{5,4},{6,7},{7,6},{8,9},{9,8},{10,11... | collective-permute-start | bytes 208904 | tf_op jit(solution)/shard_map/ppermute | solution.py:25
  6.5 5.4 %collective-permute-start.1 = (bf16[272,128]{1,0:T(8,128)(2,1)S(1)}, bf16[272,128]{1,0:T(8,128)(2,1)S(1)}, u32[]{:S(2)}, u32[]{:S(2)}) collective-permute-start(bf16[272,128]{1,0:T(8,128)(2,1)S(1)} %get-tuple-element.39.refs_1_.refs_2_), channel_id=1, source_target_pairs={{0,2},{1,3},{2,0},{3,1},{4,6},{5,7},{6,4},{7,5},{8,10},{9,11},{10,... | collective-permute-start | bytes 208904 | tf_op jit(solution)/shard_map/ppermute | solution.py:25
  8.1 8.3 %collective-permute-start.4 = (bf16[272,128]{1,0:T(8,128)(2,1)S(1)}, bf16[272,128]{1,0:T(8,128)(2,1)S(1)}, u32[]{:S(2)}, u32[]{:S(2)}) collective-permute-start(bf16[272,128]{1,0:T(8,128)(2,1)S(1)} %get-tuple-element.39.refs_1_.refs_2_), channel_id=1, source_target_pairs={{0,6},{1,5},{2,4},{3,7},{4,2},{5,1},{6,0},{7,3},{8,14},{9,13},{10,... | collective-permute-start | bytes 208904 | tf_op jit(solution)/shard_map/ppermute | solution.py:239
  10.6 6.2 %collective-permute-start.5 = (bf16[272,128]{1,0:T(8,128)(2,1)S(1)}, bf16[272,128]{1,0:T(8,128)(2,1)S(1)}, u32[]{:S(2)}, u32[]{:S(2)}) collective-permute-start(bf16[272,128]{1,0:T(8,128)(2,1)S(1)} %collective-permute-done.refs_2_.refs_3_), channel_id=1, source_target_pairs={{0,6},{1,5},{2,4},{3,7},{4,2},{5,1},{6,0},{7,3},{8,14},{9,13},{10,... | collective-permute-start | bytes 208904 | tf_op jit(solution)/shard_map/ppermute | solution.py:239
  12.9 7.9 %collective-permute-start.10 = (bf16[544,128]{1,0:T(8,128)(2,1)S(1)}, bf16[544,128]{1,0:T(8,128)(2,1)S(1)}, u32[]{:S(2)}, u32[]{:S(2)}) collective-permute-start(bf16[544,128]{1,0:T(8,128)(2,1)S(1)} %slice.7), channel_id=1, source_target_pairs={{0,16},{8,24},{16,0},{24,8},{1,17},{9,25},{17,1},{25,9},{2,18},{10... | collective-permute-start | bytes 417800 | tf_op jit(solution)/shard_map/ppermute | solution.py:25
  14.5 6.3 %collective-permute-start.9 = (bf16[512,128]{1,0:T(8,128)(2,1)S(1)}, bf16[512,128]{1,0:T(8,128)(2,1)S(1)}, u32[]{:S(2)}, u32[]{:S(2)}) collective-permute-start(bf16[512,128]{1,0:T(8,128)(2,1)S(1)} %slice.6), channel_id=1, source_target_pairs={{0,8},{8,0},{16,24},{24,16},{1,9},{9,1},{17,25},{25,17},{2,10},{10... | collective-permute-start | bytes 393224 | tf_op jit(solution)/shard_map/ppermute | solution.py:25
  16.8 2.4 %collective-permute-start.6 = (bf16[272,128]{1,0:T(8,128)(2,1)S(1)}, bf16[272,128]{1,0:T(8,128)(2,1)S(1)}, u32[]{:S(2)}, u32[]{:S(2)}) collective-permute-start(bf16[272,128]{1,0:T(8,128)(2,1)S(1)} %collective-permute-done.1.refs_3_.refs_4_), channel_id=1, source_target_pairs={{0,1},{1,0},{2,3},{3,2},{4,5},{5,4},{6,7},{7,6},{8,9},{9,8},{10,11... | collective-permute-start | bytes 208904 | tf_op jit(solution)/shard_map/ppermute | solution.py:25
  17.6 1.6 %collective-permute-start.7 = (bf16[272,128]{1,0:T(8,128)(2,1)S(1)}, bf16[272,128]{1,0:T(8,128)(2,1)S(1)}, u32[]{:S(2)}, u32[]{:S(2)}) collective-permute-start(bf16[272,128]{1,0:T(8,128)(2,1)S(1)} %collective-permute-done.4.refs_3_.refs_5_), channel_id=1, source_target_pairs={{0,1},{1,0},{2,3},{3,2},{4,5},{5,4},{6,7},{7,6},{8,9},{9,8},{10,11... | collective-permute-start | bytes 208904 | tf_op jit(solution)/shard_map/ppermute | solution.py:25
  17.6 1.6 %collective-permute-start.8 = (bf16[272,128]{1,0:T(8,128)(2,1)S(1)}, bf16[272,128]{1,0:T(8,128)(2,1)S(1)}, u32[]{:S(2)}, u32[]{:S(2)}) collective-permute-start(bf16[272,128]{1,0:T(8,128)(2,1)S(1)} %collective-permute-done.5.refs_4_.refs_6_), channel_id=1, source_target_pairs={{0,1},{1,0},{2,3},{3,2},{4,5},{5,4},{6,7},{7,6},{8,9},{9,8},{10,11... | collective-permute-start | bytes 208904 | tf_op jit(solution)/shard_map/ppermute | solution.py:25
  21.7 1.6 %collective-permute-start.11 = (bf16[4,256,128]{2,1,0:T(8,128)(2,1)S(1)}, bf16[4,256,128]{2,1,0:T(8,128)(2,1)S(1)}, u32[]{:S(2)}, u32[]{:S(2)}) collective-permute-start(bf16[4,256,128]{2,1,0:T(8,128)(2,1)S(1)} %get-tuple-element.62), channel_id=1, source_target_pairs={{0,1},{1,0},{2,3},{3,2},{4,5},{5,4},{6,7},{7,6},{8,9},{9,8},{10,11... | collective-permute-start | bytes 786440 | tf_op jit(solution)/shard_map/ppermute | solution.py:25
  21.9 6.0 %collective-permute-start.15 = (bf16[128,512]{1,0:T(8,128)(2,1)S(1)}, bf16[128,512]{1,0:T(8,128)(2,1)S(1)}, u32[]{:S(2)}, u32[]{:S(2)}) collective-permute-start(bf16[128,512]{1,0:T(8,128)(2,1)S(1)} %get-tuple-element.69), channel_id=1, source_target_pairs={{0,8},{8,0},{16,24},{24,16},{1,9},{9,1},{17,25},{25,17},{2,10},{10... | collective-permute-start | bytes 393224 | tf_op jit(solution)/shard_map/ppermute | solution.py:25
  23.3 7.7 %collective-permute-start.12 = (bf16[256,128]{1,0:T(8,128)(2,1)S(1)}, bf16[256,128]{1,0:T(8,128)(2,1)S(1)}, u32[]{:S(2)}, u32[]{:S(2)}) collective-permute-start(bf16[256,128]{1,0:T(8,128)(2,1)S(1)} %get-tuple-element.65), channel_id=1, source_target_pairs={{0,6},{1,5},{2,4},{3,7},{4,2},{5,1},{6,0},{7,3},{8,14},{9,13},{10,... | collective-permute-start | bytes 196616 | tf_op jit(solution)/shard_map/ppermute | solution.py:239
  26.8 5.9 %collective-permute-start.13 = (bf16[256,128]{1,0:T(8,128)(2,1)S(1)}, bf16[256,128]{1,0:T(8,128)(2,1)S(1)}, u32[]{:S(2)}, u32[]{:S(2)}) collective-permute-start(bf16[256,128]{1,0:T(8,128)(2,1)S(1)} %get-tuple-element.66), channel_id=1, source_target_pairs={{0,4},{1,7},{2,6},{3,5},{4,0},{5,3},{6,2},{7,1},{8,12},{9,15},{10,... | collective-permute-start | bytes 196616 | tf_op jit(solution)/shard_map/ppermute | solution.py:239
  26.8 7.9 %collective-permute-start.16 = (bf16[128,512]{1,0:T(8,128)(2,1)S(1)}, bf16[128,512]{1,0:T(8,128)(2,1)S(1)}, u32[]{:S(2)}, u32[]{:S(2)}) collective-permute-start(bf16[128,512]{1,0:T(8,128)(2,1)S(1)} %get-tuple-element.71), channel_id=1, source_target_pairs={{0,16},{8,24},{16,0},{24,8},{1,17},{9,25},{17,1},{25,9},{2,18},{10... | collective-permute-start | bytes 393224 | tf_op jit(solution)/shard_map/ppermute | solution.py:25
  27.8 6.9 %collective-permute-start.17 = (bf16[128,512]{1,0:T(8,128)(2,1)S(1)}, bf16[128,512]{1,0:T(8,128)(2,1)S(1)}, u32[]{:S(2)}, u32[]{:S(2)}) collective-permute-start(bf16[128,512]{1,0:T(8,128)(2,1)S(1)} %get-tuple-element.72), channel_id=1, source_target_pairs={{0,24},{8,16},{16,8},{24,0},{1,25},{9,17},{17,9},{25,1},{2,26},{10... | collective-permute-start | bytes 393224 | tf_op jit(solution)/shard_map/ppermute | solution.py:25
  29.6 5.1 %collective-permute-start.14 = (bf16[256,128]{1,0:T(8,128)(2,1)S(1)}, bf16[256,128]{1,0:T(8,128)(2,1)S(1)}, u32[]{:S(2)}, u32[]{:S(2)}) collective-permute-start(bf16[256,128]{1,0:T(8,128)(2,1)S(1)} %get-tuple-element.67), channel_id=1, source_target_pairs={{0,2},{1,3},{2,0},{3,1},{4,6},{5,7},{6,4},{7,5},{8,10},{9,11},{10,... | collective-permute-start | bytes 196616 | tf_op jit(solution)/shard_map/ppermute | solution.py:25

commit v12 on v11

--- a/solution.py
+++ b/solution.py
@@ -299,7 +299,7 @@
     dkv_own, dkv_near = add_call(dkv_own, dkv_got, 0, [F32, BF])
 
     got = [swapped(dq, "outer", s + 1) for s, dq in enumerate(dqs)]
-    dq_last, got[0] = lax.optimization_barrier((dq_last, got[0]))
+    dq_last, *got = lax.optimization_barrier((dq_last, *got))
     got.append(swapped(dq_last, "outer", nq - 1))
     dkv = []
     for t in range(1, nz // 2):

time: 35.7 us -> 34.8 us (0.975)
  waiting for transfers between devices: 4.51 us -> 3.5 us
    ppermute x14, waiting for transfers between devices: 2.44 us -> 1.34 us  [swapped(): return lax.ppermute(block, axis, pairs)]
where the time goes in v12:
time: 34.8 us; the launch traced here: 34.6 us
  starting transfers between devices  21.7 us (62%)
  Pallas kernels  8.62 us (25%)
  waiting for transfers between devices  3.5 us (10%)
  between operations  0.78 us (2%)
    ppermute x14, starting transfers between devices, swapped(): return lax.ppermute(block, axis, pairs)  14.2 us
    ppermute x4, starting transfers between devices, crossed(): return lax.ppermute(block, 'inner', pairs)  7.48 us
    pallas_call x7, Pallas kernels, blocks_call(): pl.pallas_call(functools.partial(blocks_kernel, plan, rows, heads, scale)...  6.39 us
    ppermute x4, waiting for transfers between devices, crossed(): return lax.ppermute(block, 'inner', pairs)  2.17 us
    ppermute x14, waiting for transfers between devices, swapped(): return lax.ppermute(block, axis, pairs)  1.34 us
    pallas_call x1, Pallas kernels, on_device(): pl.pallas_call(pack_kernel, out_shape=(sds((2 * hr + 32, width), BF), sds...  1.33 us
    pallas_call x1, Pallas kernels, on_device(): pl.pallas_call(functools.partial(final_kernel, rows, heads, scale), out_s...  0.81 us
  transfers between devices with their start and end apart: 18, of which 5 were waited for; matrix products, arithmetic and copies ran while one was open for 0% of the time, Pallas kernels for 16%

profile of v12, /device:TPU:0, one launch (start us, length us, event | category | flops | bytes accessed | tf_op | source)
XLA Modules:
  0.0 34.6 jit_solution(13849128128728624631)
XLA Ops:
  0.6 1.3 %shard_map.94 = (bf16[1056,128]{1,0:T(8,128)(2,1)S(1)}, bf16[272,128]{1,0:T(8,128)(2,1)S(1)}) custom-call(bf16[128,512]{1,0:T(8,128)(2,1)} %q_ref.1, bf16[128,128]{1,0:T(8,128)(2,1)} %k_ref.1, bf16[128,128]{1,0:T(8,128)(2,1)} %v_ref.1, bf16[128,512]{1,0:T(8,128)(2,1)} %o_ref.1, bf16[128,512]{1,0:T(8,128)(2,1)} %g_ref.1, f32[4,128]{1,0:T(4,128)} %lse_ref.1, ...), custom_call_target="tpu_custom_call" | custom-call | flops 1000 | bytes 1000 | tf_op jit(solution)/shard_map/pallas_call | solution.py:251
  2.0 3.0 %collective-permute-start.2 = (bf16[1056,128]{1,0:T(8,128)(2,1)S(1)}, bf16[1056,128]{1,0:T(8,128)(2,1)S(1)}, u32[]{:S(2)}, u32[]{:S(2)}) collective-permute-start(bf16[1056,128]{1,0:T(8,128)(2,1)S(1)} %get-tuple-element.39.refs_0_), channel_id=1, source_target_pairs={{0,8},{8,0},{16,24},{24,16},{1,9},{9,1},{17,25},{25,17},{2,10},{10... | collective-permute-start | bytes 811016 | tf_op jit(solution)/shard_map/ppermute | solution.py:25
  5.0 1.5 %collective-permute-start.3 = (bf16[1056,128]{1,0:T(8,128)(2,1)S(1)}, bf16[1056,128]{1,0:T(8,128)(2,1)S(1)}, u32[]{:S(2)}, u32[]{:S(2)}) collective-permute-start(bf16[1056,128]{1,0:T(8,128)(2,1)S(1)} %get-tuple-element.39.refs_0_), channel_id=1, source_target_pairs={{0,16},{8,24},{16,0},{24,8},{1,17},{9,25},{17,1},{25,9},{2,18},{10... | collective-permute-start | bytes 811016 | tf_op jit(solution)/shard_map/ppermute | solution.py:25
  6.5 0.0 collective-permute-start
  6.5 1.6 %collective-permute-start.1 = (bf16[272,128]{1,0:T(8,128)(2,1)S(1)}, bf16[272,128]{1,0:T(8,128)(2,1)S(1)}, u32[]{:S(2)}, u32[]{:S(2)}) collective-permute-start(bf16[272,128]{1,0:T(8,128)(2,1)S(1)} %get-tuple-element.40.refs_1_.refs_2_), channel_id=1, source_target_pairs={{0,2},{1,3},{2,0},{3,1},{4,6},{5,7},{6,4},{7,5},{8,10},{9,11},{10,... | collective-permute-start | bytes 208904 | tf_op jit(solution)/shard_map/ppermute | solution.py:25
  8.1 2.5 %collective-permute-start.4 = (bf16[272,128]{1,0:T(8,128)(2,1)S(1)}, bf16[272,128]{1,0:T(8,128)(2,1)S(1)}, u32[]{:S(2)}, u32[]{:S(2)}) collective-permute-start(bf16[272,128]{1,0:T(8,128)(2,1)S(1)} %get-tuple-element.40.refs_1_.refs_2_), channel_id=1, source_target_pairs={{0,6},{1,5},{2,4},{3,7},{4,2},{5,1},{6,0},{7,3},{8,14},{9,13},{10,... | collective-permute-start | bytes 208904 | tf_op jit(solution)/shard_map/ppermute | solution.py:239
  10.6 0.0 collective-permute-done.refs_2_.refs_3_
  10.6 1.3 %collective-permute-start.5 = (bf16[272,128]{1,0:T(8,128)(2,1)S(1)}, bf16[272,128]{1,0:T(8,128)(2,1)S(1)}, u32[]{:S(2)}, u32[]{:S(2)}) collective-permute-start(bf16[272,128]{1,0:T(8,128)(2,1)S(1)} %collective-permute-done.refs_2_.refs_3_), channel_id=1, source_target_pairs={{0,6},{1,5},{2,4},{3,7},{4,2},{5,1},{6,0},{7,3},{8,14},{9,13},{10,... | collective-permute-start | bytes 208904 | tf_op jit(solution)/shard_map/ppermute | solution.py:239
  11.9 0.7 %shard_map.95 = (f32[128,512]{1,0:T(8,128)S(1)}, f32[3,256,128]{2,1,0:T(8,128)S(1)}) custom-call(bf16[1056,128]{1,0:T(8,128)(2,1)S(1)} %get-tuple-element.39.refs_0_, bf16[272,128]{1,0:T(8,128)(2,1)S(1)} %get-tuple-element.40.refs_1_.refs_2_, bf16[272,128]{1,0:T(8,128)(2,1)S(1)} %collective-permute-done.refs_2_.refs_3_, ...), custom_call_target="tpu_custom_call" | custom-call | flops 1000 | bytes 1000 | tf_op jit(solution)/shard_map/pallas_call | solution.py:188
  12.6 0.3 collective-permute-done.3.refs_1_.refs_2_
  12.9 1.6 %collective-permute-start.10 = (bf16[544,128]{1,0:T(8,128)(2,1)S(1)}, bf16[544,128]{1,0:T(8,128)(2,1)S(1)}, u32[]{:S(2)}, u32[]{:S(2)}) collective-permute-start(bf16[544,128]{1,0:T(8,128)(2,1)S(1)} %slice.7), channel_id=1, source_target_pairs={{0,16},{8,24},{16,0},{24,8},{1,17},{9,25},{17,1},{25,9},{2,18},{10... | collective-permute-start | bytes 417800 | tf_op jit(solution)/shard_map/ppermute | solution.py:25
  14.5 0.6 %collective-permute-start.9 = (bf16[512,128]{1,0:T(8,128)(2,1)S(1)}, bf16[512,128]{1,0:T(8,128)(2,1)S(1)}, u32[]{:S(2)}, u32[]{:S(2)}) collective-permute-start(bf16[512,128]{1,0:T(8,128)(2,1)S(1)} %slice.6), channel_id=1, source_target_pairs={{0,8},{8,0},{16,24},{24,16},{1,9},{9,1},{17,25},{25,17},{2,10},{10... | collective-permute-start | bytes 393224 | tf_op jit(solution)/shard_map/ppermute | solution.py:25
  15.1 1.3 %shard_map.96 = (f32[128,512]{1,0:T(8,128)S(1)}, f32[128,512]{1,0:T(8,128)S(1)}, f32[3,256,128]{2,1,0:T(8,128)S(1)}) custom-call(bf16[1056,128]{1,0:T(8,128)(2,1)S(1)} %collective-permute-done.2.refs_0_.refs_1_, bf16[1056,128]{1,0:T(8,128)(2,1)S(1)} %collective-permute-done.3.refs_1_.refs_2_, bf16[272,128]{1,0:T(8,128)(2,1)S(1)} %get-tuple-element.40.refs_1_.refs_2_, ...), custom_call_target="tpu_custom_call" | custom-call | flops 1000 | bytes 1000 | tf_op jit(solution)/shard_map/pallas_call | solution.py:188
  16.4 0.4 %collective-permute-done.5.refs_4_.refs_6_ = bf16[272,128]{1,0:T(8,128)(2,1)S(1)} collective-permute-done((bf16[272,128]{1,0:T(8,128)(2,1)S(1)}, bf16[272,128]{1,0:T(8,128)(2,1)S(1)}, u32[]{:S(2)}, u32[]{:S(2)}) %collective-permute-start.5) | collective-permute-done | bytes 69664 | tf_op jit(solution)/shard_map/ppermute | solution.py:239
  16.8 0.8 %collective-permute-start.6 = (bf16[272,128]{1,0:T(8,128)(2,1)S(1)}, bf16[272,128]{1,0:T(8,128)(2,1)S(1)}, u32[]{:S(2)}, u32[]{:S(2)}) collective-permute-start(bf16[272,128]{1,0:T(8,128)(2,1)S(1)} %collective-permute-done.1.refs_3_.refs_4_), channel_id=1, source_target_pairs={{0,1},{1,0},{2,3},{3,2},{4,5},{5,4},{6,7},{7,6},{8,9},{9,8},{10,11... | collective-permute-start | bytes 208904 | tf_op jit(solution)/shard_map/ppermute | solution.py:25
  17.6 0.0 collective-permute-start.7
  17.6 0.5 %collective-permute-start.8 = (bf16[272,128]{1,0:T(8,128)(2,1)S(1)}, bf16[272,128]{1,0:T(8,128)(2,1)S(1)}, u32[]{:S(2)}, u32[]{:S(2)}) collective-permute-start(bf16[272,128]{1,0:T(8,128)(2,1)S(1)} %collective-permute-done.5.refs_4_.refs_6_), channel_id=1, source_target_pairs={{0,1},{1,0},{2,3},{3,2},{4,5},{5,4},{6,7},{7,6},{8,9},{9,8},{10,11... | collective-permute-start | bytes 208904 | tf_op jit(solution)/shard_map/ppermute | solution.py:25
  18.1 1.1 %shard_map.97 = (f32[128,512]{1,0:T(8,128)S(1)}, f32[128,512]{1,0:T(8,128)S(1)}, f32[128,512]{1,0:T(8,128)S(1)}, f32[2,256,128]{2,1,0:T(8,128)S(1)}) custom-call(bf16[1056,128]{1,0:T(8,128)(2,1)S(1)} %get-tuple-element.39.refs_0_, bf16[1056,128]{1,0:T(8,128)(2,1)S(1)} %collective-permute-done.2.refs_0_.refs_1_, ...), custom_call_target="tpu_custom_call" | custom-call | flops 1000 | bytes 1000 | tf_op jit(solution)/shard_map/pallas_call | solution.py:188
  19.2 1.6 %shard_map.98 = (f32[128,512]{1,0:T(8,128)S(1)}, bf16[128,512]{1,0:T(8,128)(2,1)S(1)}, bf16[128,512]{1,0:T(8,128)(2,1)S(1)}, f32[3,256,128]{2,1,0:T(8,128)S(1)}) custom-call(bf16[1056,128]{1,0:T(8,128)(2,1)S(1)} %get-tuple-element.39.refs_0_, bf16[1056,128]{1,0:T(8,128)(2,1)S(1)} %collective-permute-done.2.refs_0_.refs_1_, ...), custom_call_target="tpu_custom_call" | custom-call | flops 1000 | bytes 1000 | tf_op jit(solution)/shard_map/pallas_call | solution.py:188
  20.9 0.8 %shard_map.99 = (f32[128,512]{1,0:T(8,128)S(1)}, bf16[4,256,128]{2,1,0:T(8,128)(2,1)S(1)}) custom-call(bf16[512,128]{1,0:T(8,128)(2,1)S(1)} %collective-permute-done.9.refs_0_, bf16[544,128]{1,0:T(8,128)(2,1)S(1)} %collective-permute-done.10.refs_1_, bf16[272,128]{1,0:T(8,128)(2,1)S(1)} %get-tuple-element.40.refs_1_.refs_2_, ...), custom_call_target="tpu_custom_call" | custom-call | flops 1000 | bytes 1000 | tf_op jit(solution)/shard_map/pallas_call | solution.py:188
  21.7 0.2 collective-permute-start.11
  21.9 0.8 %collective-permute-start.15 = (bf16[128,512]{1,0:T(8,128)(2,1)S(1)}, bf16[128,512]{1,0:T(8,128)(2,1)S(1)}, u32[]{:S(2)}, u32[]{:S(2)}) collective-permute-start(bf16[128,512]{1,0:T(8,128)(2,1)S(1)} %get-tuple-element.70), channel_id=1, source_target_pairs={{0,8},{8,0},{16,24},{24,16},{1,9},{9,1},{17,25},{25,17},{2,10},{10... | collective-permute-start | bytes 393224 | tf_op jit(solution)/shard_map/ppermute | solution.py:25
  22.6 0.5 %collective-permute-start.16 = (bf16[128,512]{1,0:T(8,128)(2,1)S(1)}, bf16[128,512]{1,0:T(8,128)(2,1)S(1)}, u32[]{:S(2)}, u32[]{:S(2)}) collective-permute-start(bf16[128,512]{1,0:T(8,128)(2,1)S(1)} %get-tuple-element.71), channel_id=1, source_target_pairs={{0,16},{8,24},{16,0},{24,8},{1,17},{9,25},{17,1},{25,9},{2,18},{10... | collective-permute-start | bytes 393224 | tf_op jit(solution)/shard_map/ppermute | solution.py:25
  23.1 0.5 %shard_map.100 = (f32[128,512]{1,0:T(8,128)S(1)}, f32[2,256,128]{2,1,0:T(8,128)S(1)}) custom-call(bf16[512,128]{1,0:T(8,128)(2,1)S(1)} %collective-permute-done.9.refs_0_, bf16[544,128]{1,0:T(8,128)(2,1)S(1)} %collective-permute-done.10.refs_1_, bf16[272,128]{1,0:T(8,128)(2,1)S(1)} %get-tuple-element.40.refs_1_.refs_2_, ...), custom_call_target="tpu_custom_call" | custom-call | flops 1000 | bytes 1000 | tf_op jit(solution)/shard_map/pallas_call | solution.py:188
  23.7 3.7 %collective-permute-start.12 = (bf16[256,128]{1,0:T(8,128)(2,1)S(1)}, bf16[256,128]{1,0:T(8,128)(2,1)S(1)}, u32[]{:S(2)}, u32[]{:S(2)}) collective-permute-start(bf16[256,128]{1,0:T(8,128)(2,1)S(1)} %get-tuple-element.66), channel_id=1, source_target_pairs={{0,6},{1,5},{2,4},{3,7},{4,2},{5,1},{6,0},{7,3},{8,14},{9,13},{10,... | collective-permute-start | bytes 196616 | tf_op jit(solution)/shard_map/ppermute | solution.py:239
  27.3 0.5 %shard_map.101 = (bf16[128,512]{1,0:T(8,128)(2,1)S(1)}, f32[2,256,128]{2,1,0:T(8,128)S(1)}) custom-call(bf16[512,128]{1,0:T(8,128)(2,1)S(1)} %collective-permute-done.9.refs_0_, bf16[544,128]{1,0:T(8,128)(2,1)S(1)} %collective-permute-done.10.refs_1_, bf16[272,128]{1,0:T(8,128)(2,1)S(1)} %get-tuple-element.40.refs_1_.refs_2_, ...), custom_call_target="tpu_custom_call" | custom-call | flops 1000 | bytes 1000 | tf_op jit(solution)/shard_map/pallas_call | solution.py:188
  27.8 0.1 collective-permute-done.16.refs_1_
  27.9 1.5 %collective-permute-start.17 = (bf16[128,512]{1,0:T(8,128)(2,1)S(1)}, bf16[128,512]{1,0:T(8,128)(2,1)S(1)}, u32[]{:S(2)}, u32[]{:S(2)}) collective-permute-start(bf16[128,512]{1,0:T(8,128)(2,1)S(1)} %get-tuple-element.74), channel_id=1, source_target_pairs={{0,24},{8,16},{16,8},{24,0},{1,25},{9,17},{17,9},{25,1},{2,26},{10... | collective-permute-start | bytes 393224 | tf_op jit(solution)/shard_map/ppermute | solution.py:25
  29.4 1.6 %collective-permute-start.14 = (bf16[256,128]{1,0:T(8,128)(2,1)S(1)}, bf16[256,128]{1,0:T(8,128)(2,1)S(1)}, u32[]{:S(2)}, u32[]{:S(2)}) collective-permute-start(bf16[256,128]{1,0:T(8,128)(2,1)S(1)} %get-tuple-element.68), channel_id=1, source_target_pairs={{0,2},{1,3},{2,0},{3,1},{4,6},{5,7},{6,4},{7,5},{8,10},{9,11},{10,... | collective-permute-start | bytes 196616 | tf_op jit(solution)/shard_map/ppermute | solution.py:25
  31.0 1.8 %collective-permute-done.13.refs_1_ = bf16[256,128]{1,0:T(8,128)(2,1)S(1)} collective-permute-done((bf16[256,128]{1,0:T(8,128)(2,1)S(1)}, bf16[256,128]{1,0:T(8,128)(2,1)S(1)}, u32[]{:S(2)}, u32[]{:S(2)}) %collective-permute-start.13) | collective-permute-done | bytes 65568 | tf_op jit(solution)/shard_map/ppermute | solution.py:239
  32.9 0.9 %collective-permute-done.17.refs_2_ = bf16[128,512]{1,0:T(8,128)(2,1)S(1)} collective-permute-done((bf16[128,512]{1,0:T(8,128)(2,1)S(1)}, bf16[128,512]{1,0:T(8,128)(2,1)S(1)}, u32[]{:S(2)}, u32[]{:S(2)}) %collective-permute-start.17) | collective-permute-done | bytes 131104 | tf_op jit(solution)/shard_map/ppermute | solution.py:25
  33.8 0.8 %shard_map.105 = (bf16[128,512]{1,0:T(8,128)(2,1)}, bf16[128,128]{1,0:T(8,128)(2,1)}, bf16[128,128]{1,0:T(8,128)(2,1)}) custom-call(f32[128,512]{1,0:T(8,128)S(1)} %get-tuple-element.56.dq_own, f32[256,128]{1,0:T(8,128)S(1)} %shard_map.104.dkv_ref, bf16[256,128]{1,0:T(8,128)(2,1)S(1)} %collective-permute-done.14.near_ref, ...), custom_call_target="tpu_custom_call" | custom-call | flops 1000 | bytes 1000 | tf_op jit(solution)/shard_map/pallas_call | solution.py:319
  (18 shorter events, 0.1 us)
Async XLA Ops:
  2.0 10.6 %collective-permute-start.2 = (bf16[1056,128]{1,0:T(8,128)(2,1)S(1)}, bf16[1056,128]{1,0:T(8,128)(2,1)S(1)}, u32[]{:S(2)}, u32[]{:S(2)}) collective-permute-start(bf16[1056,128]{1,0:T(8,128)(2,1)S(1)} %get-tuple-element.39.refs_0_), channel_id=1, source_target_pairs={{0,8},{8,0},{16,24},{24,16},{1,9},{9,1},{17,25},{25,17},{2,10},{10... | collective-permute-start | bytes 811016 | tf_op jit(solution)/shard_map/ppermute | solution.py:25
  5.0 7.9 %collective-permute-start.3 = (bf16[1056,128]{1,0:T(8,128)(2,1)S(1)}, bf16[1056,128]{1,0:T(8,128)(2,1)S(1)}, u32[]{:S(2)}, u32[]{:S(2)}) collective-permute-start(bf16[1056,128]{1,0:T(8,128)(2,1)S(1)} %get-tuple-element.39.refs_0_), channel_id=1, source_target_pairs={{0,16},{8,24},{16,0},{24,8},{1,17},{9,25},{17,1},{25,9},{2,18},{10... | collective-permute-start | bytes 811016 | tf_op jit(solution)/shard_map/ppermute | solution.py:25
  6.5 4.1 %collective-permute-start = (bf16[272,128]{1,0:T(8,128)(2,1)S(1)}, bf16[272,128]{1,0:T(8,128)(2,1)S(1)}, u32[]{:S(2)}, u32[]{:S(2)}) collective-permute-start(bf16[272,128]{1,0:T(8,128)(2,1)S(1)} %get-tuple-element.40.refs_1_.refs_2_), channel_id=1, source_target_pairs={{0,1},{1,0},{2,3},{3,2},{4,5},{5,4},{6,7},{7,6},{8,9},{9,8},{10,11... | collective-permute-start | bytes 208904 | tf_op jit(solution)/shard_map/ppermute | solution.py:25
  6.5 5.4 %collective-permute-start.1 = (bf16[272,128]{1,0:T(8,128)(2,1)S(1)}, bf16[272,128]{1,0:T(8,128)(2,1)S(1)}, u32[]{:S(2)}, u32[]{:S(2)}) collective-permute-start(bf16[272,128]{1,0:T(8,128)(2,1)S(1)} %get-tuple-element.40.refs_1_.refs_2_), channel_id=1, source_target_pairs={{0,2},{1,3},{2,0},{3,1},{4,6},{5,7},{6,4},{7,5},{8,10},{9,11},{10,... | collective-permute-start | bytes 208904 | tf_op jit(solution)/shard_map/ppermute | solution.py:25
  8.1 8.3 %collective-permute-start.4 = (bf16[272,128]{1,0:T(8,128)(2,1)S(1)}, bf16[272,128]{1,0:T(8,128)(2,1)S(1)}, u32[]{:S(2)}, u32[]{:S(2)}) collective-permute-start(bf16[272,128]{1,0:T(8,128)(2,1)S(1)} %get-tuple-element.40.refs_1_.refs_2_), channel_id=1, source_target_pairs={{0,6},{1,5},{2,4},{3,7},{4,2},{5,1},{6,0},{7,3},{8,14},{9,13},{10,... | collective-permute-start | bytes 208904 | tf_op jit(solution)/shard_map/ppermute | solution.py:239
  10.6 6.2 %collective-permute-start.5 = (bf16[272,128]{1,0:T(8,128)(2,1)S(1)}, bf16[272,128]{1,0:T(8,128)(2,1)S(1)}, u32[]{:S(2)}, u32[]{:S(2)}) collective-permute-start(bf16[272,128]{1,0:T(8,128)(2,1)S(1)} %collective-permute-done.refs_2_.refs_3_), channel_id=1, source_target_pairs={{0,6},{1,5},{2,4},{3,7},{4,2},{5,1},{6,0},{7,3},{8,14},{9,13},{10,... | collective-permute-start | bytes 208904 | tf_op jit(solution)/shard_map/ppermute | solution.py:239
  12.9 7.9 %collective-permute-start.10 = (bf16[544,128]{1,0:T(8,128)(2,1)S(1)}, bf16[544,128]{1,0:T(8,128)(2,1)S(1)}, u32[]{:S(2)}, u32[]{:S(2)}) collective-permute-start(bf16[544,128]{1,0:T(8,128)(2,1)S(1)} %slice.7), channel_id=1, source_target_pairs={{0,16},{8,24},{16,0},{24,8},{1,17},{9,25},{17,1},{25,9},{2,18},{10... | collective-permute-start | bytes 417800 | tf_op jit(solution)/shard_map/ppermute | solution.py:25
  14.5 6.3 %collective-permute-start.9 = (bf16[512,128]{1,0:T(8,128)(2,1)S(1)}, bf16[512,128]{1,0:T(8,128)(2,1)S(1)}, u32[]{:S(2)}, u32[]{:S(2)}) collective-permute-start(bf16[512,128]{1,0:T(8,128)(2,1)S(1)} %slice.6), channel_id=1, source_target_pairs={{0,8},{8,0},{16,24},{24,16},{1,9},{9,1},{17,25},{25,17},{2,10},{10... | collective-permute-start | bytes 393224 | tf_op jit(solution)/shard_map/ppermute | solution.py:25
  16.8 2.4 %collective-permute-start.6 = (bf16[272,128]{1,0:T(8,128)(2,1)S(1)}, bf16[272,128]{1,0:T(8,128)(2,1)S(1)}, u32[]{:S(2)}, u32[]{:S(2)}) collective-permute-start(bf16[272,128]{1,0:T(8,128)(2,1)S(1)} %collective-permute-done.1.refs_3_.refs_4_), channel_id=1, source_target_pairs={{0,1},{1,0},{2,3},{3,2},{4,5},{5,4},{6,7},{7,6},{8,9},{9,8},{10,11... | collective-permute-start | bytes 208904 | tf_op jit(solution)/shard_map/ppermute | solution.py:25
  17.6 1.6 %collective-permute-start.7 = (bf16[272,128]{1,0:T(8,128)(2,1)S(1)}, bf16[272,128]{1,0:T(8,128)(2,1)S(1)}, u32[]{:S(2)}, u32[]{:S(2)}) collective-permute-start(bf16[272,128]{1,0:T(8,128)(2,1)S(1)} %collective-permute-done.4.refs_3_.refs_5_), channel_id=1, source_target_pairs={{0,1},{1,0},{2,3},{3,2},{4,5},{5,4},{6,7},{7,6},{8,9},{9,8},{10,11... | collective-permute-start | bytes 208904 | tf_op jit(solution)/shard_map/ppermute | solution.py:25
  17.6 1.6 %collective-permute-start.8 = (bf16[272,128]{1,0:T(8,128)(2,1)S(1)}, bf16[272,128]{1,0:T(8,128)(2,1)S(1)}, u32[]{:S(2)}, u32[]{:S(2)}) collective-permute-start(bf16[272,128]{1,0:T(8,128)(2,1)S(1)} %collective-permute-done.5.refs_4_.refs_6_), channel_id=1, source_target_pairs={{0,1},{1,0},{2,3},{3,2},{4,5},{5,4},{6,7},{7,6},{8,9},{9,8},{10,11... | collective-permute-start | bytes 208904 | tf_op jit(solution)/shard_map/ppermute | solution.py:25
  21.7 2.0 %collective-permute-start.11 = (bf16[4,256,128]{2,1,0:T(8,128)(2,1)S(1)}, bf16[4,256,128]{2,1,0:T(8,128)(2,1)S(1)}, u32[]{:S(2)}, u32[]{:S(2)}) collective-permute-start(bf16[4,256,128]{2,1,0:T(8,128)(2,1)S(1)} %get-tuple-element.63), channel_id=1, source_target_pairs={{0,1},{1,0},{2,3},{3,2},{4,5},{5,4},{6,7},{7,6},{8,9},{9,8},{10,11... | collective-permute-start | bytes 786440 | tf_op jit(solution)/shard_map/ppermute | solution.py:25
  21.9 6.0 %collective-permute-start.15 = (bf16[128,512]{1,0:T(8,128)(2,1)S(1)}, bf16[128,512]{1,0:T(8,128)(2,1)S(1)}, u32[]{:S(2)}, u32[]{:S(2)}) collective-permute-start(bf16[128,512]{1,0:T(8,128)(2,1)S(1)} %get-tuple-element.70), channel_id=1, source_target_pairs={{0,8},{8,0},{16,24},{24,16},{1,9},{9,1},{17,25},{25,17},{2,10},{10... | collective-permute-start | bytes 393224 | tf_op jit(solution)/shard_map/ppermute | solution.py:25
  22.6 5.3 %collective-permute-start.16 = (bf16[128,512]{1,0:T(8,128)(2,1)S(1)}, bf16[128,512]{1,0:T(8,128)(2,1)S(1)}, u32[]{:S(2)}, u32[]{:S(2)}) collective-permute-start(bf16[128,512]{1,0:T(8,128)(2,1)S(1)} %get-tuple-element.71), channel_id=1, source_target_pairs={{0,16},{8,24},{16,0},{24,8},{1,17},{9,25},{17,1},{25,9},{2,18},{10... | collective-permute-start | bytes 393224 | tf_op jit(solution)/shard_map/ppermute | solution.py:25
  23.7 7.3 %collective-permute-start.12 = (bf16[256,128]{1,0:T(8,128)(2,1)S(1)}, bf16[256,128]{1,0:T(8,128)(2,1)S(1)}, u32[]{:S(2)}, u32[]{:S(2)}) collective-permute-start(bf16[256,128]{1,0:T(8,128)(2,1)S(1)} %get-tuple-element.66), channel_id=1, source_target_pairs={{0,6},{1,5},{2,4},{3,7},{4,2},{5,1},{6,0},{7,3},{8,14},{9,13},{10,... | collective-permute-start | bytes 196616 | tf_op jit(solution)/shard_map/ppermute | solution.py:239
  27.3 5.5 %collective-permute-start.13 = (bf16[256,128]{1,0:T(8,128)(2,1)S(1)}, bf16[256,128]{1,0:T(8,128)(2,1)S(1)}, u32[]{:S(2)}, u32[]{:S(2)}) collective-permute-start(bf16[256,128]{1,0:T(8,128)(2,1)S(1)} %get-tuple-element.67), channel_id=1, source_target_pairs={{0,4},{1,7},{2,6},{3,5},{4,0},{5,3},{6,2},{7,1},{8,12},{9,15},{10,... | collective-permute-start | bytes 196616 | tf_op jit(solution)/shard_map/ppermute | solution.py:239
  27.9 5.9 %collective-permute-start.17 = (bf16[128,512]{1,0:T(8,128)(2,1)S(1)}, bf16[128,512]{1,0:T(8,128)(2,1)S(1)}, u32[]{:S(2)}, u32[]{:S(2)}) collective-permute-start(bf16[128,512]{1,0:T(8,128)(2,1)S(1)} %get-tuple-element.74), channel_id=1, source_target_pairs={{0,24},{8,16},{16,8},{24,0},{1,25},{9,17},{17,9},{25,1},{2,26},{10... | collective-permute-start | bytes 393224 | tf_op jit(solution)/shard_map/ppermute | solution.py:25
  29.4 4.3 %collective-permute-start.14 = (bf16[256,128]{1,0:T(8,128)(2,1)S(1)}, bf16[256,128]{1,0:T(8,128)(2,1)S(1)}, u32[]{:S(2)}, u32[]{:S(2)}) collective-permute-start(bf16[256,128]{1,0:T(8,128)(2,1)S(1)} %get-tuple-element.68), channel_id=1, source_target_pairs={{0,2},{1,3},{2,0},{3,1},{4,6},{5,7},{6,4},{7,5},{8,10},{9,11},{10,... | collective-permute-start | bytes 196616 | tf_op jit(solution)/shard_map/ppermute | solution.py:25

commit v13 on v12

--- a/solution.py
+++ b/solution.py
@@ -270,27 +270,33 @@
     early = [kv, sib, near]
     dq_own, acc = blocks_call([x], early, range(3), *common, F32, F32, diagonal=True)
 
+    near_sib = swapped(near, "inner", 1)
     xs = [swapped(x, "outer", s) for s in range(1, nq - 1)]
-    dq_own, acc, *xs = lax.optimization_barrier((dq_own, acc, *xs))
+    dqs = [dq_own]
+    for s in range(nq - 2):
+        late = (near_sib,) if s == nq - 3 else ()
+        xs[s], acc, *late = lax.optimization_barrier((xs[s], acc, *late))
+        dq, acc = blocks_call([xs[s]], early, range(3), *common, F32, F32, acc=[(acc, n) for n in range(3)])
+        dqs.append(dq)
+    (near_sib,) = late
     halves = [xs[nq - 3][:hr], xs[((nq - 1) ^ (nq // 2)) - 1][hr:]]
     corner = [swapped(halves[0], "outer", 1), swapped(halves[1], "outer", nq // 2)]
-    *dqs, acc = blocks_call(xs, early, range(3), *common, F32, F32, acc=[(acc, n) for n in range(3)])
-
-    *fetched, acc = lax.optimization_barrier((near, *direct, acc))
-    direct = fetched[1:]
-    traded = [swapped(block, "inner", 1) for block in fetched]
+
+    *direct, acc = lax.optimization_barrier((*direct, acc))
+    traded = [swapped(block, "inner", 1) for block in direct]
+    direct = [near_sib, *direct]
     xs = [x, *xs]
     n_d, n_t = len(direct), len(traded)
-    *dqs, acc_d = blocks_call(xs, direct, range(n_d), *common, F32, F32, dq_in=(dq_own, *dqs))
+    *dqs, acc_d = blocks_call(xs, direct, range(n_d), *common, F32, F32, dq_in=dqs)
     types = [F32] + [BF] * (nq - 2)
     dq_own, *dqs, acc_t = blocks_call(xs, traded, range(n_t), *common, F32, types, dq_in=dqs)
 
     arrays = [*early, *direct, *traded]
     accs = [(a, n) for a, count in ((acc, 3), (acc_d, n_d), (acc_t, n_t)) for n in range(count)]
-    theirs, ours = [1, 3 + n_d], [0, 2]
-    for t in range(0, n_d, 2):
-        theirs += [4 + n_d + t, 3 + t + 1]
-        ours += [3 + t, 4 + n_d + t + 1]
+    theirs, ours = [1, 3], [0, 2]
+    for t in range(0, n_t, 2):
+        theirs += [3 + n_d + t, 4 + t + 1]
+        ours += [4 + t, 3 + n_d + t + 1]
     dq_last, dkv_sib = blocks_call([corner], arrays, theirs, *common, BF, F32, acc=accs)
     dkv_got = swapped(dkv_sib, "inner", 1)
     dq_last, dkv_far = blocks_call([corner], arrays, ours[2:], *common, F32, F32, acc=accs, dq_in=[dq_last])

time: 34.8 us -> 37.8 us (1.086)
  waiting for transfers between devices: 3.5 us -> 9.49 us
  starting transfers between devices: 21.7 us -> 18.6 us
    ppermute x14, waiting for transfers between devices: 1.34 us -> 4.9 us  [swapped(): return lax.ppermute(block, axis, pairs)]
    ppermute x4, waiting for transfers between devices: 2.17 us -> 4.6 us  [crossed(): return lax.ppermute(block, 'inner', pairs)]
    ppermute x14, starting transfers between devices: 14.2 us -> 11.8 us  [swapped(): return lax.ppermute(block, axis, pairs)]
    ppermute x4, starting transfers between devices: 7.48 us -> 6.83 us  [crossed(): return lax.ppermute(block, 'inner', pairs)]
    pallas_call x7 -> x8, Pallas kernels: 6.39 us -> 6.47 us  [blocks_call(): pl.pallas_call(functools.partial(blocks_kernel, plan, rows, heads, scale)...]
  transfers between devices with their start and end apart: 18 -> 18, of which waited for: 5 -> 6; matrix products, arithmetic and copies ran while one was open for 0% -> 0% of each run, Pallas kernels for 16% -> 15%
where the time goes in v13:
time: 37.8 us; the launch traced here: 37.7 us
  starting transfers between devices  18.6 us (49%)
  waiting for transfers between devices  9.49 us (25%)
  Pallas kernels  8.69 us (23%)
  between operations  0.81 us (2%)
    ppermute x14, starting transfers between devices, swapped(): return lax.ppermute(block, axis, pairs)  11.8 us
    ppermute x4, starting transfers between devices, crossed(): return lax.ppermute(block, 'inner', pairs)  6.83 us
    pallas_call x8, Pallas kernels, blocks_call(): pl.pallas_call(functools.partial(blocks_kernel, plan, rows, heads, scale)...  6.47 us
    ppermute x14, waiting for transfers between devices, swapped(): return lax.ppermute(block, axis, pairs)  4.9 us
    ppermute x4, waiting for transfers between devices, crossed(): return lax.ppermute(block, 'inner', pairs)  4.6 us
    pallas_call x1, Pallas kernels, on_device(): pl.pallas_call(pack_kernel, out_shape=(sds((2 * hr + 32, width), BF), sds...  1.34 us
    pallas_call x1, Pallas kernels, on_device(): pl.pallas_call(functools.partial(final_kernel, rows, heads, scale), out_s...  0.8 us
  transfers between devices with their start and end apart: 18, of which 6 were waited for; matrix products, arithmetic and copies ran while one was open for 0% of the time, Pallas kernels for 15%

profile of v13, /device:TPU:0, one launch (start us, length us, event | category | flops | bytes accessed | tf_op | source)
XLA Modules:
  0.0 37.7 jit_solution(3060107090562888800)
XLA Ops:
  0.6 1.3 %shard_map.94 = (bf16[1056,128]{1,0:T(8,128)(2,1)S(1)}, bf16[272,128]{1,0:T(8,128)(2,1)S(1)}) custom-call(bf16[128,512]{1,0:T(8,128)(2,1)} %q_ref.1, bf16[128,128]{1,0:T(8,128)(2,1)} %k_ref.1, bf16[128,128]{1,0:T(8,128)(2,1)} %v_ref.1, bf16[128,512]{1,0:T(8,128)(2,1)} %o_ref.1, bf16[128,512]{1,0:T(8,128)(2,1)} %g_ref.1, f32[4,128]{1,0:T(4,128)} %lse_ref.1, ...), custom_call_target="tpu_custom_call" | custom-call | flops 1000 | bytes 1000 | tf_op jit(solution)/shard_map/pallas_call | solution.py:251
  2.0 3.0 %collective-permute-start = (bf16[1056,128]{1,0:T(8,128)(2,1)S(1)}, bf16[1056,128]{1,0:T(8,128)(2,1)S(1)}, u32[]{:S(2)}, u32[]{:S(2)}) collective-permute-start(bf16[1056,128]{1,0:T(8,128)(2,1)S(1)} %get-tuple-element.40.refs_0_), channel_id=1, source_target_pairs={{0,8},{8,0},{16,24},{24,16},{1,9},{9,1},{17,25},{25,17},{2,10},{10... | collective-permute-start | bytes 811016 | tf_op jit(solution)/shard_map/ppermute | solution.py:25
  5.0 1.5 %collective-permute-start.3 = (bf16[1056,128]{1,0:T(8,128)(2,1)S(1)}, bf16[1056,128]{1,0:T(8,128)(2,1)S(1)}, u32[]{:S(2)}, u32[]{:S(2)}) collective-permute-start(bf16[1056,128]{1,0:T(8,128)(2,1)S(1)} %get-tuple-element.40.refs_0_), channel_id=1, source_target_pairs={{0,16},{8,24},{16,0},{24,8},{1,17},{9,25},{17,1},{25,9},{2,18},{10... | collective-permute-start | bytes 811016 | tf_op jit(solution)/shard_map/ppermute | solution.py:25
  6.5 1.6 %collective-permute-start.2 = (bf16[272,128]{1,0:T(8,128)(2,1)S(1)}, bf16[272,128]{1,0:T(8,128)(2,1)S(1)}, u32[]{:S(2)}, u32[]{:S(2)}) collective-permute-start(bf16[272,128]{1,0:T(8,128)(2,1)S(1)} %get-tuple-element.41.refs_1_.refs_2_), channel_id=1, source_target_pairs={{0,2},{1,3},{2,0},{3,1},{4,6},{5,7},{6,4},{7,5},{8,10},{9,11},{10,... | collective-permute-start | bytes 208904 | tf_op jit(solution)/shard_map/ppermute | solution.py:25
  8.1 0.0 collective-permute-start.1
  8.1 2.7 %collective-permute-done.2.refs_3_.refs_4_ = bf16[272,128]{1,0:T(8,128)(2,1)S(1)} collective-permute-done((bf16[272,128]{1,0:T(8,128)(2,1)S(1)}, bf16[272,128]{1,0:T(8,128)(2,1)S(1)}, u32[]{:S(2)}, u32[]{:S(2)}) %collective-permute-start.2) | collective-permute-done | bytes 69664 | tf_op jit(solution)/shard_map/ppermute | solution.py:25
  10.8 0.0 collective-permute-start.4
  10.8 3.6 %collective-permute-start.5 = (bf16[272,128]{1,0:T(8,128)(2,1)S(1)}, bf16[272,128]{1,0:T(8,128)(2,1)S(1)}, u32[]{:S(2)}, u32[]{:S(2)}) collective-permute-start(bf16[272,128]{1,0:T(8,128)(2,1)S(1)} %get-tuple-element.41.refs_1_.refs_2_), channel_id=1, source_target_pairs={{0,6},{1,5},{2,4},{3,7},{4,2},{5,1},{6,0},{7,3},{8,14},{9,13},{10,... | collective-permute-start | bytes 208904 | tf_op jit(solution)/shard_map/ppermute | solution.py:239
  14.4 0.2 collective-permute-start.6
  14.6 0.7 %shard_map.95 = (f32[128,512]{1,0:T(8,128)S(1)}, f32[3,256,128]{2,1,0:T(8,128)S(1)}) custom-call(bf16[1056,128]{1,0:T(8,128)(2,1)S(1)} %get-tuple-element.40.refs_0_, bf16[272,128]{1,0:T(8,128)(2,1)S(1)} %get-tuple-element.41.refs_1_.refs_2_, bf16[272,128]{1,0:T(8,128)(2,1)S(1)} %collective-permute-done.1.refs_2_.refs_3_, ...), custom_call_target="tpu_custom_call" | custom-call | flops 1000 | bytes 1000 | tf_op jit(solution)/shard_map/pallas_call | solution.py:188
  15.3 0.6 %collective-permute-start.10 = (bf16[544,128]{1,0:T(8,128)(2,1)S(1)}, bf16[544,128]{1,0:T(8,128)(2,1)S(1)}, u32[]{:S(2)}, u32[]{:S(2)}) collective-permute-start(bf16[544,128]{1,0:T(8,128)(2,1)S(1)} %slice.7), channel_id=1, source_target_pairs={{0,16},{8,24},{16,0},{24,8},{1,17},{9,25},{17,1},{25,9},{2,18},{10... | collective-permute-start | bytes 417800 | tf_op jit(solution)/shard_map/ppermute | solution.py:25
  15.9 0.7 %shard_map.96 = (f32[128,512]{1,0:T(8,128)S(1)}, f32[3,256,128]{2,1,0:T(8,128)S(1)}) custom-call(bf16[1056,128]{1,0:T(8,128)(2,1)S(1)} %collective-permute-done.refs_0_.refs_1_, bf16[272,128]{1,0:T(8,128)(2,1)S(1)} %get-tuple-element.41.refs_1_.refs_2_, bf16[272,128]{1,0:T(8,128)(2,1)S(1)} %collective-permute-done.1.refs_2_.refs_3_, ...), custom_call_target="tpu_custom_call" | custom-call | flops 1000 | bytes 1000 | tf_op jit(solution)/shard_map/pallas_call | solution.py:188
  16.6 0.5 %collective-permute-start.9 = (bf16[512,128]{1,0:T(8,128)(2,1)S(1)}, bf16[512,128]{1,0:T(8,128)(2,1)S(1)}, u32[]{:S(2)}, u32[]{:S(2)}) collective-permute-start(bf16[512,128]{1,0:T(8,128)(2,1)S(1)} %slice.6), channel_id=1, source_target_pairs={{0,8},{8,0},{16,24},{24,16},{1,9},{9,1},{17,25},{25,17},{2,10},{10... | collective-permute-start | bytes 393224 | tf_op jit(solution)/shard_map/ppermute | solution.py:25
  17.1 0.7 %shard_map.97 = (f32[128,512]{1,0:T(8,128)S(1)}, f32[3,256,128]{2,1,0:T(8,128)S(1)}) custom-call(bf16[1056,128]{1,0:T(8,128)(2,1)S(1)} %collective-permute-done.3.refs_0_.refs_2_, bf16[272,128]{1,0:T(8,128)(2,1)S(1)} %get-tuple-element.41.refs_1_.refs_2_, bf16[272,128]{1,0:T(8,128)(2,1)S(1)} %collective-permute-done.1.refs_2_.refs_3_, ...), custom_call_target="tpu_custom_call" | custom-call | flops 1000 | bytes 1000 | tf_op jit(solution)/shard_map/pallas_call | solution.py:188
  17.8 2.9 %collective-permute-done.6.refs_5_.refs_7_ = bf16[272,128]{1,0:T(8,128)(2,1)S(1)} collective-permute-done((bf16[272,128]{1,0:T(8,128)(2,1)S(1)}, bf16[272,128]{1,0:T(8,128)(2,1)S(1)}, u32[]{:S(2)}, u32[]{:S(2)}) %collective-permute-start.6) | collective-permute-done | bytes 69664 | tf_op jit(solution)/shard_map/ppermute | solution.py:239
  20.6 0.5 %collective-permute-start.8 = (bf16[272,128]{1,0:T(8,128)(2,1)S(1)}, bf16[272,128]{1,0:T(8,128)(2,1)S(1)}, u32[]{:S(2)}, u32[]{:S(2)}) collective-permute-start(bf16[272,128]{1,0:T(8,128)(2,1)S(1)} %collective-permute-done.6.refs_5_.refs_7_), channel_id=1, source_target_pairs={{0,1},{1,0},{2,3},{3,2},{4,5},{5,4},{6,7},{7,6},{8,9},{9,8},{10,11... | collective-permute-start | bytes 208904 | tf_op jit(solution)/shard_map/ppermute | solution.py:25
  21.1 1.6 %shard_map.98 = (f32[128,512]{1,0:T(8,128)S(1)}, f32[128,512]{1,0:T(8,128)S(1)}, f32[128,512]{1,0:T(8,128)S(1)}, f32[3,256,128]{2,1,0:T(8,128)S(1)}) custom-call(bf16[1056,128]{1,0:T(8,128)(2,1)S(1)} %get-tuple-element.40.refs_0_, bf16[1056,128]{1,0:T(8,128)(2,1)S(1)} %collective-permute-done.refs_0_.refs_1_, ...), custom_call_target="tpu_custom_call" | custom-call | flops 1000 | bytes 1000 | tf_op jit(solution)/shard_map/pallas_call | solution.py:188
  22.8 1.1 %shard_map.99 = (f32[128,512]{1,0:T(8,128)S(1)}, bf16[128,512]{1,0:T(8,128)(2,1)S(1)}, bf16[128,512]{1,0:T(8,128)(2,1)S(1)}, f32[2,256,128]{2,1,0:T(8,128)S(1)}) custom-call(bf16[1056,128]{1,0:T(8,128)(2,1)S(1)} %get-tuple-element.40.refs_0_, bf16[1056,128]{1,0:T(8,128)(2,1)S(1)} %collective-permute-done.refs_0_.refs_1_, ...), custom_call_target="tpu_custom_call" | custom-call | flops 1000 | bytes 1000 | tf_op jit(solution)/shard_map/pallas_call | solution.py:188
  23.9 0.8 %shard_map.100 = (f32[128,512]{1,0:T(8,128)S(1)}, bf16[4,256,128]{2,1,0:T(8,128)(2,1)S(1)}) custom-call(bf16[512,128]{1,0:T(8,128)(2,1)S(1)} %collective-permute-done.9.refs_0_, bf16[544,128]{1,0:T(8,128)(2,1)S(1)} %collective-permute-done.10.refs_1_, bf16[272,128]{1,0:T(8,128)(2,1)S(1)} %get-tuple-element.41.refs_1_.refs_2_, ...), custom_call_target="tpu_custom_call" | custom-call | flops 1000 | bytes 1000 | tf_op jit(solution)/shard_map/pallas_call | solution.py:188
  24.7 0.1 collective-permute-start.11
  24.8 0.6 %collective-permute-start.15 = (bf16[128,512]{1,0:T(8,128)(2,1)S(1)}, bf16[128,512]{1,0:T(8,128)(2,1)S(1)}, u32[]{:S(2)}, u32[]{:S(2)}) collective-permute-start(bf16[128,512]{1,0:T(8,128)(2,1)S(1)} %get-tuple-element.72), channel_id=1, source_target_pairs={{0,8},{8,0},{16,24},{24,16},{1,9},{9,1},{17,25},{25,17},{2,10},{10... | collective-permute-start | bytes 393224 | tf_op jit(solution)/shard_map/ppermute | solution.py:25
  25.4 0.5 %collective-permute-start.16 = (bf16[128,512]{1,0:T(8,128)(2,1)S(1)}, bf16[128,512]{1,0:T(8,128)(2,1)S(1)}, u32[]{:S(2)}, u32[]{:S(2)}) collective-permute-start(bf16[128,512]{1,0:T(8,128)(2,1)S(1)} %get-tuple-element.73), channel_id=1, source_target_pairs={{0,16},{8,24},{16,0},{24,8},{1,17},{9,25},{17,1},{25,9},{2,18},{10... | collective-permute-start | bytes 393224 | tf_op jit(solution)/shard_map/ppermute | solution.py:25
  25.9 0.5 %shard_map.101 = (f32[128,512]{1,0:T(8,128)S(1)}, f32[2,256,128]{2,1,0:T(8,128)S(1)}) custom-call(bf16[512,128]{1,0:T(8,128)(2,1)S(1)} %collective-permute-done.9.refs_0_, bf16[544,128]{1,0:T(8,128)(2,1)S(1)} %collective-permute-done.10.refs_1_, bf16[272,128]{1,0:T(8,128)(2,1)S(1)} %get-tuple-element.41.refs_1_.refs_2_, ...), custom_call_target="tpu_custom_call" | custom-call | flops 1000 | bytes 1000 | tf_op jit(solution)/shard_map/pallas_call | solution.py:188
  26.4 3.0 %collective-permute-start.12 = (bf16[256,128]{1,0:T(8,128)(2,1)S(1)}, bf16[256,128]{1,0:T(8,128)(2,1)S(1)}, u32[]{:S(2)}, u32[]{:S(2)}) collective-permute-start(bf16[256,128]{1,0:T(8,128)(2,1)S(1)} %get-tuple-element.68), channel_id=1, source_target_pairs={{0,6},{1,5},{2,4},{3,7},{4,2},{5,1},{6,0},{7,3},{8,14},{9,13},{10,... | collective-permute-start | bytes 196616 | tf_op jit(solution)/shard_map/ppermute | solution.py:239
  29.5 0.5 %shard_map.102 = (bf16[128,512]{1,0:T(8,128)(2,1)S(1)}, f32[2,256,128]{2,1,0:T(8,128)S(1)}) custom-call(bf16[512,128]{1,0:T(8,128)(2,1)S(1)} %collective-permute-done.9.refs_0_, bf16[544,128]{1,0:T(8,128)(2,1)S(1)} %collective-permute-done.10.refs_1_, bf16[272,128]{1,0:T(8,128)(2,1)S(1)} %get-tuple-element.41.refs_1_.refs_2_, ...), custom_call_target="tpu_custom_call" | custom-call | flops 1000 | bytes 1000 | tf_op jit(solution)/shard_map/pallas_call | solution.py:188
  29.9 0.8 %collective-permute-done.15.refs_0_ = bf16[128,512]{1,0:T(8,128)(2,1)S(1)} collective-permute-done((bf16[128,512]{1,0:T(8,128)(2,1)S(1)}, bf16[128,512]{1,0:T(8,128)(2,1)S(1)}, u32[]{:S(2)}, u32[]{:S(2)}) %collective-permute-start.15) | collective-permute-done | bytes 131104 | tf_op jit(solution)/shard_map/ppermute | solution.py:25
  30.7 0.3 collective-permute-done.16.refs_1_
  31.0 1.5 %collective-permute-start.17 = (bf16[128,512]{1,0:T(8,128)(2,1)S(1)}, bf16[128,512]{1,0:T(8,128)(2,1)S(1)}, u32[]{:S(2)}, u32[]{:S(2)}) collective-permute-start(bf16[128,512]{1,0:T(8,128)(2,1)S(1)} %get-tuple-element.76), channel_id=1, source_target_pairs={{0,24},{8,16},{16,8},{24,0},{1,25},{9,17},{17,9},{25,1},{2,26},{10... | collective-permute-start | bytes 393224 | tf_op jit(solution)/shard_map/ppermute | solution.py:25
  32.5 1.5 %collective-permute-start.14 = (bf16[256,128]{1,0:T(8,128)(2,1)S(1)}, bf16[256,128]{1,0:T(8,128)(2,1)S(1)}, u32[]{:S(2)}, u32[]{:S(2)}) collective-permute-start(bf16[256,128]{1,0:T(8,128)(2,1)S(1)} %get-tuple-element.70), channel_id=1, source_target_pairs={{0,2},{1,3},{2,0},{3,1},{4,6},{5,7},{6,4},{7,5},{8,10},{9,11},{10,... | collective-permute-start | bytes 196616 | tf_op jit(solution)/shard_map/ppermute | solution.py:25
  34.0 1.7 %collective-permute-done.13.refs_1_ = bf16[256,128]{1,0:T(8,128)(2,1)S(1)} collective-permute-done((bf16[256,128]{1,0:T(8,128)(2,1)S(1)}, bf16[256,128]{1,0:T(8,128)(2,1)S(1)}, u32[]{:S(2)}, u32[]{:S(2)}) %collective-permute-start.13) | collective-permute-done | bytes 65568 | tf_op jit(solution)/shard_map/ppermute | solution.py:239
  35.8 1.1 %collective-permute-done.17.refs_2_ = bf16[128,512]{1,0:T(8,128)(2,1)S(1)} collective-permute-done((bf16[128,512]{1,0:T(8,128)(2,1)S(1)}, bf16[128,512]{1,0:T(8,128)(2,1)S(1)}, u32[]{:S(2)}, u32[]{:S(2)}) %collective-permute-start.17) | collective-permute-done | bytes 131104 | tf_op jit(solution)/shard_map/ppermute | solution.py:25
  36.8 0.8 %shard_map.106 = (bf16[128,512]{1,0:T(8,128)(2,1)}, bf16[128,128]{1,0:T(8,128)(2,1)}, bf16[128,128]{1,0:T(8,128)(2,1)}) custom-call(f32[128,512]{1,0:T(8,128)S(1)} %get-tuple-element.58.dq_own, f32[256,128]{1,0:T(8,128)S(1)} %shard_map.105.dkv_ref, bf16[256,128]{1,0:T(8,128)(2,1)S(1)} %collective-permute-done.14.near_ref, ...), custom_call_target="tpu_custom_call" | custom-call | flops 1000 | bytes 1000 | tf_op jit(solution)/shard_map/pallas_call | solution.py:325
  (19 shorter events, 0.1 us)
Async XLA Ops:
  2.0 13.3 %collective-permute-start = (bf16[1056,128]{1,0:T(8,128)(2,1)S(1)}, bf16[1056,128]{1,0:T(8,128)(2,1)S(1)}, u32[]{:S(2)}, u32[]{:S(2)}) collective-permute-start(bf16[1056,128]{1,0:T(8,128)(2,1)S(1)} %get-tuple-element.40.refs_0_), channel_id=1, source_target_pairs={{0,8},{8,0},{16,24},{24,16},{1,9},{9,1},{17,25},{25,17},{2,10},{10... | collective-permute-start | bytes 811016 | tf_op jit(solution)/shard_map/ppermute | solution.py:25
  5.0 11.6 %collective-permute-start.3 = (bf16[1056,128]{1,0:T(8,128)(2,1)S(1)}, bf16[1056,128]{1,0:T(8,128)(2,1)S(1)}, u32[]{:S(2)}, u32[]{:S(2)}) collective-permute-start(bf16[1056,128]{1,0:T(8,128)(2,1)S(1)} %get-tuple-element.40.refs_0_), channel_id=1, source_target_pairs={{0,16},{8,24},{16,0},{24,8},{1,17},{9,25},{17,1},{25,9},{2,18},{10... | collective-permute-start | bytes 811016 | tf_op jit(solution)/shard_map/ppermute | solution.py:25
  6.5 4.3 %collective-permute-start.2 = (bf16[272,128]{1,0:T(8,128)(2,1)S(1)}, bf16[272,128]{1,0:T(8,128)(2,1)S(1)}, u32[]{:S(2)}, u32[]{:S(2)}) collective-permute-start(bf16[272,128]{1,0:T(8,128)(2,1)S(1)} %get-tuple-element.41.refs_1_.refs_2_), channel_id=1, source_target_pairs={{0,2},{1,3},{2,0},{3,1},{4,6},{5,7},{6,4},{7,5},{8,10},{9,11},{10,... | collective-permute-start | bytes 208904 | tf_op jit(solution)/shard_map/ppermute | solution.py:25
  8.1 6.3 %collective-permute-start.1 = (bf16[272,128]{1,0:T(8,128)(2,1)S(1)}, bf16[272,128]{1,0:T(8,128)(2,1)S(1)}, u32[]{:S(2)}, u32[]{:S(2)}) collective-permute-start(bf16[272,128]{1,0:T(8,128)(2,1)S(1)} %get-tuple-element.41.refs_1_.refs_2_), channel_id=1, source_target_pairs={{0,1},{1,0},{2,3},{3,2},{4,5},{5,4},{6,7},{7,6},{8,9},{9,8},{10,11... | collective-permute-start | bytes 208904 | tf_op jit(solution)/shard_map/ppermute | solution.py:25
  10.8 5.8 %collective-permute-start.4 = (bf16[272,128]{1,0:T(8,128)(2,1)S(1)}, bf16[272,128]{1,0:T(8,128)(2,1)S(1)}, u32[]{:S(2)}, u32[]{:S(2)}) collective-permute-start(bf16[272,128]{1,0:T(8,128)(2,1)S(1)} %collective-permute-done.2.refs_3_.refs_4_), channel_id=1, source_target_pairs={{0,1},{1,0},{2,3},{3,2},{4,5},{5,4},{6,7},{7,6},{8,9},{9,8},{10,11... | collective-permute-start | bytes 208904 | tf_op jit(solution)/shard_map/ppermute | solution.py:25
  10.8 6.9 %collective-permute-start.5 = (bf16[272,128]{1,0:T(8,128)(2,1)S(1)}, bf16[272,128]{1,0:T(8,128)(2,1)S(1)}, u32[]{:S(2)}, u32[]{:S(2)}) collective-permute-start(bf16[272,128]{1,0:T(8,128)(2,1)S(1)} %get-tuple-element.41.refs_1_.refs_2_), channel_id=1, source_target_pairs={{0,6},{1,5},{2,4},{3,7},{4,2},{5,1},{6,0},{7,3},{8,14},{9,13},{10,... | collective-permute-start | bytes 208904 | tf_op jit(solution)/shard_map/ppermute | solution.py:239
  14.4 6.2 %collective-permute-start.6 = (bf16[272,128]{1,0:T(8,128)(2,1)S(1)}, bf16[272,128]{1,0:T(8,128)(2,1)S(1)}, u32[]{:S(2)}, u32[]{:S(2)}) collective-permute-start(bf16[272,128]{1,0:T(8,128)(2,1)S(1)} %collective-permute-done.1.refs_2_.refs_3_), channel_id=1, source_target_pairs={{0,6},{1,5},{2,4},{3,7},{4,2},{5,1},{6,0},{7,3},{8,14},{9,13},{10,... | collective-permute-start | bytes 208904 | tf_op jit(solution)/shard_map/ppermute | solution.py:239
  15.3 8.6 %collective-permute-start.10 = (bf16[544,128]{1,0:T(8,128)(2,1)S(1)}, bf16[544,128]{1,0:T(8,128)(2,1)S(1)}, u32[]{:S(2)}, u32[]{:S(2)}) collective-permute-start(bf16[544,128]{1,0:T(8,128)(2,1)S(1)} %slice.7), channel_id=1, source_target_pairs={{0,16},{8,24},{16,0},{24,8},{1,17},{9,25},{17,1},{25,9},{2,18},{10... | collective-permute-start | bytes 417800 | tf_op jit(solution)/shard_map/ppermute | solution.py:25
  16.6 7.3 %collective-permute-start.9 = (bf16[512,128]{1,0:T(8,128)(2,1)S(1)}, bf16[512,128]{1,0:T(8,128)(2,1)S(1)}, u32[]{:S(2)}, u32[]{:S(2)}) collective-permute-start(bf16[512,128]{1,0:T(8,128)(2,1)S(1)} %slice.6), channel_id=1, source_target_pairs={{0,8},{8,0},{16,24},{24,16},{1,9},{9,1},{17,25},{25,17},{2,10},{10... | collective-permute-start | bytes 393224 | tf_op jit(solution)/shard_map/ppermute | solution.py:25
  20.6 2.1 %collective-permute-start.7 = (bf16[272,128]{1,0:T(8,128)(2,1)S(1)}, bf16[272,128]{1,0:T(8,128)(2,1)S(1)}, u32[]{:S(2)}, u32[]{:S(2)}) collective-permute-start(bf16[272,128]{1,0:T(8,128)(2,1)S(1)} %collective-permute-done.5.refs_4_.refs_6_), channel_id=1, source_target_pairs={{0,1},{1,0},{2,3},{3,2},{4,5},{5,4},{6,7},{7,6},{8,9},{9,8},{10,11... | collective-permute-start | bytes 208904 | tf_op jit(solution)/shard_map/ppermute | solution.py:25
  20.6 2.1 %collective-permute-start.8 = (bf16[272,128]{1,0:T(8,128)(2,1)S(1)}, bf16[272,128]{1,0:T(8,128)(2,1)S(1)}, u32[]{:S(2)}, u32[]{:S(2)}) collective-permute-start(bf16[272,128]{1,0:T(8,128)(2,1)S(1)} %collective-permute-done.6.refs_5_.refs_7_), channel_id=1, source_target_pairs={{0,1},{1,0},{2,3},{3,2},{4,5},{5,4},{6,7},{7,6},{8,9},{9,8},{10,11... | collective-permute-start | bytes 208904 | tf_op jit(solution)/shard_map/ppermute | solution.py:25
  24.7 1.7 %collective-permute-start.11 = (bf16[4,256,128]{2,1,0:T(8,128)(2,1)S(1)}, bf16[4,256,128]{2,1,0:T(8,128)(2,1)S(1)}, u32[]{:S(2)}, u32[]{:S(2)}) collective-permute-start(bf16[4,256,128]{2,1,0:T(8,128)(2,1)S(1)} %get-tuple-element.65), channel_id=1, source_target_pairs={{0,1},{1,0},{2,3},{3,2},{4,5},{5,4},{6,7},{7,6},{8,9},{9,8},{10,11... | collective-permute-start | bytes 786440 | tf_op jit(solution)/shard_map/ppermute | solution.py:25
  24.8 5.9 %collective-permute-start.15 = (bf16[128,512]{1,0:T(8,128)(2,1)S(1)}, bf16[128,512]{1,0:T(8,128)(2,1)S(1)}, u32[]{:S(2)}, u32[]{:S(2)}) collective-permute-start(bf16[128,512]{1,0:T(8,128)(2,1)S(1)} %get-tuple-element.72), channel_id=1, source_target_pairs={{0,8},{8,0},{16,24},{24,16},{1,9},{9,1},{17,25},{25,17},{2,10},{10... | collective-permute-start | bytes 393224 | tf_op jit(solution)/shard_map/ppermute | solution.py:25
  25.4 5.6 %collective-permute-start.16 = (bf16[128,512]{1,0:T(8,128)(2,1)S(1)}, bf16[128,512]{1,0:T(8,128)(2,1)S(1)}, u32[]{:S(2)}, u32[]{:S(2)}) collective-permute-start(bf16[128,512]{1,0:T(8,128)(2,1)S(1)} %get-tuple-element.73), channel_id=1, source_target_pairs={{0,16},{8,24},{16,0},{24,8},{1,17},{9,25},{17,1},{25,9},{2,18},{10... | collective-permute-start | bytes 393224 | tf_op jit(solution)/shard_map/ppermute | solution.py:25
  26.4 7.6 %collective-permute-start.12 = (bf16[256,128]{1,0:T(8,128)(2,1)S(1)}, bf16[256,128]{1,0:T(8,128)(2,1)S(1)}, u32[]{:S(2)}, u32[]{:S(2)}) collective-permute-start(bf16[256,128]{1,0:T(8,128)(2,1)S(1)} %get-tuple-element.68), channel_id=1, source_target_pairs={{0,6},{1,5},{2,4},{3,7},{4,2},{5,1},{6,0},{7,3},{8,14},{9,13},{10,... | collective-permute-start | bytes 196616 | tf_op jit(solution)/shard_map/ppermute | solution.py:239
  29.4 6.3 %collective-permute-start.13 = (bf16[256,128]{1,0:T(8,128)(2,1)S(1)}, bf16[256,128]{1,0:T(8,128)(2,1)S(1)}, u32[]{:S(2)}, u32[]{:S(2)}) collective-permute-start(bf16[256,128]{1,0:T(8,128)(2,1)S(1)} %get-tuple-element.69), channel_id=1, source_target_pairs={{0,4},{1,7},{2,6},{3,5},{4,0},{5,3},{6,2},{7,1},{8,12},{9,15},{10,... | collective-permute-start | bytes 196616 | tf_op jit(solution)/shard_map/ppermute | solution.py:239
  31.0 5.9 %collective-permute-start.17 = (bf16[128,512]{1,0:T(8,128)(2,1)S(1)}, bf16[128,512]{1,0:T(8,128)(2,1)S(1)}, u32[]{:S(2)}, u32[]{:S(2)}) collective-permute-start(bf16[128,512]{1,0:T(8,128)(2,1)S(1)} %get-tuple-element.76), channel_id=1, source_target_pairs={{0,24},{8,16},{16,8},{24,0},{1,25},{9,17},{17,9},{25,1},{2,26},{10... | collective-permute-start | bytes 393224 | tf_op jit(solution)/shard_map/ppermute | solution.py:25
  32.5 4.4 %collective-permute-start.14 = (bf16[256,128]{1,0:T(8,128)(2,1)S(1)}, bf16[256,128]{1,0:T(8,128)(2,1)S(1)}, u32[]{:S(2)}, u32[]{:S(2)}) collective-permute-start(bf16[256,128]{1,0:T(8,128)(2,1)S(1)} %get-tuple-element.70), channel_id=1, source_target_pairs={{0,2},{1,3},{2,0},{3,1},{4,6},{5,7},{6,4},{7,5},{8,10},{9,11},{10,... | collective-permute-start | bytes 196616 | tf_op jit(solution)/shard_map/ppermute | solution.py:25

commit v14 on v12

--- a/solution.py
+++ b/solution.py
@@ -271,17 +271,20 @@
     dq_own, acc = blocks_call([x], early, range(3), *common, F32, F32, diagonal=True)
 
     xs = [swapped(x, "outer", s) for s in range(1, nq - 1)]
-    dq_own, acc, *xs = lax.optimization_barrier((dq_own, acc, *xs))
+    dqs = [dq_own]
+    for s in range(nq - 2):
+        xs[s], acc = lax.optimization_barrier((xs[s], acc))
+        dq, acc = blocks_call([xs[s]], early, range(3), *common, F32, F32, acc=[(acc, n) for n in range(3)])
+        dqs.append(dq)
     halves = [xs[nq - 3][:hr], xs[((nq - 1) ^ (nq // 2)) - 1][hr:]]
     corner = [swapped(halves[0], "outer", 1), swapped(halves[1], "outer", nq // 2)]
-    *dqs, acc = blocks_call(xs, early, range(3), *common, F32, F32, acc=[(acc, n) for n in range(3)])
 
     *fetched, acc = lax.optimization_barrier((near, *direct, acc))
     direct = fetched[1:]
     traded = [swapped(block, "inner", 1) for block in fetched]
     xs = [x, *xs]
     n_d, n_t = len(direct), len(traded)
-    *dqs, acc_d = blocks_call(xs, direct, range(n_d), *common, F32, F32, dq_in=(dq_own, *dqs))
+    *dqs, acc_d = blocks_call(xs, direct, range(n_d), *common, F32, F32, dq_in=dqs)
     types = [F32] + [BF] * (nq - 2)
     dq_own, *dqs, acc_t = blocks_call(xs, traded, range(n_t), *common, F32, types, dq_in=dqs)
 

time: 34.8 us -> 34.8 us (level)
    pallas_call x7 -> x8, Pallas kernels: 6.39 us -> 6.46 us  [blocks_call(): pl.pallas_call(functools.partial(blocks_kernel, plan, rows, heads, scale)...]
  transfers between devices with their start and end apart: 18 -> 18, of which waited for: 5 -> 4; matrix products, arithmetic and copies ran while one was open for 0% -> 0% of each run, Pallas kernels for 16% -> 17%
where the time goes in v14:
time: 34.8 us; the launch traced here: 34.6 us
  starting transfers between devices  21.7 us (62%)
  Pallas kernels  8.68 us (25%)
  waiting for transfers between devices  3.41 us (10%)
  between operations  0.8 us (2%)
    ppermute x14, starting transfers between devices, swapped(): return lax.ppermute(block, axis, pairs)  14 us
    ppermute x4, starting transfers between devices, crossed(): return lax.ppermute(block, 'inner', pairs)  7.64 us
    pallas_call x8, Pallas kernels, blocks_call(): pl.pallas_call(functools.partial(blocks_kernel, plan, rows, heads, scale)...  6.46 us
    ppermute x4, waiting for transfers between devices, crossed(): return lax.ppermute(block, 'inner', pairs)  2.23 us
    pallas_call x1, Pallas kernels, on_device(): pl.pallas_call(pack_kernel, out_shape=(sds((2 * hr + 32, width), BF), sds...  1.34 us
    ppermute x14, waiting for transfers between devices, swapped(): return lax.ppermute(block, axis, pairs)  1.18 us
    pallas_call x1, Pallas kernels, on_device(): pl.pallas_call(functools.partial(final_kernel, rows, heads, scale), out_s...  0.8 us
  transfers between devices with their start and end apart: 18, of which 4 were waited for; matrix products, arithmetic and copies ran while one was open for 0% of the time, Pallas kernels for 17%

profile of v14, /device:TPU:0, one launch (start us, length us, event | category | flops | bytes accessed | tf_op | source)
XLA Modules:
  0.0 34.6 jit_solution(5818543271293599633)
XLA Ops:
  0.6 1.3 %shard_map.94 = (bf16[1056,128]{1,0:T(8,128)(2,1)S(1)}, bf16[272,128]{1,0:T(8,128)(2,1)S(1)}) custom-call(bf16[128,512]{1,0:T(8,128)(2,1)} %q_ref.1, bf16[128,128]{1,0:T(8,128)(2,1)} %k_ref.1, bf16[128,128]{1,0:T(8,128)(2,1)} %v_ref.1, bf16[128,512]{1,0:T(8,128)(2,1)} %o_ref.1, bf16[128,512]{1,0:T(8,128)(2,1)} %g_ref.1, f32[4,128]{1,0:T(4,128)} %lse_ref.1, ...), custom_call_target="tpu_custom_call" | custom-call | flops 1000 | bytes 1000 | tf_op jit(solution)/shard_map/pallas_call | solution.py:251
  2.0 3.0 %collective-permute-start = (bf16[1056,128]{1,0:T(8,128)(2,1)S(1)}, bf16[1056,128]{1,0:T(8,128)(2,1)S(1)}, u32[]{:S(2)}, u32[]{:S(2)}) collective-permute-start(bf16[1056,128]{1,0:T(8,128)(2,1)S(1)} %get-tuple-element.40.refs_0_), channel_id=1, source_target_pairs={{0,8},{8,0},{16,24},{24,16},{1,9},{9,1},{17,25},{25,17},{2,10},{10... | collective-permute-start | bytes 811016 | tf_op jit(solution)/shard_map/ppermute | solution.py:25
  5.0 1.5 %collective-permute-start.3 = (bf16[1056,128]{1,0:T(8,128)(2,1)S(1)}, bf16[1056,128]{1,0:T(8,128)(2,1)S(1)}, u32[]{:S(2)}, u32[]{:S(2)}) collective-permute-start(bf16[1056,128]{1,0:T(8,128)(2,1)S(1)} %get-tuple-element.40.refs_0_), channel_id=1, source_target_pairs={{0,16},{8,24},{16,0},{24,8},{1,17},{9,25},{17,1},{25,9},{2,18},{10... | collective-permute-start | bytes 811016 | tf_op jit(solution)/shard_map/ppermute | solution.py:25
  6.5 1.6 %collective-permute-start.2 = (bf16[272,128]{1,0:T(8,128)(2,1)S(1)}, bf16[272,128]{1,0:T(8,128)(2,1)S(1)}, u32[]{:S(2)}, u32[]{:S(2)}) collective-permute-start(bf16[272,128]{1,0:T(8,128)(2,1)S(1)} %get-tuple-element.41.refs_1_.refs_2_), channel_id=1, source_target_pairs={{0,2},{1,3},{2,0},{3,1},{4,6},{5,7},{6,4},{7,5},{8,10},{9,11},{10,... | collective-permute-start | bytes 208904 | tf_op jit(solution)/shard_map/ppermute | solution.py:25
  8.1 2.5 %collective-permute-start.4 = (bf16[272,128]{1,0:T(8,128)(2,1)S(1)}, bf16[272,128]{1,0:T(8,128)(2,1)S(1)}, u32[]{:S(2)}, u32[]{:S(2)}) collective-permute-start(bf16[272,128]{1,0:T(8,128)(2,1)S(1)} %get-tuple-element.41.refs_1_.refs_2_), channel_id=1, source_target_pairs={{0,6},{1,5},{2,4},{3,7},{4,2},{5,1},{6,0},{7,3},{8,14},{9,13},{10,... | collective-permute-start | bytes 208904 | tf_op jit(solution)/shard_map/ppermute | solution.py:239
  10.6 1.3 %collective-permute-start.5 = (bf16[272,128]{1,0:T(8,128)(2,1)S(1)}, bf16[272,128]{1,0:T(8,128)(2,1)S(1)}, u32[]{:S(2)}, u32[]{:S(2)}) collective-permute-start(bf16[272,128]{1,0:T(8,128)(2,1)S(1)} %collective-permute-done.1.refs_2_.refs_3_), channel_id=1, source_target_pairs={{0,6},{1,5},{2,4},{3,7},{4,2},{5,1},{6,0},{7,3},{8,14},{9,13},{10,... | collective-permute-start | bytes 208904 | tf_op jit(solution)/shard_map/ppermute | solution.py:239
  11.9 0.7 %shard_map.95 = (f32[128,512]{1,0:T(8,128)S(1)}, f32[3,256,128]{2,1,0:T(8,128)S(1)}) custom-call(bf16[1056,128]{1,0:T(8,128)(2,1)S(1)} %get-tuple-element.40.refs_0_, bf16[272,128]{1,0:T(8,128)(2,1)S(1)} %get-tuple-element.41.refs_1_.refs_2_, bf16[272,128]{1,0:T(8,128)(2,1)S(1)} %collective-permute-done.1.refs_2_.refs_3_, ...), custom_call_target="tpu_custom_call" | custom-call | flops 1000 | bytes 1000 | tf_op jit(solution)/shard_map/pallas_call | solution.py:188
  12.6 0.0 collective-permute-done.refs_0_.refs_1_
  12.6 0.7 %collective-permute-start.10 = (bf16[544,128]{1,0:T(8,128)(2,1)S(1)}, bf16[544,128]{1,0:T(8,128)(2,1)S(1)}, u32[]{:S(2)}, u32[]{:S(2)}) collective-permute-start(bf16[544,128]{1,0:T(8,128)(2,1)S(1)} %slice.7), channel_id=1, source_target_pairs={{0,16},{8,24},{16,0},{24,8},{1,17},{9,25},{17,1},{25,9},{2,18},{10... | collective-permute-start | bytes 417800 | tf_op jit(solution)/shard_map/ppermute | solution.py:25
  13.3 0.7 %shard_map.96 = (f32[128,512]{1,0:T(8,128)S(1)}, f32[3,256,128]{2,1,0:T(8,128)S(1)}) custom-call(bf16[1056,128]{1,0:T(8,128)(2,1)S(1)} %collective-permute-done.refs_0_.refs_1_, bf16[272,128]{1,0:T(8,128)(2,1)S(1)} %get-tuple-element.41.refs_1_.refs_2_, bf16[272,128]{1,0:T(8,128)(2,1)S(1)} %collective-permute-done.1.refs_2_.refs_3_, ...), custom_call_target="tpu_custom_call" | custom-call | flops 1000 | bytes 1000 | tf_op jit(solution)/shard_map/pallas_call | solution.py:188
  14.0 0.0 collective-permute-done.3.refs_0_.refs_2_
  14.0 1.6 %collective-permute-start.9 = (bf16[512,128]{1,0:T(8,128)(2,1)S(1)}, bf16[512,128]{1,0:T(8,128)(2,1)S(1)}, u32[]{:S(2)}, u32[]{:S(2)}) collective-permute-start(bf16[512,128]{1,0:T(8,128)(2,1)S(1)} %slice.6), channel_id=1, source_target_pairs={{0,8},{8,0},{16,24},{24,16},{1,9},{9,1},{17,25},{25,17},{2,10},{10... | collective-permute-start | bytes 393224 | tf_op jit(solution)/shard_map/ppermute | solution.py:25
  15.6 0.7 %shard_map.97 = (f32[128,512]{1,0:T(8,128)S(1)}, f32[3,256,128]{2,1,0:T(8,128)S(1)}) custom-call(bf16[1056,128]{1,0:T(8,128)(2,1)S(1)} %collective-permute-done.3.refs_0_.refs_2_, bf16[272,128]{1,0:T(8,128)(2,1)S(1)} %get-tuple-element.41.refs_1_.refs_2_, bf16[272,128]{1,0:T(8,128)(2,1)S(1)} %collective-permute-done.1.refs_2_.refs_3_, ...), custom_call_target="tpu_custom_call" | custom-call | flops 1000 | bytes 1000 | tf_op jit(solution)/shard_map/pallas_call | solution.py:188
  16.3 0.5 %collective-permute-done.5.refs_4_.refs_6_ = bf16[272,128]{1,0:T(8,128)(2,1)S(1)} collective-permute-done((bf16[272,128]{1,0:T(8,128)(2,1)S(1)}, bf16[272,128]{1,0:T(8,128)(2,1)S(1)}, u32[]{:S(2)}, u32[]{:S(2)}) %collective-permute-start.5) | collective-permute-done | bytes 69664 | tf_op jit(solution)/shard_map/ppermute | solution.py:239
  16.8 0.8 %collective-permute-start.6 = (bf16[272,128]{1,0:T(8,128)(2,1)S(1)}, bf16[272,128]{1,0:T(8,128)(2,1)S(1)}, u32[]{:S(2)}, u32[]{:S(2)}) collective-permute-start(bf16[272,128]{1,0:T(8,128)(2,1)S(1)} %collective-permute-done.2.refs_3_.refs_4_), channel_id=1, source_target_pairs={{0,1},{1,0},{2,3},{3,2},{4,5},{5,4},{6,7},{7,6},{8,9},{9,8},{10,11... | collective-permute-start | bytes 208904 | tf_op jit(solution)/shard_map/ppermute | solution.py:25
  17.6 0.0 collective-permute-start.7
  17.6 0.5 %collective-permute-start.8 = (bf16[272,128]{1,0:T(8,128)(2,1)S(1)}, bf16[272,128]{1,0:T(8,128)(2,1)S(1)}, u32[]{:S(2)}, u32[]{:S(2)}) collective-permute-start(bf16[272,128]{1,0:T(8,128)(2,1)S(1)} %collective-permute-done.5.refs_4_.refs_6_), channel_id=1, source_target_pairs={{0,1},{1,0},{2,3},{3,2},{4,5},{5,4},{6,7},{7,6},{8,9},{9,8},{10,11... | collective-permute-start | bytes 208904 | tf_op jit(solution)/shard_map/ppermute | solution.py:25
  18.1 1.1 %shard_map.98 = (f32[128,512]{1,0:T(8,128)S(1)}, f32[128,512]{1,0:T(8,128)S(1)}, f32[128,512]{1,0:T(8,128)S(1)}, f32[2,256,128]{2,1,0:T(8,128)S(1)}) custom-call(bf16[1056,128]{1,0:T(8,128)(2,1)S(1)} %get-tuple-element.40.refs_0_, bf16[1056,128]{1,0:T(8,128)(2,1)S(1)} %collective-permute-done.refs_0_.refs_1_, ...), custom_call_target="tpu_custom_call" | custom-call | flops 1000 | bytes 1000 | tf_op jit(solution)/shard_map/pallas_call | solution.py:188
  19.2 1.6 %shard_map.99 = (f32[128,512]{1,0:T(8,128)S(1)}, bf16[128,512]{1,0:T(8,128)(2,1)S(1)}, bf16[128,512]{1,0:T(8,128)(2,1)S(1)}, f32[3,256,128]{2,1,0:T(8,128)S(1)}) custom-call(bf16[1056,128]{1,0:T(8,128)(2,1)S(1)} %get-tuple-element.40.refs_0_, bf16[1056,128]{1,0:T(8,128)(2,1)S(1)} %collective-permute-done.refs_0_.refs_1_, ...), custom_call_target="tpu_custom_call" | custom-call | flops 1000 | bytes 1000 | tf_op jit(solution)/shard_map/pallas_call | solution.py:188
  20.9 0.8 %shard_map.100 = (f32[128,512]{1,0:T(8,128)S(1)}, bf16[4,256,128]{2,1,0:T(8,128)(2,1)S(1)}) custom-call(bf16[512,128]{1,0:T(8,128)(2,1)S(1)} %collective-permute-done.9.refs_0_, bf16[544,128]{1,0:T(8,128)(2,1)S(1)} %collective-permute-done.10.refs_1_, bf16[272,128]{1,0:T(8,128)(2,1)S(1)} %get-tuple-element.41.refs_1_.refs_2_, ...), custom_call_target="tpu_custom_call" | custom-call | flops 1000 | bytes 1000 | tf_op jit(solution)/shard_map/pallas_call | solution.py:188
  21.7 0.2 collective-permute-start.11
  21.9 0.6 %collective-permute-start.15 = (bf16[128,512]{1,0:T(8,128)(2,1)S(1)}, bf16[128,512]{1,0:T(8,128)(2,1)S(1)}, u32[]{:S(2)}, u32[]{:S(2)}) collective-permute-start(bf16[128,512]{1,0:T(8,128)(2,1)S(1)} %get-tuple-element.72), channel_id=1, source_target_pairs={{0,8},{8,0},{16,24},{24,16},{1,9},{9,1},{17,25},{25,17},{2,10},{10... | collective-permute-start | bytes 393224 | tf_op jit(solution)/shard_map/ppermute | solution.py:25
  22.4 0.5 %collective-permute-start.16 = (bf16[128,512]{1,0:T(8,128)(2,1)S(1)}, bf16[128,512]{1,0:T(8,128)(2,1)S(1)}, u32[]{:S(2)}, u32[]{:S(2)}) collective-permute-start(bf16[128,512]{1,0:T(8,128)(2,1)S(1)} %get-tuple-element.73), channel_id=1, source_target_pairs={{0,16},{8,24},{16,0},{24,8},{1,17},{9,25},{17,1},{25,9},{2,18},{10... | collective-permute-start | bytes 393224 | tf_op jit(solution)/shard_map/ppermute | solution.py:25
  22.9 0.5 %shard_map.101 = (f32[128,512]{1,0:T(8,128)S(1)}, f32[2,256,128]{2,1,0:T(8,128)S(1)}) custom-call(bf16[512,128]{1,0:T(8,128)(2,1)S(1)} %collective-permute-done.9.refs_0_, bf16[544,128]{1,0:T(8,128)(2,1)S(1)} %collective-permute-done.10.refs_1_, bf16[272,128]{1,0:T(8,128)(2,1)S(1)} %get-tuple-element.41.refs_1_.refs_2_, ...), custom_call_target="tpu_custom_call" | custom-call | flops 1000 | bytes 1000 | tf_op jit(solution)/shard_map/pallas_call | solution.py:188
  23.5 3.8 %collective-permute-start.12 = (bf16[256,128]{1,0:T(8,128)(2,1)S(1)}, bf16[256,128]{1,0:T(8,128)(2,1)S(1)}, u32[]{:S(2)}, u32[]{:S(2)}) collective-permute-start(bf16[256,128]{1,0:T(8,128)(2,1)S(1)} %get-tuple-element.68), channel_id=1, source_target_pairs={{0,6},{1,5},{2,4},{3,7},{4,2},{5,1},{6,0},{7,3},{8,14},{9,13},{10,... | collective-permute-start | bytes 196616 | tf_op jit(solution)/shard_map/ppermute | solution.py:239
  27.3 0.5 %shard_map.102 = (bf16[128,512]{1,0:T(8,128)(2,1)S(1)}, f32[2,256,128]{2,1,0:T(8,128)S(1)}) custom-call(bf16[512,128]{1,0:T(8,128)(2,1)S(1)} %collective-permute-done.9.refs_0_, bf16[544,128]{1,0:T(8,128)(2,1)S(1)} %collective-permute-done.10.refs_1_, bf16[272,128]{1,0:T(8,128)(2,1)S(1)} %get-tuple-element.41.refs_1_.refs_2_, ...), custom_call_target="tpu_custom_call" | custom-call | flops 1000 | bytes 1000 | tf_op jit(solution)/shard_map/pallas_call | solution.py:188
  27.8 0.1 collective-permute-done.16.refs_1_
  27.9 1.4 %collective-permute-start.17 = (bf16[128,512]{1,0:T(8,128)(2,1)S(1)}, bf16[128,512]{1,0:T(8,128)(2,1)S(1)}, u32[]{:S(2)}, u32[]{:S(2)}) collective-permute-start(bf16[128,512]{1,0:T(8,128)(2,1)S(1)} %get-tuple-element.76), channel_id=1, source_target_pairs={{0,24},{8,16},{16,8},{24,0},{1,25},{9,17},{17,9},{25,1},{2,26},{10... | collective-permute-start | bytes 393224 | tf_op jit(solution)/shard_map/ppermute | solution.py:25
  29.4 1.6 %collective-permute-start.14 = (bf16[256,128]{1,0:T(8,128)(2,1)S(1)}, bf16[256,128]{1,0:T(8,128)(2,1)S(1)}, u32[]{:S(2)}, u32[]{:S(2)}) collective-permute-start(bf16[256,128]{1,0:T(8,128)(2,1)S(1)} %get-tuple-element.70), channel_id=1, source_target_pairs={{0,2},{1,3},{2,0},{3,1},{4,6},{5,7},{6,4},{7,5},{8,10},{9,11},{10,... | collective-permute-start | bytes 196616 | tf_op jit(solution)/shard_map/ppermute | solution.py:25
  31.0 1.7 %collective-permute-done.13.refs_1_ = bf16[256,128]{1,0:T(8,128)(2,1)S(1)} collective-permute-done((bf16[256,128]{1,0:T(8,128)(2,1)S(1)}, bf16[256,128]{1,0:T(8,128)(2,1)S(1)}, u32[]{:S(2)}, u32[]{:S(2)}) %collective-permute-start.13) | collective-permute-done | bytes 65568 | tf_op jit(solution)/shard_map/ppermute | solution.py:239
  32.8 1.0 %collective-permute-done.17.refs_2_ = bf16[128,512]{1,0:T(8,128)(2,1)S(1)} collective-permute-done((bf16[128,512]{1,0:T(8,128)(2,1)S(1)}, bf16[128,512]{1,0:T(8,128)(2,1)S(1)}, u32[]{:S(2)}, u32[]{:S(2)}) %collective-permute-start.17) | collective-permute-done | bytes 131104 | tf_op jit(solution)/shard_map/ppermute | solution.py:25
  33.8 0.8 %shard_map.106 = (bf16[128,512]{1,0:T(8,128)(2,1)}, bf16[128,128]{1,0:T(8,128)(2,1)}, bf16[128,128]{1,0:T(8,128)(2,1)}) custom-call(f32[128,512]{1,0:T(8,128)S(1)} %get-tuple-element.58.dq_own, f32[256,128]{1,0:T(8,128)S(1)} %shard_map.105.dkv_ref, bf16[256,128]{1,0:T(8,128)(2,1)S(1)} %collective-permute-done.14.near_ref, ...), custom_call_target="tpu_custom_call" | custom-call | flops 1000 | bytes 1000 | tf_op jit(solution)/shard_map/pallas_call | solution.py:322
  (19 shorter events, 0.1 us)
Async XLA Ops:
  2.0 10.6 %collective-permute-start = (bf16[1056,128]{1,0:T(8,128)(2,1)S(1)}, bf16[1056,128]{1,0:T(8,128)(2,1)S(1)}, u32[]{:S(2)}, u32[]{:S(2)}) collective-permute-start(bf16[1056,128]{1,0:T(8,128)(2,1)S(1)} %get-tuple-element.40.refs_0_), channel_id=1, source_target_pairs={{0,8},{8,0},{16,24},{24,16},{1,9},{9,1},{17,25},{25,17},{2,10},{10... | collective-permute-start | bytes 811016 | tf_op jit(solution)/shard_map/ppermute | solution.py:25
  5.0 9.0 %collective-permute-start.3 = (bf16[1056,128]{1,0:T(8,128)(2,1)S(1)}, bf16[1056,128]{1,0:T(8,128)(2,1)S(1)}, u32[]{:S(2)}, u32[]{:S(2)}) collective-permute-start(bf16[1056,128]{1,0:T(8,128)(2,1)S(1)} %get-tuple-element.40.refs_0_), channel_id=1, source_target_pairs={{0,16},{8,24},{16,0},{24,8},{1,17},{9,25},{17,1},{25,9},{2,18},{10... | collective-permute-start | bytes 811016 | tf_op jit(solution)/shard_map/ppermute | solution.py:25
  6.5 4.1 %collective-permute-start.1 = (bf16[272,128]{1,0:T(8,128)(2,1)S(1)}, bf16[272,128]{1,0:T(8,128)(2,1)S(1)}, u32[]{:S(2)}, u32[]{:S(2)}) collective-permute-start(bf16[272,128]{1,0:T(8,128)(2,1)S(1)} %get-tuple-element.41.refs_1_.refs_2_), channel_id=1, source_target_pairs={{0,1},{1,0},{2,3},{3,2},{4,5},{5,4},{6,7},{7,6},{8,9},{9,8},{10,11... | collective-permute-start | bytes 208904 | tf_op jit(solution)/shard_map/ppermute | solution.py:25
  6.5 5.4 %collective-permute-start.2 = (bf16[272,128]{1,0:T(8,128)(2,1)S(1)}, bf16[272,128]{1,0:T(8,128)(2,1)S(1)}, u32[]{:S(2)}, u32[]{:S(2)}) collective-permute-start(bf16[272,128]{1,0:T(8,128)(2,1)S(1)} %get-tuple-element.41.refs_1_.refs_2_), channel_id=1, source_target_pairs={{0,2},{1,3},{2,0},{3,1},{4,6},{5,7},{6,4},{7,5},{8,10},{9,11},{10,... | collective-permute-start | bytes 208904 | tf_op jit(solution)/shard_map/ppermute | solution.py:25
  8.1 8.2 %collective-permute-start.4 = (bf16[272,128]{1,0:T(8,128)(2,1)S(1)}, bf16[272,128]{1,0:T(8,128)(2,1)S(1)}, u32[]{:S(2)}, u32[]{:S(2)}) collective-permute-start(bf16[272,128]{1,0:T(8,128)(2,1)S(1)} %get-tuple-element.41.refs_1_.refs_2_), channel_id=1, source_target_pairs={{0,6},{1,5},{2,4},{3,7},{4,2},{5,1},{6,0},{7,3},{8,14},{9,13},{10,... | collective-permute-start | bytes 208904 | tf_op jit(solution)/shard_map/ppermute | solution.py:239
  10.6 6.2 %collective-permute-start.5 = (bf16[272,128]{1,0:T(8,128)(2,1)S(1)}, bf16[272,128]{1,0:T(8,128)(2,1)S(1)}, u32[]{:S(2)}, u32[]{:S(2)}) collective-permute-start(bf16[272,128]{1,0:T(8,128)(2,1)S(1)} %collective-permute-done.1.refs_2_.refs_3_), channel_id=1, source_target_pairs={{0,6},{1,5},{2,4},{3,7},{4,2},{5,1},{6,0},{7,3},{8,14},{9,13},{10,... | collective-permute-start | bytes 208904 | tf_op jit(solution)/shard_map/ppermute | solution.py:239
  12.6 8.3 %collective-permute-start.10 = (bf16[544,128]{1,0:T(8,128)(2,1)S(1)}, bf16[544,128]{1,0:T(8,128)(2,1)S(1)}, u32[]{:S(2)}, u32[]{:S(2)}) collective-permute-start(bf16[544,128]{1,0:T(8,128)(2,1)S(1)} %slice.7), channel_id=1, source_target_pairs={{0,16},{8,24},{16,0},{24,8},{1,17},{9,25},{17,1},{25,9},{2,18},{10... | collective-permute-start | bytes 417800 | tf_op jit(solution)/shard_map/ppermute | solution.py:25
  14.0 6.9 %collective-permute-start.9 = (bf16[512,128]{1,0:T(8,128)(2,1)S(1)}, bf16[512,128]{1,0:T(8,128)(2,1)S(1)}, u32[]{:S(2)}, u32[]{:S(2)}) collective-permute-start(bf16[512,128]{1,0:T(8,128)(2,1)S(1)} %slice.6), channel_id=1, source_target_pairs={{0,8},{8,0},{16,24},{24,16},{1,9},{9,1},{17,25},{25,17},{2,10},{10... | collective-permute-start | bytes 393224 | tf_op jit(solution)/shard_map/ppermute | solution.py:25
  16.8 2.4 %collective-permute-start.6 = (bf16[272,128]{1,0:T(8,128)(2,1)S(1)}, bf16[272,128]{1,0:T(8,128)(2,1)S(1)}, u32[]{:S(2)}, u32[]{:S(2)}) collective-permute-start(bf16[272,128]{1,0:T(8,128)(2,1)S(1)} %collective-permute-done.2.refs_3_.refs_4_), channel_id=1, source_target_pairs={{0,1},{1,0},{2,3},{3,2},{4,5},{5,4},{6,7},{7,6},{8,9},{9,8},{10,11... | collective-permute-start | bytes 208904 | tf_op jit(solution)/shard_map/ppermute | solution.py:25
  17.6 1.6 %collective-permute-start.7 = (bf16[272,128]{1,0:T(8,128)(2,1)S(1)}, bf16[272,128]{1,0:T(8,128)(2,1)S(1)}, u32[]{:S(2)}, u32[]{:S(2)}) collective-permute-start(bf16[272,128]{1,0:T(8,128)(2,1)S(1)} %collective-permute-done.4.refs_3_.refs_5_), channel_id=1, source_target_pairs={{0,1},{1,0},{2,3},{3,2},{4,5},{5,4},{6,7},{7,6},{8,9},{9,8},{10,11... | collective-permute-start | bytes 208904 | tf_op jit(solution)/shard_map/ppermute | solution.py:25
  17.6 1.6 %collective-permute-start.8 = (bf16[272,128]{1,0:T(8,128)(2,1)S(1)}, bf16[272,128]{1,0:T(8,128)(2,1)S(1)}, u32[]{:S(2)}, u32[]{:S(2)}) collective-permute-start(bf16[272,128]{1,0:T(8,128)(2,1)S(1)} %collective-permute-done.5.refs_4_.refs_6_), channel_id=1, source_target_pairs={{0,1},{1,0},{2,3},{3,2},{4,5},{5,4},{6,7},{7,6},{8,9},{9,8},{10,11... | collective-permute-start | bytes 208904 | tf_op jit(solution)/shard_map/ppermute | solution.py:25
  21.7 1.7 %collective-permute-start.11 = (bf16[4,256,128]{2,1,0:T(8,128)(2,1)S(1)}, bf16[4,256,128]{2,1,0:T(8,128)(2,1)S(1)}, u32[]{:S(2)}, u32[]{:S(2)}) collective-permute-start(bf16[4,256,128]{2,1,0:T(8,128)(2,1)S(1)} %get-tuple-element.65), channel_id=1, source_target_pairs={{0,1},{1,0},{2,3},{3,2},{4,5},{5,4},{6,7},{7,6},{8,9},{9,8},{10,11... | collective-permute-start | bytes 786440 | tf_op jit(solution)/shard_map/ppermute | solution.py:25
  21.9 5.9 %collective-permute-start.15 = (bf16[128,512]{1,0:T(8,128)(2,1)S(1)}, bf16[128,512]{1,0:T(8,128)(2,1)S(1)}, u32[]{:S(2)}, u32[]{:S(2)}) collective-permute-start(bf16[128,512]{1,0:T(8,128)(2,1)S(1)} %get-tuple-element.72), channel_id=1, source_target_pairs={{0,8},{8,0},{16,24},{24,16},{1,9},{9,1},{17,25},{25,17},{2,10},{10... | collective-permute-start | bytes 393224 | tf_op jit(solution)/shard_map/ppermute | solution.py:25
  22.4 5.5 %collective-permute-start.16 = (bf16[128,512]{1,0:T(8,128)(2,1)S(1)}, bf16[128,512]{1,0:T(8,128)(2,1)S(1)}, u32[]{:S(2)}, u32[]{:S(2)}) collective-permute-start(bf16[128,512]{1,0:T(8,128)(2,1)S(1)} %get-tuple-element.73), channel_id=1, source_target_pairs={{0,16},{8,24},{16,0},{24,8},{1,17},{9,25},{17,1},{25,9},{2,18},{10... | collective-permute-start | bytes 393224 | tf_op jit(solution)/shard_map/ppermute | solution.py:25
  23.5 7.6 %collective-permute-start.12 = (bf16[256,128]{1,0:T(8,128)(2,1)S(1)}, bf16[256,128]{1,0:T(8,128)(2,1)S(1)}, u32[]{:S(2)}, u32[]{:S(2)}) collective-permute-start(bf16[256,128]{1,0:T(8,128)(2,1)S(1)} %get-tuple-element.68), channel_id=1, source_target_pairs={{0,6},{1,5},{2,4},{3,7},{4,2},{5,1},{6,0},{7,3},{8,14},{9,13},{10,... | collective-permute-start | bytes 196616 | tf_op jit(solution)/shard_map/ppermute | solution.py:239
  27.3 5.5 %collective-permute-start.13 = (bf16[256,128]{1,0:T(8,128)(2,1)S(1)}, bf16[256,128]{1,0:T(8,128)(2,1)S(1)}, u32[]{:S(2)}, u32[]{:S(2)}) collective-permute-start(bf16[256,128]{1,0:T(8,128)(2,1)S(1)} %get-tuple-element.69), channel_id=1, source_target_pairs={{0,4},{1,7},{2,6},{3,5},{4,0},{5,3},{6,2},{7,1},{8,12},{9,15},{10,... | collective-permute-start | bytes 196616 | tf_op jit(solution)/shard_map/ppermute | solution.py:239
  27.9 5.9 %collective-permute-start.17 = (bf16[128,512]{1,0:T(8,128)(2,1)S(1)}, bf16[128,512]{1,0:T(8,128)(2,1)S(1)}, u32[]{:S(2)}, u32[]{:S(2)}) collective-permute-start(bf16[128,512]{1,0:T(8,128)(2,1)S(1)} %get-tuple-element.76), channel_id=1, source_target_pairs={{0,24},{8,16},{16,8},{24,0},{1,25},{9,17},{17,9},{25,1},{2,26},{10... | collective-permute-start | bytes 393224 | tf_op jit(solution)/shard_map/ppermute | solution.py:25
  29.4 4.4 %collective-permute-start.14 = (bf16[256,128]{1,0:T(8,128)(2,1)S(1)}, bf16[256,128]{1,0:T(8,128)(2,1)S(1)}, u32[]{:S(2)}, u32[]{:S(2)}) collective-permute-start(bf16[256,128]{1,0:T(8,128)(2,1)S(1)} %get-tuple-element.70), channel_id=1, source_target_pairs={{0,2},{1,3},{2,0},{3,1},{4,6},{5,7},{6,4},{7,5},{8,10},{9,11},{10,... | collective-permute-start | bytes 196616 | tf_op jit(solution)/shard_map/ppermute | solution.py:25

commit v15 on v13

--- a/solution.py
+++ b/solution.py
@@ -102,59 +102,80 @@
         lse = e[0:heads] + e[heads : 2 * heads] + e[2 * heads : 3 * heads]
         delta = e[3 * heads : 4 * heads] + e[4 * heads : 5 * heads] + e[5 * heads : 6 * heads]
         rowed.append((lse, delta, e[6 * heads : 6 * heads + 1]))
+    group = 3 if len(slots) == 3 else 2
+    loaded = {}
+
+    def chunk(c):
+        if c not in loaded:
+            ks, vs, runs = [], [], []
+            for n in slots[c : c + group]:
+                ks.append(kv_refs[n][:rows, :])
+                vs.append(kv_refs[n][rows : 2 * rows, :])
+                e = kv_refs[n][2 * rows :, :].astype(F32)
+                runs += [e[r : r + 1] for r in range(per)]
+            kt = jnp.concatenate([b.astype(F32).T.astype(BF) for b in ks], axis=1)
+            loaded[c] = (jnp.concatenate(ks, axis=0), jnp.concatenate(vs, axis=0), kt, runs)
+        return loaded[c]
+
+    def products(c, b, n):
+        k, v, _, _ = chunk(c)
+        q_ref, g_ref = x_refs[b]
+        q = q_ref[n * COLS : (n + 1) * COLS, :]
+        g = g_ref[n * COLS : (n + 1) * COLS, :]
+        return q, g, dot(k, q, NT), dot(v, g, NT)
+
+    def weights(c, b, n, st, dpt):
+        lse, delta, run = rowed[b]
+        p_rows, d_rows = [], []
+        for r, krun in enumerate(chunk(c)[3]):
+            sl = slice(r * RUN, (r + 1) * RUN)
+            p_heads, d_heads = [], []
+            for h in range(step):
+                hl = slice(h * rows, (h + 1) * rows)
+                head = n * step + h
+                row = jnp.where(krun <= run, lse[head : head + 1], 1e30)
+                arg = st[sl, hl] * (scale * LOG2E) - row
+                if plan["diagonal"] and b == 0 and c == 0 and r < per:
+                    i = lax.broadcasted_iota(jnp.int32, (RUN, rows), 1) - r * RUN
+                    j = lax.broadcasted_iota(jnp.int32, (RUN, rows), 0)
+                    arg = jnp.where((i >= 0) & (i < j), -1e30, arg)
+                p = jnp.exp2(arg)
+                p_heads.append(p.astype(BF))
+                d_heads.append((p * (dpt[sl, hl] - delta[head : head + 1])).astype(BF))
+            p_rows.append(jnp.concatenate(p_heads, axis=1))
+            d_rows.append(jnp.concatenate(d_heads, axis=1))
+        return jnp.concatenate(p_rows, axis=0), jnp.concatenate(d_rows, axis=0)
+
+    def plus(total, part):
+        return part if total is None else total + part
+
     dqt = [[None] * (hr // COLS) for _ in x_refs]
-    group = 3 if len(slots) == 3 else 2
-    for c in range(0, len(slots), group):
-        ks, vs, runs = [], [], []
-        for n in slots[c : c + group]:
-            ks.append(kv_refs[n][:rows, :])
-            vs.append(kv_refs[n][rows : 2 * rows, :])
-            e = kv_refs[n][2 * rows :, :].astype(F32)
-            runs += [e[r : r + 1] for r in range(per)]
-        k = jnp.concatenate(ks, axis=0)
-        v = jnp.concatenate(vs, axis=0)
-        kt = jnp.concatenate([b.astype(F32).T.astype(BF) for b in ks], axis=1)
-        dk = dv = None
-        for b, (q_ref, g_ref) in enumerate(x_refs):
-            lse, delta, run = rowed[b]
-            for n in range(hr // COLS):
-                q = q_ref[n * COLS : (n + 1) * COLS, :]
-                g = g_ref[n * COLS : (n + 1) * COLS, :]
-                st = dot(k, q, NT)
-                dpt = dot(v, g, NT)
-                p_rows, d_rows = [], []
-                for r in range(len(runs)):
-                    sl = slice(r * RUN, (r + 1) * RUN)
-                    p_heads, d_heads = [], []
-                    for h in range(step):
-                        hl = slice(h * rows, (h + 1) * rows)
-                        head = n * step + h
-                        row = jnp.where(runs[r] <= run, lse[head : head + 1], 1e30)
-                        arg = st[sl, hl] * (scale * LOG2E) - row
-                        if plan["diagonal"] and b == 0 and c == 0 and r < per:
-                            i = lax.broadcasted_iota(jnp.int32, (RUN, rows), 1) - r * RUN
-                            j = lax.broadcasted_iota(jnp.int32, (RUN, rows), 0)
-                            arg = jnp.where((i >= 0) & (i < j), -1e30, arg)
-                        p = jnp.exp2(arg)
-                        p_heads.append(p.astype(BF))
-                        d_heads.append((p * (dpt[sl, hl] - delta[head : head + 1])).astype(BF))
-                    p_rows.append(jnp.concatenate(p_heads, axis=1))
-                    d_rows.append(jnp.concatenate(d_heads, axis=1))
-                p = jnp.concatenate(p_rows, axis=0)
-                d = jnp.concatenate(d_rows, axis=0)
-                dv_n, dk_n, dq_n = dot(p, g), dot(d, q), dot(kt, d)
-                dv = dv_n if dv is None else dv + dv_n
-                dk = dk_n if dk is None else dk + dk_n
-                old = dqt[b][n]
-                dqt[b][n] = dq_n if old is None else old + dq_n
-        for j, n in enumerate(slots[c : c + group]):
+    units = [
+        (c, b, n)
+        for c in range(0, len(slots), group)
+        for b in range(len(x_refs))
+        for n in range(hr // COLS)
+    ]
+    dk = dv = None
+    ahead = products(*units[0])
+    for at, (c, b, n) in enumerate(units):
+        q, g, st, dpt = ahead
+        if at + 1 < len(units):
+            ahead = products(*units[at + 1])
+        p, d = weights(c, b, n, st, dpt)
+        dv, dk = plus(dv, dot(p, g)), plus(dk, dot(d, q))
+        dqt[b][n] = plus(dqt[b][n], dot(chunk(c)[2], d))
+        if at + 1 < len(units) and units[at + 1][0] == c:
+            continue
+        for j, slot in enumerate(slots[c : c + group]):
             dk_j, dv_j = dk[j * rows : (j + 1) * rows], dv[j * rows : (j + 1) * rows]
             if plan["acc"]:
-                acc_ref, at = acc_refs[plan["at"][n][0]], plan["at"][n][1]
-                dk_j += acc_ref[at, :rows, :]
-                dv_j += acc_ref[at, rows:, :]
+                acc_ref, place = acc_refs[plan["at"][slot][0]], plan["at"][slot][1]
+                dk_j += acc_ref[place, :rows, :]
+                dv_j += acc_ref[place, rows:, :]
             dkv_ref[c + j, :rows, :] = dk_j.astype(dkv_ref.dtype)
             dkv_ref[c + j, rows:, :] = dv_j.astype(dkv_ref.dtype)
+        dk = dv = None
     for b, dq_ref in enumerate(dq_refs):
         for n in range(hr // COLS):
             cols = slice(n * COLS, (n + 1) * COLS)
@@ -218,17 +239,25 @@
     refs[-1][...] = total
 
 
-def final_kernel(rows, heads, scale, dq_own, dkv_ref, near_ref, *refs):
-    dq_refs, (gq_ref, gk_ref, gv_ref) = refs[:-3], refs[-3:]
-    dq = dq_own[...]
-    for r in dq_refs:
-        dq = dq + r[...].astype(F32)
+def sum_call(own, got, flops):
+    return pl.pallas_call(
+        sum_kernel,
+        out_shape=jax.ShapeDtypeStruct(own.shape, F32),
+        in_specs=[VMEM] * (1 + len(got)),
+        out_specs=VMEM,
+        compiler_params=SMALL,
+        cost_estimate=pl.CostEstimate(flops=flops, bytes_accessed=1000, transcendentals=0),
+    )(own, *got)
+
+
+def final_kernel(rows, heads, scale, dq_ref, dq_far, dkv_ref, dkv_near, gq_ref, gk_ref, gv_ref):
+    dkv = dkv_ref[...] + dkv_near[...].astype(F32)
+    gk_ref[...] = (scale * dkv[:rows]).astype(BF)
+    gv_ref[...] = dkv[rows:].astype(BF)
+    dq = dq_ref[...] + dq_far[...].astype(F32)
     for h in range(heads):
         part = dq[:, h * rows : (h + 1) * rows]
         gq_ref[:, h * 128 : (h + 1) * 128] = (scale * part).T.astype(BF)
-    dkv = dkv_ref[...] + near_ref[...].astype(F32)
-    gk_ref[...] = (scale * dkv[:rows]).astype(BF)
-    gv_ref[...] = dkv[rows:].astype(BF)
 
 
 def crossed(block, t, other):
@@ -270,21 +299,18 @@
     early = [kv, sib, near]
     dq_own, acc = blocks_call([x], early, range(3), *common, F32, F32, diagonal=True)
 
-    near_sib = swapped(near, "inner", 1)
     xs = [swapped(x, "outer", s) for s in range(1, nq - 1)]
     dqs = [dq_own]
     for s in range(nq - 2):
-        late = (near_sib,) if s == nq - 3 else ()
-        xs[s], acc, *late = lax.optimization_barrier((xs[s], acc, *late))
+        xs[s], acc = lax.optimization_barrier((xs[s], acc))
         dq, acc = blocks_call([xs[s]], early, range(3), *common, F32, F32, acc=[(acc, n) for n in range(3)])
         dqs.append(dq)
-    (near_sib,) = late
     halves = [xs[nq - 3][:hr], xs[((nq - 1) ^ (nq // 2)) - 1][hr:]]
     corner = [swapped(halves[0], "outer", 1), swapped(halves[1], "outer", nq // 2)]
 
     *direct, acc = lax.optimization_barrier((*direct, acc))
     traded = [swapped(block, "inner", 1) for block in direct]
-    direct = [near_sib, *direct]
+    direct = [swapped(near, "inner", 1), *direct]
     xs = [x, *xs]
     n_d, n_t = len(direct), len(traded)
     *dqs, acc_d = blocks_call(xs, direct, range(n_d), *common, F32, F32, dq_in=dqs)
@@ -305,31 +331,23 @@
     dkv_own, dkv_near = add_call(dkv_own, dkv_got, 0, [F32, BF])
 
     got = [swapped(dq, "outer", s + 1) for s, dq in enumerate(dqs)]
-    dq_last, *got = lax.optimization_barrier((dq_last, *got))
-    got.append(swapped(dq_last, "outer", nq - 1))
+    dq_far = swapped(dq_last, "outer", nq - 1)
     dkv = []
     for t in range(1, nz // 2):
         dkv.append(crossed(far[2 * t - 2], t, False))
         dkv.append(crossed(far[2 * t - 1], t, True))
     dkv_near = swapped(dkv_near, "inner", 2)
 
-    dkv_sum = pl.pallas_call(
-        sum_kernel,
-        out_shape=sds((2 * rows, width), F32),
-        in_specs=[VMEM] * (nz - 1),
-        out_specs=VMEM,
-        compiler_params=SMALL,
-        cost_estimate=pl.CostEstimate(flops=1_500_000_000, bytes_accessed=1000, transcendentals=0),
-    )(dkv_own, *dkv)
-
+    dkv_sum = sum_call(dkv_own, dkv, 1_500_000_000)
+    dq_sum = sum_call(dq_own, got, 100_000_000)
     return pl.pallas_call(
         functools.partial(final_kernel, rows, heads, scale),
         out_shape=(sds((rows, heads * width), BF), sds((rows, width), BF), sds((rows, width), BF)),
-        in_specs=[VMEM] * (3 + len(got)),
+        in_specs=[VMEM] * 4,
         out_specs=(VMEM,) * 3,
         compiler_params=SMALL,
         cost_estimate=QUICK,
-    )(dq_own, dkv_sum, dkv_near, *got)
+    )(dq_sum, dq_far, dkv_sum, dkv_near)
 
 
 def solution(mesh):

time: 37.8 us -> 34.7 us (0.918)
  waiting for transfers between devices: 9.49 us -> 3.3 us
  starting transfers between devices: 18.6 us -> 21.6 us
    ppermute x14, waiting for transfers between devices: 4.9 us -> 1.12 us  [swapped(): return lax.ppermute(block, axis, pairs)]
    ppermute x4, waiting for transfers between devices: 4.6 us -> 2.19 us  [crossed(): return lax.ppermute(block, 'inner', pairs)]
    ppermute x14, starting transfers between devices: 11.8 us -> 14 us  [swapped(): return lax.ppermute(block, axis, pairs)]
    ppermute x4, starting transfers between devices: 6.83 us -> 7.65 us  [crossed(): return lax.ppermute(block, 'inner', pairs)]
  transfers between devices with their start and end apart: 18 -> 18, of which waited for: 6 -> 3; matrix products, arithmetic and copies ran while one was open for 0% -> 0% of each run, Pallas kernels for 15% -> 17%
where the time goes in v15:
time: 34.7 us; the launch traced here: 34.5 us
  starting transfers between devices  21.6 us (62%)
  Pallas kernels  8.75 us (25%)
  waiting for transfers between devices  3.3 us (10%)
  between operations  0.8 us (2%)
    ppermute x14, starting transfers between devices, swapped(): return lax.ppermute(block, axis, pairs)  14 us
    ppermute x4, starting transfers between devices, crossed(): return lax.ppermute(block, 'inner', pairs)  7.65 us
    pallas_call x8, Pallas kernels, blocks_call(): pl.pallas_call(functools.partial(blocks_kernel, plan, rows, heads, scale)...  6.51 us
    ppermute x4, waiting for transfers between devices, crossed(): return lax.ppermute(block, 'inner', pairs)  2.19 us
    pallas_call x1, Pallas kernels, on_device(): pl.pallas_call(pack_kernel, out_shape=(sds((2 * hr + 32, width), BF), sds...  1.34 us
    ppermute x14, waiting for transfers between devices, swapped(): return lax.ppermute(block, axis, pairs)  1.12 us
    pallas_call x1, Pallas kernels, on_device(): pl.pallas_call(functools.partial(final_kernel, rows, heads, scale), out_s...  0.77 us
  transfers between devices with their start and end apart: 18, of which 3 were waited for; matrix products, arithmetic and copies ran while one was open for 0% of the time, Pallas kernels for 17%

profile of v15, /device:TPU:0, one launch (start us, length us, event | category | flops | bytes accessed | tf_op | source)
XLA Modules:
  0.0 34.5 jit_solution(1494376164117726358)
XLA Ops:
  0.6 1.3 %shard_map.94 = (bf16[1056,128]{1,0:T(8,128)(2,1)S(1)}, bf16[272,128]{1,0:T(8,128)(2,1)S(1)}) custom-call(bf16[128,512]{1,0:T(8,128)(2,1)} %q_ref.1, bf16[128,128]{1,0:T(8,128)(2,1)} %k_ref.1, bf16[128,128]{1,0:T(8,128)(2,1)} %v_ref.1, bf16[128,512]{1,0:T(8,128)(2,1)} %o_ref.1, bf16[128,512]{1,0:T(8,128)(2,1)} %g_ref.1, f32[4,128]{1,0:T(4,128)} %lse_ref.1, ...), custom_call_target="tpu_custom_call" | custom-call | flops 1000 | bytes 1000 | tf_op jit(solution)/shard_map/pallas_call | solution.py:280
  2.0 3.0 %collective-permute-start = (bf16[1056,128]{1,0:T(8,128)(2,1)S(1)}, bf16[1056,128]{1,0:T(8,128)(2,1)S(1)}, u32[]{:S(2)}, u32[]{:S(2)}) collective-permute-start(bf16[1056,128]{1,0:T(8,128)(2,1)S(1)} %get-tuple-element.36.refs_0_), channel_id=1, source_target_pairs={{0,8},{8,0},{16,24},{24,16},{1,9},{9,1},{17,25},{25,17},{2,10},{10... | collective-permute-start | bytes 811016 | tf_op jit(solution)/shard_map/ppermute | solution.py:25
  5.0 1.5 %collective-permute-start.3 = (bf16[1056,128]{1,0:T(8,128)(2,1)S(1)}, bf16[1056,128]{1,0:T(8,128)(2,1)S(1)}, u32[]{:S(2)}, u32[]{:S(2)}) collective-permute-start(bf16[1056,128]{1,0:T(8,128)(2,1)S(1)} %get-tuple-element.36.refs_0_), channel_id=1, source_target_pairs={{0,16},{8,24},{16,0},{24,8},{1,17},{9,25},{17,1},{25,9},{2,18},{10... | collective-permute-start | bytes 811016 | tf_op jit(solution)/shard_map/ppermute | solution.py:25
  6.5 1.6 %collective-permute-start.2 = (bf16[272,128]{1,0:T(8,128)(2,1)S(1)}, bf16[272,128]{1,0:T(8,128)(2,1)S(1)}, u32[]{:S(2)}, u32[]{:S(2)}) collective-permute-start(bf16[272,128]{1,0:T(8,128)(2,1)S(1)} %get-tuple-element.37.refs_1_.refs_2_), channel_id=1, source_target_pairs={{0,2},{1,3},{2,0},{3,1},{4,6},{5,7},{6,4},{7,5},{8,10},{9,11},{10,... | collective-permute-start | bytes 208904 | tf_op jit(solution)/shard_map/ppermute | solution.py:25
  8.1 2.5 %collective-permute-start.4 = (bf16[272,128]{1,0:T(8,128)(2,1)S(1)}, bf16[272,128]{1,0:T(8,128)(2,1)S(1)}, u32[]{:S(2)}, u32[]{:S(2)}) collective-permute-start(bf16[272,128]{1,0:T(8,128)(2,1)S(1)} %get-tuple-element.37.refs_1_.refs_2_), channel_id=1, source_target_pairs={{0,6},{1,5},{2,4},{3,7},{4,2},{5,1},{6,0},{7,3},{8,14},{9,13},{10,... | collective-permute-start | bytes 208904 | tf_op jit(solution)/shard_map/ppermute | solution.py:268
  10.6 1.3 %collective-permute-start.5 = (bf16[272,128]{1,0:T(8,128)(2,1)S(1)}, bf16[272,128]{1,0:T(8,128)(2,1)S(1)}, u32[]{:S(2)}, u32[]{:S(2)}) collective-permute-start(bf16[272,128]{1,0:T(8,128)(2,1)S(1)} %collective-permute-done.1.refs_2_.refs_3_), channel_id=1, source_target_pairs={{0,6},{1,5},{2,4},{3,7},{4,2},{5,1},{6,0},{7,3},{8,14},{9,13},{10,... | collective-permute-start | bytes 208904 | tf_op jit(solution)/shard_map/ppermute | solution.py:268
  11.9 0.7 %shard_map.95 = (f32[128,512]{1,0:T(8,128)S(1)}, f32[3,256,128]{2,1,0:T(8,128)S(1)}) custom-call(bf16[1056,128]{1,0:T(8,128)(2,1)S(1)} %get-tuple-element.36.refs_0_, bf16[272,128]{1,0:T(8,128)(2,1)S(1)} %get-tuple-element.37.refs_1_.refs_2_, bf16[272,128]{1,0:T(8,128)(2,1)S(1)} %collective-permute-done.1.refs_2_.refs_3_, ...), custom_call_target="tpu_custom_call" | custom-call | flops 1000 | bytes 1000 | tf_op jit(solution)/shard_map/pallas_call | solution.py:209
  12.6 0.7 %collective-permute-start.12 = (bf16[544,128]{1,0:T(8,128)(2,1)S(1)}, bf16[544,128]{1,0:T(8,128)(2,1)S(1)}, u32[]{:S(2)}, u32[]{:S(2)}) collective-permute-start(bf16[544,128]{1,0:T(8,128)(2,1)S(1)} %slice.7), channel_id=1, source_target_pairs={{0,16},{8,24},{16,0},{24,8},{1,17},{9,25},{17,1},{25,9},{2,18},{10... | collective-permute-start | bytes 417800 | tf_op jit(solution)/shard_map/ppermute | solution.py:25
  13.3 0.7 %shard_map.96 = (f32[128,512]{1,0:T(8,128)S(1)}, f32[3,256,128]{2,1,0:T(8,128)S(1)}) custom-call(bf16[1056,128]{1,0:T(8,128)(2,1)S(1)} %collective-permute-done.refs_0_.refs_1_, bf16[272,128]{1,0:T(8,128)(2,1)S(1)} %get-tuple-element.37.refs_1_.refs_2_, bf16[272,128]{1,0:T(8,128)(2,1)S(1)} %collective-permute-done.1.refs_2_.refs_3_, ...), custom_call_target="tpu_custom_call" | custom-call | flops 1000 | bytes 1000 | tf_op jit(solution)/shard_map/pallas_call | solution.py:209
  14.0 0.0 collective-permute-done.3.refs_0_.refs_2_
  14.0 1.6 %collective-permute-start.11 = (bf16[512,128]{1,0:T(8,128)(2,1)S(1)}, bf16[512,128]{1,0:T(8,128)(2,1)S(1)}, u32[]{:S(2)}, u32[]{:S(2)}) collective-permute-start(bf16[512,128]{1,0:T(8,128)(2,1)S(1)} %slice.6), channel_id=1, source_target_pairs={{0,8},{8,0},{16,24},{24,16},{1,9},{9,1},{17,25},{25,17},{2,10},{10... | collective-permute-start | bytes 393224 | tf_op jit(solution)/shard_map/ppermute | solution.py:25
  15.6 0.7 %shard_map.97 = (f32[128,512]{1,0:T(8,128)S(1)}, f32[3,256,128]{2,1,0:T(8,128)S(1)}) custom-call(bf16[1056,128]{1,0:T(8,128)(2,1)S(1)} %collective-permute-done.3.refs_0_.refs_2_, bf16[272,128]{1,0:T(8,128)(2,1)S(1)} %get-tuple-element.37.refs_1_.refs_2_, bf16[272,128]{1,0:T(8,128)(2,1)S(1)} %collective-permute-done.1.refs_2_.refs_3_, ...), custom_call_target="tpu_custom_call" | custom-call | flops 1000 | bytes 1000 | tf_op jit(solution)/shard_map/pallas_call | solution.py:209
  16.3 0.5 %collective-permute-done.5.refs_5_.refs_7_ = bf16[272,128]{1,0:T(8,128)(2,1)S(1)} collective-permute-done((bf16[272,128]{1,0:T(8,128)(2,1)S(1)}, bf16[272,128]{1,0:T(8,128)(2,1)S(1)}, u32[]{:S(2)}, u32[]{:S(2)}) %collective-permute-start.5) | collective-permute-done | bytes 69664 | tf_op jit(solution)/shard_map/ppermute | solution.py:268
  16.8 0.8 %collective-permute-start.6 = (bf16[272,128]{1,0:T(8,128)(2,1)S(1)}, bf16[272,128]{1,0:T(8,128)(2,1)S(1)}, u32[]{:S(2)}, u32[]{:S(2)}) collective-permute-start(bf16[272,128]{1,0:T(8,128)(2,1)S(1)} %collective-permute-done.4.refs_4_.refs_6_), channel_id=1, source_target_pairs={{0,1},{1,0},{2,3},{3,2},{4,5},{5,4},{6,7},{7,6},{8,9},{9,8},{10,11... | collective-permute-start | bytes 208904 | tf_op jit(solution)/shard_map/ppermute | solution.py:25
  17.6 0.0 collective-permute-start.7
  17.6 0.0 collective-permute-done.8.refs_3_.refs_5_
  17.6 1.6 %shard_map.98 = (f32[128,512]{1,0:T(8,128)S(1)}, f32[128,512]{1,0:T(8,128)S(1)}, f32[128,512]{1,0:T(8,128)S(1)}, f32[3,256,128]{2,1,0:T(8,128)S(1)}) custom-call(bf16[1056,128]{1,0:T(8,128)(2,1)S(1)} %get-tuple-element.36.refs_0_, bf16[1056,128]{1,0:T(8,128)(2,1)S(1)} %collective-permute-done.refs_0_.refs_1_, ...), custom_call_target="tpu_custom_call" | custom-call | flops 1000 | bytes 1000 | tf_op jit(solution)/shard_map/pallas_call | solution.py:209
  19.2 0.0 collective-permute-done.6.refs_3_.refs_8_
  19.2 1.1 %shard_map.99 = (f32[128,512]{1,0:T(8,128)S(1)}, bf16[128,512]{1,0:T(8,128)(2,1)S(1)}, bf16[128,512]{1,0:T(8,128)(2,1)S(1)}, f32[2,256,128]{2,1,0:T(8,128)S(1)}) custom-call(bf16[1056,128]{1,0:T(8,128)(2,1)S(1)} %get-tuple-element.36.refs_0_, bf16[1056,128]{1,0:T(8,128)(2,1)S(1)} %collective-permute-done.refs_0_.refs_1_, ...), custom_call_target="tpu_custom_call" | custom-call | flops 1000 | bytes 1000 | tf_op jit(solution)/shard_map/pallas_call | solution.py:209
  20.4 0.0 collective-permute-done.11.refs_0_
  20.4 0.8 %shard_map.101 = (f32[128,512]{1,0:T(8,128)S(1)}, bf16[4,256,128]{2,1,0:T(8,128)(2,1)S(1)}) custom-call(bf16[512,128]{1,0:T(8,128)(2,1)S(1)} %collective-permute-done.11.refs_0_, bf16[544,128]{1,0:T(8,128)(2,1)S(1)} %collective-permute-done.12.refs_1_, bf16[272,128]{1,0:T(8,128)(2,1)S(1)} %get-tuple-element.37.refs_1_.refs_2_, ...), custom_call_target="tpu_custom_call" | custom-call | flops 1000 | bytes 1000 | tf_op jit(solution)/shard_map/pallas_call | solution.py:209
  21.2 0.6 %collective-permute-start.14 = (bf16[4,256,128]{2,1,0:T(8,128)(2,1)S(1)}, bf16[4,256,128]{2,1,0:T(8,128)(2,1)S(1)}, u32[]{:S(2)}, u32[]{:S(2)}) collective-permute-start(bf16[4,256,128]{2,1,0:T(8,128)(2,1)S(1)} %get-tuple-element.63), channel_id=1, source_target_pairs={{0,1},{1,0},{2,3},{3,2},{4,5},{5,4},{6,7},{7,6},{8,9},{9,8},{10,11... | collective-permute-start | bytes 786440 | tf_op jit(solution)/shard_map/ppermute | solution.py:25
  21.8 0.5 %collective-permute-start.10 = (bf16[128,512]{1,0:T(8,128)(2,1)S(1)}, bf16[128,512]{1,0:T(8,128)(2,1)S(1)}, u32[]{:S(2)}, u32[]{:S(2)}) collective-permute-start(bf16[128,512]{1,0:T(8,128)(2,1)S(1)} %get-tuple-element.55), channel_id=1, source_target_pairs={{0,16},{8,24},{16,0},{24,8},{1,17},{9,25},{17,1},{25,9},{2,18},{10... | collective-permute-start | bytes 393224 | tf_op jit(solution)/shard_map/ppermute | solution.py:25
  22.3 0.7 %collective-permute-start.9 = (bf16[128,512]{1,0:T(8,128)(2,1)S(1)}, bf16[128,512]{1,0:T(8,128)(2,1)S(1)}, u32[]{:S(2)}, u32[]{:S(2)}) collective-permute-start(bf16[128,512]{1,0:T(8,128)(2,1)S(1)} %get-tuple-element.54), channel_id=1, source_target_pairs={{0,8},{8,0},{16,24},{24,16},{1,9},{9,1},{17,25},{25,17},{2,10},{10... | collective-permute-start | bytes 393224 | tf_op jit(solution)/shard_map/ppermute | solution.py:25
  23.0 0.5 %shard_map.102 = (f32[128,512]{1,0:T(8,128)S(1)}, f32[2,256,128]{2,1,0:T(8,128)S(1)}) custom-call(bf16[512,128]{1,0:T(8,128)(2,1)S(1)} %collective-permute-done.11.refs_0_, bf16[544,128]{1,0:T(8,128)(2,1)S(1)} %collective-permute-done.12.refs_1_, bf16[272,128]{1,0:T(8,128)(2,1)S(1)} %get-tuple-element.37.refs_1_.refs_2_, ...), custom_call_target="tpu_custom_call" | custom-call | flops 1000 | bytes 1000 | tf_op jit(solution)/shard_map/pallas_call | solution.py:209
  23.5 3.8 %collective-permute-start.15 = (bf16[256,128]{1,0:T(8,128)(2,1)S(1)}, bf16[256,128]{1,0:T(8,128)(2,1)S(1)}, u32[]{:S(2)}, u32[]{:S(2)}) collective-permute-start(bf16[256,128]{1,0:T(8,128)(2,1)S(1)} %get-tuple-element.66), channel_id=1, source_target_pairs={{0,6},{1,5},{2,4},{3,7},{4,2},{5,1},{6,0},{7,3},{8,14},{9,13},{10,... | collective-permute-start | bytes 196616 | tf_op jit(solution)/shard_map/ppermute | solution.py:268
  27.3 0.5 %shard_map.103 = (bf16[128,512]{1,0:T(8,128)(2,1)S(1)}, f32[2,256,128]{2,1,0:T(8,128)S(1)}) custom-call(bf16[512,128]{1,0:T(8,128)(2,1)S(1)} %collective-permute-done.11.refs_0_, bf16[544,128]{1,0:T(8,128)(2,1)S(1)} %collective-permute-done.12.refs_1_, bf16[272,128]{1,0:T(8,128)(2,1)S(1)} %get-tuple-element.37.refs_1_.refs_2_, ...), custom_call_target="tpu_custom_call" | custom-call | flops 1000 | bytes 1000 | tf_op jit(solution)/shard_map/pallas_call | solution.py:209
  27.8 1.5 %collective-permute-start.13 = (bf16[128,512]{1,0:T(8,128)(2,1)S(1)}, bf16[128,512]{1,0:T(8,128)(2,1)S(1)}, u32[]{:S(2)}, u32[]{:S(2)}) collective-permute-start(bf16[128,512]{1,0:T(8,128)(2,1)S(1)} %get-tuple-element.61), channel_id=1, source_target_pairs={{0,24},{8,16},{16,8},{24,0},{1,25},{9,17},{17,9},{25,1},{2,26},{10... | collective-permute-start | bytes 393224 | tf_op jit(solution)/shard_map/ppermute | solution.py:25
  29.4 1.6 %collective-permute-start.17 = (bf16[256,128]{1,0:T(8,128)(2,1)S(1)}, bf16[256,128]{1,0:T(8,128)(2,1)S(1)}, u32[]{:S(2)}, u32[]{:S(2)}) collective-permute-start(bf16[256,128]{1,0:T(8,128)(2,1)S(1)} %get-tuple-element.68), channel_id=1, source_target_pairs={{0,2},{1,3},{2,0},{3,1},{4,6},{5,7},{6,4},{7,5},{8,10},{9,11},{10,... | collective-permute-start | bytes 196616 | tf_op jit(solution)/shard_map/ppermute | solution.py:25
  31.0 1.7 %collective-permute-done.16.refs_1_ = bf16[256,128]{1,0:T(8,128)(2,1)S(1)} collective-permute-done((bf16[256,128]{1,0:T(8,128)(2,1)S(1)}, bf16[256,128]{1,0:T(8,128)(2,1)S(1)}, u32[]{:S(2)}, u32[]{:S(2)}) %collective-permute-start.16) | collective-permute-done | bytes 65568 | tf_op jit(solution)/shard_map/ppermute | solution.py:268
  32.7 1.1 %collective-permute-done.13.dq_far = bf16[128,512]{1,0:T(8,128)(2,1)S(1)} collective-permute-done((bf16[128,512]{1,0:T(8,128)(2,1)S(1)}, bf16[128,512]{1,0:T(8,128)(2,1)S(1)}, u32[]{:S(2)}, u32[]{:S(2)}) %collective-permute-start.13) | collective-permute-done | bytes 131104 | tf_op jit(solution)/shard_map/ppermute | solution.py:25
  33.7 0.8 %shard_map.107 = (bf16[128,512]{1,0:T(8,128)(2,1)}, bf16[128,128]{1,0:T(8,128)(2,1)}, bf16[128,128]{1,0:T(8,128)(2,1)}) custom-call(f32[128,512]{1,0:T(8,128)S(1)} %shard_map.100.dq_ref, bf16[128,512]{1,0:T(8,128)(2,1)S(1)} %collective-permute-done.13.dq_far, f32[256,128]{1,0:T(8,128)S(1)} %shard_map.106.dkv_ref, ...), custom_call_target="tpu_custom_call" | custom-call | flops 1000 | bytes 1000 | tf_op jit(solution)/shard_map/pallas_call | solution.py:343
  (20 shorter events, 0.2 us)
Async XLA Ops:
  2.0 10.6 %collective-permute-start = (bf16[1056,128]{1,0:T(8,128)(2,1)S(1)}, bf16[1056,128]{1,0:T(8,128)(2,1)S(1)}, u32[]{:S(2)}, u32[]{:S(2)}) collective-permute-start(bf16[1056,128]{1,0:T(8,128)(2,1)S(1)} %get-tuple-element.36.refs_0_), channel_id=1, source_target_pairs={{0,8},{8,0},{16,24},{24,16},{1,9},{9,1},{17,25},{25,17},{2,10},{10... | collective-permute-start | bytes 811016 | tf_op jit(solution)/shard_map/ppermute | solution.py:25
  5.0 9.0 %collective-permute-start.3 = (bf16[1056,128]{1,0:T(8,128)(2,1)S(1)}, bf16[1056,128]{1,0:T(8,128)(2,1)S(1)}, u32[]{:S(2)}, u32[]{:S(2)}) collective-permute-start(bf16[1056,128]{1,0:T(8,128)(2,1)S(1)} %get-tuple-element.36.refs_0_), channel_id=1, source_target_pairs={{0,16},{8,24},{16,0},{24,8},{1,17},{9,25},{17,1},{25,9},{2,18},{10... | collective-permute-start | bytes 811016 | tf_op jit(solution)/shard_map/ppermute | solution.py:25
  6.5 4.1 %collective-permute-start.1 = (bf16[272,128]{1,0:T(8,128)(2,1)S(1)}, bf16[272,128]{1,0:T(8,128)(2,1)S(1)}, u32[]{:S(2)}, u32[]{:S(2)}) collective-permute-start(bf16[272,128]{1,0:T(8,128)(2,1)S(1)} %get-tuple-element.37.refs_1_.refs_2_), channel_id=1, source_target_pairs={{0,1},{1,0},{2,3},{3,2},{4,5},{5,4},{6,7},{7,6},{8,9},{9,8},{10,11... | collective-permute-start | bytes 208904 | tf_op jit(solution)/shard_map/ppermute | solution.py:25
  6.5 5.4 %collective-permute-start.2 = (bf16[272,128]{1,0:T(8,128)(2,1)S(1)}, bf16[272,128]{1,0:T(8,128)(2,1)S(1)}, u32[]{:S(2)}, u32[]{:S(2)}) collective-permute-start(bf16[272,128]{1,0:T(8,128)(2,1)S(1)} %get-tuple-element.37.refs_1_.refs_2_), channel_id=1, source_target_pairs={{0,2},{1,3},{2,0},{3,1},{4,6},{5,7},{6,4},{7,5},{8,10},{9,11},{10,... | collective-permute-start | bytes 208904 | tf_op jit(solution)/shard_map/ppermute | solution.py:25
  8.1 8.2 %collective-permute-start.4 = (bf16[272,128]{1,0:T(8,128)(2,1)S(1)}, bf16[272,128]{1,0:T(8,128)(2,1)S(1)}, u32[]{:S(2)}, u32[]{:S(2)}) collective-permute-start(bf16[272,128]{1,0:T(8,128)(2,1)S(1)} %get-tuple-element.37.refs_1_.refs_2_), channel_id=1, source_target_pairs={{0,6},{1,5},{2,4},{3,7},{4,2},{5,1},{6,0},{7,3},{8,14},{9,13},{10,... | collective-permute-start | bytes 208904 | tf_op jit(solution)/shard_map/ppermute | solution.py:268
  10.6 6.2 %collective-permute-start.5 = (bf16[272,128]{1,0:T(8,128)(2,1)S(1)}, bf16[272,128]{1,0:T(8,128)(2,1)S(1)}, u32[]{:S(2)}, u32[]{:S(2)}) collective-permute-start(bf16[272,128]{1,0:T(8,128)(2,1)S(1)} %collective-permute-done.1.refs_2_.refs_3_), channel_id=1, source_target_pairs={{0,6},{1,5},{2,4},{3,7},{4,2},{5,1},{6,0},{7,3},{8,14},{9,13},{10,... | collective-permute-start | bytes 208904 | tf_op jit(solution)/shard_map/ppermute | solution.py:268
  12.6 7.8 %collective-permute-start.12 = (bf16[544,128]{1,0:T(8,128)(2,1)S(1)}, bf16[544,128]{1,0:T(8,128)(2,1)S(1)}, u32[]{:S(2)}, u32[]{:S(2)}) collective-permute-start(bf16[544,128]{1,0:T(8,128)(2,1)S(1)} %slice.7), channel_id=1, source_target_pairs={{0,16},{8,24},{16,0},{24,8},{1,17},{9,25},{17,1},{25,9},{2,18},{10... | collective-permute-start | bytes 417800 | tf_op jit(solution)/shard_map/ppermute | solution.py:25
  14.0 6.4 %collective-permute-start.11 = (bf16[512,128]{1,0:T(8,128)(2,1)S(1)}, bf16[512,128]{1,0:T(8,128)(2,1)S(1)}, u32[]{:S(2)}, u32[]{:S(2)}) collective-permute-start(bf16[512,128]{1,0:T(8,128)(2,1)S(1)} %slice.6), channel_id=1, source_target_pairs={{0,8},{8,0},{16,24},{24,16},{1,9},{9,1},{17,25},{25,17},{2,10},{10... | collective-permute-start | bytes 393224 | tf_op jit(solution)/shard_map/ppermute | solution.py:25
  15.6 2.0 %collective-permute-start.8 = (bf16[272,128]{1,0:T(8,128)(2,1)S(1)}, bf16[272,128]{1,0:T(8,128)(2,1)S(1)}, u32[]{:S(2)}, u32[]{:S(2)}) collective-permute-start(bf16[272,128]{1,0:T(8,128)(2,1)S(1)} %collective-permute-done.2.refs_3_.refs_4_), channel_id=1, source_target_pairs={{0,1},{1,0},{2,3},{3,2},{4,5},{5,4},{6,7},{7,6},{8,9},{9,8},{10,11... | collective-permute-start | bytes 208904 | tf_op jit(solution)/shard_map/ppermute | solution.py:25
  16.8 2.4 %collective-permute-start.6 = (bf16[272,128]{1,0:T(8,128)(2,1)S(1)}, bf16[272,128]{1,0:T(8,128)(2,1)S(1)}, u32[]{:S(2)}, u32[]{:S(2)}) collective-permute-start(bf16[272,128]{1,0:T(8,128)(2,1)S(1)} %collective-permute-done.4.refs_4_.refs_6_), channel_id=1, source_target_pairs={{0,1},{1,0},{2,3},{3,2},{4,5},{5,4},{6,7},{7,6},{8,9},{9,8},{10,11... | collective-permute-start | bytes 208904 | tf_op jit(solution)/shard_map/ppermute | solution.py:25
  17.6 1.6 %collective-permute-start.7 = (bf16[272,128]{1,0:T(8,128)(2,1)S(1)}, bf16[272,128]{1,0:T(8,128)(2,1)S(1)}, u32[]{:S(2)}, u32[]{:S(2)}) collective-permute-start(bf16[272,128]{1,0:T(8,128)(2,1)S(1)} %collective-permute-done.5.refs_5_.refs_7_), channel_id=1, source_target_pairs={{0,1},{1,0},{2,3},{3,2},{4,5},{5,4},{6,7},{7,6},{8,9},{9,8},{10,11... | collective-permute-start | bytes 208904 | tf_op jit(solution)/shard_map/ppermute | solution.py:25
  21.2 2.3 %collective-permute-start.14 = (bf16[4,256,128]{2,1,0:T(8,128)(2,1)S(1)}, bf16[4,256,128]{2,1,0:T(8,128)(2,1)S(1)}, u32[]{:S(2)}, u32[]{:S(2)}) collective-permute-start(bf16[4,256,128]{2,1,0:T(8,128)(2,1)S(1)} %get-tuple-element.63), channel_id=1, source_target_pairs={{0,1},{1,0},{2,3},{3,2},{4,5},{5,4},{6,7},{7,6},{8,9},{9,8},{10,11... | collective-permute-start | bytes 786440 | tf_op jit(solution)/shard_map/ppermute | solution.py:25
  21.8 7.5 %collective-permute-start.10 = (bf16[128,512]{1,0:T(8,128)(2,1)S(1)}, bf16[128,512]{1,0:T(8,128)(2,1)S(1)}, u32[]{:S(2)}, u32[]{:S(2)}) collective-permute-start(bf16[128,512]{1,0:T(8,128)(2,1)S(1)} %get-tuple-element.55), channel_id=1, source_target_pairs={{0,16},{8,24},{16,0},{24,8},{1,17},{9,25},{17,1},{25,9},{2,18},{10... | collective-permute-start | bytes 393224 | tf_op jit(solution)/shard_map/ppermute | solution.py:25
  22.3 7.0 %collective-permute-start.9 = (bf16[128,512]{1,0:T(8,128)(2,1)S(1)}, bf16[128,512]{1,0:T(8,128)(2,1)S(1)}, u32[]{:S(2)}, u32[]{:S(2)}) collective-permute-start(bf16[128,512]{1,0:T(8,128)(2,1)S(1)} %get-tuple-element.54), channel_id=1, source_target_pairs={{0,8},{8,0},{16,24},{24,16},{1,9},{9,1},{17,25},{25,17},{2,10},{10... | collective-permute-start | bytes 393224 | tf_op jit(solution)/shard_map/ppermute | solution.py:25
  23.5 7.4 %collective-permute-start.15 = (bf16[256,128]{1,0:T(8,128)(2,1)S(1)}, bf16[256,128]{1,0:T(8,128)(2,1)S(1)}, u32[]{:S(2)}, u32[]{:S(2)}) collective-permute-start(bf16[256,128]{1,0:T(8,128)(2,1)S(1)} %get-tuple-element.66), channel_id=1, source_target_pairs={{0,6},{1,5},{2,4},{3,7},{4,2},{5,1},{6,0},{7,3},{8,14},{9,13},{10,... | collective-permute-start | bytes 196616 | tf_op jit(solution)/shard_map/ppermute | solution.py:268
  27.3 5.3 %collective-permute-start.16 = (bf16[256,128]{1,0:T(8,128)(2,1)S(1)}, bf16[256,128]{1,0:T(8,128)(2,1)S(1)}, u32[]{:S(2)}, u32[]{:S(2)}) collective-permute-start(bf16[256,128]{1,0:T(8,128)(2,1)S(1)} %get-tuple-element.67), channel_id=1, source_target_pairs={{0,4},{1,7},{2,6},{3,5},{4,0},{5,3},{6,2},{7,1},{8,12},{9,15},{10,... | collective-permute-start | bytes 196616 | tf_op jit(solution)/shard_map/ppermute | solution.py:268
  27.8 5.9 %collective-permute-start.13 = (bf16[128,512]{1,0:T(8,128)(2,1)S(1)}, bf16[128,512]{1,0:T(8,128)(2,1)S(1)}, u32[]{:S(2)}, u32[]{:S(2)}) collective-permute-start(bf16[128,512]{1,0:T(8,128)(2,1)S(1)} %get-tuple-element.61), channel_id=1, source_target_pairs={{0,24},{8,16},{16,8},{24,0},{1,25},{9,17},{17,9},{25,1},{2,26},{10... | collective-permute-start | bytes 393224 | tf_op jit(solution)/shard_map/ppermute | solution.py:25
  29.4 4.4 %collective-permute-start.17 = (bf16[256,128]{1,0:T(8,128)(2,1)S(1)}, bf16[256,128]{1,0:T(8,128)(2,1)S(1)}, u32[]{:S(2)}, u32[]{:S(2)}) collective-permute-start(bf16[256,128]{1,0:T(8,128)(2,1)S(1)} %get-tuple-element.68), channel_id=1, source_target_pairs={{0,2},{1,3},{2,0},{3,1},{4,6},{5,7},{6,4},{7,5},{8,10},{9,11},{10,... | collective-permute-start | bytes 196616 | tf_op jit(solution)/shard_map/ppermute | solution.py:25

commit v16 on v15

--- a/solution.py
+++ b/solution.py
@@ -250,8 +250,11 @@
     )(own, *got)
 
 
-def final_kernel(rows, heads, scale, dq_ref, dq_far, dkv_ref, dkv_near, gq_ref, gk_ref, gv_ref):
-    dkv = dkv_ref[...] + dkv_near[...].astype(F32)
+def final_kernel(rows, heads, scale, dq_ref, dq_far, dkv_ref, *refs):
+    late, (gq_ref, gk_ref, gv_ref) = refs[:-3], refs[-3:]
+    dkv = dkv_ref[...]
+    for ref in late:
+        dkv = dkv + ref[...].astype(F32)
     gk_ref[...] = (scale * dkv[:rows]).astype(BF)
     gv_ref[...] = dkv[rows:].astype(BF)
     dq = dq_ref[...] + dq_far[...].astype(F32)
@@ -332,22 +335,20 @@
 
     got = [swapped(dq, "outer", s + 1) for s, dq in enumerate(dqs)]
     dq_far = swapped(dq_last, "outer", nq - 1)
-    dkv = []
-    for t in range(1, nz // 2):
-        dkv.append(crossed(far[2 * t - 2], t, False))
-        dkv.append(crossed(far[2 * t - 1], t, True))
-    dkv_near = swapped(dkv_near, "inner", 2)
+    dkv = [crossed(far[2 * t - 2], t, False) for t in range(1, nz // 2)]
+    late = [crossed(far[2 * t - 1], t, True) for t in range(1, nz // 2)]
+    late.append(swapped(dkv_near, "inner", 2))
 
     dkv_sum = sum_call(dkv_own, dkv, 1_500_000_000)
     dq_sum = sum_call(dq_own, got, 100_000_000)
     return pl.pallas_call(
         functools.partial(final_kernel, rows, heads, scale),
         out_shape=(sds((rows, heads * width), BF), sds((rows, width), BF), sds((rows, width), BF)),
-        in_specs=[VMEM] * 4,
+        in_specs=[VMEM] * (3 + len(late)),
         out_specs=(VMEM,) * 3,
         compiler_params=SMALL,
         cost_estimate=QUICK,
-    )(dq_sum, dq_far, dkv_sum, dkv_near)
+    )(dq_sum, dq_far, dkv_sum, *late)
 
 
 def solution(mesh):

time: 34.7 us -> 35.9 us (1.035)
  starting transfers between devices: 21.6 us -> 22.6 us
    ppermute x14, waiting for transfers between devices: 1.12 us -> 1.94 us  [swapped(): return lax.ppermute(block, axis, pairs)]
    ppermute x4, waiting for transfers between devices: 2.19 us -> 1.61 us  [crossed(): return lax.ppermute(block, 'inner', pairs)]
    ppermute x4, starting transfers between devices: 7.65 us -> 8.13 us  [crossed(): return lax.ppermute(block, 'inner', pairs)]
    ppermute x14, starting transfers between devices: 14 us -> 14.4 us  [swapped(): return lax.ppermute(block, axis, pairs)]
  transfers between devices with their start and end apart: 18 -> 18, of which waited for: 3 -> 4; matrix products, arithmetic and copies ran while one was open for 0% -> 0% of each run, Pallas kernels for 17% -> 16%
where the time goes in v16:
time: 35.9 us; the launch traced here: 35.7 us
  starting transfers between devices  22.6 us (63%)
  Pallas kernels  8.75 us (24%)
  waiting for transfers between devices  3.55 us (10%)
  between operations  0.8 us (2%)
    ppermute x14, starting transfers between devices, swapped(): return lax.ppermute(block, axis, pairs)  14.4 us
    ppermute x4, starting transfers between devices, crossed(): return lax.ppermute(block, 'inner', pairs)  8.13 us
    pallas_call x8, Pallas kernels, blocks_call(): pl.pallas_call(functools.partial(blocks_kernel, plan, rows, heads, scale)...  6.51 us
    ppermute x14, waiting for transfers between devices, swapped(): return lax.ppermute(block, axis, pairs)  1.94 us
    ppermute x4, waiting for transfers between devices, crossed(): return lax.ppermute(block, 'inner', pairs)  1.61 us
    pallas_call x1, Pallas kernels, on_device(): pl.pallas_call(pack_kernel, out_shape=(sds((2 * hr + 32, width), BF), sds...  1.34 us
    pallas_call x1, Pallas kernels, on_device(): pl.pallas_call(functools.partial(final_kernel, rows, heads, scale), out_s...  0.77 us
  transfers between devices with their start and end apart: 18, of which 4 were waited for; matrix products, arithmetic and copies ran while one was open for 0% of the time, Pallas kernels for 16%

profile of v16, /device:TPU:0, one launch (start us, length us, event | category | flops | bytes accessed | tf_op | source)
XLA Modules:
  0.0 35.7 jit_solution(11093311321617517937)
XLA Ops:
  0.6 1.3 %shard_map.94 = (bf16[1056,128]{1,0:T(8,128)(2,1)S(1)}, bf16[272,128]{1,0:T(8,128)(2,1)S(1)}) custom-call(bf16[128,512]{1,0:T(8,128)(2,1)} %q_ref.1, bf16[128,128]{1,0:T(8,128)(2,1)} %k_ref.1, bf16[128,128]{1,0:T(8,128)(2,1)} %v_ref.1, bf16[128,512]{1,0:T(8,128)(2,1)} %o_ref.1, bf16[128,512]{1,0:T(8,128)(2,1)} %g_ref.1, f32[4,128]{1,0:T(4,128)} %lse_ref.1, ...), custom_call_target="tpu_custom_call" | custom-call | flops 1000 | bytes 1000 | tf_op jit(solution)/shard_map/pallas_call | solution.py:283
  2.0 3.0 %collective-permute-start = (bf16[1056,128]{1,0:T(8,128)(2,1)S(1)}, bf16[1056,128]{1,0:T(8,128)(2,1)S(1)}, u32[]{:S(2)}, u32[]{:S(2)}) collective-permute-start(bf16[1056,128]{1,0:T(8,128)(2,1)S(1)} %get-tuple-element.36.refs_0_), channel_id=1, source_target_pairs={{0,8},{8,0},{16,24},{24,16},{1,9},{9,1},{17,25},{25,17},{2,10},{10... | collective-permute-start | bytes 811016 | tf_op jit(solution)/shard_map/ppermute | solution.py:25
  5.0 1.5 %collective-permute-start.3 = (bf16[1056,128]{1,0:T(8,128)(2,1)S(1)}, bf16[1056,128]{1,0:T(8,128)(2,1)S(1)}, u32[]{:S(2)}, u32[]{:S(2)}) collective-permute-start(bf16[1056,128]{1,0:T(8,128)(2,1)S(1)} %get-tuple-element.36.refs_0_), channel_id=1, source_target_pairs={{0,16},{8,24},{16,0},{24,8},{1,17},{9,25},{17,1},{25,9},{2,18},{10... | collective-permute-start | bytes 811016 | tf_op jit(solution)/shard_map/ppermute | solution.py:25
  6.5 0.0 collective-permute-start.1
  6.5 1.6 %collective-permute-start.2 = (bf16[272,128]{1,0:T(8,128)(2,1)S(1)}, bf16[272,128]{1,0:T(8,128)(2,1)S(1)}, u32[]{:S(2)}, u32[]{:S(2)}) collective-permute-start(bf16[272,128]{1,0:T(8,128)(2,1)S(1)} %get-tuple-element.37.refs_1_.refs_2_), channel_id=1, source_target_pairs={{0,2},{1,3},{2,0},{3,1},{4,6},{5,7},{6,4},{7,5},{8,10},{9,11},{10,... | collective-permute-start | bytes 208904 | tf_op jit(solution)/shard_map/ppermute | solution.py:25
  8.1 2.5 %collective-permute-start.4 = (bf16[272,128]{1,0:T(8,128)(2,1)S(1)}, bf16[272,128]{1,0:T(8,128)(2,1)S(1)}, u32[]{:S(2)}, u32[]{:S(2)}) collective-permute-start(bf16[272,128]{1,0:T(8,128)(2,1)S(1)} %get-tuple-element.37.refs_1_.refs_2_), channel_id=1, source_target_pairs={{0,6},{1,5},{2,4},{3,7},{4,2},{5,1},{6,0},{7,3},{8,14},{9,13},{10,... | collective-permute-start | bytes 208904 | tf_op jit(solution)/shard_map/ppermute | solution.py:271
  10.6 0.0 collective-permute-done.1.refs_2_.refs_3_
  10.6 1.3 %collective-permute-start.5 = (bf16[272,128]{1,0:T(8,128)(2,1)S(1)}, bf16[272,128]{1,0:T(8,128)(2,1)S(1)}, u32[]{:S(2)}, u32[]{:S(2)}) collective-permute-start(bf16[272,128]{1,0:T(8,128)(2,1)S(1)} %collective-permute-done.1.refs_2_.refs_3_), channel_id=1, source_target_pairs={{0,6},{1,5},{2,4},{3,7},{4,2},{5,1},{6,0},{7,3},{8,14},{9,13},{10,... | collective-permute-start | bytes 208904 | tf_op jit(solution)/shard_map/ppermute | solution.py:271
  11.9 0.7 %shard_map.95 = (f32[128,512]{1,0:T(8,128)S(1)}, f32[3,256,128]{2,1,0:T(8,128)S(1)}) custom-call(bf16[1056,128]{1,0:T(8,128)(2,1)S(1)} %get-tuple-element.36.refs_0_, bf16[272,128]{1,0:T(8,128)(2,1)S(1)} %get-tuple-element.37.refs_1_.refs_2_, bf16[272,128]{1,0:T(8,128)(2,1)S(1)} %collective-permute-done.1.refs_2_.refs_3_, ...), custom_call_target="tpu_custom_call" | custom-call | flops 1000 | bytes 1000 | tf_op jit(solution)/shard_map/pallas_call | solution.py:209
  12.6 0.7 %collective-permute-start.12 = (bf16[544,128]{1,0:T(8,128)(2,1)S(1)}, bf16[544,128]{1,0:T(8,128)(2,1)S(1)}, u32[]{:S(2)}, u32[]{:S(2)}) collective-permute-start(bf16[544,128]{1,0:T(8,128)(2,1)S(1)} %slice.7), channel_id=1, source_target_pairs={{0,16},{8,24},{16,0},{24,8},{1,17},{9,25},{17,1},{25,9},{2,18},{10... | collective-permute-start | bytes 417800 | tf_op jit(solution)/shard_map/ppermute | solution.py:25
  13.3 0.7 %shard_map.96 = (f32[128,512]{1,0:T(8,128)S(1)}, f32[3,256,128]{2,1,0:T(8,128)S(1)}) custom-call(bf16[1056,128]{1,0:T(8,128)(2,1)S(1)} %collective-permute-done.refs_0_.refs_1_, bf16[272,128]{1,0:T(8,128)(2,1)S(1)} %get-tuple-element.37.refs_1_.refs_2_, bf16[272,128]{1,0:T(8,128)(2,1)S(1)} %collective-permute-done.1.refs_2_.refs_3_, ...), custom_call_target="tpu_custom_call" | custom-call | flops 1000 | bytes 1000 | tf_op jit(solution)/shard_map/pallas_call | solution.py:209
  14.0 1.6 %collective-permute-start.11 = (bf16[512,128]{1,0:T(8,128)(2,1)S(1)}, bf16[512,128]{1,0:T(8,128)(2,1)S(1)}, u32[]{:S(2)}, u32[]{:S(2)}) collective-permute-start(bf16[512,128]{1,0:T(8,128)(2,1)S(1)} %slice.6), channel_id=1, source_target_pairs={{0,8},{8,0},{16,24},{24,16},{1,9},{9,1},{17,25},{25,17},{2,10},{10... | collective-permute-start | bytes 393224 | tf_op jit(solution)/shard_map/ppermute | solution.py:25
  15.6 0.7 %shard_map.97 = (f32[128,512]{1,0:T(8,128)S(1)}, f32[3,256,128]{2,1,0:T(8,128)S(1)}) custom-call(bf16[1056,128]{1,0:T(8,128)(2,1)S(1)} %collective-permute-done.3.refs_0_.refs_2_, bf16[272,128]{1,0:T(8,128)(2,1)S(1)} %get-tuple-element.37.refs_1_.refs_2_, bf16[272,128]{1,0:T(8,128)(2,1)S(1)} %collective-permute-done.1.refs_2_.refs_3_, ...), custom_call_target="tpu_custom_call" | custom-call | flops 1000 | bytes 1000 | tf_op jit(solution)/shard_map/pallas_call | solution.py:209
  16.3 0.5 %collective-permute-done.5.refs_5_.refs_7_ = bf16[272,128]{1,0:T(8,128)(2,1)S(1)} collective-permute-done((bf16[272,128]{1,0:T(8,128)(2,1)S(1)}, bf16[272,128]{1,0:T(8,128)(2,1)S(1)}, u32[]{:S(2)}, u32[]{:S(2)}) %collective-permute-start.5) | collective-permute-done | bytes 69664 | tf_op jit(solution)/shard_map/ppermute | solution.py:271
  16.8 0.8 %collective-permute-start.6 = (bf16[272,128]{1,0:T(8,128)(2,1)S(1)}, bf16[272,128]{1,0:T(8,128)(2,1)S(1)}, u32[]{:S(2)}, u32[]{:S(2)}) collective-permute-start(bf16[272,128]{1,0:T(8,128)(2,1)S(1)} %collective-permute-done.4.refs_4_.refs_6_), channel_id=1, source_target_pairs={{0,1},{1,0},{2,3},{3,2},{4,5},{5,4},{6,7},{7,6},{8,9},{9,8},{10,11... | collective-permute-start | bytes 208904 | tf_op jit(solution)/shard_map/ppermute | solution.py:25
  17.6 0.0 collective-permute-start.7
  17.6 1.6 %shard_map.98 = (f32[128,512]{1,0:T(8,128)S(1)}, f32[128,512]{1,0:T(8,128)S(1)}, f32[128,512]{1,0:T(8,128)S(1)}, f32[3,256,128]{2,1,0:T(8,128)S(1)}) custom-call(bf16[1056,128]{1,0:T(8,128)(2,1)S(1)} %get-tuple-element.36.refs_0_, bf16[1056,128]{1,0:T(8,128)(2,1)S(1)} %collective-permute-done.refs_0_.refs_1_, ...), custom_call_target="tpu_custom_call" | custom-call | flops 1000 | bytes 1000 | tf_op jit(solution)/shard_map/pallas_call | solution.py:209
  19.2 1.1 %shard_map.99 = (f32[128,512]{1,0:T(8,128)S(1)}, bf16[128,512]{1,0:T(8,128)(2,1)S(1)}, bf16[128,512]{1,0:T(8,128)(2,1)S(1)}, f32[2,256,128]{2,1,0:T(8,128)S(1)}) custom-call(bf16[1056,128]{1,0:T(8,128)(2,1)S(1)} %get-tuple-element.36.refs_0_, bf16[1056,128]{1,0:T(8,128)(2,1)S(1)} %collective-permute-done.refs_0_.refs_1_, ...), custom_call_target="tpu_custom_call" | custom-call | flops 1000 | bytes 1000 | tf_op jit(solution)/shard_map/pallas_call | solution.py:209
  20.4 0.8 %shard_map.101 = (f32[128,512]{1,0:T(8,128)S(1)}, bf16[4,256,128]{2,1,0:T(8,128)(2,1)S(1)}) custom-call(bf16[512,128]{1,0:T(8,128)(2,1)S(1)} %collective-permute-done.11.refs_0_, bf16[544,128]{1,0:T(8,128)(2,1)S(1)} %collective-permute-done.12.refs_1_, bf16[272,128]{1,0:T(8,128)(2,1)S(1)} %get-tuple-element.37.refs_1_.refs_2_, ...), custom_call_target="tpu_custom_call" | custom-call | flops 1000 | bytes 1000 | tf_op jit(solution)/shard_map/pallas_call | solution.py:209
  21.2 0.6 %collective-permute-start.14 = (bf16[4,256,128]{2,1,0:T(8,128)(2,1)S(1)}, bf16[4,256,128]{2,1,0:T(8,128)(2,1)S(1)}, u32[]{:S(2)}, u32[]{:S(2)}) collective-permute-start(bf16[4,256,128]{2,1,0:T(8,128)(2,1)S(1)} %get-tuple-element.63), channel_id=1, source_target_pairs={{0,1},{1,0},{2,3},{3,2},{4,5},{5,4},{6,7},{7,6},{8,9},{9,8},{10,11... | collective-permute-start | bytes 786440 | tf_op jit(solution)/shard_map/ppermute | solution.py:25
  21.8 0.5 %collective-permute-start.10 = (bf16[128,512]{1,0:T(8,128)(2,1)S(1)}, bf16[128,512]{1,0:T(8,128)(2,1)S(1)}, u32[]{:S(2)}, u32[]{:S(2)}) collective-permute-start(bf16[128,512]{1,0:T(8,128)(2,1)S(1)} %get-tuple-element.55), channel_id=1, source_target_pairs={{0,16},{8,24},{16,0},{24,8},{1,17},{9,25},{17,1},{25,9},{2,18},{10... | collective-permute-start | bytes 393224 | tf_op jit(solution)/shard_map/ppermute | solution.py:25
  22.3 0.7 %collective-permute-start.9 = (bf16[128,512]{1,0:T(8,128)(2,1)S(1)}, bf16[128,512]{1,0:T(8,128)(2,1)S(1)}, u32[]{:S(2)}, u32[]{:S(2)}) collective-permute-start(bf16[128,512]{1,0:T(8,128)(2,1)S(1)} %get-tuple-element.54), channel_id=1, source_target_pairs={{0,8},{8,0},{16,24},{24,16},{1,9},{9,1},{17,25},{25,17},{2,10},{10... | collective-permute-start | bytes 393224 | tf_op jit(solution)/shard_map/ppermute | solution.py:25
  23.0 0.5 %shard_map.102 = (f32[128,512]{1,0:T(8,128)S(1)}, f32[2,256,128]{2,1,0:T(8,128)S(1)}) custom-call(bf16[512,128]{1,0:T(8,128)(2,1)S(1)} %collective-permute-done.11.refs_0_, bf16[544,128]{1,0:T(8,128)(2,1)S(1)} %collective-permute-done.12.refs_1_, bf16[272,128]{1,0:T(8,128)(2,1)S(1)} %get-tuple-element.37.refs_1_.refs_2_, ...), custom_call_target="tpu_custom_call" | custom-call | flops 1000 | bytes 1000 | tf_op jit(solution)/shard_map/pallas_call | solution.py:209
  23.5 3.8 %collective-permute-start.15 = (bf16[256,128]{1,0:T(8,128)(2,1)S(1)}, bf16[256,128]{1,0:T(8,128)(2,1)S(1)}, u32[]{:S(2)}, u32[]{:S(2)}) collective-permute-start(bf16[256,128]{1,0:T(8,128)(2,1)S(1)} %get-tuple-element.66), channel_id=1, source_target_pairs={{0,6},{1,5},{2,4},{3,7},{4,2},{5,1},{6,0},{7,3},{8,14},{9,13},{10,... | collective-permute-start | bytes 196616 | tf_op jit(solution)/shard_map/ppermute | solution.py:271
  27.3 0.5 %shard_map.103 = (bf16[128,512]{1,0:T(8,128)(2,1)S(1)}, f32[2,256,128]{2,1,0:T(8,128)S(1)}) custom-call(bf16[512,128]{1,0:T(8,128)(2,1)S(1)} %collective-permute-done.11.refs_0_, bf16[544,128]{1,0:T(8,128)(2,1)S(1)} %collective-permute-done.12.refs_1_, bf16[272,128]{1,0:T(8,128)(2,1)S(1)} %get-tuple-element.37.refs_1_.refs_2_, ...), custom_call_target="tpu_custom_call" | custom-call | flops 1000 | bytes 1000 | tf_op jit(solution)/shard_map/pallas_call | solution.py:209
  27.8 1.5 %collective-permute-start.13 = (bf16[128,512]{1,0:T(8,128)(2,1)S(1)}, bf16[128,512]{1,0:T(8,128)(2,1)S(1)}, u32[]{:S(2)}, u32[]{:S(2)}) collective-permute-start(bf16[128,512]{1,0:T(8,128)(2,1)S(1)} %get-tuple-element.61), channel_id=1, source_target_pairs={{0,24},{8,16},{16,8},{24,0},{1,25},{9,17},{17,9},{25,1},{2,26},{10... | collective-permute-start | bytes 393224 | tf_op jit(solution)/shard_map/ppermute | solution.py:25
  29.3 0.5 %collective-permute-start.16 = (bf16[256,128]{1,0:T(8,128)(2,1)S(1)}, bf16[256,128]{1,0:T(8,128)(2,1)S(1)}, u32[]{:S(2)}, u32[]{:S(2)}) collective-permute-start(bf16[256,128]{1,0:T(8,128)(2,1)S(1)} %get-tuple-element.67), channel_id=1, source_target_pairs={{0,4},{1,7},{2,6},{3,5},{4,0},{5,3},{6,2},{7,1},{8,12},{9,15},{10,... | collective-permute-start | bytes 196616 | tf_op jit(solution)/shard_map/ppermute | solution.py:271
  29.9 2.0 %collective-permute-start.17 = (bf16[256,128]{1,0:T(8,128)(2,1)S(1)}, bf16[256,128]{1,0:T(8,128)(2,1)S(1)}, u32[]{:S(2)}, u32[]{:S(2)}) collective-permute-start(bf16[256,128]{1,0:T(8,128)(2,1)S(1)} %get-tuple-element.68), channel_id=1, source_target_pairs={{0,2},{1,3},{2,0},{3,1},{4,6},{5,7},{6,4},{7,5},{8,10},{9,11},{10,... | collective-permute-start | bytes 196616 | tf_op jit(solution)/shard_map/ppermute | solution.py:25
  31.9 1.8 %collective-permute-done.13.dq_far = bf16[128,512]{1,0:T(8,128)(2,1)S(1)} collective-permute-done((bf16[128,512]{1,0:T(8,128)(2,1)S(1)}, bf16[128,512]{1,0:T(8,128)(2,1)S(1)}, u32[]{:S(2)}, u32[]{:S(2)}) %collective-permute-start.13) | collective-permute-done | bytes 131104 | tf_op jit(solution)/shard_map/ppermute | solution.py:25
  33.7 1.1 %collective-permute-done.16.refs_0_ = bf16[256,128]{1,0:T(8,128)(2,1)S(1)} collective-permute-done((bf16[256,128]{1,0:T(8,128)(2,1)S(1)}, bf16[256,128]{1,0:T(8,128)(2,1)S(1)}, u32[]{:S(2)}, u32[]{:S(2)}) %collective-permute-start.16) | collective-permute-done | bytes 65568 | tf_op jit(solution)/shard_map/ppermute | solution.py:271
  34.8 0.1 collective-permute-done.17.refs_1_
  34.9 0.8 %shard_map.107 = (bf16[128,512]{1,0:T(8,128)(2,1)}, bf16[128,128]{1,0:T(8,128)(2,1)}, bf16[128,128]{1,0:T(8,128)(2,1)}) custom-call(f32[128,512]{1,0:T(8,128)S(1)} %shard_map.100.dq_ref, bf16[128,512]{1,0:T(8,128)(2,1)S(1)} %collective-permute-done.13.dq_far, f32[256,128]{1,0:T(8,128)S(1)} %shard_map.106.dkv_ref, ...), custom_call_target="tpu_custom_call" | custom-call | flops 1000 | bytes 1000 | tf_op jit(solution)/shard_map/pallas_call | solution.py:344
  (20 shorter events, 0.2 us)
Async XLA Ops:
  2.0 10.6 %collective-permute-start = (bf16[1056,128]{1,0:T(8,128)(2,1)S(1)}, bf16[1056,128]{1,0:T(8,128)(2,1)S(1)}, u32[]{:S(2)}, u32[]{:S(2)}) collective-permute-start(bf16[1056,128]{1,0:T(8,128)(2,1)S(1)} %get-tuple-element.36.refs_0_), channel_id=1, source_target_pairs={{0,8},{8,0},{16,24},{24,16},{1,9},{9,1},{17,25},{25,17},{2,10},{10... | collective-permute-start | bytes 811016 | tf_op jit(solution)/shard_map/ppermute | solution.py:25
  5.0 9.0 %collective-permute-start.3 = (bf16[1056,128]{1,0:T(8,128)(2,1)S(1)}, bf16[1056,128]{1,0:T(8,128)(2,1)S(1)}, u32[]{:S(2)}, u32[]{:S(2)}) collective-permute-start(bf16[1056,128]{1,0:T(8,128)(2,1)S(1)} %get-tuple-element.36.refs_0_), channel_id=1, source_target_pairs={{0,16},{8,24},{16,0},{24,8},{1,17},{9,25},{17,1},{25,9},{2,18},{10... | collective-permute-start | bytes 811016 | tf_op jit(solution)/shard_map/ppermute | solution.py:25
  6.5 4.1 %collective-permute-start.1 = (bf16[272,128]{1,0:T(8,128)(2,1)S(1)}, bf16[272,128]{1,0:T(8,128)(2,1)S(1)}, u32[]{:S(2)}, u32[]{:S(2)}) collective-permute-start(bf16[272,128]{1,0:T(8,128)(2,1)S(1)} %get-tuple-element.37.refs_1_.refs_2_), channel_id=1, source_target_pairs={{0,1},{1,0},{2,3},{3,2},{4,5},{5,4},{6,7},{7,6},{8,9},{9,8},{10,11... | collective-permute-start | bytes 208904 | tf_op jit(solution)/shard_map/ppermute | solution.py:25
  6.5 5.4 %collective-permute-start.2 = (bf16[272,128]{1,0:T(8,128)(2,1)S(1)}, bf16[272,128]{1,0:T(8,128)(2,1)S(1)}, u32[]{:S(2)}, u32[]{:S(2)}) collective-permute-start(bf16[272,128]{1,0:T(8,128)(2,1)S(1)} %get-tuple-element.37.refs_1_.refs_2_), channel_id=1, source_target_pairs={{0,2},{1,3},{2,0},{3,1},{4,6},{5,7},{6,4},{7,5},{8,10},{9,11},{10,... | collective-permute-start | bytes 208904 | tf_op jit(solution)/shard_map/ppermute | solution.py:25
  8.1 8.2 %collective-permute-start.4 = (bf16[272,128]{1,0:T(8,128)(2,1)S(1)}, bf16[272,128]{1,0:T(8,128)(2,1)S(1)}, u32[]{:S(2)}, u32[]{:S(2)}) collective-permute-start(bf16[272,128]{1,0:T(8,128)(2,1)S(1)} %get-tuple-element.37.refs_1_.refs_2_), channel_id=1, source_target_pairs={{0,6},{1,5},{2,4},{3,7},{4,2},{5,1},{6,0},{7,3},{8,14},{9,13},{10,... | collective-permute-start | bytes 208904 | tf_op jit(solution)/shard_map/ppermute | solution.py:271
  10.6 6.2 %collective-permute-start.5 = (bf16[272,128]{1,0:T(8,128)(2,1)S(1)}, bf16[272,128]{1,0:T(8,128)(2,1)S(1)}, u32[]{:S(2)}, u32[]{:S(2)}) collective-permute-start(bf16[272,128]{1,0:T(8,128)(2,1)S(1)} %collective-permute-done.1.refs_2_.refs_3_), channel_id=1, source_target_pairs={{0,6},{1,5},{2,4},{3,7},{4,2},{5,1},{6,0},{7,3},{8,14},{9,13},{10,... | collective-permute-start | bytes 208904 | tf_op jit(solution)/shard_map/ppermute | solution.py:271
  12.6 7.8 %collective-permute-start.12 = (bf16[544,128]{1,0:T(8,128)(2,1)S(1)}, bf16[544,128]{1,0:T(8,128)(2,1)S(1)}, u32[]{:S(2)}, u32[]{:S(2)}) collective-permute-start(bf16[544,128]{1,0:T(8,128)(2,1)S(1)} %slice.7), channel_id=1, source_target_pairs={{0,16},{8,24},{16,0},{24,8},{1,17},{9,25},{17,1},{25,9},{2,18},{10... | collective-permute-start | bytes 417800 | tf_op jit(solution)/shard_map/ppermute | solution.py:25
  14.0 6.4 %collective-permute-start.11 = (bf16[512,128]{1,0:T(8,128)(2,1)S(1)}, bf16[512,128]{1,0:T(8,128)(2,1)S(1)}, u32[]{:S(2)}, u32[]{:S(2)}) collective-permute-start(bf16[512,128]{1,0:T(8,128)(2,1)S(1)} %slice.6), channel_id=1, source_target_pairs={{0,8},{8,0},{16,24},{24,16},{1,9},{9,1},{17,25},{25,17},{2,10},{10... | collective-permute-start | bytes 393224 | tf_op jit(solution)/shard_map/ppermute | solution.py:25
  15.6 2.0 %collective-permute-start.8 = (bf16[272,128]{1,0:T(8,128)(2,1)S(1)}, bf16[272,128]{1,0:T(8,128)(2,1)S(1)}, u32[]{:S(2)}, u32[]{:S(2)}) collective-permute-start(bf16[272,128]{1,0:T(8,128)(2,1)S(1)} %collective-permute-done.2.refs_3_.refs_4_), channel_id=1, source_target_pairs={{0,1},{1,0},{2,3},{3,2},{4,5},{5,4},{6,7},{7,6},{8,9},{9,8},{10,11... | collective-permute-start | bytes 208904 | tf_op jit(solution)/shard_map/ppermute | solution.py:25
  16.8 2.4 %collective-permute-start.6 = (bf16[272,128]{1,0:T(8,128)(2,1)S(1)}, bf16[272,128]{1,0:T(8,128)(2,1)S(1)}, u32[]{:S(2)}, u32[]{:S(2)}) collective-permute-start(bf16[272,128]{1,0:T(8,128)(2,1)S(1)} %collective-permute-done.4.refs_4_.refs_6_), channel_id=1, source_target_pairs={{0,1},{1,0},{2,3},{3,2},{4,5},{5,4},{6,7},{7,6},{8,9},{9,8},{10,11... | collective-permute-start | bytes 208904 | tf_op jit(solution)/shard_map/ppermute | solution.py:25
  17.6 1.6 %collective-permute-start.7 = (bf16[272,128]{1,0:T(8,128)(2,1)S(1)}, bf16[272,128]{1,0:T(8,128)(2,1)S(1)}, u32[]{:S(2)}, u32[]{:S(2)}) collective-permute-start(bf16[272,128]{1,0:T(8,128)(2,1)S(1)} %collective-permute-done.5.refs_5_.refs_7_), channel_id=1, source_target_pairs={{0,1},{1,0},{2,3},{3,2},{4,5},{5,4},{6,7},{7,6},{8,9},{9,8},{10,11... | collective-permute-start | bytes 208904 | tf_op jit(solution)/shard_map/ppermute | solution.py:25
  21.2 2.3 %collective-permute-start.14 = (bf16[4,256,128]{2,1,0:T(8,128)(2,1)S(1)}, bf16[4,256,128]{2,1,0:T(8,128)(2,1)S(1)}, u32[]{:S(2)}, u32[]{:S(2)}) collective-permute-start(bf16[4,256,128]{2,1,0:T(8,128)(2,1)S(1)} %get-tuple-element.63), channel_id=1, source_target_pairs={{0,1},{1,0},{2,3},{3,2},{4,5},{5,4},{6,7},{7,6},{8,9},{9,8},{10,11... | collective-permute-start | bytes 786440 | tf_op jit(solution)/shard_map/ppermute | solution.py:25
  21.8 7.5 %collective-permute-start.10 = (bf16[128,512]{1,0:T(8,128)(2,1)S(1)}, bf16[128,512]{1,0:T(8,128)(2,1)S(1)}, u32[]{:S(2)}, u32[]{:S(2)}) collective-permute-start(bf16[128,512]{1,0:T(8,128)(2,1)S(1)} %get-tuple-element.55), channel_id=1, source_target_pairs={{0,16},{8,24},{16,0},{24,8},{1,17},{9,25},{17,1},{25,9},{2,18},{10... | collective-permute-start | bytes 393224 | tf_op jit(solution)/shard_map/ppermute | solution.py:25
  22.3 7.0 %collective-permute-start.9 = (bf16[128,512]{1,0:T(8,128)(2,1)S(1)}, bf16[128,512]{1,0:T(8,128)(2,1)S(1)}, u32[]{:S(2)}, u32[]{:S(2)}) collective-permute-start(bf16[128,512]{1,0:T(8,128)(2,1)S(1)} %get-tuple-element.54), channel_id=1, source_target_pairs={{0,8},{8,0},{16,24},{24,16},{1,9},{9,1},{17,25},{25,17},{2,10},{10... | collective-permute-start | bytes 393224 | tf_op jit(solution)/shard_map/ppermute | solution.py:25
  23.5 8.4 %collective-permute-start.15 = (bf16[256,128]{1,0:T(8,128)(2,1)S(1)}, bf16[256,128]{1,0:T(8,128)(2,1)S(1)}, u32[]{:S(2)}, u32[]{:S(2)}) collective-permute-start(bf16[256,128]{1,0:T(8,128)(2,1)S(1)} %get-tuple-element.66), channel_id=1, source_target_pairs={{0,6},{1,5},{2,4},{3,7},{4,2},{5,1},{6,0},{7,3},{8,14},{9,13},{10,... | collective-permute-start | bytes 196616 | tf_op jit(solution)/shard_map/ppermute | solution.py:271
  27.8 5.9 %collective-permute-start.13 = (bf16[128,512]{1,0:T(8,128)(2,1)S(1)}, bf16[128,512]{1,0:T(8,128)(2,1)S(1)}, u32[]{:S(2)}, u32[]{:S(2)}) collective-permute-start(bf16[128,512]{1,0:T(8,128)(2,1)S(1)} %get-tuple-element.61), channel_id=1, source_target_pairs={{0,24},{8,16},{16,8},{24,0},{1,25},{9,17},{17,9},{25,1},{2,26},{10... | collective-permute-start | bytes 393224 | tf_op jit(solution)/shard_map/ppermute | solution.py:25
  29.3 5.5 %collective-permute-start.16 = (bf16[256,128]{1,0:T(8,128)(2,1)S(1)}, bf16[256,128]{1,0:T(8,128)(2,1)S(1)}, u32[]{:S(2)}, u32[]{:S(2)}) collective-permute-start(bf16[256,128]{1,0:T(8,128)(2,1)S(1)} %get-tuple-element.67), channel_id=1, source_target_pairs={{0,4},{1,7},{2,6},{3,5},{4,0},{5,3},{6,2},{7,1},{8,12},{9,15},{10,... | collective-permute-start | bytes 196616 | tf_op jit(solution)/shard_map/ppermute | solution.py:271
  29.9 5.0 %collective-permute-start.17 = (bf16[256,128]{1,0:T(8,128)(2,1)S(1)}, bf16[256,128]{1,0:T(8,128)(2,1)S(1)}, u32[]{:S(2)}, u32[]{:S(2)}) collective-permute-start(bf16[256,128]{1,0:T(8,128)(2,1)S(1)} %get-tuple-element.68), channel_id=1, source_target_pairs={{0,2},{1,3},{2,0},{3,1},{4,6},{5,7},{6,4},{7,5},{8,10},{9,11},{10,... | collective-permute-start | bytes 196616 | tf_op jit(solution)/shard_map/ppermute | solution.py:25

commit v17 on v15

--- a/solution.py
+++ b/solution.py
@@ -83,22 +83,29 @@
 
 def blocks_kernel(plan, rows, heads, scale, *refs):
     refs = list(refs)
-    x_refs = []
-    for parts in plan["parts"]:
-        whole = refs.pop(0)
-        x_refs.append((whole, whole.at[heads * rows :, :] if parts == 1 else refs.pop(0)))
+    x_refs = [[refs.pop(0) for _ in range(parts)] for parts in plan["parts"]]
     kv_refs = [refs.pop(0) for _ in range(plan["kv"])]
     acc_refs = [refs.pop(0) for _ in range(plan["acc"])]
     dq_in = [refs.pop(0) for _ in range(plan["dq_in"])]
     dq_refs, dkv_ref = refs[:-1], refs[-1]
     width = x_refs[0][0].shape[1]
     hr = heads * rows
+
+    def taken(b, start, stop):
+        first, cut = x_refs[b][0], x_refs[b][0].shape[0]
+        if stop <= cut:
+            return first[start:stop, :]
+        rest = x_refs[b][1]
+        if start >= cut:
+            return rest[start - cut : stop - cut, :]
+        return jnp.concatenate([first[start:, :], rest[: stop - cut, :]], axis=0)
+
     per = rows // RUN
     step = COLS // rows
     slots = plan["slots"]
     rowed = []
-    for _, g_ref in x_refs:
-        e = g_ref[hr:, :].astype(F32)
+    for b in range(len(x_refs)):
+        e = taken(b, 2 * hr, 2 * hr + 32).astype(F32)
         lse = e[0:heads] + e[heads : 2 * heads] + e[2 * heads : 3 * heads]
         delta = e[3 * heads : 4 * heads] + e[4 * heads : 5 * heads] + e[5 * heads : 6 * heads]
         rowed.append((lse, delta, e[6 * heads : 6 * heads + 1]))
@@ -119,9 +126,8 @@
 
     def products(c, b, n):
         k, v, _, _ = chunk(c)
-        q_ref, g_ref = x_refs[b]
-        q = q_ref[n * COLS : (n + 1) * COLS, :]
-        g = g_ref[n * COLS : (n + 1) * COLS, :]
+        q = taken(b, n * COLS, (n + 1) * COLS)
+        g = taken(b, hr + n * COLS, hr + (n + 1) * COLS)
         return q, g, dot(k, q, NT), dot(v, g, NT)
 
     def weights(c, b, n, st, dpt):
@@ -299,14 +305,16 @@
     early = [kv, sib, near]
     dq_own, acc = blocks_call([x], early, range(3), *common, F32, F32, diagonal=True)
 
+    cut = hr + 32
+    top, acc = lax.optimization_barrier((x[:cut], acc))
     xs = [swapped(x, "outer", s) for s in range(1, nq - 1)]
     dqs = [dq_own]
     for s in range(nq - 2):
         xs[s], acc = lax.optimization_barrier((xs[s], acc))
         dq, acc = blocks_call([xs[s]], early, range(3), *common, F32, F32, acc=[(acc, n) for n in range(3)])
         dqs.append(dq)
-    halves = [xs[nq - 3][:hr], xs[((nq - 1) ^ (nq // 2)) - 1][hr:]]
-    corner = [swapped(halves[0], "outer", 1), swapped(halves[1], "outer", nq // 2)]
+    passed = xs[((nq - 1) ^ (nq // 2)) - 1][cut:]
+    corner = [swapped(top, "outer", nq - 1), swapped(passed, "outer", nq // 2)]
 
     *direct, acc = lax.optimization_barrier((*direct, acc))
     traded = [swapped(block, "inner", 1) for block in direct]

time: 34.7 us -> 34.8 us (level)
    ppermute x14, starting transfers between devices: 14 us -> 14.4 us  [swapped(): return lax.ppermute(block, axis, pairs)]
  transfers between devices with their start and end apart: 18 -> 18, of which waited for: 3 -> 4; matrix products, arithmetic and copies ran while one was open for 0% -> 0% of each run, Pallas kernels for 17% -> 17%
where the time goes in v17:
time: 34.8 us; the launch traced here: 34.6 us
  starting transfers between devices  21.9 us (63%)
  Pallas kernels  8.75 us (25%)
  waiting for transfers between devices  3.18 us (9%)
  between operations  0.8 us (2%)
    ppermute x14, starting transfers between devices, swapped(): return lax.ppermute(block, axis, pairs)  14.4 us
    ppermute x4, starting transfers between devices, crossed(): return lax.ppermute(block, 'inner', pairs)  7.5 us
    pallas_call x8, Pallas kernels, blocks_call(): pl.pallas_call(functools.partial(blocks_kernel, plan, rows, heads, scale)...  6.52 us
    ppermute x4, waiting for transfers between devices, crossed(): return lax.ppermute(block, 'inner', pairs)  2.24 us
    pallas_call x1, Pallas kernels, on_device(): pl.pallas_call(pack_kernel, out_shape=(sds((2 * hr + 32, width), BF), sds...  1.34 us
    ppermute x14, waiting for transfers between devices, swapped(): return lax.ppermute(block, axis, pairs)  0.94 us
    pallas_call x1, Pallas kernels, on_device(): pl.pallas_call(functools.partial(final_kernel, rows, heads, scale), out_s...  0.76 us
  transfers between devices with their start and end apart: 18, of which 4 were waited for; matrix products, arithmetic and copies ran while one was open for 0% of the time, Pallas kernels for 17%

profile of v17, /device:TPU:0, one launch (start us, length us, event | category | flops | bytes accessed | tf_op | source)
XLA Modules:
  0.0 34.6 jit_solution(12591573331911992329)
XLA Ops:
  0.6 1.3 %shard_map.94 = (bf16[1056,128]{1,0:T(8,128)(2,1)S(1)}, bf16[272,128]{1,0:T(8,128)(2,1)S(1)}) custom-call(bf16[128,512]{1,0:T(8,128)(2,1)} %q_ref.1, bf16[128,128]{1,0:T(8,128)(2,1)} %k_ref.1, bf16[128,128]{1,0:T(8,128)(2,1)} %v_ref.1, bf16[128,512]{1,0:T(8,128)(2,1)} %o_ref.1, bf16[128,512]{1,0:T(8,128)(2,1)} %g_ref.1, f32[4,128]{1,0:T(4,128)} %lse_ref.1, ...), custom_call_target="tpu_custom_call" | custom-call | flops 1000 | bytes 1000 | tf_op jit(solution)/shard_map/pallas_call | solution.py:286
  2.0 3.0 %collective-permute-start = (bf16[1056,128]{1,0:T(8,128)(2,1)S(1)}, bf16[1056,128]{1,0:T(8,128)(2,1)S(1)}, u32[]{:S(2)}, u32[]{:S(2)}) collective-permute-start(bf16[1056,128]{1,0:T(8,128)(2,1)S(1)} %get-tuple-element.38.refs_0_), channel_id=1, source_target_pairs={{0,8},{8,0},{16,24},{24,16},{1,9},{9,1},{17,25},{25,17},{2,10},{10... | collective-permute-start | bytes 811016 | tf_op jit(solution)/shard_map/ppermute | solution.py:25
  5.0 1.5 %collective-permute-start.3 = (bf16[1056,128]{1,0:T(8,128)(2,1)S(1)}, bf16[1056,128]{1,0:T(8,128)(2,1)S(1)}, u32[]{:S(2)}, u32[]{:S(2)}) collective-permute-start(bf16[1056,128]{1,0:T(8,128)(2,1)S(1)} %get-tuple-element.38.refs_0_), channel_id=1, source_target_pairs={{0,16},{8,24},{16,0},{24,8},{1,17},{9,25},{17,1},{25,9},{2,18},{10... | collective-permute-start | bytes 811016 | tf_op jit(solution)/shard_map/ppermute | solution.py:25
  6.5 0.0 collective-permute-start.1
  6.5 1.6 %collective-permute-start.2 = (bf16[272,128]{1,0:T(8,128)(2,1)S(1)}, bf16[272,128]{1,0:T(8,128)(2,1)S(1)}, u32[]{:S(2)}, u32[]{:S(2)}) collective-permute-start(bf16[272,128]{1,0:T(8,128)(2,1)S(1)} %get-tuple-element.39.refs_1_.refs_2_), channel_id=1, source_target_pairs={{0,2},{1,3},{2,0},{3,1},{4,6},{5,7},{6,4},{7,5},{8,10},{9,11},{10,... | collective-permute-start | bytes 208904 | tf_op jit(solution)/shard_map/ppermute | solution.py:25
  8.1 2.5 %collective-permute-start.4 = (bf16[272,128]{1,0:T(8,128)(2,1)S(1)}, bf16[272,128]{1,0:T(8,128)(2,1)S(1)}, u32[]{:S(2)}, u32[]{:S(2)}) collective-permute-start(bf16[272,128]{1,0:T(8,128)(2,1)S(1)} %get-tuple-element.39.refs_1_.refs_2_), channel_id=1, source_target_pairs={{0,6},{1,5},{2,4},{3,7},{4,2},{5,1},{6,0},{7,3},{8,14},{9,13},{10,... | collective-permute-start | bytes 208904 | tf_op jit(solution)/shard_map/ppermute | solution.py:274
  10.6 0.0 collective-permute-done.1.refs_2_.refs_3_
  10.6 1.3 %collective-permute-start.5 = (bf16[272,128]{1,0:T(8,128)(2,1)S(1)}, bf16[272,128]{1,0:T(8,128)(2,1)S(1)}, u32[]{:S(2)}, u32[]{:S(2)}) collective-permute-start(bf16[272,128]{1,0:T(8,128)(2,1)S(1)} %collective-permute-done.1.refs_2_.refs_3_), channel_id=1, source_target_pairs={{0,6},{1,5},{2,4},{3,7},{4,2},{5,1},{6,0},{7,3},{8,14},{9,13},{10,... | collective-permute-start | bytes 208904 | tf_op jit(solution)/shard_map/ppermute | solution.py:274
  11.9 0.7 %shard_map.95 = (f32[128,512]{1,0:T(8,128)S(1)}, f32[3,256,128]{2,1,0:T(8,128)S(1)}) custom-call(bf16[1056,128]{1,0:T(8,128)(2,1)S(1)} %get-tuple-element.38.refs_0_, bf16[272,128]{1,0:T(8,128)(2,1)S(1)} %get-tuple-element.39.refs_1_.refs_2_, bf16[272,128]{1,0:T(8,128)(2,1)S(1)} %collective-permute-done.1.refs_2_.refs_3_, ...), custom_call_target="tpu_custom_call" | custom-call | flops 1000 | bytes 1000 | tf_op jit(solution)/shard_map/pallas_call | solution.py:215
  12.6 0.5 %collective-permute-start.11 = (bf16[544,128]{1,0:T(8,128)(2,1)S(1)}, bf16[544,128]{1,0:T(8,128)(2,1)S(1)}, u32[]{:S(2)}, u32[]{:S(2)}) collective-permute-start(bf16[544,128]{1,0:T(8,128)(2,1)S(1)} %slice.6), channel_id=1, source_target_pairs={{0,24},{8,16},{16,8},{24,0},{1,25},{9,17},{17,9},{25,1},{2,26},{10... | collective-permute-start | bytes 417800 | tf_op jit(solution)/shard_map/ppermute | solution.py:25
  13.2 1.6 %collective-permute-start.12 = (bf16[512,128]{1,0:T(8,128)(2,1)S(1)}, bf16[512,128]{1,0:T(8,128)(2,1)S(1)}, u32[]{:S(2)}, u32[]{:S(2)}) collective-permute-start(bf16[512,128]{1,0:T(8,128)(2,1)S(1)} %slice.7), channel_id=1, source_target_pairs={{0,16},{8,24},{16,0},{24,8},{1,17},{9,25},{17,1},{25,9},{2,18},{10... | collective-permute-start | bytes 393224 | tf_op jit(solution)/shard_map/ppermute | solution.py:25
  14.7 0.7 %shard_map.96 = (f32[128,512]{1,0:T(8,128)S(1)}, f32[3,256,128]{2,1,0:T(8,128)S(1)}) custom-call(bf16[1056,128]{1,0:T(8,128)(2,1)S(1)} %collective-permute-done.refs_0_.refs_1_, bf16[272,128]{1,0:T(8,128)(2,1)S(1)} %get-tuple-element.39.refs_1_.refs_2_, bf16[272,128]{1,0:T(8,128)(2,1)S(1)} %collective-permute-done.1.refs_2_.refs_3_, ...), custom_call_target="tpu_custom_call" | custom-call | flops 1000 | bytes 1000 | tf_op jit(solution)/shard_map/pallas_call | solution.py:215
  15.4 0.1 collective-permute-start.8
  15.5 0.7 %shard_map.97 = (f32[128,512]{1,0:T(8,128)S(1)}, f32[3,256,128]{2,1,0:T(8,128)S(1)}) custom-call(bf16[1056,128]{1,0:T(8,128)(2,1)S(1)} %collective-permute-done.3.refs_0_.refs_2_, bf16[272,128]{1,0:T(8,128)(2,1)S(1)} %get-tuple-element.39.refs_1_.refs_2_, bf16[272,128]{1,0:T(8,128)(2,1)S(1)} %collective-permute-done.1.refs_2_.refs_3_, ...), custom_call_target="tpu_custom_call" | custom-call | flops 1000 | bytes 1000 | tf_op jit(solution)/shard_map/pallas_call | solution.py:215
  16.2 0.6 %collective-permute-done.5.refs_5_.refs_7_ = bf16[272,128]{1,0:T(8,128)(2,1)S(1)} collective-permute-done((bf16[272,128]{1,0:T(8,128)(2,1)S(1)}, bf16[272,128]{1,0:T(8,128)(2,1)S(1)}, u32[]{:S(2)}, u32[]{:S(2)}) %collective-permute-start.5) | collective-permute-done | bytes 69664 | tf_op jit(solution)/shard_map/ppermute | solution.py:274
  16.8 1.1 %collective-permute-start.6 = (bf16[272,128]{1,0:T(8,128)(2,1)S(1)}, bf16[272,128]{1,0:T(8,128)(2,1)S(1)}, u32[]{:S(2)}, u32[]{:S(2)}) collective-permute-start(bf16[272,128]{1,0:T(8,128)(2,1)S(1)} %collective-permute-done.4.refs_4_.refs_6_), channel_id=1, source_target_pairs={{0,1},{1,0},{2,3},{3,2},{4,5},{5,4},{6,7},{7,6},{8,9},{9,8},{10,11... | collective-permute-start | bytes 208904 | tf_op jit(solution)/shard_map/ppermute | solution.py:25
  17.9 0.0 collective-permute-start.7
  17.9 1.6 %shard_map.98 = (f32[128,512]{1,0:T(8,128)S(1)}, f32[128,512]{1,0:T(8,128)S(1)}, f32[128,512]{1,0:T(8,128)S(1)}, f32[3,256,128]{2,1,0:T(8,128)S(1)}) custom-call(bf16[1056,128]{1,0:T(8,128)(2,1)S(1)} %get-tuple-element.38.refs_0_, bf16[1056,128]{1,0:T(8,128)(2,1)S(1)} %collective-permute-done.refs_0_.refs_1_, ...), custom_call_target="tpu_custom_call" | custom-call | flops 1000 | bytes 1000 | tf_op jit(solution)/shard_map/pallas_call | solution.py:215
  19.5 1.1 %shard_map.99 = (f32[128,512]{1,0:T(8,128)S(1)}, bf16[128,512]{1,0:T(8,128)(2,1)S(1)}, bf16[128,512]{1,0:T(8,128)(2,1)S(1)}, f32[2,256,128]{2,1,0:T(8,128)S(1)}) custom-call(bf16[1056,128]{1,0:T(8,128)(2,1)S(1)} %get-tuple-element.38.refs_0_, bf16[1056,128]{1,0:T(8,128)(2,1)S(1)} %collective-permute-done.refs_0_.refs_1_, ...), custom_call_target="tpu_custom_call" | custom-call | flops 1000 | bytes 1000 | tf_op jit(solution)/shard_map/pallas_call | solution.py:215
  20.7 0.8 %shard_map.101 = (f32[128,512]{1,0:T(8,128)S(1)}, bf16[4,256,128]{2,1,0:T(8,128)(2,1)S(1)}) custom-call(bf16[544,128]{1,0:T(8,128)(2,1)S(1)} %collective-permute-done.11.refs_0_, bf16[512,128]{1,0:T(8,128)(2,1)S(1)} %collective-permute-done.12.refs_1_, bf16[272,128]{1,0:T(8,128)(2,1)S(1)} %get-tuple-element.39.refs_1_.refs_2_, ...), custom_call_target="tpu_custom_call" | custom-call | flops 1000 | bytes 1000 | tf_op jit(solution)/shard_map/pallas_call | solution.py:215
  21.5 0.6 %collective-permute-start.14 = (bf16[4,256,128]{2,1,0:T(8,128)(2,1)S(1)}, bf16[4,256,128]{2,1,0:T(8,128)(2,1)S(1)}, u32[]{:S(2)}, u32[]{:S(2)}) collective-permute-start(bf16[4,256,128]{2,1,0:T(8,128)(2,1)S(1)} %get-tuple-element.67), channel_id=1, source_target_pairs={{0,1},{1,0},{2,3},{3,2},{4,5},{5,4},{6,7},{7,6},{8,9},{9,8},{10,11... | collective-permute-start | bytes 786440 | tf_op jit(solution)/shard_map/ppermute | solution.py:25
  22.1 0.5 %collective-permute-start.10 = (bf16[128,512]{1,0:T(8,128)(2,1)S(1)}, bf16[128,512]{1,0:T(8,128)(2,1)S(1)}, u32[]{:S(2)}, u32[]{:S(2)}) collective-permute-start(bf16[128,512]{1,0:T(8,128)(2,1)S(1)} %get-tuple-element.58), channel_id=1, source_target_pairs={{0,16},{8,24},{16,0},{24,8},{1,17},{9,25},{17,1},{25,9},{2,18},{10... | collective-permute-start | bytes 393224 | tf_op jit(solution)/shard_map/ppermute | solution.py:25
  22.6 0.5 %collective-permute-start.9 = (bf16[128,512]{1,0:T(8,128)(2,1)S(1)}, bf16[128,512]{1,0:T(8,128)(2,1)S(1)}, u32[]{:S(2)}, u32[]{:S(2)}) collective-permute-start(bf16[128,512]{1,0:T(8,128)(2,1)S(1)} %get-tuple-element.57), channel_id=1, source_target_pairs={{0,8},{8,0},{16,24},{24,16},{1,9},{9,1},{17,25},{25,17},{2,10},{10... | collective-permute-start | bytes 393224 | tf_op jit(solution)/shard_map/ppermute | solution.py:25
  23.1 0.5 %shard_map.102 = (f32[128,512]{1,0:T(8,128)S(1)}, f32[2,256,128]{2,1,0:T(8,128)S(1)}) custom-call(bf16[544,128]{1,0:T(8,128)(2,1)S(1)} %collective-permute-done.11.refs_0_, bf16[512,128]{1,0:T(8,128)(2,1)S(1)} %collective-permute-done.12.refs_1_, bf16[272,128]{1,0:T(8,128)(2,1)S(1)} %get-tuple-element.39.refs_1_.refs_2_, ...), custom_call_target="tpu_custom_call" | custom-call | flops 1000 | bytes 1000 | tf_op jit(solution)/shard_map/pallas_call | solution.py:215
  23.6 3.7 %collective-permute-start.15 = (bf16[256,128]{1,0:T(8,128)(2,1)S(1)}, bf16[256,128]{1,0:T(8,128)(2,1)S(1)}, u32[]{:S(2)}, u32[]{:S(2)}) collective-permute-start(bf16[256,128]{1,0:T(8,128)(2,1)S(1)} %get-tuple-element.70), channel_id=1, source_target_pairs={{0,6},{1,5},{2,4},{3,7},{4,2},{5,1},{6,0},{7,3},{8,14},{9,13},{10,... | collective-permute-start | bytes 196616 | tf_op jit(solution)/shard_map/ppermute | solution.py:274
  27.3 0.5 %shard_map.103 = (bf16[128,512]{1,0:T(8,128)(2,1)S(1)}, f32[2,256,128]{2,1,0:T(8,128)S(1)}) custom-call(bf16[544,128]{1,0:T(8,128)(2,1)S(1)} %collective-permute-done.11.refs_0_, bf16[512,128]{1,0:T(8,128)(2,1)S(1)} %collective-permute-done.12.refs_1_, bf16[272,128]{1,0:T(8,128)(2,1)S(1)} %get-tuple-element.39.refs_1_.refs_2_, ...), custom_call_target="tpu_custom_call" | custom-call | flops 1000 | bytes 1000 | tf_op jit(solution)/shard_map/pallas_call | solution.py:215
  27.8 1.6 %collective-permute-start.13 = (bf16[128,512]{1,0:T(8,128)(2,1)S(1)}, bf16[128,512]{1,0:T(8,128)(2,1)S(1)}, u32[]{:S(2)}, u32[]{:S(2)}) collective-permute-start(bf16[128,512]{1,0:T(8,128)(2,1)S(1)} %get-tuple-element.65), channel_id=1, source_target_pairs={{0,24},{8,16},{16,8},{24,0},{1,25},{9,17},{17,9},{25,1},{2,26},{10... | collective-permute-start | bytes 393224 | tf_op jit(solution)/shard_map/ppermute | solution.py:25
  29.5 1.7 %collective-permute-start.17 = (bf16[256,128]{1,0:T(8,128)(2,1)S(1)}, bf16[256,128]{1,0:T(8,128)(2,1)S(1)}, u32[]{:S(2)}, u32[]{:S(2)}) collective-permute-start(bf16[256,128]{1,0:T(8,128)(2,1)S(1)} %get-tuple-element.72), channel_id=1, source_target_pairs={{0,2},{1,3},{2,0},{3,1},{4,6},{5,7},{6,4},{7,5},{8,10},{9,11},{10,... | collective-permute-start | bytes 196616 | tf_op jit(solution)/shard_map/ppermute | solution.py:25
  31.2 1.7 %collective-permute-done.16.refs_1_ = bf16[256,128]{1,0:T(8,128)(2,1)S(1)} collective-permute-done((bf16[256,128]{1,0:T(8,128)(2,1)S(1)}, bf16[256,128]{1,0:T(8,128)(2,1)S(1)}, u32[]{:S(2)}, u32[]{:S(2)}) %collective-permute-start.16) | collective-permute-done | bytes 65568 | tf_op jit(solution)/shard_map/ppermute | solution.py:274
  33.0 0.8 %collective-permute-done.13.dq_far = bf16[128,512]{1,0:T(8,128)(2,1)S(1)} collective-permute-done((bf16[128,512]{1,0:T(8,128)(2,1)S(1)}, bf16[128,512]{1,0:T(8,128)(2,1)S(1)}, u32[]{:S(2)}, u32[]{:S(2)}) %collective-permute-start.13) | collective-permute-done | bytes 131104 | tf_op jit(solution)/shard_map/ppermute | solution.py:25
  33.7 0.1 collective-permute-done.17.dkv_near
  33.9 0.8 %shard_map.107 = (bf16[128,512]{1,0:T(8,128)(2,1)}, bf16[128,128]{1,0:T(8,128)(2,1)}, bf16[128,128]{1,0:T(8,128)(2,1)}) custom-call(f32[128,512]{1,0:T(8,128)S(1)} %shard_map.100.dq_ref, bf16[128,512]{1,0:T(8,128)(2,1)S(1)} %collective-permute-done.13.dq_far, f32[256,128]{1,0:T(8,128)S(1)} %shard_map.106.dkv_ref, ...), custom_call_target="tpu_custom_call" | custom-call | flops 1000 | bytes 1000 | tf_op jit(solution)/shard_map/pallas_call | solution.py:351
  (20 shorter events, 0.2 us)
Async XLA Ops:
  2.0 11.2 %collective-permute-start = (bf16[1056,128]{1,0:T(8,128)(2,1)S(1)}, bf16[1056,128]{1,0:T(8,128)(2,1)S(1)}, u32[]{:S(2)}, u32[]{:S(2)}) collective-permute-start(bf16[1056,128]{1,0:T(8,128)(2,1)S(1)} %get-tuple-element.38.refs_0_), channel_id=1, source_target_pairs={{0,8},{8,0},{16,24},{24,16},{1,9},{9,1},{17,25},{25,17},{2,10},{10... | collective-permute-start | bytes 811016 | tf_op jit(solution)/shard_map/ppermute | solution.py:25
  5.0 10.4 %collective-permute-start.3 = (bf16[1056,128]{1,0:T(8,128)(2,1)S(1)}, bf16[1056,128]{1,0:T(8,128)(2,1)S(1)}, u32[]{:S(2)}, u32[]{:S(2)}) collective-permute-start(bf16[1056,128]{1,0:T(8,128)(2,1)S(1)} %get-tuple-element.38.refs_0_), channel_id=1, source_target_pairs={{0,16},{8,24},{16,0},{24,8},{1,17},{9,25},{17,1},{25,9},{2,18},{10... | collective-permute-start | bytes 811016 | tf_op jit(solution)/shard_map/ppermute | solution.py:25
  6.5 4.1 %collective-permute-start.1 = (bf16[272,128]{1,0:T(8,128)(2,1)S(1)}, bf16[272,128]{1,0:T(8,128)(2,1)S(1)}, u32[]{:S(2)}, u32[]{:S(2)}) collective-permute-start(bf16[272,128]{1,0:T(8,128)(2,1)S(1)} %get-tuple-element.39.refs_1_.refs_2_), channel_id=1, source_target_pairs={{0,1},{1,0},{2,3},{3,2},{4,5},{5,4},{6,7},{7,6},{8,9},{9,8},{10,11... | collective-permute-start | bytes 208904 | tf_op jit(solution)/shard_map/ppermute | solution.py:25
  6.5 5.4 %collective-permute-start.2 = (bf16[272,128]{1,0:T(8,128)(2,1)S(1)}, bf16[272,128]{1,0:T(8,128)(2,1)S(1)}, u32[]{:S(2)}, u32[]{:S(2)}) collective-permute-start(bf16[272,128]{1,0:T(8,128)(2,1)S(1)} %get-tuple-element.39.refs_1_.refs_2_), channel_id=1, source_target_pairs={{0,2},{1,3},{2,0},{3,1},{4,6},{5,7},{6,4},{7,5},{8,10},{9,11},{10,... | collective-permute-start | bytes 208904 | tf_op jit(solution)/shard_map/ppermute | solution.py:25
  8.1 8.1 %collective-permute-start.4 = (bf16[272,128]{1,0:T(8,128)(2,1)S(1)}, bf16[272,128]{1,0:T(8,128)(2,1)S(1)}, u32[]{:S(2)}, u32[]{:S(2)}) collective-permute-start(bf16[272,128]{1,0:T(8,128)(2,1)S(1)} %get-tuple-element.39.refs_1_.refs_2_), channel_id=1, source_target_pairs={{0,6},{1,5},{2,4},{3,7},{4,2},{5,1},{6,0},{7,3},{8,14},{9,13},{10,... | collective-permute-start | bytes 208904 | tf_op jit(solution)/shard_map/ppermute | solution.py:274
  10.6 6.2 %collective-permute-start.5 = (bf16[272,128]{1,0:T(8,128)(2,1)S(1)}, bf16[272,128]{1,0:T(8,128)(2,1)S(1)}, u32[]{:S(2)}, u32[]{:S(2)}) collective-permute-start(bf16[272,128]{1,0:T(8,128)(2,1)S(1)} %collective-permute-done.1.refs_2_.refs_3_), channel_id=1, source_target_pairs={{0,6},{1,5},{2,4},{3,7},{4,2},{5,1},{6,0},{7,3},{8,14},{9,13},{10,... | collective-permute-start | bytes 208904 | tf_op jit(solution)/shard_map/ppermute | solution.py:274
  12.6 8.1 %collective-permute-start.11 = (bf16[544,128]{1,0:T(8,128)(2,1)S(1)}, bf16[544,128]{1,0:T(8,128)(2,1)S(1)}, u32[]{:S(2)}, u32[]{:S(2)}) collective-permute-start(bf16[544,128]{1,0:T(8,128)(2,1)S(1)} %slice.6), channel_id=1, source_target_pairs={{0,24},{8,16},{16,8},{24,0},{1,25},{9,17},{17,9},{25,1},{2,26},{10... | collective-permute-start | bytes 417800 | tf_op jit(solution)/shard_map/ppermute | solution.py:25
  13.2 7.5 %collective-permute-start.12 = (bf16[512,128]{1,0:T(8,128)(2,1)S(1)}, bf16[512,128]{1,0:T(8,128)(2,1)S(1)}, u32[]{:S(2)}, u32[]{:S(2)}) collective-permute-start(bf16[512,128]{1,0:T(8,128)(2,1)S(1)} %slice.7), channel_id=1, source_target_pairs={{0,16},{8,24},{16,0},{24,8},{1,17},{9,25},{17,1},{25,9},{2,18},{10... | collective-permute-start | bytes 393224 | tf_op jit(solution)/shard_map/ppermute | solution.py:25
  15.4 2.4 %collective-permute-start.8 = (bf16[272,128]{1,0:T(8,128)(2,1)S(1)}, bf16[272,128]{1,0:T(8,128)(2,1)S(1)}, u32[]{:S(2)}, u32[]{:S(2)}) collective-permute-start(bf16[272,128]{1,0:T(8,128)(2,1)S(1)} %collective-permute-done.2.refs_3_.refs_4_), channel_id=1, source_target_pairs={{0,1},{1,0},{2,3},{3,2},{4,5},{5,4},{6,7},{7,6},{8,9},{9,8},{10,11... | collective-permute-start | bytes 208904 | tf_op jit(solution)/shard_map/ppermute | solution.py:25
  16.8 2.7 %collective-permute-start.6 = (bf16[272,128]{1,0:T(8,128)(2,1)S(1)}, bf16[272,128]{1,0:T(8,128)(2,1)S(1)}, u32[]{:S(2)}, u32[]{:S(2)}) collective-permute-start(bf16[272,128]{1,0:T(8,128)(2,1)S(1)} %collective-permute-done.4.refs_4_.refs_6_), channel_id=1, source_target_pairs={{0,1},{1,0},{2,3},{3,2},{4,5},{5,4},{6,7},{7,6},{8,9},{9,8},{10,11... | collective-permute-start | bytes 208904 | tf_op jit(solution)/shard_map/ppermute | solution.py:25
  17.9 1.6 %collective-permute-start.7 = (bf16[272,128]{1,0:T(8,128)(2,1)S(1)}, bf16[272,128]{1,0:T(8,128)(2,1)S(1)}, u32[]{:S(2)}, u32[]{:S(2)}) collective-permute-start(bf16[272,128]{1,0:T(8,128)(2,1)S(1)} %collective-permute-done.5.refs_5_.refs_7_), channel_id=1, source_target_pairs={{0,1},{1,0},{2,3},{3,2},{4,5},{5,4},{6,7},{7,6},{8,9},{9,8},{10,11... | collective-permute-start | bytes 208904 | tf_op jit(solution)/shard_map/ppermute | solution.py:25
  21.5 2.1 %collective-permute-start.14 = (bf16[4,256,128]{2,1,0:T(8,128)(2,1)S(1)}, bf16[4,256,128]{2,1,0:T(8,128)(2,1)S(1)}, u32[]{:S(2)}, u32[]{:S(2)}) collective-permute-start(bf16[4,256,128]{2,1,0:T(8,128)(2,1)S(1)} %get-tuple-element.67), channel_id=1, source_target_pairs={{0,1},{1,0},{2,3},{3,2},{4,5},{5,4},{6,7},{7,6},{8,9},{9,8},{10,11... | collective-permute-start | bytes 786440 | tf_op jit(solution)/shard_map/ppermute | solution.py:25
  22.1 7.4 %collective-permute-start.10 = (bf16[128,512]{1,0:T(8,128)(2,1)S(1)}, bf16[128,512]{1,0:T(8,128)(2,1)S(1)}, u32[]{:S(2)}, u32[]{:S(2)}) collective-permute-start(bf16[128,512]{1,0:T(8,128)(2,1)S(1)} %get-tuple-element.58), channel_id=1, source_target_pairs={{0,16},{8,24},{16,0},{24,8},{1,17},{9,25},{17,1},{25,9},{2,18},{10... | collective-permute-start | bytes 393224 | tf_op jit(solution)/shard_map/ppermute | solution.py:25
  22.6 6.9 %collective-permute-start.9 = (bf16[128,512]{1,0:T(8,128)(2,1)S(1)}, bf16[128,512]{1,0:T(8,128)(2,1)S(1)}, u32[]{:S(2)}, u32[]{:S(2)}) collective-permute-start(bf16[128,512]{1,0:T(8,128)(2,1)S(1)} %get-tuple-element.57), channel_id=1, source_target_pairs={{0,8},{8,0},{16,24},{24,16},{1,9},{9,1},{17,25},{25,17},{2,10},{10... | collective-permute-start | bytes 393224 | tf_op jit(solution)/shard_map/ppermute | solution.py:25
  23.6 7.6 %collective-permute-start.15 = (bf16[256,128]{1,0:T(8,128)(2,1)S(1)}, bf16[256,128]{1,0:T(8,128)(2,1)S(1)}, u32[]{:S(2)}, u32[]{:S(2)}) collective-permute-start(bf16[256,128]{1,0:T(8,128)(2,1)S(1)} %get-tuple-element.70), channel_id=1, source_target_pairs={{0,6},{1,5},{2,4},{3,7},{4,2},{5,1},{6,0},{7,3},{8,14},{9,13},{10,... | collective-permute-start | bytes 196616 | tf_op jit(solution)/shard_map/ppermute | solution.py:274
  27.3 5.6 %collective-permute-start.16 = (bf16[256,128]{1,0:T(8,128)(2,1)S(1)}, bf16[256,128]{1,0:T(8,128)(2,1)S(1)}, u32[]{:S(2)}, u32[]{:S(2)}) collective-permute-start(bf16[256,128]{1,0:T(8,128)(2,1)S(1)} %get-tuple-element.71), channel_id=1, source_target_pairs={{0,4},{1,7},{2,6},{3,5},{4,0},{5,3},{6,2},{7,1},{8,12},{9,15},{10,... | collective-permute-start | bytes 196616 | tf_op jit(solution)/shard_map/ppermute | solution.py:274
  27.8 5.9 %collective-permute-start.13 = (bf16[128,512]{1,0:T(8,128)(2,1)S(1)}, bf16[128,512]{1,0:T(8,128)(2,1)S(1)}, u32[]{:S(2)}, u32[]{:S(2)}) collective-permute-start(bf16[128,512]{1,0:T(8,128)(2,1)S(1)} %get-tuple-element.65), channel_id=1, source_target_pairs={{0,24},{8,16},{16,8},{24,0},{1,25},{9,17},{17,9},{25,1},{2,26},{10... | collective-permute-start | bytes 393224 | tf_op jit(solution)/shard_map/ppermute | solution.py:25
  29.5 4.3 %collective-permute-start.17 = (bf16[256,128]{1,0:T(8,128)(2,1)S(1)}, bf16[256,128]{1,0:T(8,128)(2,1)S(1)}, u32[]{:S(2)}, u32[]{:S(2)}) collective-permute-start(bf16[256,128]{1,0:T(8,128)(2,1)S(1)} %get-tuple-element.72), channel_id=1, source_target_pairs={{0,2},{1,3},{2,0},{3,1},{4,6},{5,7},{6,4},{7,5},{8,10},{9,11},{10,... | collective-permute-start | bytes 196616 | tf_op jit(solution)/shard_map/ppermute | solution.py:25

commit v18 on v15

--- a/solution.py
+++ b/solution.py
@@ -216,14 +216,14 @@
     )(*args)
 
 
-def add_kernel(start, own_ref, got_ref, *refs):
+def add_kernel(own_ref, got_ref, *refs):
     for n, ref in enumerate(refs):
-        ref[...] = (own_ref[n] + got_ref[start + n].astype(F32)).astype(ref.dtype)
-
-
-def add_call(own, got, start, types):
+        ref[...] = (own_ref[n] + got_ref[n].astype(F32)).astype(ref.dtype)
+
+
+def add_call(own, got, types):
     return pl.pallas_call(
-        functools.partial(add_kernel, start),
+        add_kernel,
         out_shape=tuple(jax.ShapeDtypeStruct(own.shape[1:], t) for t in types),
         in_specs=[VMEM] * 2,
         out_specs=(VMEM,) * len(types),
@@ -250,11 +250,14 @@
     )(own, *got)
 
 
-def final_kernel(rows, heads, scale, dq_ref, dq_far, dkv_ref, dkv_near, gq_ref, gk_ref, gv_ref):
+def final_kernel(rows, heads, scale, dq_ref, dkv_ref, dkv_near, *refs):
+    got, (gq_ref, gk_ref, gv_ref) = refs[:-3], refs[-3:]
     dkv = dkv_ref[...] + dkv_near[...].astype(F32)
     gk_ref[...] = (scale * dkv[:rows]).astype(BF)
     gv_ref[...] = dkv[rows:].astype(BF)
-    dq = dq_ref[...] + dq_far[...].astype(F32)
+    dq = dq_ref[...]
+    for ref in got:
+        dq = dq + ref[...].astype(F32)
     for h in range(heads):
         part = dq[:, h * rows : (h + 1) * rows]
         gq_ref[:, h * 128 : (h + 1) * 128] = (scale * part).T.astype(BF)
@@ -325,13 +328,10 @@
         ours += [4 + t, 3 + n_d + t + 1]
     dq_last, dkv_sib = blocks_call([corner], arrays, theirs, *common, BF, F32, acc=accs)
     dkv_got = swapped(dkv_sib, "inner", 1)
-    dq_last, dkv_far = blocks_call([corner], arrays, ours[2:], *common, F32, F32, acc=accs, dq_in=[dq_last])
-    dq_last, dkv_own = blocks_call([corner], arrays, ours[:2], *common, F32, BF, acc=accs, dq_in=[dq_last])
-    far = add_call(dkv_far, dkv_got, 2, [BF] * (nz - 2))
-    dkv_own, dkv_near = add_call(dkv_own, dkv_got, 0, [F32, BF])
-
+    dq_last, dkv_own = blocks_call([corner], arrays, ours, *common, F32, BF, acc=accs, dq_in=[dq_last])
+    dq_far = swapped(dq_last, "outer", nq - 1)
+    dkv_own, dkv_near, *far = add_call(dkv_own, dkv_got, [F32] + [BF] * (nz - 1))
     got = [swapped(dq, "outer", s + 1) for s, dq in enumerate(dqs)]
-    dq_far = swapped(dq_last, "outer", nq - 1)
     dkv = []
     for t in range(1, nz // 2):
         dkv.append(crossed(far[2 * t - 2], t, False))
@@ -339,15 +339,15 @@
     dkv_near = swapped(dkv_near, "inner", 2)
 
     dkv_sum = sum_call(dkv_own, dkv, 1_500_000_000)
-    dq_sum = sum_call(dq_own, got, 100_000_000)
+    dq_sum = sum_call(dq_own, [dq_far], 100_000_000)
     return pl.pallas_call(
         functools.partial(final_kernel, rows, heads, scale),
         out_shape=(sds((rows, heads * width), BF), sds((rows, width), BF), sds((rows, width), BF)),
-        in_specs=[VMEM] * 4,
+        in_specs=[VMEM] * (3 + len(got)),
         out_specs=(VMEM,) * 3,
         compiler_params=SMALL,
         cost_estimate=QUICK,
-    )(dq_sum, dq_far, dkv_sum, dkv_near)
+    )(dq_sum, dkv_sum, dkv_near, *got)
 
 
 def solution(mesh):

time: 34.7 us -> 34.5 us (level)
    pallas_call x8 -> x7, Pallas kernels: 6.51 us -> 6.36 us  [blocks_call(): pl.pallas_call(functools.partial(blocks_kernel, plan, rows, heads, scale)...]
  transfers between devices with their start and end apart: 18 -> 18, of which waited for: 3 -> 4; matrix products, arithmetic and copies ran while one was open for 0% -> 0% of each run, Pallas kernels for 17% -> 17%
where the time goes in v18:
time: 34.5 us; the launch traced here: 34.3 us
  starting transfers between devices  21.6 us (63%)
  Pallas kernels  8.6 us (25%)
  waiting for transfers between devices  3.25 us (9%)
  between operations  0.79 us (2%)
    ppermute x14, starting transfers between devices, swapped(): return lax.ppermute(block, axis, pairs)  14 us
    ppermute x4, starting transfers between devices, crossed(): return lax.ppermute(block, 'inner', pairs)  7.66 us
    pallas_call x7, Pallas kernels, blocks_call(): pl.pallas_call(functools.partial(blocks_kernel, plan, rows, heads, scale)...  6.36 us
    ppermute x4, waiting for transfers between devices, crossed(): return lax.ppermute(block, 'inner', pairs)  2.36 us
    pallas_call x1, Pallas kernels, on_device(): pl.pallas_call(pack_kernel, out_shape=(sds((2 * hr + 32, width), BF), sds...  1.34 us
    ppermute x14, waiting for transfers between devices, swapped(): return lax.ppermute(block, axis, pairs)  0.89 us
    pallas_call x1, Pallas kernels, on_device(): pl.pallas_call(functools.partial(final_kernel, rows, heads, scale), out_s...  0.78 us
  transfers between devices with their start and end apart: 18, of which 4 were waited for; matrix products, arithmetic and copies ran while one was open for 0% of the time, Pallas kernels for 17%

profile of v18, /device:TPU:0, one launch (start us, length us, event | category | flops | bytes accessed | tf_op | source)
XLA Modules:
  0.0 34.3 jit_solution(2047710902370768703)
XLA Ops:
  0.6 1.3 %shard_map.94 = (bf16[1056,128]{1,0:T(8,128)(2,1)S(1)}, bf16[272,128]{1,0:T(8,128)(2,1)S(1)}) custom-call(bf16[128,512]{1,0:T(8,128)(2,1)} %q_ref.1, bf16[128,128]{1,0:T(8,128)(2,1)} %k_ref.1, bf16[128,128]{1,0:T(8,128)(2,1)} %v_ref.1, bf16[128,512]{1,0:T(8,128)(2,1)} %o_ref.1, bf16[128,512]{1,0:T(8,128)(2,1)} %g_ref.1, f32[4,128]{1,0:T(4,128)} %lse_ref.1, ...), custom_call_target="tpu_custom_call" | custom-call | flops 1000 | bytes 1000 | tf_op jit(solution)/shard_map/pallas_call | solution.py:283
  2.0 3.0 %collective-permute-start = (bf16[1056,128]{1,0:T(8,128)(2,1)S(1)}, bf16[1056,128]{1,0:T(8,128)(2,1)S(1)}, u32[]{:S(2)}, u32[]{:S(2)}) collective-permute-start(bf16[1056,128]{1,0:T(8,128)(2,1)S(1)} %get-tuple-element.34.refs_0_), channel_id=1, source_target_pairs={{0,8},{8,0},{16,24},{24,16},{1,9},{9,1},{17,25},{25,17},{2,10},{10... | collective-permute-start | bytes 811016 | tf_op jit(solution)/shard_map/ppermute | solution.py:25
  5.0 1.5 %collective-permute-start.3 = (bf16[1056,128]{1,0:T(8,128)(2,1)S(1)}, bf16[1056,128]{1,0:T(8,128)(2,1)S(1)}, u32[]{:S(2)}, u32[]{:S(2)}) collective-permute-start(bf16[1056,128]{1,0:T(8,128)(2,1)S(1)} %get-tuple-element.34.refs_0_), channel_id=1, source_target_pairs={{0,16},{8,24},{16,0},{24,8},{1,17},{9,25},{17,1},{25,9},{2,18},{10... | collective-permute-start | bytes 811016 | tf_op jit(solution)/shard_map/ppermute | solution.py:25
  6.5 1.6 %collective-permute-start.2 = (bf16[272,128]{1,0:T(8,128)(2,1)S(1)}, bf16[272,128]{1,0:T(8,128)(2,1)S(1)}, u32[]{:S(2)}, u32[]{:S(2)}) collective-permute-start(bf16[272,128]{1,0:T(8,128)(2,1)S(1)} %get-tuple-element.35.refs_1_.refs_2_), channel_id=1, source_target_pairs={{0,2},{1,3},{2,0},{3,1},{4,6},{5,7},{6,4},{7,5},{8,10},{9,11},{10,... | collective-permute-start | bytes 208904 | tf_op jit(solution)/shard_map/ppermute | solution.py:25
  8.1 2.5 %collective-permute-start.4 = (bf16[272,128]{1,0:T(8,128)(2,1)S(1)}, bf16[272,128]{1,0:T(8,128)(2,1)S(1)}, u32[]{:S(2)}, u32[]{:S(2)}) collective-permute-start(bf16[272,128]{1,0:T(8,128)(2,1)S(1)} %get-tuple-element.35.refs_1_.refs_2_), channel_id=1, source_target_pairs={{0,6},{1,5},{2,4},{3,7},{4,2},{5,1},{6,0},{7,3},{8,14},{9,13},{10,... | collective-permute-start | bytes 208904 | tf_op jit(solution)/shard_map/ppermute | solution.py:271
  10.6 1.3 %collective-permute-start.5 = (bf16[272,128]{1,0:T(8,128)(2,1)S(1)}, bf16[272,128]{1,0:T(8,128)(2,1)S(1)}, u32[]{:S(2)}, u32[]{:S(2)}) collective-permute-start(bf16[272,128]{1,0:T(8,128)(2,1)S(1)} %collective-permute-done.1.refs_2_.refs_3_), channel_id=1, source_target_pairs={{0,6},{1,5},{2,4},{3,7},{4,2},{5,1},{6,0},{7,3},{8,14},{9,13},{10,... | collective-permute-start | bytes 208904 | tf_op jit(solution)/shard_map/ppermute | solution.py:271
  11.9 0.7 %shard_map.95 = (f32[128,512]{1,0:T(8,128)S(1)}, f32[3,256,128]{2,1,0:T(8,128)S(1)}) custom-call(bf16[1056,128]{1,0:T(8,128)(2,1)S(1)} %get-tuple-element.34.refs_0_, bf16[272,128]{1,0:T(8,128)(2,1)S(1)} %get-tuple-element.35.refs_1_.refs_2_, bf16[272,128]{1,0:T(8,128)(2,1)S(1)} %collective-permute-done.1.refs_2_.refs_3_, ...), custom_call_target="tpu_custom_call" | custom-call | flops 1000 | bytes 1000 | tf_op jit(solution)/shard_map/pallas_call | solution.py:209
  12.6 0.7 %collective-permute-start.10 = (bf16[544,128]{1,0:T(8,128)(2,1)S(1)}, bf16[544,128]{1,0:T(8,128)(2,1)S(1)}, u32[]{:S(2)}, u32[]{:S(2)}) collective-permute-start(bf16[544,128]{1,0:T(8,128)(2,1)S(1)} %slice.7), channel_id=1, source_target_pairs={{0,16},{8,24},{16,0},{24,8},{1,17},{9,25},{17,1},{25,9},{2,18},{10... | collective-permute-start | bytes 417800 | tf_op jit(solution)/shard_map/ppermute | solution.py:25
  13.3 0.7 %shard_map.96 = (f32[128,512]{1,0:T(8,128)S(1)}, f32[3,256,128]{2,1,0:T(8,128)S(1)}) custom-call(bf16[1056,128]{1,0:T(8,128)(2,1)S(1)} %collective-permute-done.refs_0_.refs_1_, bf16[272,128]{1,0:T(8,128)(2,1)S(1)} %get-tuple-element.35.refs_1_.refs_2_, bf16[272,128]{1,0:T(8,128)(2,1)S(1)} %collective-permute-done.1.refs_2_.refs_3_, ...), custom_call_target="tpu_custom_call" | custom-call | flops 1000 | bytes 1000 | tf_op jit(solution)/shard_map/pallas_call | solution.py:209
  14.0 1.6 %collective-permute-start.9 = (bf16[512,128]{1,0:T(8,128)(2,1)S(1)}, bf16[512,128]{1,0:T(8,128)(2,1)S(1)}, u32[]{:S(2)}, u32[]{:S(2)}) collective-permute-start(bf16[512,128]{1,0:T(8,128)(2,1)S(1)} %slice.6), channel_id=1, source_target_pairs={{0,8},{8,0},{16,24},{24,16},{1,9},{9,1},{17,25},{25,17},{2,10},{10... | collective-permute-start | bytes 393224 | tf_op jit(solution)/shard_map/ppermute | solution.py:25
  15.6 0.0 collective-permute-start.8
  15.6 0.7 %shard_map.97 = (f32[128,512]{1,0:T(8,128)S(1)}, f32[3,256,128]{2,1,0:T(8,128)S(1)}) custom-call(bf16[1056,128]{1,0:T(8,128)(2,1)S(1)} %collective-permute-done.3.refs_0_.refs_2_, bf16[272,128]{1,0:T(8,128)(2,1)S(1)} %get-tuple-element.35.refs_1_.refs_2_, bf16[272,128]{1,0:T(8,128)(2,1)S(1)} %collective-permute-done.1.refs_2_.refs_3_, ...), custom_call_target="tpu_custom_call" | custom-call | flops 1000 | bytes 1000 | tf_op jit(solution)/shard_map/pallas_call | solution.py:209
  16.3 0.5 %collective-permute-done.5.refs_5_.refs_7_ = bf16[272,128]{1,0:T(8,128)(2,1)S(1)} collective-permute-done((bf16[272,128]{1,0:T(8,128)(2,1)S(1)}, bf16[272,128]{1,0:T(8,128)(2,1)S(1)}, u32[]{:S(2)}, u32[]{:S(2)}) %collective-permute-start.5) | collective-permute-done | bytes 69664 | tf_op jit(solution)/shard_map/ppermute | solution.py:271
  16.8 0.8 %collective-permute-start.6 = (bf16[272,128]{1,0:T(8,128)(2,1)S(1)}, bf16[272,128]{1,0:T(8,128)(2,1)S(1)}, u32[]{:S(2)}, u32[]{:S(2)}) collective-permute-start(bf16[272,128]{1,0:T(8,128)(2,1)S(1)} %collective-permute-done.4.refs_4_.refs_6_), channel_id=1, source_target_pairs={{0,1},{1,0},{2,3},{3,2},{4,5},{5,4},{6,7},{7,6},{8,9},{9,8},{10,11... | collective-permute-start | bytes 208904 | tf_op jit(solution)/shard_map/ppermute | solution.py:25
  17.6 0.0 collective-permute-start.7
  17.6 0.0 collective-permute-done.8.refs_3_.refs_5_
  17.6 1.6 %shard_map.98 = (f32[128,512]{1,0:T(8,128)S(1)}, f32[128,512]{1,0:T(8,128)S(1)}, f32[128,512]{1,0:T(8,128)S(1)}, f32[3,256,128]{2,1,0:T(8,128)S(1)}) custom-call(bf16[1056,128]{1,0:T(8,128)(2,1)S(1)} %get-tuple-element.34.refs_0_, bf16[1056,128]{1,0:T(8,128)(2,1)S(1)} %collective-permute-done.refs_0_.refs_1_, ...), custom_call_target="tpu_custom_call" | custom-call | flops 1000 | bytes 1000 | tf_op jit(solution)/shard_map/pallas_call | solution.py:209
  19.2 0.0 collective-permute-done.6.refs_3_.refs_8_
  19.2 1.1 %shard_map.99 = (f32[128,512]{1,0:T(8,128)S(1)}, bf16[128,512]{1,0:T(8,128)(2,1)S(1)}, bf16[128,512]{1,0:T(8,128)(2,1)S(1)}, f32[2,256,128]{2,1,0:T(8,128)S(1)}) custom-call(bf16[1056,128]{1,0:T(8,128)(2,1)S(1)} %get-tuple-element.34.refs_0_, bf16[1056,128]{1,0:T(8,128)(2,1)S(1)} %collective-permute-done.refs_0_.refs_1_, ...), custom_call_target="tpu_custom_call" | custom-call | flops 1000 | bytes 1000 | tf_op jit(solution)/shard_map/pallas_call | solution.py:209
  20.4 0.8 %shard_map.100 = (f32[128,512]{1,0:T(8,128)S(1)}, bf16[4,256,128]{2,1,0:T(8,128)(2,1)S(1)}) custom-call(bf16[512,128]{1,0:T(8,128)(2,1)S(1)} %collective-permute-done.9.refs_0_, bf16[544,128]{1,0:T(8,128)(2,1)S(1)} %collective-permute-done.10.refs_1_, bf16[272,128]{1,0:T(8,128)(2,1)S(1)} %get-tuple-element.35.refs_1_.refs_2_, ...), custom_call_target="tpu_custom_call" | custom-call | flops 1000 | bytes 1000 | tf_op jit(solution)/shard_map/pallas_call | solution.py:209
  21.2 0.6 %collective-permute-start.12 = (bf16[4,256,128]{2,1,0:T(8,128)(2,1)S(1)}, bf16[4,256,128]{2,1,0:T(8,128)(2,1)S(1)}, u32[]{:S(2)}, u32[]{:S(2)}) collective-permute-start(bf16[4,256,128]{2,1,0:T(8,128)(2,1)S(1)} %get-tuple-element.58), channel_id=1, source_target_pairs={{0,1},{1,0},{2,3},{3,2},{4,5},{5,4},{6,7},{7,6},{8,9},{9,8},{10,11... | collective-permute-start | bytes 786440 | tf_op jit(solution)/shard_map/ppermute | solution.py:25
  21.8 0.8 %shard_map.101 = (bf16[128,512]{1,0:T(8,128)(2,1)S(1)}, f32[4,256,128]{2,1,0:T(8,128)S(1)}) custom-call(bf16[512,128]{1,0:T(8,128)(2,1)S(1)} %collective-permute-done.9.refs_0_, bf16[544,128]{1,0:T(8,128)(2,1)S(1)} %collective-permute-done.10.refs_1_, bf16[272,128]{1,0:T(8,128)(2,1)S(1)} %get-tuple-element.35.refs_1_.refs_2_, ...), custom_call_target="tpu_custom_call" | custom-call | flops 1000 | bytes 1000 | tf_op jit(solution)/shard_map/pallas_call | solution.py:209
  22.6 0.7 %collective-permute-start.11 = (bf16[128,512]{1,0:T(8,128)(2,1)S(1)}, bf16[128,512]{1,0:T(8,128)(2,1)S(1)}, u32[]{:S(2)}, u32[]{:S(2)}) collective-permute-start(bf16[128,512]{1,0:T(8,128)(2,1)S(1)} %get-tuple-element.56), channel_id=1, source_target_pairs={{0,24},{8,16},{16,8},{24,0},{1,25},{9,17},{17,9},{25,1},{2,26},{10... | collective-permute-start | bytes 393224 | tf_op jit(solution)/shard_map/ppermute | solution.py:25
  23.3 0.1 shard_map.103
  23.4 3.8 %collective-permute-start.13 = (bf16[256,128]{1,0:T(8,128)(2,1)S(1)}, bf16[256,128]{1,0:T(8,128)(2,1)S(1)}, u32[]{:S(2)}, u32[]{:S(2)}) collective-permute-start(bf16[256,128]{1,0:T(8,128)(2,1)S(1)} %get-tuple-element.60), channel_id=1, source_target_pairs={{0,6},{1,5},{2,4},{3,7},{4,2},{5,1},{6,0},{7,3},{8,14},{9,13},{10,... | collective-permute-start | bytes 196616 | tf_op jit(solution)/shard_map/ppermute | solution.py:271
  27.2 0.6 %collective-permute-start.16 = (bf16[128,512]{1,0:T(8,128)(2,1)S(1)}, bf16[128,512]{1,0:T(8,128)(2,1)S(1)}, u32[]{:S(2)}, u32[]{:S(2)}) collective-permute-start(bf16[128,512]{1,0:T(8,128)(2,1)S(1)} %get-tuple-element.63), channel_id=1, source_target_pairs={{0,8},{8,0},{16,24},{24,16},{1,9},{9,1},{17,25},{25,17},{2,10},{10... | collective-permute-start | bytes 393224 | tf_op jit(solution)/shard_map/ppermute | solution.py:25
  27.7 1.4 %collective-permute-start.17 = (bf16[128,512]{1,0:T(8,128)(2,1)S(1)}, bf16[128,512]{1,0:T(8,128)(2,1)S(1)}, u32[]{:S(2)}, u32[]{:S(2)}) collective-permute-start(bf16[128,512]{1,0:T(8,128)(2,1)S(1)} %get-tuple-element.64), channel_id=1, source_target_pairs={{0,16},{8,24},{16,0},{24,8},{1,17},{9,25},{17,1},{25,9},{2,18},{10... | collective-permute-start | bytes 393224 | tf_op jit(solution)/shard_map/ppermute | solution.py:25
  29.2 1.6 %collective-permute-start.15 = (bf16[256,128]{1,0:T(8,128)(2,1)S(1)}, bf16[256,128]{1,0:T(8,128)(2,1)S(1)}, u32[]{:S(2)}, u32[]{:S(2)}) collective-permute-start(bf16[256,128]{1,0:T(8,128)(2,1)S(1)} %get-tuple-element.62), channel_id=1, source_target_pairs={{0,2},{1,3},{2,0},{3,1},{4,6},{5,7},{6,4},{7,5},{8,10},{9,11},{10,... | collective-permute-start | bytes 196616 | tf_op jit(solution)/shard_map/ppermute | solution.py:25
  30.8 1.8 %collective-permute-done.14.refs_1_ = bf16[256,128]{1,0:T(8,128)(2,1)S(1)} collective-permute-done((bf16[256,128]{1,0:T(8,128)(2,1)S(1)}, bf16[256,128]{1,0:T(8,128)(2,1)S(1)}, u32[]{:S(2)}, u32[]{:S(2)}) %collective-permute-start.14) | collective-permute-done | bytes 65568 | tf_op jit(solution)/shard_map/ppermute | solution.py:271
  32.7 0.1 collective-permute-done.17.refs_1_
  32.7 0.8 %collective-permute-done.15.dkv_near = bf16[256,128]{1,0:T(8,128)(2,1)S(1)} collective-permute-done((bf16[256,128]{1,0:T(8,128)(2,1)S(1)}, bf16[256,128]{1,0:T(8,128)(2,1)S(1)}, u32[]{:S(2)}, u32[]{:S(2)}) %collective-permute-start.15) | collective-permute-done | bytes 65568 | tf_op jit(solution)/shard_map/ppermute | solution.py:25
  33.5 0.8 %shard_map.105 = (bf16[128,512]{1,0:T(8,128)(2,1)}, bf16[128,128]{1,0:T(8,128)(2,1)}, bf16[128,128]{1,0:T(8,128)(2,1)}) custom-call(f32[128,512]{1,0:T(8,128)S(1)} %shard_map.102.dq_ref, f32[256,128]{1,0:T(8,128)S(1)} %shard_map.104.dkv_ref, bf16[256,128]{1,0:T(8,128)(2,1)S(1)} %collective-permute-done.15.dkv_near, ...), custom_call_target="tpu_custom_call" | custom-call | flops 1000 | bytes 1000 | tf_op jit(solution)/shard_map/pallas_call | solution.py:343
  (18 shorter events, 0.1 us)
Async XLA Ops:
  2.0 10.6 %collective-permute-start = (bf16[1056,128]{1,0:T(8,128)(2,1)S(1)}, bf16[1056,128]{1,0:T(8,128)(2,1)S(1)}, u32[]{:S(2)}, u32[]{:S(2)}) collective-permute-start(bf16[1056,128]{1,0:T(8,128)(2,1)S(1)} %get-tuple-element.34.refs_0_), channel_id=1, source_target_pairs={{0,8},{8,0},{16,24},{24,16},{1,9},{9,1},{17,25},{25,17},{2,10},{10... | collective-permute-start | bytes 811016 | tf_op jit(solution)/shard_map/ppermute | solution.py:25
  5.0 9.0 %collective-permute-start.3 = (bf16[1056,128]{1,0:T(8,128)(2,1)S(1)}, bf16[1056,128]{1,0:T(8,128)(2,1)S(1)}, u32[]{:S(2)}, u32[]{:S(2)}) collective-permute-start(bf16[1056,128]{1,0:T(8,128)(2,1)S(1)} %get-tuple-element.34.refs_0_), channel_id=1, source_target_pairs={{0,16},{8,24},{16,0},{24,8},{1,17},{9,25},{17,1},{25,9},{2,18},{10... | collective-permute-start | bytes 811016 | tf_op jit(solution)/shard_map/ppermute | solution.py:25
  6.5 4.1 %collective-permute-start.1 = (bf16[272,128]{1,0:T(8,128)(2,1)S(1)}, bf16[272,128]{1,0:T(8,128)(2,1)S(1)}, u32[]{:S(2)}, u32[]{:S(2)}) collective-permute-start(bf16[272,128]{1,0:T(8,128)(2,1)S(1)} %get-tuple-element.35.refs_1_.refs_2_), channel_id=1, source_target_pairs={{0,1},{1,0},{2,3},{3,2},{4,5},{5,4},{6,7},{7,6},{8,9},{9,8},{10,11... | collective-permute-start | bytes 208904 | tf_op jit(solution)/shard_map/ppermute | solution.py:25
  6.5 5.4 %collective-permute-start.2 = (bf16[272,128]{1,0:T(8,128)(2,1)S(1)}, bf16[272,128]{1,0:T(8,128)(2,1)S(1)}, u32[]{:S(2)}, u32[]{:S(2)}) collective-permute-start(bf16[272,128]{1,0:T(8,128)(2,1)S(1)} %get-tuple-element.35.refs_1_.refs_2_), channel_id=1, source_target_pairs={{0,2},{1,3},{2,0},{3,1},{4,6},{5,7},{6,4},{7,5},{8,10},{9,11},{10,... | collective-permute-start | bytes 208904 | tf_op jit(solution)/shard_map/ppermute | solution.py:25
  8.1 8.2 %collective-permute-start.4 = (bf16[272,128]{1,0:T(8,128)(2,1)S(1)}, bf16[272,128]{1,0:T(8,128)(2,1)S(1)}, u32[]{:S(2)}, u32[]{:S(2)}) collective-permute-start(bf16[272,128]{1,0:T(8,128)(2,1)S(1)} %get-tuple-element.35.refs_1_.refs_2_), channel_id=1, source_target_pairs={{0,6},{1,5},{2,4},{3,7},{4,2},{5,1},{6,0},{7,3},{8,14},{9,13},{10,... | collective-permute-start | bytes 208904 | tf_op jit(solution)/shard_map/ppermute | solution.py:271
  10.6 6.2 %collective-permute-start.5 = (bf16[272,128]{1,0:T(8,128)(2,1)S(1)}, bf16[272,128]{1,0:T(8,128)(2,1)S(1)}, u32[]{:S(2)}, u32[]{:S(2)}) collective-permute-start(bf16[272,128]{1,0:T(8,128)(2,1)S(1)} %collective-permute-done.1.refs_2_.refs_3_), channel_id=1, source_target_pairs={{0,6},{1,5},{2,4},{3,7},{4,2},{5,1},{6,0},{7,3},{8,14},{9,13},{10,... | collective-permute-start | bytes 208904 | tf_op jit(solution)/shard_map/ppermute | solution.py:271
  12.6 7.8 %collective-permute-start.10 = (bf16[544,128]{1,0:T(8,128)(2,1)S(1)}, bf16[544,128]{1,0:T(8,128)(2,1)S(1)}, u32[]{:S(2)}, u32[]{:S(2)}) collective-permute-start(bf16[544,128]{1,0:T(8,128)(2,1)S(1)} %slice.7), channel_id=1, source_target_pairs={{0,16},{8,24},{16,0},{24,8},{1,17},{9,25},{17,1},{25,9},{2,18},{10... | collective-permute-start | bytes 417800 | tf_op jit(solution)/shard_map/ppermute | solution.py:25
  14.0 6.4 %collective-permute-start.9 = (bf16[512,128]{1,0:T(8,128)(2,1)S(1)}, bf16[512,128]{1,0:T(8,128)(2,1)S(1)}, u32[]{:S(2)}, u32[]{:S(2)}) collective-permute-start(bf16[512,128]{1,0:T(8,128)(2,1)S(1)} %slice.6), channel_id=1, source_target_pairs={{0,8},{8,0},{16,24},{24,16},{1,9},{9,1},{17,25},{25,17},{2,10},{10... | collective-permute-start | bytes 393224 | tf_op jit(solution)/shard_map/ppermute | solution.py:25
  15.6 2.0 %collective-permute-start.8 = (bf16[272,128]{1,0:T(8,128)(2,1)S(1)}, bf16[272,128]{1,0:T(8,128)(2,1)S(1)}, u32[]{:S(2)}, u32[]{:S(2)}) collective-permute-start(bf16[272,128]{1,0:T(8,128)(2,1)S(1)} %collective-permute-done.2.refs_3_.refs_4_), channel_id=1, source_target_pairs={{0,1},{1,0},{2,3},{3,2},{4,5},{5,4},{6,7},{7,6},{8,9},{9,8},{10,11... | collective-permute-start | bytes 208904 | tf_op jit(solution)/shard_map/ppermute | solution.py:25
  16.8 2.4 %collective-permute-start.6 = (bf16[272,128]{1,0:T(8,128)(2,1)S(1)}, bf16[272,128]{1,0:T(8,128)(2,1)S(1)}, u32[]{:S(2)}, u32[]{:S(2)}) collective-permute-start(bf16[272,128]{1,0:T(8,128)(2,1)S(1)} %collective-permute-done.4.refs_4_.refs_6_), channel_id=1, source_target_pairs={{0,1},{1,0},{2,3},{3,2},{4,5},{5,4},{6,7},{7,6},{8,9},{9,8},{10,11... | collective-permute-start | bytes 208904 | tf_op jit(solution)/shard_map/ppermute | solution.py:25
  17.6 1.6 %collective-permute-start.7 = (bf16[272,128]{1,0:T(8,128)(2,1)S(1)}, bf16[272,128]{1,0:T(8,128)(2,1)S(1)}, u32[]{:S(2)}, u32[]{:S(2)}) collective-permute-start(bf16[272,128]{1,0:T(8,128)(2,1)S(1)} %collective-permute-done.5.refs_5_.refs_7_), channel_id=1, source_target_pairs={{0,1},{1,0},{2,3},{3,2},{4,5},{5,4},{6,7},{7,6},{8,9},{9,8},{10,11... | collective-permute-start | bytes 208904 | tf_op jit(solution)/shard_map/ppermute | solution.py:25
  21.2 2.1 %collective-permute-start.12 = (bf16[4,256,128]{2,1,0:T(8,128)(2,1)S(1)}, bf16[4,256,128]{2,1,0:T(8,128)(2,1)S(1)}, u32[]{:S(2)}, u32[]{:S(2)}) collective-permute-start(bf16[4,256,128]{2,1,0:T(8,128)(2,1)S(1)} %get-tuple-element.58), channel_id=1, source_target_pairs={{0,1},{1,0},{2,3},{3,2},{4,5},{5,4},{6,7},{7,6},{8,9},{9,8},{10,11... | collective-permute-start | bytes 786440 | tf_op jit(solution)/shard_map/ppermute | solution.py:25
  22.6 6.6 %collective-permute-start.11 = (bf16[128,512]{1,0:T(8,128)(2,1)S(1)}, bf16[128,512]{1,0:T(8,128)(2,1)S(1)}, u32[]{:S(2)}, u32[]{:S(2)}) collective-permute-start(bf16[128,512]{1,0:T(8,128)(2,1)S(1)} %get-tuple-element.56), channel_id=1, source_target_pairs={{0,24},{8,16},{16,8},{24,0},{1,25},{9,17},{17,9},{25,1},{2,26},{10... | collective-permute-start | bytes 393224 | tf_op jit(solution)/shard_map/ppermute | solution.py:25
  23.4 7.4 %collective-permute-start.13 = (bf16[256,128]{1,0:T(8,128)(2,1)S(1)}, bf16[256,128]{1,0:T(8,128)(2,1)S(1)}, u32[]{:S(2)}, u32[]{:S(2)}) collective-permute-start(bf16[256,128]{1,0:T(8,128)(2,1)S(1)} %get-tuple-element.60), channel_id=1, source_target_pairs={{0,6},{1,5},{2,4},{3,7},{4,2},{5,1},{6,0},{7,3},{8,14},{9,13},{10,... | collective-permute-start | bytes 196616 | tf_op jit(solution)/shard_map/ppermute | solution.py:271
  27.2 5.4 %collective-permute-start.14 = (bf16[256,128]{1,0:T(8,128)(2,1)S(1)}, bf16[256,128]{1,0:T(8,128)(2,1)S(1)}, u32[]{:S(2)}, u32[]{:S(2)}) collective-permute-start(bf16[256,128]{1,0:T(8,128)(2,1)S(1)} %get-tuple-element.61), channel_id=1, source_target_pairs={{0,4},{1,7},{2,6},{3,5},{4,0},{5,3},{6,2},{7,1},{8,12},{9,15},{10,... | collective-permute-start | bytes 196616 | tf_op jit(solution)/shard_map/ppermute | solution.py:271
  27.2 5.5 %collective-permute-start.16 = (bf16[128,512]{1,0:T(8,128)(2,1)S(1)}, bf16[128,512]{1,0:T(8,128)(2,1)S(1)}, u32[]{:S(2)}, u32[]{:S(2)}) collective-permute-start(bf16[128,512]{1,0:T(8,128)(2,1)S(1)} %get-tuple-element.63), channel_id=1, source_target_pairs={{0,8},{8,0},{16,24},{24,16},{1,9},{9,1},{17,25},{25,17},{2,10},{10... | collective-permute-start | bytes 393224 | tf_op jit(solution)/shard_map/ppermute | solution.py:25
  27.7 5.0 %collective-permute-start.17 = (bf16[128,512]{1,0:T(8,128)(2,1)S(1)}, bf16[128,512]{1,0:T(8,128)(2,1)S(1)}, u32[]{:S(2)}, u32[]{:S(2)}) collective-permute-start(bf16[128,512]{1,0:T(8,128)(2,1)S(1)} %get-tuple-element.64), channel_id=1, source_target_pairs={{0,16},{8,24},{16,0},{24,8},{1,17},{9,25},{17,1},{25,9},{2,18},{10... | collective-permute-start | bytes 393224 | tf_op jit(solution)/shard_map/ppermute | solution.py:25
  29.2 4.3 %collective-permute-start.15 = (bf16[256,128]{1,0:T(8,128)(2,1)S(1)}, bf16[256,128]{1,0:T(8,128)(2,1)S(1)}, u32[]{:S(2)}, u32[]{:S(2)}) collective-permute-start(bf16[256,128]{1,0:T(8,128)(2,1)S(1)} %get-tuple-element.62), channel_id=1, source_target_pairs={{0,2},{1,3},{2,0},{3,1},{4,6},{5,7},{6,4},{7,5},{8,10},{9,11},{10,... | collective-permute-start | bytes 196616 | tf_op jit(solution)/shard_map/ppermute | solution.py:25

commit v19 on v18

--- a/solution.py
+++ b/solution.py
@@ -250,17 +250,18 @@
     )(own, *got)
 
 
-def final_kernel(rows, heads, scale, dq_ref, dkv_ref, dkv_near, *refs):
-    got, (gq_ref, gk_ref, gv_ref) = refs[:-3], refs[-3:]
-    dkv = dkv_ref[...] + dkv_near[...].astype(F32)
-    gk_ref[...] = (scale * dkv[:rows]).astype(BF)
-    gv_ref[...] = dkv[rows:].astype(BF)
+def query_kernel(rows, heads, scale, dq_ref, *refs):
     dq = dq_ref[...]
-    for ref in got:
+    for ref in refs[:-1]:
         dq = dq + ref[...].astype(F32)
     for h in range(heads):
         part = dq[:, h * rows : (h + 1) * rows]
-        gq_ref[:, h * 128 : (h + 1) * 128] = (scale * part).T.astype(BF)
+        refs[-1][:, h * 128 : (h + 1) * 128] = (scale * part).T.astype(BF)
+
+
+def key_kernel(rows, scale, dkv_ref, near_ref, gk_ref, gv_ref):
+    gk_ref[...] = (scale * (dkv_ref[:rows, :] + near_ref[:rows, :].astype(F32))).astype(BF)
+    gv_ref[...] = (dkv_ref[rows:, :] + near_ref[rows:, :].astype(F32)).astype(BF)
 
 
 def crossed(block, t, other):
@@ -340,14 +341,25 @@
 
     dkv_sum = sum_call(dkv_own, dkv, 1_500_000_000)
     dq_sum = sum_call(dq_own, [dq_far], 100_000_000)
-    return pl.pallas_call(
-        functools.partial(final_kernel, rows, heads, scale),
-        out_shape=(sds((rows, heads * width), BF), sds((rows, width), BF), sds((rows, width), BF)),
-        in_specs=[VMEM] * (3 + len(got)),
-        out_specs=(VMEM,) * 3,
-        compiler_params=SMALL,
-        cost_estimate=QUICK,
-    )(dq_sum, dkv_sum, dkv_near, *got)
+    dq_sum, dkv_sum = lax.optimization_barrier((dq_sum, dkv_sum))
+    grad_query = pl.pallas_call(
+        functools.partial(query_kernel, rows, heads, scale),
+        out_shape=sds((rows, heads * width), BF),
+        in_specs=[VMEM] * (1 + len(got)),
+        out_specs=VMEM,
+        compiler_params=SMALL,
+        cost_estimate=QUICK,
+    )(dq_sum, *got)
+    dkv_near, grad_query = lax.optimization_barrier((dkv_near, grad_query))
+    grad_key, grad_value = pl.pallas_call(
+        functools.partial(key_kernel, rows, scale),
+        out_shape=(sds((rows, width), BF),) * 2,
+        in_specs=[VMEM] * 2,
+        out_specs=(VMEM,) * 2,
+        compiler_params=SMALL,
+        cost_estimate=QUICK,
+    )(dkv_sum, dkv_near)
+    return grad_query, grad_key, grad_value
 
 
 def solution(mesh):

time: 34.5 us -> 34.3 us (level)
  waiting for transfers between devices: 3.25 us -> 2.47 us
  Pallas kernels: 8.6 us -> 9.23 us
    ppermute x14, waiting for transfers between devices: 0.89 us -> 0.11 us  [swapped(): return lax.ppermute(block, axis, pairs)]
    pallas_call x1 -> x2, Pallas kernels: 0.78 us -> 1.41 us  [the longest x1 0.77 us: on_device(): pl.pallas_call(functools.partial(query_kernel, rows, heads, scale), out_s...]
  transfers between devices with their start and end apart: 18 -> 18, of which waited for: 4 -> 3; matrix products, arithmetic and copies ran while one was open for 0% -> 0% of each run, Pallas kernels for 17% -> 19%
where the time goes in v19:
time: 34.3 us; the launch traced here: 34.2 us
  starting transfers between devices  21.6 us (63%)
  Pallas kernels  9.23 us (27%)
  waiting for transfers between devices  2.47 us (7%)
  between operations  0.79 us (2%)
    ppermute x14, starting transfers between devices, swapped(): return lax.ppermute(block, axis, pairs)  14 us
    ppermute x4, starting transfers between devices, crossed(): return lax.ppermute(block, 'inner', pairs)  7.66 us
    pallas_call x7, Pallas kernels, blocks_call(): pl.pallas_call(functools.partial(blocks_kernel, plan, rows, heads, scale)...  6.36 us
    ppermute x4, waiting for transfers between devices, crossed(): return lax.ppermute(block, 'inner', pairs)  2.36 us
    pallas_call x1, Pallas kernels, on_device(): pl.pallas_call(pack_kernel, out_shape=(sds((2 * hr + 32, width), BF), sds...  1.34 us
    pallas_call x1, Pallas kernels, on_device(): pl.pallas_call(functools.partial(query_kernel, rows, heads, scale), out_s...  0.77 us
  transfers between devices with their start and end apart: 18, of which 3 were waited for; matrix products, arithmetic and copies ran while one was open for 0% of the time, Pallas kernels for 19%

profile of v19, /device:TPU:0, one launch (start us, length us, event | category | flops | bytes accessed | tf_op | source)
XLA Modules:
  0.0 34.2 jit_solution(7797030929265712819)
XLA Ops:
  0.6 1.3 %shard_map.94 = (bf16[1056,128]{1,0:T(8,128)(2,1)S(1)}, bf16[272,128]{1,0:T(8,128)(2,1)S(1)}) custom-call(bf16[128,512]{1,0:T(8,128)(2,1)} %q_ref.1, bf16[128,128]{1,0:T(8,128)(2,1)} %k_ref.1, bf16[128,128]{1,0:T(8,128)(2,1)} %v_ref.1, bf16[128,512]{1,0:T(8,128)(2,1)} %o_ref.1, bf16[128,512]{1,0:T(8,128)(2,1)} %g_ref.1, f32[4,128]{1,0:T(4,128)} %lse_ref.1, ...), custom_call_target="tpu_custom_call" | custom-call | flops 1000 | bytes 1000 | tf_op jit(solution)/shard_map/pallas_call | solution.py:284
  2.0 3.0 %collective-permute-start.1 = (bf16[1056,128]{1,0:T(8,128)(2,1)S(1)}, bf16[1056,128]{1,0:T(8,128)(2,1)S(1)}, u32[]{:S(2)}, u32[]{:S(2)}) collective-permute-start(bf16[1056,128]{1,0:T(8,128)(2,1)S(1)} %get-tuple-element.40.refs_0_), channel_id=1, source_target_pairs={{0,8},{8,0},{16,24},{24,16},{1,9},{9,1},{17,25},{25,17},{2,10},{10... | collective-permute-start | bytes 811016 | tf_op jit(solution)/shard_map/ppermute | solution.py:25
  5.0 1.5 %collective-permute-start = (bf16[1056,128]{1,0:T(8,128)(2,1)S(1)}, bf16[1056,128]{1,0:T(8,128)(2,1)S(1)}, u32[]{:S(2)}, u32[]{:S(2)}) collective-permute-start(bf16[1056,128]{1,0:T(8,128)(2,1)S(1)} %get-tuple-element.40.refs_0_), channel_id=1, source_target_pairs={{0,16},{8,24},{16,0},{24,8},{1,17},{9,25},{17,1},{25,9},{2,18},{10... | collective-permute-start | bytes 811016 | tf_op jit(solution)/shard_map/ppermute | solution.py:25
  6.5 0.0 collective-permute-start.2
  6.5 1.6 %collective-permute-start.3 = (bf16[272,128]{1,0:T(8,128)(2,1)S(1)}, bf16[272,128]{1,0:T(8,128)(2,1)S(1)}, u32[]{:S(2)}, u32[]{:S(2)}) collective-permute-start(bf16[272,128]{1,0:T(8,128)(2,1)S(1)} %get-tuple-element.41.refs_1_.refs_2_), channel_id=1, source_target_pairs={{0,2},{1,3},{2,0},{3,1},{4,6},{5,7},{6,4},{7,5},{8,10},{9,11},{10,... | collective-permute-start | bytes 208904 | tf_op jit(solution)/shard_map/ppermute | solution.py:25
  8.1 2.5 %collective-permute-start.7 = (bf16[272,128]{1,0:T(8,128)(2,1)S(1)}, bf16[272,128]{1,0:T(8,128)(2,1)S(1)}, u32[]{:S(2)}, u32[]{:S(2)}) collective-permute-start(bf16[272,128]{1,0:T(8,128)(2,1)S(1)} %get-tuple-element.41.refs_1_.refs_2_), channel_id=1, source_target_pairs={{0,6},{1,5},{2,4},{3,7},{4,2},{5,1},{6,0},{7,3},{8,14},{9,13},{10,... | collective-permute-start | bytes 208904 | tf_op jit(solution)/shard_map/ppermute | solution.py:272
  10.6 0.0 collective-permute-done.2.refs_2_.refs_3_
  10.6 1.3 %collective-permute-start.8 = (bf16[272,128]{1,0:T(8,128)(2,1)S(1)}, bf16[272,128]{1,0:T(8,128)(2,1)S(1)}, u32[]{:S(2)}, u32[]{:S(2)}) collective-permute-start(bf16[272,128]{1,0:T(8,128)(2,1)S(1)} %collective-permute-done.2.refs_2_.refs_3_), channel_id=1, source_target_pairs={{0,6},{1,5},{2,4},{3,7},{4,2},{5,1},{6,0},{7,3},{8,14},{9,13},{10,... | collective-permute-start | bytes 208904 | tf_op jit(solution)/shard_map/ppermute | solution.py:272
  11.9 0.7 %shard_map.95 = (f32[128,512]{1,0:T(8,128)S(1)}, f32[3,256,128]{2,1,0:T(8,128)S(1)}) custom-call(bf16[1056,128]{1,0:T(8,128)(2,1)S(1)} %get-tuple-element.40.refs_0_, bf16[272,128]{1,0:T(8,128)(2,1)S(1)} %get-tuple-element.41.refs_1_.refs_2_, bf16[272,128]{1,0:T(8,128)(2,1)S(1)} %collective-permute-done.2.refs_2_.refs_3_, ...), custom_call_target="tpu_custom_call" | custom-call | flops 1000 | bytes 1000 | tf_op jit(solution)/shard_map/pallas_call | solution.py:209
  12.6 0.7 %collective-permute-start.5 = (bf16[544,128]{1,0:T(8,128)(2,1)S(1)}, bf16[544,128]{1,0:T(8,128)(2,1)S(1)}, u32[]{:S(2)}, u32[]{:S(2)}) collective-permute-start(bf16[544,128]{1,0:T(8,128)(2,1)S(1)} %slice.7), channel_id=1, source_target_pairs={{0,16},{8,24},{16,0},{24,8},{1,17},{9,25},{17,1},{25,9},{2,18},{10... | collective-permute-start | bytes 417800 | tf_op jit(solution)/shard_map/ppermute | solution.py:25
  13.3 0.7 %shard_map.96 = (f32[128,512]{1,0:T(8,128)S(1)}, f32[3,256,128]{2,1,0:T(8,128)S(1)}) custom-call(bf16[1056,128]{1,0:T(8,128)(2,1)S(1)} %collective-permute-done.1.refs_0_.refs_1_, bf16[272,128]{1,0:T(8,128)(2,1)S(1)} %get-tuple-element.41.refs_1_.refs_2_, bf16[272,128]{1,0:T(8,128)(2,1)S(1)} %collective-permute-done.2.refs_2_.refs_3_, ...), custom_call_target="tpu_custom_call" | custom-call | flops 1000 | bytes 1000 | tf_op jit(solution)/shard_map/pallas_call | solution.py:209
  14.0 1.6 %collective-permute-start.4 = (bf16[512,128]{1,0:T(8,128)(2,1)S(1)}, bf16[512,128]{1,0:T(8,128)(2,1)S(1)}, u32[]{:S(2)}, u32[]{:S(2)}) collective-permute-start(bf16[512,128]{1,0:T(8,128)(2,1)S(1)} %slice.6), channel_id=1, source_target_pairs={{0,8},{8,0},{16,24},{24,16},{1,9},{9,1},{17,25},{25,17},{2,10},{10... | collective-permute-start | bytes 393224 | tf_op jit(solution)/shard_map/ppermute | solution.py:25
  15.6 0.7 %shard_map.97 = (f32[128,512]{1,0:T(8,128)S(1)}, f32[3,256,128]{2,1,0:T(8,128)S(1)}) custom-call(bf16[1056,128]{1,0:T(8,128)(2,1)S(1)} %collective-permute-done.refs_0_.refs_2_, bf16[272,128]{1,0:T(8,128)(2,1)S(1)} %get-tuple-element.41.refs_1_.refs_2_, bf16[272,128]{1,0:T(8,128)(2,1)S(1)} %collective-permute-done.2.refs_2_.refs_3_, ...), custom_call_target="tpu_custom_call" | custom-call | flops 1000 | bytes 1000 | tf_op jit(solution)/shard_map/pallas_call | solution.py:209
  16.3 0.5 %collective-permute-done.8.refs_5_.refs_7_ = bf16[272,128]{1,0:T(8,128)(2,1)S(1)} collective-permute-done((bf16[272,128]{1,0:T(8,128)(2,1)S(1)}, bf16[272,128]{1,0:T(8,128)(2,1)S(1)}, u32[]{:S(2)}, u32[]{:S(2)}) %collective-permute-start.8) | collective-permute-done | bytes 69664 | tf_op jit(solution)/shard_map/ppermute | solution.py:272
  16.8 0.8 %collective-permute-start.10 = (bf16[272,128]{1,0:T(8,128)(2,1)S(1)}, bf16[272,128]{1,0:T(8,128)(2,1)S(1)}, u32[]{:S(2)}, u32[]{:S(2)}) collective-permute-start(bf16[272,128]{1,0:T(8,128)(2,1)S(1)} %collective-permute-done.8.refs_5_.refs_7_), channel_id=1, source_target_pairs={{0,1},{1,0},{2,3},{3,2},{4,5},{5,4},{6,7},{7,6},{8,9},{9,8},{10,11... | collective-permute-start | bytes 208904 | tf_op jit(solution)/shard_map/ppermute | solution.py:25
  17.6 0.0 collective-permute-start.9
  17.6 1.6 %shard_map.98 = (f32[128,512]{1,0:T(8,128)S(1)}, f32[128,512]{1,0:T(8,128)S(1)}, f32[128,512]{1,0:T(8,128)S(1)}, f32[3,256,128]{2,1,0:T(8,128)S(1)}) custom-call(bf16[1056,128]{1,0:T(8,128)(2,1)S(1)} %get-tuple-element.40.refs_0_, bf16[1056,128]{1,0:T(8,128)(2,1)S(1)} %collective-permute-done.1.refs_0_.refs_1_, ...), custom_call_target="tpu_custom_call" | custom-call | flops 1000 | bytes 1000 | tf_op jit(solution)/shard_map/pallas_call | solution.py:209
  19.2 1.1 %shard_map.99 = (f32[128,512]{1,0:T(8,128)S(1)}, bf16[128,512]{1,0:T(8,128)(2,1)S(1)}, bf16[128,512]{1,0:T(8,128)(2,1)S(1)}, f32[2,256,128]{2,1,0:T(8,128)S(1)}) custom-call(bf16[1056,128]{1,0:T(8,128)(2,1)S(1)} %get-tuple-element.40.refs_0_, bf16[1056,128]{1,0:T(8,128)(2,1)S(1)} %collective-permute-done.1.refs_0_.refs_1_, ...), custom_call_target="tpu_custom_call" | custom-call | flops 1000 | bytes 1000 | tf_op jit(solution)/shard_map/pallas_call | solution.py:209
  20.4 0.8 %shard_map.100 = (f32[128,512]{1,0:T(8,128)S(1)}, bf16[4,256,128]{2,1,0:T(8,128)(2,1)S(1)}) custom-call(bf16[512,128]{1,0:T(8,128)(2,1)S(1)} %collective-permute-done.4.refs_0_, bf16[544,128]{1,0:T(8,128)(2,1)S(1)} %collective-permute-done.5.refs_1_, bf16[272,128]{1,0:T(8,128)(2,1)S(1)} %get-tuple-element.41.refs_1_.refs_2_, ...), custom_call_target="tpu_custom_call" | custom-call | flops 1000 | bytes 1000 | tf_op jit(solution)/shard_map/pallas_call | solution.py:209
  21.2 0.6 %collective-permute-start.11 = (bf16[4,256,128]{2,1,0:T(8,128)(2,1)S(1)}, bf16[4,256,128]{2,1,0:T(8,128)(2,1)S(1)}, u32[]{:S(2)}, u32[]{:S(2)}) collective-permute-start(bf16[4,256,128]{2,1,0:T(8,128)(2,1)S(1)} %get-tuple-element.62), channel_id=1, source_target_pairs={{0,1},{1,0},{2,3},{3,2},{4,5},{5,4},{6,7},{7,6},{8,9},{9,8},{10,11... | collective-permute-start | bytes 786440 | tf_op jit(solution)/shard_map/ppermute | solution.py:25
  21.8 0.8 %shard_map.101 = (bf16[128,512]{1,0:T(8,128)(2,1)S(1)}, f32[4,256,128]{2,1,0:T(8,128)S(1)}) custom-call(bf16[512,128]{1,0:T(8,128)(2,1)S(1)} %collective-permute-done.4.refs_0_, bf16[544,128]{1,0:T(8,128)(2,1)S(1)} %collective-permute-done.5.refs_1_, bf16[272,128]{1,0:T(8,128)(2,1)S(1)} %get-tuple-element.41.refs_1_.refs_2_, ...), custom_call_target="tpu_custom_call" | custom-call | flops 1000 | bytes 1000 | tf_op jit(solution)/shard_map/pallas_call | solution.py:209
  22.6 0.7 %collective-permute-start.13 = (bf16[128,512]{1,0:T(8,128)(2,1)S(1)}, bf16[128,512]{1,0:T(8,128)(2,1)S(1)}, u32[]{:S(2)}, u32[]{:S(2)}) collective-permute-start(bf16[128,512]{1,0:T(8,128)(2,1)S(1)} %get-tuple-element.65), channel_id=1, source_target_pairs={{0,24},{8,16},{16,8},{24,0},{1,25},{9,17},{17,9},{25,1},{2,26},{10... | collective-permute-start | bytes 393224 | tf_op jit(solution)/shard_map/ppermute | solution.py:25
  23.3 0.1 shard_map.102
  23.4 3.8 %collective-permute-start.14 = (bf16[256,128]{1,0:T(8,128)(2,1)S(1)}, bf16[256,128]{1,0:T(8,128)(2,1)S(1)}, u32[]{:S(2)}, u32[]{:S(2)}) collective-permute-start(bf16[256,128]{1,0:T(8,128)(2,1)S(1)} %get-tuple-element.67), channel_id=1, source_target_pairs={{0,6},{1,5},{2,4},{3,7},{4,2},{5,1},{6,0},{7,3},{8,14},{9,13},{10,... | collective-permute-start | bytes 196616 | tf_op jit(solution)/shard_map/ppermute | solution.py:272
  27.2 0.6 %collective-permute-start.16 = (bf16[128,512]{1,0:T(8,128)(2,1)S(1)}, bf16[128,512]{1,0:T(8,128)(2,1)S(1)}, u32[]{:S(2)}, u32[]{:S(2)}) collective-permute-start(bf16[128,512]{1,0:T(8,128)(2,1)S(1)} %get-tuple-element.70), channel_id=1, source_target_pairs={{0,8},{8,0},{16,24},{24,16},{1,9},{9,1},{17,25},{25,17},{2,10},{10... | collective-permute-start | bytes 393224 | tf_op jit(solution)/shard_map/ppermute | solution.py:25
  27.7 1.4 %collective-permute-start.17 = (bf16[128,512]{1,0:T(8,128)(2,1)S(1)}, bf16[128,512]{1,0:T(8,128)(2,1)S(1)}, u32[]{:S(2)}, u32[]{:S(2)}) collective-permute-start(bf16[128,512]{1,0:T(8,128)(2,1)S(1)} %get-tuple-element.71), channel_id=1, source_target_pairs={{0,16},{8,24},{16,0},{24,8},{1,17},{9,25},{17,1},{25,9},{2,18},{10... | collective-permute-start | bytes 393224 | tf_op jit(solution)/shard_map/ppermute | solution.py:25
  29.2 1.6 %collective-permute-start.12 = (bf16[256,128]{1,0:T(8,128)(2,1)S(1)}, bf16[256,128]{1,0:T(8,128)(2,1)S(1)}, u32[]{:S(2)}, u32[]{:S(2)}) collective-permute-start(bf16[256,128]{1,0:T(8,128)(2,1)S(1)} %get-tuple-element.63), channel_id=1, source_target_pairs={{0,2},{1,3},{2,0},{3,1},{4,6},{5,7},{6,4},{7,5},{8,10},{9,11},{10,... | collective-permute-start | bytes 196616 | tf_op jit(solution)/shard_map/ppermute | solution.py:25
  30.8 1.8 %collective-permute-done.15.refs_1_ = bf16[256,128]{1,0:T(8,128)(2,1)S(1)} collective-permute-done((bf16[256,128]{1,0:T(8,128)(2,1)S(1)}, bf16[256,128]{1,0:T(8,128)(2,1)S(1)}, u32[]{:S(2)}, u32[]{:S(2)}) %collective-permute-start.15) | collective-permute-done | bytes 65568 | tf_op jit(solution)/shard_map/ppermute | solution.py:272
  32.7 0.1 collective-permute-done.17.refs_1_
  32.7 0.8 %shard_map.105 = bf16[128,512]{1,0:T(8,128)(2,1)} custom-call(f32[128,512]{1,0:T(8,128)S(1)} %shard_map.103.dq_ref, bf16[128,512]{1,0:T(8,128)(2,1)S(1)} %collective-permute-done.16.refs_0_, bf16[128,512]{1,0:T(8,128)(2,1)S(1)} %collective-permute-done.17.refs_1_), custom_call_target="tpu_custom_call" | custom-call | flops 1000 | bytes 1000 | tf_op jit(solution)/shard_map/pallas_call | solution.py:345
  33.5 0.0 collective-permute-done.12.near_ref
  33.5 0.6 %shard_map.106 = (bf16[128,128]{1,0:T(8,128)(2,1)}, bf16[128,128]{1,0:T(8,128)(2,1)}) custom-call(f32[256,128]{1,0:T(8,128)S(1)} %shard_map.104.dkv_ref, bf16[256,128]{1,0:T(8,128)(2,1)S(1)} %collective-permute-done.12.near_ref), custom_call_target="tpu_custom_call" | custom-call | flops 1000 | bytes 1000 | tf_op jit(solution)/shard_map/pallas_call | solution.py:354
  (19 shorter events, 0.1 us)
Async XLA Ops:
  2.0 10.6 %collective-permute-start.1 = (bf16[1056,128]{1,0:T(8,128)(2,1)S(1)}, bf16[1056,128]{1,0:T(8,128)(2,1)S(1)}, u32[]{:S(2)}, u32[]{:S(2)}) collective-permute-start(bf16[1056,128]{1,0:T(8,128)(2,1)S(1)} %get-tuple-element.40.refs_0_), channel_id=1, source_target_pairs={{0,8},{8,0},{16,24},{24,16},{1,9},{9,1},{17,25},{25,17},{2,10},{10... | collective-permute-start | bytes 811016 | tf_op jit(solution)/shard_map/ppermute | solution.py:25
  5.0 9.0 %collective-permute-start = (bf16[1056,128]{1,0:T(8,128)(2,1)S(1)}, bf16[1056,128]{1,0:T(8,128)(2,1)S(1)}, u32[]{:S(2)}, u32[]{:S(2)}) collective-permute-start(bf16[1056,128]{1,0:T(8,128)(2,1)S(1)} %get-tuple-element.40.refs_0_), channel_id=1, source_target_pairs={{0,16},{8,24},{16,0},{24,8},{1,17},{9,25},{17,1},{25,9},{2,18},{10... | collective-permute-start | bytes 811016 | tf_op jit(solution)/shard_map/ppermute | solution.py:25
  6.5 4.1 %collective-permute-start.2 = (bf16[272,128]{1,0:T(8,128)(2,1)S(1)}, bf16[272,128]{1,0:T(8,128)(2,1)S(1)}, u32[]{:S(2)}, u32[]{:S(2)}) collective-permute-start(bf16[272,128]{1,0:T(8,128)(2,1)S(1)} %get-tuple-element.41.refs_1_.refs_2_), channel_id=1, source_target_pairs={{0,1},{1,0},{2,3},{3,2},{4,5},{5,4},{6,7},{7,6},{8,9},{9,8},{10,11... | collective-permute-start | bytes 208904 | tf_op jit(solution)/shard_map/ppermute | solution.py:25
  6.5 5.4 %collective-permute-start.3 = (bf16[272,128]{1,0:T(8,128)(2,1)S(1)}, bf16[272,128]{1,0:T(8,128)(2,1)S(1)}, u32[]{:S(2)}, u32[]{:S(2)}) collective-permute-start(bf16[272,128]{1,0:T(8,128)(2,1)S(1)} %get-tuple-element.41.refs_1_.refs_2_), channel_id=1, source_target_pairs={{0,2},{1,3},{2,0},{3,1},{4,6},{5,7},{6,4},{7,5},{8,10},{9,11},{10,... | collective-permute-start | bytes 208904 | tf_op jit(solution)/shard_map/ppermute | solution.py:25
  8.1 8.2 %collective-permute-start.7 = (bf16[272,128]{1,0:T(8,128)(2,1)S(1)}, bf16[272,128]{1,0:T(8,128)(2,1)S(1)}, u32[]{:S(2)}, u32[]{:S(2)}) collective-permute-start(bf16[272,128]{1,0:T(8,128)(2,1)S(1)} %get-tuple-element.41.refs_1_.refs_2_), channel_id=1, source_target_pairs={{0,6},{1,5},{2,4},{3,7},{4,2},{5,1},{6,0},{7,3},{8,14},{9,13},{10,... | collective-permute-start | bytes 208904 | tf_op jit(solution)/shard_map/ppermute | solution.py:272
  10.6 6.2 %collective-permute-start.8 = (bf16[272,128]{1,0:T(8,128)(2,1)S(1)}, bf16[272,128]{1,0:T(8,128)(2,1)S(1)}, u32[]{:S(2)}, u32[]{:S(2)}) collective-permute-start(bf16[272,128]{1,0:T(8,128)(2,1)S(1)} %collective-permute-done.2.refs_2_.refs_3_), channel_id=1, source_target_pairs={{0,6},{1,5},{2,4},{3,7},{4,2},{5,1},{6,0},{7,3},{8,14},{9,13},{10,... | collective-permute-start | bytes 208904 | tf_op jit(solution)/shard_map/ppermute | solution.py:272
  12.6 7.8 %collective-permute-start.5 = (bf16[544,128]{1,0:T(8,128)(2,1)S(1)}, bf16[544,128]{1,0:T(8,128)(2,1)S(1)}, u32[]{:S(2)}, u32[]{:S(2)}) collective-permute-start(bf16[544,128]{1,0:T(8,128)(2,1)S(1)} %slice.7), channel_id=1, source_target_pairs={{0,16},{8,24},{16,0},{24,8},{1,17},{9,25},{17,1},{25,9},{2,18},{10... | collective-permute-start | bytes 417800 | tf_op jit(solution)/shard_map/ppermute | solution.py:25
  14.0 6.4 %collective-permute-start.4 = (bf16[512,128]{1,0:T(8,128)(2,1)S(1)}, bf16[512,128]{1,0:T(8,128)(2,1)S(1)}, u32[]{:S(2)}, u32[]{:S(2)}) collective-permute-start(bf16[512,128]{1,0:T(8,128)(2,1)S(1)} %slice.6), channel_id=1, source_target_pairs={{0,8},{8,0},{16,24},{24,16},{1,9},{9,1},{17,25},{25,17},{2,10},{10... | collective-permute-start | bytes 393224 | tf_op jit(solution)/shard_map/ppermute | solution.py:25
  15.6 2.0 %collective-permute-start.6 = (bf16[272,128]{1,0:T(8,128)(2,1)S(1)}, bf16[272,128]{1,0:T(8,128)(2,1)S(1)}, u32[]{:S(2)}, u32[]{:S(2)}) collective-permute-start(bf16[272,128]{1,0:T(8,128)(2,1)S(1)} %collective-permute-done.3.refs_3_.refs_4_), channel_id=1, source_target_pairs={{0,1},{1,0},{2,3},{3,2},{4,5},{5,4},{6,7},{7,6},{8,9},{9,8},{10,11... | collective-permute-start | bytes 208904 | tf_op jit(solution)/shard_map/ppermute | solution.py:25
  16.8 2.4 %collective-permute-start.10 = (bf16[272,128]{1,0:T(8,128)(2,1)S(1)}, bf16[272,128]{1,0:T(8,128)(2,1)S(1)}, u32[]{:S(2)}, u32[]{:S(2)}) collective-permute-start(bf16[272,128]{1,0:T(8,128)(2,1)S(1)} %collective-permute-done.8.refs_5_.refs_7_), channel_id=1, source_target_pairs={{0,1},{1,0},{2,3},{3,2},{4,5},{5,4},{6,7},{7,6},{8,9},{9,8},{10,11... | collective-permute-start | bytes 208904 | tf_op jit(solution)/shard_map/ppermute | solution.py:25
  17.6 1.6 %collective-permute-start.9 = (bf16[272,128]{1,0:T(8,128)(2,1)S(1)}, bf16[272,128]{1,0:T(8,128)(2,1)S(1)}, u32[]{:S(2)}, u32[]{:S(2)}) collective-permute-start(bf16[272,128]{1,0:T(8,128)(2,1)S(1)} %collective-permute-done.7.refs_4_.refs_6_), channel_id=1, source_target_pairs={{0,1},{1,0},{2,3},{3,2},{4,5},{5,4},{6,7},{7,6},{8,9},{9,8},{10,11... | collective-permute-start | bytes 208904 | tf_op jit(solution)/shard_map/ppermute | solution.py:25
  21.2 2.1 %collective-permute-start.11 = (bf16[4,256,128]{2,1,0:T(8,128)(2,1)S(1)}, bf16[4,256,128]{2,1,0:T(8,128)(2,1)S(1)}, u32[]{:S(2)}, u32[]{:S(2)}) collective-permute-start(bf16[4,256,128]{2,1,0:T(8,128)(2,1)S(1)} %get-tuple-element.62), channel_id=1, source_target_pairs={{0,1},{1,0},{2,3},{3,2},{4,5},{5,4},{6,7},{7,6},{8,9},{9,8},{10,11... | collective-permute-start | bytes 786440 | tf_op jit(solution)/shard_map/ppermute | solution.py:25
  22.6 6.6 %collective-permute-start.13 = (bf16[128,512]{1,0:T(8,128)(2,1)S(1)}, bf16[128,512]{1,0:T(8,128)(2,1)S(1)}, u32[]{:S(2)}, u32[]{:S(2)}) collective-permute-start(bf16[128,512]{1,0:T(8,128)(2,1)S(1)} %get-tuple-element.65), channel_id=1, source_target_pairs={{0,24},{8,16},{16,8},{24,0},{1,25},{9,17},{17,9},{25,1},{2,26},{10... | collective-permute-start | bytes 393224 | tf_op jit(solution)/shard_map/ppermute | solution.py:25
  23.4 7.4 %collective-permute-start.14 = (bf16[256,128]{1,0:T(8,128)(2,1)S(1)}, bf16[256,128]{1,0:T(8,128)(2,1)S(1)}, u32[]{:S(2)}, u32[]{:S(2)}) collective-permute-start(bf16[256,128]{1,0:T(8,128)(2,1)S(1)} %get-tuple-element.67), channel_id=1, source_target_pairs={{0,6},{1,5},{2,4},{3,7},{4,2},{5,1},{6,0},{7,3},{8,14},{9,13},{10,... | collective-permute-start | bytes 196616 | tf_op jit(solution)/shard_map/ppermute | solution.py:272
  27.2 5.4 %collective-permute-start.15 = (bf16[256,128]{1,0:T(8,128)(2,1)S(1)}, bf16[256,128]{1,0:T(8,128)(2,1)S(1)}, u32[]{:S(2)}, u32[]{:S(2)}) collective-permute-start(bf16[256,128]{1,0:T(8,128)(2,1)S(1)} %get-tuple-element.68), channel_id=1, source_target_pairs={{0,4},{1,7},{2,6},{3,5},{4,0},{5,3},{6,2},{7,1},{8,12},{9,15},{10,... | collective-permute-start | bytes 196616 | tf_op jit(solution)/shard_map/ppermute | solution.py:272
  27.2 5.5 %collective-permute-start.16 = (bf16[128,512]{1,0:T(8,128)(2,1)S(1)}, bf16[128,512]{1,0:T(8,128)(2,1)S(1)}, u32[]{:S(2)}, u32[]{:S(2)}) collective-permute-start(bf16[128,512]{1,0:T(8,128)(2,1)S(1)} %get-tuple-element.70), channel_id=1, source_target_pairs={{0,8},{8,0},{16,24},{24,16},{1,9},{9,1},{17,25},{25,17},{2,10},{10... | collective-permute-start | bytes 393224 | tf_op jit(solution)/shard_map/ppermute | solution.py:25
  27.7 5.0 %collective-permute-start.17 = (bf16[128,512]{1,0:T(8,128)(2,1)S(1)}, bf16[128,512]{1,0:T(8,128)(2,1)S(1)}, u32[]{:S(2)}, u32[]{:S(2)}) collective-permute-start(bf16[128,512]{1,0:T(8,128)(2,1)S(1)} %get-tuple-element.71), channel_id=1, source_target_pairs={{0,16},{8,24},{16,0},{24,8},{1,17},{9,25},{17,1},{25,9},{2,18},{10... | collective-permute-start | bytes 393224 | tf_op jit(solution)/shard_map/ppermute | solution.py:25
  29.2 4.3 %collective-permute-start.12 = (bf16[256,128]{1,0:T(8,128)(2,1)S(1)}, bf16[256,128]{1,0:T(8,128)(2,1)S(1)}, u32[]{:S(2)}, u32[]{:S(2)}) collective-permute-start(bf16[256,128]{1,0:T(8,128)(2,1)S(1)} %get-tuple-element.63), channel_id=1, source_target_pairs={{0,2},{1,3},{2,0},{3,1},{4,6},{5,7},{6,4},{7,5},{8,10},{9,11},{10,... | collective-permute-start | bytes 196616 | tf_op jit(solution)/shard_map/ppermute | solution.py:25

commit v20 on v19

--- a/solution.py
+++ b/solution.py
@@ -304,13 +304,11 @@
     dq_own, acc = blocks_call([x], early, range(3), *common, F32, F32, diagonal=True)
 
     xs = [swapped(x, "outer", s) for s in range(1, nq - 1)]
-    dqs = [dq_own]
-    for s in range(nq - 2):
-        xs[s], acc = lax.optimization_barrier((xs[s], acc))
-        dq, acc = blocks_call([xs[s]], early, range(3), *common, F32, F32, acc=[(acc, n) for n in range(3)])
-        dqs.append(dq)
+    *xs, acc = lax.optimization_barrier((*xs, acc))
     halves = [xs[nq - 3][:hr], xs[((nq - 1) ^ (nq // 2)) - 1][hr:]]
     corner = [swapped(halves[0], "outer", 1), swapped(halves[1], "outer", nq // 2)]
+    *dqs, acc = blocks_call(xs, early, range(3), *common, F32, F32, acc=[(acc, n) for n in range(3)])
+    dqs = [dq_own, *dqs]
 
     *direct, acc = lax.optimization_barrier((*direct, acc))
     traded = [swapped(block, "inner", 1) for block in direct]

time: 34.3 us -> 34.4 us (level)
    pallas_call x7 -> x6, Pallas kernels: 6.36 us -> 6.21 us  [blocks_call(): pl.pallas_call(functools.partial(blocks_kernel, plan, rows, heads, scale)...]
  transfers between devices with their start and end apart: 18 -> 18, of which waited for: 3 -> 3; matrix products, arithmetic and copies ran while one was open for 0% -> 0% of each run, Pallas kernels for 19% -> 18%
where the time goes in v20:
time: 34.4 us; the launch traced here: 34.2 us
  starting transfers between devices  21.6 us (63%)
  Pallas kernels  9.08 us (26%)
  waiting for transfers between devices  2.81 us (8%)
  between operations  0.77 us (2%)
    ppermute x14, starting transfers between devices, swapped(): return lax.ppermute(block, axis, pairs)  14.1 us
    ppermute x4, starting transfers between devices, crossed(): return lax.ppermute(block, 'inner', pairs)  7.5 us
    pallas_call x6, Pallas kernels, blocks_call(): pl.pallas_call(functools.partial(blocks_kernel, plan, rows, heads, scale)...  6.21 us
    ppermute x4, waiting for transfers between devices, crossed(): return lax.ppermute(block, 'inner', pairs)  2.44 us
    pallas_call x1, Pallas kernels, on_device(): pl.pallas_call(pack_kernel, out_shape=(sds((2 * hr + 32, width), BF), sds...  1.34 us
    pallas_call x1, Pallas kernels, on_device(): pl.pallas_call(functools.partial(query_kernel, rows, heads, scale), out_s...  0.78 us
  transfers between devices with their start and end apart: 18, of which 3 were waited for; matrix products, arithmetic and copies ran while one was open for 0% of the time, Pallas kernels for 18%

profile of v20, /device:TPU:0, one launch (start us, length us, event | category | flops | bytes accessed | tf_op | source)
XLA Modules:
  0.0 34.2 jit_solution(14522257849587731024)
XLA Ops:
  0.6 1.3 %shard_map.94 = (bf16[1056,128]{1,0:T(8,128)(2,1)S(1)}, bf16[272,128]{1,0:T(8,128)(2,1)S(1)}) custom-call(bf16[128,512]{1,0:T(8,128)(2,1)} %q_ref.1, bf16[128,128]{1,0:T(8,128)(2,1)} %k_ref.1, bf16[128,128]{1,0:T(8,128)(2,1)} %v_ref.1, bf16[128,512]{1,0:T(8,128)(2,1)} %o_ref.1, bf16[128,512]{1,0:T(8,128)(2,1)} %g_ref.1, f32[4,128]{1,0:T(4,128)} %lse_ref.1, ...), custom_call_target="tpu_custom_call" | custom-call | flops 1000 | bytes 1000 | tf_op jit(solution)/shard_map/pallas_call | solution.py:284
  2.0 3.0 %collective-permute-start = (bf16[1056,128]{1,0:T(8,128)(2,1)S(1)}, bf16[1056,128]{1,0:T(8,128)(2,1)S(1)}, u32[]{:S(2)}, u32[]{:S(2)}) collective-permute-start(bf16[1056,128]{1,0:T(8,128)(2,1)S(1)} %get-tuple-element.38.refs_0_), channel_id=1, source_target_pairs={{0,8},{8,0},{16,24},{24,16},{1,9},{9,1},{17,25},{25,17},{2,10},{10... | collective-permute-start | bytes 811016 | tf_op jit(solution)/shard_map/ppermute | solution.py:25
  5.0 1.5 %collective-permute-start.1 = (bf16[1056,128]{1,0:T(8,128)(2,1)S(1)}, bf16[1056,128]{1,0:T(8,128)(2,1)S(1)}, u32[]{:S(2)}, u32[]{:S(2)}) collective-permute-start(bf16[1056,128]{1,0:T(8,128)(2,1)S(1)} %get-tuple-element.38.refs_0_), channel_id=1, source_target_pairs={{0,16},{8,24},{16,0},{24,8},{1,17},{9,25},{17,1},{25,9},{2,18},{10... | collective-permute-start | bytes 811016 | tf_op jit(solution)/shard_map/ppermute | solution.py:25
  6.5 1.6 %collective-permute-start.3 = (bf16[272,128]{1,0:T(8,128)(2,1)S(1)}, bf16[272,128]{1,0:T(8,128)(2,1)S(1)}, u32[]{:S(2)}, u32[]{:S(2)}) collective-permute-start(bf16[272,128]{1,0:T(8,128)(2,1)S(1)} %get-tuple-element.39.refs_1_.refs_2_), channel_id=1, source_target_pairs={{0,2},{1,3},{2,0},{3,1},{4,6},{5,7},{6,4},{7,5},{8,10},{9,11},{10,... | collective-permute-start | bytes 208904 | tf_op jit(solution)/shard_map/ppermute | solution.py:25
  8.1 2.5 %collective-permute-start.7 = (bf16[272,128]{1,0:T(8,128)(2,1)S(1)}, bf16[272,128]{1,0:T(8,128)(2,1)S(1)}, u32[]{:S(2)}, u32[]{:S(2)}) collective-permute-start(bf16[272,128]{1,0:T(8,128)(2,1)S(1)} %get-tuple-element.39.refs_1_.refs_2_), channel_id=1, source_target_pairs={{0,6},{1,5},{2,4},{3,7},{4,2},{5,1},{6,0},{7,3},{8,14},{9,13},{10,... | collective-permute-start | bytes 208904 | tf_op jit(solution)/shard_map/ppermute | solution.py:272
  10.6 1.3 %collective-permute-start.8 = (bf16[272,128]{1,0:T(8,128)(2,1)S(1)}, bf16[272,128]{1,0:T(8,128)(2,1)S(1)}, u32[]{:S(2)}, u32[]{:S(2)}) collective-permute-start(bf16[272,128]{1,0:T(8,128)(2,1)S(1)} %collective-permute-done.2.refs_2_.refs_3_), channel_id=1, source_target_pairs={{0,6},{1,5},{2,4},{3,7},{4,2},{5,1},{6,0},{7,3},{8,14},{9,13},{10,... | collective-permute-start | bytes 208904 | tf_op jit(solution)/shard_map/ppermute | solution.py:272
  11.9 0.7 %shard_map.95 = (f32[128,512]{1,0:T(8,128)S(1)}, f32[3,256,128]{2,1,0:T(8,128)S(1)}) custom-call(bf16[1056,128]{1,0:T(8,128)(2,1)S(1)} %get-tuple-element.38.refs_0_, bf16[272,128]{1,0:T(8,128)(2,1)S(1)} %get-tuple-element.39.refs_1_.refs_2_, bf16[272,128]{1,0:T(8,128)(2,1)S(1)} %collective-permute-done.2.refs_2_.refs_3_, ...), custom_call_target="tpu_custom_call" | custom-call | flops 1000 | bytes 1000 | tf_op jit(solution)/shard_map/pallas_call | solution.py:209
  12.6 0.0 collective-permute-done.refs_0_.refs_1_
  12.6 0.3 collective-permute-done.1.refs_1_.refs_2_
  12.9 1.6 %collective-permute-start.5 = (bf16[544,128]{1,0:T(8,128)(2,1)S(1)}, bf16[544,128]{1,0:T(8,128)(2,1)S(1)}, u32[]{:S(2)}, u32[]{:S(2)}) collective-permute-start(bf16[544,128]{1,0:T(8,128)(2,1)S(1)} %slice.7), channel_id=1, source_target_pairs={{0,16},{8,24},{16,0},{24,8},{1,17},{9,25},{17,1},{25,9},{2,18},{10... | collective-permute-start | bytes 417800 | tf_op jit(solution)/shard_map/ppermute | solution.py:25
  14.5 0.6 %collective-permute-start.4 = (bf16[512,128]{1,0:T(8,128)(2,1)S(1)}, bf16[512,128]{1,0:T(8,128)(2,1)S(1)}, u32[]{:S(2)}, u32[]{:S(2)}) collective-permute-start(bf16[512,128]{1,0:T(8,128)(2,1)S(1)} %slice.6), channel_id=1, source_target_pairs={{0,8},{8,0},{16,24},{24,16},{1,9},{9,1},{17,25},{25,17},{2,10},{10... | collective-permute-start | bytes 393224 | tf_op jit(solution)/shard_map/ppermute | solution.py:25
  15.1 0.0 collective-permute-start.6
  15.1 1.2 %shard_map.96 = (f32[128,512]{1,0:T(8,128)S(1)}, f32[128,512]{1,0:T(8,128)S(1)}, f32[3,256,128]{2,1,0:T(8,128)S(1)}) custom-call(bf16[1056,128]{1,0:T(8,128)(2,1)S(1)} %collective-permute-done.refs_0_.refs_1_, bf16[1056,128]{1,0:T(8,128)(2,1)S(1)} %collective-permute-done.1.refs_1_.refs_2_, bf16[272,128]{1,0:T(8,128)(2,1)S(1)} %get-tuple-element.39.refs_1_.refs_2_, ...), custom_call_target="tpu_custom_call" | custom-call | flops 1000 | bytes 1000 | tf_op jit(solution)/shard_map/pallas_call | solution.py:209
  16.3 0.0 collective-permute-done.7.refs_4_.refs_6_
  16.3 0.4 %collective-permute-done.8.refs_5_.refs_7_ = bf16[272,128]{1,0:T(8,128)(2,1)S(1)} collective-permute-done((bf16[272,128]{1,0:T(8,128)(2,1)S(1)}, bf16[272,128]{1,0:T(8,128)(2,1)S(1)}, u32[]{:S(2)}, u32[]{:S(2)}) %collective-permute-start.8) | collective-permute-done | bytes 69664 | tf_op jit(solution)/shard_map/ppermute | solution.py:272
  16.8 0.8 %collective-permute-start.10 = (bf16[272,128]{1,0:T(8,128)(2,1)S(1)}, bf16[272,128]{1,0:T(8,128)(2,1)S(1)}, u32[]{:S(2)}, u32[]{:S(2)}) collective-permute-start(bf16[272,128]{1,0:T(8,128)(2,1)S(1)} %collective-permute-done.8.refs_5_.refs_7_), channel_id=1, source_target_pairs={{0,1},{1,0},{2,3},{3,2},{4,5},{5,4},{6,7},{7,6},{8,9},{9,8},{10,11... | collective-permute-start | bytes 208904 | tf_op jit(solution)/shard_map/ppermute | solution.py:25
  17.6 0.0 collective-permute-start.9
  17.6 0.0 collective-permute-done.6.refs_3_.refs_5_
  17.6 1.6 %shard_map.97 = (f32[128,512]{1,0:T(8,128)S(1)}, f32[128,512]{1,0:T(8,128)S(1)}, f32[128,512]{1,0:T(8,128)S(1)}, f32[3,256,128]{2,1,0:T(8,128)S(1)}) custom-call(bf16[1056,128]{1,0:T(8,128)(2,1)S(1)} %get-tuple-element.38.refs_0_, bf16[1056,128]{1,0:T(8,128)(2,1)S(1)} %collective-permute-done.refs_0_.refs_1_, ...), custom_call_target="tpu_custom_call" | custom-call | flops 1000 | bytes 1000 | tf_op jit(solution)/shard_map/pallas_call | solution.py:209
  19.2 1.1 %shard_map.98 = (f32[128,512]{1,0:T(8,128)S(1)}, bf16[128,512]{1,0:T(8,128)(2,1)S(1)}, bf16[128,512]{1,0:T(8,128)(2,1)S(1)}, f32[2,256,128]{2,1,0:T(8,128)S(1)}) custom-call(bf16[1056,128]{1,0:T(8,128)(2,1)S(1)} %get-tuple-element.38.refs_0_, bf16[1056,128]{1,0:T(8,128)(2,1)S(1)} %collective-permute-done.refs_0_.refs_1_, ...), custom_call_target="tpu_custom_call" | custom-call | flops 1000 | bytes 1000 | tf_op jit(solution)/shard_map/pallas_call | solution.py:209
  20.4 0.8 %shard_map.99 = (f32[128,512]{1,0:T(8,128)S(1)}, bf16[4,256,128]{2,1,0:T(8,128)(2,1)S(1)}) custom-call(bf16[512,128]{1,0:T(8,128)(2,1)S(1)} %collective-permute-done.4.refs_0_, bf16[544,128]{1,0:T(8,128)(2,1)S(1)} %collective-permute-done.5.refs_1_, bf16[272,128]{1,0:T(8,128)(2,1)S(1)} %get-tuple-element.39.refs_1_.refs_2_, ...), custom_call_target="tpu_custom_call" | custom-call | flops 1000 | bytes 1000 | tf_op jit(solution)/shard_map/pallas_call | solution.py:209
  21.2 0.6 %collective-permute-start.11 = (bf16[4,256,128]{2,1,0:T(8,128)(2,1)S(1)}, bf16[4,256,128]{2,1,0:T(8,128)(2,1)S(1)}, u32[]{:S(2)}, u32[]{:S(2)}) collective-permute-start(bf16[4,256,128]{2,1,0:T(8,128)(2,1)S(1)} %get-tuple-element.58), channel_id=1, source_target_pairs={{0,1},{1,0},{2,3},{3,2},{4,5},{5,4},{6,7},{7,6},{8,9},{9,8},{10,11... | collective-permute-start | bytes 786440 | tf_op jit(solution)/shard_map/ppermute | solution.py:25
  21.8 0.8 %shard_map.100 = (bf16[128,512]{1,0:T(8,128)(2,1)S(1)}, f32[4,256,128]{2,1,0:T(8,128)S(1)}) custom-call(bf16[512,128]{1,0:T(8,128)(2,1)S(1)} %collective-permute-done.4.refs_0_, bf16[544,128]{1,0:T(8,128)(2,1)S(1)} %collective-permute-done.5.refs_1_, bf16[272,128]{1,0:T(8,128)(2,1)S(1)} %get-tuple-element.39.refs_1_.refs_2_, ...), custom_call_target="tpu_custom_call" | custom-call | flops 1000 | bytes 1000 | tf_op jit(solution)/shard_map/pallas_call | solution.py:209
  22.6 0.8 %collective-permute-start.13 = (bf16[128,512]{1,0:T(8,128)(2,1)S(1)}, bf16[128,512]{1,0:T(8,128)(2,1)S(1)}, u32[]{:S(2)}, u32[]{:S(2)}) collective-permute-start(bf16[128,512]{1,0:T(8,128)(2,1)S(1)} %get-tuple-element.61), channel_id=1, source_target_pairs={{0,24},{8,16},{16,8},{24,0},{1,25},{9,17},{17,9},{25,1},{2,26},{10... | collective-permute-start | bytes 393224 | tf_op jit(solution)/shard_map/ppermute | solution.py:25
  23.4 0.1 shard_map.101
  23.5 3.7 %collective-permute-start.14 = (bf16[256,128]{1,0:T(8,128)(2,1)S(1)}, bf16[256,128]{1,0:T(8,128)(2,1)S(1)}, u32[]{:S(2)}, u32[]{:S(2)}) collective-permute-start(bf16[256,128]{1,0:T(8,128)(2,1)S(1)} %get-tuple-element.63), channel_id=1, source_target_pairs={{0,6},{1,5},{2,4},{3,7},{4,2},{5,1},{6,0},{7,3},{8,14},{9,13},{10,... | collective-permute-start | bytes 196616 | tf_op jit(solution)/shard_map/ppermute | solution.py:272
  27.2 0.5 %collective-permute-start.16 = (bf16[128,512]{1,0:T(8,128)(2,1)S(1)}, bf16[128,512]{1,0:T(8,128)(2,1)S(1)}, u32[]{:S(2)}, u32[]{:S(2)}) collective-permute-start(bf16[128,512]{1,0:T(8,128)(2,1)S(1)} %get-tuple-element.66), channel_id=1, source_target_pairs={{0,8},{8,0},{16,24},{24,16},{1,9},{9,1},{17,25},{25,17},{2,10},{10... | collective-permute-start | bytes 393224 | tf_op jit(solution)/shard_map/ppermute | solution.py:25
  27.7 1.5 %collective-permute-start.17 = (bf16[128,512]{1,0:T(8,128)(2,1)S(1)}, bf16[128,512]{1,0:T(8,128)(2,1)S(1)}, u32[]{:S(2)}, u32[]{:S(2)}) collective-permute-start(bf16[128,512]{1,0:T(8,128)(2,1)S(1)} %get-tuple-element.67), channel_id=1, source_target_pairs={{0,16},{8,24},{16,0},{24,8},{1,17},{9,25},{17,1},{25,9},{2,18},{10... | collective-permute-start | bytes 393224 | tf_op jit(solution)/shard_map/ppermute | solution.py:25
  29.3 1.5 %collective-permute-start.12 = (bf16[256,128]{1,0:T(8,128)(2,1)S(1)}, bf16[256,128]{1,0:T(8,128)(2,1)S(1)}, u32[]{:S(2)}, u32[]{:S(2)}) collective-permute-start(bf16[256,128]{1,0:T(8,128)(2,1)S(1)} %get-tuple-element.59), channel_id=1, source_target_pairs={{0,2},{1,3},{2,0},{3,1},{4,6},{5,7},{6,4},{7,5},{8,10},{9,11},{10,... | collective-permute-start | bytes 196616 | tf_op jit(solution)/shard_map/ppermute | solution.py:25
  30.8 2.0 %collective-permute-done.15.refs_1_ = bf16[256,128]{1,0:T(8,128)(2,1)S(1)} collective-permute-done((bf16[256,128]{1,0:T(8,128)(2,1)S(1)}, bf16[256,128]{1,0:T(8,128)(2,1)S(1)}, u32[]{:S(2)}, u32[]{:S(2)}) %collective-permute-start.15) | collective-permute-done | bytes 65568 | tf_op jit(solution)/shard_map/ppermute | solution.py:272
  32.8 0.8 %shard_map.104 = bf16[128,512]{1,0:T(8,128)(2,1)} custom-call(f32[128,512]{1,0:T(8,128)S(1)} %shard_map.102.dq_ref, bf16[128,512]{1,0:T(8,128)(2,1)S(1)} %collective-permute-done.16.refs_0_, bf16[128,512]{1,0:T(8,128)(2,1)S(1)} %collective-permute-done.17.refs_1_), custom_call_target="tpu_custom_call" | custom-call | flops 1000 | bytes 1000 | tf_op jit(solution)/shard_map/pallas_call | solution.py:343
  33.6 0.6 %shard_map.105 = (bf16[128,128]{1,0:T(8,128)(2,1)}, bf16[128,128]{1,0:T(8,128)(2,1)}) custom-call(f32[256,128]{1,0:T(8,128)S(1)} %shard_map.103.dkv_ref, bf16[256,128]{1,0:T(8,128)(2,1)S(1)} %collective-permute-done.12.near_ref), custom_call_target="tpu_custom_call" | custom-call | flops 1000 | bytes 1000 | tf_op jit(solution)/shard_map/pallas_call | solution.py:352
  (18 shorter events, 0.1 us)
Async XLA Ops:
  2.0 10.6 %collective-permute-start = (bf16[1056,128]{1,0:T(8,128)(2,1)S(1)}, bf16[1056,128]{1,0:T(8,128)(2,1)S(1)}, u32[]{:S(2)}, u32[]{:S(2)}) collective-permute-start(bf16[1056,128]{1,0:T(8,128)(2,1)S(1)} %get-tuple-element.38.refs_0_), channel_id=1, source_target_pairs={{0,8},{8,0},{16,24},{24,16},{1,9},{9,1},{17,25},{25,17},{2,10},{10... | collective-permute-start | bytes 811016 | tf_op jit(solution)/shard_map/ppermute | solution.py:25
  5.0 7.9 %collective-permute-start.1 = (bf16[1056,128]{1,0:T(8,128)(2,1)S(1)}, bf16[1056,128]{1,0:T(8,128)(2,1)S(1)}, u32[]{:S(2)}, u32[]{:S(2)}) collective-permute-start(bf16[1056,128]{1,0:T(8,128)(2,1)S(1)} %get-tuple-element.38.refs_0_), channel_id=1, source_target_pairs={{0,16},{8,24},{16,0},{24,8},{1,17},{9,25},{17,1},{25,9},{2,18},{10... | collective-permute-start | bytes 811016 | tf_op jit(solution)/shard_map/ppermute | solution.py:25
  6.5 4.1 %collective-permute-start.2 = (bf16[272,128]{1,0:T(8,128)(2,1)S(1)}, bf16[272,128]{1,0:T(8,128)(2,1)S(1)}, u32[]{:S(2)}, u32[]{:S(2)}) collective-permute-start(bf16[272,128]{1,0:T(8,128)(2,1)S(1)} %get-tuple-element.39.refs_1_.refs_2_), channel_id=1, source_target_pairs={{0,1},{1,0},{2,3},{3,2},{4,5},{5,4},{6,7},{7,6},{8,9},{9,8},{10,11... | collective-permute-start | bytes 208904 | tf_op jit(solution)/shard_map/ppermute | solution.py:25
  6.5 5.4 %collective-permute-start.3 = (bf16[272,128]{1,0:T(8,128)(2,1)S(1)}, bf16[272,128]{1,0:T(8,128)(2,1)S(1)}, u32[]{:S(2)}, u32[]{:S(2)}) collective-permute-start(bf16[272,128]{1,0:T(8,128)(2,1)S(1)} %get-tuple-element.39.refs_1_.refs_2_), channel_id=1, source_target_pairs={{0,2},{1,3},{2,0},{3,1},{4,6},{5,7},{6,4},{7,5},{8,10},{9,11},{10,... | collective-permute-start | bytes 208904 | tf_op jit(solution)/shard_map/ppermute | solution.py:25
  8.1 8.2 %collective-permute-start.7 = (bf16[272,128]{1,0:T(8,128)(2,1)S(1)}, bf16[272,128]{1,0:T(8,128)(2,1)S(1)}, u32[]{:S(2)}, u32[]{:S(2)}) collective-permute-start(bf16[272,128]{1,0:T(8,128)(2,1)S(1)} %get-tuple-element.39.refs_1_.refs_2_), channel_id=1, source_target_pairs={{0,6},{1,5},{2,4},{3,7},{4,2},{5,1},{6,0},{7,3},{8,14},{9,13},{10,... | collective-permute-start | bytes 208904 | tf_op jit(solution)/shard_map/ppermute | solution.py:272
  10.6 6.2 %collective-permute-start.8 = (bf16[272,128]{1,0:T(8,128)(2,1)S(1)}, bf16[272,128]{1,0:T(8,128)(2,1)S(1)}, u32[]{:S(2)}, u32[]{:S(2)}) collective-permute-start(bf16[272,128]{1,0:T(8,128)(2,1)S(1)} %collective-permute-done.2.refs_2_.refs_3_), channel_id=1, source_target_pairs={{0,6},{1,5},{2,4},{3,7},{4,2},{5,1},{6,0},{7,3},{8,14},{9,13},{10,... | collective-permute-start | bytes 208904 | tf_op jit(solution)/shard_map/ppermute | solution.py:272
  12.9 7.4 %collective-permute-start.5 = (bf16[544,128]{1,0:T(8,128)(2,1)S(1)}, bf16[544,128]{1,0:T(8,128)(2,1)S(1)}, u32[]{:S(2)}, u32[]{:S(2)}) collective-permute-start(bf16[544,128]{1,0:T(8,128)(2,1)S(1)} %slice.7), channel_id=1, source_target_pairs={{0,16},{8,24},{16,0},{24,8},{1,17},{9,25},{17,1},{25,9},{2,18},{10... | collective-permute-start | bytes 417800 | tf_op jit(solution)/shard_map/ppermute | solution.py:25
  14.5 5.8 %collective-permute-start.4 = (bf16[512,128]{1,0:T(8,128)(2,1)S(1)}, bf16[512,128]{1,0:T(8,128)(2,1)S(1)}, u32[]{:S(2)}, u32[]{:S(2)}) collective-permute-start(bf16[512,128]{1,0:T(8,128)(2,1)S(1)} %slice.6), channel_id=1, source_target_pairs={{0,8},{8,0},{16,24},{24,16},{1,9},{9,1},{17,25},{25,17},{2,10},{10... | collective-permute-start | bytes 393224 | tf_op jit(solution)/shard_map/ppermute | solution.py:25
  15.1 2.5 %collective-permute-start.6 = (bf16[272,128]{1,0:T(8,128)(2,1)S(1)}, bf16[272,128]{1,0:T(8,128)(2,1)S(1)}, u32[]{:S(2)}, u32[]{:S(2)}) collective-permute-start(bf16[272,128]{1,0:T(8,128)(2,1)S(1)} %collective-permute-done.3.refs_3_.refs_4_), channel_id=1, source_target_pairs={{0,1},{1,0},{2,3},{3,2},{4,5},{5,4},{6,7},{7,6},{8,9},{9,8},{10,11... | collective-permute-start | bytes 208904 | tf_op jit(solution)/shard_map/ppermute | solution.py:25
  16.8 2.4 %collective-permute-start.10 = (bf16[272,128]{1,0:T(8,128)(2,1)S(1)}, bf16[272,128]{1,0:T(8,128)(2,1)S(1)}, u32[]{:S(2)}, u32[]{:S(2)}) collective-permute-start(bf16[272,128]{1,0:T(8,128)(2,1)S(1)} %collective-permute-done.8.refs_5_.refs_7_), channel_id=1, source_target_pairs={{0,1},{1,0},{2,3},{3,2},{4,5},{5,4},{6,7},{7,6},{8,9},{9,8},{10,11... | collective-permute-start | bytes 208904 | tf_op jit(solution)/shard_map/ppermute | solution.py:25
  17.6 1.6 %collective-permute-start.9 = (bf16[272,128]{1,0:T(8,128)(2,1)S(1)}, bf16[272,128]{1,0:T(8,128)(2,1)S(1)}, u32[]{:S(2)}, u32[]{:S(2)}) collective-permute-start(bf16[272,128]{1,0:T(8,128)(2,1)S(1)} %collective-permute-done.7.refs_4_.refs_6_), channel_id=1, source_target_pairs={{0,1},{1,0},{2,3},{3,2},{4,5},{5,4},{6,7},{7,6},{8,9},{9,8},{10,11... | collective-permute-start | bytes 208904 | tf_op jit(solution)/shard_map/ppermute | solution.py:25
  21.2 2.2 %collective-permute-start.11 = (bf16[4,256,128]{2,1,0:T(8,128)(2,1)S(1)}, bf16[4,256,128]{2,1,0:T(8,128)(2,1)S(1)}, u32[]{:S(2)}, u32[]{:S(2)}) collective-permute-start(bf16[4,256,128]{2,1,0:T(8,128)(2,1)S(1)} %get-tuple-element.58), channel_id=1, source_target_pairs={{0,1},{1,0},{2,3},{3,2},{4,5},{5,4},{6,7},{7,6},{8,9},{9,8},{10,11... | collective-permute-start | bytes 786440 | tf_op jit(solution)/shard_map/ppermute | solution.py:25
  22.6 6.6 %collective-permute-start.13 = (bf16[128,512]{1,0:T(8,128)(2,1)S(1)}, bf16[128,512]{1,0:T(8,128)(2,1)S(1)}, u32[]{:S(2)}, u32[]{:S(2)}) collective-permute-start(bf16[128,512]{1,0:T(8,128)(2,1)S(1)} %get-tuple-element.61), channel_id=1, source_target_pairs={{0,24},{8,16},{16,8},{24,0},{1,25},{9,17},{17,9},{25,1},{2,26},{10... | collective-permute-start | bytes 393224 | tf_op jit(solution)/shard_map/ppermute | solution.py:25
  23.5 7.3 %collective-permute-start.14 = (bf16[256,128]{1,0:T(8,128)(2,1)S(1)}, bf16[256,128]{1,0:T(8,128)(2,1)S(1)}, u32[]{:S(2)}, u32[]{:S(2)}) collective-permute-start(bf16[256,128]{1,0:T(8,128)(2,1)S(1)} %get-tuple-element.63), channel_id=1, source_target_pairs={{0,6},{1,5},{2,4},{3,7},{4,2},{5,1},{6,0},{7,3},{8,14},{9,13},{10,... | collective-permute-start | bytes 196616 | tf_op jit(solution)/shard_map/ppermute | solution.py:272
  27.2 5.6 %collective-permute-start.15 = (bf16[256,128]{1,0:T(8,128)(2,1)S(1)}, bf16[256,128]{1,0:T(8,128)(2,1)S(1)}, u32[]{:S(2)}, u32[]{:S(2)}) collective-permute-start(bf16[256,128]{1,0:T(8,128)(2,1)S(1)} %get-tuple-element.64), channel_id=1, source_target_pairs={{0,4},{1,7},{2,6},{3,5},{4,0},{5,3},{6,2},{7,1},{8,12},{9,15},{10,... | collective-permute-start | bytes 196616 | tf_op jit(solution)/shard_map/ppermute | solution.py:272
  27.2 5.6 %collective-permute-start.16 = (bf16[128,512]{1,0:T(8,128)(2,1)S(1)}, bf16[128,512]{1,0:T(8,128)(2,1)S(1)}, u32[]{:S(2)}, u32[]{:S(2)}) collective-permute-start(bf16[128,512]{1,0:T(8,128)(2,1)S(1)} %get-tuple-element.66), channel_id=1, source_target_pairs={{0,8},{8,0},{16,24},{24,16},{1,9},{9,1},{17,25},{25,17},{2,10},{10... | collective-permute-start | bytes 393224 | tf_op jit(solution)/shard_map/ppermute | solution.py:25
  27.7 5.1 %collective-permute-start.17 = (bf16[128,512]{1,0:T(8,128)(2,1)S(1)}, bf16[128,512]{1,0:T(8,128)(2,1)S(1)}, u32[]{:S(2)}, u32[]{:S(2)}) collective-permute-start(bf16[128,512]{1,0:T(8,128)(2,1)S(1)} %get-tuple-element.67), channel_id=1, source_target_pairs={{0,16},{8,24},{16,0},{24,8},{1,17},{9,25},{17,1},{25,9},{2,18},{10... | collective-permute-start | bytes 393224 | tf_op jit(solution)/shard_map/ppermute | solution.py:25
  29.3 4.3 %collective-permute-start.12 = (bf16[256,128]{1,0:T(8,128)(2,1)S(1)}, bf16[256,128]{1,0:T(8,128)(2,1)S(1)}, u32[]{:S(2)}, u32[]{:S(2)}) collective-permute-start(bf16[256,128]{1,0:T(8,128)(2,1)S(1)} %get-tuple-element.59), channel_id=1, source_target_pairs={{0,2},{1,3},{2,0},{3,1},{4,6},{5,7},{6,4},{7,5},{8,10},{9,11},{10,... | collective-permute-start | bytes 196616 | tf_op jit(solution)/shard_map/ppermute | solution.py:25

commit v21 on v20

--- a/solution.py
+++ b/solution.py
@@ -251,12 +251,19 @@
 
 
 def query_kernel(rows, heads, scale, dq_ref, *refs):
-    dq = dq_ref[...]
-    for ref in refs[:-1]:
-        dq = dq + ref[...].astype(F32)
+    dq_refs, (gq_ref, part_s, sems) = refs[:-3], refs[-3:]
+    copies = []
     for h in range(heads):
-        part = dq[:, h * rows : (h + 1) * rows]
-        refs[-1][:, h * 128 : (h + 1) * 128] = (scale * part).T.astype(BF)
+        at = slice(h * rows, (h + 1) * rows)
+        dq = dq_ref[:, at]
+        for ref in dq_refs:
+            dq = dq + ref[:, at].astype(F32)
+        part_s[h] = (scale * dq).T.astype(BF)
+        width = part_s.shape[2]
+        copies.append(pltpu.make_async_copy(part_s.at[h], gq_ref.at[:, pl.ds(h * width, width)], sems.at[h]))
+        copies[-1].start()
+    for copy in copies:
+        copy.wait()
 
 
 def key_kernel(rows, scale, dkv_ref, near_ref, gk_ref, gv_ref):
@@ -344,7 +351,8 @@
         functools.partial(query_kernel, rows, heads, scale),
         out_shape=sds((rows, heads * width), BF),
         in_specs=[VMEM] * (1 + len(got)),
-        out_specs=VMEM,
+        out_specs=pl.BlockSpec(memory_space=pltpu.HBM),
+        scratch_shapes=[pltpu.VMEM((heads, rows, width), BF), pltpu.SemaphoreType.DMA((heads,))],
         compiler_params=SMALL,
         cost_estimate=QUICK,
     )(dq_sum, *got)

time: 34.4 us -> 34.5 us (level)
  no operation moved by 1% of the time
where the time goes in v21:
time: 34.5 us; the launch traced here: 34.3 us
  starting transfers between devices  21.6 us (63%)
  Pallas kernels  9.11 us (26%)
  waiting for transfers between devices  2.81 us (8%)
  between operations  0.79 us (2%)
    ppermute x14, starting transfers between devices, swapped(): return lax.ppermute(block, axis, pairs)  14.1 us
    ppermute x4, starting transfers between devices, crossed(): return lax.ppermute(block, 'inner', pairs)  7.5 us
    pallas_call x6, Pallas kernels, blocks_call(): pl.pallas_call(functools.partial(blocks_kernel, plan, rows, heads, scale)...  6.21 us
    ppermute x4, waiting for transfers between devices, crossed(): return lax.ppermute(block, 'inner', pairs)  2.44 us
    pallas_call x1, Pallas kernels, on_device(): pl.pallas_call(pack_kernel, out_shape=(sds((2 * hr + 32, width), BF), sds...  1.34 us
    pallas_call x1, Pallas kernels, on_device(): pl.pallas_call(functools.partial(query_kernel, rows, heads, scale), out_s...  0.8 us
  transfers between devices with their start and end apart: 18, of which 3 were waited for; matrix products, arithmetic and copies ran while one was open for 0% of the time, Pallas kernels for 18%

profile of v21, /device:TPU:0, one launch (start us, length us, event | category | flops | bytes accessed | tf_op | source)
XLA Modules:
  0.0 34.3 jit_solution(8012977841696239962)
XLA Ops:
  0.6 1.3 %shard_map.94 = (bf16[1056,128]{1,0:T(8,128)(2,1)S(1)}, bf16[272,128]{1,0:T(8,128)(2,1)S(1)}) custom-call(bf16[128,512]{1,0:T(8,128)(2,1)} %q_ref.1, bf16[128,128]{1,0:T(8,128)(2,1)} %k_ref.1, bf16[128,128]{1,0:T(8,128)(2,1)} %v_ref.1, bf16[128,512]{1,0:T(8,128)(2,1)} %o_ref.1, bf16[128,512]{1,0:T(8,128)(2,1)} %g_ref.1, f32[4,128]{1,0:T(4,128)} %lse_ref.1, ...), custom_call_target="tpu_custom_call" | custom-call | flops 1000 | bytes 1000 | tf_op jit(solution)/shard_map/pallas_call | solution.py:291
  2.0 3.0 %collective-permute-start = (bf16[1056,128]{1,0:T(8,128)(2,1)S(1)}, bf16[1056,128]{1,0:T(8,128)(2,1)S(1)}, u32[]{:S(2)}, u32[]{:S(2)}) collective-permute-start(bf16[1056,128]{1,0:T(8,128)(2,1)S(1)} %get-tuple-element.38.refs_0_), channel_id=1, source_target_pairs={{0,8},{8,0},{16,24},{24,16},{1,9},{9,1},{17,25},{25,17},{2,10},{10... | collective-permute-start | bytes 811016 | tf_op jit(solution)/shard_map/ppermute | solution.py:25
  5.0 1.5 %collective-permute-start.1 = (bf16[1056,128]{1,0:T(8,128)(2,1)S(1)}, bf16[1056,128]{1,0:T(8,128)(2,1)S(1)}, u32[]{:S(2)}, u32[]{:S(2)}) collective-permute-start(bf16[1056,128]{1,0:T(8,128)(2,1)S(1)} %get-tuple-element.38.refs_0_), channel_id=1, source_target_pairs={{0,16},{8,24},{16,0},{24,8},{1,17},{9,25},{17,1},{25,9},{2,18},{10... | collective-permute-start | bytes 811016 | tf_op jit(solution)/shard_map/ppermute | solution.py:25
  6.5 1.6 %collective-permute-start.3 = (bf16[272,128]{1,0:T(8,128)(2,1)S(1)}, bf16[272,128]{1,0:T(8,128)(2,1)S(1)}, u32[]{:S(2)}, u32[]{:S(2)}) collective-permute-start(bf16[272,128]{1,0:T(8,128)(2,1)S(1)} %get-tuple-element.39.refs_1_.refs_2_), channel_id=1, source_target_pairs={{0,2},{1,3},{2,0},{3,1},{4,6},{5,7},{6,4},{7,5},{8,10},{9,11},{10,... | collective-permute-start | bytes 208904 | tf_op jit(solution)/shard_map/ppermute | solution.py:25
  8.1 2.5 %collective-permute-start.7 = (bf16[272,128]{1,0:T(8,128)(2,1)S(1)}, bf16[272,128]{1,0:T(8,128)(2,1)S(1)}, u32[]{:S(2)}, u32[]{:S(2)}) collective-permute-start(bf16[272,128]{1,0:T(8,128)(2,1)S(1)} %get-tuple-element.39.refs_1_.refs_2_), channel_id=1, source_target_pairs={{0,6},{1,5},{2,4},{3,7},{4,2},{5,1},{6,0},{7,3},{8,14},{9,13},{10,... | collective-permute-start | bytes 208904 | tf_op jit(solution)/shard_map/ppermute | solution.py:279
  10.6 0.0 collective-permute-done.2.refs_2_.refs_3_
  10.6 1.3 %collective-permute-start.8 = (bf16[272,128]{1,0:T(8,128)(2,1)S(1)}, bf16[272,128]{1,0:T(8,128)(2,1)S(1)}, u32[]{:S(2)}, u32[]{:S(2)}) collective-permute-start(bf16[272,128]{1,0:T(8,128)(2,1)S(1)} %collective-permute-done.2.refs_2_.refs_3_), channel_id=1, source_target_pairs={{0,6},{1,5},{2,4},{3,7},{4,2},{5,1},{6,0},{7,3},{8,14},{9,13},{10,... | collective-permute-start | bytes 208904 | tf_op jit(solution)/shard_map/ppermute | solution.py:279
  11.9 0.7 %shard_map.95 = (f32[128,512]{1,0:T(8,128)S(1)}, f32[3,256,128]{2,1,0:T(8,128)S(1)}) custom-call(bf16[1056,128]{1,0:T(8,128)(2,1)S(1)} %get-tuple-element.38.refs_0_, bf16[272,128]{1,0:T(8,128)(2,1)S(1)} %get-tuple-element.39.refs_1_.refs_2_, bf16[272,128]{1,0:T(8,128)(2,1)S(1)} %collective-permute-done.2.refs_2_.refs_3_, ...), custom_call_target="tpu_custom_call" | custom-call | flops 1000 | bytes 1000 | tf_op jit(solution)/shard_map/pallas_call | solution.py:209
  12.6 0.0 collective-permute-done.refs_0_.refs_1_
  12.6 0.3 collective-permute-done.1.refs_1_.refs_2_
  12.9 1.6 %collective-permute-start.5 = (bf16[544,128]{1,0:T(8,128)(2,1)S(1)}, bf16[544,128]{1,0:T(8,128)(2,1)S(1)}, u32[]{:S(2)}, u32[]{:S(2)}) collective-permute-start(bf16[544,128]{1,0:T(8,128)(2,1)S(1)} %slice.7), channel_id=1, source_target_pairs={{0,16},{8,24},{16,0},{24,8},{1,17},{9,25},{17,1},{25,9},{2,18},{10... | collective-permute-start | bytes 417800 | tf_op jit(solution)/shard_map/ppermute | solution.py:25
  14.5 0.6 %collective-permute-start.4 = (bf16[512,128]{1,0:T(8,128)(2,1)S(1)}, bf16[512,128]{1,0:T(8,128)(2,1)S(1)}, u32[]{:S(2)}, u32[]{:S(2)}) collective-permute-start(bf16[512,128]{1,0:T(8,128)(2,1)S(1)} %slice.6), channel_id=1, source_target_pairs={{0,8},{8,0},{16,24},{24,16},{1,9},{9,1},{17,25},{25,17},{2,10},{10... | collective-permute-start | bytes 393224 | tf_op jit(solution)/shard_map/ppermute | solution.py:25
  15.1 0.0 collective-permute-start.6
  15.1 1.2 %shard_map.96 = (f32[128,512]{1,0:T(8,128)S(1)}, f32[128,512]{1,0:T(8,128)S(1)}, f32[3,256,128]{2,1,0:T(8,128)S(1)}) custom-call(bf16[1056,128]{1,0:T(8,128)(2,1)S(1)} %collective-permute-done.refs_0_.refs_1_, bf16[1056,128]{1,0:T(8,128)(2,1)S(1)} %collective-permute-done.1.refs_1_.refs_2_, bf16[272,128]{1,0:T(8,128)(2,1)S(1)} %get-tuple-element.39.refs_1_.refs_2_, ...), custom_call_target="tpu_custom_call" | custom-call | flops 1000 | bytes 1000 | tf_op jit(solution)/shard_map/pallas_call | solution.py:209
  16.3 0.0 collective-permute-done.7.refs_4_.refs_6_
  16.3 0.4 %collective-permute-done.8.refs_5_.refs_7_ = bf16[272,128]{1,0:T(8,128)(2,1)S(1)} collective-permute-done((bf16[272,128]{1,0:T(8,128)(2,1)S(1)}, bf16[272,128]{1,0:T(8,128)(2,1)S(1)}, u32[]{:S(2)}, u32[]{:S(2)}) %collective-permute-start.8) | collective-permute-done | bytes 69664 | tf_op jit(solution)/shard_map/ppermute | solution.py:279
  16.8 0.8 %collective-permute-start.10 = (bf16[272,128]{1,0:T(8,128)(2,1)S(1)}, bf16[272,128]{1,0:T(8,128)(2,1)S(1)}, u32[]{:S(2)}, u32[]{:S(2)}) collective-permute-start(bf16[272,128]{1,0:T(8,128)(2,1)S(1)} %collective-permute-done.8.refs_5_.refs_7_), channel_id=1, source_target_pairs={{0,1},{1,0},{2,3},{3,2},{4,5},{5,4},{6,7},{7,6},{8,9},{9,8},{10,11... | collective-permute-start | bytes 208904 | tf_op jit(solution)/shard_map/ppermute | solution.py:25
  17.6 0.0 collective-permute-start.9
  17.6 1.6 %shard_map.97 = (f32[128,512]{1,0:T(8,128)S(1)}, f32[128,512]{1,0:T(8,128)S(1)}, f32[128,512]{1,0:T(8,128)S(1)}, f32[3,256,128]{2,1,0:T(8,128)S(1)}) custom-call(bf16[1056,128]{1,0:T(8,128)(2,1)S(1)} %get-tuple-element.38.refs_0_, bf16[1056,128]{1,0:T(8,128)(2,1)S(1)} %collective-permute-done.refs_0_.refs_1_, ...), custom_call_target="tpu_custom_call" | custom-call | flops 1000 | bytes 1000 | tf_op jit(solution)/shard_map/pallas_call | solution.py:209
  19.2 1.1 %shard_map.98 = (f32[128,512]{1,0:T(8,128)S(1)}, bf16[128,512]{1,0:T(8,128)(2,1)S(1)}, bf16[128,512]{1,0:T(8,128)(2,1)S(1)}, f32[2,256,128]{2,1,0:T(8,128)S(1)}) custom-call(bf16[1056,128]{1,0:T(8,128)(2,1)S(1)} %get-tuple-element.38.refs_0_, bf16[1056,128]{1,0:T(8,128)(2,1)S(1)} %collective-permute-done.refs_0_.refs_1_, ...), custom_call_target="tpu_custom_call" | custom-call | flops 1000 | bytes 1000 | tf_op jit(solution)/shard_map/pallas_call | solution.py:209
  20.4 0.8 %shard_map.99 = (f32[128,512]{1,0:T(8,128)S(1)}, bf16[4,256,128]{2,1,0:T(8,128)(2,1)S(1)}) custom-call(bf16[512,128]{1,0:T(8,128)(2,1)S(1)} %collective-permute-done.4.refs_0_, bf16[544,128]{1,0:T(8,128)(2,1)S(1)} %collective-permute-done.5.refs_1_, bf16[272,128]{1,0:T(8,128)(2,1)S(1)} %get-tuple-element.39.refs_1_.refs_2_, ...), custom_call_target="tpu_custom_call" | custom-call | flops 1000 | bytes 1000 | tf_op jit(solution)/shard_map/pallas_call | solution.py:209
  21.2 0.6 %collective-permute-start.11 = (bf16[4,256,128]{2,1,0:T(8,128)(2,1)S(1)}, bf16[4,256,128]{2,1,0:T(8,128)(2,1)S(1)}, u32[]{:S(2)}, u32[]{:S(2)}) collective-permute-start(bf16[4,256,128]{2,1,0:T(8,128)(2,1)S(1)} %get-tuple-element.58), channel_id=1, source_target_pairs={{0,1},{1,0},{2,3},{3,2},{4,5},{5,4},{6,7},{7,6},{8,9},{9,8},{10,11... | collective-permute-start | bytes 786440 | tf_op jit(solution)/shard_map/ppermute | solution.py:25
  21.8 0.8 %shard_map.100 = (bf16[128,512]{1,0:T(8,128)(2,1)S(1)}, f32[4,256,128]{2,1,0:T(8,128)S(1)}) custom-call(bf16[512,128]{1,0:T(8,128)(2,1)S(1)} %collective-permute-done.4.refs_0_, bf16[544,128]{1,0:T(8,128)(2,1)S(1)} %collective-permute-done.5.refs_1_, bf16[272,128]{1,0:T(8,128)(2,1)S(1)} %get-tuple-element.39.refs_1_.refs_2_, ...), custom_call_target="tpu_custom_call" | custom-call | flops 1000 | bytes 1000 | tf_op jit(solution)/shard_map/pallas_call | solution.py:209
  22.6 0.8 %collective-permute-start.13 = (bf16[128,512]{1,0:T(8,128)(2,1)S(1)}, bf16[128,512]{1,0:T(8,128)(2,1)S(1)}, u32[]{:S(2)}, u32[]{:S(2)}) collective-permute-start(bf16[128,512]{1,0:T(8,128)(2,1)S(1)} %get-tuple-element.61), channel_id=1, source_target_pairs={{0,24},{8,16},{16,8},{24,0},{1,25},{9,17},{17,9},{25,1},{2,26},{10... | collective-permute-start | bytes 393224 | tf_op jit(solution)/shard_map/ppermute | solution.py:25
  23.4 0.1 shard_map.101
  23.5 3.7 %collective-permute-start.14 = (bf16[256,128]{1,0:T(8,128)(2,1)S(1)}, bf16[256,128]{1,0:T(8,128)(2,1)S(1)}, u32[]{:S(2)}, u32[]{:S(2)}) collective-permute-start(bf16[256,128]{1,0:T(8,128)(2,1)S(1)} %get-tuple-element.63), channel_id=1, source_target_pairs={{0,6},{1,5},{2,4},{3,7},{4,2},{5,1},{6,0},{7,3},{8,14},{9,13},{10,... | collective-permute-start | bytes 196616 | tf_op jit(solution)/shard_map/ppermute | solution.py:279
  27.2 0.5 %collective-permute-start.16 = (bf16[128,512]{1,0:T(8,128)(2,1)S(1)}, bf16[128,512]{1,0:T(8,128)(2,1)S(1)}, u32[]{:S(2)}, u32[]{:S(2)}) collective-permute-start(bf16[128,512]{1,0:T(8,128)(2,1)S(1)} %get-tuple-element.66), channel_id=1, source_target_pairs={{0,8},{8,0},{16,24},{24,16},{1,9},{9,1},{17,25},{25,17},{2,10},{10... | collective-permute-start | bytes 393224 | tf_op jit(solution)/shard_map/ppermute | solution.py:25
  27.7 1.5 %collective-permute-start.17 = (bf16[128,512]{1,0:T(8,128)(2,1)S(1)}, bf16[128,512]{1,0:T(8,128)(2,1)S(1)}, u32[]{:S(2)}, u32[]{:S(2)}) collective-permute-start(bf16[128,512]{1,0:T(8,128)(2,1)S(1)} %get-tuple-element.67), channel_id=1, source_target_pairs={{0,16},{8,24},{16,0},{24,8},{1,17},{9,25},{17,1},{25,9},{2,18},{10... | collective-permute-start | bytes 393224 | tf_op jit(solution)/shard_map/ppermute | solution.py:25
  29.3 1.5 %collective-permute-start.12 = (bf16[256,128]{1,0:T(8,128)(2,1)S(1)}, bf16[256,128]{1,0:T(8,128)(2,1)S(1)}, u32[]{:S(2)}, u32[]{:S(2)}) collective-permute-start(bf16[256,128]{1,0:T(8,128)(2,1)S(1)} %get-tuple-element.59), channel_id=1, source_target_pairs={{0,2},{1,3},{2,0},{3,1},{4,6},{5,7},{6,4},{7,5},{8,10},{9,11},{10,... | collective-permute-start | bytes 196616 | tf_op jit(solution)/shard_map/ppermute | solution.py:25
  30.8 2.0 %collective-permute-done.15.refs_1_ = bf16[256,128]{1,0:T(8,128)(2,1)S(1)} collective-permute-done((bf16[256,128]{1,0:T(8,128)(2,1)S(1)}, bf16[256,128]{1,0:T(8,128)(2,1)S(1)}, u32[]{:S(2)}, u32[]{:S(2)}) %collective-permute-start.15) | collective-permute-done | bytes 65568 | tf_op jit(solution)/shard_map/ppermute | solution.py:279
  32.8 0.8 %shard_map.104 = bf16[128,512]{1,0:T(8,128)(2,1)} custom-call(f32[128,512]{1,0:T(8,128)S(1)} %shard_map.102.dq_ref, bf16[128,512]{1,0:T(8,128)(2,1)S(1)} %collective-permute-done.16.refs_0_, bf16[128,512]{1,0:T(8,128)(2,1)S(1)} %collective-permute-done.17.refs_1_), custom_call_target="tpu_custom_call" | custom-call | flops 1000 | bytes 1000 | tf_op jit(solution)/shard_map/pallas_call | solution.py:350
  33.6 0.6 %shard_map.105 = (bf16[128,128]{1,0:T(8,128)(2,1)}, bf16[128,128]{1,0:T(8,128)(2,1)}) custom-call(f32[256,128]{1,0:T(8,128)S(1)} %shard_map.103.dkv_ref, bf16[256,128]{1,0:T(8,128)(2,1)S(1)} %collective-permute-done.12.near_ref), custom_call_target="tpu_custom_call" | custom-call | flops 1000 | bytes 1000 | tf_op jit(solution)/shard_map/pallas_call | solution.py:360
  (18 shorter events, 0.1 us)
Async XLA Ops:
  2.0 10.6 %collective-permute-start = (bf16[1056,128]{1,0:T(8,128)(2,1)S(1)}, bf16[1056,128]{1,0:T(8,128)(2,1)S(1)}, u32[]{:S(2)}, u32[]{:S(2)}) collective-permute-start(bf16[1056,128]{1,0:T(8,128)(2,1)S(1)} %get-tuple-element.38.refs_0_), channel_id=1, source_target_pairs={{0,8},{8,0},{16,24},{24,16},{1,9},{9,1},{17,25},{25,17},{2,10},{10... | collective-permute-start | bytes 811016 | tf_op jit(solution)/shard_map/ppermute | solution.py:25
  5.0 7.9 %collective-permute-start.1 = (bf16[1056,128]{1,0:T(8,128)(2,1)S(1)}, bf16[1056,128]{1,0:T(8,128)(2,1)S(1)}, u32[]{:S(2)}, u32[]{:S(2)}) collective-permute-start(bf16[1056,128]{1,0:T(8,128)(2,1)S(1)} %get-tuple-element.38.refs_0_), channel_id=1, source_target_pairs={{0,16},{8,24},{16,0},{24,8},{1,17},{9,25},{17,1},{25,9},{2,18},{10... | collective-permute-start | bytes 811016 | tf_op jit(solution)/shard_map/ppermute | solution.py:25
  6.5 4.1 %collective-permute-start.2 = (bf16[272,128]{1,0:T(8,128)(2,1)S(1)}, bf16[272,128]{1,0:T(8,128)(2,1)S(1)}, u32[]{:S(2)}, u32[]{:S(2)}) collective-permute-start(bf16[272,128]{1,0:T(8,128)(2,1)S(1)} %get-tuple-element.39.refs_1_.refs_2_), channel_id=1, source_target_pairs={{0,1},{1,0},{2,3},{3,2},{4,5},{5,4},{6,7},{7,6},{8,9},{9,8},{10,11... | collective-permute-start | bytes 208904 | tf_op jit(solution)/shard_map/ppermute | solution.py:25
  6.5 5.4 %collective-permute-start.3 = (bf16[272,128]{1,0:T(8,128)(2,1)S(1)}, bf16[272,128]{1,0:T(8,128)(2,1)S(1)}, u32[]{:S(2)}, u32[]{:S(2)}) collective-permute-start(bf16[272,128]{1,0:T(8,128)(2,1)S(1)} %get-tuple-element.39.refs_1_.refs_2_), channel_id=1, source_target_pairs={{0,2},{1,3},{2,0},{3,1},{4,6},{5,7},{6,4},{7,5},{8,10},{9,11},{10,... | collective-permute-start | bytes 208904 | tf_op jit(solution)/shard_map/ppermute | solution.py:25
  8.1 8.2 %collective-permute-start.7 = (bf16[272,128]{1,0:T(8,128)(2,1)S(1)}, bf16[272,128]{1,0:T(8,128)(2,1)S(1)}, u32[]{:S(2)}, u32[]{:S(2)}) collective-permute-start(bf16[272,128]{1,0:T(8,128)(2,1)S(1)} %get-tuple-element.39.refs_1_.refs_2_), channel_id=1, source_target_pairs={{0,6},{1,5},{2,4},{3,7},{4,2},{5,1},{6,0},{7,3},{8,14},{9,13},{10,... | collective-permute-start | bytes 208904 | tf_op jit(solution)/shard_map/ppermute | solution.py:279
  10.6 6.2 %collective-permute-start.8 = (bf16[272,128]{1,0:T(8,128)(2,1)S(1)}, bf16[272,128]{1,0:T(8,128)(2,1)S(1)}, u32[]{:S(2)}, u32[]{:S(2)}) collective-permute-start(bf16[272,128]{1,0:T(8,128)(2,1)S(1)} %collective-permute-done.2.refs_2_.refs_3_), channel_id=1, source_target_pairs={{0,6},{1,5},{2,4},{3,7},{4,2},{5,1},{6,0},{7,3},{8,14},{9,13},{10,... | collective-permute-start | bytes 208904 | tf_op jit(solution)/shard_map/ppermute | solution.py:279
  12.9 7.4 %collective-permute-start.5 = (bf16[544,128]{1,0:T(8,128)(2,1)S(1)}, bf16[544,128]{1,0:T(8,128)(2,1)S(1)}, u32[]{:S(2)}, u32[]{:S(2)}) collective-permute-start(bf16[544,128]{1,0:T(8,128)(2,1)S(1)} %slice.7), channel_id=1, source_target_pairs={{0,16},{8,24},{16,0},{24,8},{1,17},{9,25},{17,1},{25,9},{2,18},{10... | collective-permute-start | bytes 417800 | tf_op jit(solution)/shard_map/ppermute | solution.py:25
  14.5 5.8 %collective-permute-start.4 = (bf16[512,128]{1,0:T(8,128)(2,1)S(1)}, bf16[512,128]{1,0:T(8,128)(2,1)S(1)}, u32[]{:S(2)}, u32[]{:S(2)}) collective-permute-start(bf16[512,128]{1,0:T(8,128)(2,1)S(1)} %slice.6), channel_id=1, source_target_pairs={{0,8},{8,0},{16,24},{24,16},{1,9},{9,1},{17,25},{25,17},{2,10},{10... | collective-permute-start | bytes 393224 | tf_op jit(solution)/shard_map/ppermute | solution.py:25
  15.1 2.5 %collective-permute-start.6 = (bf16[272,128]{1,0:T(8,128)(2,1)S(1)}, bf16[272,128]{1,0:T(8,128)(2,1)S(1)}, u32[]{:S(2)}, u32[]{:S(2)}) collective-permute-start(bf16[272,128]{1,0:T(8,128)(2,1)S(1)} %collective-permute-done.3.refs_3_.refs_4_), channel_id=1, source_target_pairs={{0,1},{1,0},{2,3},{3,2},{4,5},{5,4},{6,7},{7,6},{8,9},{9,8},{10,11... | collective-permute-start | bytes 208904 | tf_op jit(solution)/shard_map/ppermute | solution.py:25
  16.8 2.4 %collective-permute-start.10 = (bf16[272,128]{1,0:T(8,128)(2,1)S(1)}, bf16[272,128]{1,0:T(8,128)(2,1)S(1)}, u32[]{:S(2)}, u32[]{:S(2)}) collective-permute-start(bf16[272,128]{1,0:T(8,128)(2,1)S(1)} %collective-permute-done.8.refs_5_.refs_7_), channel_id=1, source_target_pairs={{0,1},{1,0},{2,3},{3,2},{4,5},{5,4},{6,7},{7,6},{8,9},{9,8},{10,11... | collective-permute-start | bytes 208904 | tf_op jit(solution)/shard_map/ppermute | solution.py:25
  17.6 1.6 %collective-permute-start.9 = (bf16[272,128]{1,0:T(8,128)(2,1)S(1)}, bf16[272,128]{1,0:T(8,128)(2,1)S(1)}, u32[]{:S(2)}, u32[]{:S(2)}) collective-permute-start(bf16[272,128]{1,0:T(8,128)(2,1)S(1)} %collective-permute-done.7.refs_4_.refs_6_), channel_id=1, source_target_pairs={{0,1},{1,0},{2,3},{3,2},{4,5},{5,4},{6,7},{7,6},{8,9},{9,8},{10,11... | collective-permute-start | bytes 208904 | tf_op jit(solution)/shard_map/ppermute | solution.py:25
  21.2 2.2 %collective-permute-start.11 = (bf16[4,256,128]{2,1,0:T(8,128)(2,1)S(1)}, bf16[4,256,128]{2,1,0:T(8,128)(2,1)S(1)}, u32[]{:S(2)}, u32[]{:S(2)}) collective-permute-start(bf16[4,256,128]{2,1,0:T(8,128)(2,1)S(1)} %get-tuple-element.58), channel_id=1, source_target_pairs={{0,1},{1,0},{2,3},{3,2},{4,5},{5,4},{6,7},{7,6},{8,9},{9,8},{10,11... | collective-permute-start | bytes 786440 | tf_op jit(solution)/shard_map/ppermute | solution.py:25
  22.6 6.6 %collective-permute-start.13 = (bf16[128,512]{1,0:T(8,128)(2,1)S(1)}, bf16[128,512]{1,0:T(8,128)(2,1)S(1)}, u32[]{:S(2)}, u32[]{:S(2)}) collective-permute-start(bf16[128,512]{1,0:T(8,128)(2,1)S(1)} %get-tuple-element.61), channel_id=1, source_target_pairs={{0,24},{8,16},{16,8},{24,0},{1,25},{9,17},{17,9},{25,1},{2,26},{10... | collective-permute-start | bytes 393224 | tf_op jit(solution)/shard_map/ppermute | solution.py:25
  23.5 7.3 %collective-permute-start.14 = (bf16[256,128]{1,0:T(8,128)(2,1)S(1)}, bf16[256,128]{1,0:T(8,128)(2,1)S(1)}, u32[]{:S(2)}, u32[]{:S(2)}) collective-permute-start(bf16[256,128]{1,0:T(8,128)(2,1)S(1)} %get-tuple-element.63), channel_id=1, source_target_pairs={{0,6},{1,5},{2,4},{3,7},{4,2},{5,1},{6,0},{7,3},{8,14},{9,13},{10,... | collective-permute-start | bytes 196616 | tf_op jit(solution)/shard_map/ppermute | solution.py:279
  27.2 5.6 %collective-permute-start.15 = (bf16[256,128]{1,0:T(8,128)(2,1)S(1)}, bf16[256,128]{1,0:T(8,128)(2,1)S(1)}, u32[]{:S(2)}, u32[]{:S(2)}) collective-permute-start(bf16[256,128]{1,0:T(8,128)(2,1)S(1)} %get-tuple-element.64), channel_id=1, source_target_pairs={{0,4},{1,7},{2,6},{3,5},{4,0},{5,3},{6,2},{7,1},{8,12},{9,15},{10,... | collective-permute-start | bytes 196616 | tf_op jit(solution)/shard_map/ppermute | solution.py:279
  27.2 5.6 %collective-permute-start.16 = (bf16[128,512]{1,0:T(8,128)(2,1)S(1)}, bf16[128,512]{1,0:T(8,128)(2,1)S(1)}, u32[]{:S(2)}, u32[]{:S(2)}) collective-permute-start(bf16[128,512]{1,0:T(8,128)(2,1)S(1)} %get-tuple-element.66), channel_id=1, source_target_pairs={{0,8},{8,0},{16,24},{24,16},{1,9},{9,1},{17,25},{25,17},{2,10},{10... | collective-permute-start | bytes 393224 | tf_op jit(solution)/shard_map/ppermute | solution.py:25
  27.7 5.1 %collective-permute-start.17 = (bf16[128,512]{1,0:T(8,128)(2,1)S(1)}, bf16[128,512]{1,0:T(8,128)(2,1)S(1)}, u32[]{:S(2)}, u32[]{:S(2)}) collective-permute-start(bf16[128,512]{1,0:T(8,128)(2,1)S(1)} %get-tuple-element.67), channel_id=1, source_target_pairs={{0,16},{8,24},{16,0},{24,8},{1,17},{9,25},{17,1},{25,9},{2,18},{10... | collective-permute-start | bytes 393224 | tf_op jit(solution)/shard_map/ppermute | solution.py:25
  29.3 4.4 %collective-permute-start.12 = (bf16[256,128]{1,0:T(8,128)(2,1)S(1)}, bf16[256,128]{1,0:T(8,128)(2,1)S(1)}, u32[]{:S(2)}, u32[]{:S(2)}) collective-permute-start(bf16[256,128]{1,0:T(8,128)(2,1)S(1)} %get-tuple-element.59), channel_id=1, source_target_pairs={{0,2},{1,3},{2,0},{3,1},{4,6},{5,7},{6,4},{7,5},{8,10},{9,11},{10,... | collective-permute-start | bytes 196616 | tf_op jit(solution)/shard_map/ppermute | solution.py:25

commit v22 on v21

--- a/solution.py
+++ b/solution.py
@@ -40,7 +40,7 @@
 def pack_kernel(q_ref, k_ref, v_ref, o_ref, g_ref, lse_ref, pos_ref, x_ref, kv_ref, o_s, lse_s, pos_s, sems):
     rows, width = k_ref.shape
     heads = q_ref.shape[1] // width
-    moves = [(lse_ref, lse_s), (pos_ref, pos_s), (o_ref, o_s)]
+    moves = [(o_ref, o_s), (lse_ref, lse_s), (pos_ref, pos_s)]
     for h in range(heads):
         cols = pl.ds(h * width, width)
         moves.append((g_ref.at[:, cols], x_ref.at[pl.ds((heads + h) * rows, rows), :]))
@@ -102,7 +102,7 @@
         lse = e[0:heads] + e[heads : 2 * heads] + e[2 * heads : 3 * heads]
         delta = e[3 * heads : 4 * heads] + e[4 * heads : 5 * heads] + e[5 * heads : 6 * heads]
         rowed.append((lse, delta, e[6 * heads : 6 * heads + 1]))
-    group = 3 if len(slots) == 3 else 2
+    group = len(slots) if len(slots) <= 4 else 2
     loaded = {}
 
     def chunk(c):

time: 34.5 us -> 34.4 us (level)
  no operation moved by 1% of the time
where the time goes in v22:
time: 34.4 us; the launch traced here: 34.3 us
  starting transfers between devices  21.6 us (63%)
  Pallas kernels  9.07 us (26%)
  waiting for transfers between devices  2.82 us (8%)
  between operations  0.79 us (2%)
    ppermute x14, starting transfers between devices, swapped(): return lax.ppermute(block, axis, pairs)  14.1 us
    ppermute x4, starting transfers between devices, crossed(): return lax.ppermute(block, 'inner', pairs)  7.5 us
    pallas_call x6, Pallas kernels, blocks_call(): pl.pallas_call(functools.partial(blocks_kernel, plan, rows, heads, scale)...  6.2 us
    ppermute x4, waiting for transfers between devices, crossed(): return lax.ppermute(block, 'inner', pairs)  2.46 us
    pallas_call x1, Pallas kernels, on_device(): pl.pallas_call(pack_kernel, out_shape=(sds((2 * hr + 32, width), BF), sds...  1.31 us
    pallas_call x1, Pallas kernels, on_device(): pl.pallas_call(functools.partial(query_kernel, rows, heads, scale), out_s...  0.8 us
  transfers between devices with their start and end apart: 18, of which 3 were waited for; matrix products, arithmetic and copies ran while one was open for 0% of the time, Pallas kernels for 18%

profile of v22, /device:TPU:0, one launch (start us, length us, event | category | flops | bytes accessed | tf_op | source)
XLA Modules:
  0.0 34.3 jit_solution(9710531966992924346)
XLA Ops:
  0.6 1.3 %shard_map.94 = (bf16[1056,128]{1,0:T(8,128)(2,1)S(1)}, bf16[272,128]{1,0:T(8,128)(2,1)S(1)}) custom-call(bf16[128,512]{1,0:T(8,128)(2,1)} %q_ref.1, bf16[128,128]{1,0:T(8,128)(2,1)} %k_ref.1, bf16[128,128]{1,0:T(8,128)(2,1)} %v_ref.1, bf16[128,512]{1,0:T(8,128)(2,1)} %o_ref.1, bf16[128,512]{1,0:T(8,128)(2,1)} %g_ref.1, f32[4,128]{1,0:T(4,128)} %lse_ref.1, ...), custom_call_target="tpu_custom_call" | custom-call | flops 1000 | bytes 1000 | tf_op jit(solution)/shard_map/pallas_call | solution.py:291
  1.9 3.0 %collective-permute-start = (bf16[1056,128]{1,0:T(8,128)(2,1)S(1)}, bf16[1056,128]{1,0:T(8,128)(2,1)S(1)}, u32[]{:S(2)}, u32[]{:S(2)}) collective-permute-start(bf16[1056,128]{1,0:T(8,128)(2,1)S(1)} %get-tuple-element.38.refs_0_), channel_id=1, source_target_pairs={{0,8},{8,0},{16,24},{24,16},{1,9},{9,1},{17,25},{25,17},{2,10},{10... | collective-permute-start | bytes 811016 | tf_op jit(solution)/shard_map/ppermute | solution.py:25
  5.0 1.5 %collective-permute-start.1 = (bf16[1056,128]{1,0:T(8,128)(2,1)S(1)}, bf16[1056,128]{1,0:T(8,128)(2,1)S(1)}, u32[]{:S(2)}, u32[]{:S(2)}) collective-permute-start(bf16[1056,128]{1,0:T(8,128)(2,1)S(1)} %get-tuple-element.38.refs_0_), channel_id=1, source_target_pairs={{0,16},{8,24},{16,0},{24,8},{1,17},{9,25},{17,1},{25,9},{2,18},{10... | collective-permute-start | bytes 811016 | tf_op jit(solution)/shard_map/ppermute | solution.py:25
  6.5 1.6 %collective-permute-start.3 = (bf16[272,128]{1,0:T(8,128)(2,1)S(1)}, bf16[272,128]{1,0:T(8,128)(2,1)S(1)}, u32[]{:S(2)}, u32[]{:S(2)}) collective-permute-start(bf16[272,128]{1,0:T(8,128)(2,1)S(1)} %get-tuple-element.39.refs_1_.refs_2_), channel_id=1, source_target_pairs={{0,2},{1,3},{2,0},{3,1},{4,6},{5,7},{6,4},{7,5},{8,10},{9,11},{10,... | collective-permute-start | bytes 208904 | tf_op jit(solution)/shard_map/ppermute | solution.py:25
  8.1 2.5 %collective-permute-start.7 = (bf16[272,128]{1,0:T(8,128)(2,1)S(1)}, bf16[272,128]{1,0:T(8,128)(2,1)S(1)}, u32[]{:S(2)}, u32[]{:S(2)}) collective-permute-start(bf16[272,128]{1,0:T(8,128)(2,1)S(1)} %get-tuple-element.39.refs_1_.refs_2_), channel_id=1, source_target_pairs={{0,6},{1,5},{2,4},{3,7},{4,2},{5,1},{6,0},{7,3},{8,14},{9,13},{10,... | collective-permute-start | bytes 208904 | tf_op jit(solution)/shard_map/ppermute | solution.py:279
  10.5 0.0 collective-permute-done.2.refs_2_.refs_3_
  10.5 1.3 %collective-permute-start.8 = (bf16[272,128]{1,0:T(8,128)(2,1)S(1)}, bf16[272,128]{1,0:T(8,128)(2,1)S(1)}, u32[]{:S(2)}, u32[]{:S(2)}) collective-permute-start(bf16[272,128]{1,0:T(8,128)(2,1)S(1)} %collective-permute-done.2.refs_2_.refs_3_), channel_id=1, source_target_pairs={{0,6},{1,5},{2,4},{3,7},{4,2},{5,1},{6,0},{7,3},{8,14},{9,13},{10,... | collective-permute-start | bytes 208904 | tf_op jit(solution)/shard_map/ppermute | solution.py:279
  11.9 0.7 %shard_map.95 = (f32[128,512]{1,0:T(8,128)S(1)}, f32[3,256,128]{2,1,0:T(8,128)S(1)}) custom-call(bf16[1056,128]{1,0:T(8,128)(2,1)S(1)} %get-tuple-element.38.refs_0_, bf16[272,128]{1,0:T(8,128)(2,1)S(1)} %get-tuple-element.39.refs_1_.refs_2_, bf16[272,128]{1,0:T(8,128)(2,1)S(1)} %collective-permute-done.2.refs_2_.refs_3_, ...), custom_call_target="tpu_custom_call" | custom-call | flops 1000 | bytes 1000 | tf_op jit(solution)/shard_map/pallas_call | solution.py:209
  12.6 0.0 collective-permute-done.refs_0_.refs_1_
  12.6 0.3 collective-permute-done.1.refs_1_.refs_2_
  12.9 1.6 %collective-permute-start.5 = (bf16[544,128]{1,0:T(8,128)(2,1)S(1)}, bf16[544,128]{1,0:T(8,128)(2,1)S(1)}, u32[]{:S(2)}, u32[]{:S(2)}) collective-permute-start(bf16[544,128]{1,0:T(8,128)(2,1)S(1)} %slice.7), channel_id=1, source_target_pairs={{0,16},{8,24},{16,0},{24,8},{1,17},{9,25},{17,1},{25,9},{2,18},{10... | collective-permute-start | bytes 417800 | tf_op jit(solution)/shard_map/ppermute | solution.py:25
  14.5 0.6 %collective-permute-start.4 = (bf16[512,128]{1,0:T(8,128)(2,1)S(1)}, bf16[512,128]{1,0:T(8,128)(2,1)S(1)}, u32[]{:S(2)}, u32[]{:S(2)}) collective-permute-start(bf16[512,128]{1,0:T(8,128)(2,1)S(1)} %slice.6), channel_id=1, source_target_pairs={{0,8},{8,0},{16,24},{24,16},{1,9},{9,1},{17,25},{25,17},{2,10},{10... | collective-permute-start | bytes 393224 | tf_op jit(solution)/shard_map/ppermute | solution.py:25
  15.1 0.0 collective-permute-start.6
  15.1 1.2 %shard_map.96 = (f32[128,512]{1,0:T(8,128)S(1)}, f32[128,512]{1,0:T(8,128)S(1)}, f32[3,256,128]{2,1,0:T(8,128)S(1)}) custom-call(bf16[1056,128]{1,0:T(8,128)(2,1)S(1)} %collective-permute-done.refs_0_.refs_1_, bf16[1056,128]{1,0:T(8,128)(2,1)S(1)} %collective-permute-done.1.refs_1_.refs_2_, bf16[272,128]{1,0:T(8,128)(2,1)S(1)} %get-tuple-element.39.refs_1_.refs_2_, ...), custom_call_target="tpu_custom_call" | custom-call | flops 1000 | bytes 1000 | tf_op jit(solution)/shard_map/pallas_call | solution.py:209
  16.3 0.5 %collective-permute-done.8.refs_5_.refs_7_ = bf16[272,128]{1,0:T(8,128)(2,1)S(1)} collective-permute-done((bf16[272,128]{1,0:T(8,128)(2,1)S(1)}, bf16[272,128]{1,0:T(8,128)(2,1)S(1)}, u32[]{:S(2)}, u32[]{:S(2)}) %collective-permute-start.8) | collective-permute-done | bytes 69664 | tf_op jit(solution)/shard_map/ppermute | solution.py:279
  16.7 0.8 %collective-permute-start.10 = (bf16[272,128]{1,0:T(8,128)(2,1)S(1)}, bf16[272,128]{1,0:T(8,128)(2,1)S(1)}, u32[]{:S(2)}, u32[]{:S(2)}) collective-permute-start(bf16[272,128]{1,0:T(8,128)(2,1)S(1)} %collective-permute-done.8.refs_5_.refs_7_), channel_id=1, source_target_pairs={{0,1},{1,0},{2,3},{3,2},{4,5},{5,4},{6,7},{7,6},{8,9},{9,8},{10,11... | collective-permute-start | bytes 208904 | tf_op jit(solution)/shard_map/ppermute | solution.py:25
  17.6 0.0 collective-permute-start.9
  17.6 0.0 collective-permute-done.6.refs_3_.refs_5_
  17.6 1.6 %shard_map.97 = (f32[128,512]{1,0:T(8,128)S(1)}, f32[128,512]{1,0:T(8,128)S(1)}, f32[128,512]{1,0:T(8,128)S(1)}, f32[3,256,128]{2,1,0:T(8,128)S(1)}) custom-call(bf16[1056,128]{1,0:T(8,128)(2,1)S(1)} %get-tuple-element.38.refs_0_, bf16[1056,128]{1,0:T(8,128)(2,1)S(1)} %collective-permute-done.refs_0_.refs_1_, ...), custom_call_target="tpu_custom_call" | custom-call | flops 1000 | bytes 1000 | tf_op jit(solution)/shard_map/pallas_call | solution.py:209
  19.2 1.1 %shard_map.98 = (f32[128,512]{1,0:T(8,128)S(1)}, bf16[128,512]{1,0:T(8,128)(2,1)S(1)}, bf16[128,512]{1,0:T(8,128)(2,1)S(1)}, f32[2,256,128]{2,1,0:T(8,128)S(1)}) custom-call(bf16[1056,128]{1,0:T(8,128)(2,1)S(1)} %get-tuple-element.38.refs_0_, bf16[1056,128]{1,0:T(8,128)(2,1)S(1)} %collective-permute-done.refs_0_.refs_1_, ...), custom_call_target="tpu_custom_call" | custom-call | flops 1000 | bytes 1000 | tf_op jit(solution)/shard_map/pallas_call | solution.py:209
  20.4 0.8 %shard_map.99 = (f32[128,512]{1,0:T(8,128)S(1)}, bf16[4,256,128]{2,1,0:T(8,128)(2,1)S(1)}) custom-call(bf16[512,128]{1,0:T(8,128)(2,1)S(1)} %collective-permute-done.4.refs_0_, bf16[544,128]{1,0:T(8,128)(2,1)S(1)} %collective-permute-done.5.refs_1_, bf16[272,128]{1,0:T(8,128)(2,1)S(1)} %get-tuple-element.39.refs_1_.refs_2_, ...), custom_call_target="tpu_custom_call" | custom-call | flops 1000 | bytes 1000 | tf_op jit(solution)/shard_map/pallas_call | solution.py:209
  21.2 0.6 %collective-permute-start.11 = (bf16[4,256,128]{2,1,0:T(8,128)(2,1)S(1)}, bf16[4,256,128]{2,1,0:T(8,128)(2,1)S(1)}, u32[]{:S(2)}, u32[]{:S(2)}) collective-permute-start(bf16[4,256,128]{2,1,0:T(8,128)(2,1)S(1)} %get-tuple-element.58), channel_id=1, source_target_pairs={{0,1},{1,0},{2,3},{3,2},{4,5},{5,4},{6,7},{7,6},{8,9},{9,8},{10,11... | collective-permute-start | bytes 786440 | tf_op jit(solution)/shard_map/ppermute | solution.py:25
  21.7 0.8 %shard_map.100 = (bf16[128,512]{1,0:T(8,128)(2,1)S(1)}, f32[4,256,128]{2,1,0:T(8,128)S(1)}) custom-call(bf16[512,128]{1,0:T(8,128)(2,1)S(1)} %collective-permute-done.4.refs_0_, bf16[544,128]{1,0:T(8,128)(2,1)S(1)} %collective-permute-done.5.refs_1_, bf16[272,128]{1,0:T(8,128)(2,1)S(1)} %get-tuple-element.39.refs_1_.refs_2_, ...), custom_call_target="tpu_custom_call" | custom-call | flops 1000 | bytes 1000 | tf_op jit(solution)/shard_map/pallas_call | solution.py:209
  22.6 0.8 %collective-permute-start.13 = (bf16[128,512]{1,0:T(8,128)(2,1)S(1)}, bf16[128,512]{1,0:T(8,128)(2,1)S(1)}, u32[]{:S(2)}, u32[]{:S(2)}) collective-permute-start(bf16[128,512]{1,0:T(8,128)(2,1)S(1)} %get-tuple-element.61), channel_id=1, source_target_pairs={{0,24},{8,16},{16,8},{24,0},{1,25},{9,17},{17,9},{25,1},{2,26},{10... | collective-permute-start | bytes 393224 | tf_op jit(solution)/shard_map/ppermute | solution.py:25
  23.4 0.1 shard_map.101
  23.5 3.7 %collective-permute-start.14 = (bf16[256,128]{1,0:T(8,128)(2,1)S(1)}, bf16[256,128]{1,0:T(8,128)(2,1)S(1)}, u32[]{:S(2)}, u32[]{:S(2)}) collective-permute-start(bf16[256,128]{1,0:T(8,128)(2,1)S(1)} %get-tuple-element.63), channel_id=1, source_target_pairs={{0,6},{1,5},{2,4},{3,7},{4,2},{5,1},{6,0},{7,3},{8,14},{9,13},{10,... | collective-permute-start | bytes 196616 | tf_op jit(solution)/shard_map/ppermute | solution.py:279
  27.1 0.5 %collective-permute-start.16 = (bf16[128,512]{1,0:T(8,128)(2,1)S(1)}, bf16[128,512]{1,0:T(8,128)(2,1)S(1)}, u32[]{:S(2)}, u32[]{:S(2)}) collective-permute-start(bf16[128,512]{1,0:T(8,128)(2,1)S(1)} %get-tuple-element.66), channel_id=1, source_target_pairs={{0,8},{8,0},{16,24},{24,16},{1,9},{9,1},{17,25},{25,17},{2,10},{10... | collective-permute-start | bytes 393224 | tf_op jit(solution)/shard_map/ppermute | solution.py:25
  27.7 1.5 %collective-permute-start.17 = (bf16[128,512]{1,0:T(8,128)(2,1)S(1)}, bf16[128,512]{1,0:T(8,128)(2,1)S(1)}, u32[]{:S(2)}, u32[]{:S(2)}) collective-permute-start(bf16[128,512]{1,0:T(8,128)(2,1)S(1)} %get-tuple-element.67), channel_id=1, source_target_pairs={{0,16},{8,24},{16,0},{24,8},{1,17},{9,25},{17,1},{25,9},{2,18},{10... | collective-permute-start | bytes 393224 | tf_op jit(solution)/shard_map/ppermute | solution.py:25
  29.2 1.5 %collective-permute-start.12 = (bf16[256,128]{1,0:T(8,128)(2,1)S(1)}, bf16[256,128]{1,0:T(8,128)(2,1)S(1)}, u32[]{:S(2)}, u32[]{:S(2)}) collective-permute-start(bf16[256,128]{1,0:T(8,128)(2,1)S(1)} %get-tuple-element.59), channel_id=1, source_target_pairs={{0,2},{1,3},{2,0},{3,1},{4,6},{5,7},{6,4},{7,5},{8,10},{9,11},{10,... | collective-permute-start | bytes 196616 | tf_op jit(solution)/shard_map/ppermute | solution.py:25
  30.8 2.0 %collective-permute-done.15.refs_1_ = bf16[256,128]{1,0:T(8,128)(2,1)S(1)} collective-permute-done((bf16[256,128]{1,0:T(8,128)(2,1)S(1)}, bf16[256,128]{1,0:T(8,128)(2,1)S(1)}, u32[]{:S(2)}, u32[]{:S(2)}) %collective-permute-start.15) | collective-permute-done | bytes 65568 | tf_op jit(solution)/shard_map/ppermute | solution.py:279
  32.8 0.8 %shard_map.104 = bf16[128,512]{1,0:T(8,128)(2,1)} custom-call(f32[128,512]{1,0:T(8,128)S(1)} %shard_map.102.dq_ref, bf16[128,512]{1,0:T(8,128)(2,1)S(1)} %collective-permute-done.16.refs_0_, bf16[128,512]{1,0:T(8,128)(2,1)S(1)} %collective-permute-done.17.refs_1_), custom_call_target="tpu_custom_call" | custom-call | flops 1000 | bytes 1000 | tf_op jit(solution)/shard_map/pallas_call | solution.py:350
  33.6 0.6 %shard_map.105 = (bf16[128,128]{1,0:T(8,128)(2,1)}, bf16[128,128]{1,0:T(8,128)(2,1)}) custom-call(f32[256,128]{1,0:T(8,128)S(1)} %shard_map.103.dkv_ref, bf16[256,128]{1,0:T(8,128)(2,1)S(1)} %collective-permute-done.12.near_ref), custom_call_target="tpu_custom_call" | custom-call | flops 1000 | bytes 1000 | tf_op jit(solution)/shard_map/pallas_call | solution.py:360
  (18 shorter events, 0.1 us)
Async XLA Ops:
  1.9 10.6 %collective-permute-start = (bf16[1056,128]{1,0:T(8,128)(2,1)S(1)}, bf16[1056,128]{1,0:T(8,128)(2,1)S(1)}, u32[]{:S(2)}, u32[]{:S(2)}) collective-permute-start(bf16[1056,128]{1,0:T(8,128)(2,1)S(1)} %get-tuple-element.38.refs_0_), channel_id=1, source_target_pairs={{0,8},{8,0},{16,24},{24,16},{1,9},{9,1},{17,25},{25,17},{2,10},{10... | collective-permute-start | bytes 811016 | tf_op jit(solution)/shard_map/ppermute | solution.py:25
  5.0 7.9 %collective-permute-start.1 = (bf16[1056,128]{1,0:T(8,128)(2,1)S(1)}, bf16[1056,128]{1,0:T(8,128)(2,1)S(1)}, u32[]{:S(2)}, u32[]{:S(2)}) collective-permute-start(bf16[1056,128]{1,0:T(8,128)(2,1)S(1)} %get-tuple-element.38.refs_0_), channel_id=1, source_target_pairs={{0,16},{8,24},{16,0},{24,8},{1,17},{9,25},{17,1},{25,9},{2,18},{10... | collective-permute-start | bytes 811016 | tf_op jit(solution)/shard_map/ppermute | solution.py:25
  6.5 4.1 %collective-permute-start.2 = (bf16[272,128]{1,0:T(8,128)(2,1)S(1)}, bf16[272,128]{1,0:T(8,128)(2,1)S(1)}, u32[]{:S(2)}, u32[]{:S(2)}) collective-permute-start(bf16[272,128]{1,0:T(8,128)(2,1)S(1)} %get-tuple-element.39.refs_1_.refs_2_), channel_id=1, source_target_pairs={{0,1},{1,0},{2,3},{3,2},{4,5},{5,4},{6,7},{7,6},{8,9},{9,8},{10,11... | collective-permute-start | bytes 208904 | tf_op jit(solution)/shard_map/ppermute | solution.py:25
  6.5 5.4 %collective-permute-start.3 = (bf16[272,128]{1,0:T(8,128)(2,1)S(1)}, bf16[272,128]{1,0:T(8,128)(2,1)S(1)}, u32[]{:S(2)}, u32[]{:S(2)}) collective-permute-start(bf16[272,128]{1,0:T(8,128)(2,1)S(1)} %get-tuple-element.39.refs_1_.refs_2_), channel_id=1, source_target_pairs={{0,2},{1,3},{2,0},{3,1},{4,6},{5,7},{6,4},{7,5},{8,10},{9,11},{10,... | collective-permute-start | bytes 208904 | tf_op jit(solution)/shard_map/ppermute | solution.py:25
  8.1 8.2 %collective-permute-start.7 = (bf16[272,128]{1,0:T(8,128)(2,1)S(1)}, bf16[272,128]{1,0:T(8,128)(2,1)S(1)}, u32[]{:S(2)}, u32[]{:S(2)}) collective-permute-start(bf16[272,128]{1,0:T(8,128)(2,1)S(1)} %get-tuple-element.39.refs_1_.refs_2_), channel_id=1, source_target_pairs={{0,6},{1,5},{2,4},{3,7},{4,2},{5,1},{6,0},{7,3},{8,14},{9,13},{10,... | collective-permute-start | bytes 208904 | tf_op jit(solution)/shard_map/ppermute | solution.py:279
  10.5 6.2 %collective-permute-start.8 = (bf16[272,128]{1,0:T(8,128)(2,1)S(1)}, bf16[272,128]{1,0:T(8,128)(2,1)S(1)}, u32[]{:S(2)}, u32[]{:S(2)}) collective-permute-start(bf16[272,128]{1,0:T(8,128)(2,1)S(1)} %collective-permute-done.2.refs_2_.refs_3_), channel_id=1, source_target_pairs={{0,6},{1,5},{2,4},{3,7},{4,2},{5,1},{6,0},{7,3},{8,14},{9,13},{10,... | collective-permute-start | bytes 208904 | tf_op jit(solution)/shard_map/ppermute | solution.py:279
  12.9 7.4 %collective-permute-start.5 = (bf16[544,128]{1,0:T(8,128)(2,1)S(1)}, bf16[544,128]{1,0:T(8,128)(2,1)S(1)}, u32[]{:S(2)}, u32[]{:S(2)}) collective-permute-start(bf16[544,128]{1,0:T(8,128)(2,1)S(1)} %slice.7), channel_id=1, source_target_pairs={{0,16},{8,24},{16,0},{24,8},{1,17},{9,25},{17,1},{25,9},{2,18},{10... | collective-permute-start | bytes 417800 | tf_op jit(solution)/shard_map/ppermute | solution.py:25
  14.5 5.8 %collective-permute-start.4 = (bf16[512,128]{1,0:T(8,128)(2,1)S(1)}, bf16[512,128]{1,0:T(8,128)(2,1)S(1)}, u32[]{:S(2)}, u32[]{:S(2)}) collective-permute-start(bf16[512,128]{1,0:T(8,128)(2,1)S(1)} %slice.6), channel_id=1, source_target_pairs={{0,8},{8,0},{16,24},{24,16},{1,9},{9,1},{17,25},{25,17},{2,10},{10... | collective-permute-start | bytes 393224 | tf_op jit(solution)/shard_map/ppermute | solution.py:25
  15.1 2.5 %collective-permute-start.6 = (bf16[272,128]{1,0:T(8,128)(2,1)S(1)}, bf16[272,128]{1,0:T(8,128)(2,1)S(1)}, u32[]{:S(2)}, u32[]{:S(2)}) collective-permute-start(bf16[272,128]{1,0:T(8,128)(2,1)S(1)} %collective-permute-done.3.refs_3_.refs_4_), channel_id=1, source_target_pairs={{0,1},{1,0},{2,3},{3,2},{4,5},{5,4},{6,7},{7,6},{8,9},{9,8},{10,11... | collective-permute-start | bytes 208904 | tf_op jit(solution)/shard_map/ppermute | solution.py:25
  16.7 2.4 %collective-permute-start.10 = (bf16[272,128]{1,0:T(8,128)(2,1)S(1)}, bf16[272,128]{1,0:T(8,128)(2,1)S(1)}, u32[]{:S(2)}, u32[]{:S(2)}) collective-permute-start(bf16[272,128]{1,0:T(8,128)(2,1)S(1)} %collective-permute-done.8.refs_5_.refs_7_), channel_id=1, source_target_pairs={{0,1},{1,0},{2,3},{3,2},{4,5},{5,4},{6,7},{7,6},{8,9},{9,8},{10,11... | collective-permute-start | bytes 208904 | tf_op jit(solution)/shard_map/ppermute | solution.py:25
  17.6 1.6 %collective-permute-start.9 = (bf16[272,128]{1,0:T(8,128)(2,1)S(1)}, bf16[272,128]{1,0:T(8,128)(2,1)S(1)}, u32[]{:S(2)}, u32[]{:S(2)}) collective-permute-start(bf16[272,128]{1,0:T(8,128)(2,1)S(1)} %collective-permute-done.7.refs_4_.refs_6_), channel_id=1, source_target_pairs={{0,1},{1,0},{2,3},{3,2},{4,5},{5,4},{6,7},{7,6},{8,9},{9,8},{10,11... | collective-permute-start | bytes 208904 | tf_op jit(solution)/shard_map/ppermute | solution.py:25
  21.2 2.2 %collective-permute-start.11 = (bf16[4,256,128]{2,1,0:T(8,128)(2,1)S(1)}, bf16[4,256,128]{2,1,0:T(8,128)(2,1)S(1)}, u32[]{:S(2)}, u32[]{:S(2)}) collective-permute-start(bf16[4,256,128]{2,1,0:T(8,128)(2,1)S(1)} %get-tuple-element.58), channel_id=1, source_target_pairs={{0,1},{1,0},{2,3},{3,2},{4,5},{5,4},{6,7},{7,6},{8,9},{9,8},{10,11... | collective-permute-start | bytes 786440 | tf_op jit(solution)/shard_map/ppermute | solution.py:25
  22.6 6.6 %collective-permute-start.13 = (bf16[128,512]{1,0:T(8,128)(2,1)S(1)}, bf16[128,512]{1,0:T(8,128)(2,1)S(1)}, u32[]{:S(2)}, u32[]{:S(2)}) collective-permute-start(bf16[128,512]{1,0:T(8,128)(2,1)S(1)} %get-tuple-element.61), channel_id=1, source_target_pairs={{0,24},{8,16},{16,8},{24,0},{1,25},{9,17},{17,9},{25,1},{2,26},{10... | collective-permute-start | bytes 393224 | tf_op jit(solution)/shard_map/ppermute | solution.py:25
  23.5 7.3 %collective-permute-start.14 = (bf16[256,128]{1,0:T(8,128)(2,1)S(1)}, bf16[256,128]{1,0:T(8,128)(2,1)S(1)}, u32[]{:S(2)}, u32[]{:S(2)}) collective-permute-start(bf16[256,128]{1,0:T(8,128)(2,1)S(1)} %get-tuple-element.63), channel_id=1, source_target_pairs={{0,6},{1,5},{2,4},{3,7},{4,2},{5,1},{6,0},{7,3},{8,14},{9,13},{10,... | collective-permute-start | bytes 196616 | tf_op jit(solution)/shard_map/ppermute | solution.py:279
  27.1 5.6 %collective-permute-start.15 = (bf16[256,128]{1,0:T(8,128)(2,1)S(1)}, bf16[256,128]{1,0:T(8,128)(2,1)S(1)}, u32[]{:S(2)}, u32[]{:S(2)}) collective-permute-start(bf16[256,128]{1,0:T(8,128)(2,1)S(1)} %get-tuple-element.64), channel_id=1, source_target_pairs={{0,4},{1,7},{2,6},{3,5},{4,0},{5,3},{6,2},{7,1},{8,12},{9,15},{10,... | collective-permute-start | bytes 196616 | tf_op jit(solution)/shard_map/ppermute | solution.py:279
  27.1 5.6 %collective-permute-start.16 = (bf16[128,512]{1,0:T(8,128)(2,1)S(1)}, bf16[128,512]{1,0:T(8,128)(2,1)S(1)}, u32[]{:S(2)}, u32[]{:S(2)}) collective-permute-start(bf16[128,512]{1,0:T(8,128)(2,1)S(1)} %get-tuple-element.66), channel_id=1, source_target_pairs={{0,8},{8,0},{16,24},{24,16},{1,9},{9,1},{17,25},{25,17},{2,10},{10... | collective-permute-start | bytes 393224 | tf_op jit(solution)/shard_map/ppermute | solution.py:25
  27.7 5.1 %collective-permute-start.17 = (bf16[128,512]{1,0:T(8,128)(2,1)S(1)}, bf16[128,512]{1,0:T(8,128)(2,1)S(1)}, u32[]{:S(2)}, u32[]{:S(2)}) collective-permute-start(bf16[128,512]{1,0:T(8,128)(2,1)S(1)} %get-tuple-element.67), channel_id=1, source_target_pairs={{0,16},{8,24},{16,0},{24,8},{1,17},{9,25},{17,1},{25,9},{2,18},{10... | collective-permute-start | bytes 393224 | tf_op jit(solution)/shard_map/ppermute | solution.py:25
  29.2 4.4 %collective-permute-start.12 = (bf16[256,128]{1,0:T(8,128)(2,1)S(1)}, bf16[256,128]{1,0:T(8,128)(2,1)S(1)}, u32[]{:S(2)}, u32[]{:S(2)}) collective-permute-start(bf16[256,128]{1,0:T(8,128)(2,1)S(1)} %get-tuple-element.59), channel_id=1, source_target_pairs={{0,2},{1,3},{2,0},{3,1},{4,6},{5,7},{6,4},{7,5},{8,10},{9,11},{10,... | collective-permute-start | bytes 196616 | tf_op jit(solution)/shard_map/ppermute | solution.py:25
